TPU v7x, 32 devices: a whole 2x2x4 slice. The times are simulated.
32 devices in a mesh: dp: 4 (over y, x), seq: 8 (over z, core).
Axes of the slice: x: 2, y: 2, z: 4, core: 2. Of those that a mesh axis runs over, the one named last changes fastest.
Arguments:
- queries: bfloat16 [4, 1024, 512], P('dp', 'seq'), may hold values from -6 to 6
- key_rows: bfloat16 [4, 1024, 512], P('dp', 'seq'), may hold values from -6 to 6
- value_rows: bfloat16 [4, 1024, 512], P('dp', 'seq'), may hold values from -6 to 6
- out_grad: bfloat16 [4, 1024, 1024], P('dp', 'seq'), may hold values from -6 to 6
- out_weight: bfloat16 [512, 1024], P('seq'), may hold values from -0.25 to 0.25
- norm_gain: float32 [256], replicated, may hold values from 0.1 to 1.9
Outputs:
- query_grad: bfloat16 [4, 1024, 512], P('dp', 'seq')
- key_grad: bfloat16 [4, 1024, 512], P('dp', 'seq')
- value_grad: bfloat16 [4, 1024, 512], P('dp', 'seq')
- weight_grad: float32 [512, 1024], P('seq')
All inputs are finite; a program needn't handle non-finite values.
Results may differ from a plain program's by a relative error of at most 0.025.
Values may be sent and summed in bfloat16 or wider, within the bound.
No kernel may reach another device: no remote copies, remote signals or barrier semaphores. Data moves between devices by JAX's collectives and lax.ppermute only.
A program may use at most 64 MiB of HBM per device.

v0:
```python
import math

import jax
import jax.numpy as jnp
from jax import lax
from jax.sharding import PartitionSpec as P

DH = 128
SOFT_HEADS = 2
LIN_HEADS = 2
WINDOW = 256
HALF = 128


norm_eps = 1e-06


def with_halo(block, sides, width):
    for axis, dim in sides:
        count = lax.axis_size(axis)
        forward = [(i, i + 1) for i in range(count - 1)]
        forward.append((count - 1, 0))
        backward = [(target, source) for source, target in forward]
        low = lax.ppermute(
            lax.slice_in_dim(block, block.shape[dim] - width, None, axis=dim), axis, forward
        )
        high = lax.ppermute(lax.slice_in_dim(block, 0, width, axis=dim), axis, backward)
        block = jnp.concatenate([low, block, high], axis=dim)
    return block


def from_behind(value, axis, steps):
    count = lax.axis_size(axis)
    pairs = [(source, (source + steps) % count) for source in range(count)]
    return lax.ppermute(value, axis, pairs)


def unit_plus(values):
    return jnp.where(values > 0, values + 1.0, jnp.exp(jnp.minimum(values, 0.0)))


def unit_slope(values):
    return jnp.where(values > 0, 1.0, jnp.exp(jnp.minimum(values, 0.0)))


def body(queries, key_rows, value_rows, out_grad, out_weight, norm_gain):
    highest = lax.Precision.HIGHEST
    query_all = queries[0]
    key_all = key_rows[0]
    value_all = value_rows[0]
    grad_out = out_grad[0]
    tok_rows = query_all.shape[0]
    soft = SOFT_HEADS * DH
    factor = DH ** (-0.5)
    span_rows = tok_rows + 2 * HALF
    key_value = jnp.stack([key_all[:, :soft], value_all[:, :soft]])
    padded = with_halo(key_value, (("seq", 1),), HALF)
    query_soft = query_all[:, :soft].reshape(tok_rows, SOFT_HEADS, DH)
    key_soft = padded[0].reshape(span_rows, SOFT_HEADS, DH)
    value_soft = padded[1].reshape(span_rows, SOFT_HEADS, DH)
    scores = (
        jnp.einsum("ihd,jhd->hij", query_soft, key_soft, preferred_element_type=jnp.float32)
        * factor
    )
    row_pos = lax.broadcasted_iota(jnp.int32, (tok_rows, span_rows), 0)
    col_pos = lax.broadcasted_iota(jnp.int32, (tok_rows, span_rows), 1)
    inside = (col_pos >= row_pos) & (col_pos < row_pos + WINDOW)
    scores = jnp.where(inside, scores, -1e30)
    row_peak = jnp.max(scores, axis=2, keepdims=True)
    exp_terms = jnp.where(inside, jnp.exp(scores - row_peak), 0.0)
    attn_probs = exp_terms / jnp.sum(exp_terms, axis=2, keepdims=True)
    probs_low = attn_probs.astype(jnp.bfloat16)
    attn_soft = jnp.einsum(
        "hij,jhd->ihd", probs_low, value_soft, preferred_element_type=jnp.float32
    ).astype(jnp.bfloat16)
    query_lin = query_all[:, soft:].astype(jnp.float32).reshape(tok_rows, LIN_HEADS, DH)
    key_lin = key_all[:, soft:].astype(jnp.float32).reshape(tok_rows, LIN_HEADS, DH)
    value_lin = value_all[:, soft:].astype(jnp.float32).reshape(tok_rows, LIN_HEADS, DH)
    phi_query = unit_plus(query_lin)
    phi_key = unit_plus(key_lin)
    state_term = jnp.einsum("jha,jhb->hab", phi_key, value_lin, precision=highest)
    lin_state = lax.psum(state_term, "seq")
    lin_u = jnp.einsum("iha,hab->ihb", phi_query, lin_state, precision=highest)
    lin_r = lax.rsqrt(jnp.mean(lin_u * lin_u, axis=2, keepdims=True) + norm_eps)
    gain_heads = norm_gain.reshape(LIN_HEADS, DH)
    attn_lin = (gain_heads * lin_u * lin_r).astype(jnp.bfloat16)
    attn = jnp.concatenate(
        [attn_soft.reshape(tok_rows, soft), attn_lin.reshape(tok_rows, LIN_HEADS * DH)], axis=1
    )
    d_attn = lax.dot_general(
        grad_out,
        lax.all_gather(out_weight, "seq", axis=0, tiled=True),
        (((1,), (1,)), ((), ())),
        preferred_element_type=jnp.float32,
    ).astype(jnp.bfloat16)
    n_seq = lax.axis_size("seq")
    n_plasmid = lax.axis_size("dp")
    token_total = n_plasmid * n_seq * tok_rows
    local_term = lax.psum_scatter(
        lax.dot_general(
            attn, grad_out, (((0,), (0,)), ((), ())), preferred_element_type=jnp.float32
        ),
        "seq",
        scatter_dimension=0,
        tiled=True,
    )
    summed = lax.psum(local_term, "dp")
    weight_grad = summed * (1.0 / math.sqrt(token_total))
    dattn_soft = d_attn[:, :soft].reshape(tok_rows, SOFT_HEADS, DH)
    dprob = jnp.einsum("ihd,jhd->hij", dattn_soft, value_soft, preferred_element_type=jnp.float32)
    row_delta = jnp.sum(dattn_soft.astype(jnp.float32) * attn_soft.astype(jnp.float32), axis=2)
    dscore = (attn_probs * (dprob - row_delta.T[:, :, None])).astype(jnp.bfloat16)
    dq_soft = (
        jnp.einsum("hij,jhd->ihd", dscore, key_soft, preferred_element_type=jnp.float32) * factor
    )
    dk_span = (
        jnp.einsum("hij,ihd->jhd", dscore, query_soft, preferred_element_type=jnp.float32) * factor
    )
    dv_span = jnp.einsum("hij,ihd->jhd", probs_low, dattn_soft, preferred_element_type=jnp.float32)
    span_grads = jnp.stack([dk_span, dv_span]).reshape(2, span_rows, soft)
    from_next = from_behind(span_grads[:, :HALF], "seq", -1)
    from_prev = from_behind(span_grads[:, tok_rows + HALF :], "seq", 1)
    middle = span_grads[:, HALF : HALF + tok_rows]
    middle = middle + from_prev
    middle = middle + from_next
    lin_grad = gain_heads * d_attn[:, soft:].astype(jnp.float32).reshape(tok_rows, LIN_HEADS, DH)
    grad_u = lin_r * lin_grad - lin_u * lin_r**3 * jnp.mean(lin_grad * lin_u, axis=2, keepdims=True)
    dstate_term = jnp.einsum("iha,ihb->hab", phi_query, grad_u, precision=highest)
    dstate = lax.psum(dstate_term, "seq")
    dq_lin = jnp.einsum("ihb,hab->iha", grad_u, lin_state, precision=highest) * unit_slope(
        query_lin
    )
    dk_lin = jnp.einsum("jhb,hab->jha", value_lin, dstate, precision=highest) * unit_slope(key_lin)
    dv_lin = jnp.einsum("jha,hab->jhb", phi_key, dstate, precision=highest)
    lin_width = LIN_HEADS * DH
    query_grad = jnp.concatenate(
        [dq_soft.reshape(tok_rows, soft), dq_lin.reshape(tok_rows, lin_width)], axis=1
    ).astype(jnp.bfloat16)
    key_grad = jnp.concatenate([middle[0], dk_lin.reshape(tok_rows, lin_width)], axis=1).astype(
        jnp.bfloat16
    )
    value_grad = jnp.concatenate([middle[1], dv_lin.reshape(tok_rows, lin_width)], axis=1).astype(
        jnp.bfloat16
    )
    return (query_grad[None], key_grad[None], value_grad[None], weight_grad)


def solution(mesh):
    return jax.shard_map(
        body,
        mesh=mesh,
        in_specs=(
            P("dp", "seq", None),
            P("dp", "seq", None),
            P("dp", "seq", None),
            P("dp", "seq", None),
            P("seq", None),
            P(),
        ),
        out_specs=(
            P("dp", "seq", None),
            P("dp", "seq", None),
            P("dp", "seq", None),
            P("seq", None),
        ),
        check_vma=False,
    )
```

profile of v0, /device:TPU:0, one launch (start us, length us, event | category | flops | bytes accessed | tf_op | source)
XLA Modules:
  0.0 238.0 jit_solution(2345525448332055656)
XLA Ops:
  7.2 0.0 copy-start
  7.2 0.0 copy-start.2
  7.2 0.0 all-gather.2.cloned.1.call-start
  7.2 0.7 all-gather.2.cloned.1.call-update
  7.9 0.0 all-reduce.4.cloned.1.call-start
  8.0 1.0 copy.38
  9.0 1.0 copy.39
  10.1 4.5 %collective-permute-start.1 = (bf16[2,128,256]{1,2,0:T(8,128)(2,1)S(1)}, bf16[2,128,256]{1,2,0:T(8,128)(2,1)S(1)}, u32[]{:S(2)}, u32[]{:S(2)}) collective-permute-start(bf16[2,128,256]{1,2,0:T(8,128)(2,1)S(1)} %pad_maximum_fusion.2), channel_id=1, source_target_pairs={{1,0},{2,1},{3,2},{4,3},{5,4},{6,5},{7,6},{0,7},{9,8},{10,9},{11,1... | collective-permute-start | bytes 393224 | tf_op jit(solution)/shard_map/ppermute | solution.py:27
  14.6 0.0 collective-permute-start
  14.7 0.9 fusion.45
  15.6 0.0 all-reduce.4.cloned.1.call-update
  15.6 0.0 all-reduce.6.cloned.1.call-start
  15.7 0.0 copy-done.2
  15.7 0.1 copy.40
  15.9 1.2 collective-permute-done.1
  17.1 3.7 %collective-permute-done = bf16[2,128,256]{1,2,0:T(8,128)(2,1)S(1)} collective-permute-done((bf16[2,128,256]{1,2,0:T(8,128)(2,1)S(1)}, bf16[2,128,256]{1,2,0:T(8,128)(2,1)S(1)}, u32[]{:S(2)}, u32[]{:S(2)}) %collective-permute-start) | collective-permute-done | bytes 131104 | tf_op jit(solution)/shard_map/ppermute | solution.py:24
  20.8 0.1 pad_maximum_fusion
  20.9 0.0 copy-start.3
  20.9 0.4 fusion.44
  21.3 13.2 %all-gather.2.cloned.1.call-done = bf16[512,1024]{1,0:T(8,128)(2,1)} async-done(((bf16[64,1024]{1,0:T(8,128)(2,1)}), bf16[512,1024]{1,0:T(8,128)(2,1)}) %all-gather.2.cloned.1.call-update) | async-done | bytes 1048592 | tf_op jit(solution)/shard_map/all_gather | solution.py:92
  34.5 0.0 copy-done
  34.5 1.7 convolution_convert_fusion
  36.2 0.1 copy.85
  36.3 0.1 copy.84
  36.4 54.8 %all-reduce.4.cloned.1.call-done = f32[2,128,128]{2,1,0:T(8,128)} async-done(((f32[2,128,128]{2,1,0:T(8,128)}), f32[2,128,128]{2,1,0:T(8,128)}) %all-reduce.4.cloned.1.call-update) | async-done | bytes 131088 | tf_op jit(solution)/shard_map/psum | solution.py:82
  91.2 0.0 copy-done.3
  91.3 1.3 multiply_reduce_fusion.1
  92.6 0.1 multiply_convert_fusion
  92.7 1.1 fusion.33
  93.8 0.0 all-reduce.6.cloned.1.call-update
  93.8 0.0 reduce-scatter.2.cloned.1.call-start
  93.9 0.6 multiply_reduce_fusion.2
  94.4 0.0 copy-start.1
  94.5 1.8 fusion.19
  96.2 0.0 reduce-scatter.2.cloned.1.call-update
  96.2 0.0 all-reduce.8.cloned.1.call-start
  96.3 0.0 copy-done.1
  96.3 0.3 fusion.11
  96.7 0.1 copy.55
  96.8 0.3 fusion.8
  97.0 0.2 fusion.12
  97.2 0.1 copy.54
  97.4 0.2 fusion.3
  97.6 0.2 copy.58
  97.7 0.5 fusion.38
  98.3 0.1 collective-permute-start.2
  98.4 3.5 %collective-permute-start.3 = (f32[2,128,256]{1,2,0:T(8,128)S(1)}, f32[2,128,256]{1,2,0:T(8,128)S(1)}, u32[]{:S(2)}, u32[]{:S(2)}) collective-permute-start(f32[2,128,256]{1,2,0:T(8,128)S(1)} %get-tuple-element.11), channel_id=1, source_target_pairs={{0,7},{1,0},{2,1},{3,2},{4,3},{5,4},{6,5},{7,6},{8,15},{9,8},{10,9... | collective-permute-start | bytes 786440 | tf_op jit(solution)/shard_map/ppermute | solution.py:35
  101.9 0.7 pad_maximum_fusion.3
  102.6 45.7 %all-reduce.6.cloned.1.call-done = f32[2,128,128]{2,1,0:T(8,128)} async-done(((f32[2,128,128]{2,1,0:T(8,128)}), f32[2,128,128]{2,1,0:T(8,128)}) %all-reduce.6.cloned.1.call-update) | async-done | bytes 131088 | tf_op jit(solution)/shard_map/psum | solution.py:129
  148.3 1.3 convolution_convert_fusion.2
  149.6 1.1 fusion.13
  150.7 0.0 collective-permute-done.2
  150.7 0.0 collective-permute-done.3
  150.8 34.5 %reduce-scatter.2.cloned.1.call-done = f32[64,1024]{1,0:T(8,128)} async-done(((f32[512,1024]{1,0:T(8,128)}), f32[64,1024]{1,0:T(8,128)}) %reduce-scatter.2.cloned.1.call-update) | async-done | bytes 262160 | tf_op jit(solution)/shard_map/reduce_scatter | solution.py:99
  185.3 0.0 all-reduce.8.cloned.1.call-update
  185.3 0.8 copy.66
  186.1 0.8 copy.65
  186.9 42.9 %all-reduce.8.cloned.1.call-done = f32[64,1024]{1,0:T(8,128)} async-done(((f32[64,1024]{1,0:T(8,128)}), f32[64,1024]{1,0:T(8,128)}) %all-reduce.8.cloned.1.call-update) | async-done | bytes 262160 | tf_op jit(solution)/shard_map/psum | solution.py:107
  229.8 1.7 broadcast_multiply_fusion
  (16 shorter events, 0.3 us)
Async XLA Ops:
  7.2 27.3 %copy-start = (bf16[1,128,1024]{2,1,0:T(8,128)(2,1)S(1)}, bf16[1,128,1024]{2,1,0:T(8,128)(2,1)}, u32[]{:S(2)}) copy-start(bf16[1,128,1024]{2,1,0:T(8,128)(2,1)} %param.9) | copy-start | bytes 786436
  7.2 8.5 %copy-start.2 = (bf16[1,128,512]{2,1,0:T(8,128)(2,1)S(1)}, bf16[1,128,512]{2,1,0:T(8,128)(2,1)}, u32[]{:S(2)}) copy-start(bf16[1,128,512]{2,1,0:T(8,128)(2,1)} %param.6) | copy-start | bytes 393220
  7.2 27.3 %all-gather.2.cloned.1.call-start = ((), (), s32[]{:S(2)}) async-start(), calls=%async_computation.1 | async-start | bytes 1179648 | tf_op jit(solution)/shard_map/all_gather | solution.py:92
  7.9 83.3 %all-reduce.4.cloned.1.call-start = ((), (), s32[]{:S(2)}) async-start(), calls=%async_computation.2 | async-start | bytes 262144 | tf_op jit(solution)/shard_map/psum | solution.py:82
  10.1 7.1 %collective-permute-start.1 = (bf16[2,128,256]{1,2,0:T(8,128)(2,1)S(1)}, bf16[2,128,256]{1,2,0:T(8,128)(2,1)S(1)}, u32[]{:S(2)}, u32[]{:S(2)}) collective-permute-start(bf16[2,128,256]{1,2,0:T(8,128)(2,1)S(1)} %pad_maximum_fusion.2), channel_id=1, source_target_pairs={{1,0},{2,1},{3,2},{4,3},{5,4},{6,5},{7,6},{0,7},{9,8},{10,9},{11,1... | collective-permute-start | bytes 393224 | tf_op jit(solution)/shard_map/ppermute | solution.py:27
  14.6 6.2 %collective-permute-start = (bf16[2,128,256]{1,2,0:T(8,128)(2,1)S(1)}, bf16[2,128,256]{1,2,0:T(8,128)(2,1)S(1)}, u32[]{:S(2)}, u32[]{:S(2)}) collective-permute-start(bf16[2,128,256]{1,2,0:T(8,128)(2,1)S(1)} %pad_maximum_fusion.2), channel_id=1, source_target_pairs={{0,1},{1,2},{2,3},{3,4},{4,5},{5,6},{6,7},{7,0},{8,9},{9,10},{10,1... | collective-permute-start | bytes 393224 | tf_op jit(solution)/shard_map/ppermute | solution.py:24
  15.6 132.7 %all-reduce.6.cloned.1.call-start = ((), (), s32[]{:S(2)}) async-start(), calls=%async_computation.3 | async-start | bytes 262144 | tf_op jit(solution)/shard_map/psum | solution.py:129
  20.9 70.4 %copy-start.3 = (f32[256]{0:T(256)S(1)}, f32[256]{0:T(256)}, u32[]{:S(2)}) copy-start(f32[256]{0:T(256)} %param.11) | copy-start | bytes 3076
  93.8 91.4 %reduce-scatter.2.cloned.1.call-start = ((), (), s32[]{:S(2)}) async-start(), calls=%async_computation.4 | async-start | bytes 2359296 | tf_op jit(solution)/shard_map/reduce_scatter | solution.py:99
  94.4 1.8 copy-start.1
  96.2 133.5 %all-reduce.8.cloned.1.call-start = ((), (), s32[]{:S(2)}) async-start(), calls=%async_computation.5 | async-start | bytes 524288 | tf_op jit(solution)/shard_map/psum | solution.py:107
  98.3 52.4 %collective-permute-start.2 = (f32[2,128,256]{1,2,0:T(8,128)S(1)}, f32[2,128,256]{1,2,0:T(8,128)S(1)}, u32[]{:S(2)}, u32[]{:S(2)}) collective-permute-start(f32[2,128,256]{1,2,0:T(8,128)S(1)} %get-tuple-element.10), channel_id=1, source_target_pairs={{0,1},{1,2},{2,3},{3,4},{4,5},{5,6},{6,7},{7,0},{8,9},{9,10},{10,1... | collective-permute-start | bytes 786440 | tf_op jit(solution)/shard_map/ppermute | solution.py:35
  98.4 52.3 %collective-permute-start.3 = (f32[2,128,256]{1,2,0:T(8,128)S(1)}, f32[2,128,256]{1,2,0:T(8,128)S(1)}, u32[]{:S(2)}, u32[]{:S(2)}) collective-permute-start(f32[2,128,256]{1,2,0:T(8,128)S(1)} %get-tuple-element.11), channel_id=1, source_target_pairs={{0,7},{1,0},{2,1},{3,2},{4,3},{5,4},{6,5},{7,6},{8,15},{9,8},{10,9... | collective-permute-start | bytes 786440 | tf_op jit(solution)/shard_map/ppermute | solution.py:35
Sparse Core Ops, SparseCore 0:
  9.6 24.8 all-gather.1
  37.4 53.8 all-reduce.3
  94.2 54.0 all-reduce.5
  150.5 34.7 reduce-scatter.1
  188.0 41.6 all-reduce.7
where the time goes:
time: 238 us
  waiting for transfers between devices  197 us (83%)
  between operations  14.1 us (6%)
  matrix products  11.7 us (5%)
  starting transfers between devices  8.33 us (4%)
  local copies, waits for them, and re-layouts  4.38 us (2%)
  other arithmetic  2.76 us (1%)
    psum x1, waiting for transfers between devices, body(): lin_state = lax.psum(state_term, 'seq')  54.8 us
    psum x1, waiting for transfers between devices, body(): dstate = lax.psum(dstate_term, 'seq')  45.7 us
    psum x1, waiting for transfers between devices, body(): summed = lax.psum(local_term, 'dp')  42.9 us
    reduce_scatter x1, waiting for transfers between devices, body(): lax.psum_scatter(lax.dot_general(attn, grad_out, (((0,), (0,)), ((), ()))...  34.5 us
    all_gather x1, waiting for transfers between devices, body(): lax.all_gather(out_weight, 'seq', axis=0, tiled=True)  13.2 us
  transfers between devices with their start and end apart: 9, of which 7 were waited for; matrix products, arithmetic and copies ran while one was open for 6% of the time, Pallas kernels for 0%

commit v1 on v0

v1 whole, which is shorter than its diff:
```python
import functools
import math

import jax
import jax.numpy as jnp
from jax import lax
from jax.experimental import pallas as pl
from jax.experimental.pallas import tpu as pltpu
from jax.sharding import PartitionSpec as P

DH = 128
SOFT_HEADS = 2
LIN_HEADS = 2
HEADS = SOFT_HEADS + LIN_HEADS
WINDOW = 256
HALF = 128
norm_eps = 1e-06
FACTOR = DH ** (-0.5)
BF = jnp.bfloat16
F32 = jnp.float32
NN = (((1,), (0,)), ((), ()))
NT = (((1,), (1,)), ((), ()))
TN = (((0,), (0,)), ((), ()))


def unit_plus(values):
    return jnp.where(values > 0, values + 1.0, jnp.exp(jnp.minimum(values, 0.0)))


def unit_slope(values):
    return jnp.where(values > 0, 1.0, jnp.exp(jnp.minimum(values, 0.0)))


def mm(a, b, dims=NN):
    return lax.dot_general(a, b, dims, preferred_element_type=F32)


def halves(x):
    high = x.astype(BF)
    return high, (x - high.astype(F32)).astype(BF)


def mm3(a, b, dims=NN):
    a_high, a_low = halves(a)
    b_high, b_low = halves(b)
    return mm(a_high, b_high, dims) + (mm(a_high, b_low, dims) + mm(a_low, b_high, dims))


def mm2(a, b, dims=NN):
    a_high, a_low = halves(a)
    return mm(a_high, b, dims) + mm(a_low, b, dims)


def at(start, size=DH):
    return pl.ds(pl.multiple_of(start, size), size)


def places():
    seq = lax.axis_index("seq")
    return lax.rem(seq, 2), lax.div(seq, 2), lax.axis_index("dp")


def call(kernel, name, outs, args, scratch=(), flops=0):
    vmem = pl.BlockSpec(memory_space=pltpu.VMEM)
    size = sum(math.prod(x.shape) * x.dtype.itemsize for x in list(args) + list(outs))
    return pl.pallas_call(
        kernel,
        name=name,
        out_shape=list(outs),
        in_specs=[vmem] * len(args),
        out_specs=[vmem] * len(outs),
        scratch_shapes=list(scratch),
        compiler_params=pltpu.CompilerParams(vmem_limit_bytes=24 * 2**20),
        cost_estimate=pl.CostEstimate(flops=flops, bytes_accessed=size, transcendentals=0),
    )(*args)


def like(shape, dtype):
    return jax.ShapeDtypeStruct(shape, dtype)


def pack_kernel(q, k, v, lin_other, mixed_other, kv_other, kv_mine):
    core, _, _ = places()
    mine, other = core * DH, (1 - core) * DH
    soft = SOFT_HEADS * DH
    lin_other[:, :DH] = k[:, at(soft + other)]
    lin_other[:, DH:] = v[:, at(soft + other)]
    mixed_other[:, :DH] = q[:, at(other)]
    mixed_other[:, DH : 2 * DH] = q[:, at(soft + other)]
    mixed_other[:, 2 * DH : 3 * DH] = k[:, at(other)]
    mixed_other[:, 3 * DH :] = v[:, at(other)]
    kv_other[:, :DH] = k[:, at(other)]
    kv_other[:, DH:] = v[:, at(other)]
    kv_mine[:, :DH] = k[:, at(mine)]
    kv_mine[:, DH:] = v[:, at(mine)]


def state_kernel(k, v, lin_recv, state, state_low):
    core, _, _ = places()
    mine = SOFT_HEADS * DH + core * DH
    own = mm2(unit_plus(k[:, at(mine)].astype(F32)), v[:, at(mine)], TN)
    far = mm2(unit_plus(lin_recv[:, :DH].astype(F32)), lin_recv[:, DH:], TN)
    total = own + far
    state[...] = total
    state_low[...] = total.astype(BF)


def soft_forward_kernel(
    q, k, v, og, mixed, og_recv, near, far,
    qs, ks, vs, ogs, probs, attn, *wg,
):
    core, _, dp = places()
    rows = q.shape[0]
    mine = core * DH
    own, pair = core * rows, (1 - core) * rows
    qs[at(own, rows), :] = q[:, at(mine)]
    qs[at(pair, rows), :] = mixed[:, :DH]
    ks[at(HALF + own), :] = k[:, at(mine)]
    vs[at(HALF + own), :] = v[:, at(mine)]
    ks[at(HALF + pair), :] = mixed[:, 2 * DH : 3 * DH]
    vs[at(HALF + pair), :] = mixed[:, 3 * DH :]
    near_at, far_at = core * (HALF + 2 * rows), (1 - core) * (HALF + 2 * rows)
    ks[at(near_at), :] = near[:, :DH]
    vs[at(near_at), :] = near[:, DH:]
    ks[at(far_at), :] = far[:, :DH]
    vs[at(far_at), :] = far[:, DH:]
    ogs[at(own, rows), :] = og[...]
    ogs[at(pair, rows), :] = og_recv[...]
    span = rows + 2 * HALF
    row_pos = lax.broadcasted_iota(jnp.int32, (rows, span), 0)
    col_pos = lax.broadcasted_iota(jnp.int32, (rows, span), 1)
    inside = (col_pos >= row_pos) & (col_pos < row_pos + WINDOW)
    for block in range(2):
        first = block * rows
        scores = mm(qs[first : first + rows, :], ks[first : first + span, :], NT) * FACTOR
        scores = jnp.where(inside, scores, -1e30)
        peak = jnp.max(scores, axis=1, keepdims=True)
        terms = jnp.where(inside, jnp.exp(scores - peak), 0.0)
        share = terms / jnp.sum(terms, axis=1, keepdims=True)
        probs[block] = share
        attn[first : first + rows, :] = mm(share.astype(BF), vs[first : first + span, :]).astype(BF)
    weight_parts(attn[...], ogs, dp, wg)


def weight_parts(attn, ogs, dp, outs):
    if len(outs) == 1:
        outs[0][...] = mm(attn, ogs[...], TN)
        return
    width = ogs.shape[1] // len(outs)
    for step, out in enumerate(outs):
        part = mm(attn, ogs[:, at((dp ^ step) * width, width)], TN)
        out[...] = part.astype(out.dtype)


def lin_forward_kernel(count, state, *refs):
    others = refs[:count]
    q, mixed, ogs, gain, u_out, total_out = refs[count : count + 6]
    wg = refs[count + 6 :]
    core, _, dp = places()
    total = state[...]
    for other in others:
        total = total + other[...].astype(F32)
    total_out[...] = total
    rows = q.shape[0]
    own, pair = core * rows, (1 - core) * rows
    mine = SOFT_HEADS * DH + core * DH
    u_out[at(own, rows), :] = mm3(unit_plus(q[:, at(mine)].astype(F32)), total)
    u_out[at(pair, rows), :] = mm3(unit_plus(mixed[:, DH : 2 * DH].astype(F32)), total)
    u = u_out[...]
    r = lax.rsqrt(jnp.mean(u * u, axis=1, keepdims=True) + norm_eps)
    attn = (gain[pl.ds(core, 1), :] * u * r).astype(BF)
    weight_parts(attn, ogs, dp, wg)


def dattn_kernel(count, *refs):
    ogs, out, weights = refs[count : count + 3]
    core, z, dp = places()
    if count == 1:
        weights[...] = refs[0][...]
    else:
        for step in range(count):
            parts, rows, width = refs[step].shape
            for index in range(parts):
                weights[at((z ^ index) * rows, rows), at((dp ^ step) * width, width)] = refs[step][index]
    out[...] = mm(ogs[...], weights[...], NT)


def lin_backward_kernel(
    u, total, dattn, q, mixed, gain, dq_own, dq_pair, dstate, dstate_low, grads
):
    core, _, _ = places()
    rows = q.shape[0]
    mine = SOFT_HEADS * DH + core * DH
    u_all = u[...]
    r = lax.rsqrt(jnp.mean(u_all * u_all, axis=1, keepdims=True) + norm_eps)
    lin_grad = gain[pl.ds(core, 1), :] * dattn[:, DH:]
    grad_u = r * lin_grad - u_all * (r * r * r) * jnp.mean(lin_grad * u_all, axis=1, keepdims=True)
    grads[...] = grad_u
    total_state = total[...]
    result = jnp.zeros(dstate.shape, F32)
    own, pair = core * rows, (1 - core) * rows
    for first, values, out in (
        (own, q[:, at(mine)], dq_own),
        (pair, mixed[:, DH : 2 * DH], dq_pair),
    ):
        wide = values.astype(F32)
        part = grads[at(first, rows), :]
        result = result + mm3(unit_plus(wide), part, TN)
        out[...] = (mm3(part, total_state, NT) * unit_slope(wide)).astype(BF)
    dstate[...] = result
    dstate_low[...] = result.astype(BF)


def soft_backward_kernel(
    qs, ks, vs, probs, attn, dattn, dq_own, dk_own, dv_own, to_pair, to_near, to_far,
    dq_all, dk_all, dv_all,
):
    core, _, _ = places()
    rows = qs.shape[0] // 2
    span = rows + 2 * HALF
    dk_all[...] = jnp.zeros_like(dk_all)
    dv_all[...] = jnp.zeros_like(dv_all)
    for block in range(2):
        first = block * rows
        here, window = slice(first, first + rows), slice(first, first + span)
        grad = dattn[here, :DH].astype(BF)
        share = probs[block]
        delta = jnp.sum(grad.astype(F32) * attn[here, :].astype(F32), axis=1, keepdims=True)
        dscore = (share * (mm(grad, vs[window, :], NT) - delta)).astype(BF)
        dq_all[here, :] = mm(dscore, ks[window, :]) * FACTOR
        dk_all[window, :] += mm(dscore, qs[here, :], TN) * FACTOR
        dv_all[window, :] += mm(share.astype(BF), grad, TN)
    own, pair = core * rows, (1 - core) * rows
    near_at, far_at = core * (HALF + 2 * rows), (1 - core) * (HALF + 2 * rows)
    dq_own[...] = dq_all[at(own, rows), :].astype(BF)
    dk_own[...] = dk_all[at(HALF + own), :]
    dv_own[...] = dv_all[at(HALF + own), :]
    to_pair[:, :DH] = dq_all[at(pair, rows), :].astype(BF)
    to_pair[:, DH : 2 * DH] = dk_all[at(HALF + pair), :].astype(BF)
    to_pair[:, 2 * DH :] = dv_all[at(HALF + pair), :].astype(BF)
    to_near[:, :DH] = dk_all[at(near_at), :].astype(BF)
    to_near[:, DH:] = dv_all[at(near_at), :].astype(BF)
    to_far[:, :DH] = dk_all[at(far_at), :].astype(BF)
    to_far[:, DH:] = dv_all[at(far_at), :].astype(BF)


def lin_final_kernel(count, dstate, *refs):
    others = refs[:count]
    k, v, lin_recv, own_out, pair_out = refs[count:]
    core, _, _ = places()
    total = dstate[...]
    for other in others:
        total = total + other[...].astype(F32)
    mine = SOFT_HEADS * DH + core * DH
    for keys, values, out in (
        (k[:, at(mine)], v[:, at(mine)], own_out),
        (lin_recv[:, :DH], lin_recv[:, DH:], pair_out),
    ):
        wide = keys.astype(F32)
        high, low = halves(total)
        dk = mm(values, high, NT) + mm(values, low, NT)
        out[:, :DH] = (dk * unit_slope(wide)).astype(BF)
        out[:, DH:] = mm3(unit_plus(wide), total).astype(BF)


def output_kernel(
    dq_soft, dk_soft, dv_soft, dq_lin, lin_own, soft_pair, dq_pair, lin_pair, near, far,
    dq, dk, dv,
):
    core, _, _ = places()
    soft = SOFT_HEADS * DH
    mine, other = core * DH, (1 - core) * DH
    dq[0, :, at(mine)] = dq_soft[...]
    dq[0, :, at(other)] = soft_pair[:, :DH]
    dq[0, :, at(soft + mine)] = dq_lin[...]
    dq[0, :, at(soft + other)] = dq_pair[...]
    for out, own, first in ((dk, dk_soft, 0), (dv, dv_soft, DH)):
        cols = slice(first, first + DH)
        out[0, :, at(mine)] = (own[...] + far[:, cols].astype(F32)).astype(BF)
        out[0, :, at(other)] = (
            soft_pair[:, DH + first : 2 * DH + first].astype(F32) + near[:, cols].astype(F32)
        ).astype(BF)
        out[0, :, at(soft + mine)] = lin_own[:, cols]
        out[0, :, at(soft + other)] = lin_pair[:, cols]


def weight_rows_kernel(count, *refs):
    outs = refs[2 * count : 3 * count]
    sums = refs[3 * count]
    _, z, _ = places()
    rows = outs[0].shape[0]
    for group in range(2):
        total = refs[group * count][...]
        for other in refs[group * count + 1 : (group + 1) * count]:
            total = total + other[...].astype(F32)
        for half in range(2):
            sums[2 * group + half] = total[half * rows : (half + 1) * rows]
    for step, out in enumerate(outs):
        out[...] = sums[z ^ step].astype(out.dtype)


def weight_sum_kernel(scale, *refs):
    total = refs[0][...].astype(F32)
    for other in refs[1:-1]:
        total = total + other[...].astype(F32)
    refs[-1][...] = total * scale


def weight_join_kernel(*refs):
    _, _, dp = places()
    out = refs[-1]
    width = refs[0].shape[1]
    for step, part in enumerate(refs[:-1]):
        out[:, at((dp ^ step) * width, width)] = part[...].astype(F32)


def body(n_dp, n_seq, queries, key_rows, value_rows, out_grad, out_weight, norm_gain):
    q, k, v, og = queries[0], key_rows[0], value_rows[0], out_grad[0]
    rows, model = og.shape
    chips = n_seq // 2
    every = range(n_seq)
    pair = [(s, s ^ 1) for s in every]
    to_near = [(s, (s + 1) % n_seq if s % 2 else (s - 1) % n_seq) for s in every]
    to_far = [(s, (s + 2) % n_seq if s % 2 else (s - 2) % n_seq) for s in every]
    from_far = [(target, source) for source, target in to_far]
    core = lax.axis_index("seq") % 2
    direct = chips == HEADS and n_dp == 4
    count = n_dp if direct else 1
    move = functools.partial(lax.ppermute, axis_name="seq")

    def over_chips(low, wide):
        if direct:
            return [
                move(low, perm=[(s, s ^ (2 * step)) for s in every]) for step in range(1, chips)
            ]
        slots = jnp.stack([jnp.where(core == head, wide, 0.0) for head in range(2)])
        total = lax.psum(slots, "seq")
        return [jnp.where(core == 0, total[0], total[1]) - wide]

    def over_dp(value):
        return [
            lax.ppermute(value if not isinstance(value, list) else value[step], "dp",
                         [(d, d ^ step) for d in range(n_dp)])
            for step in range(1, n_dp)
        ]

    og_recv = move(og, perm=pair)
    if direct:
        width = model // n_dp
        w_part = lax.dynamic_slice_in_dim(out_weight, lax.axis_index("dp") * width, width, axis=1)
        w_got = []
        for step in range(chips):
            perm = []
            for s in every:
                z, b = s // 2, s % 2
                perm.append((s, 2 * (((z // 2) * 2 + b) ^ step) + z % 2))
            w_got.append(move(w_part, perm=perm))
        w_mine = jnp.stack(w_got)
        weights = [w_mine] + over_dp(w_mine)
    else:
        w_all = lax.all_gather(out_weight, "seq", axis=0, tiled=True).reshape(2, 2, DH, model)
        weights = [jnp.where(core == 0, w_all[:, 0], w_all[:, 1]).reshape(2 * DH, model)]

    lin_other, mixed_other, kv_other, kv_mine = call(
        pack_kernel, "pack",
        [like((rows, 2 * DH), BF), like((rows, 4 * DH), BF), like((rows, 2 * DH), BF), like((rows, 2 * DH), BF)],
        [q, k, v],
    )
    lin_recv = move(lin_other, perm=pair)
    near = move(kv_other, perm=to_near)
    far = move(kv_mine, perm=to_far)
    mixed = move(mixed_other, perm=pair)

    state, state_low = call(
        state_kernel, "state", [like((DH, DH), F32), like((DH, DH), BF)], [k, v, lin_recv],
        flops=4 * 2 * rows * DH * DH,
    )
    state_others = over_chips(state_low, state)

    span = 2 * rows + 2 * HALF
    part = model // count
    wg_shapes = [like((DH, part), F32)] + [like((DH, part), BF)] * (count - 1)
    wg_flops = 2 * 2 * rows * DH * model
    qs, ks, vs, ogs, probs, attn, *wg_soft = call(
        soft_forward_kernel, "soft_forward",
        [
            like((2 * rows, DH), BF), like((span, DH), BF), like((span, DH), BF),
            like((2 * rows, model), BF), like((2, rows, rows + 2 * HALF), F32), like((2 * rows, DH), BF),
        ] + wg_shapes,
        [q, k, v, og, mixed, og_recv, near, far],
        flops=wg_flops,
    )
    gain = norm_gain.reshape(LIN_HEADS, DH)
    u, total, *wg_lin = call(
        functools.partial(lin_forward_kernel, len(state_others)), "lin_forward",
        [like((2 * rows, DH), F32), like((DH, DH), F32)] + wg_shapes,
        [state] + state_others + [q, mixed, ogs, gain],
        flops=wg_flops,
    )
    dattn = call(
        functools.partial(dattn_kernel, count), "d_attn", [like((2 * rows, 2 * DH), F32)],
        weights + [ogs], scratch=[pltpu.VMEM((2 * DH, model), BF)],
        flops=2 * wg_flops,
    )[0]
    if direct:
        wg_soft = wg_soft[:1] + over_dp(wg_soft)
        wg_lin = wg_lin[:1] + over_dp(wg_lin)

    dq_lin, dq_lin_pair, dstate, dstate_low = call(
        lin_backward_kernel, "lin_backward",
        [like((rows, DH), BF), like((rows, DH), BF), like((DH, DH), F32), like((DH, DH), BF)],
        [u, total, dattn, q, mixed, gain],
        scratch=[pltpu.VMEM((2 * rows, DH), F32)],
        flops=wg_flops,
    )
    dstate_others = over_chips(dstate_low, dstate)
    dq_soft, dk_soft, dv_soft, soft_pair, back_near, back_far = call(
        soft_backward_kernel, "soft_backward",
        [
            like((rows, DH), BF), like((rows, DH), F32), like((rows, DH), F32),
            like((rows, 3 * DH), BF), like((rows, 2 * DH), BF), like((rows, 2 * DH), BF),
        ],
        [qs, ks, vs, probs, attn, dattn],
        scratch=[pltpu.VMEM((2 * rows, DH), F32), pltpu.VMEM((span, DH), F32), pltpu.VMEM((span, DH), F32)],
        flops=wg_flops,
    )
    dq_lin_pair = move(dq_lin_pair, perm=pair)
    soft_pair = move(soft_pair, perm=pair)
    back_near = move(back_near, perm=to_near)
    back_far = move(back_far, perm=from_far)

    scale = 1.0 / math.sqrt(n_dp * n_seq * rows)
    if direct:
        pieces = call(
            functools.partial(weight_rows_kernel, count), "weight_rows",
            [like((DH // 2, part), BF)] * chips,
            list(wg_soft) + list(wg_lin),
            scratch=[pltpu.VMEM((chips, DH // 2, part), F32)],
        )
        got = []
        for step in range(chips):
            perm = []
            for s in every:
                m = (s // 2) ^ step
                perm.append((s, 2 * (2 * (m // 2) + s % 2) + m % 2))
            got.append(move(pieces[step], perm=perm))
        summed = call(
            functools.partial(weight_sum_kernel, scale), "weight_sum", [like((DH // 2, part), F32)], got
        )[0]
        weight_grad = call(
            weight_join_kernel, "weight_join", [like((DH // 2, model), F32)], [summed] + over_dp(summed)
        )[0]
    else:
        groups = jnp.stack([wg_soft[0], wg_lin[0]])
        slots = jnp.stack([jnp.where(core == head, groups, 0.0) for head in range(2)], axis=1)
        local = lax.psum_scatter(
            slots.reshape(HEADS * DH, model), "seq", scatter_dimension=0, tiled=True
        )
        weight_grad = lax.psum(local, "dp") * scale

    lin_own, lin_pair = call(
        functools.partial(lin_final_kernel, len(dstate_others)), "lin_final",
        [like((rows, 2 * DH), BF), like((rows, 2 * DH), BF)],
        [dstate] + dstate_others + [k, v, lin_recv],
        flops=wg_flops // 4,
    )
    lin_pair = move(lin_pair, perm=pair)
    shape = like((1, rows, HEADS * DH), BF)
    dq, dk, dv = call(
        output_kernel, "outputs", [shape] * 3,
        [dq_soft, dk_soft, dv_soft, dq_lin, lin_own, soft_pair, dq_lin_pair, lin_pair, back_near, back_far],
    )
    return dq, dk, dv, weight_grad


def solution(mesh):
    return jax.shard_map(
        functools.partial(body, mesh.shape["dp"], mesh.shape["seq"]),
        mesh=mesh,
        in_specs=(
            P("dp", "seq", None),
            P("dp", "seq", None),
            P("dp", "seq", None),
            P("dp", "seq", None),
            P("seq", None),
            P(),
        ),
        out_specs=(
            P("dp", "seq", None),
            P("dp", "seq", None),
            P("dp", "seq", None),
            P("seq", None),
        ),
        check_vma=False,
    )
```

time: 238 us -> 69.6 us (0.29)
  waiting for transfers between devices: 197 us -> 13.1 us
  starting transfers between devices: 8.33 us -> 46.1 us
  between operations: 14.1 us -> 0.89 us
  matrix products: 11.7 us -> 0 us
  Pallas kernels: 0 us -> 5.53 us
  other arithmetic: 2.76 us -> 0.02 us
    psum x3 -> x0, waiting for transfers between devices: 143 us -> none  [the longest x1 54.8 us: body(): lin_state = lax.psum(state_term, 'seq')]
    ppermute x4 -> x36, starting transfers between devices: 8.13 us -> 46.1 us  [the longest x12 14.9 us: over_dp(): lax.ppermute(value if not isinstance(value, list) else value[step], 'dp',...]
    reduce_scatter x1 -> x0, waiting for transfers between devices: 34.5 us -> none  [body(): lax.psum_scatter(lax.dot_general(attn, grad_out, (((0,), (0,)), ((), ()))...]
    all_gather x1 -> x0, waiting for transfers between devices: 13.2 us -> none  [body(): lax.all_gather(out_weight, 'seq', axis=0, tiled=True)]
    dot_general x13 -> x0, matrix products: 11.3 us -> none  [the longest x1 1.76 us: body(): lax.dot_general(attn, grad_out, (((0,), (0,)), ((), ())), preferred_eleme...]
    ppermute x4 -> x36, waiting for transfers between devices: 4.89 us -> 13.1 us  [the longest x6 3.55 us: over_chips(): move(low, perm=[(s, s ^ 2 * step) for s in every])]
    pallas_call x0 -> x12, Pallas kernels: none -> 5.53 us  [call(): pl.pallas_call(kernel, name=name, out_shape=list(outs), in_specs=[vmem] *...]
  transfers between devices with their start and end apart: 9 -> 36, of which waited for: 7 -> 7; matrix products, arithmetic and copies ran while one was open for 6% -> 0% of each run, Pallas kernels for 0% -> 7%
where the time goes in v1:
time: 69.6 us; the launch traced here: 69.4 us
  starting transfers between devices  46.1 us (66%)
  waiting for transfers between devices  13.1 us (19%)
  Pallas kernels  5.53 us (8%)
  local copies, waits for them, and re-layouts  3.79 us (5%)
  between operations  0.89 us (1%)
    ppermute x12, starting transfers between devices, over_dp(): lax.ppermute(value if not isinstance(value, list) else value[step], 'dp',...  14.9 us
    ppermute x6, starting transfers between devices, over_chips(): move(low, perm=[(s, s ^ 2 * step) for s in every])  9.83 us
    ppermute x4, starting transfers between devices, body(): w_got.append(move(w_part, perm=perm))  5.71 us
    pallas_call x12, Pallas kernels, call(): pl.pallas_call(kernel, name=name, out_shape=list(outs), in_specs=[vmem] *...  5.53 us
    ppermute x4, starting transfers between devices, body(): got.append(move(pieces[step], perm=perm))  5.33 us
    ppermute x1, starting transfers between devices, body(): near = move(kv_other, perm=to_near)  4.09 us
    unnamed x16, local copies, waits for them, and re-layouts  3.79 us
    ppermute x6, waiting for transfers between devices, over_chips(): move(low, perm=[(s, s ^ 2 * step) for s in every])  3.55 us
  transfers between devices with their start and end apart: 36, of which 7 were waited for; matrix products, arithmetic and copies ran while one was open for 0% of the time, Pallas kernels for 7%

profile of v1, /device:TPU:0, one launch (start us, length us, event | category | flops | bytes accessed | tf_op | source)
XLA Modules:
  0.0 69.4 jit_solution(17548690615630213781)
XLA Ops:
  0.6 0.0 copy-start
  0.6 0.5 collective-permute-start.1
  1.2 0.4 copy-done
  1.5 5.0 %collective-permute-start.7 = (bf16[64,256]{1,0:T(8,128)(2,1)S(1)}, bf16[64,256]{1,0:T(8,128)(2,1)S(1)}, u32[]{:S(2)}, u32[]{:S(2)}) collective-permute-start(bf16[64,256]{1,0:T(8,128)(2,1)S(1)} %constant_dynamic-slice_fusion), channel_id=1, source_target_pairs={{0,6},{1,4},{2,7},{3,5},{4,2},{5,0},{6,3},{7,1},{8,14},{9,12},{10,... | collective-permute-start | bytes 98312 | tf_op jit(solution)/shard_map/ppermute | solution.py:357
  6.6 0.0 collective-permute-start.5
  6.6 0.7 collective-permute-start.4
  7.3 0.0 copy-start.1
  7.3 0.9 %copy-done.1 = bf16[1,128,512]{2,1,0:T(8,128)(2,1)S(1)} copy-done((bf16[1,128,512]{2,1,0:T(8,128)(2,1)S(1)}, bf16[1,128,512]{2,1,0:T(8,128)(2,1)}, u32[]{:S(2)}) %copy-start.1) | copy-done | bytes 131096
  8.2 0.9 %copy-done.3 = bf16[1,128,512]{2,1,0:T(8,128)(2,1)S(1)} copy-done((bf16[1,128,512]{2,1,0:T(8,128)(2,1)S(1)}, bf16[1,128,512]{2,1,0:T(8,128)(2,1)}, u32[]{:S(2)}) %copy-start.3) | copy-done | bytes 131096
  9.1 0.9 %copy-done.5 = bf16[1,128,512]{2,1,0:T(8,128)(2,1)S(1)} copy-done((bf16[1,128,512]{2,1,0:T(8,128)(2,1)S(1)}, bf16[1,128,512]{2,1,0:T(8,128)(2,1)}, u32[]{:S(2)}) %copy-start.5) | copy-done | bytes 131096
  10.0 0.1 pack.1
  10.0 1.8 %collective-permute-start = (bf16[128,512]{1,0:T(8,128)(2,1)S(1)}, bf16[128,512]{1,0:T(8,128)(2,1)S(1)}, u32[]{:S(2)}, u32[]{:S(2)}) collective-permute-start(bf16[128,512]{1,0:T(8,128)(2,1)S(1)} %get-tuple-element.45), channel_id=1, source_target_pairs={{0,1},{1,0},{2,3},{3,2},{4,5},{5,4},{6,7},{7,6},{8,9},{9,8},{10,11... | collective-permute-start | bytes 393224 | tf_op jit(solution)/shard_map/ppermute | solution.py:372
  11.9 4.1 %collective-permute-start.2 = (bf16[128,256]{1,0:T(8,128)(2,1)S(1)}, bf16[128,256]{1,0:T(8,128)(2,1)S(1)}, u32[]{:S(2)}, u32[]{:S(2)}) collective-permute-start(bf16[128,256]{1,0:T(8,128)(2,1)S(1)} %get-tuple-element.46), channel_id=1, source_target_pairs={{0,7},{1,2},{2,1},{3,4},{4,3},{5,6},{6,5},{7,0},{8,15},{9,10},{10,... | collective-permute-start | bytes 196616 | tf_op jit(solution)/shard_map/ppermute | solution.py:370
  16.0 0.0 collective-permute-done.5
  16.0 0.0 collective-permute-start.3
  16.0 0.0 collective-permute-start.11
  16.1 0.0 copy-start.2
  16.1 0.0 copy-start.4
  16.1 0.0 copy-start.6
  16.1 2.2 %collective-permute-done.2.near = bf16[128,256]{1,0:T(8,128)(2,1)S(1)} collective-permute-done((bf16[128,256]{1,0:T(8,128)(2,1)S(1)}, bf16[128,256]{1,0:T(8,128)(2,1)S(1)}, u32[]{:S(2)}, u32[]{:S(2)}) %collective-permute-start.2) | collective-permute-done | bytes 65568 | tf_op jit(solution)/shard_map/ppermute | solution.py:370
  18.4 1.5 %collective-permute-start.8 = (bf16[4,64,256]{2,1,0:T(8,128)(2,1)S(1)}, bf16[4,64,256]{2,1,0:T(8,128)(2,1)S(1)}, u32[]{:S(2)}, u32[]{:S(2)}) collective-permute-start(bf16[4,64,256]{2,1,0:T(8,128)(2,1)S(1)} %pad_maximum_fusion.refs_0_), channel_id=1, source_target_pairs={{0,8},{8,0},{16,24},{24,16},{1,9},{9,1},{17,25},{25,17},{2,10},{10... | collective-permute-start | bytes 393224 | tf_op jit(solution)/shard_map/ppermute | solution.py:342
  19.8 0.5 collective-permute-done.3.far
  20.3 1.5 %collective-permute-start.9 = (bf16[4,64,256]{2,1,0:T(8,128)(2,1)S(1)}, bf16[4,64,256]{2,1,0:T(8,128)(2,1)S(1)}, u32[]{:S(2)}, u32[]{:S(2)}) collective-permute-start(bf16[4,64,256]{2,1,0:T(8,128)(2,1)S(1)} %pad_maximum_fusion.refs_0_), channel_id=1, source_target_pairs={{0,16},{8,24},{16,0},{24,8},{1,17},{9,25},{17,1},{25,9},{2,18},{10... | collective-permute-start | bytes 393224 | tf_op jit(solution)/shard_map/ppermute | solution.py:342
  21.9 0.0 collective-permute-done.11.lin_recv.refs_5_
  21.9 1.4 %collective-permute-start.10 = (bf16[4,64,256]{2,1,0:T(8,128)(2,1)S(1)}, bf16[4,64,256]{2,1,0:T(8,128)(2,1)S(1)}, u32[]{:S(2)}, u32[]{:S(2)}) collective-permute-start(bf16[4,64,256]{2,1,0:T(8,128)(2,1)S(1)} %pad_maximum_fusion.refs_0_), channel_id=1, source_target_pairs={{0,24},{8,16},{16,8},{24,0},{1,25},{9,17},{17,9},{25,1},{2,26},{10... | collective-permute-start | bytes 393224 | tf_op jit(solution)/shard_map/ppermute | solution.py:342
  23.3 0.2 state.1
  23.6 0.1 collective-permute-start.12
  23.7 2.9 %collective-permute-start.13 = (bf16[128,128]{1,0:T(8,128)(2,1)S(1)}, bf16[128,128]{1,0:T(8,128)(2,1)S(1)}, u32[]{:S(2)}, u32[]{:S(2)}) collective-permute-start(bf16[128,128]{1,0:T(8,128)(2,1)S(1)} %get-tuple-element.59), channel_id=1, source_target_pairs={{0,4},{1,5},{2,6},{3,7},{4,0},{5,1},{6,2},{7,3},{8,12},{9,13},{10,... | collective-permute-start | bytes 98312 | tf_op jit(solution)/shard_map/ppermute | solution.py:334
  26.6 1.1 %soft_forward.1 = (bf16[256,128]{1,0:T(8,128)(2,1)S(1)}, bf16[512,128]{1,0:T(8,128)(2,1)S(1)}, bf16[512,128]{1,0:T(8,128)(2,1)S(1)}, bf16[256,1024]{1,0:T(8,128)...) custom-call(bf16[128,512]{1,0:T(8,128)(2,1)S(1)} %bitcast.18, ...), custom_call_target="tpu_custom_call" | custom-call | flops 67108864 | bytes 2818048 | tf_op jit(solution)/shard_map/soft_forward/pallas_call | solution.py:66
  27.7 0.6 collective-permute-start.23
  28.3 0.2 collective-permute-done.13.refs_1_
  28.5 2.4 %collective-permute-start.14 = (bf16[128,128]{1,0:T(8,128)(2,1)S(1)}, bf16[128,128]{1,0:T(8,128)(2,1)S(1)}, u32[]{:S(2)}, u32[]{:S(2)}) collective-permute-start(bf16[128,128]{1,0:T(8,128)(2,1)S(1)} %get-tuple-element.59), channel_id=1, source_target_pairs={{0,6},{1,7},{2,4},{3,5},{4,2},{5,3},{6,0},{7,1},{8,14},{9,15},{10,... | collective-permute-start | bytes 98312 | tf_op jit(solution)/shard_map/ppermute | solution.py:334
  30.9 3.3 %collective-permute-done.14.refs_2_ = bf16[128,128]{1,0:T(8,128)(2,1)S(1)} collective-permute-done((bf16[128,128]{1,0:T(8,128)(2,1)S(1)}, bf16[128,128]{1,0:T(8,128)(2,1)S(1)}, u32[]{:S(2)}, u32[]{:S(2)}) %collective-permute-start.14) | collective-permute-done | bytes 32800 | tf_op jit(solution)/shard_map/ppermute | solution.py:334
  34.3 1.5 %collective-permute-start.24 = (bf16[128,256]{1,0:T(8,128)(2,1)S(1)}, bf16[128,256]{1,0:T(8,128)(2,1)S(1)}, u32[]{:S(2)}, u32[]{:S(2)}) collective-permute-start(bf16[128,256]{1,0:T(8,128)(2,1)S(1)} %get-tuple-element.76), channel_id=1, source_target_pairs={{0,16},{8,24},{16,0},{24,8},{1,17},{9,25},{17,1},{25,9},{2,18},{10... | collective-permute-start | bytes 196616 | tf_op jit(solution)/shard_map/ppermute | solution.py:342
  35.8 0.7 copy-done.7
  36.5 0.6 lin_forward.1
  37.1 1.3 %collective-permute-start.25 = (bf16[128,256]{1,0:T(8,128)(2,1)S(1)}, bf16[128,256]{1,0:T(8,128)(2,1)S(1)}, u32[]{:S(2)}, u32[]{:S(2)}) collective-permute-start(bf16[128,256]{1,0:T(8,128)(2,1)S(1)} %get-tuple-element.77), channel_id=1, source_target_pairs={{0,24},{8,16},{16,8},{24,0},{1,25},{9,17},{17,9},{25,1},{2,26},{10... | collective-permute-start | bytes 196616 | tf_op jit(solution)/shard_map/ppermute | solution.py:342
  38.4 0.7 %collective-permute-start.26 = (bf16[128,256]{1,0:T(8,128)(2,1)S(1)}, bf16[128,256]{1,0:T(8,128)(2,1)S(1)}, u32[]{:S(2)}, u32[]{:S(2)}) collective-permute-start(bf16[128,256]{1,0:T(8,128)(2,1)S(1)} %get-tuple-element.79), channel_id=1, source_target_pairs={{0,8},{8,0},{16,24},{24,16},{1,9},{9,1},{17,25},{25,17},{2,10},{10... | collective-permute-start | bytes 196616 | tf_op jit(solution)/shard_map/ppermute | solution.py:342
  39.1 1.5 %collective-permute-start.27 = (bf16[128,256]{1,0:T(8,128)(2,1)S(1)}, bf16[128,256]{1,0:T(8,128)(2,1)S(1)}, u32[]{:S(2)}, u32[]{:S(2)}) collective-permute-start(bf16[128,256]{1,0:T(8,128)(2,1)S(1)} %get-tuple-element.80), channel_id=1, source_target_pairs={{0,16},{8,24},{16,0},{24,8},{1,17},{9,25},{17,1},{25,9},{2,18},{10... | collective-permute-start | bytes 196616 | tf_op jit(solution)/shard_map/ppermute | solution.py:342
  40.6 1.2 %collective-permute-start.28 = (bf16[128,256]{1,0:T(8,128)(2,1)S(1)}, bf16[128,256]{1,0:T(8,128)(2,1)S(1)}, u32[]{:S(2)}, u32[]{:S(2)}) collective-permute-start(bf16[128,256]{1,0:T(8,128)(2,1)S(1)} %get-tuple-element.81), channel_id=1, source_target_pairs={{0,24},{8,16},{16,8},{24,0},{1,25},{9,17},{17,9},{25,1},{2,26},{10... | collective-permute-start | bytes 196616 | tf_op jit(solution)/shard_map/ppermute | solution.py:342
  41.9 0.4 d_attn.1.dattn
  42.3 0.5 lin_backward.1
  42.7 0.1 collective-permute-start.15
  42.8 2.7 %collective-permute-start.16 = (bf16[128,128]{1,0:T(8,128)(2,1)S(1)}, bf16[128,128]{1,0:T(8,128)(2,1)S(1)}, u32[]{:S(2)}, u32[]{:S(2)}) collective-permute-start(bf16[128,128]{1,0:T(8,128)(2,1)S(1)} %get-tuple-element.64), channel_id=1, source_target_pairs={{0,4},{1,5},{2,6},{3,7},{4,0},{5,1},{6,2},{7,3},{8,12},{9,13},{10,... | collective-permute-start | bytes 98312 | tf_op jit(solution)/shard_map/ppermute | solution.py:334
  45.5 1.7 %collective-permute-start.17 = (bf16[128,128]{1,0:T(8,128)(2,1)S(1)}, bf16[128,128]{1,0:T(8,128)(2,1)S(1)}, u32[]{:S(2)}, u32[]{:S(2)}) collective-permute-start(bf16[128,128]{1,0:T(8,128)(2,1)S(1)} %get-tuple-element.64), channel_id=1, source_target_pairs={{0,6},{1,7},{2,4},{3,5},{4,2},{5,3},{6,0},{7,1},{8,14},{9,15},{10,... | collective-permute-start | bytes 98312 | tf_op jit(solution)/shard_map/ppermute | solution.py:334
  47.2 0.1 weight_rows.1
  47.3 0.7 collective-permute-start.29
  48.0 0.6 collective-permute-start.30
  48.6 0.7 %soft_backward.1 = (bf16[128,128]{1,0:T(8,128)(2,1)S(1)}, f32[128,128]{1,0:T(8,128)S(1)}, f32[128,128]{1,0:T(8,128)S(1)}, bf16[128,384]{1,0:T(8,128)(2,1)S(1)}, ...) custom-call(bf16[256,128]{1,0:T(8,128)(2,1)S(1)} %get-tuple-element.48.qs, ...), custom_call_target="tpu_custom_call" | custom-call | flops 67108864 | bytes 1441792 | tf_op jit(solution)/shard_map/soft_backward/pallas_call | solution.py:66
  49.3 3.6 %collective-permute-start.31 = (bf16[64,256]{1,0:T(8,128)(2,1)S(1)}, bf16[64,256]{1,0:T(8,128)(2,1)S(1)}, u32[]{:S(2)}, u32[]{:S(2)}) collective-permute-start(bf16[64,256]{1,0:T(8,128)(2,1)S(1)} %get-tuple-element.84), channel_id=1, source_target_pairs={{0,4},{1,6},{2,5},{3,7},{4,0},{5,2},{6,1},{7,3},{8,12},{9,14},{10,... | collective-permute-start | bytes 98312 | tf_op jit(solution)/shard_map/ppermute | solution.py:446
  52.9 1.1 %collective-permute-start.22 = (bf16[128,256]{1,0:T(8,128)(2,1)S(1)}, bf16[128,256]{1,0:T(8,128)(2,1)S(1)}, u32[]{:S(2)}, u32[]{:S(2)}) collective-permute-start(bf16[128,256]{1,0:T(8,128)(2,1)S(1)} %get-tuple-element.70), channel_id=1, source_target_pairs={{6,0},{3,1},{0,2},{5,3},{2,4},{7,5},{4,6},{1,7},{14,8},{11,9},{8,1... | collective-permute-start | bytes 196616 | tf_op jit(solution)/shard_map/ppermute | solution.py:430
  54.0 0.5 collective-permute-start.32
  54.5 2.2 %collective-permute-start.18 = (bf16[128,384]{1,0:T(8,128)(2,1)S(1)}, bf16[128,384]{1,0:T(8,128)(2,1)S(1)}, u32[]{:S(2)}, u32[]{:S(2)}) collective-permute-start(bf16[128,384]{1,0:T(8,128)(2,1)S(1)} %get-tuple-element.66), channel_id=1, source_target_pairs={{0,1},{1,0},{2,3},{3,2},{4,5},{5,4},{6,7},{7,6},{8,9},{9,8},{10,11... | collective-permute-start | bytes 294920 | tf_op jit(solution)/shard_map/ppermute | solution.py:428
  56.7 0.1 collective-permute-start.19
  56.8 0.3 lin_final.1
  57.1 3.4 %collective-permute-done.32.refs_3_ = bf16[64,256]{1,0:T(8,128)(2,1)S(1)} collective-permute-done((bf16[64,256]{1,0:T(8,128)(2,1)S(1)}, bf16[64,256]{1,0:T(8,128)(2,1)S(1)}, u32[]{:S(2)}, u32[]{:S(2)}) %collective-permute-start.32) | collective-permute-done | bytes 32800 | tf_op jit(solution)/shard_map/ppermute | solution.py:446
  60.4 0.4 collective-permute-start.20
  60.9 1.0 %collective-permute-start.33 = (f32[64,256]{1,0:T(8,128)S(1)}, f32[64,256]{1,0:T(8,128)S(1)}, u32[]{:S(2)}, u32[]{:S(2)}) collective-permute-start(f32[64,256]{1,0:T(8,128)S(1)} %weight_sum.1.refs_0_), channel_id=1, source_target_pairs={{0,8},{8,0},{16,24},{24,16},{1,9},{9,1},{17,25},{25,17},{2,10},{10... | collective-permute-start | bytes 196616 | tf_op jit(solution)/shard_map/ppermute | solution.py:342
  61.9 1.5 %collective-permute-start.34 = (f32[64,256]{1,0:T(8,128)S(1)}, f32[64,256]{1,0:T(8,128)S(1)}, u32[]{:S(2)}, u32[]{:S(2)}) collective-permute-start(f32[64,256]{1,0:T(8,128)S(1)} %weight_sum.1.refs_0_), channel_id=1, source_target_pairs={{0,16},{8,24},{16,0},{24,8},{1,17},{9,25},{17,1},{25,9},{2,18},{10... | collective-permute-start | bytes 196616 | tf_op jit(solution)/shard_map/ppermute | solution.py:342
  63.5 1.0 %collective-permute-start.35 = (f32[64,256]{1,0:T(8,128)S(1)}, f32[64,256]{1,0:T(8,128)S(1)}, u32[]{:S(2)}, u32[]{:S(2)}) collective-permute-start(f32[64,256]{1,0:T(8,128)S(1)} %weight_sum.1.refs_0_), channel_id=1, source_target_pairs={{0,24},{8,16},{16,8},{24,0},{1,25},{9,17},{17,9},{25,1},{2,26},{10... | collective-permute-start | bytes 196616 | tf_op jit(solution)/shard_map/ppermute | solution.py:342
  64.5 0.8 %outputs.1 = (bf16[1,128,512]{2,1,0:T(8,128)(2,1)}, bf16[1,128,512]{2,1,0:T(8,128)(2,1)}, bf16[1,128,512]{2,1,0:T(8,128)(2,1)}) custom-call(bf16[128,128]{1,0:T(8,128)(2,1)S(1)} %get-tuple-element.54.dq_soft, f32[128,128]{1,0:T(8,128)S(1)} %get-tuple-element.55.dk_soft, f32[128,128]{1,0:T(8,128)S(1)} %get-tuple-element.56.dv_soft, ...), custom_call_target="tpu_custom_call" | custom-call | bytes 983040 | tf_op jit(solution)/shard_map/outputs/pallas_call | solution.py:66
  65.3 0.9 %collective-permute-done.34.refs_2_ = f32[64,256]{1,0:T(8,128)S(1)} collective-permute-done((f32[64,256]{1,0:T(8,128)S(1)}, f32[64,256]{1,0:T(8,128)S(1)}, u32[]{:S(2)}, u32[]{:S(2)}) %collective-permute-start.34) | collective-permute-done | bytes 65568 | tf_op jit(solution)/shard_map/ppermute | solution.py:342
  66.2 2.4 %collective-permute-done.35.refs_3_ = f32[64,256]{1,0:T(8,128)S(1)} collective-permute-done((f32[64,256]{1,0:T(8,128)S(1)}, f32[64,256]{1,0:T(8,128)S(1)}, u32[]{:S(2)}, u32[]{:S(2)}) %collective-permute-start.35) | collective-permute-done | bytes 65568 | tf_op jit(solution)/shard_map/ppermute | solution.py:342
  68.6 0.7 %weight_join.1 = f32[64,1024]{1,0:T(8,128)} custom-call(f32[64,256]{1,0:T(8,128)S(1)} %weight_sum.1.refs_0_, f32[64,256]{1,0:T(8,128)S(1)} %collective-permute-done.33.refs_1_, f32[64,256]{1,0:T(8,128)S(1)} %collective-permute-done.34.refs_2_, f32[64,256]{1,0:T(8,128)S(1)} %collective-permute-done.35.refs_3_), custom_call_target="tpu_custom_call" | custom-call | bytes 524288 | tf_op jit(solution)/shard_map/weight_join/pallas_call | solution.py:66
  (38 shorter events, 0.1 us)
Async XLA Ops:
  0.6 0.9 %copy-start = (bf16[64,1024]{1,0:T(8,128)(2,1)S(1)}, bf16[64,1024]{1,0:T(8,128)(2,1)}, u32[]{:S(2)}) copy-start(bf16[64,1024]{1,0:T(8,128)(2,1)} %param.10) | copy-start | bytes 393220
  0.6 23.0 %collective-permute-start.1 = (bf16[128,1024]{1,0:T(8,128)(2,1)}, bf16[128,1024]{1,0:T(8,128)(2,1)S(1)}, u32[]{:S(2)}, u32[]{:S(2)}) collective-permute-start(bf16[128,1024]{1,0:T(8,128)(2,1)} %bitcast.21), channel_id=1, source_target_pairs={{0,1},{1,0},{2,3},{3,2},{4,5},{5,4},{6,7},{7,6},{8,9},{9,8},{10,11... | collective-permute-start | bytes 786440 | tf_op jit(solution)/shard_map/ppermute | solution.py:347
  1.5 8.5 %collective-permute-start.7 = (bf16[64,256]{1,0:T(8,128)(2,1)S(1)}, bf16[64,256]{1,0:T(8,128)(2,1)S(1)}, u32[]{:S(2)}, u32[]{:S(2)}) collective-permute-start(bf16[64,256]{1,0:T(8,128)(2,1)S(1)} %constant_dynamic-slice_fusion), channel_id=1, source_target_pairs={{0,6},{1,4},{2,7},{3,5},{4,2},{5,0},{6,3},{7,1},{8,14},{9,12},{10,... | collective-permute-start | bytes 98312 | tf_op jit(solution)/shard_map/ppermute | solution.py:357
  6.6 5.3 %collective-permute-start.6 = (bf16[64,256]{1,0:T(8,128)(2,1)S(1)}, bf16[64,256]{1,0:T(8,128)(2,1)S(1)}, u32[]{:S(2)}, u32[]{:S(2)}) collective-permute-start(bf16[64,256]{1,0:T(8,128)(2,1)S(1)} %constant_dynamic-slice_fusion), channel_id=1, source_target_pairs={{0,4},{1,6},{2,5},{3,7},{4,0},{5,2},{6,1},{7,3},{8,12},{9,14},{10,... | collective-permute-start | bytes 98312 | tf_op jit(solution)/shard_map/ppermute | solution.py:357
  6.6 9.4 %collective-permute-start.5 = (bf16[64,256]{1,0:T(8,128)(2,1)S(1)}, bf16[64,256]{1,0:T(8,128)(2,1)S(1)}, u32[]{:S(2)}, u32[]{:S(2)}) collective-permute-start(bf16[64,256]{1,0:T(8,128)(2,1)S(1)} %constant_dynamic-slice_fusion), channel_id=1, source_target_pairs={{0,2},{1,0},{2,3},{3,1},{4,6},{5,4},{6,7},{7,5},{8,10},{9,8},{10,1... | collective-permute-start | bytes 98312 | tf_op jit(solution)/shard_map/ppermute | solution.py:357
  6.6 9.4 %collective-permute-start.4 = (bf16[64,256]{1,0:T(8,128)(2,1)S(1)}, bf16[64,256]{1,0:T(8,128)(2,1)S(1)}, u32[]{:S(2)}, u32[]{:S(2)}) collective-permute-start(bf16[64,256]{1,0:T(8,128)(2,1)S(1)} %constant_dynamic-slice_fusion), channel_id=1, source_target_pairs={{0,0},{1,2},{2,1},{3,3},{4,4},{5,6},{6,5},{7,7},{8,8},{9,10},{10,9... | collective-permute-start | bytes 98312 | tf_op jit(solution)/shard_map/ppermute | solution.py:357
  7.3 0.9 %copy-start.1 = (bf16[1,128,512]{2,1,0:T(8,128)(2,1)S(1)}, bf16[1,128,512]{2,1,0:T(8,128)(2,1)}, u32[]{:S(2)}) copy-start(bf16[1,128,512]{2,1,0:T(8,128)(2,1)} %param.7) | copy-start | bytes 393220
  8.2 0.9 %copy-start.3 = (bf16[1,128,512]{2,1,0:T(8,128)(2,1)S(1)}, bf16[1,128,512]{2,1,0:T(8,128)(2,1)}, u32[]{:S(2)}) copy-start(bf16[1,128,512]{2,1,0:T(8,128)(2,1)} %param.8) | copy-start | bytes 393220
  9.1 0.9 %copy-start.5 = (bf16[1,128,512]{2,1,0:T(8,128)(2,1)S(1)}, bf16[1,128,512]{2,1,0:T(8,128)(2,1)}, u32[]{:S(2)}) copy-start(bf16[1,128,512]{2,1,0:T(8,128)(2,1)} %param.6) | copy-start | bytes 393220
  10.0 13.5 %collective-permute-start = (bf16[128,512]{1,0:T(8,128)(2,1)S(1)}, bf16[128,512]{1,0:T(8,128)(2,1)S(1)}, u32[]{:S(2)}, u32[]{:S(2)}) collective-permute-start(bf16[128,512]{1,0:T(8,128)(2,1)S(1)} %get-tuple-element.45), channel_id=1, source_target_pairs={{0,1},{1,0},{2,3},{3,2},{4,5},{5,4},{6,7},{7,6},{8,9},{9,8},{10,11... | collective-permute-start | bytes 393224 | tf_op jit(solution)/shard_map/ppermute | solution.py:372
  11.9 6.5 %collective-permute-start.2 = (bf16[128,256]{1,0:T(8,128)(2,1)S(1)}, bf16[128,256]{1,0:T(8,128)(2,1)S(1)}, u32[]{:S(2)}, u32[]{:S(2)}) collective-permute-start(bf16[128,256]{1,0:T(8,128)(2,1)S(1)} %get-tuple-element.46), channel_id=1, source_target_pairs={{0,7},{1,2},{2,1},{3,4},{4,3},{5,6},{6,5},{7,0},{8,15},{9,10},{10,... | collective-permute-start | bytes 196616 | tf_op jit(solution)/shard_map/ppermute | solution.py:370
  16.0 4.4 %collective-permute-start.3 = (bf16[128,256]{1,0:T(8,128)(2,1)S(1)}, bf16[128,256]{1,0:T(8,128)(2,1)S(1)}, u32[]{:S(2)}, u32[]{:S(2)}) collective-permute-start(bf16[128,256]{1,0:T(8,128)(2,1)S(1)} %get-tuple-element.47), channel_id=1, source_target_pairs={{0,6},{1,3},{2,0},{3,5},{4,2},{5,7},{6,4},{7,1},{8,14},{9,11},{10,... | collective-permute-start | bytes 196616 | tf_op jit(solution)/shard_map/ppermute | solution.py:371
  16.0 5.9 %collective-permute-start.11 = (bf16[128,256]{1,0:T(8,128)(2,1)S(1)}, bf16[128,256]{1,0:T(8,128)(2,1)S(1)}, u32[]{:S(2)}, u32[]{:S(2)}) collective-permute-start(bf16[128,256]{1,0:T(8,128)(2,1)S(1)} %get-tuple-element.57), channel_id=1, source_target_pairs={{0,1},{1,0},{2,3},{3,2},{4,5},{5,4},{6,7},{7,6},{8,9},{9,8},{10,11... | collective-permute-start | bytes 196616 | tf_op jit(solution)/shard_map/ppermute | solution.py:369
  16.1 7.2 %copy-start.2 = (bf16[1,128,512]{2,1,0:T(8,128)(2,1)S(1)}, bf16[1,128,512]{2,1,0:T(8,128)(2,1)}, u32[]{:S(2)}) copy-start(bf16[1,128,512]{2,1,0:T(8,128)(2,1)} %param.7) | copy-start | bytes 393220
  16.1 7.2 %copy-start.4 = (bf16[1,128,512]{2,1,0:T(8,128)(2,1)S(1)}, bf16[1,128,512]{2,1,0:T(8,128)(2,1)}, u32[]{:S(2)}) copy-start(bf16[1,128,512]{2,1,0:T(8,128)(2,1)} %param.8) | copy-start | bytes 393220
  16.1 10.5 %copy-start.6 = (bf16[1,128,1024]{2,1,0:T(8,128)(2,1)S(1)}, bf16[1,128,1024]{2,1,0:T(8,128)(2,1)}, u32[]{:S(2)}) copy-start(bf16[1,128,1024]{2,1,0:T(8,128)(2,1)} %param.9) | copy-start | bytes 786436
  18.4 18.7 %collective-permute-start.8 = (bf16[4,64,256]{2,1,0:T(8,128)(2,1)S(1)}, bf16[4,64,256]{2,1,0:T(8,128)(2,1)S(1)}, u32[]{:S(2)}, u32[]{:S(2)}) collective-permute-start(bf16[4,64,256]{2,1,0:T(8,128)(2,1)S(1)} %pad_maximum_fusion.refs_0_), channel_id=1, source_target_pairs={{0,8},{8,0},{16,24},{24,16},{1,9},{9,1},{17,25},{25,17},{2,10},{10... | collective-permute-start | bytes 393224 | tf_op jit(solution)/shard_map/ppermute | solution.py:342
  20.3 18.0 %collective-permute-start.9 = (bf16[4,64,256]{2,1,0:T(8,128)(2,1)S(1)}, bf16[4,64,256]{2,1,0:T(8,128)(2,1)S(1)}, u32[]{:S(2)}, u32[]{:S(2)}) collective-permute-start(bf16[4,64,256]{2,1,0:T(8,128)(2,1)S(1)} %pad_maximum_fusion.refs_0_), channel_id=1, source_target_pairs={{0,16},{8,24},{16,0},{24,8},{1,17},{9,25},{17,1},{25,9},{2,18},{10... | collective-permute-start | bytes 393224 | tf_op jit(solution)/shard_map/ppermute | solution.py:342
  21.9 17.2 %collective-permute-start.10 = (bf16[4,64,256]{2,1,0:T(8,128)(2,1)S(1)}, bf16[4,64,256]{2,1,0:T(8,128)(2,1)S(1)}, u32[]{:S(2)}, u32[]{:S(2)}) collective-permute-start(bf16[4,64,256]{2,1,0:T(8,128)(2,1)S(1)} %pad_maximum_fusion.refs_0_), channel_id=1, source_target_pairs={{0,24},{8,16},{16,8},{24,0},{1,25},{9,17},{17,9},{25,1},{2,26},{10... | collective-permute-start | bytes 393224 | tf_op jit(solution)/shard_map/ppermute | solution.py:342
  23.6 4.1 %collective-permute-start.12 = (bf16[128,128]{1,0:T(8,128)(2,1)S(1)}, bf16[128,128]{1,0:T(8,128)(2,1)S(1)}, u32[]{:S(2)}, u32[]{:S(2)}) collective-permute-start(bf16[128,128]{1,0:T(8,128)(2,1)S(1)} %get-tuple-element.59), channel_id=1, source_target_pairs={{0,2},{1,3},{2,0},{3,1},{4,6},{5,7},{6,4},{7,5},{8,10},{9,11},{10,... | collective-permute-start | bytes 98312 | tf_op jit(solution)/shard_map/ppermute | solution.py:334
  23.7 4.9 %collective-permute-start.13 = (bf16[128,128]{1,0:T(8,128)(2,1)S(1)}, bf16[128,128]{1,0:T(8,128)(2,1)S(1)}, u32[]{:S(2)}, u32[]{:S(2)}) collective-permute-start(bf16[128,128]{1,0:T(8,128)(2,1)S(1)} %get-tuple-element.59), channel_id=1, source_target_pairs={{0,4},{1,5},{2,6},{3,7},{4,0},{5,1},{6,2},{7,3},{8,12},{9,13},{10,... | collective-permute-start | bytes 98312 | tf_op jit(solution)/shard_map/ppermute | solution.py:334
  27.7 12.9 %collective-permute-start.23 = (bf16[128,256]{1,0:T(8,128)(2,1)S(1)}, bf16[128,256]{1,0:T(8,128)(2,1)S(1)}, u32[]{:S(2)}, u32[]{:S(2)}) collective-permute-start(bf16[128,256]{1,0:T(8,128)(2,1)S(1)} %get-tuple-element.75), channel_id=1, source_target_pairs={{0,8},{8,0},{16,24},{24,16},{1,9},{9,1},{17,25},{25,17},{2,10},{10... | collective-permute-start | bytes 196616 | tf_op jit(solution)/shard_map/ppermute | solution.py:342
  28.5 5.7 %collective-permute-start.14 = (bf16[128,128]{1,0:T(8,128)(2,1)S(1)}, bf16[128,128]{1,0:T(8,128)(2,1)S(1)}, u32[]{:S(2)}, u32[]{:S(2)}) collective-permute-start(bf16[128,128]{1,0:T(8,128)(2,1)S(1)} %get-tuple-element.59), channel_id=1, source_target_pairs={{0,6},{1,7},{2,4},{3,5},{4,2},{5,3},{6,0},{7,1},{8,14},{9,15},{10,... | collective-permute-start | bytes 98312 | tf_op jit(solution)/shard_map/ppermute | solution.py:334
  34.3 8.5 %collective-permute-start.24 = (bf16[128,256]{1,0:T(8,128)(2,1)S(1)}, bf16[128,256]{1,0:T(8,128)(2,1)S(1)}, u32[]{:S(2)}, u32[]{:S(2)}) collective-permute-start(bf16[128,256]{1,0:T(8,128)(2,1)S(1)} %get-tuple-element.76), channel_id=1, source_target_pairs={{0,16},{8,24},{16,0},{24,8},{1,17},{9,25},{17,1},{25,9},{2,18},{10... | collective-permute-start | bytes 196616 | tf_op jit(solution)/shard_map/ppermute | solution.py:342
  35.8 0.7 copy-start.7
  37.1 5.8 %collective-permute-start.25 = (bf16[128,256]{1,0:T(8,128)(2,1)S(1)}, bf16[128,256]{1,0:T(8,128)(2,1)S(1)}, u32[]{:S(2)}, u32[]{:S(2)}) collective-permute-start(bf16[128,256]{1,0:T(8,128)(2,1)S(1)} %get-tuple-element.77), channel_id=1, source_target_pairs={{0,24},{8,16},{16,8},{24,0},{1,25},{9,17},{17,9},{25,1},{2,26},{10... | collective-permute-start | bytes 196616 | tf_op jit(solution)/shard_map/ppermute | solution.py:342
  38.4 7.2 %collective-permute-start.26 = (bf16[128,256]{1,0:T(8,128)(2,1)S(1)}, bf16[128,256]{1,0:T(8,128)(2,1)S(1)}, u32[]{:S(2)}, u32[]{:S(2)}) collective-permute-start(bf16[128,256]{1,0:T(8,128)(2,1)S(1)} %get-tuple-element.79), channel_id=1, source_target_pairs={{0,8},{8,0},{16,24},{24,16},{1,9},{9,1},{17,25},{25,17},{2,10},{10... | collective-permute-start | bytes 196616 | tf_op jit(solution)/shard_map/ppermute | solution.py:342
  39.1 8.1 %collective-permute-start.27 = (bf16[128,256]{1,0:T(8,128)(2,1)S(1)}, bf16[128,256]{1,0:T(8,128)(2,1)S(1)}, u32[]{:S(2)}, u32[]{:S(2)}) collective-permute-start(bf16[128,256]{1,0:T(8,128)(2,1)S(1)} %get-tuple-element.80), channel_id=1, source_target_pairs={{0,16},{8,24},{16,0},{24,8},{1,17},{9,25},{17,1},{25,9},{2,18},{10... | collective-permute-start | bytes 196616 | tf_op jit(solution)/shard_map/ppermute | solution.py:342
  40.6 6.6 %collective-permute-start.28 = (bf16[128,256]{1,0:T(8,128)(2,1)S(1)}, bf16[128,256]{1,0:T(8,128)(2,1)S(1)}, u32[]{:S(2)}, u32[]{:S(2)}) collective-permute-start(bf16[128,256]{1,0:T(8,128)(2,1)S(1)} %get-tuple-element.81), channel_id=1, source_target_pairs={{0,24},{8,16},{16,8},{24,0},{1,25},{9,17},{17,9},{25,1},{2,26},{10... | collective-permute-start | bytes 196616 | tf_op jit(solution)/shard_map/ppermute | solution.py:342
  42.7 6.6 %collective-permute-start.15 = (bf16[128,128]{1,0:T(8,128)(2,1)S(1)}, bf16[128,128]{1,0:T(8,128)(2,1)S(1)}, u32[]{:S(2)}, u32[]{:S(2)}) collective-permute-start(bf16[128,128]{1,0:T(8,128)(2,1)S(1)} %get-tuple-element.64), channel_id=1, source_target_pairs={{0,2},{1,3},{2,0},{3,1},{4,6},{5,7},{6,4},{7,5},{8,10},{9,11},{10,... | collective-permute-start | bytes 98312 | tf_op jit(solution)/shard_map/ppermute | solution.py:334
  42.8 10.1 %collective-permute-start.16 = (bf16[128,128]{1,0:T(8,128)(2,1)S(1)}, bf16[128,128]{1,0:T(8,128)(2,1)S(1)}, u32[]{:S(2)}, u32[]{:S(2)}) collective-permute-start(bf16[128,128]{1,0:T(8,128)(2,1)S(1)} %get-tuple-element.64), channel_id=1, source_target_pairs={{0,4},{1,5},{2,6},{3,7},{4,0},{5,1},{6,2},{7,3},{8,12},{9,13},{10,... | collective-permute-start | bytes 98312 | tf_op jit(solution)/shard_map/ppermute | solution.py:334
  45.5 7.4 %collective-permute-start.17 = (bf16[128,128]{1,0:T(8,128)(2,1)S(1)}, bf16[128,128]{1,0:T(8,128)(2,1)S(1)}, u32[]{:S(2)}, u32[]{:S(2)}) collective-permute-start(bf16[128,128]{1,0:T(8,128)(2,1)S(1)} %get-tuple-element.64), channel_id=1, source_target_pairs={{0,6},{1,7},{2,4},{3,5},{4,2},{5,3},{6,0},{7,1},{8,14},{9,15},{10,... | collective-permute-start | bytes 98312 | tf_op jit(solution)/shard_map/ppermute | solution.py:334
  47.3 6.7 %collective-permute-start.29 = (bf16[64,256]{1,0:T(8,128)(2,1)S(1)}, bf16[64,256]{1,0:T(8,128)(2,1)S(1)}, u32[]{:S(2)}, u32[]{:S(2)}) collective-permute-start(bf16[64,256]{1,0:T(8,128)(2,1)S(1)} %get-tuple-element.82), channel_id=1, source_target_pairs={{0,0},{1,2},{2,1},{3,3},{4,4},{5,6},{6,5},{7,7},{8,8},{9,10},{10,9... | collective-permute-start | bytes 98312 | tf_op jit(solution)/shard_map/ppermute | solution.py:446
  48.0 6.5 %collective-permute-start.30 = (bf16[64,256]{1,0:T(8,128)(2,1)S(1)}, bf16[64,256]{1,0:T(8,128)(2,1)S(1)}, u32[]{:S(2)}, u32[]{:S(2)}) collective-permute-start(bf16[64,256]{1,0:T(8,128)(2,1)S(1)} %get-tuple-element.83), channel_id=1, source_target_pairs={{0,1},{1,3},{2,0},{3,2},{4,5},{5,7},{6,4},{7,6},{8,9},{9,11},{10,8... | collective-permute-start | bytes 98312 | tf_op jit(solution)/shard_map/ppermute | solution.py:446
  49.3 7.3 %collective-permute-start.31 = (bf16[64,256]{1,0:T(8,128)(2,1)S(1)}, bf16[64,256]{1,0:T(8,128)(2,1)S(1)}, u32[]{:S(2)}, u32[]{:S(2)}) collective-permute-start(bf16[64,256]{1,0:T(8,128)(2,1)S(1)} %get-tuple-element.84), channel_id=1, source_target_pairs={{0,4},{1,6},{2,5},{3,7},{4,0},{5,2},{6,1},{7,3},{8,12},{9,14},{10,... | collective-permute-start | bytes 98312 | tf_op jit(solution)/shard_map/ppermute | solution.py:446
  52.9 9.0 %collective-permute-start.21 = (bf16[128,256]{1,0:T(8,128)(2,1)S(1)}, bf16[128,256]{1,0:T(8,128)(2,1)S(1)}, u32[]{:S(2)}, u32[]{:S(2)}) collective-permute-start(bf16[128,256]{1,0:T(8,128)(2,1)S(1)} %get-tuple-element.69), channel_id=1, source_target_pairs={{0,7},{1,2},{2,1},{3,4},{4,3},{5,6},{6,5},{7,0},{8,15},{9,10},{10,... | collective-permute-start | bytes 196616 | tf_op jit(solution)/shard_map/ppermute | solution.py:429
  52.9 10.5 %collective-permute-start.22 = (bf16[128,256]{1,0:T(8,128)(2,1)S(1)}, bf16[128,256]{1,0:T(8,128)(2,1)S(1)}, u32[]{:S(2)}, u32[]{:S(2)}) collective-permute-start(bf16[128,256]{1,0:T(8,128)(2,1)S(1)} %get-tuple-element.70), channel_id=1, source_target_pairs={{6,0},{3,1},{0,2},{5,3},{2,4},{7,5},{4,6},{1,7},{14,8},{11,9},{8,1... | collective-permute-start | bytes 196616 | tf_op jit(solution)/shard_map/ppermute | solution.py:430
  54.0 6.4 %collective-permute-start.32 = (bf16[64,256]{1,0:T(8,128)(2,1)S(1)}, bf16[64,256]{1,0:T(8,128)(2,1)S(1)}, u32[]{:S(2)}, u32[]{:S(2)}) collective-permute-start(bf16[64,256]{1,0:T(8,128)(2,1)S(1)} %get-tuple-element.85), channel_id=1, source_target_pairs={{0,5},{1,7},{2,4},{3,6},{4,1},{5,3},{6,0},{7,2},{8,13},{9,15},{10,... | collective-permute-start | bytes 98312 | tf_op jit(solution)/shard_map/ppermute | solution.py:446
  54.5 9.9 %collective-permute-start.18 = (bf16[128,384]{1,0:T(8,128)(2,1)S(1)}, bf16[128,384]{1,0:T(8,128)(2,1)S(1)}, u32[]{:S(2)}, u32[]{:S(2)}) collective-permute-start(bf16[128,384]{1,0:T(8,128)(2,1)S(1)} %get-tuple-element.66), channel_id=1, source_target_pairs={{0,1},{1,0},{2,3},{3,2},{4,5},{5,4},{6,7},{7,6},{8,9},{9,8},{10,11... | collective-permute-start | bytes 294920 | tf_op jit(solution)/shard_map/ppermute | solution.py:428
  56.7 4.2 %collective-permute-start.19 = (bf16[128,128]{1,0:T(8,128)(2,1)S(1)}, bf16[128,128]{1,0:T(8,128)(2,1)S(1)}, u32[]{:S(2)}, u32[]{:S(2)}) collective-permute-start(bf16[128,128]{1,0:T(8,128)(2,1)S(1)} %get-tuple-element.67), channel_id=1, source_target_pairs={{0,1},{1,0},{2,3},{3,2},{4,5},{5,4},{6,7},{7,6},{8,9},{9,8},{10,11... | collective-permute-start | bytes 98312 | tf_op jit(solution)/shard_map/ppermute | solution.py:427
  60.4 4.0 %collective-permute-start.20 = (bf16[128,256]{1,0:T(8,128)(2,1)S(1)}, bf16[128,256]{1,0:T(8,128)(2,1)S(1)}, u32[]{:S(2)}, u32[]{:S(2)}) collective-permute-start(bf16[128,256]{1,0:T(8,128)(2,1)S(1)} %get-tuple-element.68), channel_id=1, source_target_pairs={{0,1},{1,0},{2,3},{3,2},{4,5},{5,4},{6,7},{7,6},{8,9},{9,8},{10,11... | collective-permute-start | bytes 196616 | tf_op jit(solution)/shard_map/ppermute | solution.py:467
  60.9 4.4 %collective-permute-start.33 = (f32[64,256]{1,0:T(8,128)S(1)}, f32[64,256]{1,0:T(8,128)S(1)}, u32[]{:S(2)}, u32[]{:S(2)}) collective-permute-start(f32[64,256]{1,0:T(8,128)S(1)} %weight_sum.1.refs_0_), channel_id=1, source_target_pairs={{0,8},{8,0},{16,24},{24,16},{1,9},{9,1},{17,25},{25,17},{2,10},{10... | collective-permute-start | bytes 196616 | tf_op jit(solution)/shard_map/ppermute | solution.py:342
  61.9 4.3 %collective-permute-start.34 = (f32[64,256]{1,0:T(8,128)S(1)}, f32[64,256]{1,0:T(8,128)S(1)}, u32[]{:S(2)}, u32[]{:S(2)}) collective-permute-start(f32[64,256]{1,0:T(8,128)S(1)} %weight_sum.1.refs_0_), channel_id=1, source_target_pairs={{0,16},{8,24},{16,0},{24,8},{1,17},{9,25},{17,1},{25,9},{2,18},{10... | collective-permute-start | bytes 196616 | tf_op jit(solution)/shard_map/ppermute | solution.py:342
  63.5 5.2 %collective-permute-start.35 = (f32[64,256]{1,0:T(8,128)S(1)}, f32[64,256]{1,0:T(8,128)S(1)}, u32[]{:S(2)}, u32[]{:S(2)}) collective-permute-start(f32[64,256]{1,0:T(8,128)S(1)} %weight_sum.1.refs_0_), channel_id=1, source_target_pairs={{0,24},{8,16},{16,8},{24,0},{1,25},{9,17},{17,9},{25,1},{2,26},{10... | collective-permute-start | bytes 196616 | tf_op jit(solution)/shard_map/ppermute | solution.py:342

commit v2 on v1

v2 whole, which is shorter than its diff:
```python
import functools
import math

import jax
import jax.numpy as jnp
from jax import lax
from jax.experimental import pallas as pl
from jax.experimental.pallas import tpu as pltpu
from jax.sharding import Mesh
from jax.sharding import PartitionSpec as P

DH = 128
SOFT_HEADS = 2
LIN_HEADS = 2
HEADS = SOFT_HEADS + LIN_HEADS
WINDOW = 256
HALF = 128
norm_eps = 1e-06
FACTOR = DH ** (-0.5)
BF = jnp.bfloat16
F32 = jnp.float32
NN = (((1,), (0,)), ((), ()))
NT = (((1,), (1,)), ((), ()))
TN = (((0,), (0,)), ((), ()))


def unit_plus(values):
    return jnp.where(values > 0, values + 1.0, jnp.exp(jnp.minimum(values, 0.0)))


def unit_slope(values):
    return jnp.where(values > 0, 1.0, jnp.exp(jnp.minimum(values, 0.0)))


def mm(a, b, dims=NN):
    return lax.dot_general(a, b, dims, preferred_element_type=F32)


def halves(x):
    high = x.astype(BF)
    return high, (x - high.astype(F32)).astype(BF)


def mm3(a, b, dims=NN):
    a_high, a_low = halves(a)
    b_high, b_low = halves(b)
    return mm(a_high, b_high, dims) + (mm(a_high, b_low, dims) + mm(a_low, b_high, dims))


def mm2(a, b, dims=NN):
    a_high, a_low = halves(a)
    return mm(a_high, b, dims) + mm(a_low, b, dims)


def at(start, size=DH):
    return pl.ds(pl.multiple_of(start, size), size)


def places():
    return lax.axis_index("core"), lax.axis_index("z"), lax.axis_index("dp")


def call(kernel, name, outs, args, scratch=(), flops=0, outside=0):
    vmem = pl.BlockSpec(memory_space=pltpu.VMEM)
    size = sum(math.prod(x.shape) * x.dtype.itemsize for x in list(args) + list(outs))
    return pl.pallas_call(
        kernel,
        name=name,
        out_shape=list(outs),
        in_specs=[pl.BlockSpec(memory_space=pl.ANY)] * outside + [vmem] * (len(args) - outside),
        out_specs=[vmem] * len(outs),
        scratch_shapes=list(scratch),
        compiler_params=pltpu.CompilerParams(vmem_limit_bytes=24 * 2**20),
        cost_estimate=pl.CostEstimate(flops=flops, bytes_accessed=size, transcendentals=0),
    )(*args)


def like(shape, dtype):
    return jax.ShapeDtypeStruct(shape, dtype)


QS, KS, VS, QL, KL, VL = (slice(i * DH, (i + 1) * DH) for i in range(6))


def pack_kernel(q, k, v, w, mine_out, other_out, near_out, far_out, w_out, sems):
    core, _, dp = places()
    mine, other = core * DH, (1 - core) * DH
    soft = SOFT_HEADS * DH
    copies = []

    def fetch(source, target):
        copy = pltpu.make_async_copy(source, target, sems.at[len(copies)])
        copy.start()
        copies.append(copy)

    for index, array in enumerate((q, k, v)):
        for group in range(2):
            cols = slice((3 * group + index) * DH, (3 * group + index + 1) * DH)
            fetch(array.at[:, at(soft * group + other)], other_out.at[:, cols])
            fetch(array.at[:, at(soft * group + mine)], mine_out.at[:, cols])
    for index, array in enumerate((k, v)):
        cols = slice(index * DH, (index + 1) * DH)
        fetch(array.at[:, at(other)], near_out.at[:, cols])
        fetch(array.at[:, at(mine)], far_out.at[:, cols])
    width = w_out.shape[1]
    fetch(w.at[:, at(dp * width, width)], w_out)
    for copy in copies:
        copy.wait()


def state_kernel(mine, pair, state, state_low):
    total = mm2(unit_plus(mine[:, KL].astype(F32)), mine[:, VL], TN) + mm2(
        unit_plus(pair[:, KL].astype(F32)), pair[:, VL], TN
    )
    state[...] = total
    for index in range(state_low.shape[0]):
        state_low[index] = total.astype(BF)


def soft_forward_kernel(mine, pair, og, og_recv, near, far, qs, ks, vs, ogs, probs, attn, wg):
    core, _, _ = places()
    rows = og.shape[0]
    own_at, pair_at = core * rows, (1 - core) * rows
    for source, first in ((mine, own_at), (pair, pair_at)):
        qs[at(first, rows), :] = source[:, QS]
        ks[at(HALF + first, rows), :] = source[:, KS]
        vs[at(HALF + first, rows), :] = source[:, VS]
    for source, first in ((near, core * (HALF + 2 * rows)), (far, (1 - core) * (HALF + 2 * rows))):
        ks[at(first), :] = source[:, :DH]
        vs[at(first), :] = source[:, DH:]
    ogs[at(own_at, rows), :] = og[...]
    ogs[at(pair_at, rows), :] = og_recv[...]
    span = rows + 2 * HALF
    row_pos = lax.broadcasted_iota(jnp.int32, (rows, span), 0)
    col_pos = lax.broadcasted_iota(jnp.int32, (rows, span), 1)
    inside = (col_pos >= row_pos) & (col_pos < row_pos + WINDOW)
    for block in range(2):
        here, window = slice(block * rows, (block + 1) * rows), slice(block * rows, block * rows + span)
        scores = mm(qs[here, :], ks[window, :], NT) * FACTOR
        scores = jnp.where(inside, scores, -1e30)
        peak = jnp.max(scores, axis=1, keepdims=True)
        terms = jnp.where(inside, jnp.exp(scores - peak), 0.0)
        share = terms / jnp.sum(terms, axis=1, keepdims=True)
        probs[block] = share
        attn[here, :] = mm(share.astype(BF), vs[window, :]).astype(BF)
    wg[...] = mm(attn[...], ogs[...], TN).astype(wg.dtype)


def lin_forward_kernel(state, others, mine, pair, ogs, gain, u_out, total_out, wg):
    core, z, _ = places()
    rows = mine.shape[0]
    total = state[...]
    if others is not None:
        for index in range(others.shape[0]):
            total = total + jnp.where(z == index, 0.0, others[index].astype(F32))
    total_out[...] = total
    u_out[at(core * rows, rows), :] = mm3(unit_plus(mine[:, QL].astype(F32)), total)
    u_out[at((1 - core) * rows, rows), :] = mm3(unit_plus(pair[:, QL].astype(F32)), total)
    u = u_out[...]
    r = lax.rsqrt(jnp.mean(u * u, axis=1, keepdims=True) + norm_eps)
    attn = (gain[pl.ds(core, 1), :] * u * r).astype(BF)
    wg[...] = mm(attn, ogs[...], TN).astype(wg.dtype)


def dattn_kernel(weights, ogs, out, *scratch):
    if scratch:
        dps, cores, groups, rows, width = weights.shape
        for dp in range(dps):
            for half in range(cores):
                for group in range(groups):
                    first = (group * cores + half) * rows
                    scratch[0][first : first + rows, dp * width : (dp + 1) * width] = weights[dp, half, group]
        weights = scratch[0]
    out[...] = mm(ogs[...], weights[...], NT)


def lin_backward_kernel(u, total, dattn, mine, pair, gain, dq_own, dq_pair, dstate, dstate_low, grads):
    core, _, _ = places()
    rows = mine.shape[0]
    u_all = u[...]
    r = lax.rsqrt(jnp.mean(u_all * u_all, axis=1, keepdims=True) + norm_eps)
    lin_grad = gain[pl.ds(core, 1), :] * dattn[:, DH:]
    grads[...] = r * lin_grad - u_all * (r * r * r) * jnp.mean(lin_grad * u_all, axis=1, keepdims=True)
    total_state = total[...]
    result = jnp.zeros(dstate.shape, F32)
    for first, source, out in ((core * rows, mine, dq_own), ((1 - core) * rows, pair, dq_pair)):
        wide = source[:, QL].astype(F32)
        part = grads[at(first, rows), :]
        result = result + mm3(unit_plus(wide), part, TN)
        out[...] = (mm3(part, total_state, NT) * unit_slope(wide)).astype(BF)
    dstate[...] = result
    dstate_low[...] = result.astype(BF)


def soft_backward_kernel(
    qs, ks, vs, probs, attn, dattn, dq_own, dk_own, dv_own, to_pair, to_near, to_far,
    dq_all, dk_all, dv_all,
):
    core, _, _ = places()
    rows = qs.shape[0] // 2
    span = rows + 2 * HALF
    dk_all[...] = jnp.zeros_like(dk_all)
    dv_all[...] = jnp.zeros_like(dv_all)
    for block in range(2):
        here, window = slice(block * rows, (block + 1) * rows), slice(block * rows, block * rows + span)
        grad = dattn[here, :DH].astype(BF)
        share = probs[block]
        delta = jnp.sum(grad.astype(F32) * attn[here, :].astype(F32), axis=1, keepdims=True)
        dscore = (share * (mm(grad, vs[window, :], NT) - delta)).astype(BF)
        dq_all[here, :] = mm(dscore, ks[window, :]) * FACTOR
        dk_all[window, :] += mm(dscore, qs[here, :], TN) * FACTOR
        dv_all[window, :] += mm(share.astype(BF), grad, TN)
    own, pair = core * rows, (1 - core) * rows
    near_at, far_at = core * (HALF + 2 * rows), (1 - core) * (HALF + 2 * rows)
    dq_own[...] = dq_all[at(own, rows), :].astype(BF)
    dk_own[...] = dk_all[at(HALF + own, rows), :]
    dv_own[...] = dv_all[at(HALF + own, rows), :]
    to_pair[:, :DH] = dq_all[at(pair, rows), :].astype(BF)
    to_pair[:, DH : 2 * DH] = dk_all[at(HALF + pair, rows), :].astype(BF)
    to_pair[:, 2 * DH :] = dv_all[at(HALF + pair, rows), :].astype(BF)
    to_near[:, :DH] = dk_all[at(near_at), :].astype(BF)
    to_near[:, DH:] = dv_all[at(near_at), :].astype(BF)
    to_far[:, :DH] = dk_all[at(far_at), :].astype(BF)
    to_far[:, DH:] = dv_all[at(far_at), :].astype(BF)


def lin_final_kernel(dstate, others, mine, pair, soft_pair, dq_pair, own_out, pair_out):
    _, z, _ = places()
    total = dstate[...]
    if others is not None:
        for index in range(others.shape[0]):
            total = total + jnp.where(z == index, 0.0, others[index].astype(F32))
    high, low = halves(total)
    pair_out[:, : 3 * DH] = soft_pair[...]
    pair_out[:, 3 * DH : 4 * DH] = dq_pair[...]
    for source, out, first in ((mine, own_out, 0), (pair, pair_out, 4 * DH)):
        wide, values = source[:, KL].astype(F32), source[:, VL]
        dk = mm(values, high, NT) + mm(values, low, NT)
        out[:, first : first + DH] = (dk * unit_slope(wide)).astype(BF)
        out[:, first + DH : first + 2 * DH] = mm3(unit_plus(wide), total).astype(BF)


def output_kernel(dq_soft, dk_soft, dv_soft, dq_lin, lin_own, pair, near, far, dq, dk, dv):
    core, _, _ = places()
    soft = SOFT_HEADS * DH
    mine, other = core * DH, (1 - core) * DH
    dq[0, :, at(mine)] = dq_soft[...]
    dq[0, :, at(other)] = pair[:, :DH]
    dq[0, :, at(soft + mine)] = dq_lin[...]
    dq[0, :, at(soft + other)] = pair[:, 3 * DH : 4 * DH]
    for out, own, first in ((dk, dk_soft, 0), (dv, dv_soft, DH)):
        cols = slice(first, first + DH)
        out[0, :, at(mine)] = (own[...] + far[:, cols].astype(F32)).astype(BF)
        out[0, :, at(other)] = (
            pair[:, DH + first : 2 * DH + first].astype(F32) + near[:, cols].astype(F32)
        ).astype(BF)
        out[0, :, at(soft + mine)] = lin_own[:, cols]
        out[0, :, at(soft + other)] = pair[:, 4 * DH + first : 5 * DH + first]


def weight_rows_kernel(parts, dstate, out):
    dps, cores, groups, rows, width = parts.shape
    for head in range(out.shape[0]):
        total = parts[0, head % 2, head // 2].astype(F32)
        for dp in range(1, dps):
            total = total + parts[dp, head % 2, head // 2].astype(F32)
        out[head, :rows, :] = total[:, : width // 2].astype(BF)
        out[head, rows : 2 * rows, :] = total[:, width // 2 :].astype(BF)
        out[head, 2 * rows :, :] = dstate[...]


def weight_sum_kernel(scale, parts, out):
    rows, width = out.shape[1:]
    total = parts[0, : 2 * rows, :].astype(F32)
    for index in range(1, parts.shape[0]):
        total = total + parts[index, : 2 * rows, :].astype(F32)
    total = total * scale
    for index in range(out.shape[0]):
        out[index, :, : width // 2] = total[:rows]
        out[index, :, width // 2 :] = total[rows:]


def weight_join_kernel(parts, out):
    dps, rows, width = parts.shape
    for dp in range(dps):
        out[:, dp * width : (dp + 1) * width] = parts[dp].astype(F32)


def body(n_dp, n_z, queries, key_rows, value_rows, out_grad, out_weight, norm_gain):
    q, k, v, og = queries[0], key_rows[0], value_rows[0], out_grad[0]
    rows, model = og.shape
    n_seq = 2 * n_z
    every = range(n_seq)
    axes = ("z", "core")
    pair_perm = [(0, 1), (1, 0)]
    to_near = [(s, (s + 1) % n_seq if s % 2 else (s - 1) % n_seq) for s in every]
    to_far = [(s, (s + 2) % n_seq if s % 2 else (s - 2) % n_seq) for s in every]
    from_far = [(target, source) for source, target in to_far]
    core = lax.axis_index("core")
    direct = n_z == HEADS
    width = model // n_dp
    half = DH // 2

    def swap(value, axis):
        return lax.all_to_all(value, axis, 0, 0, tiled=True)

    og_recv = lax.ppermute(og, "core", pair_perm)
    mine, other, near_out, far_out, w_part = call(
        pack_kernel, "pack",
        [
            like((rows, 6 * DH), BF), like((rows, 6 * DH), BF), like((rows, 2 * DH), BF),
            like((rows, 2 * DH), BF), like((out_weight.shape[0], width), BF),
        ],
        [q, k, v, out_weight], outside=4, scratch=[pltpu.SemaphoreType.DMA((17,))],
    )
    pair = lax.ppermute(other, "core", pair_perm)
    near = lax.ppermute(near_out, axes, to_near)
    far = lax.ppermute(far_out, axes, to_far)
    if direct:
        w_rows = swap(jnp.broadcast_to(w_part, (n_z, half, width)), "z")
        w_rows = jnp.swapaxes(w_rows.reshape(2, 2, half, width), 0, 1)
        w_rows = jnp.broadcast_to(w_rows, (n_dp, 2, 2, half, width)).reshape(2 * n_dp, 2, half, width)
        weights = swap(w_rows, ("dp", "core")).reshape(n_dp, 2, 2, half, width)
    else:
        weights = lax.all_gather(out_weight, axes, axis=0, tiled=True).reshape(2, 2, DH, model)
        weights = jnp.where(core == 0, weights[:, 0], weights[:, 1]).reshape(2 * DH, model)

    copies = n_z if direct else 1
    state, state_low = call(
        state_kernel, "state", [like((DH, DH), F32), like((copies, DH, DH), BF)], [mine, pair],
        flops=4 * 2 * rows * DH * DH,
    )
    others = [swap(state_low, "z")] if direct else []
    if not direct:
        state = lax.psum(state, "z")

    span = 2 * rows + 2 * HALF
    low = BF if direct else F32
    wg_flops = 2 * 2 * rows * DH * model
    qs, ks, vs, ogs, probs, attn, wg_soft = call(
        soft_forward_kernel, "soft_forward",
        [
            like((2 * rows, DH), BF), like((span, DH), BF), like((span, DH), BF),
            like((2 * rows, model), BF), like((2, rows, rows + 2 * HALF), F32), like((2 * rows, DH), BF),
            like((DH, model), low),
        ],
        [mine, pair, og, og_recv, near, far],
        flops=wg_flops,
    )
    gain = norm_gain.reshape(LIN_HEADS, DH)

    def optional(kernel):
        if direct:
            return kernel
        return lambda first, *refs: kernel(first, None, *refs)

    u, total, wg_lin = call(
        optional(lin_forward_kernel), "lin_forward",
        [like((2 * rows, DH), F32), like((DH, DH), F32), like((DH, model), low)],
        [state] + others + [mine, pair, ogs, gain],
        flops=wg_flops,
    )
    dattn = call(
        dattn_kernel, "d_attn", [like((2 * rows, 2 * DH), F32)], [weights, ogs],
        scratch=[pltpu.VMEM((2 * DH, model), BF)] if direct else [],
        flops=2 * wg_flops,
    )[0]
    dq_lin, dq_lin_pair, dstate, dstate_low = call(
        lin_backward_kernel, "lin_backward",
        [like((rows, DH), BF), like((rows, DH), BF), like((DH, DH), F32), like((DH, DH), BF)],
        [u, total, dattn, mine, pair, gain],
        scratch=[pltpu.VMEM((2 * rows, DH), F32)],
        flops=wg_flops,
    )
    dq_soft, dk_soft, dv_soft, soft_pair, back_near, back_far = call(
        soft_backward_kernel, "soft_backward",
        [
            like((rows, DH), BF), like((rows, DH), F32), like((rows, DH), F32),
            like((rows, 3 * DH), BF), like((rows, 2 * DH), BF), like((rows, 2 * DH), BF),
        ],
        [qs, ks, vs, probs, attn, dattn],
        scratch=[pltpu.VMEM((2 * rows, DH), F32), pltpu.VMEM((span, DH), F32), pltpu.VMEM((span, DH), F32)],
        flops=wg_flops,
    )
    back_near = lax.ppermute(back_near, axes, to_near)
    back_far = lax.ppermute(back_far, axes, from_far)

    scale = 1.0 / math.sqrt(n_dp * n_seq * rows)
    if direct:
        groups = jnp.stack([wg_soft, wg_lin]).reshape(2, 2, half, n_dp, width)
        groups = groups.transpose(3, 1, 0, 2, 4).reshape(2 * n_dp, 2, half, width)
        parts = swap(groups, ("dp", "core")).reshape(n_dp, 2, 2, half, width)
        sums = call(
            weight_rows_kernel, "weight_rows", [like((n_z, 2 * DH, DH), BF)], [parts, dstate_low]
        )[0]
        others = [swap(sums, "z")]
        summed = call(
            functools.partial(weight_sum_kernel, scale), "weight_sum",
            [like((n_dp, half, width), F32)], others,
        )[0]
        weight_grad = call(
            weight_join_kernel, "weight_join", [like((half, model), F32)], [swap(summed, "dp")]
        )[0]
        others = [others[0][:, DH:]]
    else:
        groups = jnp.stack([wg_soft, wg_lin])
        slots = jnp.stack([jnp.where(core == head, groups, 0.0) for head in range(2)], axis=1)
        local = lax.psum_scatter(
            slots.reshape(HEADS * DH, model), axes, scatter_dimension=0, tiled=True
        )
        weight_grad = lax.psum(local, "dp") * scale
        dstate = lax.psum(dstate, "z")

    lin_own, to_pair = call(
        optional(lin_final_kernel), "lin_final",
        [like((rows, 2 * DH), BF), like((rows, 6 * DH), BF)],
        [dstate] + others + [mine, pair, soft_pair, dq_lin_pair],
        flops=wg_flops // 4,
    )
    from_pair = lax.ppermute(to_pair, "core", pair_perm)
    shape = like((1, rows, HEADS * DH), BF)
    dq, dk, dv = call(
        output_kernel, "outputs", [shape] * 3,
        [dq_soft, dk_soft, dv_soft, dq_lin, lin_own, from_pair, back_near, back_far],
    )
    return dq, dk, dv, weight_grad


def solution(mesh):
    n_dp, n_seq = mesh.shape["dp"], mesh.shape["seq"]
    blocks = Mesh(mesh.devices.reshape(n_dp, n_seq // 2, 2), ("dp", "z", "core"))
    tokens, heads = P("dp", ("z", "core"), None), P(("z", "core"), None)
    return jax.shard_map(
        functools.partial(body, n_dp, n_seq // 2),
        mesh=blocks,
        in_specs=(tokens, tokens, tokens, tokens, heads, P()),
        out_specs=(tokens, tokens, tokens, heads),
        check_vma=False,
    )
```

time: 69.6 us -> 82.7 us (1.19)
  waiting for transfers between devices: 13.1 us -> 35.4 us
  starting transfers between devices: 46.1 us -> 30.5 us
  local copies, waits for them, and re-layouts: 3.79 us -> 7.1 us
  Pallas kernels: 5.53 us -> 7.82 us
    ppermute x36 -> x7, starting transfers between devices: 46.1 us -> 5.27 us  [the longest x1 1.56 us: body(): back_near = lax.ppermute(back_near, axes, to_near)]
    all_to_all x0 -> x6, waiting for transfers between devices: none -> 29.2 us  [swap(): return lax.all_to_all(value, axis, 0, 0, tiled=True)]
    all_to_all x0 -> x6, starting transfers between devices: none -> 25.2 us  [swap(): return lax.all_to_all(value, axis, 0, 0, tiled=True)]
    ppermute x36 -> x7, waiting for transfers between devices: 13.1 us -> 6.23 us  [the longest x1 3.6 us: body(): near = lax.ppermute(near_out, axes, to_near)]
    pallas_call x12, Pallas kernels: 5.53 us -> 7.82 us  [call(): pl.pallas_call(kernel, name=name, out_shape=list(outs), in_specs=[pl.Bloc...]
    broadcast_in_dim x0 -> x2, local copies, waits for them, and re-layouts: none -> 1.53 us  [the longest x1 0.86 us: body(): jnp.broadcast_to(w_rows, (n_dp, 2, 2, half, width))]
    transpose x0 -> x2, local copies, waits for them, and re-layouts: none -> 0.91 us  [the longest x1 0.9 us: body(): groups = groups.transpose(3, 1, 0, 2, 4).reshape(2 * n_dp, 2, half, width)]
    unnamed x16 -> x12, local copies, waits for them, and re-layouts: 3.79 us -> 4.29 us
  transfers between devices with their start and end apart: 36 -> 13, of which waited for: 7 -> 8; matrix products, arithmetic and copies ran while one was open for 0% -> 3% of each run, Pallas kernels for 7% -> 6%
where the time goes in v2:
time: 82.7 us; the launch traced here: 81.9 us
  waiting for transfers between devices  35.4 us (43%)
  starting transfers between devices  30.5 us (37%)
  Pallas kernels  7.82 us (9%)
  local copies, waits for them, and re-layouts  7.1 us (9%)
    all_to_all x6, waiting for transfers between devices, swap(): return lax.all_to_all(value, axis, 0, 0, tiled=True)  29.2 us
    all_to_all x6, starting transfers between devices, swap(): return lax.all_to_all(value, axis, 0, 0, tiled=True)  25.2 us
    pallas_call x12, Pallas kernels, call(): pl.pallas_call(kernel, name=name, out_shape=list(outs), in_specs=[pl.Bloc...  7.82 us
    unnamed x12, local copies, waits for them, and re-layouts  4.29 us
    ppermute x1, waiting for transfers between devices, body(): near = lax.ppermute(near_out, axes, to_near)  3.6 us
    ppermute x1, waiting for transfers between devices, body(): back_far = lax.ppermute(back_far, axes, from_far)  1.93 us
  transfers between devices with their start and end apart: 13, of which 8 were waited for; matrix products, arithmetic and copies ran while one was open for 3% of the time, Pallas kernels for 6%

profile of v2, /device:TPU:0, one launch (start us, length us, event | category | flops | bytes accessed | tf_op | source)
XLA Modules:
  0.0 81.9 jit_solution(25647062520290176)
XLA Ops:
  0.6 0.0 copy-start.1
  0.6 0.9 %copy-done.1 = bf16[1,128,512]{2,1,0:T(8,128)(2,1)S(1)} copy-done((bf16[1,128,512]{2,1,0:T(8,128)(2,1)S(1)}, bf16[1,128,512]{2,1,0:T(8,128)(2,1)}, u32[]{:S(2)}) %copy-start.1) | copy-done | bytes 131096
  1.5 0.0 copy-start.2
  1.5 0.9 %copy-done.2 = bf16[1,128,512]{2,1,0:T(8,128)(2,1)S(1)} copy-done((bf16[1,128,512]{2,1,0:T(8,128)(2,1)S(1)}, bf16[1,128,512]{2,1,0:T(8,128)(2,1)}, u32[]{:S(2)}) %copy-start.2) | copy-done | bytes 131096
  2.4 0.0 copy-start.3
  2.4 0.9 %copy-done.3 = bf16[1,128,512]{2,1,0:T(8,128)(2,1)S(1)} copy-done((bf16[1,128,512]{2,1,0:T(8,128)(2,1)S(1)}, bf16[1,128,512]{2,1,0:T(8,128)(2,1)}, u32[]{:S(2)}) %copy-start.3) | copy-done | bytes 131096
  3.3 0.0 copy-start.4
  3.3 0.9 %copy-done.4 = bf16[64,1024]{1,0:T(8,128)(2,1)S(1)} copy-done((bf16[64,1024]{1,0:T(8,128)(2,1)S(1)}, bf16[64,1024]{1,0:T(8,128)(2,1)}, u32[]{:S(2)}) %copy-start.4) | copy-done | bytes 131096
  4.3 0.3 pack.1
  4.6 0.5 collective-permute-start
  5.1 0.7 broadcast_in_dim.6
  5.7 5.9 %all-to-all-start = ((bf16[4,64,256]{2,1,0:T(8,128)(2,1)}), bf16[4,64,256]{2,1,0:T(8,128)(2,1)S(1)}, u32[]{:S(2)}, u32[]{:S(2)}) async-start(bf16[4,64,256]{2,1,0:T(8,128)(2,1)} %broadcast_in_dim.6), calls=%async_computation | async-start | bytes 262144 | tf_op jit(solution)/shard_map/all_to_all | solution.py:305
  11.6 0.0 collective-permute-done.pair
  11.6 0.9 %state.1 = (f32[128,128]{1,0:T(8,128)S(1)}, bf16[4,128,128]{2,1,0:T(8,128)(2,1)}) custom-call(bf16[128,768]{1,0:T(8,128)(2,1)S(1)} %get-tuple-element.36.mine, bf16[128,768]{1,0:T(8,128)(2,1)S(1)} %collective-permute-done.pair), custom_call_target="tpu_custom_call" | custom-call | flops 16777216 | bytes 589824 | tf_op jit(solution)/shard_map/state/pallas_call | solution.py:66
  12.5 5.5 %all-to-all-done = bf16[4,64,256]{2,1,0:T(8,128)(2,1)S(1)} async-done(((bf16[4,64,256]{2,1,0:T(8,128)(2,1)}), bf16[4,64,256]{2,1,0:T(8,128)(2,1)S(1)}, u32[]{:S(2)}, u32[]{:S(2)}) %all-to-all-start) | async-done | bytes 131104 | tf_op jit(solution)/shard_map/all_to_all | solution.py:305
  18.0 3.3 %all-to-all-start.2 = ((bf16[4,128,128]{2,1,0:T(8,128)(2,1)}), bf16[4,128,128]{2,1,0:T(8,128)(2,1)S(1)}, u32[]{:S(2)}, u32[]{:S(2)}) async-start(bf16[4,128,128]{2,1,0:T(8,128)(2,1)} %get-tuple-element.51), calls=%async_computation.2 | async-start | bytes 262144 | tf_op jit(solution)/shard_map/all_to_all | solution.py:305
  21.4 5.9 %all-to-all-done.2.others = bf16[4,128,128]{2,1,0:T(8,128)(2,1)S(1)} async-done(((bf16[4,128,128]{2,1,0:T(8,128)(2,1)}), bf16[4,128,128]{2,1,0:T(8,128)(2,1)S(1)}, u32[]{:S(2)}, u32[]{:S(2)}) %all-to-all-start.2) | async-done | bytes 131104 | tf_op jit(solution)/shard_map/all_to_all | solution.py:305
  27.3 0.9 %broadcast_in_dim.7 = bf16[4,2,2,64,256]{4,3,2,1,0:T(8,128)(2,1)} broadcast(bf16[2,2,64,256]{3,2,1,0:T(8,128)(2,1)S(1)} %copy.11), dimensions={1,2,3,4} | broadcast | bytes 655360 | tf_op jit(solution)/shard_map/broadcast_in_dim | solution.py:322
  28.1 0.0 copy-start
  28.1 3.9 %all-to-all-start.1 = ((bf16[8,2,64,256]{3,2,1,0:T(8,128)(2,1)}), bf16[8,2,64,256]{3,2,1,0:T(8,128)(2,1)S(1)}, u32[]{:S(2)}, u32[]{:S(2)}) async-start(bf16[8,2,64,256]{3,2,1,0:T(8,128)(2,1)} %bitcast.6), calls=%async_computation.1 | async-start | bytes 1048576 | tf_op jit(solution)/shard_map/all_to_all | solution.py:305
  32.0 0.0 copy-done
  32.0 0.5 collective-permute-start.1
  32.5 1.1 %collective-permute-start.2 = (bf16[128,256]{1,0:T(8,128)(2,1)S(1)}, bf16[128,256]{1,0:T(8,128)(2,1)S(1)}, u32[]{:S(2)}, u32[]{:S(2)}) collective-permute-start(bf16[128,256]{1,0:T(8,128)(2,1)S(1)} %get-tuple-element.38), channel_id=1, source_target_pairs={{0,7},{1,2},{2,1},{3,4},{4,3},{5,6},{6,5},{7,0},{8,15},{9,10},{10,... | collective-permute-start | bytes 196616 | tf_op jit(solution)/shard_map/ppermute | solution.py:317
  33.6 1.0 %collective-permute-start.3 = (bf16[128,256]{1,0:T(8,128)(2,1)S(1)}, bf16[128,256]{1,0:T(8,128)(2,1)S(1)}, u32[]{:S(2)}, u32[]{:S(2)}) collective-permute-start(bf16[128,256]{1,0:T(8,128)(2,1)S(1)} %get-tuple-element.39), channel_id=1, source_target_pairs={{0,6},{1,3},{2,0},{3,5},{4,2},{5,7},{6,4},{7,1},{8,14},{9,11},{10,... | collective-permute-start | bytes 196616 | tf_op jit(solution)/shard_map/ppermute | solution.py:318
  34.5 3.6 %collective-permute-done.2.near = bf16[128,256]{1,0:T(8,128)(2,1)S(1)} collective-permute-done((bf16[128,256]{1,0:T(8,128)(2,1)S(1)}, bf16[128,256]{1,0:T(8,128)(2,1)S(1)}, u32[]{:S(2)}, u32[]{:S(2)}) %collective-permute-start.2) | collective-permute-done | bytes 65568 | tf_op jit(solution)/shard_map/ppermute | solution.py:317
  38.1 0.7 collective-permute-done.3.far
  38.8 0.0 collective-permute-done.1.og_recv
  38.8 1.1 %soft_forward.1 = (bf16[256,128]{1,0:T(8,128)(2,1)S(1)}, bf16[512,128]{1,0:T(8,128)(2,1)S(1)}, bf16[512,128]{1,0:T(8,128)(2,1)S(1)}, bf16[256,1024]{1,0:T(8,128)...) custom-call(bf16[128,768]{1,0:T(8,128)(2,1)S(1)} %get-tuple-element.36.mine, ...), custom_call_target="tpu_custom_call" | custom-call | flops 67108864 | bytes 2621440 | tf_op jit(solution)/shard_map/soft_forward/pallas_call | solution.py:66
  40.0 0.2 stack.9
  40.2 0.0 copy-start.5
  40.2 0.7 copy-done.5
  40.8 0.6 lin_forward.1
  41.5 0.2 stack.10
  41.7 0.4 maximum_bitcast_fusion
  42.0 0.9 %copy.12 = bf16[4,2,2,64,256]{4,3,2,1,0:T(8,128)(2,1)} copy(bf16[4,2,2,64,256]{4,0,3,1,2:T(4,128)(2,1)S(1)} %maximum_bitcast_fusion) | data formatting | bytes 1048576 | tf_op jit(solution)/shard_map/transpose | solution.py:391
  42.9 0.0 all-to-all-done.1
  42.9 4.3 %all-to-all-start.3 = ((bf16[8,2,64,256]{3,2,1,0:T(8,128)(2,1)}), bf16[8,2,64,256]{3,2,1,0:T(8,128)(2,1)S(1)}, u32[]{:S(2)}, u32[]{:S(2)}) async-start(bf16[8,2,64,256]{3,2,1,0:T(8,128)(2,1)} %bitcast.23), calls=%async_computation.3 | async-start | bytes 1048576 | tf_op jit(solution)/shard_map/all_to_all | solution.py:305
  47.2 0.3 d_attn.1.dattn
  47.6 0.5 lin_backward.1
  48.0 8.9 %all-to-all-done.3 = bf16[8,2,64,256]{3,2,1,0:T(8,128)(2,1)S(1)} async-done(((bf16[8,2,64,256]{3,2,1,0:T(8,128)(2,1)}), bf16[8,2,64,256]{3,2,1,0:T(8,128)(2,1)S(1)}, u32[]{:S(2)}, u32[]{:S(2)}) %all-to-all-start.3) | async-done | bytes 524320 | tf_op jit(solution)/shard_map/all_to_all | solution.py:305
  57.0 0.8 weight_rows.1
  57.8 3.4 %all-to-all-start.4 = ((bf16[4,256,128]{2,1,0:T(8,128)(2,1)}), bf16[4,256,128]{2,1,0:T(8,128)(2,1)S(1)}, u32[]{:S(2)}, u32[]{:S(2)}) async-start(bf16[4,256,128]{2,1,0:T(8,128)(2,1)} %weight_rows.1), calls=%async_computation.4 | async-start | bytes 524288 | tf_op jit(solution)/shard_map/all_to_all | solution.py:305
  61.2 0.7 soft_backward.1
  61.9 6.0 %all-to-all-done.4.parts = bf16[4,256,128]{2,1,0:T(8,128)(2,1)S(1)} async-done(((bf16[4,256,128]{2,1,0:T(8,128)(2,1)}), bf16[4,256,128]{2,1,0:T(8,128)(2,1)S(1)}, u32[]{:S(2)}, u32[]{:S(2)}) %all-to-all-start.4) | async-done | bytes 262176 | tf_op jit(solution)/shard_map/all_to_all | solution.py:305
  67.9 0.7 weight_sum.1
  68.6 4.4 %all-to-all-start.5 = ((f32[4,64,256]{2,1,0:T(8,128)}), f32[4,64,256]{2,1,0:T(8,128)S(1)}, u32[]{:S(2)}, u32[]{:S(2)}) async-start(f32[4,64,256]{2,1,0:T(8,128)} %weight_sum.1), calls=%async_computation.5 | async-start | bytes 524288 | tf_op jit(solution)/shard_map/all_to_all | solution.py:305
  73.1 0.3 lin_final.1
  73.4 0.1 collective-permute-start.4
  73.5 1.6 %collective-permute-start.5 = (bf16[128,256]{1,0:T(8,128)(2,1)S(1)}, bf16[128,256]{1,0:T(8,128)(2,1)S(1)}, u32[]{:S(2)}, u32[]{:S(2)}) collective-permute-start(bf16[128,256]{1,0:T(8,128)(2,1)S(1)} %get-tuple-element.63), channel_id=1, source_target_pairs={{0,7},{1,2},{2,1},{3,4},{4,3},{5,6},{6,5},{7,0},{8,15},{9,10},{10,... | collective-permute-start | bytes 196616 | tf_op jit(solution)/shard_map/ppermute | solution.py:385
  75.0 0.6 collective-permute-start.6
  75.6 2.8 %all-to-all-done.5.parts = f32[4,64,256]{2,1,0:T(8,128)S(1)} async-done(((f32[4,64,256]{2,1,0:T(8,128)}), f32[4,64,256]{2,1,0:T(8,128)S(1)}, u32[]{:S(2)}, u32[]{:S(2)}) %all-to-all-start.5) | async-done | bytes 262176 | tf_op jit(solution)/shard_map/all_to_all | solution.py:305
  78.5 0.7 weight_join.1
  79.2 0.0 collective-permute-done.5.near
  79.2 1.9 %collective-permute-done.6.far = bf16[128,256]{1,0:T(8,128)(2,1)S(1)} collective-permute-done((bf16[128,256]{1,0:T(8,128)(2,1)S(1)}, bf16[128,256]{1,0:T(8,128)(2,1)S(1)}, u32[]{:S(2)}, u32[]{:S(2)}) %collective-permute-start.6) | collective-permute-done | bytes 65568 | tf_op jit(solution)/shard_map/ppermute | solution.py:386
  81.1 0.0 collective-permute-done.4.pair
  81.1 0.8 outputs.1
  (2 shorter events, 0.0 us)
Async XLA Ops:
  0.6 0.9 %copy-start.1 = (bf16[1,128,512]{2,1,0:T(8,128)(2,1)S(1)}, bf16[1,128,512]{2,1,0:T(8,128)(2,1)}, u32[]{:S(2)}) copy-start(bf16[1,128,512]{2,1,0:T(8,128)(2,1)} %param.6) | copy-start | bytes 393220
  1.5 0.9 %copy-start.2 = (bf16[1,128,512]{2,1,0:T(8,128)(2,1)S(1)}, bf16[1,128,512]{2,1,0:T(8,128)(2,1)}, u32[]{:S(2)}) copy-start(bf16[1,128,512]{2,1,0:T(8,128)(2,1)} %param.7) | copy-start | bytes 393220
  2.4 0.9 %copy-start.3 = (bf16[1,128,512]{2,1,0:T(8,128)(2,1)S(1)}, bf16[1,128,512]{2,1,0:T(8,128)(2,1)}, u32[]{:S(2)}) copy-start(bf16[1,128,512]{2,1,0:T(8,128)(2,1)} %param.8) | copy-start | bytes 393220
  3.3 0.9 %copy-start.4 = (bf16[64,1024]{1,0:T(8,128)(2,1)S(1)}, bf16[64,1024]{1,0:T(8,128)(2,1)}, u32[]{:S(2)}) copy-start(bf16[64,1024]{1,0:T(8,128)(2,1)} %w.1) | copy-start | bytes 393220
  4.6 7.1 %collective-permute-start = (bf16[128,768]{1,0:T(8,128)(2,1)S(1)}, bf16[128,768]{1,0:T(8,128)(2,1)S(1)}, u32[]{:S(2)}, u32[]{:S(2)}) collective-permute-start(bf16[128,768]{1,0:T(8,128)(2,1)S(1)} %get-tuple-element.37), channel_id=1, source_target_pairs={{0,1},{1,0},{2,3},{3,2},{4,5},{5,4},{6,7},{7,6},{8,9},{9,8},{10,11... | collective-permute-start | bytes 589832 | tf_op jit(solution)/shard_map/ppermute | solution.py:316
  5.7 12.3 %all-to-all-start = ((bf16[4,64,256]{2,1,0:T(8,128)(2,1)}), bf16[4,64,256]{2,1,0:T(8,128)(2,1)S(1)}, u32[]{:S(2)}, u32[]{:S(2)}) async-start(bf16[4,64,256]{2,1,0:T(8,128)(2,1)} %broadcast_in_dim.6), calls=%async_computation | async-start | bytes 262144 | tf_op jit(solution)/shard_map/all_to_all | solution.py:305
  18.0 9.2 %all-to-all-start.2 = ((bf16[4,128,128]{2,1,0:T(8,128)(2,1)}), bf16[4,128,128]{2,1,0:T(8,128)(2,1)S(1)}, u32[]{:S(2)}, u32[]{:S(2)}) async-start(bf16[4,128,128]{2,1,0:T(8,128)(2,1)} %get-tuple-element.51), calls=%async_computation.2 | async-start | bytes 262144 | tf_op jit(solution)/shard_map/all_to_all | solution.py:305
  28.1 3.9 %copy-start = (bf16[1,128,1024]{2,1,0:T(8,128)(2,1)S(1)}, bf16[1,128,1024]{2,1,0:T(8,128)(2,1)}, u32[]{:S(2)}) copy-start(bf16[1,128,1024]{2,1,0:T(8,128)(2,1)} %param.9) | copy-start | bytes 786436
  28.1 14.8 %all-to-all-start.1 = ((bf16[8,2,64,256]{3,2,1,0:T(8,128)(2,1)}), bf16[8,2,64,256]{3,2,1,0:T(8,128)(2,1)S(1)}, u32[]{:S(2)}, u32[]{:S(2)}) async-start(bf16[8,2,64,256]{3,2,1,0:T(8,128)(2,1)} %bitcast.6), calls=%async_computation.1 | async-start | bytes 1048576 | tf_op jit(solution)/shard_map/all_to_all | solution.py:305
  32.0 6.8 %collective-permute-start.1 = (bf16[128,1024]{1,0:T(8,128)(2,1)S(1)}, bf16[128,1024]{1,0:T(8,128)(2,1)S(1)}, u32[]{:S(2)}, u32[]{:S(2)}) collective-permute-start(bf16[128,1024]{1,0:T(8,128)(2,1)S(1)} %bitcast.16), channel_id=1, source_target_pairs={{0,1},{1,0},{2,3},{3,2},{4,5},{5,4},{6,7},{7,6},{8,9},{9,8},{10,11... | collective-permute-start | bytes 786440 | tf_op jit(solution)/shard_map/ppermute | solution.py:307
  32.5 5.7 %collective-permute-start.2 = (bf16[128,256]{1,0:T(8,128)(2,1)S(1)}, bf16[128,256]{1,0:T(8,128)(2,1)S(1)}, u32[]{:S(2)}, u32[]{:S(2)}) collective-permute-start(bf16[128,256]{1,0:T(8,128)(2,1)S(1)} %get-tuple-element.38), channel_id=1, source_target_pairs={{0,7},{1,2},{2,1},{3,4},{4,3},{5,6},{6,5},{7,0},{8,15},{9,10},{10,... | collective-permute-start | bytes 196616 | tf_op jit(solution)/shard_map/ppermute | solution.py:317
  33.6 5.2 %collective-permute-start.3 = (bf16[128,256]{1,0:T(8,128)(2,1)S(1)}, bf16[128,256]{1,0:T(8,128)(2,1)S(1)}, u32[]{:S(2)}, u32[]{:S(2)}) collective-permute-start(bf16[128,256]{1,0:T(8,128)(2,1)S(1)} %get-tuple-element.39), channel_id=1, source_target_pairs={{0,6},{1,3},{2,0},{3,5},{4,2},{5,7},{6,4},{7,1},{8,14},{9,11},{10,... | collective-permute-start | bytes 196616 | tf_op jit(solution)/shard_map/ppermute | solution.py:318
  40.2 0.7 copy-start.5
  42.9 14.0 %all-to-all-start.3 = ((bf16[8,2,64,256]{3,2,1,0:T(8,128)(2,1)}), bf16[8,2,64,256]{3,2,1,0:T(8,128)(2,1)S(1)}, u32[]{:S(2)}, u32[]{:S(2)}) async-start(bf16[8,2,64,256]{3,2,1,0:T(8,128)(2,1)} %bitcast.23), calls=%async_computation.3 | async-start | bytes 1048576 | tf_op jit(solution)/shard_map/all_to_all | solution.py:305
  57.8 10.2 %all-to-all-start.4 = ((bf16[4,256,128]{2,1,0:T(8,128)(2,1)}), bf16[4,256,128]{2,1,0:T(8,128)(2,1)S(1)}, u32[]{:S(2)}, u32[]{:S(2)}) async-start(bf16[4,256,128]{2,1,0:T(8,128)(2,1)} %weight_rows.1), calls=%async_computation.4 | async-start | bytes 524288 | tf_op jit(solution)/shard_map/all_to_all | solution.py:305
  68.6 9.8 %all-to-all-start.5 = ((f32[4,64,256]{2,1,0:T(8,128)}), f32[4,64,256]{2,1,0:T(8,128)S(1)}, u32[]{:S(2)}, u32[]{:S(2)}) async-start(f32[4,64,256]{2,1,0:T(8,128)} %weight_sum.1), calls=%async_computation.5 | async-start | bytes 524288 | tf_op jit(solution)/shard_map/all_to_all | solution.py:305
  73.4 7.7 %collective-permute-start.4 = (bf16[128,768]{1,0:T(8,128)(2,1)S(1)}, bf16[128,768]{1,0:T(8,128)(2,1)S(1)}, u32[]{:S(2)}, u32[]{:S(2)}) collective-permute-start(bf16[128,768]{1,0:T(8,128)(2,1)S(1)} %get-tuple-element.62), channel_id=1, source_target_pairs={{0,1},{1,0},{2,3},{3,2},{4,5},{5,4},{6,7},{7,6},{8,9},{9,8},{10,11... | collective-permute-start | bytes 589832 | tf_op jit(solution)/shard_map/ppermute | solution.py:420
  73.5 5.7 %collective-permute-start.5 = (bf16[128,256]{1,0:T(8,128)(2,1)S(1)}, bf16[128,256]{1,0:T(8,128)(2,1)S(1)}, u32[]{:S(2)}, u32[]{:S(2)}) collective-permute-start(bf16[128,256]{1,0:T(8,128)(2,1)S(1)} %get-tuple-element.63), channel_id=1, source_target_pairs={{0,7},{1,2},{2,1},{3,4},{4,3},{5,6},{6,5},{7,0},{8,15},{9,10},{10,... | collective-permute-start | bytes 196616 | tf_op jit(solution)/shard_map/ppermute | solution.py:385
  75.0 6.1 %collective-permute-start.6 = (bf16[128,256]{1,0:T(8,128)(2,1)S(1)}, bf16[128,256]{1,0:T(8,128)(2,1)S(1)}, u32[]{:S(2)}, u32[]{:S(2)}) collective-permute-start(bf16[128,256]{1,0:T(8,128)(2,1)S(1)} %get-tuple-element.64), channel_id=1, source_target_pairs={{6,0},{3,1},{0,2},{5,3},{2,4},{7,5},{4,6},{1,7},{14,8},{11,9},{8,1... | collective-permute-start | bytes 196616 | tf_op jit(solution)/shard_map/ppermute | solution.py:386

commit v3 on v2

v3 whole, which is shorter than its diff:
```python
import functools
import math

import jax
import jax.numpy as jnp
from jax import lax
from jax.experimental import pallas as pl
from jax.experimental.pallas import tpu as pltpu
from jax.sharding import Mesh
from jax.sharding import PartitionSpec as P

DH = 128
SOFT_HEADS = 2
LIN_HEADS = 2
HEADS = SOFT_HEADS + LIN_HEADS
WINDOW = 256
HALF = 128
norm_eps = 1e-06
FACTOR = DH ** (-0.5)
BF = jnp.bfloat16
F32 = jnp.float32
NN = (((1,), (0,)), ((), ()))
NT = (((1,), (1,)), ((), ()))
TN = (((0,), (0,)), ((), ()))


def unit_plus(values):
    return jnp.where(values > 0, values + 1.0, jnp.exp(jnp.minimum(values, 0.0)))


def unit_slope(values):
    return jnp.where(values > 0, 1.0, jnp.exp(jnp.minimum(values, 0.0)))


def mm(a, b, dims=NN):
    return lax.dot_general(a, b, dims, preferred_element_type=F32)


def halves(x):
    high = x.astype(BF)
    return high, (x - high.astype(F32)).astype(BF)


def mm3(a, b, dims=NN):
    a_high, a_low = halves(a)
    b_high, b_low = halves(b)
    return mm(a_high, b_high, dims) + (mm(a_high, b_low, dims) + mm(a_low, b_high, dims))


def mm2(a, b, dims=NN):
    a_high, a_low = halves(a)
    return mm(a_high, b, dims) + mm(a_low, b, dims)


def at(start, size=DH):
    return pl.ds(pl.multiple_of(start, size), size)


def places():
    return lax.axis_index("core"), lax.axis_index("z"), lax.axis_index("dp")


def call(kernel, name, outs, args, scratch=(), flops=0, spaces=None):
    vmem = pl.BlockSpec(memory_space=pltpu.VMEM)
    size = sum(math.prod(x.shape) * x.dtype.itemsize for x in list(args) + list(outs))
    return pl.pallas_call(
        kernel,
        name=name,
        out_shape=list(outs),
        in_specs=spaces or [vmem] * len(args),
        out_specs=[vmem] * len(outs),
        scratch_shapes=list(scratch),
        compiler_params=pltpu.CompilerParams(vmem_limit_bytes=24 * 2**20),
        cost_estimate=pl.CostEstimate(flops=flops, bytes_accessed=size, transcendentals=0),
    )(*args)


def like(shape, dtype):
    return jax.ShapeDtypeStruct(shape, dtype)


QS, KS, VS, QL, KL, VL = (slice(i * DH, (i + 1) * DH) for i in range(6))
SOFT = SOFT_HEADS * DH


def links(direct):
    core, z, dp = places()
    step = 1 + core
    turn = lax.rem(z + core, 2) if direct else 1
    return dict(
        first=1 + 2 * core, second=3 - 2 * core, step=step, other=3 - step,
        block_a=1 - turn, block_b=turn,
        halo_a=(1 - turn if direct else 1), halo_b=(turn if direct else 0),
    )


def pack_kernel(q, k, v, og, w, gain, mine_out, other_out, og_out, w_out, gain_out, sems):
    core, _, dp = places()
    mine, other = core * DH, (1 - core) * DH
    copies = []

    def fetch(source, target):
        copy = pltpu.make_async_copy(source, target, sems.at[len(copies)])
        copy.start()
        copies.append(copy)

    for index, array in enumerate((q, k, v)):
        for group in range(2):
            cols = slice((3 * group + index) * DH, (3 * group + index + 1) * DH)
            fetch(array.at[:, at(SOFT * group + other)], other_out.at[:, cols])
            fetch(array.at[:, at(SOFT * group + mine)], mine_out.at[:, cols])
    fetch(og, og_out)
    width = w_out.shape[1]
    fetch(w.at[:, at(dp * width, width)], w_out)
    fetch(gain, gain_out)
    for copy in copies:
        copy.wait()


def state_kernel(direct, mine, pair, w, state, to_a, to_b, *to_c):
    core, _, _ = places()
    total = mm2(unit_plus(mine[:, KL].astype(F32)), mine[:, VL], TN) + mm2(
        unit_plus(pair[:, KL].astype(F32)), pair[:, VL], TN
    )
    state[...] = total
    way = links(direct)
    for out, block in ((to_a, way["block_a"]), (to_b, way["block_b"])):
        here = block == core
        out[:, :DH] = jnp.where(here, mine[:, KS], pair[:, KS])
        out[:, DH : 2 * DH] = jnp.where(here, mine[:, VS], pair[:, VS])
    if direct:
        rows = w.shape[0]
        for out, first in ((to_a, 2 * DH), (to_b, 2 * DH), (to_c[0], 0)):
            out[:, first : first + DH] = total.astype(BF)
            out[:rows, first + DH :] = w[:, :DH]
            out[rows:, first + DH :] = w[:, DH:]


def relay_kernel(w, a, b, c, keep, send, heads):
    core, z, _ = places()
    way = links(True)
    rows = w.shape[0]
    heads[z] = w[...]
    for source, first, step in ((a, 3 * DH, way["first"]), (b, 3 * DH, way["second"]), (c, DH, 2)):
        heads[z ^ step, :, :DH] = source[:rows, first:]
        heads[z ^ step, :, DH:] = source[rows:, first:]
    for group in range(2):
        keep[group] = heads[2 * group + core]
        send[group] = heads[2 * group + 1 - core]


def weight_parts(direct, attn, ogs, send, keep):
    if not direct:
        keep[...] = mm(attn, ogs[...], TN)
        return
    _, _, dp = places()
    way = links(True)
    width = send.shape[1] // 2
    for index, step in enumerate((0, way["other"])):
        cols = slice(index * width, (index + 1) * width)
        keep[:, cols] = mm(attn, ogs[:, at((dp ^ step) * width, width)], TN)
        send[:, cols] = mm(attn, ogs[:, at((dp ^ step ^ way["step"]) * width, width)], TN).astype(BF)


def soft_forward_kernel(
    direct, mine, pair, og, og_recv, a, b, qs, ks, vs, ogs, probs, attn, keep, *send
):
    core, _, _ = places()
    way = links(direct)
    rows = og.shape[0]
    own_at, pair_at = core * rows, (1 - core) * rows
    for source, first in ((mine, own_at), (pair, pair_at)):
        qs[at(first, rows), :] = source[:, QS]
        ks[at(HALF + first, rows), :] = source[:, KS]
        vs[at(HALF + first, rows), :] = source[:, VS]
    for source, side in ((a, way["halo_a"]), (b, way["halo_b"])):
        first = side * (HALF + 2 * rows)
        ks[at(first), :] = source[:, :DH]
        vs[at(first), :] = source[:, DH : 2 * DH]
    ogs[at(own_at, rows), :] = og[...]
    ogs[at(pair_at, rows), :] = og_recv[...]
    span = rows + 2 * HALF
    row_pos = lax.broadcasted_iota(jnp.int32, (rows, span), 0)
    col_pos = lax.broadcasted_iota(jnp.int32, (rows, span), 1)
    inside = (col_pos >= row_pos) & (col_pos < row_pos + WINDOW)
    for block in range(2):
        here, window = slice(block * rows, (block + 1) * rows), slice(block * rows, block * rows + span)
        scores = mm(qs[here, :], ks[window, :], NT) * FACTOR
        scores = jnp.where(inside, scores, -1e30)
        peak = jnp.max(scores, axis=1, keepdims=True)
        terms = jnp.where(inside, jnp.exp(scores - peak), 0.0)
        share = terms / jnp.sum(terms, axis=1, keepdims=True)
        probs[block] = share
        attn[here, :] = mm(share.astype(BF), vs[window, :]).astype(BF)
    weight_parts(direct, attn[...], ogs, send[0] if send else None, keep)


def lin_forward_kernel(direct, state, mine, pair, ogs, gain, *refs):
    core, _, _ = places()
    rows = mine.shape[0]
    total = state[...]
    if direct:
        a, b, c, soft_send, w_keep, w_recv, u_out, total_out, keep, out, send = refs
        total = total + a[:, 2 * DH : 3 * DH].astype(F32) + b[:, 2 * DH : 3 * DH].astype(F32)
        total = total + c[:, :DH].astype(F32)
    else:
        u_out, total_out, keep = refs
        send = None
    total_out[...] = total
    u_out[at(core * rows, rows), :] = mm3(unit_plus(mine[:, QL].astype(F32)), total)
    u_out[at((1 - core) * rows, rows), :] = mm3(unit_plus(pair[:, QL].astype(F32)), total)
    u = u_out[...]
    r = lax.rsqrt(jnp.mean(u * u, axis=1, keepdims=True) + norm_eps)
    attn = (gain[pl.ds(core, 1), :] * u * r).astype(BF)
    weight_parts(direct, attn, ogs, send, keep)
    if direct:
        wide = soft_send.shape[1]
        out[:DH, :wide] = soft_send[...]
        out[DH:, :wide] = send[...]
        half = w_keep.shape[1]
        for group in range(2):
            out[at(group * DH + core * half, half), wide:] = w_keep[group]
            out[at(group * DH + (1 - core) * half, half), wide:] = w_recv[group]


def fold_kernel(keep_soft, keep_lin, sent, got, keep, send):
    width = keep.shape[1]
    for rows, source in ((slice(0, DH), keep_soft), (slice(DH, 2 * DH), keep_lin)):
        keep[rows, :] = source[:, :width] + got[rows, :width].astype(F32)
        send[rows, :width] = (source[:, width:] + got[rows, width : 2 * width].astype(F32)).astype(BF)
    send[:, width : 2 * width] = sent[:, 2 * width :]
    send[:, 2 * width :] = got[:, 2 * width :]


def rows_kernel(keep, got, own, send, total):
    core, _, _ = places()
    half = DH // 2
    width = keep.shape[1]
    total[...] = keep[...] + got[:, :width].astype(F32)
    for group in range(2):
        out = slice(group * half, (group + 1) * half)
        own[out, :] = total[at(group * DH + core * half, half), :]
        send[out, :] = total[at(group * DH + (1 - core) * half, half), :]


def lin_backward(u, total, dattn, mine, pair, gain, dq_own, dq_pair, dstate, grads):
    core, _, _ = places()
    rows = mine.shape[0]
    u_all = u[...]
    r = lax.rsqrt(jnp.mean(u_all * u_all, axis=1, keepdims=True) + norm_eps)
    lin_grad = gain[pl.ds(core, 1), :] * dattn[:, DH:]
    grads[...] = r * lin_grad - u_all * (r * r * r) * jnp.mean(lin_grad * u_all, axis=1, keepdims=True)
    total_state = total[...]
    result = jnp.zeros(dstate.shape, F32)
    for first, source, out in ((core * rows, mine, dq_own), ((1 - core) * rows, pair, dq_pair)):
        wide = source[:, QL].astype(F32)
        part = grads[at(first, rows), :]
        result = result + mm3(unit_plus(wide), part, TN)
        out[...] = (mm3(part, total_state, NT) * unit_slope(wide)).astype(BF)
    dstate[...] = result


def soft_backward(qs, ks, vs, probs, attn, dattn, dq_all, dk_all, dv_all):
    rows = qs.shape[0] // 2
    span = rows + 2 * HALF
    dk_all[...] = jnp.zeros_like(dk_all)
    dv_all[...] = jnp.zeros_like(dv_all)
    for block in range(2):
        here, window = slice(block * rows, (block + 1) * rows), slice(block * rows, block * rows + span)
        grad = dattn[here, :DH].astype(BF)
        share = probs[block]
        delta = jnp.sum(grad.astype(F32) * attn[here, :].astype(F32), axis=1, keepdims=True)
        dscore = (share * (mm(grad, vs[window, :], NT) - delta)).astype(BF)
        dq_all[here, :] = mm(dscore, ks[window, :]) * FACTOR
        dk_all[window, :] += mm(dscore, qs[here, :], TN) * FACTOR
        dv_all[window, :] += mm(share.astype(BF), grad, TN)


def backward_kernel(direct, *refs):
    if direct:
        sent, got = refs[:2]
        refs = refs[2:]
    else:
        weights = refs[0]
        refs = refs[1:]
    (ogs, u, total, mine, pair, gain, qs, ks, vs, probs, attn,
     dq_lin, dq_lin_pair, dstate, dq_soft, dk_soft, dv_soft, dattn, grads, *scratch) = refs
    if direct:
        _, _, dp = places()
        way = links(True)
        weights = scratch[0]
        width = weights.shape[1] // 4
        for source, index, step in (
            (sent, 1, 0), (sent, 2, way["step"]), (got, 1, way["other"]), (got, 2, 3),
        ):
            weights[:, at((dp ^ step) * width, width)] = source[:, index * width : (index + 1) * width]
    dattn[...] = mm(ogs[...], weights[...], NT)
    lin_backward(u, total, dattn, mine, pair, gain, dq_lin, dq_lin_pair, dstate, grads)
    soft_backward(qs, ks, vs, probs, attn, dattn, dq_soft, dk_soft, dv_soft)


def halo_kernel(direct, dk_soft, dv_soft, *refs):
    core, z, _ = places()
    way = links(direct)
    span = dk_soft.shape[0]
    if direct:
        dstate, own, got, to_a, to_b, to_c, chunk, heads = refs
        half = own.shape[0] // 2
        for group in range(2):
            rows = slice(group * half, (group + 1) * half)
            heads[2 * group + core] = own[rows, :]
            heads[2 * group + 1 - core] = got[rows, :]
        chunk[...] = heads[z]
        for out, first, step in ((to_a, 2 * DH, way["first"]), (to_b, 2 * DH, way["second"]), (to_c, 0, 2)):
            out[:, first : first + DH] = dstate[...].astype(BF)
            out[:half, first + DH :] = heads[z ^ step, :, :DH].astype(BF)
            out[half:, first + DH :] = heads[z ^ step, :, DH:].astype(BF)
    else:
        to_a, to_b = refs
    for out, side in ((to_a, way["halo_a"]), (to_b, way["halo_b"])):
        first = side * (span - HALF)
        out[:, :DH] = dk_soft[at(first), :].astype(BF)
        out[:, DH : 2 * DH] = dv_soft[at(first), :].astype(BF)


def final_kernel(
    direct, scale, dstate, mine, pair, dq_soft, dk_soft, dv_soft, dq_lin, dq_lin_pair, a, b, *refs
):
    core, _, _ = places()
    way = links(direct)
    rows = mine.shape[0]
    total = dstate[...]
    if direct:
        c, chunk, own_out, pair_out, weight_out, dk_all, dv_all = refs
        total = total + a[:, 2 * DH : 3 * DH].astype(F32) + b[:, 2 * DH : 3 * DH].astype(F32)
        total = total + c[:, :DH].astype(F32)
        half = chunk.shape[0]
        for side in range(2):
            cols, part = slice(side * DH, (side + 1) * DH), slice(side * half, (side + 1) * half)
            weight_out[:, cols] = scale * (
                chunk[:, cols] + a[part, 3 * DH :].astype(F32) + b[part, 3 * DH :].astype(F32)
                + c[part, DH:].astype(F32)
            )
    else:
        own_out, pair_out, dk_all, dv_all = refs
    for source, out, cols in ((dk_soft, dk_all, slice(0, DH)), (dv_soft, dv_all, slice(DH, 2 * DH))):
        out[...] = source[HALF : HALF + 2 * rows, :]
        out[at(way["block_a"] * rows, rows), :] += a[:, cols].astype(F32)
        out[at(way["block_b"] * rows, rows), :] += b[:, cols].astype(F32)
    high, low = halves(total)
    for source, dq, out, place in ((mine, dq_lin, own_out, core), (pair, dq_lin_pair, pair_out, 1 - core)):
        here = at(place * rows, rows)
        out[:, QS] = dq_soft[here, :].astype(BF)
        out[:, KS] = dk_all[here, :].astype(BF)
        out[:, VS] = dv_all[here, :].astype(BF)
        wide, values = source[:, KL].astype(F32), source[:, VL]
        out[:, QL] = dq[...]
        out[:, KL] = ((mm(values, high, NT) + mm(values, low, NT)) * unit_slope(wide)).astype(BF)
        out[:, VL] = mm3(unit_plus(wide), total).astype(BF)


def output_kernel(own, pair, dq, dk, dv):
    core, _, _ = places()
    for source, first in ((own, core * DH), (pair, (1 - core) * DH)):
        for index, out in enumerate((dq, dk, dv)):
            out[0, :, at(first)] = source[:, index * DH : (index + 1) * DH]
            out[0, :, at(SOFT + first)] = source[:, (3 + index) * DH : (4 + index) * DH]


def pair_up_kernel(first, second, out):
    width = first.shape[1]
    out[:, :width] = first[...]
    out[:, width:] = second[...]


def weight_join_kernel(both, got, out):
    _, _, dp = places()
    way = links(True)
    width = both.shape[1] // 2
    for source, index, step in ((both, 0, 0), (both, 1, way["step"]), (got, 0, way["other"]), (got, 1, 3)):
        out[:, at((dp ^ step) * width, width)] = source[:, index * width : (index + 1) * width].astype(F32)


def body(n_dp, n_z, queries, key_rows, value_rows, out_grad, out_weight, norm_gain):
    q, k, v, og = queries[0], key_rows[0], value_rows[0], out_grad[0]
    rows, model = og.shape
    axes = ("z", "core")
    pair_perm = [(0, 1), (1, 0)]
    core = lax.axis_index("core")
    direct = n_z == HEADS and n_dp == 4
    width = model // n_dp
    half = DH // 2

    def over_core(value):
        return lax.ppermute(value, "core", pair_perm)

    def over_z(value, which, back=False):
        pairs = []
        for z in range(n_z):
            for c in range(2):
                if direct:
                    there = z ^ (1 + 2 * c, 3 - 2 * c, 2)[which]
                else:
                    there = (z + (1 if (which == 1) != back else -1)) % n_z
                pairs.append((2 * z + c, 2 * there + c))
        return lax.ppermute(value, axes, pairs)

    def over_dp(value, which):
        pairs = [
            (2 * d + c, 2 * (d ^ (1 + c, 2 - c)[which]) + c) for d in range(n_dp) for c in range(2)
        ]
        return lax.ppermute(value, ("dp", "core"), pairs)

    og_recv = over_core(og)
    gain = norm_gain.reshape(LIN_HEADS, DH)
    mine, other, og_here, w_part, gain = call(
        pack_kernel, "pack",
        [
            like((rows, 6 * DH), BF), like((rows, 6 * DH), BF), like((rows, model), BF),
            like((out_weight.shape[0], width), BF), like((LIN_HEADS, DH), F32),
        ],
        [q, k, v, og, out_weight, gain], scratch=[pltpu.SemaphoreType.DMA((15,))],
        spaces=[pl.BlockSpec(memory_space=pltpu.HBM)] * 6,
    )
    pair = over_core(other)
    wide = 4 * DH if direct else 2 * DH
    state, to_a, to_b, *to_c = call(
        functools.partial(state_kernel, direct), "state",
        [like((DH, DH), F32), like((rows, wide), BF), like((rows, wide), BF)]
        + [like((rows, 2 * DH), BF)] * direct,
        [mine, pair, w_part],
        flops=4 * 2 * rows * DH * DH,
    )
    a, b = over_z(to_a, 0), over_z(to_b, 1)
    c = [over_z(value, 2) for value in to_c]
    if direct:
        w_keep, w_send = call(
            relay_kernel, "relay", [like((2, half, width), BF)] * 2, [w_part, a, b] + c,
            scratch=[pltpu.VMEM((HEADS, half, width), BF)],
        )
        w_recv = over_core(w_send)
    else:
        state = lax.psum(state, "z")
        weights = lax.all_gather(out_weight, axes, axis=0, tiled=True).reshape(2, 2, DH, model)
        weights = jnp.where(core == 0, weights[:, 0], weights[:, 1]).reshape(2 * DH, model)

    span = 2 * rows + 2 * HALF
    keep_width = 2 * width if direct else model
    wg_flops = 2 * 2 * rows * DH * model
    qs, ks, vs, ogs, probs, attn, keep_soft, *soft_send = call(
        functools.partial(soft_forward_kernel, direct), "soft_forward",
        [
            like((2 * rows, DH), BF), like((span, DH), BF), like((span, DH), BF),
            like((2 * rows, model), BF), like((2, rows, rows + 2 * HALF), F32), like((2 * rows, DH), BF),
            like((DH, keep_width), F32),
        ] + [like((DH, 2 * width), BF)] * direct,
        [mine, pair, og_here, og_recv, a, b],
        flops=wg_flops,
    )
    u, total, keep_lin, *sent = call(
        functools.partial(lin_forward_kernel, direct), "lin_forward",
        [like((2 * rows, DH), F32), like((DH, DH), F32), like((DH, keep_width), F32)]
        + [like((2 * DH, 3 * width), BF)] * direct,
        [state, mine, pair, ogs, gain] + ([a, b] + c + soft_send + [w_keep, w_recv] if direct else []),
        scratch=[pltpu.VMEM((DH, 2 * width), BF)] * direct,
        flops=wg_flops,
    )
    if direct:
        got = over_dp(sent[0], 0)
        keep, sent = call(
            fold_kernel, "fold", [like((2 * DH, width), F32), like((2 * DH, 3 * width), BF)],
            [keep_soft, keep_lin, sent[0], got],
        )
        got = over_dp(sent, 1)
        row_own, row_send = call(
            rows_kernel, "rows", [like((2 * half, width), F32)] * 2, [keep, got],
            scratch=[pltpu.VMEM((2 * DH, width), F32)],
        )
        row_recv = over_core(row_send)
        weights = [sent, got]
    else:
        weights = [weights]
    dq_lin, dq_lin_pair, dstate, dq_soft, dk_soft, dv_soft = call(
        functools.partial(backward_kernel, direct), "backward",
        [
            like((rows, DH), BF), like((rows, DH), BF), like((DH, DH), F32),
            like((2 * rows, DH), F32), like((span, DH), F32), like((span, DH), F32),
        ],
        weights + [ogs, u, total, mine, pair, gain, qs, ks, vs, probs, attn],
        scratch=[pltpu.VMEM((2 * rows, 2 * DH), F32), pltpu.VMEM((2 * rows, DH), F32)]
        + [pltpu.VMEM((2 * DH, model), BF)] * direct,
        flops=5 * wg_flops,
    )
    scale = 1.0 / math.sqrt(n_dp * n_z * 2 * rows)
    to_a, to_b, *rest = call(
        functools.partial(halo_kernel, direct), "halo",
        [like((rows, wide), BF), like((rows, wide), BF)]
        + [like((rows, 2 * DH), BF), like((half, width), F32)] * direct,
        [dk_soft, dv_soft] + ([dstate, row_own, row_recv] if direct else []),
        scratch=[pltpu.VMEM((HEADS, half, width), F32)] * direct,
    )
    a, b = over_z(to_a, 0, True), over_z(to_b, 1, True)
    if direct:
        rest = [over_z(rest[0], 2), rest[1]]
    else:
        dstate = lax.psum(dstate, "z")
        groups = jnp.stack([keep_soft, keep_lin])
        slots = jnp.stack([jnp.where(core == head, groups, 0.0) for head in range(2)], axis=1)
        local = lax.psum_scatter(
            slots.reshape(HEADS * DH, model), axes, scatter_dimension=0, tiled=True
        )
        weight_grad = lax.psum(local, "dp") * scale
    own_out, to_pair, *weight_part = call(
        functools.partial(final_kernel, direct, scale), "final",
        [like((rows, 6 * DH), BF), like((rows, 6 * DH), BF)] + [like((half, width), F32)] * direct,
        [dstate, mine, pair, dq_soft, dk_soft, dv_soft, dq_lin, dq_lin_pair, a, b] + rest,
        scratch=[pltpu.VMEM((2 * rows, DH), F32)] * 2,
        flops=wg_flops // 4,
    )
    from_pair = over_core(to_pair)
    if direct:
        got = over_dp(weight_part[0], 0)
        both = call(
            pair_up_kernel, "pair_up", [like((half, 2 * width), F32)], [weight_part[0], got]
        )[0]
        weight_grad = call(
            weight_join_kernel, "weight_join", [like((half, model), F32)], [both, over_dp(both, 1)]
        )[0]
    shape = like((1, rows, HEADS * DH), BF)
    dq, dk, dv = call(output_kernel, "outputs", [shape] * 3, [own_out, from_pair])
    return dq, dk, dv, weight_grad


def solution(mesh):
    n_dp, n_seq = mesh.shape["dp"], mesh.shape["seq"]
    blocks = Mesh(mesh.devices.reshape(n_dp, n_seq // 2, 2), ("dp", "z", "core"))
    tokens, heads = P("dp", ("z", "core"), None), P(("z", "core"), None)
    return jax.shard_map(
        functools.partial(body, n_dp, n_seq // 2),
        mesh=blocks,
        in_specs=(tokens, tokens, tokens, tokens, heads, P()),
        out_specs=(tokens, tokens, tokens, heads),
        check_vma=False,
    )
```

time: 82.7 us -> 64.8 us (0.78)
  starting transfers between devices: 30.5 us -> 16.4 us
  local copies, waits for them, and re-layouts: 7.1 us -> 4.29 us
  Pallas kernels: 7.82 us -> 6.83 us
    ppermute x7 -> x15, waiting for transfers between devices: 6.23 us -> 36.2 us  [the longest x4 18.8 us: over_dp(): return lax.ppermute(value, ('dp', 'core'), pairs)]
    all_to_all x6 -> x0, waiting for transfers between devices: 29.2 us -> none  [swap(): return lax.all_to_all(value, axis, 0, 0, tiled=True)]
    all_to_all x6 -> x0, starting transfers between devices: 25.2 us -> none  [swap(): return lax.all_to_all(value, axis, 0, 0, tiled=True)]
    ppermute x7 -> x15, starting transfers between devices: 5.27 us -> 16.4 us  [the longest x6 9.41 us: over_z(): return lax.ppermute(value, axes, pairs)]
    broadcast_in_dim x2 -> x0, local copies, waits for them, and re-layouts: 1.53 us -> none  [the longest x1 0.86 us: body(): jnp.broadcast_to(w_rows, (n_dp, 2, 2, half, width))]
    pallas_call x12 -> x13, Pallas kernels: 7.82 us -> 6.83 us  [call(): pl.pallas_call(kernel, name=name, out_shape=list(outs), in_specs=spaces o...]
    transpose x2 -> x0, local copies, waits for them, and re-layouts: 0.91 us -> none  [the longest x1 0.9 us: body(): groups = groups.transpose(3, 1, 0, 2, 4).reshape(2 * n_dp, 2, half, width)]
    unnamed x12 -> x10, local copies, waits for them, and re-layouts: 4.29 us -> 4.29 us
  transfers between devices with their start and end apart: 13 -> 15, of which waited for: 8 -> 8; matrix products, arithmetic and copies ran while one was open for 3% -> 0% of each run, Pallas kernels for 6% -> 6%
where the time goes in v3:
time: 64.8 us; the launch traced here: 64.5 us
  waiting for transfers between devices  36.2 us (56%)
  starting transfers between devices  16.4 us (25%)
  Pallas kernels  6.83 us (11%)
  local copies, waits for them, and re-layouts  4.29 us (7%)
  between operations  0.76 us (1%)
    ppermute x4, waiting for transfers between devices, over_dp(): return lax.ppermute(value, ('dp', 'core'), pairs)  18.8 us
    ppermute x6, waiting for transfers between devices, over_z(): return lax.ppermute(value, axes, pairs)  16.4 us
    ppermute x6, starting transfers between devices, over_z(): return lax.ppermute(value, axes, pairs)  9.41 us
    pallas_call x13, Pallas kernels, call(): pl.pallas_call(kernel, name=name, out_shape=list(outs), in_specs=spaces o...  6.83 us
    ppermute x4, starting transfers between devices, over_dp(): return lax.ppermute(value, ('dp', 'core'), pairs)  6.29 us
    unnamed x10, local copies, waits for them, and re-layouts  4.29 us
  transfers between devices with their start and end apart: 15, of which 8 were waited for; matrix products, arithmetic and copies ran while one was open for 0% of the time, Pallas kernels for 6%

profile of v3, /device:TPU:0, one launch (start us, length us, event | category | flops | bytes accessed | tf_op | source)
XLA Modules:
  0.0 64.5 jit_solution(12979945192672596990)
XLA Ops:
  0.6 0.0 copy-start.4
  0.6 0.7 %copy-done.4 = f32[256]{0:T(256)S(1)} copy-done((f32[256]{0:T(256)S(1)}, f32[256]{0:T(256)}, u32[]{:S(2)}) %copy-start.4) | copy-done | bytes 1048
  1.3 0.0 copy-start
  1.3 0.9 %copy-done = bf16[1,128,512]{2,1,0:T(8,128)(2,1)S(1)} copy-done((bf16[1,128,512]{2,1,0:T(8,128)(2,1)S(1)}, bf16[1,128,512]{2,1,0:T(8,128)(2,1)}, u32[]{:S(2)}) %copy-start) | copy-done | bytes 131096
  2.2 0.0 copy-start.1
  2.2 0.9 %copy-done.1 = bf16[1,128,512]{2,1,0:T(8,128)(2,1)S(1)} copy-done((bf16[1,128,512]{2,1,0:T(8,128)(2,1)S(1)}, bf16[1,128,512]{2,1,0:T(8,128)(2,1)}, u32[]{:S(2)}) %copy-start.1) | copy-done | bytes 131096
  3.1 0.0 copy-start.2
  3.1 0.9 %copy-done.2 = bf16[1,128,512]{2,1,0:T(8,128)(2,1)S(1)} copy-done((bf16[1,128,512]{2,1,0:T(8,128)(2,1)S(1)}, bf16[1,128,512]{2,1,0:T(8,128)(2,1)}, u32[]{:S(2)}) %copy-start.2) | copy-done | bytes 131096
  4.0 0.0 copy-start.3
  4.0 0.9 %copy-done.3 = bf16[64,1024]{1,0:T(8,128)(2,1)S(1)} copy-done((bf16[64,1024]{1,0:T(8,128)(2,1)S(1)}, bf16[64,1024]{1,0:T(8,128)(2,1)}, u32[]{:S(2)}) %copy-start.3) | copy-done | bytes 131096
  4.9 1.2 %pack.1 = (bf16[128,768]{1,0:T(8,128)(2,1)S(1)}, bf16[128,768]{1,0:T(8,128)(2,1)S(1)}, bf16[128,1024]{1,0:T(8,128)(2,1)S(1)}, bf16[64,256]{1,0:T(8,128)(2,1)S(1)}, f32[2,128]{1,0:T(2,128)S(1)}) custom-call(bf16[128,512]{1,0:T(8,128)(2,1)S(1)} %bitcast.5, bf16[128,512]{1,0:T(8,128)(2,1)S(1)} %bitcast.6, bf16[128,512]{1,0:T(8,128)(2,1)S(1)} %bitcast.7, ...), custom_call_target="tpu_custom_call" | custom-call | bytes 1476608 | tf_op jit(solution)/shard_map/pack/pallas_call | solution.py:66
  6.1 0.5 collective-permute-start
  6.6 0.1 collective-permute-start.1
  6.7 1.0 %collective-permute-done.pair.refs_6_ = bf16[128,768]{1,0:T(8,128)(2,1)S(1)} collective-permute-done((bf16[128,768]{1,0:T(8,128)(2,1)S(1)}, bf16[128,768]{1,0:T(8,128)(2,1)S(1)}, u32[]{:S(2)}, u32[]{:S(2)}) %collective-permute-start) | collective-permute-done | bytes 196640 | tf_op jit(solution)/shard_map/ppermute | solution.py:395
  7.7 0.2 state.1
  8.0 3.0 %collective-permute-start.2 = (bf16[128,512]{1,0:T(8,128)(2,1)S(1)}, bf16[128,512]{1,0:T(8,128)(2,1)S(1)}, u32[]{:S(2)}, u32[]{:S(2)}) collective-permute-start(bf16[128,512]{1,0:T(8,128)(2,1)S(1)} %get-tuple-element.51), channel_id=1, source_target_pairs={{0,2},{1,7},{2,0},{3,5},{4,6},{5,3},{6,4},{7,1},{8,10},{9,15},{10,... | collective-permute-start | bytes 393224 | tf_op jit(solution)/shard_map/ppermute | solution.py:406
  11.0 2.5 %collective-permute-start.3 = (bf16[128,512]{1,0:T(8,128)(2,1)S(1)}, bf16[128,512]{1,0:T(8,128)(2,1)S(1)}, u32[]{:S(2)}, u32[]{:S(2)}) collective-permute-start(bf16[128,512]{1,0:T(8,128)(2,1)S(1)} %get-tuple-element.52), channel_id=1, source_target_pairs={{0,6},{1,3},{2,4},{3,1},{4,2},{5,7},{6,0},{7,5},{8,14},{9,11},{10,... | collective-permute-start | bytes 393224 | tf_op jit(solution)/shard_map/ppermute | solution.py:406
  13.4 0.1 collective-permute-start.4
  13.6 8.0 %collective-permute-done.4.c.refs_2_ = bf16[128,256]{1,0:T(8,128)(2,1)S(1)} collective-permute-done((bf16[128,256]{1,0:T(8,128)(2,1)S(1)}, bf16[128,256]{1,0:T(8,128)(2,1)S(1)}, u32[]{:S(2)}, u32[]{:S(2)}) %collective-permute-start.4) | collective-permute-done | bytes 65568 | tf_op jit(solution)/shard_map/ppermute | solution.py:406
  21.6 0.0 collective-permute-done.2.a.refs_0_
  21.6 0.0 collective-permute-done.3.b.refs_1_
  21.6 0.1 collective-permute-start.5
  21.7 0.0 collective-permute-done.1.og_recv
  21.7 1.1 %soft_forward.1 = (bf16[256,128]{1,0:T(8,128)(2,1)S(1)}, bf16[512,128]{1,0:T(8,128)(2,1)S(1)}, bf16[512,128]{1,0:T(8,128)(2,1)S(1)}, bf16[256,1024]{1,0:T(8,128)...) custom-call(bf16[128,768]{1,0:T(8,128)(2,1)S(1)} %get-tuple-element., ...), custom_call_target="tpu_custom_call" | custom-call | flops 67108864 | bytes 2883584 | tf_op jit(solution)/shard_map/soft_forward/pallas_call | solution.py:66
  22.8 0.1 collective-permute-done.5.refs_5_
  22.9 0.6 lin_forward.1
  23.5 1.6 %collective-permute-start.6 = (bf16[256,768]{1,0:T(8,128)(2,1)S(1)}, bf16[256,768]{1,0:T(8,128)(2,1)S(1)}, u32[]{:S(2)}, u32[]{:S(2)}) collective-permute-start(bf16[256,768]{1,0:T(8,128)(2,1)S(1)} %get-tuple-element.62.sent), channel_id=1, source_target_pairs={{0,8},{1,17},{8,0},{9,25},{16,24},{17,1},{24,16},{25,9},{2,10},{3,... | collective-permute-start | bytes 1179656 | tf_op jit(solution)/shard_map/ppermute | solution.py:412
  25.1 6.3 %collective-permute-done.6.got = bf16[256,768]{1,0:T(8,128)(2,1)S(1)} collective-permute-done((bf16[256,768]{1,0:T(8,128)(2,1)S(1)}, bf16[256,768]{1,0:T(8,128)(2,1)S(1)}, u32[]{:S(2)}, u32[]{:S(2)}) %collective-permute-start.6) | collective-permute-done | bytes 393248 | tf_op jit(solution)/shard_map/ppermute | solution.py:412
  31.4 0.1 fold.1
  31.4 1.6 %collective-permute-start.7 = (bf16[256,768]{1,0:T(8,128)(2,1)S(1)}, bf16[256,768]{1,0:T(8,128)(2,1)S(1)}, u32[]{:S(2)}, u32[]{:S(2)}) collective-permute-start(bf16[256,768]{1,0:T(8,128)(2,1)S(1)} %get-tuple-element.63.refs_0_), channel_id=1, source_target_pairs={{0,16},{1,9},{8,24},{9,1},{16,0},{17,25},{24,8},{25,17},{2,18},{3,... | collective-permute-start | bytes 1179656 | tf_op jit(solution)/shard_map/ppermute | solution.py:412
  33.0 6.3 %collective-permute-done.7.refs_1_.got = bf16[256,768]{1,0:T(8,128)(2,1)S(1)} collective-permute-done((bf16[256,768]{1,0:T(8,128)(2,1)S(1)}, bf16[256,768]{1,0:T(8,128)(2,1)S(1)}, u32[]{:S(2)}, u32[]{:S(2)}) %collective-permute-start.7) | collective-permute-done | bytes 393248 | tf_op jit(solution)/shard_map/ppermute | solution.py:412
  39.3 0.1 rows.1
  39.3 0.1 collective-permute-start.8
  39.4 1.5 %backward.1 = (bf16[128,128]{1,0:T(8,128)(2,1)S(1)}, bf16[128,128]{1,0:T(8,128)(2,1)S(1)}, f32[128,128]{1,0:T(8,128)S(1)}, f32[256,128]{1,0:T(8,128)S(1)}, f32[5...) custom-call(bf16[256,768]{1,0:T(8,128)(2,1)S(1)} %get-tuple-element.63.refs_0_, ...), custom_call_target="tpu_custom_call" | custom-call | flops 335544320 | bytes 3474432 | tf_op jit(solution)/shard_map/backward/pallas_call | solution.py:66
  41.0 0.0 collective-permute-done.8.refs_2_
  41.0 0.1 halo.1
  41.1 0.4 collective-permute-start.9
  41.5 2.9 %collective-permute-start.10 = (bf16[128,512]{1,0:T(8,128)(2,1)S(1)}, bf16[128,512]{1,0:T(8,128)(2,1)S(1)}, u32[]{:S(2)}, u32[]{:S(2)}) collective-permute-start(bf16[128,512]{1,0:T(8,128)(2,1)S(1)} %get-tuple-element.81), channel_id=1, source_target_pairs={{0,6},{1,3},{2,4},{3,1},{4,2},{5,7},{6,0},{7,5},{8,14},{9,11},{10,... | collective-permute-start | bytes 393224 | tf_op jit(solution)/shard_map/ppermute | solution.py:406
  44.4 0.5 collective-permute-start.11
  44.9 8.4 %collective-permute-done.11.refs_0_ = bf16[128,256]{1,0:T(8,128)(2,1)S(1)} collective-permute-done((bf16[128,256]{1,0:T(8,128)(2,1)S(1)}, bf16[128,256]{1,0:T(8,128)(2,1)S(1)}, u32[]{:S(2)}, u32[]{:S(2)}) %collective-permute-start.11) | collective-permute-done | bytes 65568 | tf_op jit(solution)/shard_map/ppermute | solution.py:406
  53.2 0.0 collective-permute-done.9.a
  53.2 0.0 collective-permute-done.10.b
  53.3 0.4 final.1
  53.6 1.6 %collective-permute-start.13 = (f32[64,256]{1,0:T(8,128)S(1)}, f32[64,256]{1,0:T(8,128)S(1)}, u32[]{:S(2)}, u32[]{:S(2)}) collective-permute-start(f32[64,256]{1,0:T(8,128)S(1)} %get-tuple-element.89.first), channel_id=1, source_target_pairs={{0,8},{1,17},{8,0},{9,25},{16,24},{17,1},{24,16},{25,9},{2,10},{3,... | collective-permute-start | bytes 196616 | tf_op jit(solution)/shard_map/ppermute | solution.py:412
  55.2 0.0 collective-permute-start.12
  55.2 2.8 %collective-permute-done.13.second = f32[64,256]{1,0:T(8,128)S(1)} collective-permute-done((f32[64,256]{1,0:T(8,128)S(1)}, f32[64,256]{1,0:T(8,128)S(1)}, u32[]{:S(2)}, u32[]{:S(2)}) %collective-permute-start.13) | collective-permute-done | bytes 65568 | tf_op jit(solution)/shard_map/ppermute | solution.py:412
  58.0 1.6 %collective-permute-start.14 = (f32[64,512]{1,0:T(8,128)S(1)}, f32[64,512]{1,0:T(8,128)S(1)}, u32[]{:S(2)}, u32[]{:S(2)}) collective-permute-start(f32[64,512]{1,0:T(8,128)S(1)} %pair_up.1.both), channel_id=1, source_target_pairs={{0,16},{1,9},{8,24},{9,1},{16,0},{17,25},{24,8},{25,17},{2,18},{3,... | collective-permute-start | bytes 393224 | tf_op jit(solution)/shard_map/ppermute | solution.py:412
  59.5 3.4 %collective-permute-done.14.got = f32[64,512]{1,0:T(8,128)S(1)} collective-permute-done((f32[64,512]{1,0:T(8,128)S(1)}, f32[64,512]{1,0:T(8,128)S(1)}, u32[]{:S(2)}, u32[]{:S(2)}) %collective-permute-start.14) | collective-permute-done | bytes 131104 | tf_op jit(solution)/shard_map/ppermute | solution.py:412
  63.0 0.7 %weight_join.1 = f32[64,1024]{1,0:T(8,128)} custom-call(f32[64,512]{1,0:T(8,128)S(1)} %pair_up.1.both, f32[64,512]{1,0:T(8,128)S(1)} %collective-permute-done.14.got), custom_call_target="tpu_custom_call" | custom-call | bytes 524288 | tf_op jit(solution)/shard_map/weight_join/pallas_call | solution.py:66
  63.7 0.0 collective-permute-done.12.pair
  63.7 0.8 %outputs.1 = (bf16[1,128,512]{2,1,0:T(8,128)(2,1)}, bf16[1,128,512]{2,1,0:T(8,128)(2,1)}, bf16[1,128,512]{2,1,0:T(8,128)(2,1)}) custom-call(bf16[128,768]{1,0:T(8,128)(2,1)S(1)} %get-tuple-element.84.own, bf16[128,768]{1,0:T(8,128)(2,1)S(1)} %collective-permute-done.12.pair), custom_call_target="tpu_custom_call" | custom-call | bytes 786432 | tf_op jit(solution)/shard_map/outputs/pallas_call | solution.py:66
  (2 shorter events, 0.0 us)
Async XLA Ops:
  0.6 0.7 %copy-start.4 = (f32[256]{0:T(256)S(1)}, f32[256]{0:T(256)}, u32[]{:S(2)}) copy-start(f32[256]{0:T(256)} %param.11) | copy-start | bytes 3076
  1.3 0.9 %copy-start = (bf16[1,128,512]{2,1,0:T(8,128)(2,1)S(1)}, bf16[1,128,512]{2,1,0:T(8,128)(2,1)}, u32[]{:S(2)}) copy-start(bf16[1,128,512]{2,1,0:T(8,128)(2,1)} %param.6) | copy-start | bytes 393220
  2.2 0.9 %copy-start.1 = (bf16[1,128,512]{2,1,0:T(8,128)(2,1)S(1)}, bf16[1,128,512]{2,1,0:T(8,128)(2,1)}, u32[]{:S(2)}) copy-start(bf16[1,128,512]{2,1,0:T(8,128)(2,1)} %param.7) | copy-start | bytes 393220
  3.1 0.9 %copy-start.2 = (bf16[1,128,512]{2,1,0:T(8,128)(2,1)S(1)}, bf16[1,128,512]{2,1,0:T(8,128)(2,1)}, u32[]{:S(2)}) copy-start(bf16[1,128,512]{2,1,0:T(8,128)(2,1)} %param.8) | copy-start | bytes 393220
  4.0 0.9 %copy-start.3 = (bf16[64,1024]{1,0:T(8,128)(2,1)S(1)}, bf16[64,1024]{1,0:T(8,128)(2,1)}, u32[]{:S(2)}) copy-start(bf16[64,1024]{1,0:T(8,128)(2,1)} %w.1) | copy-start | bytes 393220
  6.1 1.6 %collective-permute-start = (bf16[128,768]{1,0:T(8,128)(2,1)S(1)}, bf16[128,768]{1,0:T(8,128)(2,1)S(1)}, u32[]{:S(2)}, u32[]{:S(2)}) collective-permute-start(bf16[128,768]{1,0:T(8,128)(2,1)S(1)} %get-tuple-element.48), channel_id=1, source_target_pairs={{0,1},{1,0},{2,3},{3,2},{4,5},{5,4},{6,7},{7,6},{8,9},{9,8},{10,11... | collective-permute-start | bytes 589832 | tf_op jit(solution)/shard_map/ppermute | solution.py:395
  6.6 15.1 %collective-permute-start.1 = (bf16[128,1024]{1,0:T(8,128)(2,1)}, bf16[128,1024]{1,0:T(8,128)(2,1)S(1)}, u32[]{:S(2)}, u32[]{:S(2)}) collective-permute-start(bf16[128,1024]{1,0:T(8,128)(2,1)} %bitcast.3.og), channel_id=1, source_target_pairs={{0,1},{1,0},{2,3},{3,2},{4,5},{5,4},{6,7},{7,6},{8,9},{9,8},{10,11... | collective-permute-start | bytes 786440 | tf_op jit(solution)/shard_map/ppermute | solution.py:395
  8.0 13.6 %collective-permute-start.2 = (bf16[128,512]{1,0:T(8,128)(2,1)S(1)}, bf16[128,512]{1,0:T(8,128)(2,1)S(1)}, u32[]{:S(2)}, u32[]{:S(2)}) collective-permute-start(bf16[128,512]{1,0:T(8,128)(2,1)S(1)} %get-tuple-element.51), channel_id=1, source_target_pairs={{0,2},{1,7},{2,0},{3,5},{4,6},{5,3},{6,4},{7,1},{8,10},{9,15},{10,... | collective-permute-start | bytes 393224 | tf_op jit(solution)/shard_map/ppermute | solution.py:406
  11.0 10.6 %collective-permute-start.3 = (bf16[128,512]{1,0:T(8,128)(2,1)S(1)}, bf16[128,512]{1,0:T(8,128)(2,1)S(1)}, u32[]{:S(2)}, u32[]{:S(2)}) collective-permute-start(bf16[128,512]{1,0:T(8,128)(2,1)S(1)} %get-tuple-element.52), channel_id=1, source_target_pairs={{0,6},{1,3},{2,4},{3,1},{4,2},{5,7},{6,0},{7,5},{8,14},{9,11},{10,... | collective-permute-start | bytes 393224 | tf_op jit(solution)/shard_map/ppermute | solution.py:406
  13.4 8.1 %collective-permute-start.4 = (bf16[128,256]{1,0:T(8,128)(2,1)S(1)}, bf16[128,256]{1,0:T(8,128)(2,1)S(1)}, u32[]{:S(2)}, u32[]{:S(2)}) collective-permute-start(bf16[128,256]{1,0:T(8,128)(2,1)S(1)} %get-tuple-element.57), channel_id=1, source_target_pairs={{0,4},{1,5},{2,6},{3,7},{4,0},{5,1},{6,2},{7,3},{8,12},{9,13},{10,... | collective-permute-start | bytes 196616 | tf_op jit(solution)/shard_map/ppermute | solution.py:406
  21.6 1.3 %collective-permute-start.5 = (bf16[2,64,256]{2,1,0:T(8,128)(2,1)S(1)}, bf16[2,64,256]{2,1,0:T(8,128)(2,1)S(1)}, u32[]{:S(2)}, u32[]{:S(2)}) collective-permute-start(bf16[2,64,256]{2,1,0:T(8,128)(2,1)S(1)} %get-tuple-element.60), channel_id=1, source_target_pairs={{0,1},{1,0},{2,3},{3,2},{4,5},{5,4},{6,7},{7,6},{8,9},{9,8},{10,11... | collective-permute-start | bytes 196616 | tf_op jit(solution)/shard_map/ppermute | solution.py:395
  23.5 7.8 %collective-permute-start.6 = (bf16[256,768]{1,0:T(8,128)(2,1)S(1)}, bf16[256,768]{1,0:T(8,128)(2,1)S(1)}, u32[]{:S(2)}, u32[]{:S(2)}) collective-permute-start(bf16[256,768]{1,0:T(8,128)(2,1)S(1)} %get-tuple-element.62.sent), channel_id=1, source_target_pairs={{0,8},{1,17},{8,0},{9,25},{16,24},{17,1},{24,16},{25,9},{2,10},{3,... | collective-permute-start | bytes 1179656 | tf_op jit(solution)/shard_map/ppermute | solution.py:412
  31.4 7.8 %collective-permute-start.7 = (bf16[256,768]{1,0:T(8,128)(2,1)S(1)}, bf16[256,768]{1,0:T(8,128)(2,1)S(1)}, u32[]{:S(2)}, u32[]{:S(2)}) collective-permute-start(bf16[256,768]{1,0:T(8,128)(2,1)S(1)} %get-tuple-element.63.refs_0_), channel_id=1, source_target_pairs={{0,16},{1,9},{8,24},{9,1},{16,0},{17,25},{24,8},{25,17},{2,18},{3,... | collective-permute-start | bytes 1179656 | tf_op jit(solution)/shard_map/ppermute | solution.py:412
  39.3 1.6 %collective-permute-start.8 = (f32[128,256]{1,0:T(8,128)S(1)}, f32[128,256]{1,0:T(8,128)S(1)}, u32[]{:S(2)}, u32[]{:S(2)}) collective-permute-start(f32[128,256]{1,0:T(8,128)S(1)} %get-tuple-element.79), channel_id=1, source_target_pairs={{0,1},{1,0},{2,3},{3,2},{4,5},{5,4},{6,7},{7,6},{8,9},{9,8},{10,11... | collective-permute-start | bytes 393224 | tf_op jit(solution)/shard_map/ppermute | solution.py:395
  41.1 12.2 %collective-permute-start.9 = (bf16[128,512]{1,0:T(8,128)(2,1)S(1)}, bf16[128,512]{1,0:T(8,128)(2,1)S(1)}, u32[]{:S(2)}, u32[]{:S(2)}) collective-permute-start(bf16[128,512]{1,0:T(8,128)(2,1)S(1)} %get-tuple-element.80), channel_id=1, source_target_pairs={{0,2},{1,7},{2,0},{3,5},{4,6},{5,3},{6,4},{7,1},{8,10},{9,15},{10,... | collective-permute-start | bytes 393224 | tf_op jit(solution)/shard_map/ppermute | solution.py:406
  41.5 11.7 %collective-permute-start.10 = (bf16[128,512]{1,0:T(8,128)(2,1)S(1)}, bf16[128,512]{1,0:T(8,128)(2,1)S(1)}, u32[]{:S(2)}, u32[]{:S(2)}) collective-permute-start(bf16[128,512]{1,0:T(8,128)(2,1)S(1)} %get-tuple-element.81), channel_id=1, source_target_pairs={{0,6},{1,3},{2,4},{3,1},{4,2},{5,7},{6,0},{7,5},{8,14},{9,11},{10,... | collective-permute-start | bytes 393224 | tf_op jit(solution)/shard_map/ppermute | solution.py:406
  44.4 8.8 %collective-permute-start.11 = (bf16[128,256]{1,0:T(8,128)(2,1)S(1)}, bf16[128,256]{1,0:T(8,128)(2,1)S(1)}, u32[]{:S(2)}, u32[]{:S(2)}) collective-permute-start(bf16[128,256]{1,0:T(8,128)(2,1)S(1)} %get-tuple-element.82), channel_id=1, source_target_pairs={{0,4},{1,5},{2,6},{3,7},{4,0},{5,1},{6,2},{7,3},{8,12},{9,13},{10,... | collective-permute-start | bytes 196616 | tf_op jit(solution)/shard_map/ppermute | solution.py:406
  53.6 4.3 %collective-permute-start.13 = (f32[64,256]{1,0:T(8,128)S(1)}, f32[64,256]{1,0:T(8,128)S(1)}, u32[]{:S(2)}, u32[]{:S(2)}) collective-permute-start(f32[64,256]{1,0:T(8,128)S(1)} %get-tuple-element.89.first), channel_id=1, source_target_pairs={{0,8},{1,17},{8,0},{9,25},{16,24},{17,1},{24,16},{25,9},{2,10},{3,... | collective-permute-start | bytes 196616 | tf_op jit(solution)/shard_map/ppermute | solution.py:412
  55.2 8.5 %collective-permute-start.12 = (bf16[128,768]{1,0:T(8,128)(2,1)S(1)}, bf16[128,768]{1,0:T(8,128)(2,1)S(1)}, u32[]{:S(2)}, u32[]{:S(2)}) collective-permute-start(bf16[128,768]{1,0:T(8,128)(2,1)S(1)} %get-tuple-element.85), channel_id=1, source_target_pairs={{0,1},{1,0},{2,3},{3,2},{4,5},{5,4},{6,7},{7,6},{8,9},{9,8},{10,11... | collective-permute-start | bytes 589832 | tf_op jit(solution)/shard_map/ppermute | solution.py:395
  58.0 5.0 %collective-permute-start.14 = (f32[64,512]{1,0:T(8,128)S(1)}, f32[64,512]{1,0:T(8,128)S(1)}, u32[]{:S(2)}, u32[]{:S(2)}) collective-permute-start(f32[64,512]{1,0:T(8,128)S(1)} %pair_up.1.both), channel_id=1, source_target_pairs={{0,16},{1,9},{8,24},{9,1},{16,0},{17,25},{24,8},{25,17},{2,18},{3,... | collective-permute-start | bytes 393224 | tf_op jit(solution)/shard_map/ppermute | solution.py:412

commit v4 on v3

--- a/solution.py
+++ b/solution.py
@@ -94,7 +94,7 @@
     )
 
 
-def pack_kernel(q, k, v, og, w, gain, mine_out, other_out, og_out, w_out, gain_out, sems):
+def pack_kernel(q, k, v, og, w, gain, mine_out, other_out, og_out, gain_out, sems):
     core, _, dp = places()
     mine, other = core * DH, (1 - core) * DH
     copies = []
@@ -104,62 +104,83 @@
         copy.start()
         copies.append(copy)
 
+    width = w.shape[1] // lax.axis_size("dp")
+    rows = w.shape[0]
     for index, array in enumerate((q, k, v)):
         for group in range(2):
             cols = slice((3 * group + index) * DH, (3 * group + index + 1) * DH)
-            fetch(array.at[:, at(SOFT * group + other)], other_out.at[:, cols])
-            fetch(array.at[:, at(SOFT * group + mine)], mine_out.at[:, cols])
-    fetch(og, og_out)
-    width = w_out.shape[1]
-    fetch(w.at[:, at(dp * width, width)], w_out)
-    fetch(gain, gain_out)
+            fetch(array.at[0, :, at(SOFT * group + other)], other_out.at[:, cols])
+            fetch(array.at[0, :, at(SOFT * group + mine)], mine_out.at[:, cols])
+    if other_out.shape[1] > 6 * DH:
+        for side in range(2):
+            fetch(
+                w.at[:, at(dp * width + side * DH)],
+                other_out.at[side * rows : (side + 1) * rows, 6 * DH :],
+            )
+    fetch(og.at[0], og_out)
+    fetch(gain.at[at(mine)], gain_out.at[0])
     for copy in copies:
         copy.wait()
 
 
-def state_kernel(direct, mine, pair, w, state, to_a, to_b, *to_c):
+def state_kernel(direct, mine, pair, *refs):
     core, _, _ = places()
     total = mm2(unit_plus(mine[:, KL].astype(F32)), mine[:, VL], TN) + mm2(
         unit_plus(pair[:, KL].astype(F32)), pair[:, VL], TN
     )
+    if direct:
+        other, state, to_a, to_b, to_c, w_head = refs
+    else:
+        state, to_a, to_b = refs
     state[...] = total
     way = links(direct)
     for out, block in ((to_a, way["block_a"]), (to_b, way["block_b"])):
         here = block == core
         out[:, :DH] = jnp.where(here, mine[:, KS], pair[:, KS])
         out[:, DH : 2 * DH] = jnp.where(here, mine[:, VS], pair[:, VS])
-    if direct:
-        rows = w.shape[0]
-        for out, first in ((to_a, 2 * DH), (to_b, 2 * DH), (to_c[0], 0)):
-            out[:, first : first + DH] = total.astype(BF)
-            out[:rows, first + DH :] = w[:, :DH]
-            out[rows:, first + DH :] = w[:, DH:]
-
-
-def relay_kernel(w, a, b, c, keep, send, heads):
+        if direct:
+            out[:, 2 * DH :] = total.astype(BF)
+    if direct:
+        to_c[...] = total.astype(BF)
+        rows = w_head.shape[0] // 2
+        for source, place in ((other, core), (pair, 1 - core)):
+            for side in range(2):
+                w_head[at(place * rows, rows), side * DH : (side + 1) * DH] = source[
+                    side * rows : (side + 1) * rows, 6 * DH :
+                ]
+
+
+def w_two_kernel(own, got, out):
+    _, z, _ = places()
+    group = lax.div(z, 2)
+    out[at(group * DH), :] = own[...]
+    out[at((1 - group) * DH), :] = got[...]
+
+
+def w_pick_kernel(own, got, out):
     core, z, _ = places()
-    way = links(True)
-    rows = w.shape[0]
-    heads[z] = w[...]
-    for source, first, step in ((a, 3 * DH, way["first"]), (b, 3 * DH, way["second"]), (c, DH, 2)):
-        heads[z ^ step, :, :DH] = source[:rows, first:]
-        heads[z ^ step, :, DH:] = source[rows:, first:]
-    for group in range(2):
-        keep[group] = heads[2 * group + core]
-        send[group] = heads[2 * group + 1 - core]
+    out[...] = jnp.where(lax.rem(z, 2) == core, own[...], got[...])
+
+
+def join_kernel(first, second, out):
+    width = first.shape[1]
+    out[:, :width] = first[...]
+    out[:, width:] = second[...]
 
 
 def weight_parts(direct, attn, ogs, send, keep):
+    high, low = halves(attn)
     if not direct:
-        keep[...] = mm(attn, ogs[...], TN)
+        keep[...] = mm(high, ogs[...], TN) + mm(low, ogs[...], TN)
         return
     _, _, dp = places()
     way = links(True)
     width = send.shape[1] // 2
     for index, step in enumerate((0, way["other"])):
         cols = slice(index * width, (index + 1) * width)
-        keep[:, cols] = mm(attn, ogs[:, at((dp ^ step) * width, width)], TN)
-        send[:, cols] = mm(attn, ogs[:, at((dp ^ step ^ way["step"]) * width, width)], TN).astype(BF)
+        near, far = at((dp ^ step) * width, width), at((dp ^ step ^ way["step"]) * width, width)
+        keep[:, cols] = mm(high, ogs[:, near], TN) + mm(low, ogs[:, near], TN)
+        send[:, cols] = (mm(high, ogs[:, far], TN) + mm(low, ogs[:, far], TN)).astype(BF)
 
 
 def soft_forward_kernel(
@@ -191,7 +212,7 @@
         terms = jnp.where(inside, jnp.exp(scores - peak), 0.0)
         share = terms / jnp.sum(terms, axis=1, keepdims=True)
         probs[block] = share
-        attn[here, :] = mm(share.astype(BF), vs[window, :]).astype(BF)
+        attn[here, :] = mm(share.astype(BF), vs[window, :])
     weight_parts(direct, attn[...], ogs, send[0] if send else None, keep)
 
 
@@ -200,43 +221,32 @@
     rows = mine.shape[0]
     total = state[...]
     if direct:
-        a, b, c, soft_send, w_keep, w_recv, u_out, total_out, keep, out, send = refs
-        total = total + a[:, 2 * DH : 3 * DH].astype(F32) + b[:, 2 * DH : 3 * DH].astype(F32)
-        total = total + c[:, :DH].astype(F32)
+        a, b, c, soft_send, u_out, total_out, keep, out = refs
+        total = total + a[:, 2 * DH :].astype(F32) + b[:, 2 * DH :].astype(F32) + c[...].astype(F32)
     else:
         u_out, total_out, keep = refs
-        send = None
     total_out[...] = total
     u_out[at(core * rows, rows), :] = mm3(unit_plus(mine[:, QL].astype(F32)), total)
     u_out[at((1 - core) * rows, rows), :] = mm3(unit_plus(pair[:, QL].astype(F32)), total)
     u = u_out[...]
     r = lax.rsqrt(jnp.mean(u * u, axis=1, keepdims=True) + norm_eps)
-    attn = (gain[pl.ds(core, 1), :] * u * r).astype(BF)
-    weight_parts(direct, attn, ogs, send, keep)
-    if direct:
-        wide = soft_send.shape[1]
-        out[:DH, :wide] = soft_send[...]
-        out[DH:, :wide] = send[...]
-        half = w_keep.shape[1]
-        for group in range(2):
-            out[at(group * DH + core * half, half), wide:] = w_keep[group]
-            out[at(group * DH + (1 - core) * half, half), wide:] = w_recv[group]
-
-
-def fold_kernel(keep_soft, keep_lin, sent, got, keep, send):
+    attn = gain[...] * u * r
+    weight_parts(direct, attn, ogs, out.at[DH:, :] if direct else None, keep)
+    if direct:
+        out[:DH, :] = soft_send[...]
+
+
+def fold_kernel(keep_soft, keep_lin, got, keep, send):
     width = keep.shape[1]
     for rows, source in ((slice(0, DH), keep_soft), (slice(DH, 2 * DH), keep_lin)):
         keep[rows, :] = source[:, :width] + got[rows, :width].astype(F32)
-        send[rows, :width] = (source[:, width:] + got[rows, width : 2 * width].astype(F32)).astype(BF)
-    send[:, width : 2 * width] = sent[:, 2 * width :]
-    send[:, 2 * width :] = got[:, 2 * width :]
+        send[rows, :] = (source[:, width:] + got[rows, width:].astype(F32)).astype(BF)
 
 
 def rows_kernel(keep, got, own, send, total):
     core, _, _ = places()
     half = DH // 2
-    width = keep.shape[1]
-    total[...] = keep[...] + got[:, :width].astype(F32)
+    total[...] = keep[...] + got[...].astype(F32)
     for group in range(2):
         out = slice(group * half, (group + 1) * half)
         own[out, :] = total[at(group * DH + core * half, half), :]
@@ -248,7 +258,7 @@
     rows = mine.shape[0]
     u_all = u[...]
     r = lax.rsqrt(jnp.mean(u_all * u_all, axis=1, keepdims=True) + norm_eps)
-    lin_grad = gain[pl.ds(core, 1), :] * dattn[:, DH:]
+    lin_grad = gain[...] * dattn[:, DH:]
     grads[...] = r * lin_grad - u_all * (r * r * r) * jnp.mean(lin_grad * u_all, axis=1, keepdims=True)
     total_state = total[...]
     result = jnp.zeros(dstate.shape, F32)
@@ -269,7 +279,7 @@
         here, window = slice(block * rows, (block + 1) * rows), slice(block * rows, block * rows + span)
         grad = dattn[here, :DH].astype(BF)
         share = probs[block]
-        delta = jnp.sum(grad.astype(F32) * attn[here, :].astype(F32), axis=1, keepdims=True)
+        delta = jnp.sum(grad.astype(F32) * attn[here, :], axis=1, keepdims=True)
         dscore = (share * (mm(grad, vs[window, :], NT) - delta)).astype(BF)
         dq_all[here, :] = mm(dscore, ks[window, :]) * FACTOR
         dk_all[window, :] += mm(dscore, qs[here, :], TN) * FACTOR
@@ -291,7 +301,7 @@
         weights = scratch[0]
         width = weights.shape[1] // 4
         for source, index, step in (
-            (sent, 1, 0), (sent, 2, way["step"]), (got, 1, way["other"]), (got, 2, 3),
+            (sent, 0, 0), (sent, 1, way["step"]), (got, 0, way["other"]), (got, 1, 3),
         ):
             weights[:, at((dp ^ step) * width, width)] = source[:, index * width : (index + 1) * width]
     dattn[...] = mm(ogs[...], weights[...], NT)
@@ -300,49 +310,49 @@
 
 
 def halo_kernel(direct, dk_soft, dv_soft, *refs):
-    core, z, _ = places()
     way = links(direct)
     span = dk_soft.shape[0]
     if direct:
-        dstate, own, got, to_a, to_b, to_c, chunk, heads = refs
-        half = own.shape[0] // 2
-        for group in range(2):
-            rows = slice(group * half, (group + 1) * half)
-            heads[2 * group + core] = own[rows, :]
-            heads[2 * group + 1 - core] = got[rows, :]
-        chunk[...] = heads[z]
-        for out, first, step in ((to_a, 2 * DH, way["first"]), (to_b, 2 * DH, way["second"]), (to_c, 0, 2)):
-            out[:, first : first + DH] = dstate[...].astype(BF)
-            out[:half, first + DH :] = heads[z ^ step, :, :DH].astype(BF)
-            out[half:, first + DH :] = heads[z ^ step, :, DH:].astype(BF)
+        dstate, to_a, to_b, to_c = refs
+        to_c[...] = dstate[...].astype(BF)
     else:
         to_a, to_b = refs
     for out, side in ((to_a, way["halo_a"]), (to_b, way["halo_b"])):
         first = side * (span - HALF)
         out[:, :DH] = dk_soft[at(first), :].astype(BF)
         out[:, DH : 2 * DH] = dv_soft[at(first), :].astype(BF)
+        if direct:
+            out[:, 2 * DH :] = dstate[...].astype(BF)
+
+
+def chunk_kernel(own, got, to_a, to_b, to_c, chunk, heads):
+    core, z, _ = places()
+    way = links(True)
+    half = chunk.shape[0]
+    for group in range(2):
+        rows = slice(group * half, (group + 1) * half)
+        heads[2 * group + core] = own[rows, :]
+        heads[2 * group + 1 - core] = got[rows, :]
+    chunk[...] = heads[z]
+    for out, step in ((to_a, way["first"]), (to_b, way["second"]), (to_c, 2)):
+        out[...] = heads[z ^ step].astype(BF)
+
+
+def weight_sum_kernel(scale, chunk, a, b, c, out):
+    out[...] = scale * (chunk[...] + a[...].astype(F32) + b[...].astype(F32) + c[...].astype(F32))
 
 
 def final_kernel(
-    direct, scale, dstate, mine, pair, dq_soft, dk_soft, dv_soft, dq_lin, dq_lin_pair, a, b, *refs
+    direct, dstate, mine, pair, dq_soft, dk_soft, dv_soft, dq_lin, dq_lin_pair, a, b, *refs
 ):
     core, _, _ = places()
     way = links(direct)
     rows = mine.shape[0]
     total = dstate[...]
-    if direct:
-        c, chunk, own_out, pair_out, weight_out, dk_all, dv_all = refs
-        total = total + a[:, 2 * DH : 3 * DH].astype(F32) + b[:, 2 * DH : 3 * DH].astype(F32)
-        total = total + c[:, :DH].astype(F32)
-        half = chunk.shape[0]
-        for side in range(2):
-            cols, part = slice(side * DH, (side + 1) * DH), slice(side * half, (side + 1) * half)
-            weight_out[:, cols] = scale * (
-                chunk[:, cols] + a[part, 3 * DH :].astype(F32) + b[part, 3 * DH :].astype(F32)
-                + c[part, DH:].astype(F32)
-            )
-    else:
-        own_out, pair_out, dk_all, dv_all = refs
+    own_out, pair_out, dk_all, dv_all = refs[-4:]
+    if direct:
+        total = total + a[:, 2 * DH :].astype(F32) + b[:, 2 * DH :].astype(F32)
+        total = total + refs[0][...].astype(F32)
     for source, out, cols in ((dk_soft, dk_all, slice(0, DH)), (dv_soft, dv_all, slice(DH, 2 * DH))):
         out[...] = source[HALF : HALF + 2 * rows, :]
         out[at(way["block_a"] * rows, rows), :] += a[:, cols].astype(F32)
@@ -367,13 +377,7 @@
             out[0, :, at(SOFT + first)] = source[:, (3 + index) * DH : (4 + index) * DH]
 
 
-def pair_up_kernel(first, second, out):
-    width = first.shape[1]
-    out[:, :width] = first[...]
-    out[:, width:] = second[...]
-
-
-def weight_join_kernel(both, got, out):
+def weight_join_kernel(both, got, _, out):
     _, _, dp = places()
     way = links(True)
     width = both.shape[1] // 2
@@ -382,8 +386,7 @@
 
 
 def body(n_dp, n_z, queries, key_rows, value_rows, out_grad, out_weight, norm_gain):
-    q, k, v, og = queries[0], key_rows[0], value_rows[0], out_grad[0]
-    rows, model = og.shape
+    rows, model = out_grad.shape[1:]
     axes = ("z", "core")
     pair_perm = [(0, 1), (1, 0)]
     core = lax.axis_index("core")
@@ -405,44 +408,55 @@
                 pairs.append((2 * z + c, 2 * there + c))
         return lax.ppermute(value, axes, pairs)
 
+    def from_matching(value, step):
+        pairs = [(2 * z + z % 2, 2 * (z ^ step) + z % 2) for z in range(n_z)]
+        return lax.ppermute(value, axes, pairs)
+
     def over_dp(value, which):
         pairs = [
             (2 * d + c, 2 * (d ^ (1 + c, 2 - c)[which]) + c) for d in range(n_dp) for c in range(2)
         ]
         return lax.ppermute(value, ("dp", "core"), pairs)
 
-    og_recv = over_core(og)
-    gain = norm_gain.reshape(LIN_HEADS, DH)
-    mine, other, og_here, w_part, gain = call(
+    def hbm(value):
+        return pltpu.with_memory_space_constraint(value, pltpu.HBM)
+
+    sent_cols = 7 * DH if direct else 6 * DH
+    mine, other, og, gain = call(
         pack_kernel, "pack",
         [
-            like((rows, 6 * DH), BF), like((rows, 6 * DH), BF), like((rows, model), BF),
-            like((out_weight.shape[0], width), BF), like((LIN_HEADS, DH), F32),
+            like((rows, 6 * DH), BF), like((rows, sent_cols), BF), like((rows, model), BF),
+            like((1, DH), F32),
         ],
-        [q, k, v, og, out_weight, gain], scratch=[pltpu.SemaphoreType.DMA((15,))],
+        [hbm(x) for x in (queries, key_rows, value_rows, out_grad, out_weight, norm_gain)],
+        scratch=[pltpu.SemaphoreType.DMA((16,))],
         spaces=[pl.BlockSpec(memory_space=pltpu.HBM)] * 6,
     )
     pair = over_core(other)
-    wide = 4 * DH if direct else 2 * DH
-    state, to_a, to_b, *to_c = call(
+    og_recv = over_core(og)
+    wide = 3 * DH if direct else 2 * DH
+    state, to_a, to_b, *rest = call(
         functools.partial(state_kernel, direct), "state",
         [like((DH, DH), F32), like((rows, wide), BF), like((rows, wide), BF)]
-        + [like((rows, 2 * DH), BF)] * direct,
-        [mine, pair, w_part],
+        + [like((DH, DH), BF), like((DH, width), BF)] * direct,
+        [mine, pair] + [other] * direct,
         flops=4 * 2 * rows * DH * DH,
     )
-    a, b = over_z(to_a, 0), over_z(to_b, 1)
-    c = [over_z(value, 2) for value in to_c]
-    if direct:
-        w_keep, w_send = call(
-            relay_kernel, "relay", [like((2, half, width), BF)] * 2, [w_part, a, b] + c,
-            scratch=[pltpu.VMEM((HEADS, half, width), BF)],
-        )
-        w_recv = over_core(w_send)
+    if direct:
+        to_c, w_head = rest
+        w_got = from_matching(w_head, 2)
+        a, b, c = over_z(to_a, 0), over_z(to_b, 1), [over_z(to_c, 2)]
+        w_two = call(w_two_kernel, "w_two", [like((2 * DH, width), BF)], [w_head, w_got])[0]
+        w_got = from_matching(w_two, 1)
+        w_own = call(w_pick_kernel, "w_pick", [like((2 * DH, width), BF)], [w_two, w_got])[0]
+        w_got = over_dp(w_own, 0)
+        w_half = call(join_kernel, "w_half", [like((2 * DH, 2 * width), BF)], [w_own, w_got])[0]
+        weights = [w_half, over_dp(w_half, 1)]
     else:
+        a, b, c = over_z(to_a, 0), over_z(to_b, 1), []
         state = lax.psum(state, "z")
         weights = lax.all_gather(out_weight, axes, axis=0, tiled=True).reshape(2, 2, DH, model)
-        weights = jnp.where(core == 0, weights[:, 0], weights[:, 1]).reshape(2 * DH, model)
+        weights = [jnp.where(core == 0, weights[:, 0], weights[:, 1]).reshape(2 * DH, model)]
 
     span = 2 * rows + 2 * HALF
     keep_width = 2 * width if direct else model
@@ -451,25 +465,24 @@
         functools.partial(soft_forward_kernel, direct), "soft_forward",
         [
             like((2 * rows, DH), BF), like((span, DH), BF), like((span, DH), BF),
-            like((2 * rows, model), BF), like((2, rows, rows + 2 * HALF), F32), like((2 * rows, DH), BF),
+            like((2 * rows, model), BF), like((2, rows, rows + 2 * HALF), F32), like((2 * rows, DH), F32),
             like((DH, keep_width), F32),
         ] + [like((DH, 2 * width), BF)] * direct,
-        [mine, pair, og_here, og_recv, a, b],
+        [mine, pair, og, og_recv, a, b],
         flops=wg_flops,
     )
     u, total, keep_lin, *sent = call(
         functools.partial(lin_forward_kernel, direct), "lin_forward",
         [like((2 * rows, DH), F32), like((DH, DH), F32), like((DH, keep_width), F32)]
-        + [like((2 * DH, 3 * width), BF)] * direct,
-        [state, mine, pair, ogs, gain] + ([a, b] + c + soft_send + [w_keep, w_recv] if direct else []),
-        scratch=[pltpu.VMEM((DH, 2 * width), BF)] * direct,
+        + [like((2 * DH, 2 * width), BF)] * direct,
+        [state, mine, pair, ogs, gain] + ([a, b] + c + soft_send if direct else []),
         flops=wg_flops,
     )
     if direct:
         got = over_dp(sent[0], 0)
         keep, sent = call(
-            fold_kernel, "fold", [like((2 * DH, width), F32), like((2 * DH, 3 * width), BF)],
-            [keep_soft, keep_lin, sent[0], got],
+            fold_kernel, "fold", [like((2 * DH, width), F32), like((2 * DH, width), BF)],
+            [keep_soft, keep_lin, got],
         )
         got = over_dp(sent, 1)
         row_own, row_send = call(
@@ -477,9 +490,11 @@
             scratch=[pltpu.VMEM((2 * DH, width), F32)],
         )
         row_recv = over_core(row_send)
-        weights = [sent, got]
-    else:
-        weights = [weights]
+        *to_chips, chunk = call(
+            chunk_kernel, "chunk", [like((half, width), BF)] * 3 + [like((half, width), F32)],
+            [row_own, row_recv], scratch=[pltpu.VMEM((HEADS, half, width), F32)],
+        )
+        chunks = [over_z(value, which) for which, value in enumerate(to_chips)]
     dq_lin, dq_lin_pair, dstate, dq_soft, dk_soft, dv_soft = call(
         functools.partial(backward_kernel, direct), "backward",
         [
@@ -492,17 +507,14 @@
         flops=5 * wg_flops,
     )
     scale = 1.0 / math.sqrt(n_dp * n_z * 2 * rows)
-    to_a, to_b, *rest = call(
+    to_a, to_b, *to_c = call(
         functools.partial(halo_kernel, direct), "halo",
-        [like((rows, wide), BF), like((rows, wide), BF)]
-        + [like((rows, 2 * DH), BF), like((half, width), F32)] * direct,
-        [dk_soft, dv_soft] + ([dstate, row_own, row_recv] if direct else []),
-        scratch=[pltpu.VMEM((HEADS, half, width), F32)] * direct,
+        [like((rows, wide), BF), like((rows, wide), BF)] + [like((DH, DH), BF)] * direct,
+        [dk_soft, dv_soft] + [dstate] * direct,
     )
     a, b = over_z(to_a, 0, True), over_z(to_b, 1, True)
-    if direct:
-        rest = [over_z(rest[0], 2), rest[1]]
-    else:
+    c = [over_z(value, 2) for value in to_c]
+    if not direct:
         dstate = lax.psum(dstate, "z")
         groups = jnp.stack([keep_soft, keep_lin])
         slots = jnp.stack([jnp.where(core == head, groups, 0.0) for head in range(2)], axis=1)
@@ -510,24 +522,29 @@
             slots.reshape(HEADS * DH, model), axes, scatter_dimension=0, tiled=True
         )
         weight_grad = lax.psum(local, "dp") * scale
-    own_out, to_pair, *weight_part = call(
-        functools.partial(final_kernel, direct, scale), "final",
-        [like((rows, 6 * DH), BF), like((rows, 6 * DH), BF)] + [like((half, width), F32)] * direct,
-        [dstate, mine, pair, dq_soft, dk_soft, dv_soft, dq_lin, dq_lin_pair, a, b] + rest,
+    own_out, to_pair = call(
+        functools.partial(final_kernel, direct), "final",
+        [like((rows, 6 * DH), BF), like((rows, 6 * DH), BF)],
+        [dstate, mine, pair, dq_soft, dk_soft, dv_soft, dq_lin, dq_lin_pair, a, b] + c,
         scratch=[pltpu.VMEM((2 * rows, DH), F32)] * 2,
         flops=wg_flops // 4,
     )
     from_pair = over_core(to_pair)
-    if direct:
-        got = over_dp(weight_part[0], 0)
-        both = call(
-            pair_up_kernel, "pair_up", [like((half, 2 * width), F32)], [weight_part[0], got]
-        )[0]
-        weight_grad = call(
-            weight_join_kernel, "weight_join", [like((half, model), F32)], [both, over_dp(both, 1)]
-        )[0]
     shape = like((1, rows, HEADS * DH), BF)
     dq, dk, dv = call(output_kernel, "outputs", [shape] * 3, [own_out, from_pair])
+    if direct:
+        summed = call(
+            functools.partial(weight_sum_kernel, scale), "weight_sum", [like((half, width), F32)],
+            [chunk] + chunks,
+        )[0]
+        got = over_dp(summed, 0)
+        both = call(join_kernel, "both", [like((half, 2 * width), F32)], [summed, got])[0]
+        got = over_dp(both, 1)
+        vmem = pl.BlockSpec(memory_space=pltpu.VMEM)
+        weight_grad = call(
+            weight_join_kernel, "weight_join", [like((half, model), F32)], [both, got, hbm(dq)],
+            spaces=[vmem, vmem, pl.BlockSpec(memory_space=pltpu.HBM)],
+        )[0]
     return dq, dk, dv, weight_grad
 
 

time: 64.8 us -> 62.5 us (0.965)
  starting transfers between devices: 16.4 us -> 28.7 us
  waiting for transfers between devices: 36.2 us -> 25.6 us
  local copies, waits for them, and re-layouts: 4.29 us -> 0 us
    ppermute x6 -> x9, waiting for transfers between devices: 16.4 us -> 7.08 us  [over_z(): return lax.ppermute(value, axes, pairs)]
    ppermute x0 -> x2, starting transfers between devices: none -> 7.16 us  [from_matching(): return lax.ppermute(value, axes, pairs)]
    unnamed x10 -> x0, local copies, waits for them, and re-layouts: 4.29 us -> none
    ppermute x4 -> x6, waiting for transfers between devices: 18.8 us -> 15.7 us  [over_dp(): return lax.ppermute(value, ('dp', 'core'), pairs)]
    ppermute x4 -> x6, starting transfers between devices: 6.29 us -> 9.14 us  [over_dp(): return lax.ppermute(value, ('dp', 'core'), pairs)]
    ppermute x6 -> x9, starting transfers between devices: 9.41 us -> 11.7 us  [over_z(): return lax.ppermute(value, axes, pairs)]
    ppermute x0 -> x2, waiting for transfers between devices: none -> 1.85 us  [from_matching(): return lax.ppermute(value, axes, pairs)]
    pallas_call x13 -> x17, Pallas kernels: 6.83 us -> 7.18 us  [call(): pl.pallas_call(kernel, name=name, out_shape=list(outs), in_specs=spaces o...]
  transfers between devices with their start and end apart: 15 -> 21, of which waited for: 8 -> 11; matrix products, arithmetic and copies ran while one was open for 0% -> 0% of each run, Pallas kernels for 6% -> 8%
where the time goes in v4:
time: 62.5 us; the launch traced here: 62.3 us
  starting transfers between devices  28.7 us (46%)
  waiting for transfers between devices  25.6 us (41%)
  Pallas kernels  7.18 us (11%)
  between operations  0.8 us (1%)
    ppermute x6, waiting for transfers between devices, over_dp(): return lax.ppermute(value, ('dp', 'core'), pairs)  15.7 us
    ppermute x9, starting transfers between devices, over_z(): return lax.ppermute(value, axes, pairs)  11.7 us
    ppermute x6, starting transfers between devices, over_dp(): return lax.ppermute(value, ('dp', 'core'), pairs)  9.14 us
    pallas_call x17, Pallas kernels, call(): pl.pallas_call(kernel, name=name, out_shape=list(outs), in_specs=spaces o...  7.18 us
    ppermute x2, starting transfers between devices, from_matching(): return lax.ppermute(value, axes, pairs)  7.16 us
    ppermute x9, waiting for transfers between devices, over_z(): return lax.ppermute(value, axes, pairs)  7.08 us
    ppermute x2, waiting for transfers between devices, from_matching(): return lax.ppermute(value, axes, pairs)  1.85 us
  transfers between devices with their start and end apart: 21, of which 11 were waited for; matrix products, arithmetic and copies ran while one was open for 0% of the time, Pallas kernels for 8%

profile of v4, /device:TPU:0, one launch (start us, length us, event | category | flops | bytes accessed | tf_op | source)
XLA Modules:
  0.0 62.3 jit_solution(4124272783136174228)
XLA Ops:
  0.6 1.3 %pack.1 = (bf16[128,768]{1,0:T(8,128)(2,1)S(1)}, bf16[128,896]{1,0:T(8,128)(2,1)S(1)}, bf16[128,1024]{1,0:T(8,128)(2,1)S(1)}, f32[1,128]{1,0:T(1,128)S(1)}) custom-call(bf16[1,128,512]{2,1,0:T(8,128)(2,1)} %q.1, bf16[1,128,512]{2,1,0:T(8,128)(2,1)} %k.1, bf16[1,128,512]{2,1,0:T(8,128)(2,1)} %v.1, bf16[1,128,1024]{2,1,0:T(8,128)(2,1)} %og.1, ...), custom_call_target="tpu_custom_call" | custom-call | bytes 1476096 | tf_op jit(solution)/shard_map/pack/pallas_call | solution.py:66
  2.0 0.5 collective-permute-start
  2.5 0.1 collective-permute-start.5
  2.6 1.0 %collective-permute-done.pair.refs_6_ = bf16[128,896]{1,0:T(8,128)(2,1)S(1)} collective-permute-done((bf16[128,896]{1,0:T(8,128)(2,1)S(1)}, bf16[128,896]{1,0:T(8,128)(2,1)S(1)}, u32[]{:S(2)}, u32[]{:S(2)}) %collective-permute-start) | collective-permute-done | bytes 229408 | tf_op jit(solution)/shard_map/ppermute | solution.py:398
  3.6 0.2 state.1
  3.9 5.9 %collective-permute-start.1 = (bf16[128,256]{1,0:T(8,128)(2,1)S(1)}, bf16[128,256]{1,0:T(8,128)(2,1)S(1)}, u32[]{:S(2)}, u32[]{:S(2)}) collective-permute-start(bf16[128,256]{1,0:T(8,128)(2,1)S(1)} %get-tuple-element.49.own), channel_id=1, source_target_pairs={{0,4},{3,7},{4,0},{7,3},{8,12},{11,15},{12,8},{15,11},{16,20},{19,... | collective-permute-start | bytes 196616 | tf_op jit(solution)/shard_map/ppermute | solution.py:413
  9.7 0.1 collective-permute-start.6
  9.8 1.5 %collective-permute-start.7 = (bf16[128,384]{1,0:T(8,128)(2,1)S(1)}, bf16[128,384]{1,0:T(8,128)(2,1)S(1)}, u32[]{:S(2)}, u32[]{:S(2)}) collective-permute-start(bf16[128,384]{1,0:T(8,128)(2,1)S(1)} %get-tuple-element.52), channel_id=1, source_target_pairs={{0,6},{1,3},{2,4},{3,1},{4,2},{5,7},{6,0},{7,5},{8,14},{9,11},{10,... | collective-permute-start | bytes 294920 | tf_op jit(solution)/shard_map/ppermute | solution.py:409
  11.3 1.8 %collective-permute-done.1.got = bf16[128,256]{1,0:T(8,128)(2,1)S(1)} collective-permute-done((bf16[128,256]{1,0:T(8,128)(2,1)S(1)}, bf16[128,256]{1,0:T(8,128)(2,1)S(1)}, u32[]{:S(2)}, u32[]{:S(2)}) %collective-permute-start.1) | collective-permute-done | bytes 65568 | tf_op jit(solution)/shard_map/ppermute | solution.py:413
  13.2 1.3 %collective-permute-start.2 = (bf16[256,256]{1,0:T(8,128)(2,1)S(1)}, bf16[256,256]{1,0:T(8,128)(2,1)S(1)}, u32[]{:S(2)}, u32[]{:S(2)}) collective-permute-start(bf16[256,256]{1,0:T(8,128)(2,1)S(1)} %w_two.1.own), channel_id=1, source_target_pairs={{0,2},{3,1},{4,6},{7,5},{8,10},{11,9},{12,14},{15,13},{16,18},{19,... | collective-permute-start | bytes 393224 | tf_op jit(solution)/shard_map/ppermute | solution.py:413
  14.5 2.3 %collective-permute-start.8 = (bf16[128,128]{1,0:T(8,128)(2,1)S(1)}, bf16[128,128]{1,0:T(8,128)(2,1)S(1)}, u32[]{:S(2)}, u32[]{:S(2)}) collective-permute-start(bf16[128,128]{1,0:T(8,128)(2,1)S(1)} %get-tuple-element.56), channel_id=1, source_target_pairs={{0,4},{1,5},{2,6},{3,7},{4,0},{5,1},{6,2},{7,3},{8,12},{9,13},{10,... | collective-permute-start | bytes 98312 | tf_op jit(solution)/shard_map/ppermute | solution.py:409
  16.8 0.0 collective-permute-done.5.og_recv
  16.8 0.5 collective-permute-done.6.a.refs_0_
  17.3 0.0 collective-permute-done.7.b.refs_1_
  17.3 1.2 %soft_forward.1 = (bf16[256,128]{1,0:T(8,128)(2,1)S(1)}, bf16[512,128]{1,0:T(8,128)(2,1)S(1)}, bf16[512,128]{1,0:T(8,128)(2,1)S(1)}, bf16[256,1024]{1,0:T(8,128)...) custom-call(bf16[128,768]{1,0:T(8,128)(2,1)S(1)} %get-tuple-element., ...), custom_call_target="tpu_custom_call" | custom-call | flops 67108864 | bytes 2916352 | tf_op jit(solution)/shard_map/soft_forward/pallas_call | solution.py:66
  18.5 1.0 %collective-permute-done.8.refs_2_ = bf16[128,128]{1,0:T(8,128)(2,1)S(1)} collective-permute-done((bf16[128,128]{1,0:T(8,128)(2,1)S(1)}, bf16[128,128]{1,0:T(8,128)(2,1)S(1)}, u32[]{:S(2)}, u32[]{:S(2)}) %collective-permute-start.8) | collective-permute-done | bytes 32800 | tf_op jit(solution)/shard_map/ppermute | solution.py:409
  19.5 0.7 %lin_forward.1 = (f32[256,128]{1,0:T(8,128)S(1)}, f32[128,128]{1,0:T(8,128)S(1)}, f32[128,512]{1,0:T(8,128)S(1)}, bf16[256,512]{1,0:T(8,128)(2,1)S(1)}) custom-call(f32[128,128]{1,0:T(8,128)S(1)} %get-tuple-element.54.state, bf16[128,768]{1,0:T(8,128)(2,1)S(1)} %get-tuple-element.47.mine.refs_5_, bf16[128,896]{1,0:T(8,128)(2,1)S(1)} %collective-permute-done.pair.refs_6_, ...), custom_call_target="tpu_custom_call" | custom-call | flops 67108864 | bytes 2097664 | tf_op jit(solution)/shard_map/lin_forward/pallas_call | solution.py:66
  20.2 2.7 %collective-permute-start.13 = (bf16[256,512]{1,0:T(8,128)(2,1)S(1)}, bf16[256,512]{1,0:T(8,128)(2,1)S(1)}, u32[]{:S(2)}, u32[]{:S(2)}) collective-permute-start(bf16[256,512]{1,0:T(8,128)(2,1)S(1)} %get-tuple-element.81), channel_id=1, source_target_pairs={{0,8},{1,17},{8,0},{9,25},{16,24},{17,1},{24,16},{25,9},{2,10},{3,... | collective-permute-start | bytes 786440 | tf_op jit(solution)/shard_map/ppermute | solution.py:419
  22.9 0.0 collective-permute-done.2.got
  23.0 0.1 collective-permute-start.3
  23.1 5.6 %collective-permute-done.3.second = bf16[256,256]{1,0:T(8,128)(2,1)S(1)} collective-permute-done((bf16[256,256]{1,0:T(8,128)(2,1)S(1)}, bf16[256,256]{1,0:T(8,128)(2,1)S(1)}, u32[]{:S(2)}, u32[]{:S(2)}) %collective-permute-start.3) | collective-permute-done | bytes 131104 | tf_op jit(solution)/shard_map/ppermute | solution.py:419
  28.7 2.1 %collective-permute-start.4 = (bf16[256,512]{1,0:T(8,128)(2,1)S(1)}, bf16[256,512]{1,0:T(8,128)(2,1)S(1)}, u32[]{:S(2)}, u32[]{:S(2)}) collective-permute-start(bf16[256,512]{1,0:T(8,128)(2,1)S(1)} %w_half.1.refs_0_), channel_id=1, source_target_pairs={{0,16},{1,9},{8,24},{9,1},{16,0},{17,25},{24,8},{25,17},{2,18},{3,... | collective-permute-start | bytes 786440 | tf_op jit(solution)/shard_map/ppermute | solution.py:419
  30.8 0.0 collective-permute-done.13.got
  30.8 0.1 fold.1
  30.9 0.1 collective-permute-start.14
  31.0 5.6 %collective-permute-done.14.got = bf16[256,256]{1,0:T(8,128)(2,1)S(1)} collective-permute-done((bf16[256,256]{1,0:T(8,128)(2,1)S(1)}, bf16[256,256]{1,0:T(8,128)(2,1)S(1)}, u32[]{:S(2)}, u32[]{:S(2)}) %collective-permute-start.14) | collective-permute-done | bytes 131104 | tf_op jit(solution)/shard_map/ppermute | solution.py:419
  36.6 0.1 rows.1
  36.6 0.1 collective-permute-start.15
  36.7 0.0 collective-permute-done.4.refs_1_
  36.7 1.5 %backward.1 = (bf16[128,128]{1,0:T(8,128)(2,1)S(1)}, bf16[128,128]{1,0:T(8,128)(2,1)S(1)}, f32[128,128]{1,0:T(8,128)S(1)}, f32[256,128]{1,0:T(8,128)S(1)}, f32[5...) custom-call(bf16[256,512]{1,0:T(8,128)(2,1)S(1)} %w_half.1.refs_0_, bf16[256,512]{1,0:T(8,128)(2,1)S(1)} %collective-permute-done.4.refs_1_, ...), custom_call_target="tpu_custom_call" | custom-call | flops 335544320 | bytes 3310080 | tf_op jit(solution)/shard_map/backward/pallas_call | solution.py:66
  38.3 1.6 %collective-permute-start.10 = (bf16[128,384]{1,0:T(8,128)(2,1)S(1)}, bf16[128,384]{1,0:T(8,128)(2,1)S(1)}, u32[]{:S(2)}, u32[]{:S(2)}) collective-permute-start(bf16[128,384]{1,0:T(8,128)(2,1)S(1)} %get-tuple-element.72), channel_id=1, source_target_pairs={{0,6},{1,3},{2,4},{3,1},{4,2},{5,7},{6,0},{7,5},{8,14},{9,11},{10,... | collective-permute-start | bytes 294920 | tf_op jit(solution)/shard_map/ppermute | solution.py:409
  39.9 0.8 %collective-permute-start.9 = (bf16[128,384]{1,0:T(8,128)(2,1)S(1)}, bf16[128,384]{1,0:T(8,128)(2,1)S(1)}, u32[]{:S(2)}, u32[]{:S(2)}) collective-permute-start(bf16[128,384]{1,0:T(8,128)(2,1)S(1)} %get-tuple-element.71), channel_id=1, source_target_pairs={{0,2},{1,7},{2,0},{3,5},{4,6},{5,3},{6,4},{7,1},{8,10},{9,15},{10,... | collective-permute-start | bytes 294920 | tf_op jit(solution)/shard_map/ppermute | solution.py:409
  40.7 2.0 %collective-permute-start.11 = (bf16[128,128]{1,0:T(8,128)(2,1)S(1)}, bf16[128,128]{1,0:T(8,128)(2,1)S(1)}, u32[]{:S(2)}, u32[]{:S(2)}) collective-permute-start(bf16[128,128]{1,0:T(8,128)(2,1)S(1)} %get-tuple-element.73), channel_id=1, source_target_pairs={{0,4},{1,5},{2,6},{3,7},{4,0},{5,1},{6,2},{7,3},{8,12},{9,13},{10,... | collective-permute-start | bytes 98312 | tf_op jit(solution)/shard_map/ppermute | solution.py:409
  42.8 0.0 collective-permute-done.15.got
  42.8 0.1 collective-permute-start.16
  42.9 2.3 %collective-permute-start.17 = (bf16[64,256]{1,0:T(8,128)(2,1)S(1)}, bf16[64,256]{1,0:T(8,128)(2,1)S(1)}, u32[]{:S(2)}, u32[]{:S(2)}) collective-permute-start(bf16[64,256]{1,0:T(8,128)(2,1)S(1)} %get-tuple-element.88), channel_id=1, source_target_pairs={{0,6},{1,3},{2,4},{3,1},{4,2},{5,7},{6,0},{7,5},{8,14},{9,11},{10,... | collective-permute-start | bytes 98312 | tf_op jit(solution)/shard_map/ppermute | solution.py:409
  45.3 2.2 %collective-permute-done.11.refs_0_ = bf16[128,128]{1,0:T(8,128)(2,1)S(1)} collective-permute-done((bf16[128,128]{1,0:T(8,128)(2,1)S(1)}, bf16[128,128]{1,0:T(8,128)(2,1)S(1)}, u32[]{:S(2)}, u32[]{:S(2)}) %collective-permute-start.11) | collective-permute-done | bytes 32800 | tf_op jit(solution)/shard_map/ppermute | solution.py:409
  47.4 1.0 %collective-permute-start.18 = (bf16[64,256]{1,0:T(8,128)(2,1)S(1)}, bf16[64,256]{1,0:T(8,128)(2,1)S(1)}, u32[]{:S(2)}, u32[]{:S(2)}) collective-permute-start(bf16[64,256]{1,0:T(8,128)(2,1)S(1)} %get-tuple-element.89), channel_id=1, source_target_pairs={{0,4},{1,5},{2,6},{3,7},{4,0},{5,1},{6,2},{7,3},{8,12},{9,13},{10,... | collective-permute-start | bytes 98312 | tf_op jit(solution)/shard_map/ppermute | solution.py:409
  48.4 0.0 collective-permute-done.10.b
  48.4 0.0 collective-permute-done.9.a
  48.4 0.4 final.1
  48.8 0.1 collective-permute-start.12
  48.8 0.0 collective-permute-done.16.a
  48.9 0.2 collective-permute-done.17.b
  49.0 3.2 %collective-permute-done.18.c = bf16[64,256]{1,0:T(8,128)(2,1)S(1)} collective-permute-done((bf16[64,256]{1,0:T(8,128)(2,1)S(1)}, bf16[64,256]{1,0:T(8,128)(2,1)S(1)}, u32[]{:S(2)}, u32[]{:S(2)}) %collective-permute-start.18) | collective-permute-done | bytes 32800 | tf_op jit(solution)/shard_map/ppermute | solution.py:409
  52.2 2.1 %collective-permute-start.19 = (f32[64,256]{1,0:T(8,128)S(1)}, f32[64,256]{1,0:T(8,128)S(1)}, u32[]{:S(2)}, u32[]{:S(2)}) collective-permute-start(f32[64,256]{1,0:T(8,128)S(1)} %weight_sum.1.first), channel_id=1, source_target_pairs={{0,8},{1,17},{8,0},{9,25},{16,24},{17,1},{24,16},{25,9},{2,10},{3,... | collective-permute-start | bytes 196616 | tf_op jit(solution)/shard_map/ppermute | solution.py:419
  54.3 2.3 %collective-permute-done.19.second = f32[64,256]{1,0:T(8,128)S(1)} collective-permute-done((f32[64,256]{1,0:T(8,128)S(1)}, f32[64,256]{1,0:T(8,128)S(1)}, u32[]{:S(2)}, u32[]{:S(2)}) %collective-permute-start.19) | collective-permute-done | bytes 65568 | tf_op jit(solution)/shard_map/ppermute | solution.py:419
  56.6 2.1 %collective-permute-start.20 = (f32[64,512]{1,0:T(8,128)S(1)}, f32[64,512]{1,0:T(8,128)S(1)}, u32[]{:S(2)}, u32[]{:S(2)}) collective-permute-start(f32[64,512]{1,0:T(8,128)S(1)} %both.1), channel_id=1, source_target_pairs={{0,16},{1,9},{8,24},{9,1},{16,0},{17,25},{24,8},{25,17},{2,18},{3,... | collective-permute-start | bytes 393224 | tf_op jit(solution)/shard_map/ppermute | solution.py:419
  58.7 0.0 collective-permute-done.12.pair
  58.7 0.8 %outputs.1 = (bf16[1,128,512]{2,1,0:T(8,128)(2,1)}, bf16[1,128,512]{2,1,0:T(8,128)(2,1)}, bf16[1,128,512]{2,1,0:T(8,128)(2,1)}) custom-call(bf16[128,768]{1,0:T(8,128)(2,1)S(1)} %get-tuple-element.74.own, bf16[128,768]{1,0:T(8,128)(2,1)S(1)} %collective-permute-done.12.pair), custom_call_target="tpu_custom_call" | custom-call | bytes 786432 | tf_op jit(solution)/shard_map/outputs/pallas_call | solution.py:66
  59.5 2.1 %collective-permute-done.20.got = f32[64,512]{1,0:T(8,128)S(1)} collective-permute-done((f32[64,512]{1,0:T(8,128)S(1)}, f32[64,512]{1,0:T(8,128)S(1)}, u32[]{:S(2)}, u32[]{:S(2)}) %collective-permute-start.20) | collective-permute-done | bytes 131104 | tf_op jit(solution)/shard_map/ppermute | solution.py:419
  61.6 0.7 %weight_join.1 = f32[64,1024]{1,0:T(8,128)} custom-call(f32[64,512]{1,0:T(8,128)S(1)} %both.1, f32[64,512]{1,0:T(8,128)S(1)} %collective-permute-done.20.got, bf16[1,128,512]{2,1,0:T(8,128)(2,1)} %get-tuple-element.43._), custom_call_target="tpu_custom_call" | custom-call | bytes 655360 | tf_op jit(solution)/shard_map/weight_join/pallas_call | solution.py:66
  (7 shorter events, 0.2 us)
Async XLA Ops:
  2.0 1.6 %collective-permute-start = (bf16[128,896]{1,0:T(8,128)(2,1)S(1)}, bf16[128,896]{1,0:T(8,128)(2,1)S(1)}, u32[]{:S(2)}, u32[]{:S(2)}) collective-permute-start(bf16[128,896]{1,0:T(8,128)(2,1)S(1)} %get-tuple-element.48.refs_0_), channel_id=1, source_target_pairs={{0,1},{1,0},{2,3},{3,2},{4,5},{5,4},{6,7},{7,6},{8,9},{9,8},{10,11... | collective-permute-start | bytes 688136 | tf_op jit(solution)/shard_map/ppermute | solution.py:398
  2.5 14.3 %collective-permute-start.5 = (bf16[128,1024]{1,0:T(8,128)(2,1)S(1)}, bf16[128,1024]{1,0:T(8,128)(2,1)S(1)}, u32[]{:S(2)}, u32[]{:S(2)}) collective-permute-start(bf16[128,1024]{1,0:T(8,128)(2,1)S(1)} %get-tuple-element.50.og), channel_id=1, source_target_pairs={{0,1},{1,0},{2,3},{3,2},{4,5},{5,4},{6,7},{7,6},{8,9},{9,8},{10,11... | collective-permute-start | bytes 786440 | tf_op jit(solution)/shard_map/ppermute | solution.py:398
  3.9 9.3 %collective-permute-start.1 = (bf16[128,256]{1,0:T(8,128)(2,1)S(1)}, bf16[128,256]{1,0:T(8,128)(2,1)S(1)}, u32[]{:S(2)}, u32[]{:S(2)}) collective-permute-start(bf16[128,256]{1,0:T(8,128)(2,1)S(1)} %get-tuple-element.49.own), channel_id=1, source_target_pairs={{0,4},{3,7},{4,0},{7,3},{8,12},{11,15},{12,8},{15,11},{16,20},{19,... | collective-permute-start | bytes 196616 | tf_op jit(solution)/shard_map/ppermute | solution.py:413
  9.7 7.6 %collective-permute-start.6 = (bf16[128,384]{1,0:T(8,128)(2,1)S(1)}, bf16[128,384]{1,0:T(8,128)(2,1)S(1)}, u32[]{:S(2)}, u32[]{:S(2)}) collective-permute-start(bf16[128,384]{1,0:T(8,128)(2,1)S(1)} %get-tuple-element.51), channel_id=1, source_target_pairs={{0,2},{1,7},{2,0},{3,5},{4,6},{5,3},{6,4},{7,1},{8,10},{9,15},{10,... | collective-permute-start | bytes 294920 | tf_op jit(solution)/shard_map/ppermute | solution.py:409
  9.8 7.5 %collective-permute-start.7 = (bf16[128,384]{1,0:T(8,128)(2,1)S(1)}, bf16[128,384]{1,0:T(8,128)(2,1)S(1)}, u32[]{:S(2)}, u32[]{:S(2)}) collective-permute-start(bf16[128,384]{1,0:T(8,128)(2,1)S(1)} %get-tuple-element.52), channel_id=1, source_target_pairs={{0,6},{1,3},{2,4},{3,1},{4,2},{5,7},{6,0},{7,5},{8,14},{9,11},{10,... | collective-permute-start | bytes 294920 | tf_op jit(solution)/shard_map/ppermute | solution.py:409
  13.2 9.8 %collective-permute-start.2 = (bf16[256,256]{1,0:T(8,128)(2,1)S(1)}, bf16[256,256]{1,0:T(8,128)(2,1)S(1)}, u32[]{:S(2)}, u32[]{:S(2)}) collective-permute-start(bf16[256,256]{1,0:T(8,128)(2,1)S(1)} %w_two.1.own), channel_id=1, source_target_pairs={{0,2},{3,1},{4,6},{7,5},{8,10},{11,9},{12,14},{15,13},{16,18},{19,... | collective-permute-start | bytes 393224 | tf_op jit(solution)/shard_map/ppermute | solution.py:413
  14.5 5.1 %collective-permute-start.8 = (bf16[128,128]{1,0:T(8,128)(2,1)S(1)}, bf16[128,128]{1,0:T(8,128)(2,1)S(1)}, u32[]{:S(2)}, u32[]{:S(2)}) collective-permute-start(bf16[128,128]{1,0:T(8,128)(2,1)S(1)} %get-tuple-element.56), channel_id=1, source_target_pairs={{0,4},{1,5},{2,6},{3,7},{4,0},{5,1},{6,2},{7,3},{8,12},{9,13},{10,... | collective-permute-start | bytes 98312 | tf_op jit(solution)/shard_map/ppermute | solution.py:409
  20.2 10.6 %collective-permute-start.13 = (bf16[256,512]{1,0:T(8,128)(2,1)S(1)}, bf16[256,512]{1,0:T(8,128)(2,1)S(1)}, u32[]{:S(2)}, u32[]{:S(2)}) collective-permute-start(bf16[256,512]{1,0:T(8,128)(2,1)S(1)} %get-tuple-element.81), channel_id=1, source_target_pairs={{0,8},{1,17},{8,0},{9,25},{16,24},{17,1},{24,16},{25,9},{2,10},{3,... | collective-permute-start | bytes 786440 | tf_op jit(solution)/shard_map/ppermute | solution.py:419
  23.0 5.7 %collective-permute-start.3 = (bf16[256,256]{1,0:T(8,128)(2,1)S(1)}, bf16[256,256]{1,0:T(8,128)(2,1)S(1)}, u32[]{:S(2)}, u32[]{:S(2)}) collective-permute-start(bf16[256,256]{1,0:T(8,128)(2,1)S(1)} %w_pick.1.first), channel_id=1, source_target_pairs={{0,8},{1,17},{8,0},{9,25},{16,24},{17,1},{24,16},{25,9},{2,10},{3,... | collective-permute-start | bytes 393224 | tf_op jit(solution)/shard_map/ppermute | solution.py:419
  28.7 8.0 %collective-permute-start.4 = (bf16[256,512]{1,0:T(8,128)(2,1)S(1)}, bf16[256,512]{1,0:T(8,128)(2,1)S(1)}, u32[]{:S(2)}, u32[]{:S(2)}) collective-permute-start(bf16[256,512]{1,0:T(8,128)(2,1)S(1)} %w_half.1.refs_0_), channel_id=1, source_target_pairs={{0,16},{1,9},{8,24},{9,1},{16,0},{17,25},{24,8},{25,17},{2,18},{3,... | collective-permute-start | bytes 786440 | tf_op jit(solution)/shard_map/ppermute | solution.py:419
  30.9 5.7 %collective-permute-start.14 = (bf16[256,256]{1,0:T(8,128)(2,1)S(1)}, bf16[256,256]{1,0:T(8,128)(2,1)S(1)}, u32[]{:S(2)}, u32[]{:S(2)}) collective-permute-start(bf16[256,256]{1,0:T(8,128)(2,1)S(1)} %get-tuple-element.83), channel_id=1, source_target_pairs={{0,16},{1,9},{8,24},{9,1},{16,0},{17,25},{24,8},{25,17},{2,18},{3,... | collective-permute-start | bytes 393224 | tf_op jit(solution)/shard_map/ppermute | solution.py:419
  36.6 6.1 %collective-permute-start.15 = (f32[128,256]{1,0:T(8,128)S(1)}, f32[128,256]{1,0:T(8,128)S(1)}, u32[]{:S(2)}, u32[]{:S(2)}) collective-permute-start(f32[128,256]{1,0:T(8,128)S(1)} %get-tuple-element.85), channel_id=1, source_target_pairs={{0,1},{1,0},{2,3},{3,2},{4,5},{5,4},{6,7},{7,6},{8,9},{9,8},{10,11... | collective-permute-start | bytes 393224 | tf_op jit(solution)/shard_map/ppermute | solution.py:398
  38.3 10.1 %collective-permute-start.10 = (bf16[128,384]{1,0:T(8,128)(2,1)S(1)}, bf16[128,384]{1,0:T(8,128)(2,1)S(1)}, u32[]{:S(2)}, u32[]{:S(2)}) collective-permute-start(bf16[128,384]{1,0:T(8,128)(2,1)S(1)} %get-tuple-element.72), channel_id=1, source_target_pairs={{0,6},{1,3},{2,4},{3,1},{4,2},{5,7},{6,0},{7,5},{8,14},{9,11},{10,... | collective-permute-start | bytes 294920 | tf_op jit(solution)/shard_map/ppermute | solution.py:409
  39.9 8.5 %collective-permute-start.9 = (bf16[128,384]{1,0:T(8,128)(2,1)S(1)}, bf16[128,384]{1,0:T(8,128)(2,1)S(1)}, u32[]{:S(2)}, u32[]{:S(2)}) collective-permute-start(bf16[128,384]{1,0:T(8,128)(2,1)S(1)} %get-tuple-element.71), channel_id=1, source_target_pairs={{0,2},{1,7},{2,0},{3,5},{4,6},{5,3},{6,4},{7,1},{8,10},{9,15},{10,... | collective-permute-start | bytes 294920 | tf_op jit(solution)/shard_map/ppermute | solution.py:409
  40.7 6.7 %collective-permute-start.11 = (bf16[128,128]{1,0:T(8,128)(2,1)S(1)}, bf16[128,128]{1,0:T(8,128)(2,1)S(1)}, u32[]{:S(2)}, u32[]{:S(2)}) collective-permute-start(bf16[128,128]{1,0:T(8,128)(2,1)S(1)} %get-tuple-element.73), channel_id=1, source_target_pairs={{0,4},{1,5},{2,6},{3,7},{4,0},{5,1},{6,2},{7,3},{8,12},{9,13},{10,... | collective-permute-start | bytes 98312 | tf_op jit(solution)/shard_map/ppermute | solution.py:409
  42.8 6.0 %collective-permute-start.16 = (bf16[64,256]{1,0:T(8,128)(2,1)S(1)}, bf16[64,256]{1,0:T(8,128)(2,1)S(1)}, u32[]{:S(2)}, u32[]{:S(2)}) collective-permute-start(bf16[64,256]{1,0:T(8,128)(2,1)S(1)} %get-tuple-element.87), channel_id=1, source_target_pairs={{0,2},{1,7},{2,0},{3,5},{4,6},{5,3},{6,4},{7,1},{8,10},{9,15},{10,... | collective-permute-start | bytes 98312 | tf_op jit(solution)/shard_map/ppermute | solution.py:409
  42.9 6.1 %collective-permute-start.17 = (bf16[64,256]{1,0:T(8,128)(2,1)S(1)}, bf16[64,256]{1,0:T(8,128)(2,1)S(1)}, u32[]{:S(2)}, u32[]{:S(2)}) collective-permute-start(bf16[64,256]{1,0:T(8,128)(2,1)S(1)} %get-tuple-element.88), channel_id=1, source_target_pairs={{0,6},{1,3},{2,4},{3,1},{4,2},{5,7},{6,0},{7,5},{8,14},{9,11},{10,... | collective-permute-start | bytes 98312 | tf_op jit(solution)/shard_map/ppermute | solution.py:409
  47.4 4.8 %collective-permute-start.18 = (bf16[64,256]{1,0:T(8,128)(2,1)S(1)}, bf16[64,256]{1,0:T(8,128)(2,1)S(1)}, u32[]{:S(2)}, u32[]{:S(2)}) collective-permute-start(bf16[64,256]{1,0:T(8,128)(2,1)S(1)} %get-tuple-element.89), channel_id=1, source_target_pairs={{0,4},{1,5},{2,6},{3,7},{4,0},{5,1},{6,2},{7,3},{8,12},{9,13},{10,... | collective-permute-start | bytes 98312 | tf_op jit(solution)/shard_map/ppermute | solution.py:409
  48.8 9.9 %collective-permute-start.12 = (bf16[128,768]{1,0:T(8,128)(2,1)S(1)}, bf16[128,768]{1,0:T(8,128)(2,1)S(1)}, u32[]{:S(2)}, u32[]{:S(2)}) collective-permute-start(bf16[128,768]{1,0:T(8,128)(2,1)S(1)} %get-tuple-element.75), channel_id=1, source_target_pairs={{0,1},{1,0},{2,3},{3,2},{4,5},{5,4},{6,7},{7,6},{8,9},{9,8},{10,11... | collective-permute-start | bytes 589832 | tf_op jit(solution)/shard_map/ppermute | solution.py:398
  52.2 4.3 %collective-permute-start.19 = (f32[64,256]{1,0:T(8,128)S(1)}, f32[64,256]{1,0:T(8,128)S(1)}, u32[]{:S(2)}, u32[]{:S(2)}) collective-permute-start(f32[64,256]{1,0:T(8,128)S(1)} %weight_sum.1.first), channel_id=1, source_target_pairs={{0,8},{1,17},{8,0},{9,25},{16,24},{17,1},{24,16},{25,9},{2,10},{3,... | collective-permute-start | bytes 196616 | tf_op jit(solution)/shard_map/ppermute | solution.py:419
  56.6 5.0 %collective-permute-start.20 = (f32[64,512]{1,0:T(8,128)S(1)}, f32[64,512]{1,0:T(8,128)S(1)}, u32[]{:S(2)}, u32[]{:S(2)}) collective-permute-start(f32[64,512]{1,0:T(8,128)S(1)} %both.1), channel_id=1, source_target_pairs={{0,16},{1,9},{8,24},{9,1},{16,0},{17,25},{24,8},{25,17},{2,18},{3,... | collective-permute-start | bytes 393224 | tf_op jit(solution)/shard_map/ppermute | solution.py:419

commit v5 on v4

--- a/solution.py
+++ b/solution.py
@@ -94,7 +94,7 @@
     )
 
 
-def pack_kernel(q, k, v, og, w, gain, mine_out, other_out, og_out, gain_out, sems):
+def pack_kernel(q, k, v, og, w, gain, mine_out, other_out, og_out, w_out, gain_out, sems):
     core, _, dp = places()
     mine, other = core * DH, (1 - core) * DH
     copies = []
@@ -104,19 +104,13 @@
         copy.start()
         copies.append(copy)
 
-    width = w.shape[1] // lax.axis_size("dp")
-    rows = w.shape[0]
     for index, array in enumerate((q, k, v)):
         for group in range(2):
             cols = slice((3 * group + index) * DH, (3 * group + index + 1) * DH)
             fetch(array.at[0, :, at(SOFT * group + other)], other_out.at[:, cols])
             fetch(array.at[0, :, at(SOFT * group + mine)], mine_out.at[:, cols])
-    if other_out.shape[1] > 6 * DH:
-        for side in range(2):
-            fetch(
-                w.at[:, at(dp * width + side * DH)],
-                other_out.at[side * rows : (side + 1) * rows, 6 * DH :],
-            )
+    width = w_out.shape[1]
+    fetch(w.at[:, at(dp * width, width)], w_out)
     fetch(og.at[0], og_out)
     fetch(gain.at[at(mine)], gain_out.at[0])
     for copy in copies:
@@ -129,7 +123,7 @@
         unit_plus(pair[:, KL].astype(F32)), pair[:, VL], TN
     )
     if direct:
-        other, state, to_a, to_b, to_c, w_head = refs
+        w, state, to_a, to_b, to_c = refs
     else:
         state, to_a, to_b = refs
     state[...] = total
@@ -138,31 +132,37 @@
         here = block == core
         out[:, :DH] = jnp.where(here, mine[:, KS], pair[:, KS])
         out[:, DH : 2 * DH] = jnp.where(here, mine[:, VS], pair[:, VS])
-        if direct:
-            out[:, 2 * DH :] = total.astype(BF)
-    if direct:
-        to_c[...] = total.astype(BF)
-        rows = w_head.shape[0] // 2
-        for source, place in ((other, core), (pair, 1 - core)):
-            for side in range(2):
-                w_head[at(place * rows, rows), side * DH : (side + 1) * DH] = source[
-                    side * rows : (side + 1) * rows, 6 * DH :
-                ]
-
-
-def w_two_kernel(own, got, out):
-    _, z, _ = places()
-    group = lax.div(z, 2)
-    out[at(group * DH), :] = own[...]
-    out[at((1 - group) * DH), :] = got[...]
-
-
-def w_pick_kernel(own, got, out):
+    if direct:
+        rows = w.shape[0]
+        for out, first in ((to_a, 2 * DH), (to_b, 2 * DH), (to_c, 0)):
+            out[:, first : first + DH] = total.astype(BF)
+            out[:rows, first + DH :] = w[:, :DH]
+            out[rows:, first + DH :] = w[:, DH:]
+
+
+def relay_kernel(w, a, b, c, keep, send, heads):
     core, z, _ = places()
-    out[...] = jnp.where(lax.rem(z, 2) == core, own[...], got[...])
-
-
-def join_kernel(first, second, out):
+    way = links(True)
+    rows = w.shape[0]
+    heads[z] = w[...]
+    for source, first, step in ((a, 3 * DH, way["first"]), (b, 3 * DH, way["second"]), (c, DH, 2)):
+        heads[z ^ step, :, :DH] = source[:rows, first:]
+        heads[z ^ step, :, DH:] = source[rows:, first:]
+    for group in range(2):
+        keep[group] = heads[2 * group + core]
+        send[group] = heads[2 * group + 1 - core]
+
+
+def w_rows_kernel(keep, got, out):
+    core, _, _ = places()
+    half = keep.shape[1]
+    for group in range(2):
+        out[at(group * DH + core * half, half), :] = keep[group]
+        out[at(group * DH + (1 - core) * half, half), :] = got[group]
+
+
+def join_kernel(first, second, *refs):
+    out = refs[-1]
     width = first.shape[1]
     out[:, :width] = first[...]
     out[:, width:] = second[...]
@@ -222,7 +222,8 @@
     total = state[...]
     if direct:
         a, b, c, soft_send, u_out, total_out, keep, out = refs
-        total = total + a[:, 2 * DH :].astype(F32) + b[:, 2 * DH :].astype(F32) + c[...].astype(F32)
+        total = total + a[:, 2 * DH : 3 * DH].astype(F32) + b[:, 2 * DH : 3 * DH].astype(F32)
+        total = total + c[:, :DH].astype(F32)
     else:
         u_out, total_out, keep = refs
     total_out[...] = total
@@ -289,7 +290,7 @@
 def backward_kernel(direct, *refs):
     if direct:
         sent, got = refs[:2]
-        refs = refs[2:]
+        refs = refs[3:]
     else:
         weights = refs[0]
         refs = refs[1:]
@@ -313,7 +314,7 @@
     way = links(direct)
     span = dk_soft.shape[0]
     if direct:
-        dstate, to_a, to_b, to_c = refs
+        dstate, _, to_a, to_b, to_c = refs
         to_c[...] = dstate[...].astype(BF)
     else:
         to_a, to_b = refs
@@ -339,7 +340,8 @@
 
 
 def weight_sum_kernel(scale, chunk, a, b, c, out):
-    out[...] = scale * (chunk[...] + a[...].astype(F32) + b[...].astype(F32) + c[...].astype(F32))
+    total = chunk[...] + a[...].astype(F32) + b[...].astype(F32) + c[...].astype(F32)
+    out[...] = (scale * total).astype(out.dtype)
 
 
 def final_kernel(
@@ -377,7 +379,7 @@
             out[0, :, at(SOFT + first)] = source[:, (3 + index) * DH : (4 + index) * DH]
 
 
-def weight_join_kernel(both, got, _, out):
+def weight_join_kernel(both, got, out):
     _, _, dp = places()
     way = links(True)
     width = both.shape[1] // 2
@@ -393,6 +395,8 @@
     direct = n_z == HEADS and n_dp == 4
     width = model // n_dp
     half = DH // 2
+
+    scale = 1.0 / math.sqrt(n_dp * n_z * 2 * rows)
 
     def over_core(value):
         return lax.ppermute(value, "core", pair_perm)
@@ -408,25 +412,22 @@
                 pairs.append((2 * z + c, 2 * there + c))
         return lax.ppermute(value, axes, pairs)
 
-    def from_matching(value, step):
-        pairs = [(2 * z + z % 2, 2 * (z ^ step) + z % 2) for z in range(n_z)]
-        return lax.ppermute(value, axes, pairs)
-
     def over_dp(value, which):
         pairs = [
             (2 * d + c, 2 * (d ^ (1 + c, 2 - c)[which]) + c) for d in range(n_dp) for c in range(2)
         ]
         return lax.ppermute(value, ("dp", "core"), pairs)
 
+    vmem = pl.BlockSpec(memory_space=pltpu.VMEM)
+
     def hbm(value):
         return pltpu.with_memory_space_constraint(value, pltpu.HBM)
 
-    sent_cols = 7 * DH if direct else 6 * DH
-    mine, other, og, gain = call(
+    mine, other, og, w_part, gain = call(
         pack_kernel, "pack",
         [
-            like((rows, 6 * DH), BF), like((rows, sent_cols), BF), like((rows, model), BF),
-            like((1, DH), F32),
+            like((rows, 6 * DH), BF), like((rows, 6 * DH), BF), like((rows, model), BF),
+            like((out_weight.shape[0], width), BF), like((1, DH), F32),
         ],
         [hbm(x) for x in (queries, key_rows, value_rows, out_grad, out_weight, norm_gain)],
         scratch=[pltpu.SemaphoreType.DMA((16,))],
@@ -434,24 +435,24 @@
     )
     pair = over_core(other)
     og_recv = over_core(og)
-    wide = 3 * DH if direct else 2 * DH
+    wide = 4 * DH if direct else 2 * DH
     state, to_a, to_b, *rest = call(
         functools.partial(state_kernel, direct), "state",
         [like((DH, DH), F32), like((rows, wide), BF), like((rows, wide), BF)]
-        + [like((DH, DH), BF), like((DH, width), BF)] * direct,
-        [mine, pair] + [other] * direct,
+        + [like((rows, 2 * DH), BF)] * direct,
+        [mine, pair] + [w_part] * direct,
         flops=4 * 2 * rows * DH * DH,
     )
     if direct:
-        to_c, w_head = rest
-        w_got = from_matching(w_head, 2)
-        a, b, c = over_z(to_a, 0), over_z(to_b, 1), [over_z(to_c, 2)]
-        w_two = call(w_two_kernel, "w_two", [like((2 * DH, width), BF)], [w_head, w_got])[0]
-        w_got = from_matching(w_two, 1)
-        w_own = call(w_pick_kernel, "w_pick", [like((2 * DH, width), BF)], [w_two, w_got])[0]
+        a, b, c = over_z(to_a, 0), over_z(to_b, 1), [over_z(rest[0], 2)]
+        w_keep, w_send = call(
+            relay_kernel, "relay", [like((2, half, width), BF)] * 2, [w_part, a, b] + c,
+            scratch=[pltpu.VMEM((HEADS, half, width), BF)],
+        )
+        w_own = call(
+            w_rows_kernel, "w_rows", [like((2 * DH, width), BF)], [w_keep, over_core(w_send)]
+        )[0]
         w_got = over_dp(w_own, 0)
-        w_half = call(join_kernel, "w_half", [like((2 * DH, 2 * width), BF)], [w_own, w_got])[0]
-        weights = [w_half, over_dp(w_half, 1)]
     else:
         a, b, c = over_z(to_a, 0), over_z(to_b, 1), []
         state = lax.psum(state, "z")
@@ -484,6 +485,10 @@
             fold_kernel, "fold", [like((2 * DH, width), F32), like((2 * DH, width), BF)],
             [keep_soft, keep_lin, got],
         )
+        w_half = call(
+            join_kernel, "w_half", [like((2 * DH, 2 * width), BF)], [w_own, w_got, sent]
+        )[0]
+        weights = [w_half, over_dp(w_half, 1)]
         got = over_dp(sent, 1)
         row_own, row_send = call(
             rows_kernel, "rows", [like((2 * half, width), F32)] * 2, [keep, got],
@@ -495,6 +500,18 @@
             [row_own, row_recv], scratch=[pltpu.VMEM((HEADS, half, width), F32)],
         )
         chunks = [over_z(value, which) for which, value in enumerate(to_chips)]
+        summed = call(
+            functools.partial(weight_sum_kernel, scale), "weight_sum", [like((half, width), BF)],
+            [chunk] + chunks,
+        )[0]
+        got = over_dp(summed, 0)
+        both = call(join_kernel, "both", [like((half, 2 * width), BF)], [summed, got])[0]
+        got = over_dp(both, 1)
+        weight_grad = call(
+            weight_join_kernel, "weight_join", [like((half, model), F32)], [both, got]
+        )[0]
+    if direct:
+        weights.append(chunk)
     dq_lin, dq_lin_pair, dstate, dq_soft, dk_soft, dv_soft = call(
         functools.partial(backward_kernel, direct), "backward",
         [
@@ -506,11 +523,11 @@
         + [pltpu.VMEM((2 * DH, model), BF)] * direct,
         flops=5 * wg_flops,
     )
-    scale = 1.0 / math.sqrt(n_dp * n_z * 2 * rows)
+    wide = 3 * DH if direct else 2 * DH
     to_a, to_b, *to_c = call(
         functools.partial(halo_kernel, direct), "halo",
         [like((rows, wide), BF), like((rows, wide), BF)] + [like((DH, DH), BF)] * direct,
-        [dk_soft, dv_soft] + [dstate] * direct,
+        [dk_soft, dv_soft] + ([dstate, summed] if direct else []),
     )
     a, b = over_z(to_a, 0, True), over_z(to_b, 1, True)
     c = [over_z(value, 2) for value in to_c]
@@ -525,26 +542,15 @@
     own_out, to_pair = call(
         functools.partial(final_kernel, direct), "final",
         [like((rows, 6 * DH), BF), like((rows, 6 * DH), BF)],
-        [dstate, mine, pair, dq_soft, dk_soft, dv_soft, dq_lin, dq_lin_pair, a, b] + c,
+        [dstate, mine, pair, dq_soft, dk_soft, dv_soft, dq_lin, dq_lin_pair, a, b] + c
+        + ([hbm(weight_grad)] if direct else []),
         scratch=[pltpu.VMEM((2 * rows, DH), F32)] * 2,
+        spaces=[vmem] * 11 + [pl.BlockSpec(memory_space=pltpu.HBM)] if direct else None,
         flops=wg_flops // 4,
     )
     from_pair = over_core(to_pair)
     shape = like((1, rows, HEADS * DH), BF)
     dq, dk, dv = call(output_kernel, "outputs", [shape] * 3, [own_out, from_pair])
-    if direct:
-        summed = call(
-            functools.partial(weight_sum_kernel, scale), "weight_sum", [like((half, width), F32)],
-            [chunk] + chunks,
-        )[0]
-        got = over_dp(summed, 0)
-        both = call(join_kernel, "both", [like((half, 2 * width), F32)], [summed, got])[0]
-        got = over_dp(both, 1)
-        vmem = pl.BlockSpec(memory_space=pltpu.VMEM)
-        weight_grad = call(
-            weight_join_kernel, "weight_join", [like((half, model), F32)], [both, got, hbm(dq)],
-            spaces=[vmem, vmem, pl.BlockSpec(memory_space=pltpu.HBM)],
-        )[0]
     return dq, dk, dv, weight_grad
 
 

time: 62.5 us -> 54.5 us (0.87)
  starting transfers between devices: 28.7 us -> 23.9 us
  waiting for transfers between devices: 25.6 us -> 22.5 us
    ppermute x6, waiting for transfers between devices: 15.7 us -> 5.23 us  [over_dp(): return lax.ppermute(value, ('dp', 'core'), pairs)]
    ppermute x2 -> x0, starting transfers between devices: 7.16 us -> none  [from_matching(): return lax.ppermute(value, axes, pairs)]
    ppermute x9, waiting for transfers between devices: 7.08 us -> 12.2 us  [over_z(): return lax.ppermute(value, axes, pairs)]
    ppermute x4 -> x5, waiting for transfers between devices: 1.04 us -> 5 us  [over_core(): return lax.ppermute(value, 'core', pair_perm)]
    ppermute x2 -> x0, waiting for transfers between devices: 1.85 us -> none  [from_matching(): return lax.ppermute(value, axes, pairs)]
    ppermute x6, starting transfers between devices: 9.14 us -> 10.3 us  [over_dp(): return lax.ppermute(value, ('dp', 'core'), pairs)]
    ppermute x9, starting transfers between devices: 11.7 us -> 12.8 us  [over_z(): return lax.ppermute(value, axes, pairs)]
  transfers between devices with their start and end apart: 21 -> 20, of which waited for: 11 -> 14; matrix products, arithmetic and copies ran while one was open for 0% -> 0% of each run, Pallas kernels for 8% -> 7%
where the time goes in v5:
time: 54.5 us; the launch traced here: 54.3 us
  starting transfers between devices  23.9 us (44%)
  waiting for transfers between devices  22.5 us (41%)
  Pallas kernels  7.2 us (13%)
  between operations  0.76 us (1%)
    ppermute x9, starting transfers between devices, over_z(): return lax.ppermute(value, axes, pairs)  12.8 us
    ppermute x9, waiting for transfers between devices, over_z(): return lax.ppermute(value, axes, pairs)  12.2 us
    ppermute x6, starting transfers between devices, over_dp(): return lax.ppermute(value, ('dp', 'core'), pairs)  10.3 us
    pallas_call x17, Pallas kernels, call(): pl.pallas_call(kernel, name=name, out_shape=list(outs), in_specs=spaces o...  7.2 us
    ppermute x6, waiting for transfers between devices, over_dp(): return lax.ppermute(value, ('dp', 'core'), pairs)  5.23 us
    ppermute x5, waiting for transfers between devices, over_core(): return lax.ppermute(value, 'core', pair_perm)  5 us
  transfers between devices with their start and end apart: 20, of which 14 were waited for; matrix products, arithmetic and copies ran while one was open for 0% of the time, Pallas kernels for 7%

profile of v5, /device:TPU:0, one launch (start us, length us, event | category | flops | bytes accessed | tf_op | source)
XLA Modules:
  0.0 54.3 jit_solution(2784463418115981788)
XLA Ops:
  0.6 1.4 %pack.1 = (bf16[128,768]{1,0:T(8,128)(2,1)S(1)}, bf16[128,768]{1,0:T(8,128)(2,1)S(1)}, bf16[128,1024]{1,0:T(8,128)(2,1)S(1)}, bf16[64,256]{1,0:T(8,128)(2,1)S(1)}, f32[1,128]{1,0:T(1,128)S(1)}) custom-call(bf16[1,128,512]{2,1,0:T(8,128)(2,1)} %q.1, bf16[1,128,512]{2,1,0:T(8,128)(2,1)} %k.1, bf16[1,128,512]{2,1,0:T(8,128)(2,1)} %v.1, ...), custom_call_target="tpu_custom_call" | custom-call | bytes 1476096 | tf_op jit(solution)/shard_map/pack/pallas_call | solution.py:66
  2.0 0.5 collective-permute-start
  2.5 0.1 collective-permute-start.6
  2.6 1.0 %collective-permute-done.pair.refs_7_ = bf16[128,768]{1,0:T(8,128)(2,1)S(1)} collective-permute-done((bf16[128,768]{1,0:T(8,128)(2,1)S(1)}, bf16[128,768]{1,0:T(8,128)(2,1)S(1)}, u32[]{:S(2)}, u32[]{:S(2)}) %collective-permute-start) | collective-permute-done | bytes 196640 | tf_op jit(solution)/shard_map/ppermute | solution.py:402
  3.6 0.2 state.1
  3.8 3.0 %collective-permute-start.1 = (bf16[128,512]{1,0:T(8,128)(2,1)S(1)}, bf16[128,512]{1,0:T(8,128)(2,1)S(1)}, u32[]{:S(2)}, u32[]{:S(2)}) collective-permute-start(bf16[128,512]{1,0:T(8,128)(2,1)S(1)} %get-tuple-element.52), channel_id=1, source_target_pairs={{0,2},{1,7},{2,0},{3,5},{4,6},{5,3},{6,4},{7,1},{8,10},{9,15},{10,... | collective-permute-start | bytes 393224 | tf_op jit(solution)/shard_map/ppermute | solution.py:413
  6.8 2.5 %collective-permute-start.2 = (bf16[128,512]{1,0:T(8,128)(2,1)S(1)}, bf16[128,512]{1,0:T(8,128)(2,1)S(1)}, u32[]{:S(2)}, u32[]{:S(2)}) collective-permute-start(bf16[128,512]{1,0:T(8,128)(2,1)S(1)} %get-tuple-element.53), channel_id=1, source_target_pairs={{0,6},{1,3},{2,4},{3,1},{4,2},{5,7},{6,0},{7,5},{8,14},{9,11},{10,... | collective-permute-start | bytes 393224 | tf_op jit(solution)/shard_map/ppermute | solution.py:413
  9.3 0.1 collective-permute-start.3
  9.4 0.0 collective-permute-done.6.og_recv
  9.4 0.4 collective-permute-done.1.a.refs_0_
  9.8 6.5 %collective-permute-done.2.b.refs_1_ = bf16[128,512]{1,0:T(8,128)(2,1)S(1)} collective-permute-done((bf16[128,512]{1,0:T(8,128)(2,1)S(1)}, bf16[128,512]{1,0:T(8,128)(2,1)S(1)}, u32[]{:S(2)}, u32[]{:S(2)}) %collective-permute-start.2) | collective-permute-done | bytes 131104 | tf_op jit(solution)/shard_map/ppermute | solution.py:413
  16.3 1.2 %soft_forward.1 = (bf16[256,128]{1,0:T(8,128)(2,1)S(1)}, bf16[512,128]{1,0:T(8,128)(2,1)S(1)}, bf16[512,128]{1,0:T(8,128)(2,1)S(1)}, bf16[256,1024]{1,0:T(8,128)...) custom-call(bf16[128,768]{1,0:T(8,128)(2,1)S(1)} %get-tuple-element., ...), custom_call_target="tpu_custom_call" | custom-call | flops 67108864 | bytes 2949120 | tf_op jit(solution)/shard_map/soft_forward/pallas_call | solution.py:66
  17.5 0.0 collective-permute-done.3.c.refs_2_
  17.5 0.7 %lin_forward.1 = (f32[256,128]{1,0:T(8,128)S(1)}, f32[128,128]{1,0:T(8,128)S(1)}, f32[128,512]{1,0:T(8,128)S(1)}, bf16[256,512]{1,0:T(8,128)(2,1)S(1)}) custom-call(f32[128,128]{1,0:T(8,128)S(1)} %get-tuple-element.59.state, bf16[128,768]{1,0:T(8,128)(2,1)S(1)} %get-tuple-element.50.mine.refs_6_, bf16[128,768]{1,0:T(8,128)(2,1)S(1)} %collective-permute-done.pair.refs_7_, ...), custom_call_target="tpu_custom_call" | custom-call | flops 67108864 | bytes 2163200 | tf_op jit(solution)/shard_map/lin_forward/pallas_call | solution.py:66
  18.2 1.6 %collective-permute-start.7 = (bf16[256,512]{1,0:T(8,128)(2,1)S(1)}, bf16[256,512]{1,0:T(8,128)(2,1)S(1)}, u32[]{:S(2)}, u32[]{:S(2)}) collective-permute-start(bf16[256,512]{1,0:T(8,128)(2,1)S(1)} %get-tuple-element.64), channel_id=1, source_target_pairs={{0,8},{1,17},{8,0},{9,25},{16,24},{17,1},{24,16},{25,9},{2,10},{3,... | collective-permute-start | bytes 786440 | tf_op jit(solution)/shard_map/ppermute | solution.py:419
  19.8 0.1 collective-permute-start.4
  19.9 1.2 %collective-permute-done.4.got = bf16[2,64,256]{2,1,0:T(8,128)(2,1)S(1)} collective-permute-done((bf16[2,64,256]{2,1,0:T(8,128)(2,1)S(1)}, bf16[2,64,256]{2,1,0:T(8,128)(2,1)S(1)}, u32[]{:S(2)}, u32[]{:S(2)}) %collective-permute-start.4) | collective-permute-done | bytes 65568 | tf_op jit(solution)/shard_map/ppermute | solution.py:402
  21.2 0.6 %collective-permute-start.5 = (bf16[256,256]{1,0:T(8,128)(2,1)S(1)}, bf16[256,256]{1,0:T(8,128)(2,1)S(1)}, u32[]{:S(2)}, u32[]{:S(2)}) collective-permute-start(bf16[256,256]{1,0:T(8,128)(2,1)S(1)} %w_rows.1.first), channel_id=1, source_target_pairs={{0,8},{1,17},{8,0},{9,25},{16,24},{17,1},{24,16},{25,9},{2,10},{3,... | collective-permute-start | bytes 393224 | tf_op jit(solution)/shard_map/ppermute | solution.py:419
  21.8 2.9 %collective-permute-done.7.got = bf16[256,512]{1,0:T(8,128)(2,1)S(1)} collective-permute-done((bf16[256,512]{1,0:T(8,128)(2,1)S(1)}, bf16[256,512]{1,0:T(8,128)(2,1)S(1)}, u32[]{:S(2)}, u32[]{:S(2)}) %collective-permute-start.7) | collective-permute-done | bytes 262176 | tf_op jit(solution)/shard_map/ppermute | solution.py:419
  24.7 0.1 fold.1
  24.7 1.9 %collective-permute-start.9 = (bf16[256,256]{1,0:T(8,128)(2,1)S(1)}, bf16[256,256]{1,0:T(8,128)(2,1)S(1)}, u32[]{:S(2)}, u32[]{:S(2)}) collective-permute-start(bf16[256,256]{1,0:T(8,128)(2,1)S(1)} %get-tuple-element.65.refs_0_), channel_id=1, source_target_pairs={{0,16},{1,9},{8,24},{9,1},{16,0},{17,25},{24,8},{25,17},{2,18},{3,... | collective-permute-start | bytes 393224 | tf_op jit(solution)/shard_map/ppermute | solution.py:419
  26.6 0.6 %collective-permute-done.5.second = bf16[256,256]{1,0:T(8,128)(2,1)S(1)} collective-permute-done((bf16[256,256]{1,0:T(8,128)(2,1)S(1)}, bf16[256,256]{1,0:T(8,128)(2,1)S(1)}, u32[]{:S(2)}, u32[]{:S(2)}) %collective-permute-start.5) | collective-permute-done | bytes 131104 | tf_op jit(solution)/shard_map/ppermute | solution.py:419
  27.1 1.9 %collective-permute-start.8 = (bf16[256,512]{1,0:T(8,128)(2,1)S(1)}, bf16[256,512]{1,0:T(8,128)(2,1)S(1)}, u32[]{:S(2)}, u32[]{:S(2)}) collective-permute-start(bf16[256,512]{1,0:T(8,128)(2,1)S(1)} %w_half.1.refs_0_), channel_id=1, source_target_pairs={{0,16},{1,9},{8,24},{9,1},{16,0},{17,25},{24,8},{25,17},{2,18},{3,... | collective-permute-start | bytes 786440 | tf_op jit(solution)/shard_map/ppermute | solution.py:419
  29.1 0.7 %collective-permute-done.9.got = bf16[256,256]{1,0:T(8,128)(2,1)S(1)} collective-permute-done((bf16[256,256]{1,0:T(8,128)(2,1)S(1)}, bf16[256,256]{1,0:T(8,128)(2,1)S(1)}, u32[]{:S(2)}, u32[]{:S(2)}) %collective-permute-start.9) | collective-permute-done | bytes 131104 | tf_op jit(solution)/shard_map/ppermute | solution.py:419
  29.8 0.1 rows.1
  29.8 0.1 collective-permute-start.10
  29.9 1.3 %collective-permute-done.10.got = f32[128,256]{1,0:T(8,128)S(1)} collective-permute-done((f32[128,256]{1,0:T(8,128)S(1)}, f32[128,256]{1,0:T(8,128)S(1)}, u32[]{:S(2)}, u32[]{:S(2)}) %collective-permute-start.10) | collective-permute-done | bytes 131104 | tf_op jit(solution)/shard_map/ppermute | solution.py:402
  31.3 0.9 %collective-permute-start.11 = (bf16[64,256]{1,0:T(8,128)(2,1)S(1)}, bf16[64,256]{1,0:T(8,128)(2,1)S(1)}, u32[]{:S(2)}, u32[]{:S(2)}) collective-permute-start(bf16[64,256]{1,0:T(8,128)(2,1)S(1)} %get-tuple-element.83), channel_id=1, source_target_pairs={{0,2},{1,7},{2,0},{3,5},{4,6},{5,3},{6,4},{7,1},{8,10},{9,15},{10,... | collective-permute-start | bytes 98312 | tf_op jit(solution)/shard_map/ppermute | solution.py:413
  32.2 3.3 %collective-permute-start.12 = (bf16[64,256]{1,0:T(8,128)(2,1)S(1)}, bf16[64,256]{1,0:T(8,128)(2,1)S(1)}, u32[]{:S(2)}, u32[]{:S(2)}) collective-permute-start(bf16[64,256]{1,0:T(8,128)(2,1)S(1)} %get-tuple-element.84), channel_id=1, source_target_pairs={{0,6},{1,3},{2,4},{3,1},{4,2},{5,7},{6,0},{7,5},{8,14},{9,11},{10,... | collective-permute-start | bytes 98312 | tf_op jit(solution)/shard_map/ppermute | solution.py:413
  35.5 0.0 collective-permute-start.13
  35.5 0.0 collective-permute-done.8.refs_1_
  35.5 1.5 %backward.1 = (bf16[128,128]{1,0:T(8,128)(2,1)S(1)}, bf16[128,128]{1,0:T(8,128)(2,1)S(1)}, f32[128,128]{1,0:T(8,128)S(1)}, f32[256,128]{1,0:T(8,128)S(1)}, f32[5...) custom-call(bf16[256,512]{1,0:T(8,128)(2,1)S(1)} %w_half.1.refs_0_, bf16[256,512]{1,0:T(8,128)(2,1)S(1)} %collective-permute-done.8.refs_1_, ...), custom_call_target="tpu_custom_call" | custom-call | flops 335544320 | bytes 3342848 | tf_op jit(solution)/shard_map/backward/pallas_call | solution.py:66
  37.0 0.0 collective-permute-done.11.a
  37.1 0.8 %collective-permute-done.12.b = bf16[64,256]{1,0:T(8,128)(2,1)S(1)} collective-permute-done((bf16[64,256]{1,0:T(8,128)(2,1)S(1)}, bf16[64,256]{1,0:T(8,128)(2,1)S(1)}, u32[]{:S(2)}, u32[]{:S(2)}) %collective-permute-start.12) | collective-permute-done | bytes 32800 | tf_op jit(solution)/shard_map/ppermute | solution.py:413
  37.9 2.4 %collective-permute-done.13.c = bf16[64,256]{1,0:T(8,128)(2,1)S(1)} collective-permute-done((bf16[64,256]{1,0:T(8,128)(2,1)S(1)}, bf16[64,256]{1,0:T(8,128)(2,1)S(1)}, u32[]{:S(2)}, u32[]{:S(2)}) %collective-permute-start.13) | collective-permute-done | bytes 32800 | tf_op jit(solution)/shard_map/ppermute | solution.py:413
  40.3 2.1 %collective-permute-start.17 = (bf16[64,256]{1,0:T(8,128)(2,1)S(1)}, bf16[64,256]{1,0:T(8,128)(2,1)S(1)}, u32[]{:S(2)}, u32[]{:S(2)}) collective-permute-start(bf16[64,256]{1,0:T(8,128)(2,1)S(1)} %weight_sum.1.refs_1_.first), channel_id=1, source_target_pairs={{0,8},{1,17},{8,0},{9,25},{16,24},{17,1},{24,16},{25,9},{2,10},{3,... | collective-permute-start | bytes 98312 | tf_op jit(solution)/shard_map/ppermute | solution.py:419
  42.5 0.4 collective-permute-start.14
  42.9 1.2 %collective-permute-start.15 = (bf16[128,384]{1,0:T(8,128)(2,1)S(1)}, bf16[128,384]{1,0:T(8,128)(2,1)S(1)}, u32[]{:S(2)}, u32[]{:S(2)}) collective-permute-start(bf16[128,384]{1,0:T(8,128)(2,1)S(1)} %get-tuple-element.87), channel_id=1, source_target_pairs={{0,6},{1,3},{2,4},{3,1},{4,2},{5,7},{6,0},{7,5},{8,14},{9,11},{10,... | collective-permute-start | bytes 294920 | tf_op jit(solution)/shard_map/ppermute | solution.py:413
  44.0 0.3 collective-permute-done.17.second
  44.4 2.2 %collective-permute-start.18 = (bf16[64,512]{1,0:T(8,128)(2,1)S(1)}, bf16[64,512]{1,0:T(8,128)(2,1)S(1)}, u32[]{:S(2)}, u32[]{:S(2)}) collective-permute-start(bf16[64,512]{1,0:T(8,128)(2,1)S(1)} %both.1), channel_id=1, source_target_pairs={{0,16},{1,9},{8,24},{9,1},{16,0},{17,25},{24,8},{25,17},{2,18},{3,... | collective-permute-start | bytes 196616 | tf_op jit(solution)/shard_map/ppermute | solution.py:419
  46.6 1.4 %collective-permute-start.16 = (bf16[128,128]{1,0:T(8,128)(2,1)S(1)}, bf16[128,128]{1,0:T(8,128)(2,1)S(1)}, u32[]{:S(2)}, u32[]{:S(2)}) collective-permute-start(bf16[128,128]{1,0:T(8,128)(2,1)S(1)} %get-tuple-element.88), channel_id=1, source_target_pairs={{0,4},{1,5},{2,6},{3,7},{4,0},{5,1},{6,2},{7,3},{8,12},{9,13},{10,... | collective-permute-start | bytes 98312 | tf_op jit(solution)/shard_map/ppermute | solution.py:413
  48.0 0.8 %collective-permute-done.18.got = bf16[64,512]{1,0:T(8,128)(2,1)S(1)} collective-permute-done((bf16[64,512]{1,0:T(8,128)(2,1)S(1)}, bf16[64,512]{1,0:T(8,128)(2,1)S(1)}, u32[]{:S(2)}, u32[]{:S(2)}) %collective-permute-start.18) | collective-permute-done | bytes 65568 | tf_op jit(solution)/shard_map/ppermute | solution.py:419
  48.8 0.7 %weight_join.1.refs_1_ = f32[64,1024]{1,0:T(8,128)} custom-call(bf16[64,512]{1,0:T(8,128)(2,1)S(1)} %both.1, bf16[64,512]{1,0:T(8,128)(2,1)S(1)} %collective-permute-done.18.got), custom_call_target="tpu_custom_call" | custom-call | bytes 393216 | tf_op jit(solution)/shard_map/weight_join/pallas_call | solution.py:66
  49.5 2.1 %collective-permute-done.16.refs_0_ = bf16[128,128]{1,0:T(8,128)(2,1)S(1)} collective-permute-done((bf16[128,128]{1,0:T(8,128)(2,1)S(1)}, bf16[128,128]{1,0:T(8,128)(2,1)S(1)}, u32[]{:S(2)}, u32[]{:S(2)}) %collective-permute-start.16) | collective-permute-done | bytes 32800 | tf_op jit(solution)/shard_map/ppermute | solution.py:413
  51.7 0.0 collective-permute-done.14.a
  51.7 0.0 collective-permute-done.15.b
  51.7 0.4 final.1
  52.0 0.1 collective-permute-start.19
  52.1 1.4 %collective-permute-done.19.pair = bf16[128,768]{1,0:T(8,128)(2,1)S(1)} collective-permute-done((bf16[128,768]{1,0:T(8,128)(2,1)S(1)}, bf16[128,768]{1,0:T(8,128)(2,1)S(1)}, u32[]{:S(2)}, u32[]{:S(2)}) %collective-permute-start.19) | collective-permute-done | bytes 196640 | tf_op jit(solution)/shard_map/ppermute | solution.py:402
  53.5 0.8 %outputs.1 = (bf16[1,128,512]{2,1,0:T(8,128)(2,1)}, bf16[1,128,512]{2,1,0:T(8,128)(2,1)}, bf16[1,128,512]{2,1,0:T(8,128)(2,1)}) custom-call(bf16[128,768]{1,0:T(8,128)(2,1)S(1)} %get-tuple-element.89.own, bf16[128,768]{1,0:T(8,128)(2,1)S(1)} %collective-permute-done.19.pair), custom_call_target="tpu_custom_call" | custom-call | bytes 786432 | tf_op jit(solution)/shard_map/outputs/pallas_call | solution.py:66
  (7 shorter events, 0.2 us)
Async XLA Ops:
  2.0 1.6 %collective-permute-start = (bf16[128,768]{1,0:T(8,128)(2,1)S(1)}, bf16[128,768]{1,0:T(8,128)(2,1)S(1)}, u32[]{:S(2)}, u32[]{:S(2)}) collective-permute-start(bf16[128,768]{1,0:T(8,128)(2,1)S(1)} %get-tuple-element.51), channel_id=1, source_target_pairs={{0,1},{1,0},{2,3},{3,2},{4,5},{5,4},{6,7},{7,6},{8,9},{9,8},{10,11... | collective-permute-start | bytes 589832 | tf_op jit(solution)/shard_map/ppermute | solution.py:402
  2.5 6.9 %collective-permute-start.6 = (bf16[128,1024]{1,0:T(8,128)(2,1)S(1)}, bf16[128,1024]{1,0:T(8,128)(2,1)S(1)}, u32[]{:S(2)}, u32[]{:S(2)}) collective-permute-start(bf16[128,1024]{1,0:T(8,128)(2,1)S(1)} %get-tuple-element.57.og), channel_id=1, source_target_pairs={{0,1},{1,0},{2,3},{3,2},{4,5},{5,4},{6,7},{7,6},{8,9},{9,8},{10,11... | collective-permute-start | bytes 786440 | tf_op jit(solution)/shard_map/ppermute | solution.py:402
  3.8 6.0 %collective-permute-start.1 = (bf16[128,512]{1,0:T(8,128)(2,1)S(1)}, bf16[128,512]{1,0:T(8,128)(2,1)S(1)}, u32[]{:S(2)}, u32[]{:S(2)}) collective-permute-start(bf16[128,512]{1,0:T(8,128)(2,1)S(1)} %get-tuple-element.52), channel_id=1, source_target_pairs={{0,2},{1,7},{2,0},{3,5},{4,6},{5,3},{6,4},{7,1},{8,10},{9,15},{10,... | collective-permute-start | bytes 393224 | tf_op jit(solution)/shard_map/ppermute | solution.py:413
  6.8 9.5 %collective-permute-start.2 = (bf16[128,512]{1,0:T(8,128)(2,1)S(1)}, bf16[128,512]{1,0:T(8,128)(2,1)S(1)}, u32[]{:S(2)}, u32[]{:S(2)}) collective-permute-start(bf16[128,512]{1,0:T(8,128)(2,1)S(1)} %get-tuple-element.53), channel_id=1, source_target_pairs={{0,6},{1,3},{2,4},{3,1},{4,2},{5,7},{6,0},{7,5},{8,14},{9,11},{10,... | collective-permute-start | bytes 393224 | tf_op jit(solution)/shard_map/ppermute | solution.py:413
  9.3 8.2 %collective-permute-start.3 = (bf16[128,256]{1,0:T(8,128)(2,1)S(1)}, bf16[128,256]{1,0:T(8,128)(2,1)S(1)}, u32[]{:S(2)}, u32[]{:S(2)}) collective-permute-start(bf16[128,256]{1,0:T(8,128)(2,1)S(1)} %get-tuple-element.54), channel_id=1, source_target_pairs={{0,4},{1,5},{2,6},{3,7},{4,0},{5,1},{6,2},{7,3},{8,12},{9,13},{10,... | collective-permute-start | bytes 196616 | tf_op jit(solution)/shard_map/ppermute | solution.py:413
  18.2 6.4 %collective-permute-start.7 = (bf16[256,512]{1,0:T(8,128)(2,1)S(1)}, bf16[256,512]{1,0:T(8,128)(2,1)S(1)}, u32[]{:S(2)}, u32[]{:S(2)}) collective-permute-start(bf16[256,512]{1,0:T(8,128)(2,1)S(1)} %get-tuple-element.64), channel_id=1, source_target_pairs={{0,8},{1,17},{8,0},{9,25},{16,24},{17,1},{24,16},{25,9},{2,10},{3,... | collective-permute-start | bytes 786440 | tf_op jit(solution)/shard_map/ppermute | solution.py:419
  19.8 1.3 %collective-permute-start.4 = (bf16[2,64,256]{2,1,0:T(8,128)(2,1)S(1)}, bf16[2,64,256]{2,1,0:T(8,128)(2,1)S(1)}, u32[]{:S(2)}, u32[]{:S(2)}) collective-permute-start(bf16[2,64,256]{2,1,0:T(8,128)(2,1)S(1)} %get-tuple-element.56), channel_id=1, source_target_pairs={{0,1},{1,0},{2,3},{3,2},{4,5},{5,4},{6,7},{7,6},{8,9},{9,8},{10,11... | collective-permute-start | bytes 196616 | tf_op jit(solution)/shard_map/ppermute | solution.py:402
  21.2 6.0 %collective-permute-start.5 = (bf16[256,256]{1,0:T(8,128)(2,1)S(1)}, bf16[256,256]{1,0:T(8,128)(2,1)S(1)}, u32[]{:S(2)}, u32[]{:S(2)}) collective-permute-start(bf16[256,256]{1,0:T(8,128)(2,1)S(1)} %w_rows.1.first), channel_id=1, source_target_pairs={{0,8},{1,17},{8,0},{9,25},{16,24},{17,1},{24,16},{25,9},{2,10},{3,... | collective-permute-start | bytes 393224 | tf_op jit(solution)/shard_map/ppermute | solution.py:419
  24.7 5.0 %collective-permute-start.9 = (bf16[256,256]{1,0:T(8,128)(2,1)S(1)}, bf16[256,256]{1,0:T(8,128)(2,1)S(1)}, u32[]{:S(2)}, u32[]{:S(2)}) collective-permute-start(bf16[256,256]{1,0:T(8,128)(2,1)S(1)} %get-tuple-element.65.refs_0_), channel_id=1, source_target_pairs={{0,16},{1,9},{8,24},{9,1},{16,0},{17,25},{24,8},{25,17},{2,18},{3,... | collective-permute-start | bytes 393224 | tf_op jit(solution)/shard_map/ppermute | solution.py:419
  27.1 8.4 %collective-permute-start.8 = (bf16[256,512]{1,0:T(8,128)(2,1)S(1)}, bf16[256,512]{1,0:T(8,128)(2,1)S(1)}, u32[]{:S(2)}, u32[]{:S(2)}) collective-permute-start(bf16[256,512]{1,0:T(8,128)(2,1)S(1)} %w_half.1.refs_0_), channel_id=1, source_target_pairs={{0,16},{1,9},{8,24},{9,1},{16,0},{17,25},{24,8},{25,17},{2,18},{3,... | collective-permute-start | bytes 786440 | tf_op jit(solution)/shard_map/ppermute | solution.py:419
  29.8 1.4 %collective-permute-start.10 = (f32[128,256]{1,0:T(8,128)S(1)}, f32[128,256]{1,0:T(8,128)S(1)}, u32[]{:S(2)}, u32[]{:S(2)}) collective-permute-start(f32[128,256]{1,0:T(8,128)S(1)} %get-tuple-element.68), channel_id=1, source_target_pairs={{0,1},{1,0},{2,3},{3,2},{4,5},{5,4},{6,7},{7,6},{8,9},{9,8},{10,11... | collective-permute-start | bytes 393224 | tf_op jit(solution)/shard_map/ppermute | solution.py:402
  31.3 5.8 %collective-permute-start.11 = (bf16[64,256]{1,0:T(8,128)(2,1)S(1)}, bf16[64,256]{1,0:T(8,128)(2,1)S(1)}, u32[]{:S(2)}, u32[]{:S(2)}) collective-permute-start(bf16[64,256]{1,0:T(8,128)(2,1)S(1)} %get-tuple-element.83), channel_id=1, source_target_pairs={{0,2},{1,7},{2,0},{3,5},{4,6},{5,3},{6,4},{7,1},{8,10},{9,15},{10,... | collective-permute-start | bytes 98312 | tf_op jit(solution)/shard_map/ppermute | solution.py:413
  32.2 5.7 %collective-permute-start.12 = (bf16[64,256]{1,0:T(8,128)(2,1)S(1)}, bf16[64,256]{1,0:T(8,128)(2,1)S(1)}, u32[]{:S(2)}, u32[]{:S(2)}) collective-permute-start(bf16[64,256]{1,0:T(8,128)(2,1)S(1)} %get-tuple-element.84), channel_id=1, source_target_pairs={{0,6},{1,3},{2,4},{3,1},{4,2},{5,7},{6,0},{7,5},{8,14},{9,11},{10,... | collective-permute-start | bytes 98312 | tf_op jit(solution)/shard_map/ppermute | solution.py:413
  35.5 4.8 %collective-permute-start.13 = (bf16[64,256]{1,0:T(8,128)(2,1)S(1)}, bf16[64,256]{1,0:T(8,128)(2,1)S(1)}, u32[]{:S(2)}, u32[]{:S(2)}) collective-permute-start(bf16[64,256]{1,0:T(8,128)(2,1)S(1)} %get-tuple-element.85), channel_id=1, source_target_pairs={{0,4},{1,5},{2,6},{3,7},{4,0},{5,1},{6,2},{7,3},{8,12},{9,13},{10,... | collective-permute-start | bytes 98312 | tf_op jit(solution)/shard_map/ppermute | solution.py:413
  40.3 4.0 %collective-permute-start.17 = (bf16[64,256]{1,0:T(8,128)(2,1)S(1)}, bf16[64,256]{1,0:T(8,128)(2,1)S(1)}, u32[]{:S(2)}, u32[]{:S(2)}) collective-permute-start(bf16[64,256]{1,0:T(8,128)(2,1)S(1)} %weight_sum.1.refs_1_.first), channel_id=1, source_target_pairs={{0,8},{1,17},{8,0},{9,25},{16,24},{17,1},{24,16},{25,9},{2,10},{3,... | collective-permute-start | bytes 98312 | tf_op jit(solution)/shard_map/ppermute | solution.py:419
  42.5 9.2 %collective-permute-start.14 = (bf16[128,384]{1,0:T(8,128)(2,1)S(1)}, bf16[128,384]{1,0:T(8,128)(2,1)S(1)}, u32[]{:S(2)}, u32[]{:S(2)}) collective-permute-start(bf16[128,384]{1,0:T(8,128)(2,1)S(1)} %get-tuple-element.86), channel_id=1, source_target_pairs={{0,2},{1,7},{2,0},{3,5},{4,6},{5,3},{6,4},{7,1},{8,10},{9,15},{10,... | collective-permute-start | bytes 294920 | tf_op jit(solution)/shard_map/ppermute | solution.py:413
  42.9 8.8 %collective-permute-start.15 = (bf16[128,384]{1,0:T(8,128)(2,1)S(1)}, bf16[128,384]{1,0:T(8,128)(2,1)S(1)}, u32[]{:S(2)}, u32[]{:S(2)}) collective-permute-start(bf16[128,384]{1,0:T(8,128)(2,1)S(1)} %get-tuple-element.87), channel_id=1, source_target_pairs={{0,6},{1,3},{2,4},{3,1},{4,2},{5,7},{6,0},{7,5},{8,14},{9,11},{10,... | collective-permute-start | bytes 294920 | tf_op jit(solution)/shard_map/ppermute | solution.py:413
  44.4 4.5 %collective-permute-start.18 = (bf16[64,512]{1,0:T(8,128)(2,1)S(1)}, bf16[64,512]{1,0:T(8,128)(2,1)S(1)}, u32[]{:S(2)}, u32[]{:S(2)}) collective-permute-start(bf16[64,512]{1,0:T(8,128)(2,1)S(1)} %both.1), channel_id=1, source_target_pairs={{0,16},{1,9},{8,24},{9,1},{16,0},{17,25},{24,8},{25,17},{2,18},{3,... | collective-permute-start | bytes 196616 | tf_op jit(solution)/shard_map/ppermute | solution.py:419
  46.6 5.1 %collective-permute-start.16 = (bf16[128,128]{1,0:T(8,128)(2,1)S(1)}, bf16[128,128]{1,0:T(8,128)(2,1)S(1)}, u32[]{:S(2)}, u32[]{:S(2)}) collective-permute-start(bf16[128,128]{1,0:T(8,128)(2,1)S(1)} %get-tuple-element.88), channel_id=1, source_target_pairs={{0,4},{1,5},{2,6},{3,7},{4,0},{5,1},{6,2},{7,3},{8,12},{9,13},{10,... | collective-permute-start | bytes 98312 | tf_op jit(solution)/shard_map/ppermute | solution.py:413
  52.0 1.5 %collective-permute-start.19 = (bf16[128,768]{1,0:T(8,128)(2,1)S(1)}, bf16[128,768]{1,0:T(8,128)(2,1)S(1)}, u32[]{:S(2)}, u32[]{:S(2)}) collective-permute-start(bf16[128,768]{1,0:T(8,128)(2,1)S(1)} %get-tuple-element.90), channel_id=1, source_target_pairs={{0,1},{1,0},{2,3},{3,2},{4,5},{5,4},{6,7},{7,6},{8,9},{9,8},{10,11... | collective-permute-start | bytes 589832 | tf_op jit(solution)/shard_map/ppermute | solution.py:402

commit v6 on v5

--- a/solution.py
+++ b/solution.py
@@ -94,9 +94,9 @@
     )
 
 
-def pack_kernel(q, k, v, og, w, gain, mine_out, other_out, og_out, w_out, gain_out, sems):
+def pack_kernel(q, k, v, og, w, gain, mine_out, og_out, w_out, gain_out, sems):
     core, _, dp = places()
-    mine, other = core * DH, (1 - core) * DH
+    mine = core * DH
     copies = []
 
     def fetch(source, target):
@@ -107,7 +107,6 @@
     for index, array in enumerate((q, k, v)):
         for group in range(2):
             cols = slice((3 * group + index) * DH, (3 * group + index + 1) * DH)
-            fetch(array.at[0, :, at(SOFT * group + other)], other_out.at[:, cols])
             fetch(array.at[0, :, at(SOFT * group + mine)], mine_out.at[:, cols])
     width = w_out.shape[1]
     fetch(w.at[:, at(dp * width, width)], w_out)
@@ -117,48 +116,49 @@
         copy.wait()
 
 
-def state_kernel(direct, mine, pair, *refs):
-    core, _, _ = places()
+def state_kernel(direct, mine, q_pair, k_pair, v_pair, state, pair, to_a, to_b, *to_c):
+    core, _, _ = places()
+    own = core * DH
+    for index, source in enumerate((q_pair, k_pair, v_pair)):
+        for group in range(2):
+            first = (3 * group + index) * DH
+            pair[:, first : first + DH] = source[0, :, at(SOFT * group + own)]
     total = mm2(unit_plus(mine[:, KL].astype(F32)), mine[:, VL], TN) + mm2(
         unit_plus(pair[:, KL].astype(F32)), pair[:, VL], TN
     )
-    if direct:
-        w, state, to_a, to_b, to_c = refs
-    else:
-        state, to_a, to_b = refs
     state[...] = total
     way = links(direct)
     for out, block in ((to_a, way["block_a"]), (to_b, way["block_b"])):
         here = block == core
         out[:, :DH] = jnp.where(here, mine[:, KS], pair[:, KS])
         out[:, DH : 2 * DH] = jnp.where(here, mine[:, VS], pair[:, VS])
-    if direct:
-        rows = w.shape[0]
-        for out, first in ((to_a, 2 * DH), (to_b, 2 * DH), (to_c, 0)):
-            out[:, first : first + DH] = total.astype(BF)
-            out[:rows, first + DH :] = w[:, :DH]
-            out[rows:, first + DH :] = w[:, DH:]
-
-
-def relay_kernel(w, a, b, c, keep, send, heads):
+        if direct:
+            out[:, 2 * DH :] = total.astype(BF)
+    if direct:
+        to_c[0][...] = total.astype(BF)
+
+
+def w_head_kernel(own, pair, out):
+    core, _, dp = places()
+    rows, width = own.shape
+    out[at(core * rows, rows), :] = own[...]
+    out[at((1 - core) * rows, rows), :] = pair[:, at(dp * width, width)]
+
+
+def w_rows_kernel(own, a, b, c, _, out):
     core, z, _ = places()
     way = links(True)
-    rows = w.shape[0]
-    heads[z] = w[...]
-    for source, first, step in ((a, 3 * DH, way["first"]), (b, 3 * DH, way["second"]), (c, DH, 2)):
-        heads[z ^ step, :, :DH] = source[:rows, first:]
-        heads[z ^ step, :, DH:] = source[rows:, first:]
-    for group in range(2):
-        keep[group] = heads[2 * group + core]
-        send[group] = heads[2 * group + 1 - core]
-
-
-def w_rows_kernel(keep, got, out):
-    core, _, _ = places()
-    half = keep.shape[1]
-    for group in range(2):
-        out[at(group * DH + core * half, half), :] = keep[group]
-        out[at(group * DH + (1 - core) * half, half), :] = got[group]
+    group = lax.div(z, 2)
+
+    @pl.when(lax.rem(z, 2) == core)
+    def _():
+        out[at(group * DH), :] = own[...]
+        out[at((1 - group) * DH), :] = c[...]
+
+    @pl.when(lax.rem(z, 2) != core)
+    def _():
+        out[at(lax.div(z ^ way["first"], 2) * DH), :] = a[...]
+        out[at(lax.div(z ^ way["second"], 2) * DH), :] = b[...]
 
 
 def join_kernel(first, second, *refs):
@@ -222,8 +222,7 @@
     total = state[...]
     if direct:
         a, b, c, soft_send, u_out, total_out, keep, out = refs
-        total = total + a[:, 2 * DH : 3 * DH].astype(F32) + b[:, 2 * DH : 3 * DH].astype(F32)
-        total = total + c[:, :DH].astype(F32)
+        total = total + a[:, 2 * DH :].astype(F32) + b[:, 2 * DH :].astype(F32) + c[...].astype(F32)
     else:
         u_out, total_out, keep = refs
     total_out[...] = total
@@ -237,7 +236,7 @@
         out[:DH, :] = soft_send[...]
 
 
-def fold_kernel(keep_soft, keep_lin, got, keep, send):
+def fold_kernel(keep_soft, keep_lin, got, _a, _b, _c, keep, send):
     width = keep.shape[1]
     for rows, source in ((slice(0, DH), keep_soft), (slice(DH, 2 * DH), keep_lin)):
         keep[rows, :] = source[:, :width] + got[rows, :width].astype(F32)
@@ -290,7 +289,7 @@
 def backward_kernel(direct, *refs):
     if direct:
         sent, got = refs[:2]
-        refs = refs[3:]
+        refs = refs[2:]
     else:
         weights = refs[0]
         refs = refs[1:]
@@ -314,7 +313,7 @@
     way = links(direct)
     span = dk_soft.shape[0]
     if direct:
-        dstate, _, to_a, to_b, to_c = refs
+        dstate, _, _, _, to_a, to_b, to_c = refs
         to_c[...] = dstate[...].astype(BF)
     else:
         to_a, to_b = refs
@@ -412,6 +411,13 @@
                 pairs.append((2 * z + c, 2 * there + c))
         return lax.ppermute(value, axes, pairs)
 
+    def from_matching(value, which):
+        pairs = []
+        for z in range(n_z):
+            c = z % 2
+            pairs.append((2 * z + c, 2 * (z ^ (1 + 2 * c, 3 - 2 * c, 2)[which]) + c))
+        return lax.ppermute(value, axes, pairs)
+
     def over_dp(value, which):
         pairs = [
             (2 * d + c, 2 * (d ^ (1 + c, 2 - c)[which]) + c) for d in range(n_dp) for c in range(2)
@@ -423,36 +429,29 @@
     def hbm(value):
         return pltpu.with_memory_space_constraint(value, pltpu.HBM)
 
-    mine, other, og, w_part, gain = call(
+    q_pair, k_pair, v_pair = over_core(queries), over_core(key_rows), over_core(value_rows)
+    og_recv = over_core(out_grad[0])
+    w_pair = over_core(out_weight)
+    mine, og, w_part, gain = call(
         pack_kernel, "pack",
         [
-            like((rows, 6 * DH), BF), like((rows, 6 * DH), BF), like((rows, model), BF),
+            like((rows, 6 * DH), BF), like((rows, model), BF),
             like((out_weight.shape[0], width), BF), like((1, DH), F32),
         ],
         [hbm(x) for x in (queries, key_rows, value_rows, out_grad, out_weight, norm_gain)],
-        scratch=[pltpu.SemaphoreType.DMA((16,))],
+        scratch=[pltpu.SemaphoreType.DMA((9,))],
         spaces=[pl.BlockSpec(memory_space=pltpu.HBM)] * 6,
     )
-    pair = over_core(other)
-    og_recv = over_core(og)
-    wide = 4 * DH if direct else 2 * DH
-    state, to_a, to_b, *rest = call(
+    wide = 3 * DH if direct else 2 * DH
+    state, pair, to_a, to_b, *rest = call(
         functools.partial(state_kernel, direct), "state",
-        [like((DH, DH), F32), like((rows, wide), BF), like((rows, wide), BF)]
-        + [like((rows, 2 * DH), BF)] * direct,
-        [mine, pair] + [w_part] * direct,
+        [like((DH, DH), F32), like((rows, 6 * DH), BF), like((rows, wide), BF), like((rows, wide), BF)]
+        + [like((DH, DH), BF)] * direct,
+        [mine, q_pair, k_pair, v_pair],
         flops=4 * 2 * rows * DH * DH,
     )
     if direct:
         a, b, c = over_z(to_a, 0), over_z(to_b, 1), [over_z(rest[0], 2)]
-        w_keep, w_send = call(
-            relay_kernel, "relay", [like((2, half, width), BF)] * 2, [w_part, a, b] + c,
-            scratch=[pltpu.VMEM((HEADS, half, width), BF)],
-        )
-        w_own = call(
-            w_rows_kernel, "w_rows", [like((2 * DH, width), BF)], [w_keep, over_core(w_send)]
-        )[0]
-        w_got = over_dp(w_own, 0)
     else:
         a, b, c = over_z(to_a, 0), over_z(to_b, 1), []
         state = lax.psum(state, "z")
@@ -481,14 +480,17 @@
     )
     if direct:
         got = over_dp(sent[0], 0)
+        w_head = call(w_head_kernel, "w_head", [like((DH, width), BF)], [w_part, w_pair])[0]
+        w_far = [from_matching(w_head, which) for which in range(3)]
         keep, sent = call(
             fold_kernel, "fold", [like((2 * DH, width), F32), like((2 * DH, width), BF)],
-            [keep_soft, keep_lin, got],
+            [keep_soft, keep_lin, got] + w_far,
         )
-        w_half = call(
-            join_kernel, "w_half", [like((2 * DH, 2 * width), BF)], [w_own, w_got, sent]
+        w_own = call(
+            w_rows_kernel, "w_rows", [like((2 * DH, width), BF)],
+            [w_head] + w_far + [sent],
         )[0]
-        weights = [w_half, over_dp(w_half, 1)]
+        w_got = over_dp(w_own, 0)
         got = over_dp(sent, 1)
         row_own, row_send = call(
             rows_kernel, "rows", [like((2 * half, width), F32)] * 2, [keep, got],
@@ -499,6 +501,10 @@
             chunk_kernel, "chunk", [like((half, width), BF)] * 3 + [like((half, width), F32)],
             [row_own, row_recv], scratch=[pltpu.VMEM((HEADS, half, width), F32)],
         )
+        w_half = call(
+            join_kernel, "w_half", [like((2 * DH, 2 * width), BF)], [w_own, w_got, chunk]
+        )[0]
+        weights = [w_half, over_dp(w_half, 1)]
         chunks = [over_z(value, which) for which, value in enumerate(to_chips)]
         summed = call(
             functools.partial(weight_sum_kernel, scale), "weight_sum", [like((half, width), BF)],
@@ -510,8 +516,6 @@
         weight_grad = call(
             weight_join_kernel, "weight_join", [like((half, model), F32)], [both, got]
         )[0]
-    if direct:
-        weights.append(chunk)
     dq_lin, dq_lin_pair, dstate, dq_soft, dk_soft, dv_soft = call(
         functools.partial(backward_kernel, direct), "backward",
         [
@@ -523,11 +527,10 @@
         + [pltpu.VMEM((2 * DH, model), BF)] * direct,
         flops=5 * wg_flops,
     )
-    wide = 3 * DH if direct else 2 * DH
     to_a, to_b, *to_c = call(
         functools.partial(halo_kernel, direct), "halo",
         [like((rows, wide), BF), like((rows, wide), BF)] + [like((DH, DH), BF)] * direct,
-        [dk_soft, dv_soft] + ([dstate, summed] if direct else []),
+        [dk_soft, dv_soft] + ([dstate] + chunks if direct else []),
     )
     a, b = over_z(to_a, 0, True), over_z(to_b, 1, True)
     c = [over_z(value, 2) for value in to_c]
@@ -543,9 +546,8 @@
         functools.partial(final_kernel, direct), "final",
         [like((rows, 6 * DH), BF), like((rows, 6 * DH), BF)],
         [dstate, mine, pair, dq_soft, dk_soft, dv_soft, dq_lin, dq_lin_pair, a, b] + c
-        + ([hbm(weight_grad)] if direct else []),
+        + ([both] if direct else []),
         scratch=[pltpu.VMEM((2 * rows, DH), F32)] * 2,
-        spaces=[vmem] * 11 + [pl.BlockSpec(memory_space=pltpu.HBM)] if direct else None,
         flops=wg_flops // 4,
     )
     from_pair = over_core(to_pair)

time: 54.5 us -> 65.3 us (1.20)
  waiting for transfers between devices: 22.5 us -> 28.4 us
  starting transfers between devices: 23.9 us -> 28.8 us
    ppermute x6, waiting for transfers between devices: 5.23 us -> 14.4 us  [over_dp(): return lax.ppermute(value, ('dp', 'core'), pairs)]
    ppermute x0 -> x3, starting transfers between devices: none -> 7.91 us  [from_matching(): return lax.ppermute(value, axes, pairs)]
    ppermute x9, waiting for transfers between devices: 12.2 us -> 7.11 us  [over_z(): return lax.ppermute(value, axes, pairs)]
    ppermute x0 -> x3, waiting for transfers between devices: none -> 4.56 us  [from_matching(): return lax.ppermute(value, axes, pairs)]
    ppermute x6, starting transfers between devices: 10.3 us -> 7.17 us  [over_dp(): return lax.ppermute(value, ('dp', 'core'), pairs)]
    ppermute x5 -> x7, waiting for transfers between devices: 5 us -> 2.33 us  [over_core(): return lax.ppermute(value, 'core', pair_perm)]
  transfers between devices with their start and end apart: 20 -> 25, of which waited for: 14 -> 12; matrix products, arithmetic and copies ran while one was open for 0% -> 0% of each run, Pallas kernels for 7% -> 8%
where the time goes in v6:
time: 65.3 us; the launch traced here: 65.1 us
  starting transfers between devices  28.8 us (44%)
  waiting for transfers between devices  28.4 us (43%)
  Pallas kernels  7.03 us (11%)
  between operations  0.84 us (1%)
    ppermute x6, waiting for transfers between devices, over_dp(): return lax.ppermute(value, ('dp', 'core'), pairs)  14.4 us
    ppermute x9, starting transfers between devices, over_z(): return lax.ppermute(value, axes, pairs)  12.5 us
    ppermute x3, starting transfers between devices, from_matching(): return lax.ppermute(value, axes, pairs)  7.91 us
    ppermute x6, starting transfers between devices, over_dp(): return lax.ppermute(value, ('dp', 'core'), pairs)  7.17 us
    ppermute x9, waiting for transfers between devices, over_z(): return lax.ppermute(value, axes, pairs)  7.11 us
    pallas_call x17, Pallas kernels, call(): pl.pallas_call(kernel, name=name, out_shape=list(outs), in_specs=spaces o...  7.03 us
    ppermute x3, waiting for transfers between devices, from_matching(): return lax.ppermute(value, axes, pairs)  4.56 us
    ppermute x7, waiting for transfers between devices, over_core(): return lax.ppermute(value, 'core', pair_perm)  2.33 us
  transfers between devices with their start and end apart: 25, of which 12 were waited for; matrix products, arithmetic and copies ran while one was open for 0% of the time, Pallas kernels for 8%

profile of v6, /device:TPU:0, one launch (start us, length us, event | category | flops | bytes accessed | tf_op | source)
XLA Modules:
  0.0 65.1 jit_solution(1261319905132803791)
XLA Ops:
  0.6 0.5 collective-permute-start.7
  1.1 0.1 collective-permute-start.4
  1.2 0.4 collective-permute-start.5
  1.7 0.1 collective-permute-start.6
  1.7 1.2 %pack.1 = (bf16[128,768]{1,0:T(8,128)(2,1)S(1)}, bf16[128,1024]{1,0:T(8,128)(2,1)S(1)}, bf16[64,256]{1,0:T(8,128)(2,1)S(1)}, f32[1,128]{1,0:T(1,128)S(1)}) custom-call(bf16[1,128,512]{2,1,0:T(8,128)(2,1)} %q.1, bf16[1,128,512]{2,1,0:T(8,128)(2,1)} %k.1, bf16[1,128,512]{2,1,0:T(8,128)(2,1)} %v.1, bf16[1,128,1024]{2,1,0:T(8,128)(2,1)} %og.1, ...), custom_call_target="tpu_custom_call" | custom-call | bytes 1279488 | tf_op jit(solution)/shard_map/pack/pallas_call | solution.py:66
  2.9 0.0 collective-permute-done.4.q_pair
  2.9 0.0 collective-permute-done.5.k_pair
  2.9 0.3 collective-permute-done.6.v_pair
  3.2 0.3 state.1
  3.5 2.9 %collective-permute-start.8 = (bf16[128,384]{1,0:T(8,128)(2,1)S(1)}, bf16[128,384]{1,0:T(8,128)(2,1)S(1)}, u32[]{:S(2)}, u32[]{:S(2)}) collective-permute-start(bf16[128,384]{1,0:T(8,128)(2,1)S(1)} %get-tuple-element.51), channel_id=1, source_target_pairs={{0,2},{1,7},{2,0},{3,5},{4,6},{5,3},{6,4},{7,1},{8,10},{9,15},{10,... | collective-permute-start | bytes 294920 | tf_op jit(solution)/shard_map/ppermute | solution.py:412
  6.4 2.5 %collective-permute-start.9 = (bf16[128,384]{1,0:T(8,128)(2,1)S(1)}, bf16[128,384]{1,0:T(8,128)(2,1)S(1)}, u32[]{:S(2)}, u32[]{:S(2)}) collective-permute-start(bf16[128,384]{1,0:T(8,128)(2,1)S(1)} %get-tuple-element.52), channel_id=1, source_target_pairs={{0,6},{1,3},{2,4},{3,1},{4,2},{5,7},{6,0},{7,5},{8,14},{9,11},{10,... | collective-permute-start | bytes 294920 | tf_op jit(solution)/shard_map/ppermute | solution.py:412
  8.9 0.1 collective-permute-start.10
  9.0 0.0 collective-permute-done.8.a.refs_0_
  9.0 5.2 %collective-permute-done.9.b.refs_1_ = bf16[128,384]{1,0:T(8,128)(2,1)S(1)} collective-permute-done((bf16[128,384]{1,0:T(8,128)(2,1)S(1)}, bf16[128,384]{1,0:T(8,128)(2,1)S(1)}, u32[]{:S(2)}, u32[]{:S(2)}) %collective-permute-start.9) | collective-permute-done | bytes 98336 | tf_op jit(solution)/shard_map/ppermute | solution.py:412
  14.2 0.0 collective-permute-done.7.og_recv
  14.2 1.2 %soft_forward.1 = (bf16[256,128]{1,0:T(8,128)(2,1)S(1)}, bf16[512,128]{1,0:T(8,128)(2,1)S(1)}, bf16[512,128]{1,0:T(8,128)(2,1)S(1)}, bf16[256,1024]{1,0:T(8,128)...) custom-call(bf16[128,768]{1,0:T(8,128)(2,1)S(1)} %get-tuple-element., ...), custom_call_target="tpu_custom_call" | custom-call | flops 67108864 | bytes 2883584 | tf_op jit(solution)/shard_map/soft_forward/pallas_call | solution.py:66
  15.4 0.0 collective-permute-done.10.refs_2_
  15.4 0.0 copy-start
  15.4 0.7 %lin_forward.1 = (f32[256,128]{1,0:T(8,128)S(1)}, f32[128,128]{1,0:T(8,128)S(1)}, f32[128,512]{1,0:T(8,128)S(1)}, bf16[256,512]{1,0:T(8,128)(2,1)S(1)}) custom-call(f32[128,128]{1,0:T(8,128)S(1)} %get-tuple-element.54.state, bf16[128,768]{1,0:T(8,128)(2,1)S(1)} %get-tuple-element.48.mine.refs_5_, bf16[128,768]{1,0:T(8,128)(2,1)S(1)} %get-tuple-element.49.pair.refs_6_, ...), custom_call_target="tpu_custom_call" | custom-call | flops 67108864 | bytes 2064896 | tf_op jit(solution)/shard_map/lin_forward/pallas_call | solution.py:66
  16.1 1.6 %collective-permute-start.11 = (bf16[256,512]{1,0:T(8,128)(2,1)S(1)}, bf16[256,512]{1,0:T(8,128)(2,1)S(1)}, u32[]{:S(2)}, u32[]{:S(2)}) collective-permute-start(bf16[256,512]{1,0:T(8,128)(2,1)S(1)} %get-tuple-element.60), channel_id=1, source_target_pairs={{0,8},{1,17},{8,0},{9,25},{16,24},{17,1},{24,16},{25,9},{2,10},{3,... | collective-permute-start | bytes 786440 | tf_op jit(solution)/shard_map/ppermute | solution.py:425
  17.7 0.0 copy-done
  17.7 0.0 collective-permute-start
  17.7 1.3 %collective-permute-done.pair = bf16[64,1024]{1,0:T(8,128)(2,1)S(1)} collective-permute-done((bf16[64,1024]{1,0:T(8,128)(2,1)S(1)}, bf16[64,1024]{1,0:T(8,128)(2,1)S(1)}, u32[]{:S(2)}, u32[]{:S(2)}) %collective-permute-start) | collective-permute-done | bytes 131104 | tf_op jit(solution)/shard_map/ppermute | solution.py:401
  19.0 2.2 %collective-permute-start.1 = (bf16[128,256]{1,0:T(8,128)(2,1)S(1)}, bf16[128,256]{1,0:T(8,128)(2,1)S(1)}, u32[]{:S(2)}, u32[]{:S(2)}) collective-permute-start(bf16[128,256]{1,0:T(8,128)(2,1)S(1)} %w_head.1.own), channel_id=1, source_target_pairs={{0,2},{3,5},{4,6},{7,1},{8,10},{11,13},{12,14},{15,9},{16,18},{19,... | collective-permute-start | bytes 196616 | tf_op jit(solution)/shard_map/ppermute | solution.py:419
  21.3 3.2 %collective-permute-start.2 = (bf16[128,256]{1,0:T(8,128)(2,1)S(1)}, bf16[128,256]{1,0:T(8,128)(2,1)S(1)}, u32[]{:S(2)}, u32[]{:S(2)}) collective-permute-start(bf16[128,256]{1,0:T(8,128)(2,1)S(1)} %w_head.1.own), channel_id=1, source_target_pairs={{0,6},{3,1},{4,2},{7,5},{8,14},{11,9},{12,10},{15,13},{16,22},{19,... | collective-permute-start | bytes 196616 | tf_op jit(solution)/shard_map/ppermute | solution.py:419
  24.5 2.5 %collective-permute-start.3 = (bf16[128,256]{1,0:T(8,128)(2,1)S(1)}, bf16[128,256]{1,0:T(8,128)(2,1)S(1)}, u32[]{:S(2)}, u32[]{:S(2)}) collective-permute-start(bf16[128,256]{1,0:T(8,128)(2,1)S(1)} %w_head.1.own), channel_id=1, source_target_pairs={{0,4},{3,7},{4,0},{7,3},{8,12},{11,15},{12,8},{15,11},{16,20},{19,... | collective-permute-start | bytes 196616 | tf_op jit(solution)/shard_map/ppermute | solution.py:419
  27.0 0.0 collective-permute-done.1._a.a
  27.0 0.0 collective-permute-done.2._b.b
  27.0 4.6 %collective-permute-done.3._c.c = bf16[128,256]{1,0:T(8,128)(2,1)S(1)} collective-permute-done((bf16[128,256]{1,0:T(8,128)(2,1)S(1)}, bf16[128,256]{1,0:T(8,128)(2,1)S(1)}, u32[]{:S(2)}, u32[]{:S(2)}) %collective-permute-start.3) | collective-permute-done | bytes 65568 | tf_op jit(solution)/shard_map/ppermute | solution.py:419
  31.5 0.0 collective-permute-done.11.got
  31.5 0.1 fold.1
  31.6 1.6 %collective-permute-start.13 = (bf16[256,256]{1,0:T(8,128)(2,1)S(1)}, bf16[256,256]{1,0:T(8,128)(2,1)S(1)}, u32[]{:S(2)}, u32[]{:S(2)}) collective-permute-start(bf16[256,256]{1,0:T(8,128)(2,1)S(1)} %get-tuple-element.61._), channel_id=1, source_target_pairs={{0,16},{1,9},{8,24},{9,1},{16,0},{17,25},{24,8},{25,17},{2,18},{3,... | collective-permute-start | bytes 393224 | tf_op jit(solution)/shard_map/ppermute | solution.py:425
  33.2 3.4 %collective-permute-done.13.got = bf16[256,256]{1,0:T(8,128)(2,1)S(1)} collective-permute-done((bf16[256,256]{1,0:T(8,128)(2,1)S(1)}, bf16[256,256]{1,0:T(8,128)(2,1)S(1)}, u32[]{:S(2)}, u32[]{:S(2)}) %collective-permute-start.13) | collective-permute-done | bytes 131104 | tf_op jit(solution)/shard_map/ppermute | solution.py:425
  36.6 0.1 rows.1
  36.7 0.1 collective-permute-start.14
  36.8 0.6 collective-permute-start.12
  37.4 0.7 %collective-permute-done.14.got = f32[128,256]{1,0:T(8,128)S(1)} collective-permute-done((f32[128,256]{1,0:T(8,128)S(1)}, f32[128,256]{1,0:T(8,128)S(1)}, u32[]{:S(2)}, u32[]{:S(2)}) %collective-permute-start.14) | collective-permute-done | bytes 131104 | tf_op jit(solution)/shard_map/ppermute | solution.py:401
  38.1 3.7 %collective-permute-done.12.second = bf16[256,256]{1,0:T(8,128)(2,1)S(1)} collective-permute-done((bf16[256,256]{1,0:T(8,128)(2,1)S(1)}, bf16[256,256]{1,0:T(8,128)(2,1)S(1)}, u32[]{:S(2)}, u32[]{:S(2)}) %collective-permute-start.12) | collective-permute-done | bytes 131104 | tf_op jit(solution)/shard_map/ppermute | solution.py:425
  41.9 1.6 %collective-permute-start.15 = (bf16[256,512]{1,0:T(8,128)(2,1)S(1)}, bf16[256,512]{1,0:T(8,128)(2,1)S(1)}, u32[]{:S(2)}, u32[]{:S(2)}) collective-permute-start(bf16[256,512]{1,0:T(8,128)(2,1)S(1)} %w_half.1.refs_0_), channel_id=1, source_target_pairs={{0,16},{1,9},{8,24},{9,1},{16,0},{17,25},{24,8},{25,17},{2,18},{3,... | collective-permute-start | bytes 786440 | tf_op jit(solution)/shard_map/ppermute | solution.py:425
  43.4 0.0 collective-permute-start.16
  43.4 2.0 %collective-permute-start.17 = (bf16[64,256]{1,0:T(8,128)(2,1)S(1)}, bf16[64,256]{1,0:T(8,128)(2,1)S(1)}, u32[]{:S(2)}, u32[]{:S(2)}) collective-permute-start(bf16[64,256]{1,0:T(8,128)(2,1)S(1)} %get-tuple-element.80), channel_id=1, source_target_pairs={{0,6},{1,3},{2,4},{3,1},{4,2},{5,7},{6,0},{7,5},{8,14},{9,11},{10,... | collective-permute-start | bytes 98312 | tf_op jit(solution)/shard_map/ppermute | solution.py:412
  45.5 1.5 %collective-permute-start.18 = (bf16[64,256]{1,0:T(8,128)(2,1)S(1)}, bf16[64,256]{1,0:T(8,128)(2,1)S(1)}, u32[]{:S(2)}, u32[]{:S(2)}) collective-permute-start(bf16[64,256]{1,0:T(8,128)(2,1)S(1)} %get-tuple-element.81), channel_id=1, source_target_pairs={{0,4},{1,5},{2,6},{3,7},{4,0},{5,1},{6,2},{7,3},{8,12},{9,13},{10,... | collective-permute-start | bytes 98312 | tf_op jit(solution)/shard_map/ppermute | solution.py:412
  46.9 1.4 %collective-permute-done.15.refs_1_ = bf16[256,512]{1,0:T(8,128)(2,1)S(1)} collective-permute-done((bf16[256,512]{1,0:T(8,128)(2,1)S(1)}, bf16[256,512]{1,0:T(8,128)(2,1)S(1)}, u32[]{:S(2)}, u32[]{:S(2)}) %collective-permute-start.15) | collective-permute-done | bytes 262176 | tf_op jit(solution)/shard_map/ppermute | solution.py:425
  48.3 1.5 %backward.1 = (bf16[128,128]{1,0:T(8,128)(2,1)S(1)}, bf16[128,128]{1,0:T(8,128)(2,1)S(1)}, f32[128,128]{1,0:T(8,128)S(1)}, f32[256,128]{1,0:T(8,128)S(1)}, f32[5...) custom-call(bf16[256,512]{1,0:T(8,128)(2,1)S(1)} %w_half.1.refs_0_, bf16[256,512]{1,0:T(8,128)(2,1)S(1)} %collective-permute-done.15.refs_1_, ...), custom_call_target="tpu_custom_call" | custom-call | flops 335544320 | bytes 3277312 | tf_op jit(solution)/shard_map/backward/pallas_call | solution.py:66
  49.8 0.0 collective-permute-done.16.refs_1_.a
  49.8 0.0 collective-permute-done.17.refs_2_.b
  49.9 0.5 collective-permute-done.18.refs_3_.c
  50.4 0.1 collective-permute-start.19
  50.4 2.9 %collective-permute-start.20 = (bf16[128,384]{1,0:T(8,128)(2,1)S(1)}, bf16[128,384]{1,0:T(8,128)(2,1)S(1)}, u32[]{:S(2)}, u32[]{:S(2)}) collective-permute-start(bf16[128,384]{1,0:T(8,128)(2,1)S(1)} %get-tuple-element.83), channel_id=1, source_target_pairs={{0,6},{1,3},{2,4},{3,1},{4,2},{5,7},{6,0},{7,5},{8,14},{9,11},{10,... | collective-permute-start | bytes 294920 | tf_op jit(solution)/shard_map/ppermute | solution.py:412
  53.3 0.6 collective-permute-start.22
  53.9 0.6 collective-permute-start.21
  54.5 2.8 %collective-permute-done.22.second = bf16[64,256]{1,0:T(8,128)(2,1)S(1)} collective-permute-done((bf16[64,256]{1,0:T(8,128)(2,1)S(1)}, bf16[64,256]{1,0:T(8,128)(2,1)S(1)}, u32[]{:S(2)}, u32[]{:S(2)}) %collective-permute-start.22) | collective-permute-done | bytes 32800 | tf_op jit(solution)/shard_map/ppermute | solution.py:425
  57.3 1.4 %collective-permute-done.21.refs_0_ = bf16[128,128]{1,0:T(8,128)(2,1)S(1)} collective-permute-done((bf16[128,128]{1,0:T(8,128)(2,1)S(1)}, bf16[128,128]{1,0:T(8,128)(2,1)S(1)}, u32[]{:S(2)}, u32[]{:S(2)}) %collective-permute-start.21) | collective-permute-done | bytes 32800 | tf_op jit(solution)/shard_map/ppermute | solution.py:412
  58.8 0.0 collective-permute-done.19.a
  58.8 0.0 collective-permute-done.20.b
  58.8 0.4 final.1
  59.1 0.1 collective-permute-start.23
  59.2 1.2 %collective-permute-start.24 = (bf16[64,512]{1,0:T(8,128)(2,1)S(1)}, bf16[64,512]{1,0:T(8,128)(2,1)S(1)}, u32[]{:S(2)}, u32[]{:S(2)}) collective-permute-start(bf16[64,512]{1,0:T(8,128)(2,1)S(1)} %both.1.refs_1_), channel_id=1, source_target_pairs={{0,16},{1,9},{8,24},{9,1},{16,0},{17,25},{24,8},{25,17},{2,18},{3,... | collective-permute-start | bytes 196616 | tf_op jit(solution)/shard_map/ppermute | solution.py:425
  60.5 3.1 %collective-permute-done.24.got = bf16[64,512]{1,0:T(8,128)(2,1)S(1)} collective-permute-done((bf16[64,512]{1,0:T(8,128)(2,1)S(1)}, bf16[64,512]{1,0:T(8,128)(2,1)S(1)}, u32[]{:S(2)}, u32[]{:S(2)}) %collective-permute-start.24) | collective-permute-done | bytes 65568 | tf_op jit(solution)/shard_map/ppermute | solution.py:425
  63.5 0.7 %weight_join.1 = f32[64,1024]{1,0:T(8,128)} custom-call(bf16[64,512]{1,0:T(8,128)(2,1)S(1)} %both.1.refs_1_, bf16[64,512]{1,0:T(8,128)(2,1)S(1)} %collective-permute-done.24.got), custom_call_target="tpu_custom_call" | custom-call | bytes 393216 | tf_op jit(solution)/shard_map/weight_join/pallas_call | solution.py:66
  64.3 0.0 collective-permute-done.23.pair
  64.3 0.8 %outputs.1 = (bf16[1,128,512]{2,1,0:T(8,128)(2,1)}, bf16[1,128,512]{2,1,0:T(8,128)(2,1)}, bf16[1,128,512]{2,1,0:T(8,128)(2,1)}) custom-call(bf16[128,768]{1,0:T(8,128)(2,1)S(1)} %get-tuple-element.85.own, bf16[128,768]{1,0:T(8,128)(2,1)S(1)} %collective-permute-done.23.pair), custom_call_target="tpu_custom_call" | custom-call | bytes 786432 | tf_op jit(solution)/shard_map/outputs/pallas_call | solution.py:66
  (7 shorter events, 0.2 us)
Async XLA Ops:
  0.6 13.6 %collective-permute-start.7 = (bf16[128,1024]{1,0:T(8,128)(2,1)}, bf16[128,1024]{1,0:T(8,128)(2,1)S(1)}, u32[]{:S(2)}, u32[]{:S(2)}) collective-permute-start(bf16[128,1024]{1,0:T(8,128)(2,1)} %bitcast.1), channel_id=1, source_target_pairs={{0,1},{1,0},{2,3},{3,2},{4,5},{5,4},{6,7},{7,6},{8,9},{9,8},{10,11... | collective-permute-start | bytes 786440 | tf_op jit(solution)/shard_map/ppermute | solution.py:401
  1.1 1.8 %collective-permute-start.4 = (bf16[1,128,512]{2,1,0:T(8,128)(2,1)}, bf16[1,128,512]{2,1,0:T(8,128)(2,1)S(1)}, u32[]{:S(2)}, u32[]{:S(2)}) collective-permute-start(bf16[1,128,512]{2,1,0:T(8,128)(2,1)} %q.1), channel_id=1, source_target_pairs={{0,1},{1,0},{2,3},{3,2},{4,5},{5,4},{6,7},{7,6},{8,9},{9,8},{10,11... | collective-permute-start | bytes 393224 | tf_op jit(solution)/shard_map/ppermute | solution.py:401
  1.2 1.7 %collective-permute-start.5 = (bf16[1,128,512]{2,1,0:T(8,128)(2,1)}, bf16[1,128,512]{2,1,0:T(8,128)(2,1)S(1)}, u32[]{:S(2)}, u32[]{:S(2)}) collective-permute-start(bf16[1,128,512]{2,1,0:T(8,128)(2,1)} %k.1), channel_id=1, source_target_pairs={{0,1},{1,0},{2,3},{3,2},{4,5},{5,4},{6,7},{7,6},{8,9},{9,8},{10,11... | collective-permute-start | bytes 393224 | tf_op jit(solution)/shard_map/ppermute | solution.py:401
  1.7 1.6 %collective-permute-start.6 = (bf16[1,128,512]{2,1,0:T(8,128)(2,1)}, bf16[1,128,512]{2,1,0:T(8,128)(2,1)S(1)}, u32[]{:S(2)}, u32[]{:S(2)}) collective-permute-start(bf16[1,128,512]{2,1,0:T(8,128)(2,1)} %v.1), channel_id=1, source_target_pairs={{0,1},{1,0},{2,3},{3,2},{4,5},{5,4},{6,7},{7,6},{8,9},{9,8},{10,11... | collective-permute-start | bytes 393224 | tf_op jit(solution)/shard_map/ppermute | solution.py:401
  3.5 5.5 %collective-permute-start.8 = (bf16[128,384]{1,0:T(8,128)(2,1)S(1)}, bf16[128,384]{1,0:T(8,128)(2,1)S(1)}, u32[]{:S(2)}, u32[]{:S(2)}) collective-permute-start(bf16[128,384]{1,0:T(8,128)(2,1)S(1)} %get-tuple-element.51), channel_id=1, source_target_pairs={{0,2},{1,7},{2,0},{3,5},{4,6},{5,3},{6,4},{7,1},{8,10},{9,15},{10,... | collective-permute-start | bytes 294920 | tf_op jit(solution)/shard_map/ppermute | solution.py:412
  6.4 7.8 %collective-permute-start.9 = (bf16[128,384]{1,0:T(8,128)(2,1)S(1)}, bf16[128,384]{1,0:T(8,128)(2,1)S(1)}, u32[]{:S(2)}, u32[]{:S(2)}) collective-permute-start(bf16[128,384]{1,0:T(8,128)(2,1)S(1)} %get-tuple-element.52), channel_id=1, source_target_pairs={{0,6},{1,3},{2,4},{3,1},{4,2},{5,7},{6,0},{7,5},{8,14},{9,11},{10,... | collective-permute-start | bytes 294920 | tf_op jit(solution)/shard_map/ppermute | solution.py:412
  8.9 6.5 %collective-permute-start.10 = (bf16[128,128]{1,0:T(8,128)(2,1)S(1)}, bf16[128,128]{1,0:T(8,128)(2,1)S(1)}, u32[]{:S(2)}, u32[]{:S(2)}) collective-permute-start(bf16[128,128]{1,0:T(8,128)(2,1)S(1)} %get-tuple-element.57), channel_id=1, source_target_pairs={{0,4},{1,5},{2,6},{3,7},{4,0},{5,1},{6,2},{7,3},{8,12},{9,13},{10,... | collective-permute-start | bytes 98312 | tf_op jit(solution)/shard_map/ppermute | solution.py:412
  15.4 2.3 %copy-start = (bf16[64,1024]{1,0:T(8,128)(2,1)S(1)}, bf16[64,1024]{1,0:T(8,128)(2,1)}, u32[]{:S(2)}) copy-start(bf16[64,1024]{1,0:T(8,128)(2,1)} %w.1) | copy-start | bytes 393220
  16.1 15.4 %collective-permute-start.11 = (bf16[256,512]{1,0:T(8,128)(2,1)S(1)}, bf16[256,512]{1,0:T(8,128)(2,1)S(1)}, u32[]{:S(2)}, u32[]{:S(2)}) collective-permute-start(bf16[256,512]{1,0:T(8,128)(2,1)S(1)} %get-tuple-element.60), channel_id=1, source_target_pairs={{0,8},{1,17},{8,0},{9,25},{16,24},{17,1},{24,16},{25,9},{2,10},{3,... | collective-permute-start | bytes 786440 | tf_op jit(solution)/shard_map/ppermute | solution.py:425
  17.7 1.3 %collective-permute-start = (bf16[64,1024]{1,0:T(8,128)(2,1)S(1)}, bf16[64,1024]{1,0:T(8,128)(2,1)S(1)}, u32[]{:S(2)}, u32[]{:S(2)}) collective-permute-start(bf16[64,1024]{1,0:T(8,128)(2,1)S(1)} %copy-done), channel_id=1, source_target_pairs={{0,1},{1,0},{2,3},{3,2},{4,5},{5,4},{6,7},{7,6},{8,9},{9,8},{10,11... | collective-permute-start | bytes 393224 | tf_op jit(solution)/shard_map/ppermute | solution.py:401
  19.0 7.9 %collective-permute-start.1 = (bf16[128,256]{1,0:T(8,128)(2,1)S(1)}, bf16[128,256]{1,0:T(8,128)(2,1)S(1)}, u32[]{:S(2)}, u32[]{:S(2)}) collective-permute-start(bf16[128,256]{1,0:T(8,128)(2,1)S(1)} %w_head.1.own), channel_id=1, source_target_pairs={{0,2},{3,5},{4,6},{7,1},{8,10},{11,13},{12,14},{15,9},{16,18},{19,... | collective-permute-start | bytes 196616 | tf_op jit(solution)/shard_map/ppermute | solution.py:419
  21.3 5.7 %collective-permute-start.2 = (bf16[128,256]{1,0:T(8,128)(2,1)S(1)}, bf16[128,256]{1,0:T(8,128)(2,1)S(1)}, u32[]{:S(2)}, u32[]{:S(2)}) collective-permute-start(bf16[128,256]{1,0:T(8,128)(2,1)S(1)} %w_head.1.own), channel_id=1, source_target_pairs={{0,6},{3,1},{4,2},{7,5},{8,14},{11,9},{12,10},{15,13},{16,22},{19,... | collective-permute-start | bytes 196616 | tf_op jit(solution)/shard_map/ppermute | solution.py:419
  24.5 7.1 %collective-permute-start.3 = (bf16[128,256]{1,0:T(8,128)(2,1)S(1)}, bf16[128,256]{1,0:T(8,128)(2,1)S(1)}, u32[]{:S(2)}, u32[]{:S(2)}) collective-permute-start(bf16[128,256]{1,0:T(8,128)(2,1)S(1)} %w_head.1.own), channel_id=1, source_target_pairs={{0,4},{3,7},{4,0},{7,3},{8,12},{11,15},{12,8},{15,11},{16,20},{19,... | collective-permute-start | bytes 196616 | tf_op jit(solution)/shard_map/ppermute | solution.py:419
  31.6 5.0 %collective-permute-start.13 = (bf16[256,256]{1,0:T(8,128)(2,1)S(1)}, bf16[256,256]{1,0:T(8,128)(2,1)S(1)}, u32[]{:S(2)}, u32[]{:S(2)}) collective-permute-start(bf16[256,256]{1,0:T(8,128)(2,1)S(1)} %get-tuple-element.61._), channel_id=1, source_target_pairs={{0,16},{1,9},{8,24},{9,1},{16,0},{17,25},{24,8},{25,17},{2,18},{3,... | collective-permute-start | bytes 393224 | tf_op jit(solution)/shard_map/ppermute | solution.py:425
  36.7 1.4 %collective-permute-start.14 = (f32[128,256]{1,0:T(8,128)S(1)}, f32[128,256]{1,0:T(8,128)S(1)}, u32[]{:S(2)}, u32[]{:S(2)}) collective-permute-start(f32[128,256]{1,0:T(8,128)S(1)} %get-tuple-element.64), channel_id=1, source_target_pairs={{0,1},{1,0},{2,3},{3,2},{4,5},{5,4},{6,7},{7,6},{8,9},{9,8},{10,11... | collective-permute-start | bytes 393224 | tf_op jit(solution)/shard_map/ppermute | solution.py:401
  36.8 5.0 %collective-permute-start.12 = (bf16[256,256]{1,0:T(8,128)(2,1)S(1)}, bf16[256,256]{1,0:T(8,128)(2,1)S(1)}, u32[]{:S(2)}, u32[]{:S(2)}) collective-permute-start(bf16[256,256]{1,0:T(8,128)(2,1)S(1)} %w_rows.1.first), channel_id=1, source_target_pairs={{0,8},{1,17},{8,0},{9,25},{16,24},{17,1},{24,16},{25,9},{2,10},{3,... | collective-permute-start | bytes 393224 | tf_op jit(solution)/shard_map/ppermute | solution.py:425
  41.9 6.4 %collective-permute-start.15 = (bf16[256,512]{1,0:T(8,128)(2,1)S(1)}, bf16[256,512]{1,0:T(8,128)(2,1)S(1)}, u32[]{:S(2)}, u32[]{:S(2)}) collective-permute-start(bf16[256,512]{1,0:T(8,128)(2,1)S(1)} %w_half.1.refs_0_), channel_id=1, source_target_pairs={{0,16},{1,9},{8,24},{9,1},{16,0},{17,25},{24,8},{25,17},{2,18},{3,... | collective-permute-start | bytes 786440 | tf_op jit(solution)/shard_map/ppermute | solution.py:425
  43.4 6.4 %collective-permute-start.16 = (bf16[64,256]{1,0:T(8,128)(2,1)S(1)}, bf16[64,256]{1,0:T(8,128)(2,1)S(1)}, u32[]{:S(2)}, u32[]{:S(2)}) collective-permute-start(bf16[64,256]{1,0:T(8,128)(2,1)S(1)} %get-tuple-element.79), channel_id=1, source_target_pairs={{0,2},{1,7},{2,0},{3,5},{4,6},{5,3},{6,4},{7,1},{8,10},{9,15},{10,... | collective-permute-start | bytes 98312 | tf_op jit(solution)/shard_map/ppermute | solution.py:412
  43.4 6.4 %collective-permute-start.17 = (bf16[64,256]{1,0:T(8,128)(2,1)S(1)}, bf16[64,256]{1,0:T(8,128)(2,1)S(1)}, u32[]{:S(2)}, u32[]{:S(2)}) collective-permute-start(bf16[64,256]{1,0:T(8,128)(2,1)S(1)} %get-tuple-element.80), channel_id=1, source_target_pairs={{0,6},{1,3},{2,4},{3,1},{4,2},{5,7},{6,0},{7,5},{8,14},{9,11},{10,... | collective-permute-start | bytes 98312 | tf_op jit(solution)/shard_map/ppermute | solution.py:412
  45.5 4.8 %collective-permute-start.18 = (bf16[64,256]{1,0:T(8,128)(2,1)S(1)}, bf16[64,256]{1,0:T(8,128)(2,1)S(1)}, u32[]{:S(2)}, u32[]{:S(2)}) collective-permute-start(bf16[64,256]{1,0:T(8,128)(2,1)S(1)} %get-tuple-element.81), channel_id=1, source_target_pairs={{0,4},{1,5},{2,6},{3,7},{4,0},{5,1},{6,2},{7,3},{8,12},{9,13},{10,... | collective-permute-start | bytes 98312 | tf_op jit(solution)/shard_map/ppermute | solution.py:412
  50.4 8.4 %collective-permute-start.19 = (bf16[128,384]{1,0:T(8,128)(2,1)S(1)}, bf16[128,384]{1,0:T(8,128)(2,1)S(1)}, u32[]{:S(2)}, u32[]{:S(2)}) collective-permute-start(bf16[128,384]{1,0:T(8,128)(2,1)S(1)} %get-tuple-element.82), channel_id=1, source_target_pairs={{0,2},{1,7},{2,0},{3,5},{4,6},{5,3},{6,4},{7,1},{8,10},{9,15},{10,... | collective-permute-start | bytes 294920 | tf_op jit(solution)/shard_map/ppermute | solution.py:412
  50.4 8.3 %collective-permute-start.20 = (bf16[128,384]{1,0:T(8,128)(2,1)S(1)}, bf16[128,384]{1,0:T(8,128)(2,1)S(1)}, u32[]{:S(2)}, u32[]{:S(2)}) collective-permute-start(bf16[128,384]{1,0:T(8,128)(2,1)S(1)} %get-tuple-element.83), channel_id=1, source_target_pairs={{0,6},{1,3},{2,4},{3,1},{4,2},{5,7},{6,0},{7,5},{8,14},{9,11},{10,... | collective-permute-start | bytes 294920 | tf_op jit(solution)/shard_map/ppermute | solution.py:412
  53.3 4.0 %collective-permute-start.22 = (bf16[64,256]{1,0:T(8,128)(2,1)S(1)}, bf16[64,256]{1,0:T(8,128)(2,1)S(1)}, u32[]{:S(2)}, u32[]{:S(2)}) collective-permute-start(bf16[64,256]{1,0:T(8,128)(2,1)S(1)} %weight_sum.1.first), channel_id=1, source_target_pairs={{0,8},{1,17},{8,0},{9,25},{16,24},{17,1},{24,16},{25,9},{2,10},{3,... | collective-permute-start | bytes 98312 | tf_op jit(solution)/shard_map/ppermute | solution.py:425
  53.9 4.8 %collective-permute-start.21 = (bf16[128,128]{1,0:T(8,128)(2,1)S(1)}, bf16[128,128]{1,0:T(8,128)(2,1)S(1)}, u32[]{:S(2)}, u32[]{:S(2)}) collective-permute-start(bf16[128,128]{1,0:T(8,128)(2,1)S(1)} %get-tuple-element.84), channel_id=1, source_target_pairs={{0,4},{1,5},{2,6},{3,7},{4,0},{5,1},{6,2},{7,3},{8,12},{9,13},{10,... | collective-permute-start | bytes 98312 | tf_op jit(solution)/shard_map/ppermute | solution.py:412
  59.1 5.1 %collective-permute-start.23 = (bf16[128,768]{1,0:T(8,128)(2,1)S(1)}, bf16[128,768]{1,0:T(8,128)(2,1)S(1)}, u32[]{:S(2)}, u32[]{:S(2)}) collective-permute-start(bf16[128,768]{1,0:T(8,128)(2,1)S(1)} %get-tuple-element.86), channel_id=1, source_target_pairs={{0,1},{1,0},{2,3},{3,2},{4,5},{5,4},{6,7},{7,6},{8,9},{9,8},{10,11... | collective-permute-start | bytes 589832 | tf_op jit(solution)/shard_map/ppermute | solution.py:401
  59.2 4.3 %collective-permute-start.24 = (bf16[64,512]{1,0:T(8,128)(2,1)S(1)}, bf16[64,512]{1,0:T(8,128)(2,1)S(1)}, u32[]{:S(2)}, u32[]{:S(2)}) collective-permute-start(bf16[64,512]{1,0:T(8,128)(2,1)S(1)} %both.1.refs_1_), channel_id=1, source_target_pairs={{0,16},{1,9},{8,24},{9,1},{16,0},{17,25},{24,8},{25,17},{2,18},{3,... | collective-permute-start | bytes 196616 | tf_op jit(solution)/shard_map/ppermute | solution.py:425

commit v7 on v6

--- a/solution.py
+++ b/solution.py
@@ -138,27 +138,23 @@
         to_c[0][...] = total.astype(BF)
 
 
-def w_head_kernel(own, pair, out):
-    core, _, dp = places()
-    rows, width = own.shape
-    out[at(core * rows, rows), :] = own[...]
-    out[at((1 - core) * rows, rows), :] = pair[:, at(dp * width, width)]
-
-
-def w_rows_kernel(own, a, b, c, _, out):
+def relay_kernel(w, a, b, c, keep, send, heads):
     core, z, _ = places()
     way = links(True)
-    group = lax.div(z, 2)
-
-    @pl.when(lax.rem(z, 2) == core)
-    def _():
-        out[at(group * DH), :] = own[...]
-        out[at((1 - group) * DH), :] = c[...]
-
-    @pl.when(lax.rem(z, 2) != core)
-    def _():
-        out[at(lax.div(z ^ way["first"], 2) * DH), :] = a[...]
-        out[at(lax.div(z ^ way["second"], 2) * DH), :] = b[...]
+    heads[z] = w[...]
+    for source, step in ((a, way["first"]), (b, way["second"]), (c, 2)):
+        heads[z ^ step] = source[...]
+    for group in range(2):
+        keep[group] = heads[2 * group + core]
+        send[group] = heads[2 * group + 1 - core]
+
+
+def w_rows_kernel(keep, got, out):
+    core, _, _ = places()
+    half = keep.shape[1]
+    for group in range(2):
+        out[at(group * DH + core * half, half), :] = keep[group]
+        out[at(group * DH + (1 - core) * half, half), :] = got[group]
 
 
 def join_kernel(first, second, *refs):
@@ -221,7 +217,7 @@
     rows = mine.shape[0]
     total = state[...]
     if direct:
-        a, b, c, soft_send, u_out, total_out, keep, out = refs
+        a, b, c, soft_send, _, u_out, total_out, keep, out = refs
         total = total + a[:, 2 * DH :].astype(F32) + b[:, 2 * DH :].astype(F32) + c[...].astype(F32)
     else:
         u_out, total_out, keep = refs
@@ -236,7 +232,7 @@
         out[:DH, :] = soft_send[...]
 
 
-def fold_kernel(keep_soft, keep_lin, got, _a, _b, _c, keep, send):
+def fold_kernel(keep_soft, keep_lin, got, keep, send):
     width = keep.shape[1]
     for rows, source in ((slice(0, DH), keep_soft), (slice(DH, 2 * DH), keep_lin)):
         keep[rows, :] = source[:, :width] + got[rows, :width].astype(F32)
@@ -411,13 +407,6 @@
                 pairs.append((2 * z + c, 2 * there + c))
         return lax.ppermute(value, axes, pairs)
 
-    def from_matching(value, which):
-        pairs = []
-        for z in range(n_z):
-            c = z % 2
-            pairs.append((2 * z + c, 2 * (z ^ (1 + 2 * c, 3 - 2 * c, 2)[which]) + c))
-        return lax.ppermute(value, axes, pairs)
-
     def over_dp(value, which):
         pairs = [
             (2 * d + c, 2 * (d ^ (1 + c, 2 - c)[which]) + c) for d in range(n_dp) for c in range(2)
@@ -431,7 +420,6 @@
 
     q_pair, k_pair, v_pair = over_core(queries), over_core(key_rows), over_core(value_rows)
     og_recv = over_core(out_grad[0])
-    w_pair = over_core(out_weight)
     mine, og, w_part, gain = call(
         pack_kernel, "pack",
         [
@@ -452,6 +440,19 @@
     )
     if direct:
         a, b, c = over_z(to_a, 0), over_z(to_b, 1), [over_z(rest[0], 2)]
+        w_keep, w_send = call(
+            relay_kernel, "relay", [like((2, half, width), BF)] * 2,
+            [w_part] + [over_z(w_part, which) for which in range(3)],
+            scratch=[pltpu.VMEM((HEADS, half, width), BF)],
+        )
+        w_own = call(
+            w_rows_kernel, "w_rows", [like((2 * DH, width), BF)], [w_keep, over_core(w_send)]
+        )[0]
+        w_got = over_dp(w_own, 0)
+        w_half = call(
+            join_kernel, "w_half", [like((2 * DH, 2 * width), BF)], [w_own, w_got]
+        )[0]
+        weights = [w_half, over_dp(w_half, 1)]
     else:
         a, b, c = over_z(to_a, 0), over_z(to_b, 1), []
         state = lax.psum(state, "z")
@@ -475,22 +476,15 @@
         functools.partial(lin_forward_kernel, direct), "lin_forward",
         [like((2 * rows, DH), F32), like((DH, DH), F32), like((DH, keep_width), F32)]
         + [like((2 * DH, 2 * width), BF)] * direct,
-        [state, mine, pair, ogs, gain] + ([a, b] + c + soft_send if direct else []),
+        [state, mine, pair, ogs, gain] + ([a, b] + c + soft_send + [w_own] if direct else []),
         flops=wg_flops,
     )
     if direct:
         got = over_dp(sent[0], 0)
-        w_head = call(w_head_kernel, "w_head", [like((DH, width), BF)], [w_part, w_pair])[0]
-        w_far = [from_matching(w_head, which) for which in range(3)]
         keep, sent = call(
             fold_kernel, "fold", [like((2 * DH, width), F32), like((2 * DH, width), BF)],
-            [keep_soft, keep_lin, got] + w_far,
+            [keep_soft, keep_lin, got],
         )
-        w_own = call(
-            w_rows_kernel, "w_rows", [like((2 * DH, width), BF)],
-            [w_head] + w_far + [sent],
-        )[0]
-        w_got = over_dp(w_own, 0)
         got = over_dp(sent, 1)
         row_own, row_send = call(
             rows_kernel, "rows", [like((2 * half, width), F32)] * 2, [keep, got],
@@ -501,10 +495,6 @@
             chunk_kernel, "chunk", [like((half, width), BF)] * 3 + [like((half, width), F32)],
             [row_own, row_recv], scratch=[pltpu.VMEM((HEADS, half, width), F32)],
         )
-        w_half = call(
-            join_kernel, "w_half", [like((2 * DH, 2 * width), BF)], [w_own, w_got, chunk]
-        )[0]
-        weights = [w_half, over_dp(w_half, 1)]
         chunks = [over_z(value, which) for which, value in enumerate(to_chips)]
         summed = call(
             functools.partial(weight_sum_kernel, scale), "weight_sum", [like((half, width), BF)],

time: 65.3 us -> 57 us (0.87)
  waiting for transfers between devices: 28.4 us -> 22.2 us
  starting transfers between devices: 28.8 us -> 26.8 us
    ppermute x3 -> x0, starting transfers between devices: 7.91 us -> none  [from_matching(): return lax.ppermute(value, axes, pairs)]
    ppermute x9 -> x12, starting transfers between devices: 12.5 us -> 17.2 us  [over_z(): return lax.ppermute(value, axes, pairs)]
    ppermute x3 -> x0, waiting for transfers between devices: 4.56 us -> none  [from_matching(): return lax.ppermute(value, axes, pairs)]
    ppermute x6, waiting for transfers between devices: 14.4 us -> 10.7 us  [over_dp(): return lax.ppermute(value, ('dp', 'core'), pairs)]
    ppermute x9 -> x12, waiting for transfers between devices: 7.11 us -> 9.03 us  [over_z(): return lax.ppermute(value, axes, pairs)]
    ppermute x6, starting transfers between devices: 7.17 us -> 8.34 us  [over_dp(): return lax.ppermute(value, ('dp', 'core'), pairs)]
  transfers between devices with their start and end apart: 25 -> 25, of which waited for: 12 -> 12; matrix products, arithmetic and copies ran while one was open for 0% -> 0% of each run, Pallas kernels for 8% -> 9%
where the time goes in v7:
time: 57 us; the launch traced here: 56.9 us
  starting transfers between devices  26.8 us (47%)
  waiting for transfers between devices  22.2 us (39%)
  Pallas kernels  7.03 us (12%)
  between operations  0.78 us (1%)
    ppermute x12, starting transfers between devices, over_z(): return lax.ppermute(value, axes, pairs)  17.2 us
    ppermute x6, waiting for transfers between devices, over_dp(): return lax.ppermute(value, ('dp', 'core'), pairs)  10.7 us
    ppermute x12, waiting for transfers between devices, over_z(): return lax.ppermute(value, axes, pairs)  9.03 us
    ppermute x6, starting transfers between devices, over_dp(): return lax.ppermute(value, ('dp', 'core'), pairs)  8.34 us
    pallas_call x17, Pallas kernels, call(): pl.pallas_call(kernel, name=name, out_shape=list(outs), in_specs=spaces o...  7.03 us
    ppermute x7, waiting for transfers between devices, over_core(): return lax.ppermute(value, 'core', pair_perm)  2.51 us
    ppermute x7, starting transfers between devices, over_core(): return lax.ppermute(value, 'core', pair_perm)  1.32 us
  transfers between devices with their start and end apart: 25, of which 12 were waited for; matrix products, arithmetic and copies ran while one was open for 0% of the time, Pallas kernels for 9%

profile of v7, /device:TPU:0, one launch (start us, length us, event | category | flops | bytes accessed | tf_op | source)
XLA Modules:
  0.0 56.9 jit_solution(8024752581506527621)
XLA Ops:
  0.6 0.5 collective-permute-start.9
  1.2 0.1 collective-permute-start.6
  1.2 0.4 collective-permute-start.7
  1.7 0.1 collective-permute-start.8
  1.7 1.2 %pack.1 = (bf16[128,768]{1,0:T(8,128)(2,1)S(1)}, bf16[128,1024]{1,0:T(8,128)(2,1)S(1)}, bf16[64,256]{1,0:T(8,128)(2,1)S(1)}, f32[1,128]{1,0:T(1,128)S(1)}) custom-call(bf16[1,128,512]{2,1,0:T(8,128)(2,1)} %q.1, bf16[1,128,512]{2,1,0:T(8,128)(2,1)} %k.1, bf16[1,128,512]{2,1,0:T(8,128)(2,1)} %v.1, bf16[1,128,1024]{2,1,0:T(8,128)(2,1)} %og.1, ...), custom_call_target="tpu_custom_call" | custom-call | bytes 1279488 | tf_op jit(solution)/shard_map/pack/pallas_call | solution.py:66
  2.9 3.1 %collective-permute-start = (bf16[64,256]{1,0:T(8,128)(2,1)S(1)}, bf16[64,256]{1,0:T(8,128)(2,1)S(1)}, u32[]{:S(2)}, u32[]{:S(2)}) collective-permute-start(bf16[64,256]{1,0:T(8,128)(2,1)S(1)} %get-tuple-element.49.w), channel_id=1, source_target_pairs={{0,2},{1,7},{2,0},{3,5},{4,6},{5,3},{6,4},{7,1},{8,10},{9,15},{10,... | collective-permute-start | bytes 98312 | tf_op jit(solution)/shard_map/ppermute | solution.py:408
  6.0 0.0 collective-permute-done.6.q_pair
  6.0 2.5 %collective-permute-start.1 = (bf16[64,256]{1,0:T(8,128)(2,1)S(1)}, bf16[64,256]{1,0:T(8,128)(2,1)S(1)}, u32[]{:S(2)}, u32[]{:S(2)}) collective-permute-start(bf16[64,256]{1,0:T(8,128)(2,1)S(1)} %get-tuple-element.49.w), channel_id=1, source_target_pairs={{0,6},{1,3},{2,4},{3,1},{4,2},{5,7},{6,0},{7,5},{8,14},{9,11},{10,... | collective-permute-start | bytes 98312 | tf_op jit(solution)/shard_map/ppermute | solution.py:408
  8.5 0.0 collective-permute-done.7.k_pair
  8.5 0.2 collective-permute-start.2
  8.7 0.0 collective-permute-done.8.v_pair
  8.7 0.3 state.1
  8.9 1.8 %collective-permute-start.10 = (bf16[128,384]{1,0:T(8,128)(2,1)S(1)}, bf16[128,384]{1,0:T(8,128)(2,1)S(1)}, u32[]{:S(2)}, u32[]{:S(2)}) collective-permute-start(bf16[128,384]{1,0:T(8,128)(2,1)S(1)} %get-tuple-element.55), channel_id=1, source_target_pairs={{0,2},{1,7},{2,0},{3,5},{4,6},{5,3},{6,4},{7,1},{8,10},{9,15},{10,... | collective-permute-start | bytes 294920 | tf_op jit(solution)/shard_map/ppermute | solution.py:408
  10.7 0.0 collective-permute-done.a
  10.7 2.5 %collective-permute-start.11 = (bf16[128,384]{1,0:T(8,128)(2,1)S(1)}, bf16[128,384]{1,0:T(8,128)(2,1)S(1)}, u32[]{:S(2)}, u32[]{:S(2)}) collective-permute-start(bf16[128,384]{1,0:T(8,128)(2,1)S(1)} %get-tuple-element.56), channel_id=1, source_target_pairs={{0,6},{1,3},{2,4},{3,1},{4,2},{5,7},{6,0},{7,5},{8,14},{9,11},{10,... | collective-permute-start | bytes 294920 | tf_op jit(solution)/shard_map/ppermute | solution.py:408
  13.2 0.0 collective-permute-done.1.b
  13.2 1.9 %collective-permute-done.2.c = bf16[64,256]{1,0:T(8,128)(2,1)S(1)} collective-permute-done((bf16[64,256]{1,0:T(8,128)(2,1)S(1)}, bf16[64,256]{1,0:T(8,128)(2,1)S(1)}, u32[]{:S(2)}, u32[]{:S(2)}) %collective-permute-start.2) | collective-permute-done | bytes 32800 | tf_op jit(solution)/shard_map/ppermute | solution.py:408
  15.2 0.1 collective-permute-start.3
  15.2 0.1 collective-permute-start.12
  15.3 1.2 %collective-permute-done.3.got = bf16[2,64,256]{2,1,0:T(8,128)(2,1)S(1)} collective-permute-done((bf16[2,64,256]{2,1,0:T(8,128)(2,1)S(1)}, bf16[2,64,256]{2,1,0:T(8,128)(2,1)S(1)}, u32[]{:S(2)}, u32[]{:S(2)}) %collective-permute-start.3) | collective-permute-done | bytes 65568 | tf_op jit(solution)/shard_map/ppermute | solution.py:397
  16.5 0.0 collective-permute-done.10.a.refs_0_
  16.5 1.0 %collective-permute-done.11.b.refs_1_ = bf16[128,384]{1,0:T(8,128)(2,1)S(1)} collective-permute-done((bf16[128,384]{1,0:T(8,128)(2,1)S(1)}, bf16[128,384]{1,0:T(8,128)(2,1)S(1)}, u32[]{:S(2)}, u32[]{:S(2)}) %collective-permute-start.11) | collective-permute-done | bytes 98336 | tf_op jit(solution)/shard_map/ppermute | solution.py:408
  17.5 0.0 collective-permute-done.9.og_recv
  17.5 1.2 %soft_forward.1 = (bf16[256,128]{1,0:T(8,128)(2,1)S(1)}, bf16[512,128]{1,0:T(8,128)(2,1)S(1)}, bf16[512,128]{1,0:T(8,128)(2,1)S(1)}, bf16[256,1024]{1,0:T(8,128)...) custom-call(bf16[128,768]{1,0:T(8,128)(2,1)S(1)} %get-tuple-element., ...), custom_call_target="tpu_custom_call" | custom-call | flops 67108864 | bytes 2883584 | tf_op jit(solution)/shard_map/soft_forward/pallas_call | solution.py:66
  18.7 1.4 %collective-permute-done.12.refs_2_ = bf16[128,128]{1,0:T(8,128)(2,1)S(1)} collective-permute-done((bf16[128,128]{1,0:T(8,128)(2,1)S(1)}, bf16[128,128]{1,0:T(8,128)(2,1)S(1)}, u32[]{:S(2)}, u32[]{:S(2)}) %collective-permute-start.12) | collective-permute-done | bytes 32800 | tf_op jit(solution)/shard_map/ppermute | solution.py:408
  20.1 0.7 %lin_forward.1 = (f32[256,128]{1,0:T(8,128)S(1)}, f32[128,128]{1,0:T(8,128)S(1)}, f32[128,512]{1,0:T(8,128)S(1)}, bf16[256,512]{1,0:T(8,128)(2,1)S(1)}) custom-call(f32[128,128]{1,0:T(8,128)S(1)} %get-tuple-element.58.state, bf16[128,768]{1,0:T(8,128)(2,1)S(1)} %get-tuple-element.52.mine.refs_5_, bf16[128,768]{1,0:T(8,128)(2,1)S(1)} %get-tuple-element.53.pair.refs_6_, ...), custom_call_target="tpu_custom_call" | custom-call | flops 67108864 | bytes 2195968 | tf_op jit(solution)/shard_map/lin_forward/pallas_call | solution.py:66
  20.8 1.6 %collective-permute-start.13 = (bf16[256,512]{1,0:T(8,128)(2,1)S(1)}, bf16[256,512]{1,0:T(8,128)(2,1)S(1)}, u32[]{:S(2)}, u32[]{:S(2)}) collective-permute-start(bf16[256,512]{1,0:T(8,128)(2,1)S(1)} %get-tuple-element.77), channel_id=1, source_target_pairs={{0,8},{1,17},{8,0},{9,25},{16,24},{17,1},{24,16},{25,9},{2,10},{3,... | collective-permute-start | bytes 786440 | tf_op jit(solution)/shard_map/ppermute | solution.py:414
  22.4 0.5 collective-permute-start.4
  22.9 4.3 %collective-permute-done.13.got = bf16[256,512]{1,0:T(8,128)(2,1)S(1)} collective-permute-done((bf16[256,512]{1,0:T(8,128)(2,1)S(1)}, bf16[256,512]{1,0:T(8,128)(2,1)S(1)}, u32[]{:S(2)}, u32[]{:S(2)}) %collective-permute-start.13) | collective-permute-done | bytes 262176 | tf_op jit(solution)/shard_map/ppermute | solution.py:414
  27.3 0.1 fold.1
  27.3 1.6 %collective-permute-start.14 = (bf16[256,256]{1,0:T(8,128)(2,1)S(1)}, bf16[256,256]{1,0:T(8,128)(2,1)S(1)}, u32[]{:S(2)}, u32[]{:S(2)}) collective-permute-start(bf16[256,256]{1,0:T(8,128)(2,1)S(1)} %get-tuple-element.79), channel_id=1, source_target_pairs={{0,16},{1,9},{8,24},{9,1},{16,0},{17,25},{24,8},{25,17},{2,18},{3,... | collective-permute-start | bytes 393224 | tf_op jit(solution)/shard_map/ppermute | solution.py:414
  28.9 0.0 collective-permute-done.4.second
  28.9 1.5 %collective-permute-start.5 = (bf16[256,512]{1,0:T(8,128)(2,1)S(1)}, bf16[256,512]{1,0:T(8,128)(2,1)S(1)}, u32[]{:S(2)}, u32[]{:S(2)}) collective-permute-start(bf16[256,512]{1,0:T(8,128)(2,1)S(1)} %w_half.1.refs_0_), channel_id=1, source_target_pairs={{0,16},{1,9},{8,24},{9,1},{16,0},{17,25},{24,8},{25,17},{2,18},{3,... | collective-permute-start | bytes 786440 | tf_op jit(solution)/shard_map/ppermute | solution.py:414
  30.4 1.9 %collective-permute-done.14.got = bf16[256,256]{1,0:T(8,128)(2,1)S(1)} collective-permute-done((bf16[256,256]{1,0:T(8,128)(2,1)S(1)}, bf16[256,256]{1,0:T(8,128)(2,1)S(1)}, u32[]{:S(2)}, u32[]{:S(2)}) %collective-permute-start.14) | collective-permute-done | bytes 131104 | tf_op jit(solution)/shard_map/ppermute | solution.py:414
  32.3 0.1 rows.1
  32.4 0.1 collective-permute-start.15
  32.5 1.3 %collective-permute-done.15.got = f32[128,256]{1,0:T(8,128)S(1)} collective-permute-done((f32[128,256]{1,0:T(8,128)S(1)}, f32[128,256]{1,0:T(8,128)S(1)}, u32[]{:S(2)}, u32[]{:S(2)}) %collective-permute-start.15) | collective-permute-done | bytes 131104 | tf_op jit(solution)/shard_map/ppermute | solution.py:397
  33.9 0.1 collective-permute-start.16
  33.9 1.5 %collective-permute-start.17 = (bf16[64,256]{1,0:T(8,128)(2,1)S(1)}, bf16[64,256]{1,0:T(8,128)(2,1)S(1)}, u32[]{:S(2)}, u32[]{:S(2)}) collective-permute-start(bf16[64,256]{1,0:T(8,128)(2,1)S(1)} %get-tuple-element.83), channel_id=1, source_target_pairs={{0,6},{1,3},{2,4},{3,1},{4,2},{5,7},{6,0},{7,5},{8,14},{9,11},{10,... | collective-permute-start | bytes 98312 | tf_op jit(solution)/shard_map/ppermute | solution.py:408
  35.5 1.9 %collective-permute-start.18 = (bf16[64,256]{1,0:T(8,128)(2,1)S(1)}, bf16[64,256]{1,0:T(8,128)(2,1)S(1)}, u32[]{:S(2)}, u32[]{:S(2)}) collective-permute-start(bf16[64,256]{1,0:T(8,128)(2,1)S(1)} %get-tuple-element.84), channel_id=1, source_target_pairs={{0,4},{1,5},{2,6},{3,7},{4,0},{5,1},{6,2},{7,3},{8,12},{9,13},{10,... | collective-permute-start | bytes 98312 | tf_op jit(solution)/shard_map/ppermute | solution.py:408
  37.4 0.0 collective-permute-done.5.refs_1_
  37.4 1.5 %backward.1 = (bf16[128,128]{1,0:T(8,128)(2,1)S(1)}, bf16[128,128]{1,0:T(8,128)(2,1)S(1)}, f32[128,128]{1,0:T(8,128)S(1)}, f32[256,128]{1,0:T(8,128)S(1)}, f32[5...) custom-call(bf16[256,512]{1,0:T(8,128)(2,1)S(1)} %w_half.1.refs_0_, bf16[256,512]{1,0:T(8,128)(2,1)S(1)} %collective-permute-done.5.refs_1_, ...), custom_call_target="tpu_custom_call" | custom-call | flops 335544320 | bytes 3277312 | tf_op jit(solution)/shard_map/backward/pallas_call | solution.py:66
  39.0 0.0 collective-permute-done.16.refs_1_.a
  39.0 0.9 %collective-permute-done.17.refs_2_.b = bf16[64,256]{1,0:T(8,128)(2,1)S(1)} collective-permute-done((bf16[64,256]{1,0:T(8,128)(2,1)S(1)}, bf16[64,256]{1,0:T(8,128)(2,1)S(1)}, u32[]{:S(2)}, u32[]{:S(2)}) %collective-permute-start.17) | collective-permute-done | bytes 32800 | tf_op jit(solution)/shard_map/ppermute | solution.py:408
  39.8 1.1 %collective-permute-done.18.refs_3_.c = bf16[64,256]{1,0:T(8,128)(2,1)S(1)} collective-permute-done((bf16[64,256]{1,0:T(8,128)(2,1)S(1)}, bf16[64,256]{1,0:T(8,128)(2,1)S(1)}, u32[]{:S(2)}, u32[]{:S(2)}) %collective-permute-start.18) | collective-permute-done | bytes 32800 | tf_op jit(solution)/shard_map/ppermute | solution.py:408
  41.0 0.4 collective-permute-start.19
  41.4 2.4 %collective-permute-start.20 = (bf16[128,384]{1,0:T(8,128)(2,1)S(1)}, bf16[128,384]{1,0:T(8,128)(2,1)S(1)}, u32[]{:S(2)}, u32[]{:S(2)}) collective-permute-start(bf16[128,384]{1,0:T(8,128)(2,1)S(1)} %get-tuple-element.86), channel_id=1, source_target_pairs={{0,6},{1,3},{2,4},{3,1},{4,2},{5,7},{6,0},{7,5},{8,14},{9,11},{10,... | collective-permute-start | bytes 294920 | tf_op jit(solution)/shard_map/ppermute | solution.py:408
  43.8 1.6 %collective-permute-start.22 = (bf16[64,256]{1,0:T(8,128)(2,1)S(1)}, bf16[64,256]{1,0:T(8,128)(2,1)S(1)}, u32[]{:S(2)}, u32[]{:S(2)}) collective-permute-start(bf16[64,256]{1,0:T(8,128)(2,1)S(1)} %weight_sum.1.first), channel_id=1, source_target_pairs={{0,8},{1,17},{8,0},{9,25},{16,24},{17,1},{24,16},{25,9},{2,10},{3,... | collective-permute-start | bytes 98312 | tf_op jit(solution)/shard_map/ppermute | solution.py:414
  45.4 0.7 %collective-permute-start.21 = (bf16[128,128]{1,0:T(8,128)(2,1)S(1)}, bf16[128,128]{1,0:T(8,128)(2,1)S(1)}, u32[]{:S(2)}, u32[]{:S(2)}) collective-permute-start(bf16[128,128]{1,0:T(8,128)(2,1)S(1)} %get-tuple-element.87), channel_id=1, source_target_pairs={{0,4},{1,5},{2,6},{3,7},{4,0},{5,1},{6,2},{7,3},{8,12},{9,13},{10,... | collective-permute-start | bytes 98312 | tf_op jit(solution)/shard_map/ppermute | solution.py:408
  46.1 1.7 %collective-permute-done.22.second = bf16[64,256]{1,0:T(8,128)(2,1)S(1)} collective-permute-done((bf16[64,256]{1,0:T(8,128)(2,1)S(1)}, bf16[64,256]{1,0:T(8,128)(2,1)S(1)}, u32[]{:S(2)}, u32[]{:S(2)}) %collective-permute-start.22) | collective-permute-done | bytes 32800 | tf_op jit(solution)/shard_map/ppermute | solution.py:414
  47.8 2.7 %collective-permute-done.21.refs_0_ = bf16[128,128]{1,0:T(8,128)(2,1)S(1)} collective-permute-done((bf16[128,128]{1,0:T(8,128)(2,1)S(1)}, bf16[128,128]{1,0:T(8,128)(2,1)S(1)}, u32[]{:S(2)}, u32[]{:S(2)}) %collective-permute-start.21) | collective-permute-done | bytes 32800 | tf_op jit(solution)/shard_map/ppermute | solution.py:408
  50.5 0.0 collective-permute-done.19.a
  50.5 0.0 collective-permute-done.20.b
  50.5 0.4 final.1
  50.9 0.1 collective-permute-start.23
  51.0 1.6 %collective-permute-start.24 = (bf16[64,512]{1,0:T(8,128)(2,1)S(1)}, bf16[64,512]{1,0:T(8,128)(2,1)S(1)}, u32[]{:S(2)}, u32[]{:S(2)}) collective-permute-start(bf16[64,512]{1,0:T(8,128)(2,1)S(1)} %both.1.refs_1_), channel_id=1, source_target_pairs={{0,16},{1,9},{8,24},{9,1},{16,0},{17,25},{24,8},{25,17},{2,18},{3,... | collective-permute-start | bytes 196616 | tf_op jit(solution)/shard_map/ppermute | solution.py:414
  52.6 2.7 %collective-permute-done.24.got = bf16[64,512]{1,0:T(8,128)(2,1)S(1)} collective-permute-done((bf16[64,512]{1,0:T(8,128)(2,1)S(1)}, bf16[64,512]{1,0:T(8,128)(2,1)S(1)}, u32[]{:S(2)}, u32[]{:S(2)}) %collective-permute-start.24) | collective-permute-done | bytes 65568 | tf_op jit(solution)/shard_map/ppermute | solution.py:414
  55.3 0.7 %weight_join.1 = f32[64,1024]{1,0:T(8,128)} custom-call(bf16[64,512]{1,0:T(8,128)(2,1)S(1)} %both.1.refs_1_, bf16[64,512]{1,0:T(8,128)(2,1)S(1)} %collective-permute-done.24.got), custom_call_target="tpu_custom_call" | custom-call | bytes 393216 | tf_op jit(solution)/shard_map/weight_join/pallas_call | solution.py:66
  56.1 0.0 collective-permute-done.23.pair
  56.1 0.8 %outputs.1 = (bf16[1,128,512]{2,1,0:T(8,128)(2,1)}, bf16[1,128,512]{2,1,0:T(8,128)(2,1)}, bf16[1,128,512]{2,1,0:T(8,128)(2,1)}) custom-call(bf16[128,768]{1,0:T(8,128)(2,1)S(1)} %get-tuple-element.89.own, bf16[128,768]{1,0:T(8,128)(2,1)S(1)} %collective-permute-done.23.pair), custom_call_target="tpu_custom_call" | custom-call | bytes 786432 | tf_op jit(solution)/shard_map/outputs/pallas_call | solution.py:66
  (7 shorter events, 0.2 us)
Async XLA Ops:
  0.6 16.9 %collective-permute-start.9 = (bf16[128,1024]{1,0:T(8,128)(2,1)}, bf16[128,1024]{1,0:T(8,128)(2,1)S(1)}, u32[]{:S(2)}, u32[]{:S(2)}) collective-permute-start(bf16[128,1024]{1,0:T(8,128)(2,1)} %bitcast.1), channel_id=1, source_target_pairs={{0,1},{1,0},{2,3},{3,2},{4,5},{5,4},{6,7},{7,6},{8,9},{9,8},{10,11... | collective-permute-start | bytes 786440 | tf_op jit(solution)/shard_map/ppermute | solution.py:397
  1.2 4.8 %collective-permute-start.6 = (bf16[1,128,512]{2,1,0:T(8,128)(2,1)}, bf16[1,128,512]{2,1,0:T(8,128)(2,1)S(1)}, u32[]{:S(2)}, u32[]{:S(2)}) collective-permute-start(bf16[1,128,512]{2,1,0:T(8,128)(2,1)} %q.1), channel_id=1, source_target_pairs={{0,1},{1,0},{2,3},{3,2},{4,5},{5,4},{6,7},{7,6},{8,9},{9,8},{10,11... | collective-permute-start | bytes 393224 | tf_op jit(solution)/shard_map/ppermute | solution.py:397
  1.2 7.2 %collective-permute-start.7 = (bf16[1,128,512]{2,1,0:T(8,128)(2,1)}, bf16[1,128,512]{2,1,0:T(8,128)(2,1)S(1)}, u32[]{:S(2)}, u32[]{:S(2)}) collective-permute-start(bf16[1,128,512]{2,1,0:T(8,128)(2,1)} %k.1), channel_id=1, source_target_pairs={{0,1},{1,0},{2,3},{3,2},{4,5},{5,4},{6,7},{7,6},{8,9},{9,8},{10,11... | collective-permute-start | bytes 393224 | tf_op jit(solution)/shard_map/ppermute | solution.py:397
  1.7 7.0 %collective-permute-start.8 = (bf16[1,128,512]{2,1,0:T(8,128)(2,1)}, bf16[1,128,512]{2,1,0:T(8,128)(2,1)S(1)}, u32[]{:S(2)}, u32[]{:S(2)}) collective-permute-start(bf16[1,128,512]{2,1,0:T(8,128)(2,1)} %v.1), channel_id=1, source_target_pairs={{0,1},{1,0},{2,3},{3,2},{4,5},{5,4},{6,7},{7,6},{8,9},{9,8},{10,11... | collective-permute-start | bytes 393224 | tf_op jit(solution)/shard_map/ppermute | solution.py:397
  2.9 7.8 %collective-permute-start = (bf16[64,256]{1,0:T(8,128)(2,1)S(1)}, bf16[64,256]{1,0:T(8,128)(2,1)S(1)}, u32[]{:S(2)}, u32[]{:S(2)}) collective-permute-start(bf16[64,256]{1,0:T(8,128)(2,1)S(1)} %get-tuple-element.49.w), channel_id=1, source_target_pairs={{0,2},{1,7},{2,0},{3,5},{4,6},{5,3},{6,4},{7,1},{8,10},{9,15},{10,... | collective-permute-start | bytes 98312 | tf_op jit(solution)/shard_map/ppermute | solution.py:408
  6.0 7.2 %collective-permute-start.1 = (bf16[64,256]{1,0:T(8,128)(2,1)S(1)}, bf16[64,256]{1,0:T(8,128)(2,1)S(1)}, u32[]{:S(2)}, u32[]{:S(2)}) collective-permute-start(bf16[64,256]{1,0:T(8,128)(2,1)S(1)} %get-tuple-element.49.w), channel_id=1, source_target_pairs={{0,6},{1,3},{2,4},{3,1},{4,2},{5,7},{6,0},{7,5},{8,14},{9,11},{10,... | collective-permute-start | bytes 98312 | tf_op jit(solution)/shard_map/ppermute | solution.py:408
  8.5 6.7 %collective-permute-start.2 = (bf16[64,256]{1,0:T(8,128)(2,1)S(1)}, bf16[64,256]{1,0:T(8,128)(2,1)S(1)}, u32[]{:S(2)}, u32[]{:S(2)}) collective-permute-start(bf16[64,256]{1,0:T(8,128)(2,1)S(1)} %get-tuple-element.49.w), channel_id=1, source_target_pairs={{0,4},{1,5},{2,6},{3,7},{4,0},{5,1},{6,2},{7,3},{8,12},{9,13},{10,... | collective-permute-start | bytes 98312 | tf_op jit(solution)/shard_map/ppermute | solution.py:408
  8.9 7.6 %collective-permute-start.10 = (bf16[128,384]{1,0:T(8,128)(2,1)S(1)}, bf16[128,384]{1,0:T(8,128)(2,1)S(1)}, u32[]{:S(2)}, u32[]{:S(2)}) collective-permute-start(bf16[128,384]{1,0:T(8,128)(2,1)S(1)} %get-tuple-element.55), channel_id=1, source_target_pairs={{0,2},{1,7},{2,0},{3,5},{4,6},{5,3},{6,4},{7,1},{8,10},{9,15},{10,... | collective-permute-start | bytes 294920 | tf_op jit(solution)/shard_map/ppermute | solution.py:408
  10.7 6.8 %collective-permute-start.11 = (bf16[128,384]{1,0:T(8,128)(2,1)S(1)}, bf16[128,384]{1,0:T(8,128)(2,1)S(1)}, u32[]{:S(2)}, u32[]{:S(2)}) collective-permute-start(bf16[128,384]{1,0:T(8,128)(2,1)S(1)} %get-tuple-element.56), channel_id=1, source_target_pairs={{0,6},{1,3},{2,4},{3,1},{4,2},{5,7},{6,0},{7,5},{8,14},{9,11},{10,... | collective-permute-start | bytes 294920 | tf_op jit(solution)/shard_map/ppermute | solution.py:408
  15.2 1.3 %collective-permute-start.3 = (bf16[2,64,256]{2,1,0:T(8,128)(2,1)S(1)}, bf16[2,64,256]{2,1,0:T(8,128)(2,1)S(1)}, u32[]{:S(2)}, u32[]{:S(2)}) collective-permute-start(bf16[2,64,256]{2,1,0:T(8,128)(2,1)S(1)} %get-tuple-element.51), channel_id=1, source_target_pairs={{0,1},{1,0},{2,3},{3,2},{4,5},{5,4},{6,7},{7,6},{8,9},{9,8},{10,11... | collective-permute-start | bytes 196616 | tf_op jit(solution)/shard_map/ppermute | solution.py:397
  15.2 4.9 %collective-permute-start.12 = (bf16[128,128]{1,0:T(8,128)(2,1)S(1)}, bf16[128,128]{1,0:T(8,128)(2,1)S(1)}, u32[]{:S(2)}, u32[]{:S(2)}) collective-permute-start(bf16[128,128]{1,0:T(8,128)(2,1)S(1)} %get-tuple-element.60), channel_id=1, source_target_pairs={{0,4},{1,5},{2,6},{3,7},{4,0},{5,1},{6,2},{7,3},{8,12},{9,13},{10,... | collective-permute-start | bytes 98312 | tf_op jit(solution)/shard_map/ppermute | solution.py:408
  20.8 6.4 %collective-permute-start.13 = (bf16[256,512]{1,0:T(8,128)(2,1)S(1)}, bf16[256,512]{1,0:T(8,128)(2,1)S(1)}, u32[]{:S(2)}, u32[]{:S(2)}) collective-permute-start(bf16[256,512]{1,0:T(8,128)(2,1)S(1)} %get-tuple-element.77), channel_id=1, source_target_pairs={{0,8},{1,17},{8,0},{9,25},{16,24},{17,1},{24,16},{25,9},{2,10},{3,... | collective-permute-start | bytes 786440 | tf_op jit(solution)/shard_map/ppermute | solution.py:414
  22.4 6.5 %collective-permute-start.4 = (bf16[256,256]{1,0:T(8,128)(2,1)S(1)}, bf16[256,256]{1,0:T(8,128)(2,1)S(1)}, u32[]{:S(2)}, u32[]{:S(2)}) collective-permute-start(bf16[256,256]{1,0:T(8,128)(2,1)S(1)} %w_rows.1.first.refs_4_), channel_id=1, source_target_pairs={{0,8},{1,17},{8,0},{9,25},{16,24},{17,1},{24,16},{25,9},{2,10},{3,... | collective-permute-start | bytes 393224 | tf_op jit(solution)/shard_map/ppermute | solution.py:414
  27.3 5.0 %collective-permute-start.14 = (bf16[256,256]{1,0:T(8,128)(2,1)S(1)}, bf16[256,256]{1,0:T(8,128)(2,1)S(1)}, u32[]{:S(2)}, u32[]{:S(2)}) collective-permute-start(bf16[256,256]{1,0:T(8,128)(2,1)S(1)} %get-tuple-element.79), channel_id=1, source_target_pairs={{0,16},{1,9},{8,24},{9,1},{16,0},{17,25},{24,8},{25,17},{2,18},{3,... | collective-permute-start | bytes 393224 | tf_op jit(solution)/shard_map/ppermute | solution.py:414
  28.9 8.5 %collective-permute-start.5 = (bf16[256,512]{1,0:T(8,128)(2,1)S(1)}, bf16[256,512]{1,0:T(8,128)(2,1)S(1)}, u32[]{:S(2)}, u32[]{:S(2)}) collective-permute-start(bf16[256,512]{1,0:T(8,128)(2,1)S(1)} %w_half.1.refs_0_), channel_id=1, source_target_pairs={{0,16},{1,9},{8,24},{9,1},{16,0},{17,25},{24,8},{25,17},{2,18},{3,... | collective-permute-start | bytes 786440 | tf_op jit(solution)/shard_map/ppermute | solution.py:414
  32.4 1.4 %collective-permute-start.15 = (f32[128,256]{1,0:T(8,128)S(1)}, f32[128,256]{1,0:T(8,128)S(1)}, u32[]{:S(2)}, u32[]{:S(2)}) collective-permute-start(f32[128,256]{1,0:T(8,128)S(1)} %get-tuple-element.81), channel_id=1, source_target_pairs={{0,1},{1,0},{2,3},{3,2},{4,5},{5,4},{6,7},{7,6},{8,9},{9,8},{10,11... | collective-permute-start | bytes 393224 | tf_op jit(solution)/shard_map/ppermute | solution.py:397
  33.9 5.1 %collective-permute-start.16 = (bf16[64,256]{1,0:T(8,128)(2,1)S(1)}, bf16[64,256]{1,0:T(8,128)(2,1)S(1)}, u32[]{:S(2)}, u32[]{:S(2)}) collective-permute-start(bf16[64,256]{1,0:T(8,128)(2,1)S(1)} %get-tuple-element.82), channel_id=1, source_target_pairs={{0,2},{1,7},{2,0},{3,5},{4,6},{5,3},{6,4},{7,1},{8,10},{9,15},{10,... | collective-permute-start | bytes 98312 | tf_op jit(solution)/shard_map/ppermute | solution.py:408
  33.9 5.9 %collective-permute-start.17 = (bf16[64,256]{1,0:T(8,128)(2,1)S(1)}, bf16[64,256]{1,0:T(8,128)(2,1)S(1)}, u32[]{:S(2)}, u32[]{:S(2)}) collective-permute-start(bf16[64,256]{1,0:T(8,128)(2,1)S(1)} %get-tuple-element.83), channel_id=1, source_target_pairs={{0,6},{1,3},{2,4},{3,1},{4,2},{5,7},{6,0},{7,5},{8,14},{9,11},{10,... | collective-permute-start | bytes 98312 | tf_op jit(solution)/shard_map/ppermute | solution.py:408
  35.5 5.4 %collective-permute-start.18 = (bf16[64,256]{1,0:T(8,128)(2,1)S(1)}, bf16[64,256]{1,0:T(8,128)(2,1)S(1)}, u32[]{:S(2)}, u32[]{:S(2)}) collective-permute-start(bf16[64,256]{1,0:T(8,128)(2,1)S(1)} %get-tuple-element.84), channel_id=1, source_target_pairs={{0,4},{1,5},{2,6},{3,7},{4,0},{5,1},{6,2},{7,3},{8,12},{9,13},{10,... | collective-permute-start | bytes 98312 | tf_op jit(solution)/shard_map/ppermute | solution.py:408
  41.0 9.6 %collective-permute-start.19 = (bf16[128,384]{1,0:T(8,128)(2,1)S(1)}, bf16[128,384]{1,0:T(8,128)(2,1)S(1)}, u32[]{:S(2)}, u32[]{:S(2)}) collective-permute-start(bf16[128,384]{1,0:T(8,128)(2,1)S(1)} %get-tuple-element.85), channel_id=1, source_target_pairs={{0,2},{1,7},{2,0},{3,5},{4,6},{5,3},{6,4},{7,1},{8,10},{9,15},{10,... | collective-permute-start | bytes 294920 | tf_op jit(solution)/shard_map/ppermute | solution.py:408
  41.4 9.2 %collective-permute-start.20 = (bf16[128,384]{1,0:T(8,128)(2,1)S(1)}, bf16[128,384]{1,0:T(8,128)(2,1)S(1)}, u32[]{:S(2)}, u32[]{:S(2)}) collective-permute-start(bf16[128,384]{1,0:T(8,128)(2,1)S(1)} %get-tuple-element.86), channel_id=1, source_target_pairs={{0,6},{1,3},{2,4},{3,1},{4,2},{5,7},{6,0},{7,5},{8,14},{9,11},{10,... | collective-permute-start | bytes 294920 | tf_op jit(solution)/shard_map/ppermute | solution.py:408
  43.8 4.0 %collective-permute-start.22 = (bf16[64,256]{1,0:T(8,128)(2,1)S(1)}, bf16[64,256]{1,0:T(8,128)(2,1)S(1)}, u32[]{:S(2)}, u32[]{:S(2)}) collective-permute-start(bf16[64,256]{1,0:T(8,128)(2,1)S(1)} %weight_sum.1.first), channel_id=1, source_target_pairs={{0,8},{1,17},{8,0},{9,25},{16,24},{17,1},{24,16},{25,9},{2,10},{3,... | collective-permute-start | bytes 98312 | tf_op jit(solution)/shard_map/ppermute | solution.py:414
  45.4 5.2 %collective-permute-start.21 = (bf16[128,128]{1,0:T(8,128)(2,1)S(1)}, bf16[128,128]{1,0:T(8,128)(2,1)S(1)}, u32[]{:S(2)}, u32[]{:S(2)}) collective-permute-start(bf16[128,128]{1,0:T(8,128)(2,1)S(1)} %get-tuple-element.87), channel_id=1, source_target_pairs={{0,4},{1,5},{2,6},{3,7},{4,0},{5,1},{6,2},{7,3},{8,12},{9,13},{10,... | collective-permute-start | bytes 98312 | tf_op jit(solution)/shard_map/ppermute | solution.py:408
  50.9 5.1 %collective-permute-start.23 = (bf16[128,768]{1,0:T(8,128)(2,1)S(1)}, bf16[128,768]{1,0:T(8,128)(2,1)S(1)}, u32[]{:S(2)}, u32[]{:S(2)}) collective-permute-start(bf16[128,768]{1,0:T(8,128)(2,1)S(1)} %get-tuple-element.90), channel_id=1, source_target_pairs={{0,1},{1,0},{2,3},{3,2},{4,5},{5,4},{6,7},{7,6},{8,9},{9,8},{10,11... | collective-permute-start | bytes 589832 | tf_op jit(solution)/shard_map/ppermute | solution.py:397
  51.0 4.3 %collective-permute-start.24 = (bf16[64,512]{1,0:T(8,128)(2,1)S(1)}, bf16[64,512]{1,0:T(8,128)(2,1)S(1)}, u32[]{:S(2)}, u32[]{:S(2)}) collective-permute-start(bf16[64,512]{1,0:T(8,128)(2,1)S(1)} %both.1.refs_1_), channel_id=1, source_target_pairs={{0,16},{1,9},{8,24},{9,1},{16,0},{17,25},{24,8},{25,17},{2,18},{3,... | collective-permute-start | bytes 196616 | tf_op jit(solution)/shard_map/ppermute | solution.py:414

commit v8 on v7

--- a/solution.py
+++ b/solution.py
@@ -116,7 +116,11 @@
         copy.wait()
 
 
-def state_kernel(direct, mine, q_pair, k_pair, v_pair, state, pair, to_a, to_b, *to_c):
+def state_kernel(direct, mine, q_pair, k_pair, v_pair, *refs):
+    if direct:
+        w, state, pair, to_a, to_b, to_c = refs
+    else:
+        state, pair, to_a, to_b = refs
     core, _, _ = places()
     own = core * DH
     for index, source in enumerate((q_pair, k_pair, v_pair)):
@@ -132,18 +136,22 @@
         here = block == core
         out[:, :DH] = jnp.where(here, mine[:, KS], pair[:, KS])
         out[:, DH : 2 * DH] = jnp.where(here, mine[:, VS], pair[:, VS])
-        if direct:
-            out[:, 2 * DH :] = total.astype(BF)
-    if direct:
-        to_c[0][...] = total.astype(BF)
+    if direct:
+        rows = w.shape[0]
+        for out, first in ((to_a, 2 * DH), (to_b, 2 * DH), (to_c, 0)):
+            out[:, first : first + DH] = total.astype(BF)
+            out[:rows, first + DH :] = w[:, :DH]
+            out[rows:, first + DH :] = w[:, DH:]
 
 
 def relay_kernel(w, a, b, c, keep, send, heads):
     core, z, _ = places()
     way = links(True)
+    rows = w.shape[0]
     heads[z] = w[...]
-    for source, step in ((a, way["first"]), (b, way["second"]), (c, 2)):
-        heads[z ^ step] = source[...]
+    for source, first, step in ((a, 3 * DH, way["first"]), (b, 3 * DH, way["second"]), (c, DH, 2)):
+        heads[z ^ step, :, :DH] = source[:rows, first:]
+        heads[z ^ step, :, DH:] = source[rows:, first:]
     for group in range(2):
         keep[group] = heads[2 * group + core]
         send[group] = heads[2 * group + 1 - core]
@@ -217,8 +225,9 @@
     rows = mine.shape[0]
     total = state[...]
     if direct:
-        a, b, c, soft_send, _, u_out, total_out, keep, out = refs
-        total = total + a[:, 2 * DH :].astype(F32) + b[:, 2 * DH :].astype(F32) + c[...].astype(F32)
+        a, b, c, soft_send, u_out, total_out, keep, out = refs
+        total = total + a[:, 2 * DH : 3 * DH].astype(F32) + b[:, 2 * DH : 3 * DH].astype(F32)
+        total = total + c[:, :DH].astype(F32)
     else:
         u_out, total_out, keep = refs
     total_out[...] = total
@@ -239,14 +248,15 @@
         send[rows, :] = (source[:, width:] + got[rows, width:].astype(F32)).astype(BF)
 
 
-def rows_kernel(keep, got, own, send, total):
-    core, _, _ = places()
+def piece_kernel(keep, got, *refs):
+    _, z, _ = places()
+    *outs, pieces = refs
     half = DH // 2
-    total[...] = keep[...] + got[...].astype(F32)
-    for group in range(2):
-        out = slice(group * half, (group + 1) * half)
-        own[out, :] = total[at(group * DH + core * half, half), :]
-        send[out, :] = total[at(group * DH + (1 - core) * half, half), :]
+    total = keep[...] + got[...].astype(F32)
+    for index in range(len(outs)):
+        pieces[index] = total[index * half : (index + 1) * half, :]
+    for step, out in enumerate(outs):
+        out[...] = pieces[z ^ step].astype(BF)
 
 
 def lin_backward(u, total, dattn, mine, pair, gain, dq_own, dq_pair, dstate, grads):
@@ -309,7 +319,7 @@
     way = links(direct)
     span = dk_soft.shape[0]
     if direct:
-        dstate, _, _, _, to_a, to_b, to_c = refs
+        dstate, *_, to_a, to_b, to_c = refs
         to_c[...] = dstate[...].astype(BF)
     else:
         to_a, to_b = refs
@@ -321,21 +331,8 @@
             out[:, 2 * DH :] = dstate[...].astype(BF)
 
 
-def chunk_kernel(own, got, to_a, to_b, to_c, chunk, heads):
-    core, z, _ = places()
-    way = links(True)
-    half = chunk.shape[0]
-    for group in range(2):
-        rows = slice(group * half, (group + 1) * half)
-        heads[2 * group + core] = own[rows, :]
-        heads[2 * group + 1 - core] = got[rows, :]
-    chunk[...] = heads[z]
-    for out, step in ((to_a, way["first"]), (to_b, way["second"]), (to_c, 2)):
-        out[...] = heads[z ^ step].astype(BF)
-
-
-def weight_sum_kernel(scale, chunk, a, b, c, out):
-    total = chunk[...] + a[...].astype(F32) + b[...].astype(F32) + c[...].astype(F32)
+def weight_sum_kernel(scale, a, b, c, d, out):
+    total = (a[...].astype(F32) + b[...].astype(F32)) + (c[...].astype(F32) + d[...].astype(F32))
     out[...] = (scale * total).astype(out.dtype)
 
 
@@ -407,6 +404,14 @@
                 pairs.append((2 * z + c, 2 * there + c))
         return lax.ppermute(value, axes, pairs)
 
+    def to_owner(value, step):
+        pairs = []
+        for z in range(n_z):
+            for c in range(2):
+                piece = z ^ step
+                pairs.append((2 * z + c, 2 * (2 * (piece // 2) + c) + piece % 2))
+        return lax.ppermute(value, axes, pairs)
+
     def over_dp(value, which):
         pairs = [
             (2 * d + c, 2 * (d ^ (1 + c, 2 - c)[which]) + c) for d in range(n_dp) for c in range(2)
@@ -430,29 +435,24 @@
         scratch=[pltpu.SemaphoreType.DMA((9,))],
         spaces=[pl.BlockSpec(memory_space=pltpu.HBM)] * 6,
     )
-    wide = 3 * DH if direct else 2 * DH
+    wide = 4 * DH if direct else 2 * DH
     state, pair, to_a, to_b, *rest = call(
         functools.partial(state_kernel, direct), "state",
         [like((DH, DH), F32), like((rows, 6 * DH), BF), like((rows, wide), BF), like((rows, wide), BF)]
-        + [like((DH, DH), BF)] * direct,
-        [mine, q_pair, k_pair, v_pair],
+        + [like((rows, 2 * DH), BF)] * direct,
+        [mine, q_pair, k_pair, v_pair] + [w_part] * direct,
         flops=4 * 2 * rows * DH * DH,
     )
     if direct:
         a, b, c = over_z(to_a, 0), over_z(to_b, 1), [over_z(rest[0], 2)]
         w_keep, w_send = call(
-            relay_kernel, "relay", [like((2, half, width), BF)] * 2,
-            [w_part] + [over_z(w_part, which) for which in range(3)],
+            relay_kernel, "relay", [like((2, half, width), BF)] * 2, [w_part, a, b] + c,
             scratch=[pltpu.VMEM((HEADS, half, width), BF)],
         )
         w_own = call(
             w_rows_kernel, "w_rows", [like((2 * DH, width), BF)], [w_keep, over_core(w_send)]
         )[0]
         w_got = over_dp(w_own, 0)
-        w_half = call(
-            join_kernel, "w_half", [like((2 * DH, 2 * width), BF)], [w_own, w_got]
-        )[0]
-        weights = [w_half, over_dp(w_half, 1)]
     else:
         a, b, c = over_z(to_a, 0), over_z(to_b, 1), []
         state = lax.psum(state, "z")
@@ -476,7 +476,7 @@
         functools.partial(lin_forward_kernel, direct), "lin_forward",
         [like((2 * rows, DH), F32), like((DH, DH), F32), like((DH, keep_width), F32)]
         + [like((2 * DH, 2 * width), BF)] * direct,
-        [state, mine, pair, ogs, gain] + ([a, b] + c + soft_send + [w_own] if direct else []),
+        [state, mine, pair, ogs, gain] + ([a, b] + c + soft_send if direct else []),
         flops=wg_flops,
     )
     if direct:
@@ -486,19 +486,18 @@
             [keep_soft, keep_lin, got],
         )
         got = over_dp(sent, 1)
-        row_own, row_send = call(
-            rows_kernel, "rows", [like((2 * half, width), F32)] * 2, [keep, got],
-            scratch=[pltpu.VMEM((2 * DH, width), F32)],
+        pieces = call(
+            piece_kernel, "pieces", [like((half, width), BF)] * HEADS, [keep, got],
+            scratch=[pltpu.VMEM((HEADS, half, width), F32)],
         )
-        row_recv = over_core(row_send)
-        *to_chips, chunk = call(
-            chunk_kernel, "chunk", [like((half, width), BF)] * 3 + [like((half, width), F32)],
-            [row_own, row_recv], scratch=[pltpu.VMEM((HEADS, half, width), F32)],
-        )
-        chunks = [over_z(value, which) for which, value in enumerate(to_chips)]
+        w_half = call(
+            join_kernel, "w_half", [like((2 * DH, 2 * width), BF)], [w_own, w_got, pieces[0]]
+        )[0]
+        weights = [w_half, over_dp(w_half, 1)]
+        chunks = [to_owner(value, step) for step, value in enumerate(pieces)]
         summed = call(
             functools.partial(weight_sum_kernel, scale), "weight_sum", [like((half, width), BF)],
-            [chunk] + chunks,
+            chunks,
         )[0]
         got = over_dp(summed, 0)
         both = call(join_kernel, "both", [like((half, 2 * width), BF)], [summed, got])[0]
@@ -517,6 +516,7 @@
         + [pltpu.VMEM((2 * DH, model), BF)] * direct,
         flops=5 * wg_flops,
     )
+    wide = 3 * DH if direct else 2 * DH
     to_a, to_b, *to_c = call(
         functools.partial(halo_kernel, direct), "halo",
         [like((rows, wide), BF), like((rows, wide), BF)] + [like((DH, DH), BF)] * direct,

time: 57 us -> 60.1 us (1.054)
  waiting for transfers between devices: 22.2 us -> 28 us
  starting transfers between devices: 26.8 us -> 24.2 us
    ppermute x12 -> x6, starting transfers between devices: 17.2 us -> 9.21 us  [over_z(): return lax.ppermute(value, axes, pairs)]
    ppermute x0 -> x4, starting transfers between devices: none -> 6.32 us  [to_owner(): return lax.ppermute(value, axes, pairs)]
    ppermute x0 -> x4, waiting for transfers between devices: none -> 4.15 us  [to_owner(): return lax.ppermute(value, axes, pairs)]
    ppermute x6, waiting for transfers between devices: 10.7 us -> 13.9 us  [over_dp(): return lax.ppermute(value, ('dp', 'core'), pairs)]
    ppermute x7 -> x6, waiting for transfers between devices: 2.51 us -> 0.02 us  [over_core(): return lax.ppermute(value, 'core', pair_perm)]
    ppermute x6, starting transfers between devices: 8.34 us -> 7.4 us  [over_dp(): return lax.ppermute(value, ('dp', 'core'), pairs)]
    ppermute x12 -> x6, waiting for transfers between devices: 9.03 us -> 9.91 us  [over_z(): return lax.ppermute(value, axes, pairs)]
    ppermute x7 -> x6, starting transfers between devices: 1.32 us -> 1.25 us  [over_core(): return lax.ppermute(value, 'core', pair_perm)]
  transfers between devices with their start and end apart: 25 -> 22, of which waited for: 12 -> 9; matrix products, arithmetic and copies ran while one was open for 0% -> 0% of each run, Pallas kernels for 9% -> 8%
where the time goes in v8:
time: 60.1 us; the launch traced here: 60 us
  waiting for transfers between devices  28 us (47%)
  starting transfers between devices  24.2 us (40%)
  Pallas kernels  6.99 us (12%)
  between operations  0.8 us (1%)
    ppermute x6, waiting for transfers between devices, over_dp(): return lax.ppermute(value, ('dp', 'core'), pairs)  13.9 us
    ppermute x6, waiting for transfers between devices, over_z(): return lax.ppermute(value, axes, pairs)  9.91 us
    ppermute x6, starting transfers between devices, over_z(): return lax.ppermute(value, axes, pairs)  9.21 us
    ppermute x6, starting transfers between devices, over_dp(): return lax.ppermute(value, ('dp', 'core'), pairs)  7.4 us
    pallas_call x16, Pallas kernels, call(): pl.pallas_call(kernel, name=name, out_shape=list(outs), in_specs=spaces o...  6.99 us
    ppermute x4, starting transfers between devices, to_owner(): return lax.ppermute(value, axes, pairs)  6.32 us
    ppermute x4, waiting for transfers between devices, to_owner(): return lax.ppermute(value, axes, pairs)  4.15 us
    ppermute x6, starting transfers between devices, over_core(): return lax.ppermute(value, 'core', pair_perm)  1.25 us
  transfers between devices with their start and end apart: 22, of which 9 were waited for; matrix products, arithmetic and copies ran while one was open for 0% of the time, Pallas kernels for 8%

profile of v8, /device:TPU:0, one launch (start us, length us, event | category | flops | bytes accessed | tf_op | source)
XLA Modules:
  0.0 60.0 jit_solution(12898488725868149776)
XLA Ops:
  0.6 0.5 collective-permute-start
  1.2 0.1 collective-permute-start.1
  1.2 0.4 collective-permute-start.2
  1.7 0.1 collective-permute-start.8
  1.7 1.2 %pack.1 = (bf16[128,768]{1,0:T(8,128)(2,1)S(1)}, bf16[128,1024]{1,0:T(8,128)(2,1)S(1)}, bf16[64,256]{1,0:T(8,128)(2,1)S(1)}, f32[1,128]{1,0:T(1,128)S(1)}) custom-call(bf16[1,128,512]{2,1,0:T(8,128)(2,1)} %q.1, bf16[1,128,512]{2,1,0:T(8,128)(2,1)} %k.1, bf16[1,128,512]{2,1,0:T(8,128)(2,1)} %v.1, bf16[1,128,1024]{2,1,0:T(8,128)(2,1)} %og.1, ...), custom_call_target="tpu_custom_call" | custom-call | bytes 1279488 | tf_op jit(solution)/shard_map/pack/pallas_call | solution.py:66
  2.9 0.0 collective-permute-done.q_pair
  2.9 0.0 collective-permute-done.1.k_pair
  2.9 0.0 collective-permute-done.2.v_pair
  3.0 0.3 state.1
  3.2 3.1 %collective-permute-start.3 = (bf16[128,512]{1,0:T(8,128)(2,1)S(1)}, bf16[128,512]{1,0:T(8,128)(2,1)S(1)}, u32[]{:S(2)}, u32[]{:S(2)}) collective-permute-start(bf16[128,512]{1,0:T(8,128)(2,1)S(1)} %get-tuple-element.49), channel_id=1, source_target_pairs={{0,2},{1,7},{2,0},{3,5},{4,6},{5,3},{6,4},{7,1},{8,10},{9,15},{10,... | collective-permute-start | bytes 393224 | tf_op jit(solution)/shard_map/ppermute | solution.py:405
  6.3 2.5 %collective-permute-start.4 = (bf16[128,512]{1,0:T(8,128)(2,1)S(1)}, bf16[128,512]{1,0:T(8,128)(2,1)S(1)}, u32[]{:S(2)}, u32[]{:S(2)}) collective-permute-start(bf16[128,512]{1,0:T(8,128)(2,1)S(1)} %get-tuple-element.50), channel_id=1, source_target_pairs={{0,6},{1,3},{2,4},{3,1},{4,2},{5,7},{6,0},{7,5},{8,14},{9,11},{10,... | collective-permute-start | bytes 393224 | tf_op jit(solution)/shard_map/ppermute | solution.py:405
  8.8 0.1 collective-permute-start.5
  8.9 0.4 collective-permute-done.3.a.refs_0_
  9.3 6.5 %collective-permute-done.4.b.refs_1_ = bf16[128,512]{1,0:T(8,128)(2,1)S(1)} collective-permute-done((bf16[128,512]{1,0:T(8,128)(2,1)S(1)}, bf16[128,512]{1,0:T(8,128)(2,1)S(1)}, u32[]{:S(2)}, u32[]{:S(2)}) %collective-permute-start.4) | collective-permute-done | bytes 131104 | tf_op jit(solution)/shard_map/ppermute | solution.py:405
  15.7 0.0 collective-permute-done.8.og_recv
  15.7 1.2 %soft_forward.1 = (bf16[256,128]{1,0:T(8,128)(2,1)S(1)}, bf16[512,128]{1,0:T(8,128)(2,1)S(1)}, bf16[512,128]{1,0:T(8,128)(2,1)S(1)}, bf16[256,1024]{1,0:T(8,128)...) custom-call(bf16[128,768]{1,0:T(8,128)(2,1)S(1)} %get-tuple-element., ...), custom_call_target="tpu_custom_call" | custom-call | flops 67108864 | bytes 2949120 | tf_op jit(solution)/shard_map/soft_forward/pallas_call | solution.py:66
  16.9 0.0 collective-permute-done.5.c.refs_2_
  16.9 0.7 %lin_forward.1 = (f32[256,128]{1,0:T(8,128)S(1)}, f32[128,128]{1,0:T(8,128)S(1)}, f32[128,512]{1,0:T(8,128)S(1)}, bf16[256,512]{1,0:T(8,128)(2,1)S(1)}) custom-call(f32[128,128]{1,0:T(8,128)S(1)} %get-tuple-element.57.state, bf16[128,768]{1,0:T(8,128)(2,1)S(1)} %get-tuple-element.48.mine.refs_5_, bf16[128,768]{1,0:T(8,128)(2,1)S(1)} %get-tuple-element.54.pair.refs_6_, ...), custom_call_target="tpu_custom_call" | custom-call | flops 67108864 | bytes 2163200 | tf_op jit(solution)/shard_map/lin_forward/pallas_call | solution.py:66
  17.6 1.6 %collective-permute-start.9 = (bf16[256,512]{1,0:T(8,128)(2,1)S(1)}, bf16[256,512]{1,0:T(8,128)(2,1)S(1)}, u32[]{:S(2)}, u32[]{:S(2)}) collective-permute-start(bf16[256,512]{1,0:T(8,128)(2,1)S(1)} %get-tuple-element.62), channel_id=1, source_target_pairs={{0,8},{1,17},{8,0},{9,25},{16,24},{17,1},{24,16},{25,9},{2,10},{3,... | collective-permute-start | bytes 786440 | tf_op jit(solution)/shard_map/ppermute | solution.py:419
  19.2 0.1 collective-permute-start.6
  19.3 5.4 %collective-permute-done.9.got = bf16[256,512]{1,0:T(8,128)(2,1)S(1)} collective-permute-done((bf16[256,512]{1,0:T(8,128)(2,1)S(1)}, bf16[256,512]{1,0:T(8,128)(2,1)S(1)}, u32[]{:S(2)}, u32[]{:S(2)}) %collective-permute-start.9) | collective-permute-done | bytes 262176 | tf_op jit(solution)/shard_map/ppermute | solution.py:419
  24.7 0.1 fold.1
  24.8 1.6 %collective-permute-start.10 = (bf16[256,256]{1,0:T(8,128)(2,1)S(1)}, bf16[256,256]{1,0:T(8,128)(2,1)S(1)}, u32[]{:S(2)}, u32[]{:S(2)}) collective-permute-start(bf16[256,256]{1,0:T(8,128)(2,1)S(1)} %get-tuple-element.64), channel_id=1, source_target_pairs={{0,16},{1,9},{8,24},{9,1},{16,0},{17,25},{24,8},{25,17},{2,18},{3,... | collective-permute-start | bytes 393224 | tf_op jit(solution)/shard_map/ppermute | solution.py:419
  26.3 0.0 collective-permute-done.6.got
  26.4 1.6 %collective-permute-start.7 = (bf16[256,256]{1,0:T(8,128)(2,1)S(1)}, bf16[256,256]{1,0:T(8,128)(2,1)S(1)}, u32[]{:S(2)}, u32[]{:S(2)}) collective-permute-start(bf16[256,256]{1,0:T(8,128)(2,1)S(1)} %w_rows.1.first), channel_id=1, source_target_pairs={{0,8},{1,17},{8,0},{9,25},{16,24},{17,1},{24,16},{25,9},{2,10},{3,... | collective-permute-start | bytes 393224 | tf_op jit(solution)/shard_map/ppermute | solution.py:419
  28.0 1.9 %collective-permute-done.10.got = bf16[256,256]{1,0:T(8,128)(2,1)S(1)} collective-permute-done((bf16[256,256]{1,0:T(8,128)(2,1)S(1)}, bf16[256,256]{1,0:T(8,128)(2,1)S(1)}, u32[]{:S(2)}, u32[]{:S(2)}) %collective-permute-start.10) | collective-permute-done | bytes 131104 | tf_op jit(solution)/shard_map/ppermute | solution.py:419
  29.8 2.9 %collective-permute-done.7.second = bf16[256,256]{1,0:T(8,128)(2,1)S(1)} collective-permute-done((bf16[256,256]{1,0:T(8,128)(2,1)S(1)}, bf16[256,256]{1,0:T(8,128)(2,1)S(1)}, u32[]{:S(2)}, u32[]{:S(2)}) %collective-permute-start.7) | collective-permute-done | bytes 131104 | tf_op jit(solution)/shard_map/ppermute | solution.py:419
  32.8 0.5 collective-permute-start.11
  33.3 0.7 %collective-permute-start.12 = (bf16[64,256]{1,0:T(8,128)(2,1)S(1)}, bf16[64,256]{1,0:T(8,128)(2,1)S(1)}, u32[]{:S(2)}, u32[]{:S(2)}) collective-permute-start(bf16[64,256]{1,0:T(8,128)(2,1)S(1)} %get-tuple-element.65.refs_0_), channel_id=1, source_target_pairs={{0,0},{1,2},{2,1},{3,3},{4,4},{5,6},{6,5},{7,7},{8,8},{9,10},{10,9... | collective-permute-start | bytes 98312 | tf_op jit(solution)/shard_map/ppermute | solution.py:413
  34.0 0.2 collective-permute-start.13
  34.2 5.4 %collective-permute-start.14 = (bf16[64,256]{1,0:T(8,128)(2,1)S(1)}, bf16[64,256]{1,0:T(8,128)(2,1)S(1)}, u32[]{:S(2)}, u32[]{:S(2)}) collective-permute-start(bf16[64,256]{1,0:T(8,128)(2,1)S(1)} %get-tuple-element.80), channel_id=1, source_target_pairs={{0,4},{1,6},{2,5},{3,7},{4,0},{5,2},{6,1},{7,3},{8,12},{9,14},{10,... | collective-permute-start | bytes 98312 | tf_op jit(solution)/shard_map/ppermute | solution.py:413
  39.7 0.0 collective-permute-start.15
  39.7 0.0 collective-permute-done.11.refs_1_
  39.7 1.5 %backward.1 = (bf16[128,128]{1,0:T(8,128)(2,1)S(1)}, bf16[128,128]{1,0:T(8,128)(2,1)S(1)}, f32[128,128]{1,0:T(8,128)S(1)}, f32[256,128]{1,0:T(8,128)S(1)}, f32[5...) custom-call(bf16[256,512]{1,0:T(8,128)(2,1)S(1)} %w_half.1.refs_0_, bf16[256,512]{1,0:T(8,128)(2,1)S(1)} %collective-permute-done.11.refs_1_, ...), custom_call_target="tpu_custom_call" | custom-call | flops 335544320 | bytes 3277312 | tf_op jit(solution)/shard_map/backward/pallas_call | solution.py:66
  41.2 0.0 collective-permute-done.12.refs_1_.a
  41.2 0.0 collective-permute-done.13.refs_2_.b
  41.2 0.7 %collective-permute-done.14.refs_3_.c = bf16[64,256]{1,0:T(8,128)(2,1)S(1)} collective-permute-done((bf16[64,256]{1,0:T(8,128)(2,1)S(1)}, bf16[64,256]{1,0:T(8,128)(2,1)S(1)}, u32[]{:S(2)}, u32[]{:S(2)}) %collective-permute-start.14) | collective-permute-done | bytes 32800 | tf_op jit(solution)/shard_map/ppermute | solution.py:413
  41.9 3.4 %collective-permute-done.15.refs_4_.d = bf16[64,256]{1,0:T(8,128)(2,1)S(1)} collective-permute-done((bf16[64,256]{1,0:T(8,128)(2,1)S(1)}, bf16[64,256]{1,0:T(8,128)(2,1)S(1)}, u32[]{:S(2)}, u32[]{:S(2)}) %collective-permute-start.15) | collective-permute-done | bytes 32800 | tf_op jit(solution)/shard_map/ppermute | solution.py:413
  45.4 0.1 collective-permute-start.16
  45.5 1.1 %collective-permute-start.17 = (bf16[128,384]{1,0:T(8,128)(2,1)S(1)}, bf16[128,384]{1,0:T(8,128)(2,1)S(1)}, u32[]{:S(2)}, u32[]{:S(2)}) collective-permute-start(bf16[128,384]{1,0:T(8,128)(2,1)S(1)} %get-tuple-element.83), channel_id=1, source_target_pairs={{0,6},{1,3},{2,4},{3,1},{4,2},{5,7},{6,0},{7,5},{8,14},{9,11},{10,... | collective-permute-start | bytes 294920 | tf_op jit(solution)/shard_map/ppermute | solution.py:405
  46.6 1.6 %collective-permute-start.19 = (bf16[64,256]{1,0:T(8,128)(2,1)S(1)}, bf16[64,256]{1,0:T(8,128)(2,1)S(1)}, u32[]{:S(2)}, u32[]{:S(2)}) collective-permute-start(bf16[64,256]{1,0:T(8,128)(2,1)S(1)} %weight_sum.1.first), channel_id=1, source_target_pairs={{0,8},{1,17},{8,0},{9,25},{16,24},{17,1},{24,16},{25,9},{2,10},{3,... | collective-permute-start | bytes 98312 | tf_op jit(solution)/shard_map/ppermute | solution.py:419
  48.2 2.4 %collective-permute-start.18 = (bf16[128,128]{1,0:T(8,128)(2,1)S(1)}, bf16[128,128]{1,0:T(8,128)(2,1)S(1)}, u32[]{:S(2)}, u32[]{:S(2)}) collective-permute-start(bf16[128,128]{1,0:T(8,128)(2,1)S(1)} %get-tuple-element.84), channel_id=1, source_target_pairs={{0,4},{1,5},{2,6},{3,7},{4,0},{5,1},{6,2},{7,3},{8,12},{9,13},{10,... | collective-permute-start | bytes 98312 | tf_op jit(solution)/shard_map/ppermute | solution.py:405
  50.6 0.0 collective-permute-done.19.second
  50.6 3.1 %collective-permute-done.18.refs_0_ = bf16[128,128]{1,0:T(8,128)(2,1)S(1)} collective-permute-done((bf16[128,128]{1,0:T(8,128)(2,1)S(1)}, bf16[128,128]{1,0:T(8,128)(2,1)S(1)}, u32[]{:S(2)}, u32[]{:S(2)}) %collective-permute-start.18) | collective-permute-done | bytes 32800 | tf_op jit(solution)/shard_map/ppermute | solution.py:405
  53.7 0.0 collective-permute-done.16.a
  53.7 0.0 collective-permute-done.17.b
  53.7 0.4 final.1
  54.0 0.1 collective-permute-start.20
  54.1 0.6 collective-permute-start.21
  54.7 3.7 %collective-permute-done.21.got = bf16[64,512]{1,0:T(8,128)(2,1)S(1)} collective-permute-done((bf16[64,512]{1,0:T(8,128)(2,1)S(1)}, bf16[64,512]{1,0:T(8,128)(2,1)S(1)}, u32[]{:S(2)}, u32[]{:S(2)}) %collective-permute-start.21) | collective-permute-done | bytes 65568 | tf_op jit(solution)/shard_map/ppermute | solution.py:419
  58.4 0.7 %weight_join.1 = f32[64,1024]{1,0:T(8,128)} custom-call(bf16[64,512]{1,0:T(8,128)(2,1)S(1)} %both.1.refs_1_, bf16[64,512]{1,0:T(8,128)(2,1)S(1)} %collective-permute-done.21.got), custom_call_target="tpu_custom_call" | custom-call | bytes 393216 | tf_op jit(solution)/shard_map/weight_join/pallas_call | solution.py:66
  59.2 0.0 collective-permute-done.20.pair
  59.2 0.8 %outputs.1 = (bf16[1,128,512]{2,1,0:T(8,128)(2,1)}, bf16[1,128,512]{2,1,0:T(8,128)(2,1)}, bf16[1,128,512]{2,1,0:T(8,128)(2,1)}) custom-call(bf16[128,768]{1,0:T(8,128)(2,1)S(1)} %get-tuple-element.85.own, bf16[128,768]{1,0:T(8,128)(2,1)S(1)} %collective-permute-done.20.pair), custom_call_target="tpu_custom_call" | custom-call | bytes 786432 | tf_op jit(solution)/shard_map/outputs/pallas_call | solution.py:66
  (7 shorter events, 0.2 us)
Async XLA Ops:
  0.6 2.3 %collective-permute-start = (bf16[1,128,512]{2,1,0:T(8,128)(2,1)}, bf16[1,128,512]{2,1,0:T(8,128)(2,1)S(1)}, u32[]{:S(2)}, u32[]{:S(2)}) collective-permute-start(bf16[1,128,512]{2,1,0:T(8,128)(2,1)} %q.1), channel_id=1, source_target_pairs={{0,1},{1,0},{2,3},{3,2},{4,5},{5,4},{6,7},{7,6},{8,9},{9,8},{10,11... | collective-permute-start | bytes 393224 | tf_op jit(solution)/shard_map/ppermute | solution.py:394
  1.2 1.8 %collective-permute-start.1 = (bf16[1,128,512]{2,1,0:T(8,128)(2,1)}, bf16[1,128,512]{2,1,0:T(8,128)(2,1)S(1)}, u32[]{:S(2)}, u32[]{:S(2)}) collective-permute-start(bf16[1,128,512]{2,1,0:T(8,128)(2,1)} %k.1), channel_id=1, source_target_pairs={{0,1},{1,0},{2,3},{3,2},{4,5},{5,4},{6,7},{7,6},{8,9},{9,8},{10,11... | collective-permute-start | bytes 393224 | tf_op jit(solution)/shard_map/ppermute | solution.py:394
  1.2 1.7 %collective-permute-start.2 = (bf16[1,128,512]{2,1,0:T(8,128)(2,1)}, bf16[1,128,512]{2,1,0:T(8,128)(2,1)S(1)}, u32[]{:S(2)}, u32[]{:S(2)}) collective-permute-start(bf16[1,128,512]{2,1,0:T(8,128)(2,1)} %v.1), channel_id=1, source_target_pairs={{0,1},{1,0},{2,3},{3,2},{4,5},{5,4},{6,7},{7,6},{8,9},{9,8},{10,11... | collective-permute-start | bytes 393224 | tf_op jit(solution)/shard_map/ppermute | solution.py:394
  1.7 14.1 %collective-permute-start.8 = (bf16[128,1024]{1,0:T(8,128)(2,1)}, bf16[128,1024]{1,0:T(8,128)(2,1)S(1)}, u32[]{:S(2)}, u32[]{:S(2)}) collective-permute-start(bf16[128,1024]{1,0:T(8,128)(2,1)} %bitcast.1), channel_id=1, source_target_pairs={{0,1},{1,0},{2,3},{3,2},{4,5},{5,4},{6,7},{7,6},{8,9},{9,8},{10,11... | collective-permute-start | bytes 786440 | tf_op jit(solution)/shard_map/ppermute | solution.py:394
  3.2 6.0 %collective-permute-start.3 = (bf16[128,512]{1,0:T(8,128)(2,1)S(1)}, bf16[128,512]{1,0:T(8,128)(2,1)S(1)}, u32[]{:S(2)}, u32[]{:S(2)}) collective-permute-start(bf16[128,512]{1,0:T(8,128)(2,1)S(1)} %get-tuple-element.49), channel_id=1, source_target_pairs={{0,2},{1,7},{2,0},{3,5},{4,6},{5,3},{6,4},{7,1},{8,10},{9,15},{10,... | collective-permute-start | bytes 393224 | tf_op jit(solution)/shard_map/ppermute | solution.py:405
  6.3 9.4 %collective-permute-start.4 = (bf16[128,512]{1,0:T(8,128)(2,1)S(1)}, bf16[128,512]{1,0:T(8,128)(2,1)S(1)}, u32[]{:S(2)}, u32[]{:S(2)}) collective-permute-start(bf16[128,512]{1,0:T(8,128)(2,1)S(1)} %get-tuple-element.50), channel_id=1, source_target_pairs={{0,6},{1,3},{2,4},{3,1},{4,2},{5,7},{6,0},{7,5},{8,14},{9,11},{10,... | collective-permute-start | bytes 393224 | tf_op jit(solution)/shard_map/ppermute | solution.py:405
  8.8 8.2 %collective-permute-start.5 = (bf16[128,256]{1,0:T(8,128)(2,1)S(1)}, bf16[128,256]{1,0:T(8,128)(2,1)S(1)}, u32[]{:S(2)}, u32[]{:S(2)}) collective-permute-start(bf16[128,256]{1,0:T(8,128)(2,1)S(1)} %get-tuple-element.51), channel_id=1, source_target_pairs={{0,4},{1,5},{2,6},{3,7},{4,0},{5,1},{6,2},{7,3},{8,12},{9,13},{10,... | collective-permute-start | bytes 196616 | tf_op jit(solution)/shard_map/ppermute | solution.py:405
  17.6 7.1 %collective-permute-start.9 = (bf16[256,512]{1,0:T(8,128)(2,1)S(1)}, bf16[256,512]{1,0:T(8,128)(2,1)S(1)}, u32[]{:S(2)}, u32[]{:S(2)}) collective-permute-start(bf16[256,512]{1,0:T(8,128)(2,1)S(1)} %get-tuple-element.62), channel_id=1, source_target_pairs={{0,8},{1,17},{8,0},{9,25},{16,24},{17,1},{24,16},{25,9},{2,10},{3,... | collective-permute-start | bytes 786440 | tf_op jit(solution)/shard_map/ppermute | solution.py:419
  19.2 7.1 %collective-permute-start.6 = (bf16[2,64,256]{2,1,0:T(8,128)(2,1)S(1)}, bf16[2,64,256]{2,1,0:T(8,128)(2,1)S(1)}, u32[]{:S(2)}, u32[]{:S(2)}) collective-permute-start(bf16[2,64,256]{2,1,0:T(8,128)(2,1)S(1)} %get-tuple-element.53), channel_id=1, source_target_pairs={{0,1},{1,0},{2,3},{3,2},{4,5},{5,4},{6,7},{7,6},{8,9},{9,8},{10,11... | collective-permute-start | bytes 196616 | tf_op jit(solution)/shard_map/ppermute | solution.py:394
  24.8 5.0 %collective-permute-start.10 = (bf16[256,256]{1,0:T(8,128)(2,1)S(1)}, bf16[256,256]{1,0:T(8,128)(2,1)S(1)}, u32[]{:S(2)}, u32[]{:S(2)}) collective-permute-start(bf16[256,256]{1,0:T(8,128)(2,1)S(1)} %get-tuple-element.64), channel_id=1, source_target_pairs={{0,16},{1,9},{8,24},{9,1},{16,0},{17,25},{24,8},{25,17},{2,18},{3,... | collective-permute-start | bytes 393224 | tf_op jit(solution)/shard_map/ppermute | solution.py:419
  26.4 6.4 %collective-permute-start.7 = (bf16[256,256]{1,0:T(8,128)(2,1)S(1)}, bf16[256,256]{1,0:T(8,128)(2,1)S(1)}, u32[]{:S(2)}, u32[]{:S(2)}) collective-permute-start(bf16[256,256]{1,0:T(8,128)(2,1)S(1)} %w_rows.1.first), channel_id=1, source_target_pairs={{0,8},{1,17},{8,0},{9,25},{16,24},{17,1},{24,16},{25,9},{2,10},{3,... | collective-permute-start | bytes 393224 | tf_op jit(solution)/shard_map/ppermute | solution.py:419
  32.8 6.8 %collective-permute-start.11 = (bf16[256,512]{1,0:T(8,128)(2,1)S(1)}, bf16[256,512]{1,0:T(8,128)(2,1)S(1)}, u32[]{:S(2)}, u32[]{:S(2)}) collective-permute-start(bf16[256,512]{1,0:T(8,128)(2,1)S(1)} %w_half.1.refs_0_), channel_id=1, source_target_pairs={{0,16},{1,9},{8,24},{9,1},{16,0},{17,25},{24,8},{25,17},{2,18},{3,... | collective-permute-start | bytes 786440 | tf_op jit(solution)/shard_map/ppermute | solution.py:419
  33.3 7.9 %collective-permute-start.12 = (bf16[64,256]{1,0:T(8,128)(2,1)S(1)}, bf16[64,256]{1,0:T(8,128)(2,1)S(1)}, u32[]{:S(2)}, u32[]{:S(2)}) collective-permute-start(bf16[64,256]{1,0:T(8,128)(2,1)S(1)} %get-tuple-element.65.refs_0_), channel_id=1, source_target_pairs={{0,0},{1,2},{2,1},{3,3},{4,4},{5,6},{6,5},{7,7},{8,8},{9,10},{10,9... | collective-permute-start | bytes 98312 | tf_op jit(solution)/shard_map/ppermute | solution.py:413
  34.0 7.2 %collective-permute-start.13 = (bf16[64,256]{1,0:T(8,128)(2,1)S(1)}, bf16[64,256]{1,0:T(8,128)(2,1)S(1)}, u32[]{:S(2)}, u32[]{:S(2)}) collective-permute-start(bf16[64,256]{1,0:T(8,128)(2,1)S(1)} %get-tuple-element.79), channel_id=1, source_target_pairs={{0,1},{1,3},{2,0},{3,2},{4,5},{5,7},{6,4},{7,6},{8,9},{9,11},{10,8... | collective-permute-start | bytes 98312 | tf_op jit(solution)/shard_map/ppermute | solution.py:413
  34.2 7.7 %collective-permute-start.14 = (bf16[64,256]{1,0:T(8,128)(2,1)S(1)}, bf16[64,256]{1,0:T(8,128)(2,1)S(1)}, u32[]{:S(2)}, u32[]{:S(2)}) collective-permute-start(bf16[64,256]{1,0:T(8,128)(2,1)S(1)} %get-tuple-element.80), channel_id=1, source_target_pairs={{0,4},{1,6},{2,5},{3,7},{4,0},{5,2},{6,1},{7,3},{8,12},{9,14},{10,... | collective-permute-start | bytes 98312 | tf_op jit(solution)/shard_map/ppermute | solution.py:413
  39.7 5.7 %collective-permute-start.15 = (bf16[64,256]{1,0:T(8,128)(2,1)S(1)}, bf16[64,256]{1,0:T(8,128)(2,1)S(1)}, u32[]{:S(2)}, u32[]{:S(2)}) collective-permute-start(bf16[64,256]{1,0:T(8,128)(2,1)S(1)} %get-tuple-element.81), channel_id=1, source_target_pairs={{0,5},{1,7},{2,4},{3,6},{4,1},{5,3},{6,0},{7,2},{8,13},{9,15},{10,... | collective-permute-start | bytes 98312 | tf_op jit(solution)/shard_map/ppermute | solution.py:413
  45.4 8.3 %collective-permute-start.16 = (bf16[128,384]{1,0:T(8,128)(2,1)S(1)}, bf16[128,384]{1,0:T(8,128)(2,1)S(1)}, u32[]{:S(2)}, u32[]{:S(2)}) collective-permute-start(bf16[128,384]{1,0:T(8,128)(2,1)S(1)} %get-tuple-element.82), channel_id=1, source_target_pairs={{0,2},{1,7},{2,0},{3,5},{4,6},{5,3},{6,4},{7,1},{8,10},{9,15},{10,... | collective-permute-start | bytes 294920 | tf_op jit(solution)/shard_map/ppermute | solution.py:405
  45.5 8.2 %collective-permute-start.17 = (bf16[128,384]{1,0:T(8,128)(2,1)S(1)}, bf16[128,384]{1,0:T(8,128)(2,1)S(1)}, u32[]{:S(2)}, u32[]{:S(2)}) collective-permute-start(bf16[128,384]{1,0:T(8,128)(2,1)S(1)} %get-tuple-element.83), channel_id=1, source_target_pairs={{0,6},{1,3},{2,4},{3,1},{4,2},{5,7},{6,0},{7,5},{8,14},{9,11},{10,... | collective-permute-start | bytes 294920 | tf_op jit(solution)/shard_map/ppermute | solution.py:405
  46.6 4.0 %collective-permute-start.19 = (bf16[64,256]{1,0:T(8,128)(2,1)S(1)}, bf16[64,256]{1,0:T(8,128)(2,1)S(1)}, u32[]{:S(2)}, u32[]{:S(2)}) collective-permute-start(bf16[64,256]{1,0:T(8,128)(2,1)S(1)} %weight_sum.1.first), channel_id=1, source_target_pairs={{0,8},{1,17},{8,0},{9,25},{16,24},{17,1},{24,16},{25,9},{2,10},{3,... | collective-permute-start | bytes 98312 | tf_op jit(solution)/shard_map/ppermute | solution.py:419
  48.2 5.5 %collective-permute-start.18 = (bf16[128,128]{1,0:T(8,128)(2,1)S(1)}, bf16[128,128]{1,0:T(8,128)(2,1)S(1)}, u32[]{:S(2)}, u32[]{:S(2)}) collective-permute-start(bf16[128,128]{1,0:T(8,128)(2,1)S(1)} %get-tuple-element.84), channel_id=1, source_target_pairs={{0,4},{1,5},{2,6},{3,7},{4,0},{5,1},{6,2},{7,3},{8,12},{9,13},{10,... | collective-permute-start | bytes 98312 | tf_op jit(solution)/shard_map/ppermute | solution.py:405
  54.0 5.1 %collective-permute-start.20 = (bf16[128,768]{1,0:T(8,128)(2,1)S(1)}, bf16[128,768]{1,0:T(8,128)(2,1)S(1)}, u32[]{:S(2)}, u32[]{:S(2)}) collective-permute-start(bf16[128,768]{1,0:T(8,128)(2,1)S(1)} %get-tuple-element.86), channel_id=1, source_target_pairs={{0,1},{1,0},{2,3},{3,2},{4,5},{5,4},{6,7},{7,6},{8,9},{9,8},{10,11... | collective-permute-start | bytes 589832 | tf_op jit(solution)/shard_map/ppermute | solution.py:394
  54.1 4.3 %collective-permute-start.21 = (bf16[64,512]{1,0:T(8,128)(2,1)S(1)}, bf16[64,512]{1,0:T(8,128)(2,1)S(1)}, u32[]{:S(2)}, u32[]{:S(2)}) collective-permute-start(bf16[64,512]{1,0:T(8,128)(2,1)S(1)} %both.1.refs_1_), channel_id=1, source_target_pairs={{0,16},{1,9},{8,24},{9,1},{16,0},{17,25},{24,8},{25,17},{2,18},{3,... | collective-permute-start | bytes 196616 | tf_op jit(solution)/shard_map/ppermute | solution.py:419

commit v9 on v5

--- a/solution.py
+++ b/solution.py
@@ -94,9 +94,9 @@
     )
 
 
-def pack_kernel(q, k, v, og, w, gain, mine_out, other_out, og_out, w_out, gain_out, sems):
+def pack_kernel(q, k, v, og, w, gain, mine_out, og_out, w_out, gain_out, sems):
     core, _, dp = places()
-    mine, other = core * DH, (1 - core) * DH
+    mine = core * DH
     copies = []
 
     def fetch(source, target):
@@ -107,7 +107,6 @@
     for index, array in enumerate((q, k, v)):
         for group in range(2):
             cols = slice((3 * group + index) * DH, (3 * group + index + 1) * DH)
-            fetch(array.at[0, :, at(SOFT * group + other)], other_out.at[:, cols])
             fetch(array.at[0, :, at(SOFT * group + mine)], mine_out.at[:, cols])
     width = w_out.shape[1]
     fetch(w.at[:, at(dp * width, width)], w_out)
@@ -117,15 +116,20 @@
         copy.wait()
 
 
-def state_kernel(direct, mine, pair, *refs):
-    core, _, _ = places()
+def state_kernel(direct, mine, q_pair, k_pair, v_pair, *refs):
+    if direct:
+        w, state, pair, to_a, to_b, to_c = refs
+    else:
+        state, pair, to_a, to_b = refs
+    core, _, _ = places()
+    own = core * DH
+    for index, source in enumerate((q_pair, k_pair, v_pair)):
+        for group in range(2):
+            first = (3 * group + index) * DH
+            pair[:, first : first + DH] = source[0, :, at(SOFT * group + own)]
     total = mm2(unit_plus(mine[:, KL].astype(F32)), mine[:, VL], TN) + mm2(
         unit_plus(pair[:, KL].astype(F32)), pair[:, VL], TN
     )
-    if direct:
-        w, state, to_a, to_b, to_c = refs
-    else:
-        state, to_a, to_b = refs
     state[...] = total
     way = links(direct)
     for out, block in ((to_a, way["block_a"]), (to_b, way["block_b"])):
@@ -314,7 +318,7 @@
     way = links(direct)
     span = dk_soft.shape[0]
     if direct:
-        dstate, _, to_a, to_b, to_c = refs
+        dstate, *_, to_a, to_b, to_c = refs
         to_c[...] = dstate[...].astype(BF)
     else:
         to_a, to_b = refs
@@ -423,24 +427,24 @@
     def hbm(value):
         return pltpu.with_memory_space_constraint(value, pltpu.HBM)
 
-    mine, other, og, w_part, gain = call(
+    q_pair, k_pair, v_pair = over_core(queries), over_core(key_rows), over_core(value_rows)
+    og_recv = over_core(out_grad[0])
+    mine, og, w_part, gain = call(
         pack_kernel, "pack",
         [
-            like((rows, 6 * DH), BF), like((rows, 6 * DH), BF), like((rows, model), BF),
+            like((rows, 6 * DH), BF), like((rows, model), BF),
             like((out_weight.shape[0], width), BF), like((1, DH), F32),
         ],
         [hbm(x) for x in (queries, key_rows, value_rows, out_grad, out_weight, norm_gain)],
-        scratch=[pltpu.SemaphoreType.DMA((16,))],
+        scratch=[pltpu.SemaphoreType.DMA((9,))],
         spaces=[pl.BlockSpec(memory_space=pltpu.HBM)] * 6,
     )
-    pair = over_core(other)
-    og_recv = over_core(og)
     wide = 4 * DH if direct else 2 * DH
-    state, to_a, to_b, *rest = call(
+    state, pair, to_a, to_b, *rest = call(
         functools.partial(state_kernel, direct), "state",
-        [like((DH, DH), F32), like((rows, wide), BF), like((rows, wide), BF)]
+        [like((DH, DH), F32), like((rows, 6 * DH), BF), like((rows, wide), BF), like((rows, wide), BF)]
         + [like((rows, 2 * DH), BF)] * direct,
-        [mine, pair] + [w_part] * direct,
+        [mine, q_pair, k_pair, v_pair] + [w_part] * direct,
         flops=4 * 2 * rows * DH * DH,
     )
     if direct:
@@ -506,9 +510,9 @@
         )[0]
         got = over_dp(summed, 0)
         both = call(join_kernel, "both", [like((half, 2 * width), BF)], [summed, got])[0]
-        got = over_dp(both, 1)
+        gathered = over_dp(both, 1)
         weight_grad = call(
-            weight_join_kernel, "weight_join", [like((half, model), F32)], [both, got]
+            weight_join_kernel, "weight_join", [like((half, model), F32)], [both, gathered]
         )[0]
     if direct:
         weights.append(chunk)
@@ -527,7 +531,7 @@
     to_a, to_b, *to_c = call(
         functools.partial(halo_kernel, direct), "halo",
         [like((rows, wide), BF), like((rows, wide), BF)] + [like((DH, DH), BF)] * direct,
-        [dk_soft, dv_soft] + ([dstate, summed] if direct else []),
+        [dk_soft, dv_soft] + ([dstate] + chunks if direct else []),
     )
     a, b = over_z(to_a, 0, True), over_z(to_b, 1, True)
     c = [over_z(value, 2) for value in to_c]
@@ -543,9 +547,8 @@
         functools.partial(final_kernel, direct), "final",
         [like((rows, 6 * DH), BF), like((rows, 6 * DH), BF)],
         [dstate, mine, pair, dq_soft, dk_soft, dv_soft, dq_lin, dq_lin_pair, a, b] + c
-        + ([hbm(weight_grad)] if direct else []),
+        + ([gathered] if direct else []),
         scratch=[pltpu.VMEM((2 * rows, DH), F32)] * 2,
-        spaces=[vmem] * 11 + [pl.BlockSpec(memory_space=pltpu.HBM)] if direct else None,
         flops=wg_flops // 4,
     )
     from_pair = over_core(to_pair)

time: 54.5 us -> 53.7 us (0.985)
  waiting for transfers between devices: 22.5 us -> 21.4 us
    ppermute x5 -> x7, waiting for transfers between devices: 5 us -> 3.28 us  [over_core(): return lax.ppermute(value, 'core', pair_perm)]
    ppermute x9, waiting for transfers between devices: 12.2 us -> 13.3 us  [over_z(): return lax.ppermute(value, axes, pairs)]
    ppermute x5 -> x7, starting transfers between devices: 0.81 us -> 1.32 us  [over_core(): return lax.ppermute(value, 'core', pair_perm)]
  transfers between devices with their start and end apart: 20 -> 22, of which waited for: 14 -> 12; matrix products, arithmetic and copies ran while one was open for 0% -> 0% of each run, Pallas kernels for 7% -> 10%
where the time goes in v9:
time: 53.7 us; the launch traced here: 53.6 us
  starting transfers between devices  24.3 us (45%)
  waiting for transfers between devices  21.4 us (40%)
  Pallas kernels  7.06 us (13%)
  between operations  0.79 us (1%)
    ppermute x9, waiting for transfers between devices, over_z(): return lax.ppermute(value, axes, pairs)  13.3 us
    ppermute x9, starting transfers between devices, over_z(): return lax.ppermute(value, axes, pairs)  12.7 us
    ppermute x6, starting transfers between devices, over_dp(): return lax.ppermute(value, ('dp', 'core'), pairs)  10.3 us
    pallas_call x17, Pallas kernels, call(): pl.pallas_call(kernel, name=name, out_shape=list(outs), in_specs=spaces o...  7.06 us
    ppermute x6, waiting for transfers between devices, over_dp(): return lax.ppermute(value, ('dp', 'core'), pairs)  4.85 us
    ppermute x7, waiting for transfers between devices, over_core(): return lax.ppermute(value, 'core', pair_perm)  3.28 us
    ppermute x7, starting transfers between devices, over_core(): return lax.ppermute(value, 'core', pair_perm)  1.32 us
  transfers between devices with their start and end apart: 22, of which 12 were waited for; matrix products, arithmetic and copies ran while one was open for 0% of the time, Pallas kernels for 10%

profile of v9, /device:TPU:0, one launch (start us, length us, event | category | flops | bytes accessed | tf_op | source)
XLA Modules:
  0.0 53.6 jit_solution(2728909165522441090)
XLA Ops:
  0.6 0.5 collective-permute-start
  1.2 0.1 collective-permute-start.1
  1.2 0.4 collective-permute-start.2
  1.7 0.1 collective-permute-start.8
  1.7 1.2 %pack.1 = (bf16[128,768]{1,0:T(8,128)(2,1)S(1)}, bf16[128,1024]{1,0:T(8,128)(2,1)S(1)}, bf16[64,256]{1,0:T(8,128)(2,1)S(1)}, f32[1,128]{1,0:T(1,128)S(1)}) custom-call(bf16[1,128,512]{2,1,0:T(8,128)(2,1)} %q.1, bf16[1,128,512]{2,1,0:T(8,128)(2,1)} %k.1, bf16[1,128,512]{2,1,0:T(8,128)(2,1)} %v.1, bf16[1,128,1024]{2,1,0:T(8,128)(2,1)} %og.1, ...), custom_call_target="tpu_custom_call" | custom-call | bytes 1279488 | tf_op jit(solution)/shard_map/pack/pallas_call | solution.py:66
  2.9 0.0 collective-permute-done.q_pair
  2.9 0.0 collective-permute-done.1.k_pair
  2.9 0.0 collective-permute-done.2.v_pair
  3.0 0.3 state.1
  3.2 3.1 %collective-permute-start.3 = (bf16[128,512]{1,0:T(8,128)(2,1)S(1)}, bf16[128,512]{1,0:T(8,128)(2,1)S(1)}, u32[]{:S(2)}, u32[]{:S(2)}) collective-permute-start(bf16[128,512]{1,0:T(8,128)(2,1)S(1)} %get-tuple-element.51), channel_id=1, source_target_pairs={{0,2},{1,7},{2,0},{3,5},{4,6},{5,3},{6,4},{7,1},{8,10},{9,15},{10,... | collective-permute-start | bytes 393224 | tf_op jit(solution)/shard_map/ppermute | solution.py:417
  6.3 2.5 %collective-permute-start.4 = (bf16[128,512]{1,0:T(8,128)(2,1)S(1)}, bf16[128,512]{1,0:T(8,128)(2,1)S(1)}, u32[]{:S(2)}, u32[]{:S(2)}) collective-permute-start(bf16[128,512]{1,0:T(8,128)(2,1)S(1)} %get-tuple-element.52), channel_id=1, source_target_pairs={{0,6},{1,3},{2,4},{3,1},{4,2},{5,7},{6,0},{7,5},{8,14},{9,11},{10,... | collective-permute-start | bytes 393224 | tf_op jit(solution)/shard_map/ppermute | solution.py:417
  8.8 0.1 collective-permute-start.5
  8.9 0.4 collective-permute-done.3.a.refs_0_
  9.3 6.5 %collective-permute-done.4.b.refs_1_ = bf16[128,512]{1,0:T(8,128)(2,1)S(1)} collective-permute-done((bf16[128,512]{1,0:T(8,128)(2,1)S(1)}, bf16[128,512]{1,0:T(8,128)(2,1)S(1)}, u32[]{:S(2)}, u32[]{:S(2)}) %collective-permute-start.4) | collective-permute-done | bytes 131104 | tf_op jit(solution)/shard_map/ppermute | solution.py:417
  15.7 0.0 collective-permute-done.8.og_recv
  15.7 1.2 %soft_forward.1 = (bf16[256,128]{1,0:T(8,128)(2,1)S(1)}, bf16[512,128]{1,0:T(8,128)(2,1)S(1)}, bf16[512,128]{1,0:T(8,128)(2,1)S(1)}, bf16[256,1024]{1,0:T(8,128)...) custom-call(bf16[128,768]{1,0:T(8,128)(2,1)S(1)} %get-tuple-element., ...), custom_call_target="tpu_custom_call" | custom-call | flops 67108864 | bytes 2949120 | tf_op jit(solution)/shard_map/soft_forward/pallas_call | solution.py:66
  16.9 0.0 collective-permute-done.5.c.refs_2_
  17.0 0.7 %lin_forward.1 = (f32[256,128]{1,0:T(8,128)S(1)}, f32[128,128]{1,0:T(8,128)S(1)}, f32[128,512]{1,0:T(8,128)S(1)}, bf16[256,512]{1,0:T(8,128)(2,1)S(1)}) custom-call(f32[128,128]{1,0:T(8,128)S(1)} %get-tuple-element.59.state, bf16[128,768]{1,0:T(8,128)(2,1)S(1)} %get-tuple-element.50.mine.refs_6_, bf16[128,768]{1,0:T(8,128)(2,1)S(1)} %get-tuple-element.56.pair.refs_7_, ...), custom_call_target="tpu_custom_call" | custom-call | flops 67108864 | bytes 2163200 | tf_op jit(solution)/shard_map/lin_forward/pallas_call | solution.py:66
  17.6 1.6 %collective-permute-start.9 = (bf16[256,512]{1,0:T(8,128)(2,1)S(1)}, bf16[256,512]{1,0:T(8,128)(2,1)S(1)}, u32[]{:S(2)}, u32[]{:S(2)}) collective-permute-start(bf16[256,512]{1,0:T(8,128)(2,1)S(1)} %get-tuple-element.64), channel_id=1, source_target_pairs={{0,8},{1,17},{8,0},{9,25},{16,24},{17,1},{24,16},{25,9},{2,10},{3,... | collective-permute-start | bytes 786440 | tf_op jit(solution)/shard_map/ppermute | solution.py:423
  19.2 0.1 collective-permute-start.6
  19.3 1.2 %collective-permute-done.6.got = bf16[2,64,256]{2,1,0:T(8,128)(2,1)S(1)} collective-permute-done((bf16[2,64,256]{2,1,0:T(8,128)(2,1)S(1)}, bf16[2,64,256]{2,1,0:T(8,128)(2,1)S(1)}, u32[]{:S(2)}, u32[]{:S(2)}) %collective-permute-start.6) | collective-permute-done | bytes 65568 | tf_op jit(solution)/shard_map/ppermute | solution.py:406
  20.6 0.6 %collective-permute-start.7 = (bf16[256,256]{1,0:T(8,128)(2,1)S(1)}, bf16[256,256]{1,0:T(8,128)(2,1)S(1)}, u32[]{:S(2)}, u32[]{:S(2)}) collective-permute-start(bf16[256,256]{1,0:T(8,128)(2,1)S(1)} %w_rows.1.first), channel_id=1, source_target_pairs={{0,8},{1,17},{8,0},{9,25},{16,24},{17,1},{24,16},{25,9},{2,10},{3,... | collective-permute-start | bytes 393224 | tf_op jit(solution)/shard_map/ppermute | solution.py:423
  21.2 2.9 %collective-permute-done.9.got = bf16[256,512]{1,0:T(8,128)(2,1)S(1)} collective-permute-done((bf16[256,512]{1,0:T(8,128)(2,1)S(1)}, bf16[256,512]{1,0:T(8,128)(2,1)S(1)}, u32[]{:S(2)}, u32[]{:S(2)}) %collective-permute-start.9) | collective-permute-done | bytes 262176 | tf_op jit(solution)/shard_map/ppermute | solution.py:423
  24.1 0.1 fold.1
  24.1 1.9 %collective-permute-start.11 = (bf16[256,256]{1,0:T(8,128)(2,1)S(1)}, bf16[256,256]{1,0:T(8,128)(2,1)S(1)}, u32[]{:S(2)}, u32[]{:S(2)}) collective-permute-start(bf16[256,256]{1,0:T(8,128)(2,1)S(1)} %get-tuple-element.65.refs_0_), channel_id=1, source_target_pairs={{0,16},{1,9},{8,24},{9,1},{16,0},{17,25},{24,8},{25,17},{2,18},{3,... | collective-permute-start | bytes 393224 | tf_op jit(solution)/shard_map/ppermute | solution.py:423
  26.0 0.5 %collective-permute-done.7.second = bf16[256,256]{1,0:T(8,128)(2,1)S(1)} collective-permute-done((bf16[256,256]{1,0:T(8,128)(2,1)S(1)}, bf16[256,256]{1,0:T(8,128)(2,1)S(1)}, u32[]{:S(2)}, u32[]{:S(2)}) %collective-permute-start.7) | collective-permute-done | bytes 131104 | tf_op jit(solution)/shard_map/ppermute | solution.py:423
  26.6 1.9 %collective-permute-start.10 = (bf16[256,512]{1,0:T(8,128)(2,1)S(1)}, bf16[256,512]{1,0:T(8,128)(2,1)S(1)}, u32[]{:S(2)}, u32[]{:S(2)}) collective-permute-start(bf16[256,512]{1,0:T(8,128)(2,1)S(1)} %w_half.1.refs_0_), channel_id=1, source_target_pairs={{0,16},{1,9},{8,24},{9,1},{16,0},{17,25},{24,8},{25,17},{2,18},{3,... | collective-permute-start | bytes 786440 | tf_op jit(solution)/shard_map/ppermute | solution.py:423
  28.5 0.7 %collective-permute-done.11.got = bf16[256,256]{1,0:T(8,128)(2,1)S(1)} collective-permute-done((bf16[256,256]{1,0:T(8,128)(2,1)S(1)}, bf16[256,256]{1,0:T(8,128)(2,1)S(1)}, u32[]{:S(2)}, u32[]{:S(2)}) %collective-permute-start.11) | collective-permute-done | bytes 131104 | tf_op jit(solution)/shard_map/ppermute | solution.py:423
  29.2 0.1 rows.1
  29.2 0.1 collective-permute-start.12
  29.3 1.3 %collective-permute-done.12.got = f32[128,256]{1,0:T(8,128)S(1)} collective-permute-done((f32[128,256]{1,0:T(8,128)S(1)}, f32[128,256]{1,0:T(8,128)S(1)}, u32[]{:S(2)}, u32[]{:S(2)}) %collective-permute-start.12) | collective-permute-done | bytes 131104 | tf_op jit(solution)/shard_map/ppermute | solution.py:406
  30.7 0.8 %collective-permute-start.13 = (bf16[64,256]{1,0:T(8,128)(2,1)S(1)}, bf16[64,256]{1,0:T(8,128)(2,1)S(1)}, u32[]{:S(2)}, u32[]{:S(2)}) collective-permute-start(bf16[64,256]{1,0:T(8,128)(2,1)S(1)} %get-tuple-element.83), channel_id=1, source_target_pairs={{0,2},{1,7},{2,0},{3,5},{4,6},{5,3},{6,4},{7,1},{8,10},{9,15},{10,... | collective-permute-start | bytes 98312 | tf_op jit(solution)/shard_map/ppermute | solution.py:417
  31.5 3.4 %collective-permute-start.14 = (bf16[64,256]{1,0:T(8,128)(2,1)S(1)}, bf16[64,256]{1,0:T(8,128)(2,1)S(1)}, u32[]{:S(2)}, u32[]{:S(2)}) collective-permute-start(bf16[64,256]{1,0:T(8,128)(2,1)S(1)} %get-tuple-element.84), channel_id=1, source_target_pairs={{0,6},{1,3},{2,4},{3,1},{4,2},{5,7},{6,0},{7,5},{8,14},{9,11},{10,... | collective-permute-start | bytes 98312 | tf_op jit(solution)/shard_map/ppermute | solution.py:417
  34.9 0.0 collective-permute-start.15
  34.9 0.0 collective-permute-done.10.refs_1_
  34.9 1.5 %backward.1 = (bf16[128,128]{1,0:T(8,128)(2,1)S(1)}, bf16[128,128]{1,0:T(8,128)(2,1)S(1)}, f32[128,128]{1,0:T(8,128)S(1)}, f32[256,128]{1,0:T(8,128)S(1)}, f32[5...) custom-call(bf16[256,512]{1,0:T(8,128)(2,1)S(1)} %w_half.1.refs_0_, bf16[256,512]{1,0:T(8,128)(2,1)S(1)} %collective-permute-done.10.refs_1_, ...), custom_call_target="tpu_custom_call" | custom-call | flops 335544320 | bytes 3342848 | tf_op jit(solution)/shard_map/backward/pallas_call | solution.py:66
  36.4 0.0 collective-permute-done.13.refs_1_.a
  36.4 0.8 %collective-permute-done.14.refs_2_.b = bf16[64,256]{1,0:T(8,128)(2,1)S(1)} collective-permute-done((bf16[64,256]{1,0:T(8,128)(2,1)S(1)}, bf16[64,256]{1,0:T(8,128)(2,1)S(1)}, u32[]{:S(2)}, u32[]{:S(2)}) %collective-permute-start.14) | collective-permute-done | bytes 32800 | tf_op jit(solution)/shard_map/ppermute | solution.py:417
  37.2 2.4 %collective-permute-done.15.refs_3_.c = bf16[64,256]{1,0:T(8,128)(2,1)S(1)} collective-permute-done((bf16[64,256]{1,0:T(8,128)(2,1)S(1)}, bf16[64,256]{1,0:T(8,128)(2,1)S(1)}, u32[]{:S(2)}, u32[]{:S(2)}) %collective-permute-start.15) | collective-permute-done | bytes 32800 | tf_op jit(solution)/shard_map/ppermute | solution.py:417
  39.7 0.1 collective-permute-start.16
  39.9 2.4 %collective-permute-start.19 = (bf16[64,256]{1,0:T(8,128)(2,1)S(1)}, bf16[64,256]{1,0:T(8,128)(2,1)S(1)}, u32[]{:S(2)}, u32[]{:S(2)}) collective-permute-start(bf16[64,256]{1,0:T(8,128)(2,1)S(1)} %weight_sum.1.first), channel_id=1, source_target_pairs={{0,8},{1,17},{8,0},{9,25},{16,24},{17,1},{24,16},{25,9},{2,10},{3,... | collective-permute-start | bytes 98312 | tf_op jit(solution)/shard_map/ppermute | solution.py:423
  42.2 1.2 %collective-permute-start.17 = (bf16[128,384]{1,0:T(8,128)(2,1)S(1)}, bf16[128,384]{1,0:T(8,128)(2,1)S(1)}, u32[]{:S(2)}, u32[]{:S(2)}) collective-permute-start(bf16[128,384]{1,0:T(8,128)(2,1)S(1)} %get-tuple-element.87), channel_id=1, source_target_pairs={{0,6},{1,3},{2,4},{3,1},{4,2},{5,7},{6,0},{7,5},{8,14},{9,11},{10,... | collective-permute-start | bytes 294920 | tf_op jit(solution)/shard_map/ppermute | solution.py:417
  43.4 0.7 %collective-permute-done.19.second = bf16[64,256]{1,0:T(8,128)(2,1)S(1)} collective-permute-done((bf16[64,256]{1,0:T(8,128)(2,1)S(1)}, bf16[64,256]{1,0:T(8,128)(2,1)S(1)}, u32[]{:S(2)}, u32[]{:S(2)}) %collective-permute-start.19) | collective-permute-done | bytes 32800 | tf_op jit(solution)/shard_map/ppermute | solution.py:423
  44.1 1.9 %collective-permute-start.20 = (bf16[64,512]{1,0:T(8,128)(2,1)S(1)}, bf16[64,512]{1,0:T(8,128)(2,1)S(1)}, u32[]{:S(2)}, u32[]{:S(2)}) collective-permute-start(bf16[64,512]{1,0:T(8,128)(2,1)S(1)} %both.1), channel_id=1, source_target_pairs={{0,16},{1,9},{8,24},{9,1},{16,0},{17,25},{24,8},{25,17},{2,18},{3,... | collective-permute-start | bytes 196616 | tf_op jit(solution)/shard_map/ppermute | solution.py:423
  46.1 1.6 %collective-permute-start.18 = (bf16[128,128]{1,0:T(8,128)(2,1)S(1)}, bf16[128,128]{1,0:T(8,128)(2,1)S(1)}, u32[]{:S(2)}, u32[]{:S(2)}) collective-permute-start(bf16[128,128]{1,0:T(8,128)(2,1)S(1)} %get-tuple-element.88), channel_id=1, source_target_pairs={{0,4},{1,5},{2,6},{3,7},{4,0},{5,1},{6,2},{7,3},{8,12},{9,13},{10,... | collective-permute-start | bytes 98312 | tf_op jit(solution)/shard_map/ppermute | solution.py:417
  47.7 3.2 %collective-permute-done.18.refs_0_ = bf16[128,128]{1,0:T(8,128)(2,1)S(1)} collective-permute-done((bf16[128,128]{1,0:T(8,128)(2,1)S(1)}, bf16[128,128]{1,0:T(8,128)(2,1)S(1)}, u32[]{:S(2)}, u32[]{:S(2)}) %collective-permute-start.18) | collective-permute-done | bytes 32800 | tf_op jit(solution)/shard_map/ppermute | solution.py:417
  50.9 0.0 collective-permute-done.16.a
  50.9 0.0 collective-permute-done.17.b
  50.9 0.0 collective-permute-done.20.refs_1_.got
  50.9 0.4 final.1
  51.3 0.1 collective-permute-start.21
  51.3 0.7 %weight_join.1 = f32[64,1024]{1,0:T(8,128)} custom-call(bf16[64,512]{1,0:T(8,128)(2,1)S(1)} %both.1, bf16[64,512]{1,0:T(8,128)(2,1)S(1)} %collective-permute-done.20.refs_1_.got), custom_call_target="tpu_custom_call" | custom-call | bytes 393216 | tf_op jit(solution)/shard_map/weight_join/pallas_call | solution.py:66
  52.1 0.7 %collective-permute-done.21.pair = bf16[128,768]{1,0:T(8,128)(2,1)S(1)} collective-permute-done((bf16[128,768]{1,0:T(8,128)(2,1)S(1)}, bf16[128,768]{1,0:T(8,128)(2,1)S(1)}, u32[]{:S(2)}, u32[]{:S(2)}) %collective-permute-start.21) | collective-permute-done | bytes 196640 | tf_op jit(solution)/shard_map/ppermute | solution.py:406
  52.8 0.8 %outputs.1 = (bf16[1,128,512]{2,1,0:T(8,128)(2,1)}, bf16[1,128,512]{2,1,0:T(8,128)(2,1)}, bf16[1,128,512]{2,1,0:T(8,128)(2,1)}) custom-call(bf16[128,768]{1,0:T(8,128)(2,1)S(1)} %get-tuple-element.89.own, bf16[128,768]{1,0:T(8,128)(2,1)S(1)} %collective-permute-done.21.pair), custom_call_target="tpu_custom_call" | custom-call | bytes 786432 | tf_op jit(solution)/shard_map/outputs/pallas_call | solution.py:66
  (7 shorter events, 0.2 us)
Async XLA Ops:
  0.6 2.3 %collective-permute-start = (bf16[1,128,512]{2,1,0:T(8,128)(2,1)}, bf16[1,128,512]{2,1,0:T(8,128)(2,1)S(1)}, u32[]{:S(2)}, u32[]{:S(2)}) collective-permute-start(bf16[1,128,512]{2,1,0:T(8,128)(2,1)} %q.1), channel_id=1, source_target_pairs={{0,1},{1,0},{2,3},{3,2},{4,5},{5,4},{6,7},{7,6},{8,9},{9,8},{10,11... | collective-permute-start | bytes 393224 | tf_op jit(solution)/shard_map/ppermute | solution.py:406
  1.2 1.8 %collective-permute-start.1 = (bf16[1,128,512]{2,1,0:T(8,128)(2,1)}, bf16[1,128,512]{2,1,0:T(8,128)(2,1)S(1)}, u32[]{:S(2)}, u32[]{:S(2)}) collective-permute-start(bf16[1,128,512]{2,1,0:T(8,128)(2,1)} %k.1), channel_id=1, source_target_pairs={{0,1},{1,0},{2,3},{3,2},{4,5},{5,4},{6,7},{7,6},{8,9},{9,8},{10,11... | collective-permute-start | bytes 393224 | tf_op jit(solution)/shard_map/ppermute | solution.py:406
  1.2 1.7 %collective-permute-start.2 = (bf16[1,128,512]{2,1,0:T(8,128)(2,1)}, bf16[1,128,512]{2,1,0:T(8,128)(2,1)S(1)}, u32[]{:S(2)}, u32[]{:S(2)}) collective-permute-start(bf16[1,128,512]{2,1,0:T(8,128)(2,1)} %v.1), channel_id=1, source_target_pairs={{0,1},{1,0},{2,3},{3,2},{4,5},{5,4},{6,7},{7,6},{8,9},{9,8},{10,11... | collective-permute-start | bytes 393224 | tf_op jit(solution)/shard_map/ppermute | solution.py:406
  1.7 14.1 %collective-permute-start.8 = (bf16[128,1024]{1,0:T(8,128)(2,1)}, bf16[128,1024]{1,0:T(8,128)(2,1)S(1)}, u32[]{:S(2)}, u32[]{:S(2)}) collective-permute-start(bf16[128,1024]{1,0:T(8,128)(2,1)} %bitcast.1), channel_id=1, source_target_pairs={{0,1},{1,0},{2,3},{3,2},{4,5},{5,4},{6,7},{7,6},{8,9},{9,8},{10,11... | collective-permute-start | bytes 786440 | tf_op jit(solution)/shard_map/ppermute | solution.py:406
  3.2 6.0 %collective-permute-start.3 = (bf16[128,512]{1,0:T(8,128)(2,1)S(1)}, bf16[128,512]{1,0:T(8,128)(2,1)S(1)}, u32[]{:S(2)}, u32[]{:S(2)}) collective-permute-start(bf16[128,512]{1,0:T(8,128)(2,1)S(1)} %get-tuple-element.51), channel_id=1, source_target_pairs={{0,2},{1,7},{2,0},{3,5},{4,6},{5,3},{6,4},{7,1},{8,10},{9,15},{10,... | collective-permute-start | bytes 393224 | tf_op jit(solution)/shard_map/ppermute | solution.py:417
  6.3 9.4 %collective-permute-start.4 = (bf16[128,512]{1,0:T(8,128)(2,1)S(1)}, bf16[128,512]{1,0:T(8,128)(2,1)S(1)}, u32[]{:S(2)}, u32[]{:S(2)}) collective-permute-start(bf16[128,512]{1,0:T(8,128)(2,1)S(1)} %get-tuple-element.52), channel_id=1, source_target_pairs={{0,6},{1,3},{2,4},{3,1},{4,2},{5,7},{6,0},{7,5},{8,14},{9,11},{10,... | collective-permute-start | bytes 393224 | tf_op jit(solution)/shard_map/ppermute | solution.py:417
  8.8 8.2 %collective-permute-start.5 = (bf16[128,256]{1,0:T(8,128)(2,1)S(1)}, bf16[128,256]{1,0:T(8,128)(2,1)S(1)}, u32[]{:S(2)}, u32[]{:S(2)}) collective-permute-start(bf16[128,256]{1,0:T(8,128)(2,1)S(1)} %get-tuple-element.53), channel_id=1, source_target_pairs={{0,4},{1,5},{2,6},{3,7},{4,0},{5,1},{6,2},{7,3},{8,12},{9,13},{10,... | collective-permute-start | bytes 196616 | tf_op jit(solution)/shard_map/ppermute | solution.py:417
  17.6 6.4 %collective-permute-start.9 = (bf16[256,512]{1,0:T(8,128)(2,1)S(1)}, bf16[256,512]{1,0:T(8,128)(2,1)S(1)}, u32[]{:S(2)}, u32[]{:S(2)}) collective-permute-start(bf16[256,512]{1,0:T(8,128)(2,1)S(1)} %get-tuple-element.64), channel_id=1, source_target_pairs={{0,8},{1,17},{8,0},{9,25},{16,24},{17,1},{24,16},{25,9},{2,10},{3,... | collective-permute-start | bytes 786440 | tf_op jit(solution)/shard_map/ppermute | solution.py:423
  19.2 1.3 %collective-permute-start.6 = (bf16[2,64,256]{2,1,0:T(8,128)(2,1)S(1)}, bf16[2,64,256]{2,1,0:T(8,128)(2,1)S(1)}, u32[]{:S(2)}, u32[]{:S(2)}) collective-permute-start(bf16[2,64,256]{2,1,0:T(8,128)(2,1)S(1)} %get-tuple-element.55), channel_id=1, source_target_pairs={{0,1},{1,0},{2,3},{3,2},{4,5},{5,4},{6,7},{7,6},{8,9},{9,8},{10,11... | collective-permute-start | bytes 196616 | tf_op jit(solution)/shard_map/ppermute | solution.py:406
  20.6 6.0 %collective-permute-start.7 = (bf16[256,256]{1,0:T(8,128)(2,1)S(1)}, bf16[256,256]{1,0:T(8,128)(2,1)S(1)}, u32[]{:S(2)}, u32[]{:S(2)}) collective-permute-start(bf16[256,256]{1,0:T(8,128)(2,1)S(1)} %w_rows.1.first), channel_id=1, source_target_pairs={{0,8},{1,17},{8,0},{9,25},{16,24},{17,1},{24,16},{25,9},{2,10},{3,... | collective-permute-start | bytes 393224 | tf_op jit(solution)/shard_map/ppermute | solution.py:423
  24.1 5.0 %collective-permute-start.11 = (bf16[256,256]{1,0:T(8,128)(2,1)S(1)}, bf16[256,256]{1,0:T(8,128)(2,1)S(1)}, u32[]{:S(2)}, u32[]{:S(2)}) collective-permute-start(bf16[256,256]{1,0:T(8,128)(2,1)S(1)} %get-tuple-element.65.refs_0_), channel_id=1, source_target_pairs={{0,16},{1,9},{8,24},{9,1},{16,0},{17,25},{24,8},{25,17},{2,18},{3,... | collective-permute-start | bytes 393224 | tf_op jit(solution)/shard_map/ppermute | solution.py:423
  26.6 8.3 %collective-permute-start.10 = (bf16[256,512]{1,0:T(8,128)(2,1)S(1)}, bf16[256,512]{1,0:T(8,128)(2,1)S(1)}, u32[]{:S(2)}, u32[]{:S(2)}) collective-permute-start(bf16[256,512]{1,0:T(8,128)(2,1)S(1)} %w_half.1.refs_0_), channel_id=1, source_target_pairs={{0,16},{1,9},{8,24},{9,1},{16,0},{17,25},{24,8},{25,17},{2,18},{3,... | collective-permute-start | bytes 786440 | tf_op jit(solution)/shard_map/ppermute | solution.py:423
  29.2 1.4 %collective-permute-start.12 = (f32[128,256]{1,0:T(8,128)S(1)}, f32[128,256]{1,0:T(8,128)S(1)}, u32[]{:S(2)}, u32[]{:S(2)}) collective-permute-start(f32[128,256]{1,0:T(8,128)S(1)} %get-tuple-element.68), channel_id=1, source_target_pairs={{0,1},{1,0},{2,3},{3,2},{4,5},{5,4},{6,7},{7,6},{8,9},{9,8},{10,11... | collective-permute-start | bytes 393224 | tf_op jit(solution)/shard_map/ppermute | solution.py:406
  30.7 5.7 %collective-permute-start.13 = (bf16[64,256]{1,0:T(8,128)(2,1)S(1)}, bf16[64,256]{1,0:T(8,128)(2,1)S(1)}, u32[]{:S(2)}, u32[]{:S(2)}) collective-permute-start(bf16[64,256]{1,0:T(8,128)(2,1)S(1)} %get-tuple-element.83), channel_id=1, source_target_pairs={{0,2},{1,7},{2,0},{3,5},{4,6},{5,3},{6,4},{7,1},{8,10},{9,15},{10,... | collective-permute-start | bytes 98312 | tf_op jit(solution)/shard_map/ppermute | solution.py:417
  31.5 5.7 %collective-permute-start.14 = (bf16[64,256]{1,0:T(8,128)(2,1)S(1)}, bf16[64,256]{1,0:T(8,128)(2,1)S(1)}, u32[]{:S(2)}, u32[]{:S(2)}) collective-permute-start(bf16[64,256]{1,0:T(8,128)(2,1)S(1)} %get-tuple-element.84), channel_id=1, source_target_pairs={{0,6},{1,3},{2,4},{3,1},{4,2},{5,7},{6,0},{7,5},{8,14},{9,11},{10,... | collective-permute-start | bytes 98312 | tf_op jit(solution)/shard_map/ppermute | solution.py:417
  34.9 4.8 %collective-permute-start.15 = (bf16[64,256]{1,0:T(8,128)(2,1)S(1)}, bf16[64,256]{1,0:T(8,128)(2,1)S(1)}, u32[]{:S(2)}, u32[]{:S(2)}) collective-permute-start(bf16[64,256]{1,0:T(8,128)(2,1)S(1)} %get-tuple-element.85), channel_id=1, source_target_pairs={{0,4},{1,5},{2,6},{3,7},{4,0},{5,1},{6,2},{7,3},{8,12},{9,13},{10,... | collective-permute-start | bytes 98312 | tf_op jit(solution)/shard_map/ppermute | solution.py:417
  39.7 11.2 %collective-permute-start.16 = (bf16[128,384]{1,0:T(8,128)(2,1)S(1)}, bf16[128,384]{1,0:T(8,128)(2,1)S(1)}, u32[]{:S(2)}, u32[]{:S(2)}) collective-permute-start(bf16[128,384]{1,0:T(8,128)(2,1)S(1)} %get-tuple-element.86), channel_id=1, source_target_pairs={{0,2},{1,7},{2,0},{3,5},{4,6},{5,3},{6,4},{7,1},{8,10},{9,15},{10,... | collective-permute-start | bytes 294920 | tf_op jit(solution)/shard_map/ppermute | solution.py:417
  39.9 4.3 %collective-permute-start.19 = (bf16[64,256]{1,0:T(8,128)(2,1)S(1)}, bf16[64,256]{1,0:T(8,128)(2,1)S(1)}, u32[]{:S(2)}, u32[]{:S(2)}) collective-permute-start(bf16[64,256]{1,0:T(8,128)(2,1)S(1)} %weight_sum.1.first), channel_id=1, source_target_pairs={{0,8},{1,17},{8,0},{9,25},{16,24},{17,1},{24,16},{25,9},{2,10},{3,... | collective-permute-start | bytes 98312 | tf_op jit(solution)/shard_map/ppermute | solution.py:423
  42.2 8.6 %collective-permute-start.17 = (bf16[128,384]{1,0:T(8,128)(2,1)S(1)}, bf16[128,384]{1,0:T(8,128)(2,1)S(1)}, u32[]{:S(2)}, u32[]{:S(2)}) collective-permute-start(bf16[128,384]{1,0:T(8,128)(2,1)S(1)} %get-tuple-element.87), channel_id=1, source_target_pairs={{0,6},{1,3},{2,4},{3,1},{4,2},{5,7},{6,0},{7,5},{8,14},{9,11},{10,... | collective-permute-start | bytes 294920 | tf_op jit(solution)/shard_map/ppermute | solution.py:417
  44.1 6.7 %collective-permute-start.20 = (bf16[64,512]{1,0:T(8,128)(2,1)S(1)}, bf16[64,512]{1,0:T(8,128)(2,1)S(1)}, u32[]{:S(2)}, u32[]{:S(2)}) collective-permute-start(bf16[64,512]{1,0:T(8,128)(2,1)S(1)} %both.1), channel_id=1, source_target_pairs={{0,16},{1,9},{8,24},{9,1},{16,0},{17,25},{24,8},{25,17},{2,18},{3,... | collective-permute-start | bytes 196616 | tf_op jit(solution)/shard_map/ppermute | solution.py:423
  46.1 4.8 %collective-permute-start.18 = (bf16[128,128]{1,0:T(8,128)(2,1)S(1)}, bf16[128,128]{1,0:T(8,128)(2,1)S(1)}, u32[]{:S(2)}, u32[]{:S(2)}) collective-permute-start(bf16[128,128]{1,0:T(8,128)(2,1)S(1)} %get-tuple-element.88), channel_id=1, source_target_pairs={{0,4},{1,5},{2,6},{3,7},{4,0},{5,1},{6,2},{7,3},{8,12},{9,13},{10,... | collective-permute-start | bytes 98312 | tf_op jit(solution)/shard_map/ppermute | solution.py:417
  51.3 1.5 %collective-permute-start.21 = (bf16[128,768]{1,0:T(8,128)(2,1)S(1)}, bf16[128,768]{1,0:T(8,128)(2,1)S(1)}, u32[]{:S(2)}, u32[]{:S(2)}) collective-permute-start(bf16[128,768]{1,0:T(8,128)(2,1)S(1)} %get-tuple-element.90), channel_id=1, source_target_pairs={{0,1},{1,0},{2,3},{3,2},{4,5},{5,4},{6,7},{7,6},{8,9},{9,8},{10,11... | collective-permute-start | bytes 589832 | tf_op jit(solution)/shard_map/ppermute | solution.py:406

commit v10 on v9

--- a/solution.py
+++ b/solution.py
@@ -142,27 +142,6 @@
             out[:, first : first + DH] = total.astype(BF)
             out[:rows, first + DH :] = w[:, :DH]
             out[rows:, first + DH :] = w[:, DH:]
-
-
-def relay_kernel(w, a, b, c, keep, send, heads):
-    core, z, _ = places()
-    way = links(True)
-    rows = w.shape[0]
-    heads[z] = w[...]
-    for source, first, step in ((a, 3 * DH, way["first"]), (b, 3 * DH, way["second"]), (c, DH, 2)):
-        heads[z ^ step, :, :DH] = source[:rows, first:]
-        heads[z ^ step, :, DH:] = source[rows:, first:]
-    for group in range(2):
-        keep[group] = heads[2 * group + core]
-        send[group] = heads[2 * group + 1 - core]
-
-
-def w_rows_kernel(keep, got, out):
-    core, _, _ = places()
-    half = keep.shape[1]
-    for group in range(2):
-        out[at(group * DH + core * half, half), :] = keep[group]
-        out[at(group * DH + (1 - core) * half, half), :] = got[group]
 
 
 def join_kernel(first, second, *refs):
@@ -225,7 +204,7 @@
     rows = mine.shape[0]
     total = state[...]
     if direct:
-        a, b, c, soft_send, u_out, total_out, keep, out = refs
+        a, b, c, soft_send, w, u_out, total_out, keep, out = refs
         total = total + a[:, 2 * DH : 3 * DH].astype(F32) + b[:, 2 * DH : 3 * DH].astype(F32)
         total = total + c[:, :DH].astype(F32)
     else:
@@ -236,26 +215,47 @@
     u = u_out[...]
     r = lax.rsqrt(jnp.mean(u * u, axis=1, keepdims=True) + norm_eps)
     attn = gain[...] * u * r
-    weight_parts(direct, attn, ogs, out.at[DH:, :] if direct else None, keep)
-    if direct:
-        out[:DH, :] = soft_send[...]
-
-
-def fold_kernel(keep_soft, keep_lin, got, keep, send):
+    weight_parts(direct, attn, ogs, out.at[DH:, : soft_send.shape[1]] if direct else None, keep)
+    if direct:
+        _, z, _ = places()
+        way = links(True)
+        rows, width = w.shape
+        first = soft_send.shape[1]
+        out[:DH, :first] = soft_send[...]
+        out[at(z * rows, rows), first:] = w[...]
+        for source, cols, step in ((a, 3 * DH, way["first"]), (b, 3 * DH, way["second"]), (c, DH, 2)):
+            here = at((z ^ step) * rows, rows)
+            out[here, first : first + DH] = source[:rows, cols:]
+            out[here, first + DH :] = source[rows:, cols:]
+
+
+def fold_kernel(keep_soft, keep_lin, sent, got, keep, send):
     width = keep.shape[1]
     for rows, source in ((slice(0, DH), keep_soft), (slice(DH, 2 * DH), keep_lin)):
         keep[rows, :] = source[:, :width] + got[rows, :width].astype(F32)
-        send[rows, :] = (source[:, width:] + got[rows, width:].astype(F32)).astype(BF)
-
-
-def rows_kernel(keep, got, own, send, total):
-    core, _, _ = places()
+        send[rows, :width] = (source[:, width:] + got[rows, width : 2 * width].astype(F32)).astype(BF)
+    send[:, width : 2 * width] = sent[:, 2 * width :]
+    send[:, 2 * width :] = got[:, 2 * width :]
+
+
+def rows_kernel(keep, sent, got, own, w_own, send, total, weights):
+    core, _, dp = places()
+    way = links(True)
     half = DH // 2
-    total[...] = keep[...] + got[...].astype(F32)
+    width = keep.shape[1]
+    total[...] = keep[...] + got[:, :width].astype(F32)
+    for source, index, step in (
+        (sent, 1, 0), (sent, 2, way["step"]), (got, 1, way["other"]), (got, 2, 3),
+    ):
+        weights[:, at((dp ^ step) * width, width)] = source[:, index * width : (index + 1) * width]
     for group in range(2):
         out = slice(group * half, (group + 1) * half)
         own[out, :] = total[at(group * DH + core * half, half), :]
-        send[out, :] = total[at(group * DH + (1 - core) * half, half), :]
+        high, low = halves(total[at(group * DH + (1 - core) * half, half), :])
+        send[out, :width] = high
+        send[out, width : 2 * width] = low
+        w_own[out, :] = weights[at((2 * group + core) * half, half), :]
+        send[out, 2 * width :] = weights[at((2 * group + 1 - core) * half, half), :]
 
 
 def lin_backward(u, total, dattn, mine, pair, gain, dq_own, dq_pair, dstate, grads):
@@ -293,22 +293,21 @@
 
 def backward_kernel(direct, *refs):
     if direct:
-        sent, got = refs[:2]
-        refs = refs[3:]
+        w_own, got = refs[:2]
+        refs = refs[2:]
     else:
         weights = refs[0]
         refs = refs[1:]
     (ogs, u, total, mine, pair, gain, qs, ks, vs, probs, attn,
      dq_lin, dq_lin_pair, dstate, dq_soft, dk_soft, dv_soft, dattn, grads, *scratch) = refs
     if direct:
-        _, _, dp = places()
-        way = links(True)
+        core, _, _ = places()
         weights = scratch[0]
-        width = weights.shape[1] // 4
-        for source, index, step in (
-            (sent, 0, 0), (sent, 1, way["step"]), (got, 0, way["other"]), (got, 1, 3),
-        ):
-            weights[:, at((dp ^ step) * width, width)] = source[:, index * width : (index + 1) * width]
+        rows, model = w_own.shape[0] // 2, weights.shape[1]
+        for group in range(2):
+            here = slice(group * rows, (group + 1) * rows)
+            weights[at(group * DH + core * rows, rows), :] = w_own[here, :]
+            weights[at(group * DH + (1 - core) * rows, rows), :] = got[here, got.shape[1] - model :]
     dattn[...] = mm(ogs[...], weights[...], NT)
     lin_backward(u, total, dattn, mine, pair, gain, dq_lin, dq_lin_pair, dstate, grads)
     soft_backward(qs, ks, vs, probs, attn, dattn, dq_soft, dk_soft, dv_soft)
@@ -318,8 +317,11 @@
     way = links(direct)
     span = dk_soft.shape[0]
     if direct:
-        dstate, *_, to_a, to_b, to_c = refs
-        to_c[...] = dstate[...].astype(BF)
+        dstate, piece, _, _, to_a, to_b, to_c = refs
+        half = piece.shape[0]
+        to_c[:, :DH] = dstate[...].astype(BF)
+        to_c[:half, DH:] = piece[:, :DH]
+        to_c[half:, DH:] = piece[:, DH:]
     else:
         to_a, to_b = refs
     for out, side in ((to_a, way["halo_a"]), (to_b, way["halo_b"])):
@@ -333,19 +335,22 @@
 def chunk_kernel(own, got, to_a, to_b, to_c, chunk, heads):
     core, z, _ = places()
     way = links(True)
-    half = chunk.shape[0]
+    half, width = chunk.shape
     for group in range(2):
         rows = slice(group * half, (group + 1) * half)
         heads[2 * group + core] = own[rows, :]
-        heads[2 * group + 1 - core] = got[rows, :]
+        heads[2 * group + 1 - core] = got[rows, :width].astype(F32) + got[rows, width : 2 * width].astype(F32)
     chunk[...] = heads[z]
     for out, step in ((to_a, way["first"]), (to_b, way["second"]), (to_c, 2)):
         out[...] = heads[z ^ step].astype(BF)
 
 
 def weight_sum_kernel(scale, chunk, a, b, c, out):
-    total = chunk[...] + a[...].astype(F32) + b[...].astype(F32) + c[...].astype(F32)
-    out[...] = (scale * total).astype(out.dtype)
+    half = chunk.shape[0]
+    for side in range(2):
+        cols, rows = slice(side * DH, (side + 1) * DH), slice(side * half, (side + 1) * half)
+        total = chunk[:, cols] + a[:, cols].astype(F32) + b[:, cols].astype(F32)
+        out[:, cols] = (scale * (total + c[rows, DH:].astype(F32))).astype(out.dtype)
 
 
 def final_kernel(
@@ -358,7 +363,7 @@
     own_out, pair_out, dk_all, dv_all = refs[-4:]
     if direct:
         total = total + a[:, 2 * DH :].astype(F32) + b[:, 2 * DH :].astype(F32)
-        total = total + refs[0][...].astype(F32)
+        total = total + refs[0][:, :DH].astype(F32)
     for source, out, cols in ((dk_soft, dk_all, slice(0, DH)), (dv_soft, dv_all, slice(DH, 2 * DH))):
         out[...] = source[HALF : HALF + 2 * rows, :]
         out[at(way["block_a"] * rows, rows), :] += a[:, cols].astype(F32)
@@ -383,7 +388,7 @@
             out[0, :, at(SOFT + first)] = source[:, (3 + index) * DH : (4 + index) * DH]
 
 
-def weight_join_kernel(both, got, out):
+def weight_join_kernel(both, got, _, out):
     _, _, dp = places()
     way = links(True)
     width = both.shape[1] // 2
@@ -449,14 +454,6 @@
     )
     if direct:
         a, b, c = over_z(to_a, 0), over_z(to_b, 1), [over_z(rest[0], 2)]
-        w_keep, w_send = call(
-            relay_kernel, "relay", [like((2, half, width), BF)] * 2, [w_part, a, b] + c,
-            scratch=[pltpu.VMEM((HEADS, half, width), BF)],
-        )
-        w_own = call(
-            w_rows_kernel, "w_rows", [like((2 * DH, width), BF)], [w_keep, over_core(w_send)]
-        )[0]
-        w_got = over_dp(w_own, 0)
     else:
         a, b, c = over_z(to_a, 0), over_z(to_b, 1), []
         state = lax.psum(state, "z")
@@ -479,43 +476,30 @@
     u, total, keep_lin, *sent = call(
         functools.partial(lin_forward_kernel, direct), "lin_forward",
         [like((2 * rows, DH), F32), like((DH, DH), F32), like((DH, keep_width), F32)]
-        + [like((2 * DH, 2 * width), BF)] * direct,
-        [state, mine, pair, ogs, gain] + ([a, b] + c + soft_send if direct else []),
+        + [like((2 * DH, 3 * width), BF)] * direct,
+        [state, mine, pair, ogs, gain] + ([a, b] + c + soft_send + [w_part] if direct else []),
         flops=wg_flops,
     )
     if direct:
         got = over_dp(sent[0], 0)
         keep, sent = call(
-            fold_kernel, "fold", [like((2 * DH, width), F32), like((2 * DH, width), BF)],
-            [keep_soft, keep_lin, got],
+            fold_kernel, "fold", [like((2 * DH, width), F32), like((2 * DH, 3 * width), BF)],
+            [keep_soft, keep_lin, sent[0], got],
         )
-        w_half = call(
-            join_kernel, "w_half", [like((2 * DH, 2 * width), BF)], [w_own, w_got, sent]
-        )[0]
-        weights = [w_half, over_dp(w_half, 1)]
         got = over_dp(sent, 1)
-        row_own, row_send = call(
-            rows_kernel, "rows", [like((2 * half, width), F32)] * 2, [keep, got],
-            scratch=[pltpu.VMEM((2 * DH, width), F32)],
+        row_own, w_own, swap = call(
+            rows_kernel, "rows",
+            [like((DH, width), F32), like((DH, model), BF), like((DH, 2 * width + model), BF)],
+            [keep, sent, got],
+            scratch=[pltpu.VMEM((2 * DH, width), F32), pltpu.VMEM((2 * DH, model), BF)],
         )
-        row_recv = over_core(row_send)
-        *to_chips, chunk = call(
+        swap = over_core(swap)
+        weights = [w_own, swap]
+        piece_a, piece_b, piece_c, chunk = call(
             chunk_kernel, "chunk", [like((half, width), BF)] * 3 + [like((half, width), F32)],
-            [row_own, row_recv], scratch=[pltpu.VMEM((HEADS, half, width), F32)],
+            [row_own, swap], scratch=[pltpu.VMEM((HEADS, half, width), F32)],
         )
-        chunks = [over_z(value, which) for which, value in enumerate(to_chips)]
-        summed = call(
-            functools.partial(weight_sum_kernel, scale), "weight_sum", [like((half, width), BF)],
-            [chunk] + chunks,
-        )[0]
-        got = over_dp(summed, 0)
-        both = call(join_kernel, "both", [like((half, 2 * width), BF)], [summed, got])[0]
-        gathered = over_dp(both, 1)
-        weight_grad = call(
-            weight_join_kernel, "weight_join", [like((half, model), F32)], [both, gathered]
-        )[0]
-    if direct:
-        weights.append(chunk)
+        chunks = [over_z(piece_a, 0), over_z(piece_b, 1)]
     dq_lin, dq_lin_pair, dstate, dq_soft, dk_soft, dv_soft = call(
         functools.partial(backward_kernel, direct), "backward",
         [
@@ -530,11 +514,19 @@
     wide = 3 * DH if direct else 2 * DH
     to_a, to_b, *to_c = call(
         functools.partial(halo_kernel, direct), "halo",
-        [like((rows, wide), BF), like((rows, wide), BF)] + [like((DH, DH), BF)] * direct,
-        [dk_soft, dv_soft] + ([dstate] + chunks if direct else []),
+        [like((rows, wide), BF), like((rows, wide), BF)] + [like((rows, 2 * DH), BF)] * direct,
+        [dk_soft, dv_soft] + ([dstate, piece_c] + chunks if direct else []),
     )
     a, b = over_z(to_a, 0, True), over_z(to_b, 1, True)
     c = [over_z(value, 2) for value in to_c]
+    if direct:
+        summed = call(
+            functools.partial(weight_sum_kernel, scale), "weight_sum", [like((half, width), BF)],
+            [chunk] + chunks + c,
+        )[0]
+        got = over_dp(summed, 0)
+        both = call(join_kernel, "both", [like((half, 2 * width), BF)], [summed, got])[0]
+        gathered = over_dp(both, 1)
     if not direct:
         dstate = lax.psum(dstate, "z")
         groups = jnp.stack([keep_soft, keep_lin])
@@ -547,13 +539,18 @@
         functools.partial(final_kernel, direct), "final",
         [like((rows, 6 * DH), BF), like((rows, 6 * DH), BF)],
         [dstate, mine, pair, dq_soft, dk_soft, dv_soft, dq_lin, dq_lin_pair, a, b] + c
-        + ([gathered] if direct else []),
+        + ([both] if direct else []),
         scratch=[pltpu.VMEM((2 * rows, DH), F32)] * 2,
         flops=wg_flops // 4,
     )
     from_pair = over_core(to_pair)
     shape = like((1, rows, HEADS * DH), BF)
     dq, dk, dv = call(output_kernel, "outputs", [shape] * 3, [own_out, from_pair])
+    if direct:
+        weight_grad = call(
+            weight_join_kernel, "weight_join", [like((half, model), F32)], [both, gathered, hbm(dq)],
+            spaces=[vmem, vmem, pl.BlockSpec(memory_space=pltpu.HBM)],
+        )[0]
     return dq, dk, dv, weight_grad
 
 

time: 53.7 us -> 59.6 us (1.11)
  waiting for transfers between devices: 21.4 us -> 30.2 us
  starting transfers between devices: 24.3 us -> 21.4 us
    ppermute x6 -> x4, waiting for transfers between devices: 4.85 us -> 17.3 us  [over_dp(): return lax.ppermute(value, ('dp', 'core'), pairs)]
    ppermute x6 -> x4, starting transfers between devices: 10.3 us -> 6.24 us  [over_dp(): return lax.ppermute(value, ('dp', 'core'), pairs)]
    ppermute x9 -> x8, waiting for transfers between devices: 13.3 us -> 11.2 us  [over_z(): return lax.ppermute(value, axes, pairs)]
    ppermute x7 -> x6, waiting for transfers between devices: 3.28 us -> 1.72 us  [over_core(): return lax.ppermute(value, 'core', pair_perm)]
    ppermute x9 -> x8, starting transfers between devices: 12.7 us -> 14 us  [over_z(): return lax.ppermute(value, axes, pairs)]
    ppermute x7 -> x6, starting transfers between devices: 1.32 us -> 1.25 us  [over_core(): return lax.ppermute(value, 'core', pair_perm)]
    pallas_call x17 -> x14, Pallas kernels: 7.06 us -> 7.05 us  [call(): pl.pallas_call(kernel, name=name, out_shape=list(outs), in_specs=spaces o...]
  transfers between devices with their start and end apart: 22 -> 18, of which waited for: 12 -> 9; matrix products, arithmetic and copies ran while one was open for 0% -> 0% of each run, Pallas kernels for 10% -> 8%
where the time goes in v10:
time: 59.6 us; the launch traced here: 59.5 us
  waiting for transfers between devices  30.2 us (51%)
  starting transfers between devices  21.4 us (36%)
  Pallas kernels  7.05 us (12%)
  between operations  0.79 us (1%)
    ppermute x4, waiting for transfers between devices, over_dp(): return lax.ppermute(value, ('dp', 'core'), pairs)  17.3 us
    ppermute x8, starting transfers between devices, over_z(): return lax.ppermute(value, axes, pairs)  14 us
    ppermute x8, waiting for transfers between devices, over_z(): return lax.ppermute(value, axes, pairs)  11.2 us
    pallas_call x14, Pallas kernels, call(): pl.pallas_call(kernel, name=name, out_shape=list(outs), in_specs=spaces o...  7.05 us
    ppermute x4, starting transfers between devices, over_dp(): return lax.ppermute(value, ('dp', 'core'), pairs)  6.24 us
    ppermute x6, waiting for transfers between devices, over_core(): return lax.ppermute(value, 'core', pair_perm)  1.72 us
    ppermute x6, starting transfers between devices, over_core(): return lax.ppermute(value, 'core', pair_perm)  1.25 us
  transfers between devices with their start and end apart: 18, of which 9 were waited for; matrix products, arithmetic and copies ran while one was open for 0% of the time, Pallas kernels for 8%

profile of v10, /device:TPU:0, one launch (start us, length us, event | category | flops | bytes accessed | tf_op | source)
XLA Modules:
  0.0 59.5 jit_solution(7444887349246598673)
XLA Ops:
  0.6 0.5 collective-permute-start
  1.2 0.1 collective-permute-start.1
  1.2 0.4 collective-permute-start.2
  1.7 0.1 collective-permute-start.3
  1.7 1.2 %pack.1 = (bf16[128,768]{1,0:T(8,128)(2,1)S(1)}, bf16[128,1024]{1,0:T(8,128)(2,1)S(1)}, bf16[64,256]{1,0:T(8,128)(2,1)S(1)}, f32[1,128]{1,0:T(1,128)S(1)}) custom-call(bf16[1,128,512]{2,1,0:T(8,128)(2,1)} %q.1, bf16[1,128,512]{2,1,0:T(8,128)(2,1)} %k.1, bf16[1,128,512]{2,1,0:T(8,128)(2,1)} %v.1, bf16[1,128,1024]{2,1,0:T(8,128)(2,1)} %og.1, ...), custom_call_target="tpu_custom_call" | custom-call | bytes 1279488 | tf_op jit(solution)/shard_map/pack/pallas_call | solution.py:66
  2.9 0.0 collective-permute-done.q_pair
  2.9 0.0 collective-permute-done.1.k_pair
  2.9 0.0 collective-permute-done.2.v_pair
  3.0 0.3 state.1
  3.2 3.1 %collective-permute-start.4 = (bf16[128,512]{1,0:T(8,128)(2,1)S(1)}, bf16[128,512]{1,0:T(8,128)(2,1)S(1)}, u32[]{:S(2)}, u32[]{:S(2)}) collective-permute-start(bf16[128,512]{1,0:T(8,128)(2,1)S(1)} %get-tuple-element.52), channel_id=1, source_target_pairs={{0,2},{1,7},{2,0},{3,5},{4,6},{5,3},{6,4},{7,1},{8,10},{9,15},{10,... | collective-permute-start | bytes 393224 | tf_op jit(solution)/shard_map/ppermute | solution.py:422
  6.3 2.5 %collective-permute-start.5 = (bf16[128,512]{1,0:T(8,128)(2,1)S(1)}, bf16[128,512]{1,0:T(8,128)(2,1)S(1)}, u32[]{:S(2)}, u32[]{:S(2)}) collective-permute-start(bf16[128,512]{1,0:T(8,128)(2,1)S(1)} %get-tuple-element.53), channel_id=1, source_target_pairs={{0,6},{1,3},{2,4},{3,1},{4,2},{5,7},{6,0},{7,5},{8,14},{9,11},{10,... | collective-permute-start | bytes 393224 | tf_op jit(solution)/shard_map/ppermute | solution.py:422
  8.8 0.1 collective-permute-start.6
  8.9 0.0 collective-permute-done.3.og_recv
  8.9 0.4 collective-permute-done.4.a.refs_0_
  9.3 6.5 %collective-permute-done.5.b.refs_1_ = bf16[128,512]{1,0:T(8,128)(2,1)S(1)} collective-permute-done((bf16[128,512]{1,0:T(8,128)(2,1)S(1)}, bf16[128,512]{1,0:T(8,128)(2,1)S(1)}, u32[]{:S(2)}, u32[]{:S(2)}) %collective-permute-start.5) | collective-permute-done | bytes 131104 | tf_op jit(solution)/shard_map/ppermute | solution.py:422
  15.7 1.2 %soft_forward.1 = (bf16[256,128]{1,0:T(8,128)(2,1)S(1)}, bf16[512,128]{1,0:T(8,128)(2,1)S(1)}, bf16[512,128]{1,0:T(8,128)(2,1)S(1)}, bf16[256,1024]{1,0:T(8,128)...) custom-call(bf16[128,768]{1,0:T(8,128)(2,1)S(1)} %get-tuple-element., ...), custom_call_target="tpu_custom_call" | custom-call | flops 67108864 | bytes 2949120 | tf_op jit(solution)/shard_map/soft_forward/pallas_call | solution.py:66
  16.9 0.0 collective-permute-done.6.refs_2_
  16.9 0.7 %lin_forward.1 = (f32[256,128]{1,0:T(8,128)S(1)}, f32[128,128]{1,0:T(8,128)S(1)}, f32[128,512]{1,0:T(8,128)S(1)}, bf16[256,768]{1,0:T(8,128)(2,1)S(1)}) custom-call(f32[128,128]{1,0:T(8,128)S(1)} %get-tuple-element.55.state, bf16[128,768]{1,0:T(8,128)(2,1)S(1)} %get-tuple-element.48.mine.refs_5_, bf16[128,768]{1,0:T(8,128)(2,1)S(1)} %get-tuple-element.50.pair.refs_6_, ...), custom_call_target="tpu_custom_call" | custom-call | flops 67108864 | bytes 2327040 | tf_op jit(solution)/shard_map/lin_forward/pallas_call | solution.py:66
  17.7 1.6 %collective-permute-start.7 = (bf16[256,768]{1,0:T(8,128)(2,1)S(1)}, bf16[256,768]{1,0:T(8,128)(2,1)S(1)}, u32[]{:S(2)}, u32[]{:S(2)}) collective-permute-start(bf16[256,768]{1,0:T(8,128)(2,1)S(1)} %get-tuple-element.61.sent), channel_id=1, source_target_pairs={{0,8},{1,17},{8,0},{9,25},{16,24},{17,1},{24,16},{25,9},{2,10},{3,... | collective-permute-start | bytes 1179656 | tf_op jit(solution)/shard_map/ppermute | solution.py:428
  19.2 6.6 %collective-permute-done.7.got = bf16[256,768]{1,0:T(8,128)(2,1)S(1)} collective-permute-done((bf16[256,768]{1,0:T(8,128)(2,1)S(1)}, bf16[256,768]{1,0:T(8,128)(2,1)S(1)}, u32[]{:S(2)}, u32[]{:S(2)}) %collective-permute-start.7) | collective-permute-done | bytes 393248 | tf_op jit(solution)/shard_map/ppermute | solution.py:428
  25.8 0.1 fold.1
  25.9 1.6 %collective-permute-start.8 = (bf16[256,768]{1,0:T(8,128)(2,1)S(1)}, bf16[256,768]{1,0:T(8,128)(2,1)S(1)}, u32[]{:S(2)}, u32[]{:S(2)}) collective-permute-start(bf16[256,768]{1,0:T(8,128)(2,1)S(1)} %get-tuple-element.63.sent), channel_id=1, source_target_pairs={{0,16},{1,9},{8,24},{9,1},{16,0},{17,25},{24,8},{25,17},{2,18},{3,... | collective-permute-start | bytes 1179656 | tf_op jit(solution)/shard_map/ppermute | solution.py:428
  27.5 6.3 %collective-permute-done.8.got = bf16[256,768]{1,0:T(8,128)(2,1)S(1)} collective-permute-done((bf16[256,768]{1,0:T(8,128)(2,1)S(1)}, bf16[256,768]{1,0:T(8,128)(2,1)S(1)}, u32[]{:S(2)}, u32[]{:S(2)}) %collective-permute-start.8) | collective-permute-done | bytes 393248 | tf_op jit(solution)/shard_map/ppermute | solution.py:428
  33.8 0.1 rows.1
  33.9 0.1 collective-permute-start.9
  34.0 1.7 %collective-permute-done.9.refs_1_.got = bf16[128,1536]{1,0:T(8,128)(2,1)S(1)} collective-permute-done((bf16[128,1536]{1,0:T(8,128)(2,1)S(1)}, bf16[128,1536]{1,0:T(8,128)(2,1)S(1)}, u32[]{:S(2)}, u32[]{:S(2)}) %collective-permute-start.9) | collective-permute-done | bytes 393248 | tf_op jit(solution)/shard_map/ppermute | solution.py:411
  35.7 0.5 collective-permute-start.10
  36.2 3.3 %collective-permute-start.11 = (bf16[64,256]{1,0:T(8,128)(2,1)S(1)}, bf16[64,256]{1,0:T(8,128)(2,1)S(1)}, u32[]{:S(2)}, u32[]{:S(2)}) collective-permute-start(bf16[64,256]{1,0:T(8,128)(2,1)S(1)} %get-tuple-element.82), channel_id=1, source_target_pairs={{0,6},{1,3},{2,4},{3,1},{4,2},{5,7},{6,0},{7,5},{8,14},{9,11},{10,... | collective-permute-start | bytes 98312 | tf_op jit(solution)/shard_map/ppermute | solution.py:422
  39.6 1.5 %backward.1 = (bf16[128,128]{1,0:T(8,128)(2,1)S(1)}, bf16[128,128]{1,0:T(8,128)(2,1)S(1)}, f32[128,128]{1,0:T(8,128)S(1)}, f32[256,128]{1,0:T(8,128)S(1)}, f32[5...) custom-call(bf16[128,1024]{1,0:T(8,128)(2,1)S(1)} %get-tuple-element.64.refs_0_, ...), custom_call_target="tpu_custom_call" | custom-call | flops 335544320 | bytes 3408384 | tf_op jit(solution)/shard_map/backward/pallas_call | solution.py:66
  41.1 0.0 collective-permute-done.10.refs_2_.a
  41.1 1.0 %collective-permute-done.11.refs_3_.b = bf16[64,256]{1,0:T(8,128)(2,1)S(1)} collective-permute-done((bf16[64,256]{1,0:T(8,128)(2,1)S(1)}, bf16[64,256]{1,0:T(8,128)(2,1)S(1)}, u32[]{:S(2)}, u32[]{:S(2)}) %collective-permute-start.11) | collective-permute-done | bytes 32800 | tf_op jit(solution)/shard_map/ppermute | solution.py:422
  42.1 1.9 %collective-permute-start.14 = (bf16[128,256]{1,0:T(8,128)(2,1)S(1)}, bf16[128,256]{1,0:T(8,128)(2,1)S(1)}, u32[]{:S(2)}, u32[]{:S(2)}) collective-permute-start(bf16[128,256]{1,0:T(8,128)(2,1)S(1)} %get-tuple-element.85), channel_id=1, source_target_pairs={{0,4},{1,5},{2,6},{3,7},{4,0},{5,1},{6,2},{7,3},{8,12},{9,13},{10,... | collective-permute-start | bytes 196616 | tf_op jit(solution)/shard_map/ppermute | solution.py:422
  44.0 2.0 %collective-permute-start.12 = (bf16[128,384]{1,0:T(8,128)(2,1)S(1)}, bf16[128,384]{1,0:T(8,128)(2,1)S(1)}, u32[]{:S(2)}, u32[]{:S(2)}) collective-permute-start(bf16[128,384]{1,0:T(8,128)(2,1)S(1)} %get-tuple-element.83), channel_id=1, source_target_pairs={{0,2},{1,7},{2,0},{3,5},{4,6},{5,3},{6,4},{7,1},{8,10},{9,15},{10,... | collective-permute-start | bytes 294920 | tf_op jit(solution)/shard_map/ppermute | solution.py:422
  46.0 0.6 %collective-permute-start.13 = (bf16[128,384]{1,0:T(8,128)(2,1)S(1)}, bf16[128,384]{1,0:T(8,128)(2,1)S(1)}, u32[]{:S(2)}, u32[]{:S(2)}) collective-permute-start(bf16[128,384]{1,0:T(8,128)(2,1)S(1)} %get-tuple-element.84), channel_id=1, source_target_pairs={{0,6},{1,3},{2,4},{3,1},{4,2},{5,7},{6,0},{7,5},{8,14},{9,11},{10,... | collective-permute-start | bytes 294920 | tf_op jit(solution)/shard_map/ppermute | solution.py:422
  46.6 3.4 %collective-permute-done.14.c.refs_0_ = bf16[128,256]{1,0:T(8,128)(2,1)S(1)} collective-permute-done((bf16[128,256]{1,0:T(8,128)(2,1)S(1)}, bf16[128,256]{1,0:T(8,128)(2,1)S(1)}, u32[]{:S(2)}, u32[]{:S(2)}) %collective-permute-start.14) | collective-permute-done | bytes 65568 | tf_op jit(solution)/shard_map/ppermute | solution.py:422
  50.0 1.5 %collective-permute-start.15 = (bf16[64,256]{1,0:T(8,128)(2,1)S(1)}, bf16[64,256]{1,0:T(8,128)(2,1)S(1)}, u32[]{:S(2)}, u32[]{:S(2)}) collective-permute-start(bf16[64,256]{1,0:T(8,128)(2,1)S(1)} %weight_sum.1.first), channel_id=1, source_target_pairs={{0,8},{1,17},{8,0},{9,25},{16,24},{17,1},{24,16},{25,9},{2,10},{3,... | collective-permute-start | bytes 98312 | tf_op jit(solution)/shard_map/ppermute | solution.py:428
  51.5 2.4 %collective-permute-done.15.second = bf16[64,256]{1,0:T(8,128)(2,1)S(1)} collective-permute-done((bf16[64,256]{1,0:T(8,128)(2,1)S(1)}, bf16[64,256]{1,0:T(8,128)(2,1)S(1)}, u32[]{:S(2)}, u32[]{:S(2)}) %collective-permute-start.15) | collective-permute-done | bytes 32800 | tf_op jit(solution)/shard_map/ppermute | solution.py:428
  54.0 0.0 collective-permute-done.12.a
  54.0 0.0 collective-permute-done.13.b
  54.0 0.4 final.1
  54.3 0.1 collective-permute-start.16
  54.4 1.6 %collective-permute-start.17 = (bf16[64,512]{1,0:T(8,128)(2,1)S(1)}, bf16[64,512]{1,0:T(8,128)(2,1)S(1)}, u32[]{:S(2)}, u32[]{:S(2)}) collective-permute-start(bf16[64,512]{1,0:T(8,128)(2,1)S(1)} %both.1.refs_1_), channel_id=1, source_target_pairs={{0,16},{1,9},{8,24},{9,1},{16,0},{17,25},{24,8},{25,17},{2,18},{3,... | collective-permute-start | bytes 196616 | tf_op jit(solution)/shard_map/ppermute | solution.py:428
  56.0 0.0 collective-permute-done.16.pair
  56.0 0.8 %outputs.1 = (bf16[1,128,512]{2,1,0:T(8,128)(2,1)}, bf16[1,128,512]{2,1,0:T(8,128)(2,1)}, bf16[1,128,512]{2,1,0:T(8,128)(2,1)}) custom-call(bf16[128,768]{1,0:T(8,128)(2,1)S(1)} %get-tuple-element.87.own, bf16[128,768]{1,0:T(8,128)(2,1)S(1)} %collective-permute-done.16.pair), custom_call_target="tpu_custom_call" | custom-call | bytes 786432 | tf_op jit(solution)/shard_map/outputs/pallas_call | solution.py:66
  56.8 1.9 %collective-permute-done.17.got = bf16[64,512]{1,0:T(8,128)(2,1)S(1)} collective-permute-done((bf16[64,512]{1,0:T(8,128)(2,1)S(1)}, bf16[64,512]{1,0:T(8,128)(2,1)S(1)}, u32[]{:S(2)}, u32[]{:S(2)}) %collective-permute-start.17) | collective-permute-done | bytes 65568 | tf_op jit(solution)/shard_map/ppermute | solution.py:428
  58.8 0.7 %weight_join.1 = f32[64,1024]{1,0:T(8,128)} custom-call(bf16[64,512]{1,0:T(8,128)(2,1)S(1)} %both.1.refs_1_, bf16[64,512]{1,0:T(8,128)(2,1)S(1)} %collective-permute-done.17.got, bf16[1,128,512]{2,1,0:T(8,128)(2,1)} %get-tuple-element.44._), custom_call_target="tpu_custom_call" | custom-call | bytes 524288 | tf_op jit(solution)/shard_map/weight_join/pallas_call | solution.py:66
  (4 shorter events, 0.1 us)
Async XLA Ops:
  0.6 2.3 %collective-permute-start = (bf16[1,128,512]{2,1,0:T(8,128)(2,1)}, bf16[1,128,512]{2,1,0:T(8,128)(2,1)S(1)}, u32[]{:S(2)}, u32[]{:S(2)}) collective-permute-start(bf16[1,128,512]{2,1,0:T(8,128)(2,1)} %q.1), channel_id=1, source_target_pairs={{0,1},{1,0},{2,3},{3,2},{4,5},{5,4},{6,7},{7,6},{8,9},{9,8},{10,11... | collective-permute-start | bytes 393224 | tf_op jit(solution)/shard_map/ppermute | solution.py:411
  1.2 1.8 %collective-permute-start.1 = (bf16[1,128,512]{2,1,0:T(8,128)(2,1)}, bf16[1,128,512]{2,1,0:T(8,128)(2,1)S(1)}, u32[]{:S(2)}, u32[]{:S(2)}) collective-permute-start(bf16[1,128,512]{2,1,0:T(8,128)(2,1)} %k.1), channel_id=1, source_target_pairs={{0,1},{1,0},{2,3},{3,2},{4,5},{5,4},{6,7},{7,6},{8,9},{9,8},{10,11... | collective-permute-start | bytes 393224 | tf_op jit(solution)/shard_map/ppermute | solution.py:411
  1.2 1.7 %collective-permute-start.2 = (bf16[1,128,512]{2,1,0:T(8,128)(2,1)}, bf16[1,128,512]{2,1,0:T(8,128)(2,1)S(1)}, u32[]{:S(2)}, u32[]{:S(2)}) collective-permute-start(bf16[1,128,512]{2,1,0:T(8,128)(2,1)} %v.1), channel_id=1, source_target_pairs={{0,1},{1,0},{2,3},{3,2},{4,5},{5,4},{6,7},{7,6},{8,9},{9,8},{10,11... | collective-permute-start | bytes 393224 | tf_op jit(solution)/shard_map/ppermute | solution.py:411
  1.7 7.2 %collective-permute-start.3 = (bf16[128,1024]{1,0:T(8,128)(2,1)}, bf16[128,1024]{1,0:T(8,128)(2,1)S(1)}, u32[]{:S(2)}, u32[]{:S(2)}) collective-permute-start(bf16[128,1024]{1,0:T(8,128)(2,1)} %bitcast.1), channel_id=1, source_target_pairs={{0,1},{1,0},{2,3},{3,2},{4,5},{5,4},{6,7},{7,6},{8,9},{9,8},{10,11... | collective-permute-start | bytes 786440 | tf_op jit(solution)/shard_map/ppermute | solution.py:411
  3.2 6.0 %collective-permute-start.4 = (bf16[128,512]{1,0:T(8,128)(2,1)S(1)}, bf16[128,512]{1,0:T(8,128)(2,1)S(1)}, u32[]{:S(2)}, u32[]{:S(2)}) collective-permute-start(bf16[128,512]{1,0:T(8,128)(2,1)S(1)} %get-tuple-element.52), channel_id=1, source_target_pairs={{0,2},{1,7},{2,0},{3,5},{4,6},{5,3},{6,4},{7,1},{8,10},{9,15},{10,... | collective-permute-start | bytes 393224 | tf_op jit(solution)/shard_map/ppermute | solution.py:422
  6.3 9.4 %collective-permute-start.5 = (bf16[128,512]{1,0:T(8,128)(2,1)S(1)}, bf16[128,512]{1,0:T(8,128)(2,1)S(1)}, u32[]{:S(2)}, u32[]{:S(2)}) collective-permute-start(bf16[128,512]{1,0:T(8,128)(2,1)S(1)} %get-tuple-element.53), channel_id=1, source_target_pairs={{0,6},{1,3},{2,4},{3,1},{4,2},{5,7},{6,0},{7,5},{8,14},{9,11},{10,... | collective-permute-start | bytes 393224 | tf_op jit(solution)/shard_map/ppermute | solution.py:422
  8.8 8.1 %collective-permute-start.6 = (bf16[128,256]{1,0:T(8,128)(2,1)S(1)}, bf16[128,256]{1,0:T(8,128)(2,1)S(1)}, u32[]{:S(2)}, u32[]{:S(2)}) collective-permute-start(bf16[128,256]{1,0:T(8,128)(2,1)S(1)} %get-tuple-element.58), channel_id=1, source_target_pairs={{0,4},{1,5},{2,6},{3,7},{4,0},{5,1},{6,2},{7,3},{8,12},{9,13},{10,... | collective-permute-start | bytes 196616 | tf_op jit(solution)/shard_map/ppermute | solution.py:422
  17.7 8.2 %collective-permute-start.7 = (bf16[256,768]{1,0:T(8,128)(2,1)S(1)}, bf16[256,768]{1,0:T(8,128)(2,1)S(1)}, u32[]{:S(2)}, u32[]{:S(2)}) collective-permute-start(bf16[256,768]{1,0:T(8,128)(2,1)S(1)} %get-tuple-element.61.sent), channel_id=1, source_target_pairs={{0,8},{1,17},{8,0},{9,25},{16,24},{17,1},{24,16},{25,9},{2,10},{3,... | collective-permute-start | bytes 1179656 | tf_op jit(solution)/shard_map/ppermute | solution.py:428
  25.9 7.8 %collective-permute-start.8 = (bf16[256,768]{1,0:T(8,128)(2,1)S(1)}, bf16[256,768]{1,0:T(8,128)(2,1)S(1)}, u32[]{:S(2)}, u32[]{:S(2)}) collective-permute-start(bf16[256,768]{1,0:T(8,128)(2,1)S(1)} %get-tuple-element.63.sent), channel_id=1, source_target_pairs={{0,16},{1,9},{8,24},{9,1},{16,0},{17,25},{24,8},{25,17},{2,18},{3,... | collective-permute-start | bytes 1179656 | tf_op jit(solution)/shard_map/ppermute | solution.py:428
  33.9 1.8 %collective-permute-start.9 = (bf16[128,1536]{1,0:T(8,128)(2,1)S(1)}, bf16[128,1536]{1,0:T(8,128)(2,1)S(1)}, u32[]{:S(2)}, u32[]{:S(2)}) collective-permute-start(bf16[128,1536]{1,0:T(8,128)(2,1)S(1)} %get-tuple-element.65), channel_id=1, source_target_pairs={{0,1},{1,0},{2,3},{3,2},{4,5},{5,4},{6,7},{7,6},{8,9},{9,8},{10,11... | collective-permute-start | bytes 1179656 | tf_op jit(solution)/shard_map/ppermute | solution.py:411
  35.7 5.3 %collective-permute-start.10 = (bf16[64,256]{1,0:T(8,128)(2,1)S(1)}, bf16[64,256]{1,0:T(8,128)(2,1)S(1)}, u32[]{:S(2)}, u32[]{:S(2)}) collective-permute-start(bf16[64,256]{1,0:T(8,128)(2,1)S(1)} %get-tuple-element.81), channel_id=1, source_target_pairs={{0,2},{1,7},{2,0},{3,5},{4,6},{5,3},{6,4},{7,1},{8,10},{9,15},{10,... | collective-permute-start | bytes 98312 | tf_op jit(solution)/shard_map/ppermute | solution.py:422
  36.2 5.8 %collective-permute-start.11 = (bf16[64,256]{1,0:T(8,128)(2,1)S(1)}, bf16[64,256]{1,0:T(8,128)(2,1)S(1)}, u32[]{:S(2)}, u32[]{:S(2)}) collective-permute-start(bf16[64,256]{1,0:T(8,128)(2,1)S(1)} %get-tuple-element.82), channel_id=1, source_target_pairs={{0,6},{1,3},{2,4},{3,1},{4,2},{5,7},{6,0},{7,5},{8,14},{9,11},{10,... | collective-permute-start | bytes 98312 | tf_op jit(solution)/shard_map/ppermute | solution.py:422
  42.1 7.8 %collective-permute-start.14 = (bf16[128,256]{1,0:T(8,128)(2,1)S(1)}, bf16[128,256]{1,0:T(8,128)(2,1)S(1)}, u32[]{:S(2)}, u32[]{:S(2)}) collective-permute-start(bf16[128,256]{1,0:T(8,128)(2,1)S(1)} %get-tuple-element.85), channel_id=1, source_target_pairs={{0,4},{1,5},{2,6},{3,7},{4,0},{5,1},{6,2},{7,3},{8,12},{9,13},{10,... | collective-permute-start | bytes 196616 | tf_op jit(solution)/shard_map/ppermute | solution.py:422
  44.0 10.0 %collective-permute-start.12 = (bf16[128,384]{1,0:T(8,128)(2,1)S(1)}, bf16[128,384]{1,0:T(8,128)(2,1)S(1)}, u32[]{:S(2)}, u32[]{:S(2)}) collective-permute-start(bf16[128,384]{1,0:T(8,128)(2,1)S(1)} %get-tuple-element.83), channel_id=1, source_target_pairs={{0,2},{1,7},{2,0},{3,5},{4,6},{5,3},{6,4},{7,1},{8,10},{9,15},{10,... | collective-permute-start | bytes 294920 | tf_op jit(solution)/shard_map/ppermute | solution.py:422
  46.0 8.0 %collective-permute-start.13 = (bf16[128,384]{1,0:T(8,128)(2,1)S(1)}, bf16[128,384]{1,0:T(8,128)(2,1)S(1)}, u32[]{:S(2)}, u32[]{:S(2)}) collective-permute-start(bf16[128,384]{1,0:T(8,128)(2,1)S(1)} %get-tuple-element.84), channel_id=1, source_target_pairs={{0,6},{1,3},{2,4},{3,1},{4,2},{5,7},{6,0},{7,5},{8,14},{9,11},{10,... | collective-permute-start | bytes 294920 | tf_op jit(solution)/shard_map/ppermute | solution.py:422
  50.0 4.0 %collective-permute-start.15 = (bf16[64,256]{1,0:T(8,128)(2,1)S(1)}, bf16[64,256]{1,0:T(8,128)(2,1)S(1)}, u32[]{:S(2)}, u32[]{:S(2)}) collective-permute-start(bf16[64,256]{1,0:T(8,128)(2,1)S(1)} %weight_sum.1.first), channel_id=1, source_target_pairs={{0,8},{1,17},{8,0},{9,25},{16,24},{17,1},{24,16},{25,9},{2,10},{3,... | collective-permute-start | bytes 98312 | tf_op jit(solution)/shard_map/ppermute | solution.py:428
  54.3 1.7 %collective-permute-start.16 = (bf16[128,768]{1,0:T(8,128)(2,1)S(1)}, bf16[128,768]{1,0:T(8,128)(2,1)S(1)}, u32[]{:S(2)}, u32[]{:S(2)}) collective-permute-start(bf16[128,768]{1,0:T(8,128)(2,1)S(1)} %get-tuple-element.88), channel_id=1, source_target_pairs={{0,1},{1,0},{2,3},{3,2},{4,5},{5,4},{6,7},{7,6},{8,9},{9,8},{10,11... | collective-permute-start | bytes 589832 | tf_op jit(solution)/shard_map/ppermute | solution.py:411
  54.4 4.3 %collective-permute-start.17 = (bf16[64,512]{1,0:T(8,128)(2,1)S(1)}, bf16[64,512]{1,0:T(8,128)(2,1)S(1)}, u32[]{:S(2)}, u32[]{:S(2)}) collective-permute-start(bf16[64,512]{1,0:T(8,128)(2,1)S(1)} %both.1.refs_1_), channel_id=1, source_target_pairs={{0,16},{1,9},{8,24},{9,1},{16,0},{17,25},{24,8},{25,17},{2,18},{3,... | collective-permute-start | bytes 196616 | tf_op jit(solution)/shard_map/ppermute | solution.py:428

commit v11 on v9

--- a/solution.py
+++ b/solution.py
@@ -314,38 +314,53 @@
     soft_backward(qs, ks, vs, probs, attn, dattn, dq_soft, dk_soft, dv_soft)
 
 
-def halo_kernel(direct, dk_soft, dv_soft, *refs):
-    way = links(direct)
-    span = dk_soft.shape[0]
-    if direct:
-        dstate, *_, to_a, to_b, to_c = refs
-        to_c[...] = dstate[...].astype(BF)
-    else:
-        to_a, to_b = refs
-    for out, side in ((to_a, way["halo_a"]), (to_b, way["halo_b"])):
-        first = side * (span - HALF)
-        out[:, :DH] = dk_soft[at(first), :].astype(BF)
-        out[:, DH : 2 * DH] = dv_soft[at(first), :].astype(BF)
-        if direct:
-            out[:, 2 * DH :] = dstate[...].astype(BF)
-
-
-def chunk_kernel(own, got, to_a, to_b, to_c, chunk, heads):
+def halo_part(out, first, dk_soft, dv_soft, side):
+    start = side * (dk_soft.shape[0] - HALF)
+    out[:, first : first + DH] = dk_soft[at(start), :].astype(BF)
+    out[:, first + DH : first + 2 * DH] = dv_soft[at(start), :].astype(BF)
+
+
+def halo_kernel(dk_soft, dv_soft, to_a, to_b):
+    way = links(False)
+    halo_part(to_a, 0, dk_soft, dv_soft, way["halo_a"])
+    halo_part(to_b, 0, dk_soft, dv_soft, way["halo_b"])
+
+
+def chunk_kernel(own, got, send, keep, heads):
     core, z, _ = places()
     way = links(True)
-    half = chunk.shape[0]
+    half = own.shape[0] // 2
     for group in range(2):
         rows = slice(group * half, (group + 1) * half)
         heads[2 * group + core] = own[rows, :]
         heads[2 * group + 1 - core] = got[rows, :]
-    chunk[...] = heads[z]
-    for out, step in ((to_a, way["first"]), (to_b, way["second"]), (to_c, 2)):
-        out[...] = heads[z ^ step].astype(BF)
-
-
-def weight_sum_kernel(scale, chunk, a, b, c, out):
-    total = chunk[...] + a[...].astype(F32) + b[...].astype(F32) + c[...].astype(F32)
-    out[...] = (scale * total).astype(out.dtype)
+    for index, step in enumerate((way["first"], 2)):
+        send[index * half : (index + 1) * half, :] = heads[z ^ step].astype(BF)
+    for index, step in enumerate((0, way["second"])):
+        keep[index * half : (index + 1) * half, :] = heads[z ^ step]
+
+
+def second_kernel(keep, got, dstate, dk_soft, dv_soft, chunk, send):
+    way = links(True)
+    half = chunk.shape[0]
+    chunk[...] = keep[:half, :] + got[:half, :].astype(F32)
+    for side in range(2):
+        cols, rows = slice(side * DH, (side + 1) * DH), slice(side * half, (side + 1) * half)
+        piece = keep[half:, cols] + got[half:, cols].astype(F32)
+        send[rows, 3 * DH :] = piece.astype(BF)
+    halo_part(send, 0, dk_soft, dv_soft, way["halo_b"])
+    send[:, 2 * DH : 3 * DH] = dstate[...].astype(BF)
+
+
+def third_kernel(scale, chunk, got, dstate, dk_soft, dv_soft, summed, total, send):
+    way = links(True)
+    half = chunk.shape[0]
+    for side in range(2):
+        cols, rows = slice(side * DH, (side + 1) * DH), slice(side * half, (side + 1) * half)
+        summed[:, cols] = (scale * (chunk[:, cols] + got[rows, 3 * DH :].astype(F32))).astype(summed.dtype)
+    total[...] = dstate[...] + got[:, 2 * DH : 3 * DH].astype(F32)
+    halo_part(send, 0, dk_soft, dv_soft, way["halo_a"])
+    send[:, 2 * DH :] = total[...].astype(BF)
 
 
 def final_kernel(
@@ -357,8 +372,7 @@
     total = dstate[...]
     own_out, pair_out, dk_all, dv_all = refs[-4:]
     if direct:
-        total = total + a[:, 2 * DH :].astype(F32) + b[:, 2 * DH :].astype(F32)
-        total = total + refs[0][...].astype(F32)
+        total = total + a[:, 2 * DH :].astype(F32)
     for source, out, cols in ((dk_soft, dk_all, slice(0, DH)), (dv_soft, dv_all, slice(DH, 2 * DH))):
         out[...] = source[HALF : HALF + 2 * rows, :]
         out[at(way["block_a"] * rows, rows), :] += a[:, cols].astype(F32)
@@ -383,7 +397,7 @@
             out[0, :, at(SOFT + first)] = source[:, (3 + index) * DH : (4 + index) * DH]
 
 
-def weight_join_kernel(both, got, out):
+def weight_join_kernel(both, got, _, out):
     _, _, dp = places()
     way = links(True)
     width = both.shape[1] // 2
@@ -499,23 +513,12 @@
             scratch=[pltpu.VMEM((2 * DH, width), F32)],
         )
         row_recv = over_core(row_send)
-        *to_chips, chunk = call(
-            chunk_kernel, "chunk", [like((half, width), BF)] * 3 + [like((half, width), F32)],
+        piece_send, piece_keep = call(
+            chunk_kernel, "chunk", [like((DH, width), BF), like((DH, width), F32)],
             [row_own, row_recv], scratch=[pltpu.VMEM((HEADS, half, width), F32)],
         )
-        chunks = [over_z(value, which) for which, value in enumerate(to_chips)]
-        summed = call(
-            functools.partial(weight_sum_kernel, scale), "weight_sum", [like((half, width), BF)],
-            [chunk] + chunks,
-        )[0]
-        got = over_dp(summed, 0)
-        both = call(join_kernel, "both", [like((half, 2 * width), BF)], [summed, got])[0]
-        gathered = over_dp(both, 1)
-        weight_grad = call(
-            weight_join_kernel, "weight_join", [like((half, model), F32)], [both, gathered]
-        )[0]
-    if direct:
-        weights.append(chunk)
+        piece_got = over_z(piece_send, 0)
+        weights.append(piece_keep)
     dq_lin, dq_lin_pair, dstate, dq_soft, dk_soft, dv_soft = call(
         functools.partial(backward_kernel, direct), "backward",
         [
@@ -528,13 +531,24 @@
         flops=5 * wg_flops,
     )
     wide = 3 * DH if direct else 2 * DH
-    to_a, to_b, *to_c = call(
-        functools.partial(halo_kernel, direct), "halo",
-        [like((rows, wide), BF), like((rows, wide), BF)] + [like((DH, DH), BF)] * direct,
-        [dk_soft, dv_soft] + ([dstate] + chunks if direct else []),
-    )
-    a, b = over_z(to_a, 0, True), over_z(to_b, 1, True)
-    c = [over_z(value, 2) for value in to_c]
+    if direct:
+        chunk, to_b = call(
+            second_kernel, "second", [like((half, width), F32), like((rows, 4 * DH), BF)],
+            [piece_keep, piece_got, dstate, dk_soft, dv_soft],
+        )
+        b = over_z(to_b, 1)
+        summed, dstate, to_a = call(
+            functools.partial(third_kernel, scale), "third",
+            [like((half, width), BF), like((DH, DH), F32), like((rows, 3 * DH), BF)],
+            [chunk, b, dstate, dk_soft, dv_soft],
+        )
+        a = over_z(to_a, 0)
+        got = over_dp(summed, 0)
+        both = call(join_kernel, "both", [like((half, 2 * width), BF)], [summed, got])[0]
+        gathered = over_dp(both, 1)
+    else:
+        to_a, to_b = call(halo_kernel, "halo", [like((rows, 2 * DH), BF)] * 2, [dk_soft, dv_soft])
+        a, b = over_z(to_a, 0, True), over_z(to_b, 1, True)
     if not direct:
         dstate = lax.psum(dstate, "z")
         groups = jnp.stack([keep_soft, keep_lin])
@@ -546,14 +560,19 @@
     own_out, to_pair = call(
         functools.partial(final_kernel, direct), "final",
         [like((rows, 6 * DH), BF), like((rows, 6 * DH), BF)],
-        [dstate, mine, pair, dq_soft, dk_soft, dv_soft, dq_lin, dq_lin_pair, a, b] + c
-        + ([gathered] if direct else []),
+        [dstate, mine, pair, dq_soft, dk_soft, dv_soft, dq_lin, dq_lin_pair, a, b]
+        + ([both] if direct else []),
         scratch=[pltpu.VMEM((2 * rows, DH), F32)] * 2,
         flops=wg_flops // 4,
     )
     from_pair = over_core(to_pair)
     shape = like((1, rows, HEADS * DH), BF)
     dq, dk, dv = call(output_kernel, "outputs", [shape] * 3, [own_out, from_pair])
+    if direct:
+        weight_grad = call(
+            weight_join_kernel, "weight_join", [like((half, model), F32)], [both, gathered, hbm(dq)],
+            spaces=[vmem, vmem, pl.BlockSpec(memory_space=pltpu.HBM)],
+        )[0]
     return dq, dk, dv, weight_grad
 
 

time: 53.7 us -> 53 us (0.987)
  starting transfers between devices: 24.3 us -> 21.1 us
  waiting for transfers between devices: 21.4 us -> 23.9 us
    ppermute x6, waiting for transfers between devices: 4.85 us -> 9.12 us  [over_dp(): return lax.ppermute(value, ('dp', 'core'), pairs)]
    ppermute x9 -> x6, starting transfers between devices: 12.7 us -> 9.67 us  [over_z(): return lax.ppermute(value, axes, pairs)]
    ppermute x9 -> x6, waiting for transfers between devices: 13.3 us -> 12.2 us  [over_z(): return lax.ppermute(value, axes, pairs)]
    ppermute x7, waiting for transfers between devices: 3.28 us -> 2.59 us  [over_core(): return lax.ppermute(value, 'core', pair_perm)]
  transfers between devices with their start and end apart: 22 -> 19, of which waited for: 12 -> 13; matrix products, arithmetic and copies ran while one was open for 0% -> 0% of each run, Pallas kernels for 10% -> 10%
where the time goes in v11:
time: 53 us; the launch traced here: 52.8 us
  waiting for transfers between devices  23.9 us (45%)
  starting transfers between devices  21.1 us (40%)
  Pallas kernels  7.04 us (13%)
  between operations  0.78 us (1%)
    ppermute x6, waiting for transfers between devices, over_z(): return lax.ppermute(value, axes, pairs)  12.2 us
    ppermute x6, starting transfers between devices, over_dp(): return lax.ppermute(value, ('dp', 'core'), pairs)  10.1 us
    ppermute x6, starting transfers between devices, over_z(): return lax.ppermute(value, axes, pairs)  9.67 us
    ppermute x6, waiting for transfers between devices, over_dp(): return lax.ppermute(value, ('dp', 'core'), pairs)  9.12 us
    pallas_call x17, Pallas kernels, call(): pl.pallas_call(kernel, name=name, out_shape=list(outs), in_specs=spaces o...  7.04 us
    ppermute x7, waiting for transfers between devices, over_core(): return lax.ppermute(value, 'core', pair_perm)  2.59 us
    ppermute x7, starting transfers between devices, over_core(): return lax.ppermute(value, 'core', pair_perm)  1.32 us
  transfers between devices with their start and end apart: 19, of which 13 were waited for; matrix products, arithmetic and copies ran while one was open for 0% of the time, Pallas kernels for 10%

profile of v11, /device:TPU:0, one launch (start us, length us, event | category | flops | bytes accessed | tf_op | source)
XLA Modules:
  0.0 52.8 jit_solution(6055334406801965891)
XLA Ops:
  0.6 0.5 collective-permute-start
  1.2 0.1 collective-permute-start.1
  1.2 0.4 collective-permute-start.2
  1.7 0.1 collective-permute-start.3
  1.7 1.2 %pack.1 = (bf16[128,768]{1,0:T(8,128)(2,1)S(1)}, bf16[128,1024]{1,0:T(8,128)(2,1)S(1)}, bf16[64,256]{1,0:T(8,128)(2,1)S(1)}, f32[1,128]{1,0:T(1,128)S(1)}) custom-call(bf16[1,128,512]{2,1,0:T(8,128)(2,1)} %q.1, bf16[1,128,512]{2,1,0:T(8,128)(2,1)} %k.1, bf16[1,128,512]{2,1,0:T(8,128)(2,1)} %v.1, bf16[1,128,1024]{2,1,0:T(8,128)(2,1)} %og.1, ...), custom_call_target="tpu_custom_call" | custom-call | bytes 1279488 | tf_op jit(solution)/shard_map/pack/pallas_call | solution.py:66
  2.9 0.0 collective-permute-done.q_pair
  2.9 0.0 collective-permute-done.1.k_pair
  2.9 0.0 collective-permute-done.2.v_pair
  3.0 0.3 state.1
  3.2 3.1 %collective-permute-start.4 = (bf16[128,512]{1,0:T(8,128)(2,1)S(1)}, bf16[128,512]{1,0:T(8,128)(2,1)S(1)}, u32[]{:S(2)}, u32[]{:S(2)}) collective-permute-start(bf16[128,512]{1,0:T(8,128)(2,1)S(1)} %get-tuple-element.53), channel_id=1, source_target_pairs={{0,2},{1,7},{2,0},{3,5},{4,6},{5,3},{6,4},{7,1},{8,10},{9,15},{10,... | collective-permute-start | bytes 393224 | tf_op jit(solution)/shard_map/ppermute | solution.py:431
  6.3 2.5 %collective-permute-start.5 = (bf16[128,512]{1,0:T(8,128)(2,1)S(1)}, bf16[128,512]{1,0:T(8,128)(2,1)S(1)}, u32[]{:S(2)}, u32[]{:S(2)}) collective-permute-start(bf16[128,512]{1,0:T(8,128)(2,1)S(1)} %get-tuple-element.54), channel_id=1, source_target_pairs={{0,6},{1,3},{2,4},{3,1},{4,2},{5,7},{6,0},{7,5},{8,14},{9,11},{10,... | collective-permute-start | bytes 393224 | tf_op jit(solution)/shard_map/ppermute | solution.py:431
  8.8 0.1 collective-permute-start.6
  8.9 0.0 collective-permute-done.3.og_recv
  8.9 0.4 collective-permute-done.4.a.refs_0_
  9.3 6.5 %collective-permute-done.5.b.refs_1_ = bf16[128,512]{1,0:T(8,128)(2,1)S(1)} collective-permute-done((bf16[128,512]{1,0:T(8,128)(2,1)S(1)}, bf16[128,512]{1,0:T(8,128)(2,1)S(1)}, u32[]{:S(2)}, u32[]{:S(2)}) %collective-permute-start.5) | collective-permute-done | bytes 131104 | tf_op jit(solution)/shard_map/ppermute | solution.py:431
  15.7 1.2 %soft_forward.1 = (bf16[256,128]{1,0:T(8,128)(2,1)S(1)}, bf16[512,128]{1,0:T(8,128)(2,1)S(1)}, bf16[512,128]{1,0:T(8,128)(2,1)S(1)}, bf16[256,1024]{1,0:T(8,128)...) custom-call(bf16[128,768]{1,0:T(8,128)(2,1)S(1)} %get-tuple-element., ...), custom_call_target="tpu_custom_call" | custom-call | flops 67108864 | bytes 2949120 | tf_op jit(solution)/shard_map/soft_forward/pallas_call | solution.py:66
  16.9 0.0 collective-permute-done.6.refs_2_.c
  16.9 0.7 %lin_forward.1 = (f32[256,128]{1,0:T(8,128)S(1)}, f32[128,128]{1,0:T(8,128)S(1)}, f32[128,512]{1,0:T(8,128)S(1)}, bf16[256,512]{1,0:T(8,128)(2,1)S(1)}) custom-call(f32[128,128]{1,0:T(8,128)S(1)} %get-tuple-element.56.state, bf16[128,768]{1,0:T(8,128)(2,1)S(1)} %get-tuple-element.49.mine.refs_6_, bf16[128,768]{1,0:T(8,128)(2,1)S(1)} %get-tuple-element.51.pair.refs_7_, ...), custom_call_target="tpu_custom_call" | custom-call | flops 67108864 | bytes 2163200 | tf_op jit(solution)/shard_map/lin_forward/pallas_call | solution.py:66
  17.6 1.6 %collective-permute-start.7 = (bf16[256,512]{1,0:T(8,128)(2,1)S(1)}, bf16[256,512]{1,0:T(8,128)(2,1)S(1)}, u32[]{:S(2)}, u32[]{:S(2)}) collective-permute-start(bf16[256,512]{1,0:T(8,128)(2,1)S(1)} %get-tuple-element.62), channel_id=1, source_target_pairs={{0,8},{1,17},{8,0},{9,25},{16,24},{17,1},{24,16},{25,9},{2,10},{3,... | collective-permute-start | bytes 786440 | tf_op jit(solution)/shard_map/ppermute | solution.py:437
  19.2 0.1 collective-permute-start.11
  19.3 1.2 %collective-permute-done.11.got = bf16[2,64,256]{2,1,0:T(8,128)(2,1)S(1)} collective-permute-done((bf16[2,64,256]{2,1,0:T(8,128)(2,1)S(1)}, bf16[2,64,256]{2,1,0:T(8,128)(2,1)S(1)}, u32[]{:S(2)}, u32[]{:S(2)}) %collective-permute-start.11) | collective-permute-done | bytes 65568 | tf_op jit(solution)/shard_map/ppermute | solution.py:420
  20.6 0.6 %collective-permute-start.12 = (bf16[256,256]{1,0:T(8,128)(2,1)S(1)}, bf16[256,256]{1,0:T(8,128)(2,1)S(1)}, u32[]{:S(2)}, u32[]{:S(2)}) collective-permute-start(bf16[256,256]{1,0:T(8,128)(2,1)S(1)} %w_rows.1.first), channel_id=1, source_target_pairs={{0,8},{1,17},{8,0},{9,25},{16,24},{17,1},{24,16},{25,9},{2,10},{3,... | collective-permute-start | bytes 393224 | tf_op jit(solution)/shard_map/ppermute | solution.py:437
  21.2 2.9 %collective-permute-done.7.got = bf16[256,512]{1,0:T(8,128)(2,1)S(1)} collective-permute-done((bf16[256,512]{1,0:T(8,128)(2,1)S(1)}, bf16[256,512]{1,0:T(8,128)(2,1)S(1)}, u32[]{:S(2)}, u32[]{:S(2)}) %collective-permute-start.7) | collective-permute-done | bytes 262176 | tf_op jit(solution)/shard_map/ppermute | solution.py:437
  24.1 0.1 fold.1
  24.1 1.9 %collective-permute-start.8 = (bf16[256,256]{1,0:T(8,128)(2,1)S(1)}, bf16[256,256]{1,0:T(8,128)(2,1)S(1)}, u32[]{:S(2)}, u32[]{:S(2)}) collective-permute-start(bf16[256,256]{1,0:T(8,128)(2,1)S(1)} %get-tuple-element.64.refs_0_), channel_id=1, source_target_pairs={{0,16},{1,9},{8,24},{9,1},{16,0},{17,25},{24,8},{25,17},{2,18},{3,... | collective-permute-start | bytes 393224 | tf_op jit(solution)/shard_map/ppermute | solution.py:437
  26.0 0.5 %collective-permute-done.12.second = bf16[256,256]{1,0:T(8,128)(2,1)S(1)} collective-permute-done((bf16[256,256]{1,0:T(8,128)(2,1)S(1)}, bf16[256,256]{1,0:T(8,128)(2,1)S(1)}, u32[]{:S(2)}, u32[]{:S(2)}) %collective-permute-start.12) | collective-permute-done | bytes 131104 | tf_op jit(solution)/shard_map/ppermute | solution.py:437
  26.5 1.9 %collective-permute-start.13 = (bf16[256,512]{1,0:T(8,128)(2,1)S(1)}, bf16[256,512]{1,0:T(8,128)(2,1)S(1)}, u32[]{:S(2)}, u32[]{:S(2)}) collective-permute-start(bf16[256,512]{1,0:T(8,128)(2,1)S(1)} %w_half.1.refs_0_), channel_id=1, source_target_pairs={{0,16},{1,9},{8,24},{9,1},{16,0},{17,25},{24,8},{25,17},{2,18},{3,... | collective-permute-start | bytes 786440 | tf_op jit(solution)/shard_map/ppermute | solution.py:437
  28.5 0.7 %collective-permute-done.8.got = bf16[256,256]{1,0:T(8,128)(2,1)S(1)} collective-permute-done((bf16[256,256]{1,0:T(8,128)(2,1)S(1)}, bf16[256,256]{1,0:T(8,128)(2,1)S(1)}, u32[]{:S(2)}, u32[]{:S(2)}) %collective-permute-start.8) | collective-permute-done | bytes 131104 | tf_op jit(solution)/shard_map/ppermute | solution.py:437
  29.2 0.1 rows.1
  29.2 0.1 collective-permute-start.9
  29.3 1.3 %collective-permute-done.9.got = f32[128,256]{1,0:T(8,128)S(1)} collective-permute-done((f32[128,256]{1,0:T(8,128)S(1)}, f32[128,256]{1,0:T(8,128)S(1)}, u32[]{:S(2)}, u32[]{:S(2)}) %collective-permute-start.9) | collective-permute-done | bytes 131104 | tf_op jit(solution)/shard_map/ppermute | solution.py:420
  30.7 0.8 %collective-permute-start.10 = (bf16[128,256]{1,0:T(8,128)(2,1)S(1)}, bf16[128,256]{1,0:T(8,128)(2,1)S(1)}, u32[]{:S(2)}, u32[]{:S(2)}) collective-permute-start(bf16[128,256]{1,0:T(8,128)(2,1)S(1)} %get-tuple-element.68), channel_id=1, source_target_pairs={{0,2},{1,7},{2,0},{3,5},{4,6},{5,3},{6,4},{7,1},{8,10},{9,15},{10,... | collective-permute-start | bytes 196616 | tf_op jit(solution)/shard_map/ppermute | solution.py:431
  31.5 1.5 %collective-permute-done.13.refs_1_ = bf16[256,512]{1,0:T(8,128)(2,1)S(1)} collective-permute-done((bf16[256,512]{1,0:T(8,128)(2,1)S(1)}, bf16[256,512]{1,0:T(8,128)(2,1)S(1)}, u32[]{:S(2)}, u32[]{:S(2)}) %collective-permute-start.13) | collective-permute-done | bytes 262176 | tf_op jit(solution)/shard_map/ppermute | solution.py:437
  33.0 1.5 %backward.1 = (bf16[128,128]{1,0:T(8,128)(2,1)S(1)}, bf16[128,128]{1,0:T(8,128)(2,1)S(1)}, f32[128,128]{1,0:T(8,128)S(1)}, f32[256,128]{1,0:T(8,128)S(1)}, f32[5...) custom-call(bf16[256,512]{1,0:T(8,128)(2,1)S(1)} %w_half.1.refs_0_, bf16[256,512]{1,0:T(8,128)(2,1)S(1)} %collective-permute-done.13.refs_1_, ...), custom_call_target="tpu_custom_call" | custom-call | flops 335544320 | bytes 3408384 | tf_op jit(solution)/shard_map/backward/pallas_call | solution.py:66
  34.5 0.5 collective-permute-done.10.got
  35.0 3.1 %collective-permute-start.14 = (bf16[128,512]{1,0:T(8,128)(2,1)S(1)}, bf16[128,512]{1,0:T(8,128)(2,1)S(1)}, u32[]{:S(2)}, u32[]{:S(2)}) collective-permute-start(bf16[128,512]{1,0:T(8,128)(2,1)S(1)} %get-tuple-element.82), channel_id=1, source_target_pairs={{0,6},{1,3},{2,4},{3,1},{4,2},{5,7},{6,0},{7,5},{8,14},{9,11},{10,... | collective-permute-start | bytes 393224 | tf_op jit(solution)/shard_map/ppermute | solution.py:431
  38.1 4.5 %collective-permute-done.14.got.b = bf16[128,512]{1,0:T(8,128)(2,1)S(1)} collective-permute-done((bf16[128,512]{1,0:T(8,128)(2,1)S(1)}, bf16[128,512]{1,0:T(8,128)(2,1)S(1)}, u32[]{:S(2)}, u32[]{:S(2)}) %collective-permute-start.14) | collective-permute-done | bytes 131104 | tf_op jit(solution)/shard_map/ppermute | solution.py:431
  42.6 0.1 collective-permute-start.15
  42.7 2.3 %collective-permute-start.16 = (bf16[64,256]{1,0:T(8,128)(2,1)S(1)}, bf16[64,256]{1,0:T(8,128)(2,1)S(1)}, u32[]{:S(2)}, u32[]{:S(2)}) collective-permute-start(bf16[64,256]{1,0:T(8,128)(2,1)S(1)} %get-tuple-element.88.first), channel_id=1, source_target_pairs={{0,8},{1,17},{8,0},{9,25},{16,24},{17,1},{24,16},{25,9},{2,10},{3,... | collective-permute-start | bytes 98312 | tf_op jit(solution)/shard_map/ppermute | solution.py:437
  45.0 1.9 %collective-permute-done.16.second = bf16[64,256]{1,0:T(8,128)(2,1)S(1)} collective-permute-done((bf16[64,256]{1,0:T(8,128)(2,1)S(1)}, bf16[64,256]{1,0:T(8,128)(2,1)S(1)}, u32[]{:S(2)}, u32[]{:S(2)}) %collective-permute-start.16) | collective-permute-done | bytes 32800 | tf_op jit(solution)/shard_map/ppermute | solution.py:437
  46.9 0.4 collective-permute-done.15.a
  47.3 0.3 final.1
  47.7 0.1 collective-permute-start.17
  47.8 1.9 %collective-permute-start.18 = (bf16[64,512]{1,0:T(8,128)(2,1)S(1)}, bf16[64,512]{1,0:T(8,128)(2,1)S(1)}, u32[]{:S(2)}, u32[]{:S(2)}) collective-permute-start(bf16[64,512]{1,0:T(8,128)(2,1)S(1)} %both.1.refs_0_), channel_id=1, source_target_pairs={{0,16},{1,9},{8,24},{9,1},{16,0},{17,25},{24,8},{25,17},{2,18},{3,... | collective-permute-start | bytes 196616 | tf_op jit(solution)/shard_map/ppermute | solution.py:437
  49.6 0.0 collective-permute-done.17.pair
  49.6 0.8 %outputs.1 = (bf16[1,128,512]{2,1,0:T(8,128)(2,1)}, bf16[1,128,512]{2,1,0:T(8,128)(2,1)}, bf16[1,128,512]{2,1,0:T(8,128)(2,1)}) custom-call(bf16[128,768]{1,0:T(8,128)(2,1)S(1)} %get-tuple-element.89.own, bf16[128,768]{1,0:T(8,128)(2,1)S(1)} %collective-permute-done.17.pair), custom_call_target="tpu_custom_call" | custom-call | bytes 786432 | tf_op jit(solution)/shard_map/outputs/pallas_call | solution.py:66
  50.4 1.6 %collective-permute-done.18.got = bf16[64,512]{1,0:T(8,128)(2,1)S(1)} collective-permute-done((bf16[64,512]{1,0:T(8,128)(2,1)S(1)}, bf16[64,512]{1,0:T(8,128)(2,1)S(1)}, u32[]{:S(2)}, u32[]{:S(2)}) %collective-permute-start.18) | collective-permute-done | bytes 65568 | tf_op jit(solution)/shard_map/ppermute | solution.py:437
  52.1 0.7 %weight_join.1 = f32[64,1024]{1,0:T(8,128)} custom-call(bf16[64,512]{1,0:T(8,128)(2,1)S(1)} %both.1.refs_0_, bf16[64,512]{1,0:T(8,128)(2,1)S(1)} %collective-permute-done.18.got, bf16[1,128,512]{2,1,0:T(8,128)(2,1)} %get-tuple-element.45._), custom_call_target="tpu_custom_call" | custom-call | bytes 524288 | tf_op jit(solution)/shard_map/weight_join/pallas_call | solution.py:66
  (7 shorter events, 0.2 us)
Async XLA Ops:
  0.6 2.3 %collective-permute-start = (bf16[1,128,512]{2,1,0:T(8,128)(2,1)}, bf16[1,128,512]{2,1,0:T(8,128)(2,1)S(1)}, u32[]{:S(2)}, u32[]{:S(2)}) collective-permute-start(bf16[1,128,512]{2,1,0:T(8,128)(2,1)} %q.1), channel_id=1, source_target_pairs={{0,1},{1,0},{2,3},{3,2},{4,5},{5,4},{6,7},{7,6},{8,9},{9,8},{10,11... | collective-permute-start | bytes 393224 | tf_op jit(solution)/shard_map/ppermute | solution.py:420
  1.2 1.8 %collective-permute-start.1 = (bf16[1,128,512]{2,1,0:T(8,128)(2,1)}, bf16[1,128,512]{2,1,0:T(8,128)(2,1)S(1)}, u32[]{:S(2)}, u32[]{:S(2)}) collective-permute-start(bf16[1,128,512]{2,1,0:T(8,128)(2,1)} %k.1), channel_id=1, source_target_pairs={{0,1},{1,0},{2,3},{3,2},{4,5},{5,4},{6,7},{7,6},{8,9},{9,8},{10,11... | collective-permute-start | bytes 393224 | tf_op jit(solution)/shard_map/ppermute | solution.py:420
  1.2 1.7 %collective-permute-start.2 = (bf16[1,128,512]{2,1,0:T(8,128)(2,1)}, bf16[1,128,512]{2,1,0:T(8,128)(2,1)S(1)}, u32[]{:S(2)}, u32[]{:S(2)}) collective-permute-start(bf16[1,128,512]{2,1,0:T(8,128)(2,1)} %v.1), channel_id=1, source_target_pairs={{0,1},{1,0},{2,3},{3,2},{4,5},{5,4},{6,7},{7,6},{8,9},{9,8},{10,11... | collective-permute-start | bytes 393224 | tf_op jit(solution)/shard_map/ppermute | solution.py:420
  1.7 7.2 %collective-permute-start.3 = (bf16[128,1024]{1,0:T(8,128)(2,1)}, bf16[128,1024]{1,0:T(8,128)(2,1)S(1)}, u32[]{:S(2)}, u32[]{:S(2)}) collective-permute-start(bf16[128,1024]{1,0:T(8,128)(2,1)} %bitcast.1), channel_id=1, source_target_pairs={{0,1},{1,0},{2,3},{3,2},{4,5},{5,4},{6,7},{7,6},{8,9},{9,8},{10,11... | collective-permute-start | bytes 786440 | tf_op jit(solution)/shard_map/ppermute | solution.py:420
  3.2 6.0 %collective-permute-start.4 = (bf16[128,512]{1,0:T(8,128)(2,1)S(1)}, bf16[128,512]{1,0:T(8,128)(2,1)S(1)}, u32[]{:S(2)}, u32[]{:S(2)}) collective-permute-start(bf16[128,512]{1,0:T(8,128)(2,1)S(1)} %get-tuple-element.53), channel_id=1, source_target_pairs={{0,2},{1,7},{2,0},{3,5},{4,6},{5,3},{6,4},{7,1},{8,10},{9,15},{10,... | collective-permute-start | bytes 393224 | tf_op jit(solution)/shard_map/ppermute | solution.py:431
  6.3 9.4 %collective-permute-start.5 = (bf16[128,512]{1,0:T(8,128)(2,1)S(1)}, bf16[128,512]{1,0:T(8,128)(2,1)S(1)}, u32[]{:S(2)}, u32[]{:S(2)}) collective-permute-start(bf16[128,512]{1,0:T(8,128)(2,1)S(1)} %get-tuple-element.54), channel_id=1, source_target_pairs={{0,6},{1,3},{2,4},{3,1},{4,2},{5,7},{6,0},{7,5},{8,14},{9,11},{10,... | collective-permute-start | bytes 393224 | tf_op jit(solution)/shard_map/ppermute | solution.py:431
  8.8 8.2 %collective-permute-start.6 = (bf16[128,256]{1,0:T(8,128)(2,1)S(1)}, bf16[128,256]{1,0:T(8,128)(2,1)S(1)}, u32[]{:S(2)}, u32[]{:S(2)}) collective-permute-start(bf16[128,256]{1,0:T(8,128)(2,1)S(1)} %get-tuple-element.59), channel_id=1, source_target_pairs={{0,4},{1,5},{2,6},{3,7},{4,0},{5,1},{6,2},{7,3},{8,12},{9,13},{10,... | collective-permute-start | bytes 196616 | tf_op jit(solution)/shard_map/ppermute | solution.py:431
  17.6 6.4 %collective-permute-start.7 = (bf16[256,512]{1,0:T(8,128)(2,1)S(1)}, bf16[256,512]{1,0:T(8,128)(2,1)S(1)}, u32[]{:S(2)}, u32[]{:S(2)}) collective-permute-start(bf16[256,512]{1,0:T(8,128)(2,1)S(1)} %get-tuple-element.62), channel_id=1, source_target_pairs={{0,8},{1,17},{8,0},{9,25},{16,24},{17,1},{24,16},{25,9},{2,10},{3,... | collective-permute-start | bytes 786440 | tf_op jit(solution)/shard_map/ppermute | solution.py:437
  19.2 1.3 %collective-permute-start.11 = (bf16[2,64,256]{2,1,0:T(8,128)(2,1)S(1)}, bf16[2,64,256]{2,1,0:T(8,128)(2,1)S(1)}, u32[]{:S(2)}, u32[]{:S(2)}) collective-permute-start(bf16[2,64,256]{2,1,0:T(8,128)(2,1)S(1)} %get-tuple-element.70), channel_id=1, source_target_pairs={{0,1},{1,0},{2,3},{3,2},{4,5},{5,4},{6,7},{7,6},{8,9},{9,8},{10,11... | collective-permute-start | bytes 196616 | tf_op jit(solution)/shard_map/ppermute | solution.py:420
  20.6 5.9 %collective-permute-start.12 = (bf16[256,256]{1,0:T(8,128)(2,1)S(1)}, bf16[256,256]{1,0:T(8,128)(2,1)S(1)}, u32[]{:S(2)}, u32[]{:S(2)}) collective-permute-start(bf16[256,256]{1,0:T(8,128)(2,1)S(1)} %w_rows.1.first), channel_id=1, source_target_pairs={{0,8},{1,17},{8,0},{9,25},{16,24},{17,1},{24,16},{25,9},{2,10},{3,... | collective-permute-start | bytes 393224 | tf_op jit(solution)/shard_map/ppermute | solution.py:437
  24.1 5.0 %collective-permute-start.8 = (bf16[256,256]{1,0:T(8,128)(2,1)S(1)}, bf16[256,256]{1,0:T(8,128)(2,1)S(1)}, u32[]{:S(2)}, u32[]{:S(2)}) collective-permute-start(bf16[256,256]{1,0:T(8,128)(2,1)S(1)} %get-tuple-element.64.refs_0_), channel_id=1, source_target_pairs={{0,16},{1,9},{8,24},{9,1},{16,0},{17,25},{24,8},{25,17},{2,18},{3,... | collective-permute-start | bytes 393224 | tf_op jit(solution)/shard_map/ppermute | solution.py:437
  26.5 6.4 %collective-permute-start.13 = (bf16[256,512]{1,0:T(8,128)(2,1)S(1)}, bf16[256,512]{1,0:T(8,128)(2,1)S(1)}, u32[]{:S(2)}, u32[]{:S(2)}) collective-permute-start(bf16[256,512]{1,0:T(8,128)(2,1)S(1)} %w_half.1.refs_0_), channel_id=1, source_target_pairs={{0,16},{1,9},{8,24},{9,1},{16,0},{17,25},{24,8},{25,17},{2,18},{3,... | collective-permute-start | bytes 786440 | tf_op jit(solution)/shard_map/ppermute | solution.py:437
  29.2 1.4 %collective-permute-start.9 = (f32[128,256]{1,0:T(8,128)S(1)}, f32[128,256]{1,0:T(8,128)S(1)}, u32[]{:S(2)}, u32[]{:S(2)}) collective-permute-start(f32[128,256]{1,0:T(8,128)S(1)} %get-tuple-element.66), channel_id=1, source_target_pairs={{0,1},{1,0},{2,3},{3,2},{4,5},{5,4},{6,7},{7,6},{8,9},{9,8},{10,11... | collective-permute-start | bytes 393224 | tf_op jit(solution)/shard_map/ppermute | solution.py:420
  30.7 4.3 %collective-permute-start.10 = (bf16[128,256]{1,0:T(8,128)(2,1)S(1)}, bf16[128,256]{1,0:T(8,128)(2,1)S(1)}, u32[]{:S(2)}, u32[]{:S(2)}) collective-permute-start(bf16[128,256]{1,0:T(8,128)(2,1)S(1)} %get-tuple-element.68), channel_id=1, source_target_pairs={{0,2},{1,7},{2,0},{3,5},{4,6},{5,3},{6,4},{7,1},{8,10},{9,15},{10,... | collective-permute-start | bytes 196616 | tf_op jit(solution)/shard_map/ppermute | solution.py:431
  35.0 7.6 %collective-permute-start.14 = (bf16[128,512]{1,0:T(8,128)(2,1)S(1)}, bf16[128,512]{1,0:T(8,128)(2,1)S(1)}, u32[]{:S(2)}, u32[]{:S(2)}) collective-permute-start(bf16[128,512]{1,0:T(8,128)(2,1)S(1)} %get-tuple-element.82), channel_id=1, source_target_pairs={{0,6},{1,3},{2,4},{3,1},{4,2},{5,7},{6,0},{7,5},{8,14},{9,11},{10,... | collective-permute-start | bytes 393224 | tf_op jit(solution)/shard_map/ppermute | solution.py:431
  42.6 4.7 %collective-permute-start.15 = (bf16[128,384]{1,0:T(8,128)(2,1)S(1)}, bf16[128,384]{1,0:T(8,128)(2,1)S(1)}, u32[]{:S(2)}, u32[]{:S(2)}) collective-permute-start(bf16[128,384]{1,0:T(8,128)(2,1)S(1)} %get-tuple-element.87), channel_id=1, source_target_pairs={{0,2},{1,7},{2,0},{3,5},{4,6},{5,3},{6,4},{7,1},{8,10},{9,15},{10,... | collective-permute-start | bytes 294920 | tf_op jit(solution)/shard_map/ppermute | solution.py:431
  42.7 4.2 %collective-permute-start.16 = (bf16[64,256]{1,0:T(8,128)(2,1)S(1)}, bf16[64,256]{1,0:T(8,128)(2,1)S(1)}, u32[]{:S(2)}, u32[]{:S(2)}) collective-permute-start(bf16[64,256]{1,0:T(8,128)(2,1)S(1)} %get-tuple-element.88.first), channel_id=1, source_target_pairs={{0,8},{1,17},{8,0},{9,25},{16,24},{17,1},{24,16},{25,9},{2,10},{3,... | collective-permute-start | bytes 98312 | tf_op jit(solution)/shard_map/ppermute | solution.py:437
  47.7 1.9 %collective-permute-start.17 = (bf16[128,768]{1,0:T(8,128)(2,1)S(1)}, bf16[128,768]{1,0:T(8,128)(2,1)S(1)}, u32[]{:S(2)}, u32[]{:S(2)}) collective-permute-start(bf16[128,768]{1,0:T(8,128)(2,1)S(1)} %get-tuple-element.90), channel_id=1, source_target_pairs={{0,1},{1,0},{2,3},{3,2},{4,5},{5,4},{6,7},{7,6},{8,9},{9,8},{10,11... | collective-permute-start | bytes 589832 | tf_op jit(solution)/shard_map/ppermute | solution.py:420
  47.8 4.3 %collective-permute-start.18 = (bf16[64,512]{1,0:T(8,128)(2,1)S(1)}, bf16[64,512]{1,0:T(8,128)(2,1)S(1)}, u32[]{:S(2)}, u32[]{:S(2)}) collective-permute-start(bf16[64,512]{1,0:T(8,128)(2,1)S(1)} %both.1.refs_0_), channel_id=1, source_target_pairs={{0,16},{1,9},{8,24},{9,1},{16,0},{17,25},{24,8},{25,17},{2,18},{3,... | collective-permute-start | bytes 196616 | tf_op jit(solution)/shard_map/ppermute | solution.py:437

commit v12 on v11

--- a/solution.py
+++ b/solution.py
@@ -340,27 +340,27 @@
         keep[index * half : (index + 1) * half, :] = heads[z ^ step]
 
 
-def second_kernel(keep, got, dstate, dk_soft, dv_soft, chunk, send):
+def second_kernel(keep, got, dstate, dk_soft, dv_soft, chunk, to_a, to_b, to_c):
     way = links(True)
     half = chunk.shape[0]
     chunk[...] = keep[:half, :] + got[:half, :].astype(F32)
     for side in range(2):
         cols, rows = slice(side * DH, (side + 1) * DH), slice(side * half, (side + 1) * half)
         piece = keep[half:, cols] + got[half:, cols].astype(F32)
-        send[rows, 3 * DH :] = piece.astype(BF)
-    halo_part(send, 0, dk_soft, dv_soft, way["halo_b"])
-    send[:, 2 * DH : 3 * DH] = dstate[...].astype(BF)
-
-
-def third_kernel(scale, chunk, got, dstate, dk_soft, dv_soft, summed, total, send):
-    way = links(True)
+        to_b[rows, 3 * DH :] = piece.astype(BF)
+    halo_part(to_a, 0, dk_soft, dv_soft, way["halo_a"])
+    halo_part(to_b, 0, dk_soft, dv_soft, way["halo_b"])
+    low = dstate[...].astype(BF)
+    to_a[:, 2 * DH :] = low
+    to_b[:, 2 * DH : 3 * DH] = low
+    to_c[...] = low
+
+
+def weight_sum_kernel(scale, chunk, got, summed):
     half = chunk.shape[0]
     for side in range(2):
         cols, rows = slice(side * DH, (side + 1) * DH), slice(side * half, (side + 1) * half)
         summed[:, cols] = (scale * (chunk[:, cols] + got[rows, 3 * DH :].astype(F32))).astype(summed.dtype)
-    total[...] = dstate[...] + got[:, 2 * DH : 3 * DH].astype(F32)
-    halo_part(send, 0, dk_soft, dv_soft, way["halo_a"])
-    send[:, 2 * DH :] = total[...].astype(BF)
 
 
 def final_kernel(
@@ -372,7 +372,8 @@
     total = dstate[...]
     own_out, pair_out, dk_all, dv_all = refs[-4:]
     if direct:
-        total = total + a[:, 2 * DH :].astype(F32)
+        total = total + a[:, 2 * DH :].astype(F32) + b[:, 2 * DH : 3 * DH].astype(F32)
+        total = total + refs[0][...].astype(F32)
     for source, out, cols in ((dk_soft, dk_all, slice(0, DH)), (dv_soft, dv_all, slice(DH, 2 * DH))):
         out[...] = source[HALF : HALF + 2 * rows, :]
         out[at(way["block_a"] * rows, rows), :] += a[:, cols].astype(F32)
@@ -532,17 +533,19 @@
     )
     wide = 3 * DH if direct else 2 * DH
     if direct:
-        chunk, to_b = call(
-            second_kernel, "second", [like((half, width), F32), like((rows, 4 * DH), BF)],
+        chunk, to_a, to_b, to_c = call(
+            second_kernel, "second",
+            [
+                like((half, width), F32), like((rows, 3 * DH), BF), like((rows, 4 * DH), BF),
+                like((DH, DH), BF),
+            ],
             [piece_keep, piece_got, dstate, dk_soft, dv_soft],
         )
-        b = over_z(to_b, 1)
-        summed, dstate, to_a = call(
-            functools.partial(third_kernel, scale), "third",
-            [like((half, width), BF), like((DH, DH), F32), like((rows, 3 * DH), BF)],
-            [chunk, b, dstate, dk_soft, dv_soft],
-        )
-        a = over_z(to_a, 0)
+        b, a, c = over_z(to_b, 1), over_z(to_a, 0), [over_z(to_c, 2)]
+        summed = call(
+            functools.partial(weight_sum_kernel, scale), "weight_sum", [like((half, width), BF)],
+            [chunk, b],
+        )[0]
         got = over_dp(summed, 0)
         both = call(join_kernel, "both", [like((half, 2 * width), BF)], [summed, got])[0]
         gathered = over_dp(both, 1)
@@ -561,7 +564,7 @@
         functools.partial(final_kernel, direct), "final",
         [like((rows, 6 * DH), BF), like((rows, 6 * DH), BF)],
         [dstate, mine, pair, dq_soft, dk_soft, dv_soft, dq_lin, dq_lin_pair, a, b]
-        + ([both] if direct else []),
+        + (c if direct else []),
         scratch=[pltpu.VMEM((2 * rows, DH), F32)] * 2,
         flops=wg_flops // 4,
     )

time: 53 us -> 55.1 us (1.040)
  starting transfers between devices: 21.1 us -> 22.4 us
  waiting for transfers between devices: 23.9 us -> 24.7 us
    ppermute x6 -> x7, starting transfers between devices: 9.67 us -> 10.9 us  [over_z(): return lax.ppermute(value, axes, pairs)]
    ppermute x6 -> x7, waiting for transfers between devices: 12.2 us -> 12.7 us  [over_z(): return lax.ppermute(value, axes, pairs)]
  transfers between devices with their start and end apart: 19 -> 20, of which waited for: 13 -> 12; matrix products, arithmetic and copies ran while one was open for 0% -> 0% of each run, Pallas kernels for 10% -> 10%
where the time goes in v12:
time: 55.1 us; the launch traced here: 54.9 us
  waiting for transfers between devices  24.7 us (45%)
  starting transfers between devices  22.4 us (41%)
  Pallas kernels  7.05 us (13%)
  between operations  0.77 us (1%)
    ppermute x7, waiting for transfers between devices, over_z(): return lax.ppermute(value, axes, pairs)  12.7 us
    ppermute x7, starting transfers between devices, over_z(): return lax.ppermute(value, axes, pairs)  10.9 us
    ppermute x6, starting transfers between devices, over_dp(): return lax.ppermute(value, ('dp', 'core'), pairs)  9.63 us
    ppermute x6, waiting for transfers between devices, over_dp(): return lax.ppermute(value, ('dp', 'core'), pairs)  9.35 us
    pallas_call x17, Pallas kernels, call(): pl.pallas_call(kernel, name=name, out_shape=list(outs), in_specs=spaces o...  7.05 us
    ppermute x7, waiting for transfers between devices, over_core(): return lax.ppermute(value, 'core', pair_perm)  2.59 us
    ppermute x7, starting transfers between devices, over_core(): return lax.ppermute(value, 'core', pair_perm)  1.83 us
  transfers between devices with their start and end apart: 20, of which 12 were waited for; matrix products, arithmetic and copies ran while one was open for 0% of the time, Pallas kernels for 10%

profile of v12, /device:TPU:0, one launch (start us, length us, event | category | flops | bytes accessed | tf_op | source)
XLA Modules:
  0.0 54.9 jit_solution(17670371868357556067)
XLA Ops:
  0.6 0.5 collective-permute-start
  1.2 0.1 collective-permute-start.1
  1.2 0.4 collective-permute-start.2
  1.7 0.1 collective-permute-start.8
  1.7 1.2 %pack.1 = (bf16[128,768]{1,0:T(8,128)(2,1)S(1)}, bf16[128,1024]{1,0:T(8,128)(2,1)S(1)}, bf16[64,256]{1,0:T(8,128)(2,1)S(1)}, f32[1,128]{1,0:T(1,128)S(1)}) custom-call(bf16[1,128,512]{2,1,0:T(8,128)(2,1)} %q.1, bf16[1,128,512]{2,1,0:T(8,128)(2,1)} %k.1, bf16[1,128,512]{2,1,0:T(8,128)(2,1)} %v.1, bf16[1,128,1024]{2,1,0:T(8,128)(2,1)} %og.1, ...), custom_call_target="tpu_custom_call" | custom-call | bytes 1279488 | tf_op jit(solution)/shard_map/pack/pallas_call | solution.py:66
  2.9 0.0 collective-permute-done.q_pair
  2.9 0.0 collective-permute-done.1.k_pair
  2.9 0.0 collective-permute-done.2.v_pair
  3.0 0.3 state.1
  3.2 3.1 %collective-permute-start.3 = (bf16[128,512]{1,0:T(8,128)(2,1)S(1)}, bf16[128,512]{1,0:T(8,128)(2,1)S(1)}, u32[]{:S(2)}, u32[]{:S(2)}) collective-permute-start(bf16[128,512]{1,0:T(8,128)(2,1)S(1)} %get-tuple-element.50), channel_id=1, source_target_pairs={{0,2},{1,7},{2,0},{3,5},{4,6},{5,3},{6,4},{7,1},{8,10},{9,15},{10,... | collective-permute-start | bytes 393224 | tf_op jit(solution)/shard_map/ppermute | solution.py:432
  6.3 2.5 %collective-permute-start.4 = (bf16[128,512]{1,0:T(8,128)(2,1)S(1)}, bf16[128,512]{1,0:T(8,128)(2,1)S(1)}, u32[]{:S(2)}, u32[]{:S(2)}) collective-permute-start(bf16[128,512]{1,0:T(8,128)(2,1)S(1)} %get-tuple-element.51), channel_id=1, source_target_pairs={{0,6},{1,3},{2,4},{3,1},{4,2},{5,7},{6,0},{7,5},{8,14},{9,11},{10,... | collective-permute-start | bytes 393224 | tf_op jit(solution)/shard_map/ppermute | solution.py:432
  8.8 0.1 collective-permute-start.5
  8.9 0.4 collective-permute-done.3.a.refs_0_
  9.3 6.5 %collective-permute-done.4.b.refs_1_ = bf16[128,512]{1,0:T(8,128)(2,1)S(1)} collective-permute-done((bf16[128,512]{1,0:T(8,128)(2,1)S(1)}, bf16[128,512]{1,0:T(8,128)(2,1)S(1)}, u32[]{:S(2)}, u32[]{:S(2)}) %collective-permute-start.4) | collective-permute-done | bytes 131104 | tf_op jit(solution)/shard_map/ppermute | solution.py:432
  15.7 0.0 collective-permute-done.8.og_recv
  15.7 1.2 %soft_forward.1 = (bf16[256,128]{1,0:T(8,128)(2,1)S(1)}, bf16[512,128]{1,0:T(8,128)(2,1)S(1)}, bf16[512,128]{1,0:T(8,128)(2,1)S(1)}, bf16[256,1024]{1,0:T(8,128)...) custom-call(bf16[128,768]{1,0:T(8,128)(2,1)S(1)} %get-tuple-element., ...), custom_call_target="tpu_custom_call" | custom-call | flops 67108864 | bytes 2949120 | tf_op jit(solution)/shard_map/soft_forward/pallas_call | solution.py:66
  16.9 0.0 collective-permute-done.5.c.refs_2_
  17.0 0.7 %lin_forward.1 = (f32[256,128]{1,0:T(8,128)S(1)}, f32[128,128]{1,0:T(8,128)S(1)}, f32[128,512]{1,0:T(8,128)S(1)}, bf16[256,512]{1,0:T(8,128)(2,1)S(1)}) custom-call(f32[128,128]{1,0:T(8,128)S(1)} %get-tuple-element.58.state, bf16[128,768]{1,0:T(8,128)(2,1)S(1)} %get-tuple-element.49.mine.refs_6_, bf16[128,768]{1,0:T(8,128)(2,1)S(1)} %get-tuple-element.55.pair.refs_7_, ...), custom_call_target="tpu_custom_call" | custom-call | flops 67108864 | bytes 2163200 | tf_op jit(solution)/shard_map/lin_forward/pallas_call | solution.py:66
  17.6 1.6 %collective-permute-start.9 = (bf16[256,512]{1,0:T(8,128)(2,1)S(1)}, bf16[256,512]{1,0:T(8,128)(2,1)S(1)}, u32[]{:S(2)}, u32[]{:S(2)}) collective-permute-start(bf16[256,512]{1,0:T(8,128)(2,1)S(1)} %get-tuple-element.63), channel_id=1, source_target_pairs={{0,8},{1,17},{8,0},{9,25},{16,24},{17,1},{24,16},{25,9},{2,10},{3,... | collective-permute-start | bytes 786440 | tf_op jit(solution)/shard_map/ppermute | solution.py:438
  19.2 0.1 collective-permute-start.6
  19.3 1.2 %collective-permute-done.6.got = bf16[2,64,256]{2,1,0:T(8,128)(2,1)S(1)} collective-permute-done((bf16[2,64,256]{2,1,0:T(8,128)(2,1)S(1)}, bf16[2,64,256]{2,1,0:T(8,128)(2,1)S(1)}, u32[]{:S(2)}, u32[]{:S(2)}) %collective-permute-start.6) | collective-permute-done | bytes 65568 | tf_op jit(solution)/shard_map/ppermute | solution.py:421
  20.6 0.6 %collective-permute-start.7 = (bf16[256,256]{1,0:T(8,128)(2,1)S(1)}, bf16[256,256]{1,0:T(8,128)(2,1)S(1)}, u32[]{:S(2)}, u32[]{:S(2)}) collective-permute-start(bf16[256,256]{1,0:T(8,128)(2,1)S(1)} %w_rows.1.first), channel_id=1, source_target_pairs={{0,8},{1,17},{8,0},{9,25},{16,24},{17,1},{24,16},{25,9},{2,10},{3,... | collective-permute-start | bytes 393224 | tf_op jit(solution)/shard_map/ppermute | solution.py:438
  21.2 2.9 %collective-permute-done.9.got = bf16[256,512]{1,0:T(8,128)(2,1)S(1)} collective-permute-done((bf16[256,512]{1,0:T(8,128)(2,1)S(1)}, bf16[256,512]{1,0:T(8,128)(2,1)S(1)}, u32[]{:S(2)}, u32[]{:S(2)}) %collective-permute-start.9) | collective-permute-done | bytes 262176 | tf_op jit(solution)/shard_map/ppermute | solution.py:438
  24.1 0.1 fold.1
  24.1 1.9 %collective-permute-start.11 = (bf16[256,256]{1,0:T(8,128)(2,1)S(1)}, bf16[256,256]{1,0:T(8,128)(2,1)S(1)}, u32[]{:S(2)}, u32[]{:S(2)}) collective-permute-start(bf16[256,256]{1,0:T(8,128)(2,1)S(1)} %get-tuple-element.64.refs_0_), channel_id=1, source_target_pairs={{0,16},{1,9},{8,24},{9,1},{16,0},{17,25},{24,8},{25,17},{2,18},{3,... | collective-permute-start | bytes 393224 | tf_op jit(solution)/shard_map/ppermute | solution.py:438
  26.0 0.5 collective-permute-done.7.second
  26.6 1.9 %collective-permute-start.10 = (bf16[256,512]{1,0:T(8,128)(2,1)S(1)}, bf16[256,512]{1,0:T(8,128)(2,1)S(1)}, u32[]{:S(2)}, u32[]{:S(2)}) collective-permute-start(bf16[256,512]{1,0:T(8,128)(2,1)S(1)} %w_half.1.refs_0_), channel_id=1, source_target_pairs={{0,16},{1,9},{8,24},{9,1},{16,0},{17,25},{24,8},{25,17},{2,18},{3,... | collective-permute-start | bytes 786440 | tf_op jit(solution)/shard_map/ppermute | solution.py:438
  28.5 0.7 %collective-permute-done.11.got = bf16[256,256]{1,0:T(8,128)(2,1)S(1)} collective-permute-done((bf16[256,256]{1,0:T(8,128)(2,1)S(1)}, bf16[256,256]{1,0:T(8,128)(2,1)S(1)}, u32[]{:S(2)}, u32[]{:S(2)}) %collective-permute-start.11) | collective-permute-done | bytes 131104 | tf_op jit(solution)/shard_map/ppermute | solution.py:438
  29.2 0.1 rows.1
  29.2 0.1 collective-permute-start.12
  29.3 1.3 %collective-permute-done.12.got = f32[128,256]{1,0:T(8,128)S(1)} collective-permute-done((f32[128,256]{1,0:T(8,128)S(1)}, f32[128,256]{1,0:T(8,128)S(1)}, u32[]{:S(2)}, u32[]{:S(2)}) %collective-permute-start.12) | collective-permute-done | bytes 131104 | tf_op jit(solution)/shard_map/ppermute | solution.py:421
  30.7 0.8 %collective-permute-start.13 = (bf16[128,256]{1,0:T(8,128)(2,1)S(1)}, bf16[128,256]{1,0:T(8,128)(2,1)S(1)}, u32[]{:S(2)}, u32[]{:S(2)}) collective-permute-start(bf16[128,256]{1,0:T(8,128)(2,1)S(1)} %get-tuple-element.82), channel_id=1, source_target_pairs={{0,2},{1,7},{2,0},{3,5},{4,6},{5,3},{6,4},{7,1},{8,10},{9,15},{10,... | collective-permute-start | bytes 196616 | tf_op jit(solution)/shard_map/ppermute | solution.py:432
  31.5 1.5 %collective-permute-done.10.refs_1_ = bf16[256,512]{1,0:T(8,128)(2,1)S(1)} collective-permute-done((bf16[256,512]{1,0:T(8,128)(2,1)S(1)}, bf16[256,512]{1,0:T(8,128)(2,1)S(1)}, u32[]{:S(2)}, u32[]{:S(2)}) %collective-permute-start.10) | collective-permute-done | bytes 262176 | tf_op jit(solution)/shard_map/ppermute | solution.py:438
  33.0 1.5 %backward.1 = (bf16[128,128]{1,0:T(8,128)(2,1)S(1)}, bf16[128,128]{1,0:T(8,128)(2,1)S(1)}, f32[128,128]{1,0:T(8,128)S(1)}, f32[256,128]{1,0:T(8,128)S(1)}, f32[5...) custom-call(bf16[256,512]{1,0:T(8,128)(2,1)S(1)} %w_half.1.refs_0_, bf16[256,512]{1,0:T(8,128)(2,1)S(1)} %collective-permute-done.10.refs_1_, ...), custom_call_target="tpu_custom_call" | custom-call | flops 335544320 | bytes 3408384 | tf_op jit(solution)/shard_map/backward/pallas_call | solution.py:66
  34.5 0.5 collective-permute-done.13.got
  35.1 3.1 %collective-permute-start.15 = (bf16[128,512]{1,0:T(8,128)(2,1)S(1)}, bf16[128,512]{1,0:T(8,128)(2,1)S(1)}, u32[]{:S(2)}, u32[]{:S(2)}) collective-permute-start(bf16[128,512]{1,0:T(8,128)(2,1)S(1)} %get-tuple-element.84), channel_id=1, source_target_pairs={{0,6},{1,3},{2,4},{3,1},{4,2},{5,7},{6,0},{7,5},{8,14},{9,11},{10,... | collective-permute-start | bytes 393224 | tf_op jit(solution)/shard_map/ppermute | solution.py:432
  38.2 0.2 collective-permute-start.14
  38.4 1.2 %collective-permute-start.16 = (bf16[128,128]{1,0:T(8,128)(2,1)S(1)}, bf16[128,128]{1,0:T(8,128)(2,1)S(1)}, u32[]{:S(2)}, u32[]{:S(2)}) collective-permute-start(bf16[128,128]{1,0:T(8,128)(2,1)S(1)} %get-tuple-element.85), channel_id=1, source_target_pairs={{0,4},{1,5},{2,6},{3,7},{4,0},{5,1},{6,2},{7,3},{8,12},{9,13},{10,... | collective-permute-start | bytes 98312 | tf_op jit(solution)/shard_map/ppermute | solution.py:432
  39.5 5.4 %collective-permute-done.16.refs_0_ = bf16[128,128]{1,0:T(8,128)(2,1)S(1)} collective-permute-done((bf16[128,128]{1,0:T(8,128)(2,1)S(1)}, bf16[128,128]{1,0:T(8,128)(2,1)S(1)}, u32[]{:S(2)}, u32[]{:S(2)}) %collective-permute-start.16) | collective-permute-done | bytes 32800 | tf_op jit(solution)/shard_map/ppermute | solution.py:432
  44.9 0.0 collective-permute-done.14.a
  45.0 0.0 collective-permute-done.15.b.got
  45.0 0.4 final.1
  45.3 0.6 %collective-permute-start.17 = (bf16[128,768]{1,0:T(8,128)(2,1)S(1)}, bf16[128,768]{1,0:T(8,128)(2,1)S(1)}, u32[]{:S(2)}, u32[]{:S(2)}) collective-permute-start(bf16[128,768]{1,0:T(8,128)(2,1)S(1)} %get-tuple-element.87), channel_id=1, source_target_pairs={{0,1},{1,0},{2,3},{3,2},{4,5},{5,4},{6,7},{7,6},{8,9},{9,8},{10,11... | collective-permute-start | bytes 589832 | tf_op jit(solution)/shard_map/ppermute | solution.py:421
  45.9 1.9 %collective-permute-start.18 = (bf16[64,256]{1,0:T(8,128)(2,1)S(1)}, bf16[64,256]{1,0:T(8,128)(2,1)S(1)}, u32[]{:S(2)}, u32[]{:S(2)}) collective-permute-start(bf16[64,256]{1,0:T(8,128)(2,1)S(1)} %weight_sum.1.first), channel_id=1, source_target_pairs={{0,8},{1,17},{8,0},{9,25},{16,24},{17,1},{24,16},{25,9},{2,10},{3,... | collective-permute-start | bytes 98312 | tf_op jit(solution)/shard_map/ppermute | solution.py:438
  47.8 2.1 %collective-permute-done.18.second = bf16[64,256]{1,0:T(8,128)(2,1)S(1)} collective-permute-done((bf16[64,256]{1,0:T(8,128)(2,1)S(1)}, bf16[64,256]{1,0:T(8,128)(2,1)S(1)}, u32[]{:S(2)}, u32[]{:S(2)}) %collective-permute-start.18) | collective-permute-done | bytes 32800 | tf_op jit(solution)/shard_map/ppermute | solution.py:438
  49.9 1.8 %collective-permute-start.19 = (bf16[64,512]{1,0:T(8,128)(2,1)S(1)}, bf16[64,512]{1,0:T(8,128)(2,1)S(1)}, u32[]{:S(2)}, u32[]{:S(2)}) collective-permute-start(bf16[64,512]{1,0:T(8,128)(2,1)S(1)} %both.1), channel_id=1, source_target_pairs={{0,16},{1,9},{8,24},{9,1},{16,0},{17,25},{24,8},{25,17},{2,18},{3,... | collective-permute-start | bytes 196616 | tf_op jit(solution)/shard_map/ppermute | solution.py:438
  51.7 0.0 collective-permute-done.17.pair
  51.7 0.8 %outputs.1 = (bf16[1,128,512]{2,1,0:T(8,128)(2,1)}, bf16[1,128,512]{2,1,0:T(8,128)(2,1)}, bf16[1,128,512]{2,1,0:T(8,128)(2,1)}) custom-call(bf16[128,768]{1,0:T(8,128)(2,1)S(1)} %get-tuple-element.86.own, bf16[128,768]{1,0:T(8,128)(2,1)S(1)} %collective-permute-done.17.pair), custom_call_target="tpu_custom_call" | custom-call | bytes 786432 | tf_op jit(solution)/shard_map/outputs/pallas_call | solution.py:66
  52.5 1.7 %collective-permute-done.19.got = bf16[64,512]{1,0:T(8,128)(2,1)S(1)} collective-permute-done((bf16[64,512]{1,0:T(8,128)(2,1)S(1)}, bf16[64,512]{1,0:T(8,128)(2,1)S(1)}, u32[]{:S(2)}, u32[]{:S(2)}) %collective-permute-start.19) | collective-permute-done | bytes 65568 | tf_op jit(solution)/shard_map/ppermute | solution.py:438
  54.2 0.7 %weight_join.1 = f32[64,1024]{1,0:T(8,128)} custom-call(bf16[64,512]{1,0:T(8,128)(2,1)S(1)} %both.1, bf16[64,512]{1,0:T(8,128)(2,1)S(1)} %collective-permute-done.19.got, bf16[1,128,512]{2,1,0:T(8,128)(2,1)} %get-tuple-element.44._), custom_call_target="tpu_custom_call" | custom-call | bytes 524288 | tf_op jit(solution)/shard_map/weight_join/pallas_call | solution.py:66
  (7 shorter events, 0.2 us)
Async XLA Ops:
  0.6 2.3 %collective-permute-start = (bf16[1,128,512]{2,1,0:T(8,128)(2,1)}, bf16[1,128,512]{2,1,0:T(8,128)(2,1)S(1)}, u32[]{:S(2)}, u32[]{:S(2)}) collective-permute-start(bf16[1,128,512]{2,1,0:T(8,128)(2,1)} %q.1), channel_id=1, source_target_pairs={{0,1},{1,0},{2,3},{3,2},{4,5},{5,4},{6,7},{7,6},{8,9},{9,8},{10,11... | collective-permute-start | bytes 393224 | tf_op jit(solution)/shard_map/ppermute | solution.py:421
  1.2 1.8 %collective-permute-start.1 = (bf16[1,128,512]{2,1,0:T(8,128)(2,1)}, bf16[1,128,512]{2,1,0:T(8,128)(2,1)S(1)}, u32[]{:S(2)}, u32[]{:S(2)}) collective-permute-start(bf16[1,128,512]{2,1,0:T(8,128)(2,1)} %k.1), channel_id=1, source_target_pairs={{0,1},{1,0},{2,3},{3,2},{4,5},{5,4},{6,7},{7,6},{8,9},{9,8},{10,11... | collective-permute-start | bytes 393224 | tf_op jit(solution)/shard_map/ppermute | solution.py:421
  1.2 1.7 %collective-permute-start.2 = (bf16[1,128,512]{2,1,0:T(8,128)(2,1)}, bf16[1,128,512]{2,1,0:T(8,128)(2,1)S(1)}, u32[]{:S(2)}, u32[]{:S(2)}) collective-permute-start(bf16[1,128,512]{2,1,0:T(8,128)(2,1)} %v.1), channel_id=1, source_target_pairs={{0,1},{1,0},{2,3},{3,2},{4,5},{5,4},{6,7},{7,6},{8,9},{9,8},{10,11... | collective-permute-start | bytes 393224 | tf_op jit(solution)/shard_map/ppermute | solution.py:421
  1.7 14.1 %collective-permute-start.8 = (bf16[128,1024]{1,0:T(8,128)(2,1)}, bf16[128,1024]{1,0:T(8,128)(2,1)S(1)}, u32[]{:S(2)}, u32[]{:S(2)}) collective-permute-start(bf16[128,1024]{1,0:T(8,128)(2,1)} %bitcast.1), channel_id=1, source_target_pairs={{0,1},{1,0},{2,3},{3,2},{4,5},{5,4},{6,7},{7,6},{8,9},{9,8},{10,11... | collective-permute-start | bytes 786440 | tf_op jit(solution)/shard_map/ppermute | solution.py:421
  3.2 6.0 %collective-permute-start.3 = (bf16[128,512]{1,0:T(8,128)(2,1)S(1)}, bf16[128,512]{1,0:T(8,128)(2,1)S(1)}, u32[]{:S(2)}, u32[]{:S(2)}) collective-permute-start(bf16[128,512]{1,0:T(8,128)(2,1)S(1)} %get-tuple-element.50), channel_id=1, source_target_pairs={{0,2},{1,7},{2,0},{3,5},{4,6},{5,3},{6,4},{7,1},{8,10},{9,15},{10,... | collective-permute-start | bytes 393224 | tf_op jit(solution)/shard_map/ppermute | solution.py:432
  6.3 9.4 %collective-permute-start.4 = (bf16[128,512]{1,0:T(8,128)(2,1)S(1)}, bf16[128,512]{1,0:T(8,128)(2,1)S(1)}, u32[]{:S(2)}, u32[]{:S(2)}) collective-permute-start(bf16[128,512]{1,0:T(8,128)(2,1)S(1)} %get-tuple-element.51), channel_id=1, source_target_pairs={{0,6},{1,3},{2,4},{3,1},{4,2},{5,7},{6,0},{7,5},{8,14},{9,11},{10,... | collective-permute-start | bytes 393224 | tf_op jit(solution)/shard_map/ppermute | solution.py:432
  8.8 8.2 %collective-permute-start.5 = (bf16[128,256]{1,0:T(8,128)(2,1)S(1)}, bf16[128,256]{1,0:T(8,128)(2,1)S(1)}, u32[]{:S(2)}, u32[]{:S(2)}) collective-permute-start(bf16[128,256]{1,0:T(8,128)(2,1)S(1)} %get-tuple-element.52), channel_id=1, source_target_pairs={{0,4},{1,5},{2,6},{3,7},{4,0},{5,1},{6,2},{7,3},{8,12},{9,13},{10,... | collective-permute-start | bytes 196616 | tf_op jit(solution)/shard_map/ppermute | solution.py:432
  17.6 6.4 %collective-permute-start.9 = (bf16[256,512]{1,0:T(8,128)(2,1)S(1)}, bf16[256,512]{1,0:T(8,128)(2,1)S(1)}, u32[]{:S(2)}, u32[]{:S(2)}) collective-permute-start(bf16[256,512]{1,0:T(8,128)(2,1)S(1)} %get-tuple-element.63), channel_id=1, source_target_pairs={{0,8},{1,17},{8,0},{9,25},{16,24},{17,1},{24,16},{25,9},{2,10},{3,... | collective-permute-start | bytes 786440 | tf_op jit(solution)/shard_map/ppermute | solution.py:438
  19.2 1.3 %collective-permute-start.6 = (bf16[2,64,256]{2,1,0:T(8,128)(2,1)S(1)}, bf16[2,64,256]{2,1,0:T(8,128)(2,1)S(1)}, u32[]{:S(2)}, u32[]{:S(2)}) collective-permute-start(bf16[2,64,256]{2,1,0:T(8,128)(2,1)S(1)} %get-tuple-element.54), channel_id=1, source_target_pairs={{0,1},{1,0},{2,3},{3,2},{4,5},{5,4},{6,7},{7,6},{8,9},{9,8},{10,11... | collective-permute-start | bytes 196616 | tf_op jit(solution)/shard_map/ppermute | solution.py:421
  20.6 6.0 %collective-permute-start.7 = (bf16[256,256]{1,0:T(8,128)(2,1)S(1)}, bf16[256,256]{1,0:T(8,128)(2,1)S(1)}, u32[]{:S(2)}, u32[]{:S(2)}) collective-permute-start(bf16[256,256]{1,0:T(8,128)(2,1)S(1)} %w_rows.1.first), channel_id=1, source_target_pairs={{0,8},{1,17},{8,0},{9,25},{16,24},{17,1},{24,16},{25,9},{2,10},{3,... | collective-permute-start | bytes 393224 | tf_op jit(solution)/shard_map/ppermute | solution.py:438
  24.1 5.0 %collective-permute-start.11 = (bf16[256,256]{1,0:T(8,128)(2,1)S(1)}, bf16[256,256]{1,0:T(8,128)(2,1)S(1)}, u32[]{:S(2)}, u32[]{:S(2)}) collective-permute-start(bf16[256,256]{1,0:T(8,128)(2,1)S(1)} %get-tuple-element.64.refs_0_), channel_id=1, source_target_pairs={{0,16},{1,9},{8,24},{9,1},{16,0},{17,25},{24,8},{25,17},{2,18},{3,... | collective-permute-start | bytes 393224 | tf_op jit(solution)/shard_map/ppermute | solution.py:438
  26.6 6.4 %collective-permute-start.10 = (bf16[256,512]{1,0:T(8,128)(2,1)S(1)}, bf16[256,512]{1,0:T(8,128)(2,1)S(1)}, u32[]{:S(2)}, u32[]{:S(2)}) collective-permute-start(bf16[256,512]{1,0:T(8,128)(2,1)S(1)} %w_half.1.refs_0_), channel_id=1, source_target_pairs={{0,16},{1,9},{8,24},{9,1},{16,0},{17,25},{24,8},{25,17},{2,18},{3,... | collective-permute-start | bytes 786440 | tf_op jit(solution)/shard_map/ppermute | solution.py:438
  29.2 1.4 %collective-permute-start.12 = (f32[128,256]{1,0:T(8,128)S(1)}, f32[128,256]{1,0:T(8,128)S(1)}, u32[]{:S(2)}, u32[]{:S(2)}) collective-permute-start(f32[128,256]{1,0:T(8,128)S(1)} %get-tuple-element.67), channel_id=1, source_target_pairs={{0,1},{1,0},{2,3},{3,2},{4,5},{5,4},{6,7},{7,6},{8,9},{9,8},{10,11... | collective-permute-start | bytes 393224 | tf_op jit(solution)/shard_map/ppermute | solution.py:421
  30.7 4.3 %collective-permute-start.13 = (bf16[128,256]{1,0:T(8,128)(2,1)S(1)}, bf16[128,256]{1,0:T(8,128)(2,1)S(1)}, u32[]{:S(2)}, u32[]{:S(2)}) collective-permute-start(bf16[128,256]{1,0:T(8,128)(2,1)S(1)} %get-tuple-element.82), channel_id=1, source_target_pairs={{0,2},{1,7},{2,0},{3,5},{4,6},{5,3},{6,4},{7,1},{8,10},{9,15},{10,... | collective-permute-start | bytes 196616 | tf_op jit(solution)/shard_map/ppermute | solution.py:432
  35.1 9.9 %collective-permute-start.15 = (bf16[128,512]{1,0:T(8,128)(2,1)S(1)}, bf16[128,512]{1,0:T(8,128)(2,1)S(1)}, u32[]{:S(2)}, u32[]{:S(2)}) collective-permute-start(bf16[128,512]{1,0:T(8,128)(2,1)S(1)} %get-tuple-element.84), channel_id=1, source_target_pairs={{0,6},{1,3},{2,4},{3,1},{4,2},{5,7},{6,0},{7,5},{8,14},{9,11},{10,... | collective-permute-start | bytes 393224 | tf_op jit(solution)/shard_map/ppermute | solution.py:432
  38.2 6.8 %collective-permute-start.14 = (bf16[128,384]{1,0:T(8,128)(2,1)S(1)}, bf16[128,384]{1,0:T(8,128)(2,1)S(1)}, u32[]{:S(2)}, u32[]{:S(2)}) collective-permute-start(bf16[128,384]{1,0:T(8,128)(2,1)S(1)} %get-tuple-element.83), channel_id=1, source_target_pairs={{0,2},{1,7},{2,0},{3,5},{4,6},{5,3},{6,4},{7,1},{8,10},{9,15},{10,... | collective-permute-start | bytes 294920 | tf_op jit(solution)/shard_map/ppermute | solution.py:432
  38.4 6.6 %collective-permute-start.16 = (bf16[128,128]{1,0:T(8,128)(2,1)S(1)}, bf16[128,128]{1,0:T(8,128)(2,1)S(1)}, u32[]{:S(2)}, u32[]{:S(2)}) collective-permute-start(bf16[128,128]{1,0:T(8,128)(2,1)S(1)} %get-tuple-element.85), channel_id=1, source_target_pairs={{0,4},{1,5},{2,6},{3,7},{4,0},{5,1},{6,2},{7,3},{8,12},{9,13},{10,... | collective-permute-start | bytes 98312 | tf_op jit(solution)/shard_map/ppermute | solution.py:432
  45.3 6.4 %collective-permute-start.17 = (bf16[128,768]{1,0:T(8,128)(2,1)S(1)}, bf16[128,768]{1,0:T(8,128)(2,1)S(1)}, u32[]{:S(2)}, u32[]{:S(2)}) collective-permute-start(bf16[128,768]{1,0:T(8,128)(2,1)S(1)} %get-tuple-element.87), channel_id=1, source_target_pairs={{0,1},{1,0},{2,3},{3,2},{4,5},{5,4},{6,7},{7,6},{8,9},{9,8},{10,11... | collective-permute-start | bytes 589832 | tf_op jit(solution)/shard_map/ppermute | solution.py:421
  45.9 4.0 %collective-permute-start.18 = (bf16[64,256]{1,0:T(8,128)(2,1)S(1)}, bf16[64,256]{1,0:T(8,128)(2,1)S(1)}, u32[]{:S(2)}, u32[]{:S(2)}) collective-permute-start(bf16[64,256]{1,0:T(8,128)(2,1)S(1)} %weight_sum.1.first), channel_id=1, source_target_pairs={{0,8},{1,17},{8,0},{9,25},{16,24},{17,1},{24,16},{25,9},{2,10},{3,... | collective-permute-start | bytes 98312 | tf_op jit(solution)/shard_map/ppermute | solution.py:438
  49.9 4.3 %collective-permute-start.19 = (bf16[64,512]{1,0:T(8,128)(2,1)S(1)}, bf16[64,512]{1,0:T(8,128)(2,1)S(1)}, u32[]{:S(2)}, u32[]{:S(2)}) collective-permute-start(bf16[64,512]{1,0:T(8,128)(2,1)S(1)} %both.1), channel_id=1, source_target_pairs={{0,16},{1,9},{8,24},{9,1},{16,0},{17,25},{24,8},{25,17},{2,18},{3,... | collective-permute-start | bytes 196616 | tf_op jit(solution)/shard_map/ppermute | solution.py:438

commit v13 on v12

--- a/solution.py
+++ b/solution.py
@@ -334,9 +334,9 @@
         rows = slice(group * half, (group + 1) * half)
         heads[2 * group + core] = own[rows, :]
         heads[2 * group + 1 - core] = got[rows, :]
-    for index, step in enumerate((way["first"], 2)):
+    for index, step in enumerate((way["first"], way["second"])):
         send[index * half : (index + 1) * half, :] = heads[z ^ step].astype(BF)
-    for index, step in enumerate((0, way["second"])):
+    for index, step in enumerate((0, 2)):
         keep[index * half : (index + 1) * half, :] = heads[z ^ step]
 
 
@@ -347,20 +347,20 @@
     for side in range(2):
         cols, rows = slice(side * DH, (side + 1) * DH), slice(side * half, (side + 1) * half)
         piece = keep[half:, cols] + got[half:, cols].astype(F32)
-        to_b[rows, 3 * DH :] = piece.astype(BF)
+        to_c[rows, DH:] = piece.astype(BF)
     halo_part(to_a, 0, dk_soft, dv_soft, way["halo_a"])
     halo_part(to_b, 0, dk_soft, dv_soft, way["halo_b"])
     low = dstate[...].astype(BF)
     to_a[:, 2 * DH :] = low
-    to_b[:, 2 * DH : 3 * DH] = low
-    to_c[...] = low
+    to_b[:, 2 * DH :] = low
+    to_c[:, :DH] = low
 
 
 def weight_sum_kernel(scale, chunk, got, summed):
     half = chunk.shape[0]
     for side in range(2):
         cols, rows = slice(side * DH, (side + 1) * DH), slice(side * half, (side + 1) * half)
-        summed[:, cols] = (scale * (chunk[:, cols] + got[rows, 3 * DH :].astype(F32))).astype(summed.dtype)
+        summed[:, cols] = (scale * (chunk[:, cols] + got[rows, DH:].astype(F32))).astype(summed.dtype)
 
 
 def final_kernel(
@@ -372,8 +372,8 @@
     total = dstate[...]
     own_out, pair_out, dk_all, dv_all = refs[-4:]
     if direct:
-        total = total + a[:, 2 * DH :].astype(F32) + b[:, 2 * DH : 3 * DH].astype(F32)
-        total = total + refs[0][...].astype(F32)
+        total = total + a[:, 2 * DH :].astype(F32) + b[:, 2 * DH :].astype(F32)
+        total = total + refs[0][:, :DH].astype(F32)
     for source, out, cols in ((dk_soft, dk_all, slice(0, DH)), (dv_soft, dv_all, slice(DH, 2 * DH))):
         out[...] = source[HALF : HALF + 2 * rows, :]
         out[at(way["block_a"] * rows, rows), :] += a[:, cols].astype(F32)
@@ -536,15 +536,15 @@
         chunk, to_a, to_b, to_c = call(
             second_kernel, "second",
             [
-                like((half, width), F32), like((rows, 3 * DH), BF), like((rows, 4 * DH), BF),
-                like((DH, DH), BF),
+                like((half, width), F32), like((rows, 3 * DH), BF), like((rows, 3 * DH), BF),
+                like((rows, 2 * DH), BF),
             ],
             [piece_keep, piece_got, dstate, dk_soft, dv_soft],
         )
-        b, a, c = over_z(to_b, 1), over_z(to_a, 0), [over_z(to_c, 2)]
+        a, b, c = over_z(to_a, 0), over_z(to_b, 1), [over_z(to_c, 2)]
         summed = call(
             functools.partial(weight_sum_kernel, scale), "weight_sum", [like((half, width), BF)],
-            [chunk, b],
+            [chunk] + c,
         )[0]
         got = over_dp(summed, 0)
         both = call(join_kernel, "both", [like((half, 2 * width), BF)], [summed, got])[0]
@@ -564,7 +564,7 @@
         functools.partial(final_kernel, direct), "final",
         [like((rows, 6 * DH), BF), like((rows, 6 * DH), BF)],
         [dstate, mine, pair, dq_soft, dk_soft, dv_soft, dq_lin, dq_lin_pair, a, b]
-        + (c if direct else []),
+        + (c + [both] if direct else []),
         scratch=[pltpu.VMEM((2 * rows, DH), F32)] * 2,
         flops=wg_flops // 4,
     )

time: 55.1 us -> 53.1 us (0.964)
  starting transfers between devices: 22.4 us -> 21.4 us
  waiting for transfers between devices: 24.7 us -> 23.7 us
    ppermute x7, waiting for transfers between devices: 12.7 us -> 11.3 us  [over_z(): return lax.ppermute(value, axes, pairs)]
where the time goes in v13:
time: 53.1 us; the launch traced here: 53 us
  waiting for transfers between devices  23.7 us (45%)
  starting transfers between devices  21.4 us (40%)
  Pallas kernels  7.06 us (13%)
  between operations  0.79 us (1%)
    ppermute x7, waiting for transfers between devices, over_z(): return lax.ppermute(value, axes, pairs)  11.3 us
    ppermute x7, starting transfers between devices, over_z(): return lax.ppermute(value, axes, pairs)  10.9 us
    ppermute x6, waiting for transfers between devices, over_dp(): return lax.ppermute(value, ('dp', 'core'), pairs)  9.88 us
    ppermute x6, starting transfers between devices, over_dp(): return lax.ppermute(value, ('dp', 'core'), pairs)  9.16 us
    pallas_call x17, Pallas kernels, call(): pl.pallas_call(kernel, name=name, out_shape=list(outs), in_specs=spaces o...  7.06 us
    ppermute x7, waiting for transfers between devices, over_core(): return lax.ppermute(value, 'core', pair_perm)  2.59 us
    ppermute x7, starting transfers between devices, over_core(): return lax.ppermute(value, 'core', pair_perm)  1.32 us
  transfers between devices with their start and end apart: 20, of which 12 were waited for; matrix products, arithmetic and copies ran while one was open for 0% of the time, Pallas kernels for 10%

profile of v13, /device:TPU:0, one launch (start us, length us, event | category | flops | bytes accessed | tf_op | source)
XLA Modules:
  0.0 53.0 jit_solution(4439978554418104376)
XLA Ops:
  0.6 0.5 collective-permute-start
  1.2 0.1 collective-permute-start.1
  1.2 0.4 collective-permute-start.2
  1.7 0.1 collective-permute-start.8
  1.7 1.2 %pack.1 = (bf16[128,768]{1,0:T(8,128)(2,1)S(1)}, bf16[128,1024]{1,0:T(8,128)(2,1)S(1)}, bf16[64,256]{1,0:T(8,128)(2,1)S(1)}, f32[1,128]{1,0:T(1,128)S(1)}) custom-call(bf16[1,128,512]{2,1,0:T(8,128)(2,1)} %q.1, bf16[1,128,512]{2,1,0:T(8,128)(2,1)} %k.1, bf16[1,128,512]{2,1,0:T(8,128)(2,1)} %v.1, bf16[1,128,1024]{2,1,0:T(8,128)(2,1)} %og.1, ...), custom_call_target="tpu_custom_call" | custom-call | bytes 1279488 | tf_op jit(solution)/shard_map/pack/pallas_call | solution.py:66
  2.9 0.0 collective-permute-done.q_pair
  2.9 0.0 collective-permute-done.1.k_pair
  2.9 0.0 collective-permute-done.2.v_pair
  3.0 0.3 state.1
  3.2 3.1 %collective-permute-start.3 = (bf16[128,512]{1,0:T(8,128)(2,1)S(1)}, bf16[128,512]{1,0:T(8,128)(2,1)S(1)}, u32[]{:S(2)}, u32[]{:S(2)}) collective-permute-start(bf16[128,512]{1,0:T(8,128)(2,1)S(1)} %get-tuple-element.50), channel_id=1, source_target_pairs={{0,2},{1,7},{2,0},{3,5},{4,6},{5,3},{6,4},{7,1},{8,10},{9,15},{10,... | collective-permute-start | bytes 393224 | tf_op jit(solution)/shard_map/ppermute | solution.py:432
  6.3 2.5 %collective-permute-start.4 = (bf16[128,512]{1,0:T(8,128)(2,1)S(1)}, bf16[128,512]{1,0:T(8,128)(2,1)S(1)}, u32[]{:S(2)}, u32[]{:S(2)}) collective-permute-start(bf16[128,512]{1,0:T(8,128)(2,1)S(1)} %get-tuple-element.51), channel_id=1, source_target_pairs={{0,6},{1,3},{2,4},{3,1},{4,2},{5,7},{6,0},{7,5},{8,14},{9,11},{10,... | collective-permute-start | bytes 393224 | tf_op jit(solution)/shard_map/ppermute | solution.py:432
  8.8 0.1 collective-permute-start.5
  8.9 0.4 collective-permute-done.3.a.refs_0_
  9.3 6.5 %collective-permute-done.4.b.refs_1_ = bf16[128,512]{1,0:T(8,128)(2,1)S(1)} collective-permute-done((bf16[128,512]{1,0:T(8,128)(2,1)S(1)}, bf16[128,512]{1,0:T(8,128)(2,1)S(1)}, u32[]{:S(2)}, u32[]{:S(2)}) %collective-permute-start.4) | collective-permute-done | bytes 131104 | tf_op jit(solution)/shard_map/ppermute | solution.py:432
  15.7 0.0 collective-permute-done.8.og_recv
  15.7 1.2 %soft_forward.1 = (bf16[256,128]{1,0:T(8,128)(2,1)S(1)}, bf16[512,128]{1,0:T(8,128)(2,1)S(1)}, bf16[512,128]{1,0:T(8,128)(2,1)S(1)}, bf16[256,1024]{1,0:T(8,128)...) custom-call(bf16[128,768]{1,0:T(8,128)(2,1)S(1)} %get-tuple-element., ...), custom_call_target="tpu_custom_call" | custom-call | flops 67108864 | bytes 2949120 | tf_op jit(solution)/shard_map/soft_forward/pallas_call | solution.py:66
  16.9 0.0 collective-permute-done.5.c.refs_2_
  17.0 0.7 %lin_forward.1 = (f32[256,128]{1,0:T(8,128)S(1)}, f32[128,128]{1,0:T(8,128)S(1)}, f32[128,512]{1,0:T(8,128)S(1)}, bf16[256,512]{1,0:T(8,128)(2,1)S(1)}) custom-call(f32[128,128]{1,0:T(8,128)S(1)} %get-tuple-element.58.state, bf16[128,768]{1,0:T(8,128)(2,1)S(1)} %get-tuple-element.49.mine.refs_6_, bf16[128,768]{1,0:T(8,128)(2,1)S(1)} %get-tuple-element.55.pair.refs_7_, ...), custom_call_target="tpu_custom_call" | custom-call | flops 67108864 | bytes 2163200 | tf_op jit(solution)/shard_map/lin_forward/pallas_call | solution.py:66
  17.6 1.6 %collective-permute-start.9 = (bf16[256,512]{1,0:T(8,128)(2,1)S(1)}, bf16[256,512]{1,0:T(8,128)(2,1)S(1)}, u32[]{:S(2)}, u32[]{:S(2)}) collective-permute-start(bf16[256,512]{1,0:T(8,128)(2,1)S(1)} %get-tuple-element.63), channel_id=1, source_target_pairs={{0,8},{1,17},{8,0},{9,25},{16,24},{17,1},{24,16},{25,9},{2,10},{3,... | collective-permute-start | bytes 786440 | tf_op jit(solution)/shard_map/ppermute | solution.py:438
  19.2 0.1 collective-permute-start.6
  19.3 1.2 %collective-permute-done.6.got = bf16[2,64,256]{2,1,0:T(8,128)(2,1)S(1)} collective-permute-done((bf16[2,64,256]{2,1,0:T(8,128)(2,1)S(1)}, bf16[2,64,256]{2,1,0:T(8,128)(2,1)S(1)}, u32[]{:S(2)}, u32[]{:S(2)}) %collective-permute-start.6) | collective-permute-done | bytes 65568 | tf_op jit(solution)/shard_map/ppermute | solution.py:421
  20.6 0.6 %collective-permute-start.7 = (bf16[256,256]{1,0:T(8,128)(2,1)S(1)}, bf16[256,256]{1,0:T(8,128)(2,1)S(1)}, u32[]{:S(2)}, u32[]{:S(2)}) collective-permute-start(bf16[256,256]{1,0:T(8,128)(2,1)S(1)} %w_rows.1.first), channel_id=1, source_target_pairs={{0,8},{1,17},{8,0},{9,25},{16,24},{17,1},{24,16},{25,9},{2,10},{3,... | collective-permute-start | bytes 393224 | tf_op jit(solution)/shard_map/ppermute | solution.py:438
  21.2 2.9 %collective-permute-done.9.got = bf16[256,512]{1,0:T(8,128)(2,1)S(1)} collective-permute-done((bf16[256,512]{1,0:T(8,128)(2,1)S(1)}, bf16[256,512]{1,0:T(8,128)(2,1)S(1)}, u32[]{:S(2)}, u32[]{:S(2)}) %collective-permute-start.9) | collective-permute-done | bytes 262176 | tf_op jit(solution)/shard_map/ppermute | solution.py:438
  24.1 0.1 fold.1
  24.1 1.9 %collective-permute-start.11 = (bf16[256,256]{1,0:T(8,128)(2,1)S(1)}, bf16[256,256]{1,0:T(8,128)(2,1)S(1)}, u32[]{:S(2)}, u32[]{:S(2)}) collective-permute-start(bf16[256,256]{1,0:T(8,128)(2,1)S(1)} %get-tuple-element.64.refs_0_), channel_id=1, source_target_pairs={{0,16},{1,9},{8,24},{9,1},{16,0},{17,25},{24,8},{25,17},{2,18},{3,... | collective-permute-start | bytes 393224 | tf_op jit(solution)/shard_map/ppermute | solution.py:438
  26.0 0.5 %collective-permute-done.7.second = bf16[256,256]{1,0:T(8,128)(2,1)S(1)} collective-permute-done((bf16[256,256]{1,0:T(8,128)(2,1)S(1)}, bf16[256,256]{1,0:T(8,128)(2,1)S(1)}, u32[]{:S(2)}, u32[]{:S(2)}) %collective-permute-start.7) | collective-permute-done | bytes 131104 | tf_op jit(solution)/shard_map/ppermute | solution.py:438
  26.6 1.9 %collective-permute-start.10 = (bf16[256,512]{1,0:T(8,128)(2,1)S(1)}, bf16[256,512]{1,0:T(8,128)(2,1)S(1)}, u32[]{:S(2)}, u32[]{:S(2)}) collective-permute-start(bf16[256,512]{1,0:T(8,128)(2,1)S(1)} %w_half.1.refs_0_), channel_id=1, source_target_pairs={{0,16},{1,9},{8,24},{9,1},{16,0},{17,25},{24,8},{25,17},{2,18},{3,... | collective-permute-start | bytes 786440 | tf_op jit(solution)/shard_map/ppermute | solution.py:438
  28.5 0.7 %collective-permute-done.11.got = bf16[256,256]{1,0:T(8,128)(2,1)S(1)} collective-permute-done((bf16[256,256]{1,0:T(8,128)(2,1)S(1)}, bf16[256,256]{1,0:T(8,128)(2,1)S(1)}, u32[]{:S(2)}, u32[]{:S(2)}) %collective-permute-start.11) | collective-permute-done | bytes 131104 | tf_op jit(solution)/shard_map/ppermute | solution.py:438
  29.2 0.1 rows.1
  29.2 0.1 collective-permute-start.12
  29.3 1.3 %collective-permute-done.12.got = f32[128,256]{1,0:T(8,128)S(1)} collective-permute-done((f32[128,256]{1,0:T(8,128)S(1)}, f32[128,256]{1,0:T(8,128)S(1)}, u32[]{:S(2)}, u32[]{:S(2)}) %collective-permute-start.12) | collective-permute-done | bytes 131104 | tf_op jit(solution)/shard_map/ppermute | solution.py:421
  30.7 0.8 %collective-permute-start.13 = (bf16[128,256]{1,0:T(8,128)(2,1)S(1)}, bf16[128,256]{1,0:T(8,128)(2,1)S(1)}, u32[]{:S(2)}, u32[]{:S(2)}) collective-permute-start(bf16[128,256]{1,0:T(8,128)(2,1)S(1)} %get-tuple-element.82), channel_id=1, source_target_pairs={{0,2},{1,7},{2,0},{3,5},{4,6},{5,3},{6,4},{7,1},{8,10},{9,15},{10,... | collective-permute-start | bytes 196616 | tf_op jit(solution)/shard_map/ppermute | solution.py:432
  31.5 1.5 %collective-permute-done.10.refs_1_ = bf16[256,512]{1,0:T(8,128)(2,1)S(1)} collective-permute-done((bf16[256,512]{1,0:T(8,128)(2,1)S(1)}, bf16[256,512]{1,0:T(8,128)(2,1)S(1)}, u32[]{:S(2)}, u32[]{:S(2)}) %collective-permute-start.10) | collective-permute-done | bytes 262176 | tf_op jit(solution)/shard_map/ppermute | solution.py:438
  33.0 1.5 %backward.1 = (bf16[128,128]{1,0:T(8,128)(2,1)S(1)}, bf16[128,128]{1,0:T(8,128)(2,1)S(1)}, f32[128,128]{1,0:T(8,128)S(1)}, f32[256,128]{1,0:T(8,128)S(1)}, f32[5...) custom-call(bf16[256,512]{1,0:T(8,128)(2,1)S(1)} %w_half.1.refs_0_, bf16[256,512]{1,0:T(8,128)(2,1)S(1)} %collective-permute-done.10.refs_1_, ...), custom_call_target="tpu_custom_call" | custom-call | flops 335544320 | bytes 3408384 | tf_op jit(solution)/shard_map/backward/pallas_call | solution.py:66
  34.5 0.5 collective-permute-done.13.got
  35.1 2.7 %collective-permute-start.16 = (bf16[128,256]{1,0:T(8,128)(2,1)S(1)}, bf16[128,256]{1,0:T(8,128)(2,1)S(1)}, u32[]{:S(2)}, u32[]{:S(2)}) collective-permute-start(bf16[128,256]{1,0:T(8,128)(2,1)S(1)} %get-tuple-element.85), channel_id=1, source_target_pairs={{0,4},{1,5},{2,6},{3,7},{4,0},{5,1},{6,2},{7,3},{8,12},{9,13},{10,... | collective-permute-start | bytes 196616 | tf_op jit(solution)/shard_map/ppermute | solution.py:432
  37.8 0.9 %collective-permute-start.14 = (bf16[128,384]{1,0:T(8,128)(2,1)S(1)}, bf16[128,384]{1,0:T(8,128)(2,1)S(1)}, u32[]{:S(2)}, u32[]{:S(2)}) collective-permute-start(bf16[128,384]{1,0:T(8,128)(2,1)S(1)} %get-tuple-element.83), channel_id=1, source_target_pairs={{0,2},{1,7},{2,0},{3,5},{4,6},{5,3},{6,4},{7,1},{8,10},{9,15},{10,... | collective-permute-start | bytes 294920 | tf_op jit(solution)/shard_map/ppermute | solution.py:432
  38.7 0.8 %collective-permute-start.15 = (bf16[128,384]{1,0:T(8,128)(2,1)S(1)}, bf16[128,384]{1,0:T(8,128)(2,1)S(1)}, u32[]{:S(2)}, u32[]{:S(2)}) collective-permute-start(bf16[128,384]{1,0:T(8,128)(2,1)S(1)} %get-tuple-element.84), channel_id=1, source_target_pairs={{0,6},{1,3},{2,4},{3,1},{4,2},{5,7},{6,0},{7,5},{8,14},{9,11},{10,... | collective-permute-start | bytes 294920 | tf_op jit(solution)/shard_map/ppermute | solution.py:432
  39.5 3.9 %collective-permute-done.16.got.refs_0_ = bf16[128,256]{1,0:T(8,128)(2,1)S(1)} collective-permute-done((bf16[128,256]{1,0:T(8,128)(2,1)S(1)}, bf16[128,256]{1,0:T(8,128)(2,1)S(1)}, u32[]{:S(2)}, u32[]{:S(2)}) %collective-permute-start.16) | collective-permute-done | bytes 65568 | tf_op jit(solution)/shard_map/ppermute | solution.py:432
  43.5 1.4 %collective-permute-start.17 = (bf16[64,256]{1,0:T(8,128)(2,1)S(1)}, bf16[64,256]{1,0:T(8,128)(2,1)S(1)}, u32[]{:S(2)}, u32[]{:S(2)}) collective-permute-start(bf16[64,256]{1,0:T(8,128)(2,1)S(1)} %weight_sum.1.first), channel_id=1, source_target_pairs={{0,8},{1,17},{8,0},{9,25},{16,24},{17,1},{24,16},{25,9},{2,10},{3,... | collective-permute-start | bytes 98312 | tf_op jit(solution)/shard_map/ppermute | solution.py:438
  44.8 2.6 %collective-permute-done.17.second = bf16[64,256]{1,0:T(8,128)(2,1)S(1)} collective-permute-done((bf16[64,256]{1,0:T(8,128)(2,1)S(1)}, bf16[64,256]{1,0:T(8,128)(2,1)S(1)}, u32[]{:S(2)}, u32[]{:S(2)}) %collective-permute-start.17) | collective-permute-done | bytes 32800 | tf_op jit(solution)/shard_map/ppermute | solution.py:438
  47.5 0.0 collective-permute-done.14.a
  47.5 0.0 collective-permute-done.15.b
  47.5 0.4 final.1
  47.9 0.1 collective-permute-start.18
  47.9 1.9 %collective-permute-start.19 = (bf16[64,512]{1,0:T(8,128)(2,1)S(1)}, bf16[64,512]{1,0:T(8,128)(2,1)S(1)}, u32[]{:S(2)}, u32[]{:S(2)}) collective-permute-start(bf16[64,512]{1,0:T(8,128)(2,1)S(1)} %both.1.refs_1_), channel_id=1, source_target_pairs={{0,16},{1,9},{8,24},{9,1},{16,0},{17,25},{24,8},{25,17},{2,18},{3,... | collective-permute-start | bytes 196616 | tf_op jit(solution)/shard_map/ppermute | solution.py:438
  49.8 0.0 collective-permute-done.18.pair
  49.8 0.8 %outputs.1 = (bf16[1,128,512]{2,1,0:T(8,128)(2,1)}, bf16[1,128,512]{2,1,0:T(8,128)(2,1)}, bf16[1,128,512]{2,1,0:T(8,128)(2,1)}) custom-call(bf16[128,768]{1,0:T(8,128)(2,1)S(1)} %get-tuple-element.87.own, bf16[128,768]{1,0:T(8,128)(2,1)S(1)} %collective-permute-done.18.pair), custom_call_target="tpu_custom_call" | custom-call | bytes 786432 | tf_op jit(solution)/shard_map/outputs/pallas_call | solution.py:66
  50.6 1.7 %collective-permute-done.19.got = bf16[64,512]{1,0:T(8,128)(2,1)S(1)} collective-permute-done((bf16[64,512]{1,0:T(8,128)(2,1)S(1)}, bf16[64,512]{1,0:T(8,128)(2,1)S(1)}, u32[]{:S(2)}, u32[]{:S(2)}) %collective-permute-start.19) | collective-permute-done | bytes 65568 | tf_op jit(solution)/shard_map/ppermute | solution.py:438
  52.3 0.7 %weight_join.1 = f32[64,1024]{1,0:T(8,128)} custom-call(bf16[64,512]{1,0:T(8,128)(2,1)S(1)} %both.1.refs_1_, bf16[64,512]{1,0:T(8,128)(2,1)S(1)} %collective-permute-done.19.got, bf16[1,128,512]{2,1,0:T(8,128)(2,1)} %get-tuple-element.44._), custom_call_target="tpu_custom_call" | custom-call | bytes 524288 | tf_op jit(solution)/shard_map/weight_join/pallas_call | solution.py:66
  (7 shorter events, 0.2 us)
Async XLA Ops:
  0.6 2.3 %collective-permute-start = (bf16[1,128,512]{2,1,0:T(8,128)(2,1)}, bf16[1,128,512]{2,1,0:T(8,128)(2,1)S(1)}, u32[]{:S(2)}, u32[]{:S(2)}) collective-permute-start(bf16[1,128,512]{2,1,0:T(8,128)(2,1)} %q.1), channel_id=1, source_target_pairs={{0,1},{1,0},{2,3},{3,2},{4,5},{5,4},{6,7},{7,6},{8,9},{9,8},{10,11... | collective-permute-start | bytes 393224 | tf_op jit(solution)/shard_map/ppermute | solution.py:421
  1.2 1.8 %collective-permute-start.1 = (bf16[1,128,512]{2,1,0:T(8,128)(2,1)}, bf16[1,128,512]{2,1,0:T(8,128)(2,1)S(1)}, u32[]{:S(2)}, u32[]{:S(2)}) collective-permute-start(bf16[1,128,512]{2,1,0:T(8,128)(2,1)} %k.1), channel_id=1, source_target_pairs={{0,1},{1,0},{2,3},{3,2},{4,5},{5,4},{6,7},{7,6},{8,9},{9,8},{10,11... | collective-permute-start | bytes 393224 | tf_op jit(solution)/shard_map/ppermute | solution.py:421
  1.2 1.7 %collective-permute-start.2 = (bf16[1,128,512]{2,1,0:T(8,128)(2,1)}, bf16[1,128,512]{2,1,0:T(8,128)(2,1)S(1)}, u32[]{:S(2)}, u32[]{:S(2)}) collective-permute-start(bf16[1,128,512]{2,1,0:T(8,128)(2,1)} %v.1), channel_id=1, source_target_pairs={{0,1},{1,0},{2,3},{3,2},{4,5},{5,4},{6,7},{7,6},{8,9},{9,8},{10,11... | collective-permute-start | bytes 393224 | tf_op jit(solution)/shard_map/ppermute | solution.py:421
  1.7 14.1 %collective-permute-start.8 = (bf16[128,1024]{1,0:T(8,128)(2,1)}, bf16[128,1024]{1,0:T(8,128)(2,1)S(1)}, u32[]{:S(2)}, u32[]{:S(2)}) collective-permute-start(bf16[128,1024]{1,0:T(8,128)(2,1)} %bitcast.1), channel_id=1, source_target_pairs={{0,1},{1,0},{2,3},{3,2},{4,5},{5,4},{6,7},{7,6},{8,9},{9,8},{10,11... | collective-permute-start | bytes 786440 | tf_op jit(solution)/shard_map/ppermute | solution.py:421
  3.2 6.0 %collective-permute-start.3 = (bf16[128,512]{1,0:T(8,128)(2,1)S(1)}, bf16[128,512]{1,0:T(8,128)(2,1)S(1)}, u32[]{:S(2)}, u32[]{:S(2)}) collective-permute-start(bf16[128,512]{1,0:T(8,128)(2,1)S(1)} %get-tuple-element.50), channel_id=1, source_target_pairs={{0,2},{1,7},{2,0},{3,5},{4,6},{5,3},{6,4},{7,1},{8,10},{9,15},{10,... | collective-permute-start | bytes 393224 | tf_op jit(solution)/shard_map/ppermute | solution.py:432
  6.3 9.4 %collective-permute-start.4 = (bf16[128,512]{1,0:T(8,128)(2,1)S(1)}, bf16[128,512]{1,0:T(8,128)(2,1)S(1)}, u32[]{:S(2)}, u32[]{:S(2)}) collective-permute-start(bf16[128,512]{1,0:T(8,128)(2,1)S(1)} %get-tuple-element.51), channel_id=1, source_target_pairs={{0,6},{1,3},{2,4},{3,1},{4,2},{5,7},{6,0},{7,5},{8,14},{9,11},{10,... | collective-permute-start | bytes 393224 | tf_op jit(solution)/shard_map/ppermute | solution.py:432
  8.8 8.2 %collective-permute-start.5 = (bf16[128,256]{1,0:T(8,128)(2,1)S(1)}, bf16[128,256]{1,0:T(8,128)(2,1)S(1)}, u32[]{:S(2)}, u32[]{:S(2)}) collective-permute-start(bf16[128,256]{1,0:T(8,128)(2,1)S(1)} %get-tuple-element.52), channel_id=1, source_target_pairs={{0,4},{1,5},{2,6},{3,7},{4,0},{5,1},{6,2},{7,3},{8,12},{9,13},{10,... | collective-permute-start | bytes 196616 | tf_op jit(solution)/shard_map/ppermute | solution.py:432
  17.6 6.4 %collective-permute-start.9 = (bf16[256,512]{1,0:T(8,128)(2,1)S(1)}, bf16[256,512]{1,0:T(8,128)(2,1)S(1)}, u32[]{:S(2)}, u32[]{:S(2)}) collective-permute-start(bf16[256,512]{1,0:T(8,128)(2,1)S(1)} %get-tuple-element.63), channel_id=1, source_target_pairs={{0,8},{1,17},{8,0},{9,25},{16,24},{17,1},{24,16},{25,9},{2,10},{3,... | collective-permute-start | bytes 786440 | tf_op jit(solution)/shard_map/ppermute | solution.py:438
  19.2 1.3 %collective-permute-start.6 = (bf16[2,64,256]{2,1,0:T(8,128)(2,1)S(1)}, bf16[2,64,256]{2,1,0:T(8,128)(2,1)S(1)}, u32[]{:S(2)}, u32[]{:S(2)}) collective-permute-start(bf16[2,64,256]{2,1,0:T(8,128)(2,1)S(1)} %get-tuple-element.54), channel_id=1, source_target_pairs={{0,1},{1,0},{2,3},{3,2},{4,5},{5,4},{6,7},{7,6},{8,9},{9,8},{10,11... | collective-permute-start | bytes 196616 | tf_op jit(solution)/shard_map/ppermute | solution.py:421
  20.6 6.0 %collective-permute-start.7 = (bf16[256,256]{1,0:T(8,128)(2,1)S(1)}, bf16[256,256]{1,0:T(8,128)(2,1)S(1)}, u32[]{:S(2)}, u32[]{:S(2)}) collective-permute-start(bf16[256,256]{1,0:T(8,128)(2,1)S(1)} %w_rows.1.first), channel_id=1, source_target_pairs={{0,8},{1,17},{8,0},{9,25},{16,24},{17,1},{24,16},{25,9},{2,10},{3,... | collective-permute-start | bytes 393224 | tf_op jit(solution)/shard_map/ppermute | solution.py:438
  24.1 5.0 %collective-permute-start.11 = (bf16[256,256]{1,0:T(8,128)(2,1)S(1)}, bf16[256,256]{1,0:T(8,128)(2,1)S(1)}, u32[]{:S(2)}, u32[]{:S(2)}) collective-permute-start(bf16[256,256]{1,0:T(8,128)(2,1)S(1)} %get-tuple-element.64.refs_0_), channel_id=1, source_target_pairs={{0,16},{1,9},{8,24},{9,1},{16,0},{17,25},{24,8},{25,17},{2,18},{3,... | collective-permute-start | bytes 393224 | tf_op jit(solution)/shard_map/ppermute | solution.py:438
  26.6 6.4 %collective-permute-start.10 = (bf16[256,512]{1,0:T(8,128)(2,1)S(1)}, bf16[256,512]{1,0:T(8,128)(2,1)S(1)}, u32[]{:S(2)}, u32[]{:S(2)}) collective-permute-start(bf16[256,512]{1,0:T(8,128)(2,1)S(1)} %w_half.1.refs_0_), channel_id=1, source_target_pairs={{0,16},{1,9},{8,24},{9,1},{16,0},{17,25},{24,8},{25,17},{2,18},{3,... | collective-permute-start | bytes 786440 | tf_op jit(solution)/shard_map/ppermute | solution.py:438
  29.2 1.4 %collective-permute-start.12 = (f32[128,256]{1,0:T(8,128)S(1)}, f32[128,256]{1,0:T(8,128)S(1)}, u32[]{:S(2)}, u32[]{:S(2)}) collective-permute-start(f32[128,256]{1,0:T(8,128)S(1)} %get-tuple-element.67), channel_id=1, source_target_pairs={{0,1},{1,0},{2,3},{3,2},{4,5},{5,4},{6,7},{7,6},{8,9},{9,8},{10,11... | collective-permute-start | bytes 393224 | tf_op jit(solution)/shard_map/ppermute | solution.py:421
  30.7 4.3 %collective-permute-start.13 = (bf16[128,256]{1,0:T(8,128)(2,1)S(1)}, bf16[128,256]{1,0:T(8,128)(2,1)S(1)}, u32[]{:S(2)}, u32[]{:S(2)}) collective-permute-start(bf16[128,256]{1,0:T(8,128)(2,1)S(1)} %get-tuple-element.82), channel_id=1, source_target_pairs={{0,2},{1,7},{2,0},{3,5},{4,6},{5,3},{6,4},{7,1},{8,10},{9,15},{10,... | collective-permute-start | bytes 196616 | tf_op jit(solution)/shard_map/ppermute | solution.py:432
  35.1 8.4 %collective-permute-start.16 = (bf16[128,256]{1,0:T(8,128)(2,1)S(1)}, bf16[128,256]{1,0:T(8,128)(2,1)S(1)}, u32[]{:S(2)}, u32[]{:S(2)}) collective-permute-start(bf16[128,256]{1,0:T(8,128)(2,1)S(1)} %get-tuple-element.85), channel_id=1, source_target_pairs={{0,4},{1,5},{2,6},{3,7},{4,0},{5,1},{6,2},{7,3},{8,12},{9,13},{10,... | collective-permute-start | bytes 196616 | tf_op jit(solution)/shard_map/ppermute | solution.py:432
  37.8 9.7 %collective-permute-start.14 = (bf16[128,384]{1,0:T(8,128)(2,1)S(1)}, bf16[128,384]{1,0:T(8,128)(2,1)S(1)}, u32[]{:S(2)}, u32[]{:S(2)}) collective-permute-start(bf16[128,384]{1,0:T(8,128)(2,1)S(1)} %get-tuple-element.83), channel_id=1, source_target_pairs={{0,2},{1,7},{2,0},{3,5},{4,6},{5,3},{6,4},{7,1},{8,10},{9,15},{10,... | collective-permute-start | bytes 294920 | tf_op jit(solution)/shard_map/ppermute | solution.py:432
  38.7 8.7 %collective-permute-start.15 = (bf16[128,384]{1,0:T(8,128)(2,1)S(1)}, bf16[128,384]{1,0:T(8,128)(2,1)S(1)}, u32[]{:S(2)}, u32[]{:S(2)}) collective-permute-start(bf16[128,384]{1,0:T(8,128)(2,1)S(1)} %get-tuple-element.84), channel_id=1, source_target_pairs={{0,6},{1,3},{2,4},{3,1},{4,2},{5,7},{6,0},{7,5},{8,14},{9,11},{10,... | collective-permute-start | bytes 294920 | tf_op jit(solution)/shard_map/ppermute | solution.py:432
  43.5 4.0 %collective-permute-start.17 = (bf16[64,256]{1,0:T(8,128)(2,1)S(1)}, bf16[64,256]{1,0:T(8,128)(2,1)S(1)}, u32[]{:S(2)}, u32[]{:S(2)}) collective-permute-start(bf16[64,256]{1,0:T(8,128)(2,1)S(1)} %weight_sum.1.first), channel_id=1, source_target_pairs={{0,8},{1,17},{8,0},{9,25},{16,24},{17,1},{24,16},{25,9},{2,10},{3,... | collective-permute-start | bytes 98312 | tf_op jit(solution)/shard_map/ppermute | solution.py:438
  47.9 1.9 %collective-permute-start.18 = (bf16[128,768]{1,0:T(8,128)(2,1)S(1)}, bf16[128,768]{1,0:T(8,128)(2,1)S(1)}, u32[]{:S(2)}, u32[]{:S(2)}) collective-permute-start(bf16[128,768]{1,0:T(8,128)(2,1)S(1)} %get-tuple-element.88), channel_id=1, source_target_pairs={{0,1},{1,0},{2,3},{3,2},{4,5},{5,4},{6,7},{7,6},{8,9},{9,8},{10,11... | collective-permute-start | bytes 589832 | tf_op jit(solution)/shard_map/ppermute | solution.py:421
  47.9 4.3 %collective-permute-start.19 = (bf16[64,512]{1,0:T(8,128)(2,1)S(1)}, bf16[64,512]{1,0:T(8,128)(2,1)S(1)}, u32[]{:S(2)}, u32[]{:S(2)}) collective-permute-start(bf16[64,512]{1,0:T(8,128)(2,1)S(1)} %both.1.refs_1_), channel_id=1, source_target_pairs={{0,16},{1,9},{8,24},{9,1},{16,0},{17,25},{24,8},{25,17},{2,18},{3,... | collective-permute-start | bytes 196616 | tf_op jit(solution)/shard_map/ppermute | solution.py:438

commit v14 on v12

--- a/solution.py
+++ b/solution.py
@@ -86,9 +86,9 @@
 def links(direct):
     core, z, dp = places()
     step = 1 + core
-    turn = lax.rem(z + core, 2) if direct else 1
+    turn = lax.rem(z + 1, 2) if direct else 1
     return dict(
-        first=1 + 2 * core, second=3 - 2 * core, step=step, other=3 - step,
+        first=3, second=1, step=step, other=3 - step,
         block_a=1 - turn, block_b=turn,
         halo_a=(1 - turn if direct else 1), halo_b=(turn if direct else 0),
     )
@@ -334,7 +334,7 @@
         rows = slice(group * half, (group + 1) * half)
         heads[2 * group + core] = own[rows, :]
         heads[2 * group + 1 - core] = got[rows, :]
-    for index, step in enumerate((way["first"], 2)):
+    for index, step in enumerate((2, way["first"])):
         send[index * half : (index + 1) * half, :] = heads[z ^ step].astype(BF)
     for index, step in enumerate((0, way["second"])):
         keep[index * half : (index + 1) * half, :] = heads[z ^ step]
@@ -425,7 +425,7 @@
         for z in range(n_z):
             for c in range(2):
                 if direct:
-                    there = z ^ (1 + 2 * c, 3 - 2 * c, 2)[which]
+                    there = z ^ (3, 1, 2)[which]
                 else:
                     there = (z + (1 if (which == 1) != back else -1)) % n_z
                 pairs.append((2 * z + c, 2 * there + c))
@@ -518,7 +518,7 @@
             chunk_kernel, "chunk", [like((DH, width), BF), like((DH, width), F32)],
             [row_own, row_recv], scratch=[pltpu.VMEM((HEADS, half, width), F32)],
         )
-        piece_got = over_z(piece_send, 0)
+        piece_got = over_z(piece_send, 2)
         weights.append(piece_keep)
     dq_lin, dq_lin_pair, dstate, dq_soft, dk_soft, dv_soft = call(
         functools.partial(backward_kernel, direct), "backward",
@@ -541,7 +541,7 @@
             ],
             [piece_keep, piece_got, dstate, dk_soft, dv_soft],
         )
-        b, a, c = over_z(to_b, 1), over_z(to_a, 0), [over_z(to_c, 2)]
+        a, b, c = over_z(to_a, 0), over_z(to_b, 1), [over_z(to_c, 2)]
         summed = call(
             functools.partial(weight_sum_kernel, scale), "weight_sum", [like((half, width), BF)],
             [chunk, b],
@@ -564,7 +564,7 @@
         functools.partial(final_kernel, direct), "final",
         [like((rows, 6 * DH), BF), like((rows, 6 * DH), BF)],
         [dstate, mine, pair, dq_soft, dk_soft, dv_soft, dq_lin, dq_lin_pair, a, b]
-        + (c if direct else []),
+        + (c + [both] if direct else []),
         scratch=[pltpu.VMEM((2 * rows, DH), F32)] * 2,
         flops=wg_flops // 4,
     )

time: 55.1 us -> 55.4 us (level)
  waiting for transfers between devices: 24.7 us -> 27.2 us
  starting transfers between devices: 22.4 us -> 20.3 us
    ppermute x7, waiting for transfers between devices: 12.7 us -> 16.4 us  [over_z(): return lax.ppermute(value, axes, pairs)]
    ppermute x6, starting transfers between devices: 9.63 us -> 7.81 us  [over_dp(): return lax.ppermute(value, ('dp', 'core'), pairs)]
    ppermute x6, waiting for transfers between devices: 9.35 us -> 7.71 us  [over_dp(): return lax.ppermute(value, ('dp', 'core'), pairs)]
  transfers between devices with their start and end apart: 20 -> 20, of which waited for: 12 -> 12; matrix products, arithmetic and copies ran while one was open for 0% -> 0% of each run, Pallas kernels for 10% -> 9%
where the time goes in v14:
time: 55.4 us; the launch traced here: 55.3 us
  waiting for transfers between devices  27.2 us (49%)
  starting transfers between devices  20.3 us (37%)
  Pallas kernels  7.04 us (13%)
  between operations  0.79 us (1%)
    ppermute x7, waiting for transfers between devices, over_z(): return lax.ppermute(value, axes, pairs)  16.4 us
    ppermute x7, starting transfers between devices, over_z(): return lax.ppermute(value, axes, pairs)  11.1 us
    ppermute x6, starting transfers between devices, over_dp(): return lax.ppermute(value, ('dp', 'core'), pairs)  7.81 us
    ppermute x6, waiting for transfers between devices, over_dp(): return lax.ppermute(value, ('dp', 'core'), pairs)  7.71 us
    pallas_call x17, Pallas kernels, call(): pl.pallas_call(kernel, name=name, out_shape=list(outs), in_specs=spaces o...  7.04 us
    ppermute x7, waiting for transfers between devices, over_core(): return lax.ppermute(value, 'core', pair_perm)  3.09 us
    ppermute x7, starting transfers between devices, over_core(): return lax.ppermute(value, 'core', pair_perm)  1.32 us
  transfers between devices with their start and end apart: 20, of which 12 were waited for; matrix products, arithmetic and copies ran while one was open for 0% of the time, Pallas kernels for 9%

profile of v14, /device:TPU:0, one launch (start us, length us, event | category | flops | bytes accessed | tf_op | source)
XLA Modules:
  0.0 55.3 jit_solution(17382608151021500110)
XLA Ops:
  0.6 0.5 collective-permute-start
  1.2 0.1 collective-permute-start.1
  1.2 0.4 collective-permute-start.2
  1.7 0.1 collective-permute-start.8
  1.7 1.2 %pack.1 = (bf16[128,768]{1,0:T(8,128)(2,1)S(1)}, bf16[128,1024]{1,0:T(8,128)(2,1)S(1)}, bf16[64,256]{1,0:T(8,128)(2,1)S(1)}, f32[1,128]{1,0:T(1,128)S(1)}) custom-call(bf16[1,128,512]{2,1,0:T(8,128)(2,1)} %q.1, bf16[1,128,512]{2,1,0:T(8,128)(2,1)} %k.1, bf16[1,128,512]{2,1,0:T(8,128)(2,1)} %v.1, bf16[1,128,1024]{2,1,0:T(8,128)(2,1)} %og.1, ...), custom_call_target="tpu_custom_call" | custom-call | bytes 1279488 | tf_op jit(solution)/shard_map/pack/pallas_call | solution.py:66
  2.9 0.0 collective-permute-done.q_pair
  2.9 0.0 collective-permute-done.1.k_pair
  2.9 0.0 collective-permute-done.2.v_pair
  3.0 0.3 state.1
  3.2 5.1 %collective-permute-start.3 = (bf16[128,512]{1,0:T(8,128)(2,1)S(1)}, bf16[128,512]{1,0:T(8,128)(2,1)S(1)}, u32[]{:S(2)}, u32[]{:S(2)}) collective-permute-start(bf16[128,512]{1,0:T(8,128)(2,1)S(1)} %get-tuple-element.50), channel_id=1, source_target_pairs={{0,6},{1,7},{2,4},{3,5},{4,2},{5,3},{6,0},{7,1},{8,14},{9,15},{10,... | collective-permute-start | bytes 393224 | tf_op jit(solution)/shard_map/ppermute | solution.py:432
  8.3 0.0 collective-permute-start.4
  8.3 0.6 %collective-permute-start.5 = (bf16[128,256]{1,0:T(8,128)(2,1)S(1)}, bf16[128,256]{1,0:T(8,128)(2,1)S(1)}, u32[]{:S(2)}, u32[]{:S(2)}) collective-permute-start(bf16[128,256]{1,0:T(8,128)(2,1)S(1)} %get-tuple-element.52), channel_id=1, source_target_pairs={{0,4},{1,5},{2,6},{3,7},{4,0},{5,1},{6,2},{7,3},{8,12},{9,13},{10,... | collective-permute-start | bytes 196616 | tf_op jit(solution)/shard_map/ppermute | solution.py:432
  9.0 3.7 %collective-permute-done.3.a.refs_0_ = bf16[128,512]{1,0:T(8,128)(2,1)S(1)} collective-permute-done((bf16[128,512]{1,0:T(8,128)(2,1)S(1)}, bf16[128,512]{1,0:T(8,128)(2,1)S(1)}, u32[]{:S(2)}, u32[]{:S(2)}) %collective-permute-start.3) | collective-permute-done | bytes 131104 | tf_op jit(solution)/shard_map/ppermute | solution.py:432
  12.7 3.3 %collective-permute-done.4.b.refs_1_ = bf16[128,512]{1,0:T(8,128)(2,1)S(1)} collective-permute-done((bf16[128,512]{1,0:T(8,128)(2,1)S(1)}, bf16[128,512]{1,0:T(8,128)(2,1)S(1)}, u32[]{:S(2)}, u32[]{:S(2)}) %collective-permute-start.4) | collective-permute-done | bytes 131104 | tf_op jit(solution)/shard_map/ppermute | solution.py:432
  16.0 0.0 collective-permute-done.8.og_recv
  16.0 1.2 %soft_forward.1 = (bf16[256,128]{1,0:T(8,128)(2,1)S(1)}, bf16[512,128]{1,0:T(8,128)(2,1)S(1)}, bf16[512,128]{1,0:T(8,128)(2,1)S(1)}, bf16[256,1024]{1,0:T(8,128)...) custom-call(bf16[128,768]{1,0:T(8,128)(2,1)S(1)} %get-tuple-element., ...), custom_call_target="tpu_custom_call" | custom-call | flops 67108864 | bytes 2949120 | tf_op jit(solution)/shard_map/soft_forward/pallas_call | solution.py:66
  17.2 0.0 collective-permute-done.5.c.refs_2_
  17.2 0.7 %lin_forward.1 = (f32[256,128]{1,0:T(8,128)S(1)}, f32[128,128]{1,0:T(8,128)S(1)}, f32[128,512]{1,0:T(8,128)S(1)}, bf16[256,512]{1,0:T(8,128)(2,1)S(1)}) custom-call(f32[128,128]{1,0:T(8,128)S(1)} %get-tuple-element.58.state, bf16[128,768]{1,0:T(8,128)(2,1)S(1)} %get-tuple-element.49.mine.refs_6_, bf16[128,768]{1,0:T(8,128)(2,1)S(1)} %get-tuple-element.55.pair.refs_7_, ...), custom_call_target="tpu_custom_call" | custom-call | flops 67108864 | bytes 2163200 | tf_op jit(solution)/shard_map/lin_forward/pallas_call | solution.py:66
  17.9 1.6 %collective-permute-start.9 = (bf16[256,512]{1,0:T(8,128)(2,1)S(1)}, bf16[256,512]{1,0:T(8,128)(2,1)S(1)}, u32[]{:S(2)}, u32[]{:S(2)}) collective-permute-start(bf16[256,512]{1,0:T(8,128)(2,1)S(1)} %get-tuple-element.63), channel_id=1, source_target_pairs={{0,8},{1,17},{8,0},{9,25},{16,24},{17,1},{24,16},{25,9},{2,10},{3,... | collective-permute-start | bytes 786440 | tf_op jit(solution)/shard_map/ppermute | solution.py:438
  19.5 0.1 collective-permute-start.6
  19.6 1.2 %collective-permute-done.6.got = bf16[2,64,256]{2,1,0:T(8,128)(2,1)S(1)} collective-permute-done((bf16[2,64,256]{2,1,0:T(8,128)(2,1)S(1)}, bf16[2,64,256]{2,1,0:T(8,128)(2,1)S(1)}, u32[]{:S(2)}, u32[]{:S(2)}) %collective-permute-start.6) | collective-permute-done | bytes 65568 | tf_op jit(solution)/shard_map/ppermute | solution.py:421
  20.8 0.7 %collective-permute-start.7 = (bf16[256,256]{1,0:T(8,128)(2,1)S(1)}, bf16[256,256]{1,0:T(8,128)(2,1)S(1)}, u32[]{:S(2)}, u32[]{:S(2)}) collective-permute-start(bf16[256,256]{1,0:T(8,128)(2,1)S(1)} %w_rows.1.first), channel_id=1, source_target_pairs={{0,8},{1,17},{8,0},{9,25},{16,24},{17,1},{24,16},{25,9},{2,10},{3,... | collective-permute-start | bytes 393224 | tf_op jit(solution)/shard_map/ppermute | solution.py:438
  21.6 2.8 %collective-permute-done.9.got = bf16[256,512]{1,0:T(8,128)(2,1)S(1)} collective-permute-done((bf16[256,512]{1,0:T(8,128)(2,1)S(1)}, bf16[256,512]{1,0:T(8,128)(2,1)S(1)}, u32[]{:S(2)}, u32[]{:S(2)}) %collective-permute-start.9) | collective-permute-done | bytes 262176 | tf_op jit(solution)/shard_map/ppermute | solution.py:438
  24.3 0.1 fold.1
  24.4 1.6 %collective-permute-start.11 = (bf16[256,256]{1,0:T(8,128)(2,1)S(1)}, bf16[256,256]{1,0:T(8,128)(2,1)S(1)}, u32[]{:S(2)}, u32[]{:S(2)}) collective-permute-start(bf16[256,256]{1,0:T(8,128)(2,1)S(1)} %get-tuple-element.64.refs_0_), channel_id=1, source_target_pairs={{0,16},{1,9},{8,24},{9,1},{16,0},{17,25},{24,8},{25,17},{2,18},{3,... | collective-permute-start | bytes 393224 | tf_op jit(solution)/shard_map/ppermute | solution.py:438
  26.0 0.0 collective-permute-done.7.second
  26.0 1.5 %collective-permute-start.10 = (bf16[256,512]{1,0:T(8,128)(2,1)S(1)}, bf16[256,512]{1,0:T(8,128)(2,1)S(1)}, u32[]{:S(2)}, u32[]{:S(2)}) collective-permute-start(bf16[256,512]{1,0:T(8,128)(2,1)S(1)} %w_half.1.refs_0_), channel_id=1, source_target_pairs={{0,16},{1,9},{8,24},{9,1},{16,0},{17,25},{24,8},{25,17},{2,18},{3,... | collective-permute-start | bytes 786440 | tf_op jit(solution)/shard_map/ppermute | solution.py:438
  27.5 2.0 %collective-permute-done.11.got = bf16[256,256]{1,0:T(8,128)(2,1)S(1)} collective-permute-done((bf16[256,256]{1,0:T(8,128)(2,1)S(1)}, bf16[256,256]{1,0:T(8,128)(2,1)S(1)}, u32[]{:S(2)}, u32[]{:S(2)}) %collective-permute-start.11) | collective-permute-done | bytes 131104 | tf_op jit(solution)/shard_map/ppermute | solution.py:438
  29.4 0.1 rows.1
  29.5 0.1 collective-permute-start.12
  29.6 1.3 %collective-permute-done.12.got = f32[128,256]{1,0:T(8,128)S(1)} collective-permute-done((f32[128,256]{1,0:T(8,128)S(1)}, f32[128,256]{1,0:T(8,128)S(1)}, u32[]{:S(2)}, u32[]{:S(2)}) %collective-permute-start.12) | collective-permute-done | bytes 131104 | tf_op jit(solution)/shard_map/ppermute | solution.py:421
  30.9 1.8 %collective-permute-start.13 = (bf16[128,256]{1,0:T(8,128)(2,1)S(1)}, bf16[128,256]{1,0:T(8,128)(2,1)S(1)}, u32[]{:S(2)}, u32[]{:S(2)}) collective-permute-start(bf16[128,256]{1,0:T(8,128)(2,1)S(1)} %get-tuple-element.82), channel_id=1, source_target_pairs={{0,4},{1,5},{2,6},{3,7},{4,0},{5,1},{6,2},{7,3},{8,12},{9,13},{10,... | collective-permute-start | bytes 196616 | tf_op jit(solution)/shard_map/ppermute | solution.py:432
  32.8 0.0 collective-permute-done.10.refs_1_
  32.8 1.5 %backward.1 = (bf16[128,128]{1,0:T(8,128)(2,1)S(1)}, bf16[128,128]{1,0:T(8,128)(2,1)S(1)}, f32[128,128]{1,0:T(8,128)S(1)}, f32[256,128]{1,0:T(8,128)S(1)}, f32[5...) custom-call(bf16[256,512]{1,0:T(8,128)(2,1)S(1)} %w_half.1.refs_0_, bf16[256,512]{1,0:T(8,128)(2,1)S(1)} %collective-permute-done.10.refs_1_, ...), custom_call_target="tpu_custom_call" | custom-call | flops 335544320 | bytes 3408384 | tf_op jit(solution)/shard_map/backward/pallas_call | solution.py:66
  34.3 3.2 %collective-permute-done.13.got = bf16[128,256]{1,0:T(8,128)(2,1)S(1)} collective-permute-done((bf16[128,256]{1,0:T(8,128)(2,1)S(1)}, bf16[128,256]{1,0:T(8,128)(2,1)S(1)}, u32[]{:S(2)}, u32[]{:S(2)}) %collective-permute-start.13) | collective-permute-done | bytes 65568 | tf_op jit(solution)/shard_map/ppermute | solution.py:432
  37.6 0.1 collective-permute-start.15
  37.7 1.9 %collective-permute-start.14 = (bf16[128,384]{1,0:T(8,128)(2,1)S(1)}, bf16[128,384]{1,0:T(8,128)(2,1)S(1)}, u32[]{:S(2)}, u32[]{:S(2)}) collective-permute-start(bf16[128,384]{1,0:T(8,128)(2,1)S(1)} %get-tuple-element.83), channel_id=1, source_target_pairs={{0,6},{1,7},{2,4},{3,5},{4,2},{5,3},{6,0},{7,1},{8,14},{9,15},{10,... | collective-permute-start | bytes 294920 | tf_op jit(solution)/shard_map/ppermute | solution.py:432
  39.6 3.8 %collective-permute-done.15.got.b = bf16[128,512]{1,0:T(8,128)(2,1)S(1)} collective-permute-done((bf16[128,512]{1,0:T(8,128)(2,1)S(1)}, bf16[128,512]{1,0:T(8,128)(2,1)S(1)}, u32[]{:S(2)}, u32[]{:S(2)}) %collective-permute-start.15) | collective-permute-done | bytes 131104 | tf_op jit(solution)/shard_map/ppermute | solution.py:432
  43.4 1.5 %collective-permute-start.17 = (bf16[64,256]{1,0:T(8,128)(2,1)S(1)}, bf16[64,256]{1,0:T(8,128)(2,1)S(1)}, u32[]{:S(2)}, u32[]{:S(2)}) collective-permute-start(bf16[64,256]{1,0:T(8,128)(2,1)S(1)} %weight_sum.1.first), channel_id=1, source_target_pairs={{0,8},{1,17},{8,0},{9,25},{16,24},{17,1},{24,16},{25,9},{2,10},{3,... | collective-permute-start | bytes 98312 | tf_op jit(solution)/shard_map/ppermute | solution.py:438
  45.0 1.6 %collective-permute-start.16 = (bf16[128,128]{1,0:T(8,128)(2,1)S(1)}, bf16[128,128]{1,0:T(8,128)(2,1)S(1)}, u32[]{:S(2)}, u32[]{:S(2)}) collective-permute-start(bf16[128,128]{1,0:T(8,128)(2,1)S(1)} %get-tuple-element.85), channel_id=1, source_target_pairs={{0,4},{1,5},{2,6},{3,7},{4,0},{5,1},{6,2},{7,3},{8,12},{9,13},{10,... | collective-permute-start | bytes 98312 | tf_op jit(solution)/shard_map/ppermute | solution.py:432
  46.5 0.9 %collective-permute-done.17.second = bf16[64,256]{1,0:T(8,128)(2,1)S(1)} collective-permute-done((bf16[64,256]{1,0:T(8,128)(2,1)S(1)}, bf16[64,256]{1,0:T(8,128)(2,1)S(1)}, u32[]{:S(2)}, u32[]{:S(2)}) %collective-permute-start.17) | collective-permute-done | bytes 32800 | tf_op jit(solution)/shard_map/ppermute | solution.py:438
  47.4 2.4 %collective-permute-done.16.refs_0_ = bf16[128,128]{1,0:T(8,128)(2,1)S(1)} collective-permute-done((bf16[128,128]{1,0:T(8,128)(2,1)S(1)}, bf16[128,128]{1,0:T(8,128)(2,1)S(1)}, u32[]{:S(2)}, u32[]{:S(2)}) %collective-permute-start.16) | collective-permute-done | bytes 32800 | tf_op jit(solution)/shard_map/ppermute | solution.py:432
  49.8 0.0 collective-permute-done.14.a
  49.8 0.4 final.1
  50.2 0.1 collective-permute-start.18
  50.2 0.9 %collective-permute-start.19 = (bf16[64,512]{1,0:T(8,128)(2,1)S(1)}, bf16[64,512]{1,0:T(8,128)(2,1)S(1)}, u32[]{:S(2)}, u32[]{:S(2)}) collective-permute-start(bf16[64,512]{1,0:T(8,128)(2,1)S(1)} %both.1.refs_1_), channel_id=1, source_target_pairs={{0,16},{1,9},{8,24},{9,1},{16,0},{17,25},{24,8},{25,17},{2,18},{3,... | collective-permute-start | bytes 196616 | tf_op jit(solution)/shard_map/ppermute | solution.py:438
  51.2 0.5 collective-permute-done.18.pair
  51.7 0.8 %outputs.1 = (bf16[1,128,512]{2,1,0:T(8,128)(2,1)}, bf16[1,128,512]{2,1,0:T(8,128)(2,1)}, bf16[1,128,512]{2,1,0:T(8,128)(2,1)}) custom-call(bf16[128,768]{1,0:T(8,128)(2,1)S(1)} %get-tuple-element.87.own, bf16[128,768]{1,0:T(8,128)(2,1)S(1)} %collective-permute-done.18.pair), custom_call_target="tpu_custom_call" | custom-call | bytes 786432 | tf_op jit(solution)/shard_map/outputs/pallas_call | solution.py:66
  52.5 2.1 %collective-permute-done.19.got = bf16[64,512]{1,0:T(8,128)(2,1)S(1)} collective-permute-done((bf16[64,512]{1,0:T(8,128)(2,1)S(1)}, bf16[64,512]{1,0:T(8,128)(2,1)S(1)}, u32[]{:S(2)}, u32[]{:S(2)}) %collective-permute-start.19) | collective-permute-done | bytes 65568 | tf_op jit(solution)/shard_map/ppermute | solution.py:438
  54.6 0.7 %weight_join.1 = f32[64,1024]{1,0:T(8,128)} custom-call(bf16[64,512]{1,0:T(8,128)(2,1)S(1)} %both.1.refs_1_, bf16[64,512]{1,0:T(8,128)(2,1)S(1)} %collective-permute-done.19.got, bf16[1,128,512]{2,1,0:T(8,128)(2,1)} %get-tuple-element.44._), custom_call_target="tpu_custom_call" | custom-call | bytes 524288 | tf_op jit(solution)/shard_map/weight_join/pallas_call | solution.py:66
  (7 shorter events, 0.2 us)
Async XLA Ops:
  0.6 2.3 %collective-permute-start = (bf16[1,128,512]{2,1,0:T(8,128)(2,1)}, bf16[1,128,512]{2,1,0:T(8,128)(2,1)S(1)}, u32[]{:S(2)}, u32[]{:S(2)}) collective-permute-start(bf16[1,128,512]{2,1,0:T(8,128)(2,1)} %q.1), channel_id=1, source_target_pairs={{0,1},{1,0},{2,3},{3,2},{4,5},{5,4},{6,7},{7,6},{8,9},{9,8},{10,11... | collective-permute-start | bytes 393224 | tf_op jit(solution)/shard_map/ppermute | solution.py:421
  1.2 1.8 %collective-permute-start.1 = (bf16[1,128,512]{2,1,0:T(8,128)(2,1)}, bf16[1,128,512]{2,1,0:T(8,128)(2,1)S(1)}, u32[]{:S(2)}, u32[]{:S(2)}) collective-permute-start(bf16[1,128,512]{2,1,0:T(8,128)(2,1)} %k.1), channel_id=1, source_target_pairs={{0,1},{1,0},{2,3},{3,2},{4,5},{5,4},{6,7},{7,6},{8,9},{9,8},{10,11... | collective-permute-start | bytes 393224 | tf_op jit(solution)/shard_map/ppermute | solution.py:421
  1.2 1.7 %collective-permute-start.2 = (bf16[1,128,512]{2,1,0:T(8,128)(2,1)}, bf16[1,128,512]{2,1,0:T(8,128)(2,1)S(1)}, u32[]{:S(2)}, u32[]{:S(2)}) collective-permute-start(bf16[1,128,512]{2,1,0:T(8,128)(2,1)} %v.1), channel_id=1, source_target_pairs={{0,1},{1,0},{2,3},{3,2},{4,5},{5,4},{6,7},{7,6},{8,9},{9,8},{10,11... | collective-permute-start | bytes 393224 | tf_op jit(solution)/shard_map/ppermute | solution.py:421
  1.7 14.3 %collective-permute-start.8 = (bf16[128,1024]{1,0:T(8,128)(2,1)}, bf16[128,1024]{1,0:T(8,128)(2,1)S(1)}, u32[]{:S(2)}, u32[]{:S(2)}) collective-permute-start(bf16[128,1024]{1,0:T(8,128)(2,1)} %bitcast.1), channel_id=1, source_target_pairs={{0,1},{1,0},{2,3},{3,2},{4,5},{5,4},{6,7},{7,6},{8,9},{9,8},{10,11... | collective-permute-start | bytes 786440 | tf_op jit(solution)/shard_map/ppermute | solution.py:421
  3.2 9.4 %collective-permute-start.3 = (bf16[128,512]{1,0:T(8,128)(2,1)S(1)}, bf16[128,512]{1,0:T(8,128)(2,1)S(1)}, u32[]{:S(2)}, u32[]{:S(2)}) collective-permute-start(bf16[128,512]{1,0:T(8,128)(2,1)S(1)} %get-tuple-element.50), channel_id=1, source_target_pairs={{0,6},{1,7},{2,4},{3,5},{4,2},{5,3},{6,0},{7,1},{8,14},{9,15},{10,... | collective-permute-start | bytes 393224 | tf_op jit(solution)/shard_map/ppermute | solution.py:432
  8.3 7.6 %collective-permute-start.4 = (bf16[128,512]{1,0:T(8,128)(2,1)S(1)}, bf16[128,512]{1,0:T(8,128)(2,1)S(1)}, u32[]{:S(2)}, u32[]{:S(2)}) collective-permute-start(bf16[128,512]{1,0:T(8,128)(2,1)S(1)} %get-tuple-element.51), channel_id=1, source_target_pairs={{0,2},{1,3},{2,0},{3,1},{4,6},{5,7},{6,4},{7,5},{8,10},{9,11},{10,... | collective-permute-start | bytes 393224 | tf_op jit(solution)/shard_map/ppermute | solution.py:432
  8.3 8.8 %collective-permute-start.5 = (bf16[128,256]{1,0:T(8,128)(2,1)S(1)}, bf16[128,256]{1,0:T(8,128)(2,1)S(1)}, u32[]{:S(2)}, u32[]{:S(2)}) collective-permute-start(bf16[128,256]{1,0:T(8,128)(2,1)S(1)} %get-tuple-element.52), channel_id=1, source_target_pairs={{0,4},{1,5},{2,6},{3,7},{4,0},{5,1},{6,2},{7,3},{8,12},{9,13},{10,... | collective-permute-start | bytes 196616 | tf_op jit(solution)/shard_map/ppermute | solution.py:432
  17.9 6.4 %collective-permute-start.9 = (bf16[256,512]{1,0:T(8,128)(2,1)S(1)}, bf16[256,512]{1,0:T(8,128)(2,1)S(1)}, u32[]{:S(2)}, u32[]{:S(2)}) collective-permute-start(bf16[256,512]{1,0:T(8,128)(2,1)S(1)} %get-tuple-element.63), channel_id=1, source_target_pairs={{0,8},{1,17},{8,0},{9,25},{16,24},{17,1},{24,16},{25,9},{2,10},{3,... | collective-permute-start | bytes 786440 | tf_op jit(solution)/shard_map/ppermute | solution.py:438
  19.5 1.3 %collective-permute-start.6 = (bf16[2,64,256]{2,1,0:T(8,128)(2,1)S(1)}, bf16[2,64,256]{2,1,0:T(8,128)(2,1)S(1)}, u32[]{:S(2)}, u32[]{:S(2)}) collective-permute-start(bf16[2,64,256]{2,1,0:T(8,128)(2,1)S(1)} %get-tuple-element.54), channel_id=1, source_target_pairs={{0,1},{1,0},{2,3},{3,2},{4,5},{5,4},{6,7},{7,6},{8,9},{9,8},{10,11... | collective-permute-start | bytes 196616 | tf_op jit(solution)/shard_map/ppermute | solution.py:421
  20.8 5.1 %collective-permute-start.7 = (bf16[256,256]{1,0:T(8,128)(2,1)S(1)}, bf16[256,256]{1,0:T(8,128)(2,1)S(1)}, u32[]{:S(2)}, u32[]{:S(2)}) collective-permute-start(bf16[256,256]{1,0:T(8,128)(2,1)S(1)} %w_rows.1.first), channel_id=1, source_target_pairs={{0,8},{1,17},{8,0},{9,25},{16,24},{17,1},{24,16},{25,9},{2,10},{3,... | collective-permute-start | bytes 393224 | tf_op jit(solution)/shard_map/ppermute | solution.py:438
  24.4 5.0 %collective-permute-start.11 = (bf16[256,256]{1,0:T(8,128)(2,1)S(1)}, bf16[256,256]{1,0:T(8,128)(2,1)S(1)}, u32[]{:S(2)}, u32[]{:S(2)}) collective-permute-start(bf16[256,256]{1,0:T(8,128)(2,1)S(1)} %get-tuple-element.64.refs_0_), channel_id=1, source_target_pairs={{0,16},{1,9},{8,24},{9,1},{16,0},{17,25},{24,8},{25,17},{2,18},{3,... | collective-permute-start | bytes 393224 | tf_op jit(solution)/shard_map/ppermute | solution.py:438
  26.0 6.8 %collective-permute-start.10 = (bf16[256,512]{1,0:T(8,128)(2,1)S(1)}, bf16[256,512]{1,0:T(8,128)(2,1)S(1)}, u32[]{:S(2)}, u32[]{:S(2)}) collective-permute-start(bf16[256,512]{1,0:T(8,128)(2,1)S(1)} %w_half.1.refs_0_), channel_id=1, source_target_pairs={{0,16},{1,9},{8,24},{9,1},{16,0},{17,25},{24,8},{25,17},{2,18},{3,... | collective-permute-start | bytes 786440 | tf_op jit(solution)/shard_map/ppermute | solution.py:438
  29.5 1.4 %collective-permute-start.12 = (f32[128,256]{1,0:T(8,128)S(1)}, f32[128,256]{1,0:T(8,128)S(1)}, u32[]{:S(2)}, u32[]{:S(2)}) collective-permute-start(f32[128,256]{1,0:T(8,128)S(1)} %get-tuple-element.67), channel_id=1, source_target_pairs={{0,1},{1,0},{2,3},{3,2},{4,5},{5,4},{6,7},{7,6},{8,9},{9,8},{10,11... | collective-permute-start | bytes 393224 | tf_op jit(solution)/shard_map/ppermute | solution.py:421
  30.9 6.6 %collective-permute-start.13 = (bf16[128,256]{1,0:T(8,128)(2,1)S(1)}, bf16[128,256]{1,0:T(8,128)(2,1)S(1)}, u32[]{:S(2)}, u32[]{:S(2)}) collective-permute-start(bf16[128,256]{1,0:T(8,128)(2,1)S(1)} %get-tuple-element.82), channel_id=1, source_target_pairs={{0,4},{1,5},{2,6},{3,7},{4,0},{5,1},{6,2},{7,3},{8,12},{9,13},{10,... | collective-permute-start | bytes 196616 | tf_op jit(solution)/shard_map/ppermute | solution.py:432
  37.6 5.8 %collective-permute-start.15 = (bf16[128,512]{1,0:T(8,128)(2,1)S(1)}, bf16[128,512]{1,0:T(8,128)(2,1)S(1)}, u32[]{:S(2)}, u32[]{:S(2)}) collective-permute-start(bf16[128,512]{1,0:T(8,128)(2,1)S(1)} %get-tuple-element.84), channel_id=1, source_target_pairs={{0,2},{1,3},{2,0},{3,1},{4,6},{5,7},{6,4},{7,5},{8,10},{9,11},{10,... | collective-permute-start | bytes 393224 | tf_op jit(solution)/shard_map/ppermute | solution.py:432
  37.7 12.1 %collective-permute-start.14 = (bf16[128,384]{1,0:T(8,128)(2,1)S(1)}, bf16[128,384]{1,0:T(8,128)(2,1)S(1)}, u32[]{:S(2)}, u32[]{:S(2)}) collective-permute-start(bf16[128,384]{1,0:T(8,128)(2,1)S(1)} %get-tuple-element.83), channel_id=1, source_target_pairs={{0,6},{1,7},{2,4},{3,5},{4,2},{5,3},{6,0},{7,1},{8,14},{9,15},{10,... | collective-permute-start | bytes 294920 | tf_op jit(solution)/shard_map/ppermute | solution.py:432
  43.4 4.0 %collective-permute-start.17 = (bf16[64,256]{1,0:T(8,128)(2,1)S(1)}, bf16[64,256]{1,0:T(8,128)(2,1)S(1)}, u32[]{:S(2)}, u32[]{:S(2)}) collective-permute-start(bf16[64,256]{1,0:T(8,128)(2,1)S(1)} %weight_sum.1.first), channel_id=1, source_target_pairs={{0,8},{1,17},{8,0},{9,25},{16,24},{17,1},{24,16},{25,9},{2,10},{3,... | collective-permute-start | bytes 98312 | tf_op jit(solution)/shard_map/ppermute | solution.py:438
  45.0 4.8 %collective-permute-start.16 = (bf16[128,128]{1,0:T(8,128)(2,1)S(1)}, bf16[128,128]{1,0:T(8,128)(2,1)S(1)}, u32[]{:S(2)}, u32[]{:S(2)}) collective-permute-start(bf16[128,128]{1,0:T(8,128)(2,1)S(1)} %get-tuple-element.85), channel_id=1, source_target_pairs={{0,4},{1,5},{2,6},{3,7},{4,0},{5,1},{6,2},{7,3},{8,12},{9,13},{10,... | collective-permute-start | bytes 98312 | tf_op jit(solution)/shard_map/ppermute | solution.py:432
  50.2 1.5 %collective-permute-start.18 = (bf16[128,768]{1,0:T(8,128)(2,1)S(1)}, bf16[128,768]{1,0:T(8,128)(2,1)S(1)}, u32[]{:S(2)}, u32[]{:S(2)}) collective-permute-start(bf16[128,768]{1,0:T(8,128)(2,1)S(1)} %get-tuple-element.88), channel_id=1, source_target_pairs={{0,1},{1,0},{2,3},{3,2},{4,5},{5,4},{6,7},{7,6},{8,9},{9,8},{10,11... | collective-permute-start | bytes 589832 | tf_op jit(solution)/shard_map/ppermute | solution.py:421
  50.2 4.3 %collective-permute-start.19 = (bf16[64,512]{1,0:T(8,128)(2,1)S(1)}, bf16[64,512]{1,0:T(8,128)(2,1)S(1)}, u32[]{:S(2)}, u32[]{:S(2)}) collective-permute-start(bf16[64,512]{1,0:T(8,128)(2,1)S(1)} %both.1.refs_1_), channel_id=1, source_target_pairs={{0,16},{1,9},{8,24},{9,1},{16,0},{17,25},{24,8},{25,17},{2,18},{3,... | collective-permute-start | bytes 196616 | tf_op jit(solution)/shard_map/ppermute | solution.py:438

commit v15 on v13

--- a/solution.py
+++ b/solution.py
@@ -138,31 +138,31 @@
         out[:, DH : 2 * DH] = jnp.where(here, mine[:, VS], pair[:, VS])
     if direct:
         rows = w.shape[0]
-        for out, first in ((to_a, 2 * DH), (to_b, 2 * DH), (to_c, 0)):
-            out[:, first : first + DH] = total.astype(BF)
-            out[:rows, first + DH :] = w[:, :DH]
-            out[rows:, first + DH :] = w[:, DH:]
-
-
-def relay_kernel(w, a, b, c, keep, send, heads):
+        low = total.astype(BF)
+        to_a[:, 2 * DH :] = low
+        to_b[:, 2 * DH :] = low
+        to_c[:, :DH] = low
+        to_c[:rows, DH:] = w[:, :DH]
+        to_c[rows:, DH:] = w[:, DH:]
+
+
+def w_two_kernel(w, c, out):
+    _, z, _ = places()
+    group = lax.div(z, 2)
+    rows = w.shape[0]
+    out[group] = w[...]
+    out[1 - group, :, :DH] = c[:rows, DH:]
+    out[1 - group, :, DH:] = c[rows:, DH:]
+
+
+def w_rows_kernel(own, cycle, diagonal, out):
     core, z, _ = places()
-    way = links(True)
-    rows = w.shape[0]
-    heads[z] = w[...]
-    for source, first, step in ((a, 3 * DH, way["first"]), (b, 3 * DH, way["second"]), (c, DH, 2)):
-        heads[z ^ step, :, :DH] = source[:rows, first:]
-        heads[z ^ step, :, DH:] = source[rows:, first:]
+    half = own.shape[1]
+    matching = lax.rem(z, 2) == core
     for group in range(2):
-        keep[group] = heads[2 * group + core]
-        send[group] = heads[2 * group + 1 - core]
-
-
-def w_rows_kernel(keep, got, out):
-    core, _, _ = places()
-    half = keep.shape[1]
-    for group in range(2):
-        out[at(group * DH + core * half, half), :] = keep[group]
-        out[at(group * DH + (1 - core) * half, half), :] = got[group]
+        near, far = at(group * DH + core * half, half), at(group * DH + (1 - core) * half, half)
+        out[near, :] = jnp.where(matching, own[group], cycle[group])
+        out[far, :] = jnp.where(matching, cycle[group], diagonal[group])
 
 
 def join_kernel(first, second, *refs):
@@ -226,7 +226,7 @@
     total = state[...]
     if direct:
         a, b, c, soft_send, u_out, total_out, keep, out = refs
-        total = total + a[:, 2 * DH : 3 * DH].astype(F32) + b[:, 2 * DH : 3 * DH].astype(F32)
+        total = total + a[:, 2 * DH :].astype(F32) + b[:, 2 * DH :].astype(F32)
         total = total + c[:, :DH].astype(F32)
     else:
         u_out, total_out, keep = refs
@@ -431,6 +431,17 @@
                 pairs.append((2 * z + c, 2 * there + c))
         return lax.ppermute(value, axes, pairs)
 
+    def to_neighbour(value, cycle):
+        pairs = []
+        for z in range(n_z):
+            core_of = z % 2
+            if cycle:
+                pairs.append((2 * z + core_of, 2 * (z ^ 1) + core_of))
+                pairs.append((2 * z + 1 - core_of, 2 * z + core_of))
+            else:
+                pairs.append((2 * z + 1 - core_of, 2 * (z ^ 1) + core_of))
+        return lax.ppermute(value, axes, pairs)
+
     def over_dp(value, which):
         pairs = [
             (2 * d + c, 2 * (d ^ (1 + c, 2 - c)[which]) + c) for d in range(n_dp) for c in range(2)
@@ -454,7 +465,7 @@
         scratch=[pltpu.SemaphoreType.DMA((9,))],
         spaces=[pl.BlockSpec(memory_space=pltpu.HBM)] * 6,
     )
-    wide = 4 * DH if direct else 2 * DH
+    wide = 3 * DH if direct else 2 * DH
     state, pair, to_a, to_b, *rest = call(
         functools.partial(state_kernel, direct), "state",
         [like((DH, DH), F32), like((rows, 6 * DH), BF), like((rows, wide), BF), like((rows, wide), BF)]
@@ -464,12 +475,10 @@
     )
     if direct:
         a, b, c = over_z(to_a, 0), over_z(to_b, 1), [over_z(rest[0], 2)]
-        w_keep, w_send = call(
-            relay_kernel, "relay", [like((2, half, width), BF)] * 2, [w_part, a, b] + c,
-            scratch=[pltpu.VMEM((HEADS, half, width), BF)],
-        )
+        w_two = call(w_two_kernel, "w_two", [like((2, half, width), BF)], [w_part] + c)[0]
         w_own = call(
-            w_rows_kernel, "w_rows", [like((2 * DH, width), BF)], [w_keep, over_core(w_send)]
+            w_rows_kernel, "w_rows", [like((2 * DH, width), BF)],
+            [w_two, to_neighbour(w_two, True), to_neighbour(w_two, False)],
         )[0]
         w_got = over_dp(w_own, 0)
     else:

time: 53.1 us -> 54.3 us (1.023)
  starting transfers between devices: 21.4 us -> 25.3 us
  waiting for transfers between devices: 23.7 us -> 21 us
    ppermute x7, waiting for transfers between devices: 11.3 us -> 8.08 us  [over_z(): return lax.ppermute(value, axes, pairs)]
    ppermute x0 -> x2, starting transfers between devices: none -> 2.88 us  [to_neighbour(): return lax.ppermute(value, axes, pairs)]
    ppermute x7, starting transfers between devices: 10.9 us -> 13.1 us  [over_z(): return lax.ppermute(value, axes, pairs)]
    ppermute x0 -> x2, waiting for transfers between devices: none -> 1.91 us  [to_neighbour(): return lax.ppermute(value, axes, pairs)]
    ppermute x6, starting transfers between devices: 9.16 us -> 8.07 us  [over_dp(): return lax.ppermute(value, ('dp', 'core'), pairs)]
    ppermute x7 -> x6, waiting for transfers between devices: 2.59 us -> 1.71 us  [over_core(): return lax.ppermute(value, 'core', pair_perm)]
    ppermute x6, waiting for transfers between devices: 9.88 us -> 9.32 us  [over_dp(): return lax.ppermute(value, ('dp', 'core'), pairs)]
    ppermute x7 -> x6, starting transfers between devices: 1.32 us -> 1.25 us  [over_core(): return lax.ppermute(value, 'core', pair_perm)]
  transfers between devices with their start and end apart: 20 -> 21, of which waited for: 12 -> 12; matrix products, arithmetic and copies ran while one was open for 0% -> 0% of each run, Pallas kernels for 10% -> 10%
where the time goes in v15:
time: 54.3 us; the launch traced here: 54.2 us
  starting transfers between devices  25.3 us (47%)
  waiting for transfers between devices  21 us (39%)
  Pallas kernels  7.03 us (13%)
  between operations  0.78 us (1%)
    ppermute x7, starting transfers between devices, over_z(): return lax.ppermute(value, axes, pairs)  13.1 us
    ppermute x6, waiting for transfers between devices, over_dp(): return lax.ppermute(value, ('dp', 'core'), pairs)  9.32 us
    ppermute x7, waiting for transfers between devices, over_z(): return lax.ppermute(value, axes, pairs)  8.08 us
    ppermute x6, starting transfers between devices, over_dp(): return lax.ppermute(value, ('dp', 'core'), pairs)  8.07 us
    pallas_call x17, Pallas kernels, call(): pl.pallas_call(kernel, name=name, out_shape=list(outs), in_specs=spaces o...  7.03 us
    ppermute x2, starting transfers between devices, to_neighbour(): return lax.ppermute(value, axes, pairs)  2.88 us
    ppermute x2, waiting for transfers between devices, to_neighbour(): return lax.ppermute(value, axes, pairs)  1.91 us
    ppermute x6, waiting for transfers between devices, over_core(): return lax.ppermute(value, 'core', pair_perm)  1.71 us
  transfers between devices with their start and end apart: 21, of which 12 were waited for; matrix products, arithmetic and copies ran while one was open for 0% of the time, Pallas kernels for 10%

profile of v15, /device:TPU:0, one launch (start us, length us, event | category | flops | bytes accessed | tf_op | source)
XLA Modules:
  0.0 54.2 jit_solution(6630246930350564027)
XLA Ops:
  0.6 0.5 collective-permute-start.7
  1.2 0.1 collective-permute-start
  1.2 0.4 collective-permute-start.1
  1.7 0.1 collective-permute-start.2
  1.7 1.2 %pack.1 = (bf16[128,768]{1,0:T(8,128)(2,1)S(1)}, bf16[128,1024]{1,0:T(8,128)(2,1)S(1)}, bf16[64,256]{1,0:T(8,128)(2,1)S(1)}, f32[1,128]{1,0:T(1,128)S(1)}) custom-call(bf16[1,128,512]{2,1,0:T(8,128)(2,1)} %q.1, bf16[1,128,512]{2,1,0:T(8,128)(2,1)} %k.1, bf16[1,128,512]{2,1,0:T(8,128)(2,1)} %v.1, bf16[1,128,1024]{2,1,0:T(8,128)(2,1)} %og.1, ...), custom_call_target="tpu_custom_call" | custom-call | bytes 1279488 | tf_op jit(solution)/shard_map/pack/pallas_call | solution.py:66
  2.9 0.0 collective-permute-done.q_pair
  2.9 0.0 collective-permute-done.1.k_pair
  2.9 0.3 collective-permute-done.2.v_pair
  3.2 0.3 state.1
  3.5 2.9 %collective-permute-start.8 = (bf16[128,384]{1,0:T(8,128)(2,1)S(1)}, bf16[128,384]{1,0:T(8,128)(2,1)S(1)}, u32[]{:S(2)}, u32[]{:S(2)}) collective-permute-start(bf16[128,384]{1,0:T(8,128)(2,1)S(1)} %get-tuple-element.51), channel_id=1, source_target_pairs={{0,2},{1,7},{2,0},{3,5},{4,6},{5,3},{6,4},{7,1},{8,10},{9,15},{10,... | collective-permute-start | bytes 294920 | tf_op jit(solution)/shard_map/ppermute | solution.py:432
  6.4 2.5 %collective-permute-start.9 = (bf16[128,384]{1,0:T(8,128)(2,1)S(1)}, bf16[128,384]{1,0:T(8,128)(2,1)S(1)}, u32[]{:S(2)}, u32[]{:S(2)}) collective-permute-start(bf16[128,384]{1,0:T(8,128)(2,1)S(1)} %get-tuple-element.52), channel_id=1, source_target_pairs={{0,6},{1,3},{2,4},{3,1},{4,2},{5,7},{6,0},{7,5},{8,14},{9,11},{10,... | collective-permute-start | bytes 294920 | tf_op jit(solution)/shard_map/ppermute | solution.py:432
  8.9 0.1 collective-permute-start.3
  9.0 0.0 collective-permute-done.8.a.refs_0_
  9.0 5.5 %collective-permute-done.9.b.refs_1_ = bf16[128,384]{1,0:T(8,128)(2,1)S(1)} collective-permute-done((bf16[128,384]{1,0:T(8,128)(2,1)S(1)}, bf16[128,384]{1,0:T(8,128)(2,1)S(1)}, u32[]{:S(2)}, u32[]{:S(2)}) %collective-permute-start.9) | collective-permute-done | bytes 98336 | tf_op jit(solution)/shard_map/ppermute | solution.py:432
  14.4 0.0 collective-permute-done.7.og_recv
  14.5 1.2 %soft_forward.1 = (bf16[256,128]{1,0:T(8,128)(2,1)S(1)}, bf16[512,128]{1,0:T(8,128)(2,1)S(1)}, bf16[512,128]{1,0:T(8,128)(2,1)S(1)}, bf16[256,1024]{1,0:T(8,128)...) custom-call(bf16[128,768]{1,0:T(8,128)(2,1)S(1)} %get-tuple-element., ...), custom_call_target="tpu_custom_call" | custom-call | flops 67108864 | bytes 2883584 | tf_op jit(solution)/shard_map/soft_forward/pallas_call | solution.py:66
  15.7 0.2 collective-permute-done.3.c.refs_2_
  15.9 0.7 %lin_forward.1 = (f32[256,128]{1,0:T(8,128)S(1)}, f32[128,128]{1,0:T(8,128)S(1)}, f32[128,512]{1,0:T(8,128)S(1)}, bf16[256,512]{1,0:T(8,128)(2,1)S(1)}) custom-call(f32[128,128]{1,0:T(8,128)S(1)} %get-tuple-element.54.state, bf16[128,768]{1,0:T(8,128)(2,1)S(1)} %get-tuple-element.47.mine.refs_6_, bf16[128,768]{1,0:T(8,128)(2,1)S(1)} %get-tuple-element.49.pair.refs_7_, ...), custom_call_target="tpu_custom_call" | custom-call | flops 67108864 | bytes 2097664 | tf_op jit(solution)/shard_map/lin_forward/pallas_call | solution.py:66
  16.6 1.6 %collective-permute-start.10 = (bf16[256,512]{1,0:T(8,128)(2,1)S(1)}, bf16[256,512]{1,0:T(8,128)(2,1)S(1)}, u32[]{:S(2)}, u32[]{:S(2)}) collective-permute-start(bf16[256,512]{1,0:T(8,128)(2,1)S(1)} %get-tuple-element.59), channel_id=1, source_target_pairs={{0,8},{1,17},{8,0},{9,25},{16,24},{17,1},{24,16},{25,9},{2,10},{3,... | collective-permute-start | bytes 786440 | tf_op jit(solution)/shard_map/ppermute | solution.py:449
  18.1 0.7 %collective-permute-start.5 = (bf16[2,64,256]{2,1,0:T(8,128)(2,1)S(1)}, bf16[2,64,256]{2,1,0:T(8,128)(2,1)S(1)}, u32[]{:S(2)}, u32[]{:S(2)}) collective-permute-start(bf16[2,64,256]{2,1,0:T(8,128)(2,1)S(1)} %w_two.1.own), channel_id=1, source_target_pairs={{1,2},{2,1},{5,6},{6,5},{9,10},{10,9},{13,14},{14,13},{17,18},{18,... | collective-permute-start | bytes 196616 | tf_op jit(solution)/shard_map/ppermute | solution.py:443
  18.8 2.2 %collective-permute-start.4 = (bf16[2,64,256]{2,1,0:T(8,128)(2,1)S(1)}, bf16[2,64,256]{2,1,0:T(8,128)(2,1)S(1)}, u32[]{:S(2)}, u32[]{:S(2)}) collective-permute-start(bf16[2,64,256]{2,1,0:T(8,128)(2,1)S(1)} %w_two.1.own), channel_id=1, source_target_pairs={{0,2},{1,0},{3,1},{2,3},{4,6},{5,4},{7,5},{6,7},{8,10},{9,8},{11,9... | collective-permute-start | bytes 196616 | tf_op jit(solution)/shard_map/ppermute | solution.py:443
  21.0 0.0 collective-permute-done.5.diagonal
  21.0 1.9 %collective-permute-done.4.cycle = bf16[2,64,256]{2,1,0:T(8,128)(2,1)S(1)} collective-permute-done((bf16[2,64,256]{2,1,0:T(8,128)(2,1)S(1)}, bf16[2,64,256]{2,1,0:T(8,128)(2,1)S(1)}, u32[]{:S(2)}, u32[]{:S(2)}) %collective-permute-start.4) | collective-permute-done | bytes 65568 | tf_op jit(solution)/shard_map/ppermute | solution.py:443
  22.9 0.8 %collective-permute-start.6 = (bf16[256,256]{1,0:T(8,128)(2,1)S(1)}, bf16[256,256]{1,0:T(8,128)(2,1)S(1)}, u32[]{:S(2)}, u32[]{:S(2)}) collective-permute-start(bf16[256,256]{1,0:T(8,128)(2,1)S(1)} %w_rows.1.first), channel_id=1, source_target_pairs={{0,8},{1,17},{8,0},{9,25},{16,24},{17,1},{24,16},{25,9},{2,10},{3,... | collective-permute-start | bytes 393224 | tf_op jit(solution)/shard_map/ppermute | solution.py:449
  23.7 0.0 collective-permute-done.10.got
  23.7 0.1 fold.1
  23.8 1.4 %collective-permute-start.12 = (bf16[256,256]{1,0:T(8,128)(2,1)S(1)}, bf16[256,256]{1,0:T(8,128)(2,1)S(1)}, u32[]{:S(2)}, u32[]{:S(2)}) collective-permute-start(bf16[256,256]{1,0:T(8,128)(2,1)S(1)} %get-tuple-element.60.refs_0_), channel_id=1, source_target_pairs={{0,16},{1,9},{8,24},{9,1},{16,0},{17,25},{24,8},{25,17},{2,18},{3,... | collective-permute-start | bytes 393224 | tf_op jit(solution)/shard_map/ppermute | solution.py:449
  25.2 2.8 %collective-permute-done.6.second = bf16[256,256]{1,0:T(8,128)(2,1)S(1)} collective-permute-done((bf16[256,256]{1,0:T(8,128)(2,1)S(1)}, bf16[256,256]{1,0:T(8,128)(2,1)S(1)}, u32[]{:S(2)}, u32[]{:S(2)}) %collective-permute-start.6) | collective-permute-done | bytes 131104 | tf_op jit(solution)/shard_map/ppermute | solution.py:449
  28.0 2.3 %collective-permute-start.11 = (bf16[256,512]{1,0:T(8,128)(2,1)S(1)}, bf16[256,512]{1,0:T(8,128)(2,1)S(1)}, u32[]{:S(2)}, u32[]{:S(2)}) collective-permute-start(bf16[256,512]{1,0:T(8,128)(2,1)S(1)} %w_half.1.refs_0_), channel_id=1, source_target_pairs={{0,16},{1,9},{8,24},{9,1},{16,0},{17,25},{24,8},{25,17},{2,18},{3,... | collective-permute-start | bytes 786440 | tf_op jit(solution)/shard_map/ppermute | solution.py:449
  30.3 0.0 collective-permute-done.12.got
  30.3 0.1 rows.1
  30.4 0.1 collective-permute-start.13
  30.5 1.3 %collective-permute-done.13.got = f32[128,256]{1,0:T(8,128)S(1)} collective-permute-done((f32[128,256]{1,0:T(8,128)S(1)}, f32[128,256]{1,0:T(8,128)S(1)}, u32[]{:S(2)}, u32[]{:S(2)}) %collective-permute-start.13) | collective-permute-done | bytes 131104 | tf_op jit(solution)/shard_map/ppermute | solution.py:421
  31.8 1.7 %collective-permute-start.14 = (bf16[128,256]{1,0:T(8,128)(2,1)S(1)}, bf16[128,256]{1,0:T(8,128)(2,1)S(1)}, u32[]{:S(2)}, u32[]{:S(2)}) collective-permute-start(bf16[128,256]{1,0:T(8,128)(2,1)S(1)} %get-tuple-element.78), channel_id=1, source_target_pairs={{0,2},{1,7},{2,0},{3,5},{4,6},{5,3},{6,4},{7,1},{8,10},{9,15},{10,... | collective-permute-start | bytes 196616 | tf_op jit(solution)/shard_map/ppermute | solution.py:432
  33.6 1.1 %collective-permute-done.11.refs_1_ = bf16[256,512]{1,0:T(8,128)(2,1)S(1)} collective-permute-done((bf16[256,512]{1,0:T(8,128)(2,1)S(1)}, bf16[256,512]{1,0:T(8,128)(2,1)S(1)}, u32[]{:S(2)}, u32[]{:S(2)}) %collective-permute-start.11) | collective-permute-done | bytes 262176 | tf_op jit(solution)/shard_map/ppermute | solution.py:449
  34.7 1.5 %backward.1 = (bf16[128,128]{1,0:T(8,128)(2,1)S(1)}, bf16[128,128]{1,0:T(8,128)(2,1)S(1)}, f32[128,128]{1,0:T(8,128)S(1)}, f32[256,128]{1,0:T(8,128)S(1)}, f32[5...) custom-call(bf16[256,512]{1,0:T(8,128)(2,1)S(1)} %w_half.1.refs_0_, bf16[256,512]{1,0:T(8,128)(2,1)S(1)} %collective-permute-done.11.refs_1_, ...), custom_call_target="tpu_custom_call" | custom-call | flops 335544320 | bytes 3408384 | tf_op jit(solution)/shard_map/backward/pallas_call | solution.py:66
  36.2 0.0 collective-permute-done.14.got
  36.3 2.9 %collective-permute-start.17 = (bf16[128,256]{1,0:T(8,128)(2,1)S(1)}, bf16[128,256]{1,0:T(8,128)(2,1)S(1)}, u32[]{:S(2)}, u32[]{:S(2)}) collective-permute-start(bf16[128,256]{1,0:T(8,128)(2,1)S(1)} %get-tuple-element.81), channel_id=1, source_target_pairs={{0,4},{1,5},{2,6},{3,7},{4,0},{5,1},{6,2},{7,3},{8,12},{9,13},{10,... | collective-permute-start | bytes 196616 | tf_op jit(solution)/shard_map/ppermute | solution.py:432
  39.2 3.0 %collective-permute-start.15 = (bf16[128,384]{1,0:T(8,128)(2,1)S(1)}, bf16[128,384]{1,0:T(8,128)(2,1)S(1)}, u32[]{:S(2)}, u32[]{:S(2)}) collective-permute-start(bf16[128,384]{1,0:T(8,128)(2,1)S(1)} %get-tuple-element.79), channel_id=1, source_target_pairs={{0,2},{1,7},{2,0},{3,5},{4,6},{5,3},{6,4},{7,1},{8,10},{9,15},{10,... | collective-permute-start | bytes 294920 | tf_op jit(solution)/shard_map/ppermute | solution.py:432
  42.2 0.0 collective-permute-start.16
  42.2 0.5 collective-permute-done.17.got.refs_0_
  42.8 0.7 %collective-permute-start.18 = (bf16[64,256]{1,0:T(8,128)(2,1)S(1)}, bf16[64,256]{1,0:T(8,128)(2,1)S(1)}, u32[]{:S(2)}, u32[]{:S(2)}) collective-permute-start(bf16[64,256]{1,0:T(8,128)(2,1)S(1)} %weight_sum.1.first), channel_id=1, source_target_pairs={{0,8},{1,17},{8,0},{9,25},{16,24},{17,1},{24,16},{25,9},{2,10},{3,... | collective-permute-start | bytes 98312 | tf_op jit(solution)/shard_map/ppermute | solution.py:449
  43.4 3.3 %collective-permute-done.18.second = bf16[64,256]{1,0:T(8,128)(2,1)S(1)} collective-permute-done((bf16[64,256]{1,0:T(8,128)(2,1)S(1)}, bf16[64,256]{1,0:T(8,128)(2,1)S(1)}, u32[]{:S(2)}, u32[]{:S(2)}) %collective-permute-start.18) | collective-permute-done | bytes 32800 | tf_op jit(solution)/shard_map/ppermute | solution.py:449
  46.7 0.0 collective-permute-done.15.a
  46.7 1.9 %collective-permute-done.16.b = bf16[128,384]{1,0:T(8,128)(2,1)S(1)} collective-permute-done((bf16[128,384]{1,0:T(8,128)(2,1)S(1)}, bf16[128,384]{1,0:T(8,128)(2,1)S(1)}, u32[]{:S(2)}, u32[]{:S(2)}) %collective-permute-start.16) | collective-permute-done | bytes 98336 | tf_op jit(solution)/shard_map/ppermute | solution.py:432
  48.7 0.4 final.1
  49.0 0.1 collective-permute-start.19
  49.1 1.3 %collective-permute-start.20 = (bf16[64,512]{1,0:T(8,128)(2,1)S(1)}, bf16[64,512]{1,0:T(8,128)(2,1)S(1)}, u32[]{:S(2)}, u32[]{:S(2)}) collective-permute-start(bf16[64,512]{1,0:T(8,128)(2,1)S(1)} %both.1.refs_1_), channel_id=1, source_target_pairs={{0,16},{1,9},{8,24},{9,1},{16,0},{17,25},{24,8},{25,17},{2,18},{3,... | collective-permute-start | bytes 196616 | tf_op jit(solution)/shard_map/ppermute | solution.py:449
  50.4 0.1 collective-permute-done.19.pair
  50.5 0.8 %outputs.1 = (bf16[1,128,512]{2,1,0:T(8,128)(2,1)}, bf16[1,128,512]{2,1,0:T(8,128)(2,1)}, bf16[1,128,512]{2,1,0:T(8,128)(2,1)}) custom-call(bf16[128,768]{1,0:T(8,128)(2,1)S(1)} %get-tuple-element.83.own, bf16[128,768]{1,0:T(8,128)(2,1)S(1)} %collective-permute-done.19.pair), custom_call_target="tpu_custom_call" | custom-call | bytes 786432 | tf_op jit(solution)/shard_map/outputs/pallas_call | solution.py:66
  51.3 2.1 %collective-permute-done.20.got = bf16[64,512]{1,0:T(8,128)(2,1)S(1)} collective-permute-done((bf16[64,512]{1,0:T(8,128)(2,1)S(1)}, bf16[64,512]{1,0:T(8,128)(2,1)S(1)}, u32[]{:S(2)}, u32[]{:S(2)}) %collective-permute-start.20) | collective-permute-done | bytes 65568 | tf_op jit(solution)/shard_map/ppermute | solution.py:449
  53.4 0.7 %weight_join.1 = f32[64,1024]{1,0:T(8,128)} custom-call(bf16[64,512]{1,0:T(8,128)(2,1)S(1)} %both.1.refs_1_, bf16[64,512]{1,0:T(8,128)(2,1)S(1)} %collective-permute-done.20.got, bf16[1,128,512]{2,1,0:T(8,128)(2,1)} %get-tuple-element.42._), custom_call_target="tpu_custom_call" | custom-call | bytes 524288 | tf_op jit(solution)/shard_map/weight_join/pallas_call | solution.py:66
  (7 shorter events, 0.2 us)
Async XLA Ops:
  0.6 13.8 %collective-permute-start.7 = (bf16[128,1024]{1,0:T(8,128)(2,1)}, bf16[128,1024]{1,0:T(8,128)(2,1)S(1)}, u32[]{:S(2)}, u32[]{:S(2)}) collective-permute-start(bf16[128,1024]{1,0:T(8,128)(2,1)} %bitcast.1), channel_id=1, source_target_pairs={{0,1},{1,0},{2,3},{3,2},{4,5},{5,4},{6,7},{7,6},{8,9},{9,8},{10,11... | collective-permute-start | bytes 786440 | tf_op jit(solution)/shard_map/ppermute | solution.py:421
  1.2 1.8 %collective-permute-start = (bf16[1,128,512]{2,1,0:T(8,128)(2,1)}, bf16[1,128,512]{2,1,0:T(8,128)(2,1)S(1)}, u32[]{:S(2)}, u32[]{:S(2)}) collective-permute-start(bf16[1,128,512]{2,1,0:T(8,128)(2,1)} %q.1), channel_id=1, source_target_pairs={{0,1},{1,0},{2,3},{3,2},{4,5},{5,4},{6,7},{7,6},{8,9},{9,8},{10,11... | collective-permute-start | bytes 393224 | tf_op jit(solution)/shard_map/ppermute | solution.py:421
  1.2 1.7 %collective-permute-start.1 = (bf16[1,128,512]{2,1,0:T(8,128)(2,1)}, bf16[1,128,512]{2,1,0:T(8,128)(2,1)S(1)}, u32[]{:S(2)}, u32[]{:S(2)}) collective-permute-start(bf16[1,128,512]{2,1,0:T(8,128)(2,1)} %k.1), channel_id=1, source_target_pairs={{0,1},{1,0},{2,3},{3,2},{4,5},{5,4},{6,7},{7,6},{8,9},{9,8},{10,11... | collective-permute-start | bytes 393224 | tf_op jit(solution)/shard_map/ppermute | solution.py:421
  1.7 1.6 %collective-permute-start.2 = (bf16[1,128,512]{2,1,0:T(8,128)(2,1)}, bf16[1,128,512]{2,1,0:T(8,128)(2,1)S(1)}, u32[]{:S(2)}, u32[]{:S(2)}) collective-permute-start(bf16[1,128,512]{2,1,0:T(8,128)(2,1)} %v.1), channel_id=1, source_target_pairs={{0,1},{1,0},{2,3},{3,2},{4,5},{5,4},{6,7},{7,6},{8,9},{9,8},{10,11... | collective-permute-start | bytes 393224 | tf_op jit(solution)/shard_map/ppermute | solution.py:421
  3.5 5.5 %collective-permute-start.8 = (bf16[128,384]{1,0:T(8,128)(2,1)S(1)}, bf16[128,384]{1,0:T(8,128)(2,1)S(1)}, u32[]{:S(2)}, u32[]{:S(2)}) collective-permute-start(bf16[128,384]{1,0:T(8,128)(2,1)S(1)} %get-tuple-element.51), channel_id=1, source_target_pairs={{0,2},{1,7},{2,0},{3,5},{4,6},{5,3},{6,4},{7,1},{8,10},{9,15},{10,... | collective-permute-start | bytes 294920 | tf_op jit(solution)/shard_map/ppermute | solution.py:432
  6.4 8.1 %collective-permute-start.9 = (bf16[128,384]{1,0:T(8,128)(2,1)S(1)}, bf16[128,384]{1,0:T(8,128)(2,1)S(1)}, u32[]{:S(2)}, u32[]{:S(2)}) collective-permute-start(bf16[128,384]{1,0:T(8,128)(2,1)S(1)} %get-tuple-element.52), channel_id=1, source_target_pairs={{0,6},{1,3},{2,4},{3,1},{4,2},{5,7},{6,0},{7,5},{8,14},{9,11},{10,... | collective-permute-start | bytes 294920 | tf_op jit(solution)/shard_map/ppermute | solution.py:432
  8.9 7.0 %collective-permute-start.3 = (bf16[128,256]{1,0:T(8,128)(2,1)S(1)}, bf16[128,256]{1,0:T(8,128)(2,1)S(1)}, u32[]{:S(2)}, u32[]{:S(2)}) collective-permute-start(bf16[128,256]{1,0:T(8,128)(2,1)S(1)} %get-tuple-element.48), channel_id=1, source_target_pairs={{0,4},{1,5},{2,6},{3,7},{4,0},{5,1},{6,2},{7,3},{8,12},{9,13},{10,... | collective-permute-start | bytes 196616 | tf_op jit(solution)/shard_map/ppermute | solution.py:432
  16.6 7.1 %collective-permute-start.10 = (bf16[256,512]{1,0:T(8,128)(2,1)S(1)}, bf16[256,512]{1,0:T(8,128)(2,1)S(1)}, u32[]{:S(2)}, u32[]{:S(2)}) collective-permute-start(bf16[256,512]{1,0:T(8,128)(2,1)S(1)} %get-tuple-element.59), channel_id=1, source_target_pairs={{0,8},{1,17},{8,0},{9,25},{16,24},{17,1},{24,16},{25,9},{2,10},{3,... | collective-permute-start | bytes 786440 | tf_op jit(solution)/shard_map/ppermute | solution.py:449
  18.1 2.9 %collective-permute-start.5 = (bf16[2,64,256]{2,1,0:T(8,128)(2,1)S(1)}, bf16[2,64,256]{2,1,0:T(8,128)(2,1)S(1)}, u32[]{:S(2)}, u32[]{:S(2)}) collective-permute-start(bf16[2,64,256]{2,1,0:T(8,128)(2,1)S(1)} %w_two.1.own), channel_id=1, source_target_pairs={{1,2},{2,1},{5,6},{6,5},{9,10},{10,9},{13,14},{14,13},{17,18},{18,... | collective-permute-start | bytes 196616 | tf_op jit(solution)/shard_map/ppermute | solution.py:443
  18.8 4.1 %collective-permute-start.4 = (bf16[2,64,256]{2,1,0:T(8,128)(2,1)S(1)}, bf16[2,64,256]{2,1,0:T(8,128)(2,1)S(1)}, u32[]{:S(2)}, u32[]{:S(2)}) collective-permute-start(bf16[2,64,256]{2,1,0:T(8,128)(2,1)S(1)} %w_two.1.own), channel_id=1, source_target_pairs={{0,2},{1,0},{3,1},{2,3},{4,6},{5,4},{7,5},{6,7},{8,10},{9,8},{11,9... | collective-permute-start | bytes 196616 | tf_op jit(solution)/shard_map/ppermute | solution.py:443
  22.9 5.0 %collective-permute-start.6 = (bf16[256,256]{1,0:T(8,128)(2,1)S(1)}, bf16[256,256]{1,0:T(8,128)(2,1)S(1)}, u32[]{:S(2)}, u32[]{:S(2)}) collective-permute-start(bf16[256,256]{1,0:T(8,128)(2,1)S(1)} %w_rows.1.first), channel_id=1, source_target_pairs={{0,8},{1,17},{8,0},{9,25},{16,24},{17,1},{24,16},{25,9},{2,10},{3,... | collective-permute-start | bytes 393224 | tf_op jit(solution)/shard_map/ppermute | solution.py:449
  23.8 6.6 %collective-permute-start.12 = (bf16[256,256]{1,0:T(8,128)(2,1)S(1)}, bf16[256,256]{1,0:T(8,128)(2,1)S(1)}, u32[]{:S(2)}, u32[]{:S(2)}) collective-permute-start(bf16[256,256]{1,0:T(8,128)(2,1)S(1)} %get-tuple-element.60.refs_0_), channel_id=1, source_target_pairs={{0,16},{1,9},{8,24},{9,1},{16,0},{17,25},{24,8},{25,17},{2,18},{3,... | collective-permute-start | bytes 393224 | tf_op jit(solution)/shard_map/ppermute | solution.py:449
  28.0 6.7 %collective-permute-start.11 = (bf16[256,512]{1,0:T(8,128)(2,1)S(1)}, bf16[256,512]{1,0:T(8,128)(2,1)S(1)}, u32[]{:S(2)}, u32[]{:S(2)}) collective-permute-start(bf16[256,512]{1,0:T(8,128)(2,1)S(1)} %w_half.1.refs_0_), channel_id=1, source_target_pairs={{0,16},{1,9},{8,24},{9,1},{16,0},{17,25},{24,8},{25,17},{2,18},{3,... | collective-permute-start | bytes 786440 | tf_op jit(solution)/shard_map/ppermute | solution.py:449
  30.4 1.4 %collective-permute-start.13 = (f32[128,256]{1,0:T(8,128)S(1)}, f32[128,256]{1,0:T(8,128)S(1)}, u32[]{:S(2)}, u32[]{:S(2)}) collective-permute-start(f32[128,256]{1,0:T(8,128)S(1)} %get-tuple-element.63), channel_id=1, source_target_pairs={{0,1},{1,0},{2,3},{3,2},{4,5},{5,4},{6,7},{7,6},{8,9},{9,8},{10,11... | collective-permute-start | bytes 393224 | tf_op jit(solution)/shard_map/ppermute | solution.py:421
  31.8 4.4 %collective-permute-start.14 = (bf16[128,256]{1,0:T(8,128)(2,1)S(1)}, bf16[128,256]{1,0:T(8,128)(2,1)S(1)}, u32[]{:S(2)}, u32[]{:S(2)}) collective-permute-start(bf16[128,256]{1,0:T(8,128)(2,1)S(1)} %get-tuple-element.78), channel_id=1, source_target_pairs={{0,2},{1,7},{2,0},{3,5},{4,6},{5,3},{6,4},{7,1},{8,10},{9,15},{10,... | collective-permute-start | bytes 196616 | tf_op jit(solution)/shard_map/ppermute | solution.py:432
  36.3 6.4 %collective-permute-start.17 = (bf16[128,256]{1,0:T(8,128)(2,1)S(1)}, bf16[128,256]{1,0:T(8,128)(2,1)S(1)}, u32[]{:S(2)}, u32[]{:S(2)}) collective-permute-start(bf16[128,256]{1,0:T(8,128)(2,1)S(1)} %get-tuple-element.81), channel_id=1, source_target_pairs={{0,4},{1,5},{2,6},{3,7},{4,0},{5,1},{6,2},{7,3},{8,12},{9,13},{10,... | collective-permute-start | bytes 196616 | tf_op jit(solution)/shard_map/ppermute | solution.py:432
  39.2 7.5 %collective-permute-start.15 = (bf16[128,384]{1,0:T(8,128)(2,1)S(1)}, bf16[128,384]{1,0:T(8,128)(2,1)S(1)}, u32[]{:S(2)}, u32[]{:S(2)}) collective-permute-start(bf16[128,384]{1,0:T(8,128)(2,1)S(1)} %get-tuple-element.79), channel_id=1, source_target_pairs={{0,2},{1,7},{2,0},{3,5},{4,6},{5,3},{6,4},{7,1},{8,10},{9,15},{10,... | collective-permute-start | bytes 294920 | tf_op jit(solution)/shard_map/ppermute | solution.py:432
  42.2 6.4 %collective-permute-start.16 = (bf16[128,384]{1,0:T(8,128)(2,1)S(1)}, bf16[128,384]{1,0:T(8,128)(2,1)S(1)}, u32[]{:S(2)}, u32[]{:S(2)}) collective-permute-start(bf16[128,384]{1,0:T(8,128)(2,1)S(1)} %get-tuple-element.80), channel_id=1, source_target_pairs={{0,6},{1,3},{2,4},{3,1},{4,2},{5,7},{6,0},{7,5},{8,14},{9,11},{10,... | collective-permute-start | bytes 294920 | tf_op jit(solution)/shard_map/ppermute | solution.py:432
  42.8 4.0 %collective-permute-start.18 = (bf16[64,256]{1,0:T(8,128)(2,1)S(1)}, bf16[64,256]{1,0:T(8,128)(2,1)S(1)}, u32[]{:S(2)}, u32[]{:S(2)}) collective-permute-start(bf16[64,256]{1,0:T(8,128)(2,1)S(1)} %weight_sum.1.first), channel_id=1, source_target_pairs={{0,8},{1,17},{8,0},{9,25},{16,24},{17,1},{24,16},{25,9},{2,10},{3,... | collective-permute-start | bytes 98312 | tf_op jit(solution)/shard_map/ppermute | solution.py:449
  49.0 1.5 %collective-permute-start.19 = (bf16[128,768]{1,0:T(8,128)(2,1)S(1)}, bf16[128,768]{1,0:T(8,128)(2,1)S(1)}, u32[]{:S(2)}, u32[]{:S(2)}) collective-permute-start(bf16[128,768]{1,0:T(8,128)(2,1)S(1)} %get-tuple-element.84), channel_id=1, source_target_pairs={{0,1},{1,0},{2,3},{3,2},{4,5},{5,4},{6,7},{7,6},{8,9},{9,8},{10,11... | collective-permute-start | bytes 589832 | tf_op jit(solution)/shard_map/ppermute | solution.py:421
  49.1 4.3 %collective-permute-start.20 = (bf16[64,512]{1,0:T(8,128)(2,1)S(1)}, bf16[64,512]{1,0:T(8,128)(2,1)S(1)}, u32[]{:S(2)}, u32[]{:S(2)}) collective-permute-start(bf16[64,512]{1,0:T(8,128)(2,1)S(1)} %both.1.refs_1_), channel_id=1, source_target_pairs={{0,16},{1,9},{8,24},{9,1},{16,0},{17,25},{24,8},{25,17},{2,18},{3,... | collective-permute-start | bytes 196616 | tf_op jit(solution)/shard_map/ppermute | solution.py:449

commit v16 on v13

--- a/solution.py
+++ b/solution.py
@@ -320,10 +320,13 @@
     out[:, first + DH : first + 2 * DH] = dv_soft[at(start), :].astype(BF)
 
 
-def halo_kernel(dk_soft, dv_soft, to_a, to_b):
-    way = links(False)
-    halo_part(to_a, 0, dk_soft, dv_soft, way["halo_a"])
-    halo_part(to_b, 0, dk_soft, dv_soft, way["halo_b"])
+def halo_kernel(direct, dk_soft, dv_soft, *refs):
+    way = links(direct)
+    to_a, to_b = refs[-2:]
+    for out, side in ((to_a, way["halo_a"]), (to_b, way["halo_b"])):
+        halo_part(out, 0, dk_soft, dv_soft, side)
+        if direct:
+            out[:, 2 * DH :] = refs[0][...].astype(BF)
 
 
 def chunk_kernel(own, got, send, keep, heads):
@@ -340,20 +343,13 @@
         keep[index * half : (index + 1) * half, :] = heads[z ^ step]
 
 
-def second_kernel(keep, got, dstate, dk_soft, dv_soft, chunk, to_a, to_b, to_c):
-    way = links(True)
+def second_kernel(keep, got, dstate, chunk, to_c):
     half = chunk.shape[0]
     chunk[...] = keep[:half, :] + got[:half, :].astype(F32)
     for side in range(2):
         cols, rows = slice(side * DH, (side + 1) * DH), slice(side * half, (side + 1) * half)
-        piece = keep[half:, cols] + got[half:, cols].astype(F32)
-        to_c[rows, DH:] = piece.astype(BF)
-    halo_part(to_a, 0, dk_soft, dv_soft, way["halo_a"])
-    halo_part(to_b, 0, dk_soft, dv_soft, way["halo_b"])
-    low = dstate[...].astype(BF)
-    to_a[:, 2 * DH :] = low
-    to_b[:, 2 * DH :] = low
-    to_c[:, :DH] = low
+        to_c[rows, DH:] = (keep[half:, cols] + got[half:, cols].astype(F32)).astype(BF)
+    to_c[:, :DH] = dstate[...].astype(BF)
 
 
 def weight_sum_kernel(scale, chunk, got, summed):
@@ -533,15 +529,11 @@
     )
     wide = 3 * DH if direct else 2 * DH
     if direct:
-        chunk, to_a, to_b, to_c = call(
-            second_kernel, "second",
-            [
-                like((half, width), F32), like((rows, 3 * DH), BF), like((rows, 3 * DH), BF),
-                like((rows, 2 * DH), BF),
-            ],
-            [piece_keep, piece_got, dstate, dk_soft, dv_soft],
+        chunk, to_c = call(
+            second_kernel, "second", [like((half, width), F32), like((rows, 2 * DH), BF)],
+            [piece_keep, piece_got, dstate],
         )
-        a, b, c = over_z(to_a, 0), over_z(to_b, 1), [over_z(to_c, 2)]
+        c = [over_z(to_c, 2)]
         summed = call(
             functools.partial(weight_sum_kernel, scale), "weight_sum", [like((half, width), BF)],
             [chunk] + c,
@@ -549,9 +541,11 @@
         got = over_dp(summed, 0)
         both = call(join_kernel, "both", [like((half, 2 * width), BF)], [summed, got])[0]
         gathered = over_dp(both, 1)
-    else:
-        to_a, to_b = call(halo_kernel, "halo", [like((rows, 2 * DH), BF)] * 2, [dk_soft, dv_soft])
-        a, b = over_z(to_a, 0, True), over_z(to_b, 1, True)
+    to_a, to_b = call(
+        functools.partial(halo_kernel, direct), "halo", [like((rows, wide), BF)] * 2,
+        [dk_soft, dv_soft] + ([dstate, summed] if direct else []),
+    )
+    a, b = over_z(to_a, 0, True), over_z(to_b, 1, True)
     if not direct:
         dstate = lax.psum(dstate, "z")
         groups = jnp.stack([keep_soft, keep_lin])
@@ -564,7 +558,7 @@
         functools.partial(final_kernel, direct), "final",
         [like((rows, 6 * DH), BF), like((rows, 6 * DH), BF)],
         [dstate, mine, pair, dq_soft, dk_soft, dv_soft, dq_lin, dq_lin_pair, a, b]
-        + (c + [both] if direct else []),
+        + (c + [gathered] if direct else []),
         scratch=[pltpu.VMEM((2 * rows, DH), F32)] * 2,
         flops=wg_flops // 4,
     )

time: 53.1 us -> 56 us (1.055)
  starting transfers between devices: 21.4 us -> 23.1 us
  waiting for transfers between devices: 23.7 us -> 24.9 us
    ppermute x6, waiting for transfers between devices: 9.88 us -> 8.07 us  [over_dp(): return lax.ppermute(value, ('dp', 'core'), pairs)]
    ppermute x7, waiting for transfers between devices: 11.3 us -> 12.9 us  [over_z(): return lax.ppermute(value, axes, pairs)]
    ppermute x7, waiting for transfers between devices: 2.59 us -> 4.01 us  [over_core(): return lax.ppermute(value, 'core', pair_perm)]
    ppermute x7, starting transfers between devices: 10.9 us -> 12.2 us  [over_z(): return lax.ppermute(value, axes, pairs)]
    pallas_call x17 -> x18, Pallas kernels: 7.06 us -> 7.05 us  [call(): pl.pallas_call(kernel, name=name, out_shape=list(outs), in_specs=spaces o...]
  transfers between devices with their start and end apart: 20 -> 20, of which waited for: 12 -> 13; matrix products, arithmetic and copies ran while one was open for 0% -> 0% of each run, Pallas kernels for 10% -> 8%
where the time goes in v16:
time: 56 us; the launch traced here: 55.9 us
  waiting for transfers between devices  24.9 us (44%)
  starting transfers between devices  23.1 us (41%)
  Pallas kernels  7.05 us (13%)
  between operations  0.79 us (1%)
    ppermute x7, waiting for transfers between devices, over_z(): return lax.ppermute(value, axes, pairs)  12.9 us
    ppermute x7, starting transfers between devices, over_z(): return lax.ppermute(value, axes, pairs)  12.2 us
    ppermute x6, starting transfers between devices, over_dp(): return lax.ppermute(value, ('dp', 'core'), pairs)  9.58 us
    ppermute x6, waiting for transfers between devices, over_dp(): return lax.ppermute(value, ('dp', 'core'), pairs)  8.07 us
    pallas_call x18, Pallas kernels, call(): pl.pallas_call(kernel, name=name, out_shape=list(outs), in_specs=spaces o...  7.05 us
    ppermute x7, waiting for transfers between devices, over_core(): return lax.ppermute(value, 'core', pair_perm)  4.01 us
    ppermute x7, starting transfers between devices, over_core(): return lax.ppermute(value, 'core', pair_perm)  1.32 us
  transfers between devices with their start and end apart: 20, of which 13 were waited for; matrix products, arithmetic and copies ran while one was open for 0% of the time, Pallas kernels for 8%

profile of v16, /device:TPU:0, one launch (start us, length us, event | category | flops | bytes accessed | tf_op | source)
XLA Modules:
  0.0 55.9 jit_solution(10916042824734456882)
XLA Ops:
  0.6 0.5 collective-permute-start
  1.2 0.1 collective-permute-start.1
  1.2 0.4 collective-permute-start.2
  1.7 0.1 collective-permute-start.8
  1.7 1.2 %pack.1 = (bf16[128,768]{1,0:T(8,128)(2,1)S(1)}, bf16[128,1024]{1,0:T(8,128)(2,1)S(1)}, bf16[64,256]{1,0:T(8,128)(2,1)S(1)}, f32[1,128]{1,0:T(1,128)S(1)}) custom-call(bf16[1,128,512]{2,1,0:T(8,128)(2,1)} %q.1, bf16[1,128,512]{2,1,0:T(8,128)(2,1)} %k.1, bf16[1,128,512]{2,1,0:T(8,128)(2,1)} %v.1, bf16[1,128,1024]{2,1,0:T(8,128)(2,1)} %og.1, ...), custom_call_target="tpu_custom_call" | custom-call | bytes 1279488 | tf_op jit(solution)/shard_map/pack/pallas_call | solution.py:66
  2.9 0.0 collective-permute-done.q_pair
  2.9 0.0 collective-permute-done.1.k_pair
  2.9 0.0 collective-permute-done.2.v_pair
  3.0 0.3 state.1
  3.2 3.1 %collective-permute-start.3 = (bf16[128,512]{1,0:T(8,128)(2,1)S(1)}, bf16[128,512]{1,0:T(8,128)(2,1)S(1)}, u32[]{:S(2)}, u32[]{:S(2)}) collective-permute-start(bf16[128,512]{1,0:T(8,128)(2,1)S(1)} %get-tuple-element.50), channel_id=1, source_target_pairs={{0,2},{1,7},{2,0},{3,5},{4,6},{5,3},{6,4},{7,1},{8,10},{9,15},{10,... | collective-permute-start | bytes 393224 | tf_op jit(solution)/shard_map/ppermute | solution.py:428
  6.3 2.5 %collective-permute-start.4 = (bf16[128,512]{1,0:T(8,128)(2,1)S(1)}, bf16[128,512]{1,0:T(8,128)(2,1)S(1)}, u32[]{:S(2)}, u32[]{:S(2)}) collective-permute-start(bf16[128,512]{1,0:T(8,128)(2,1)S(1)} %get-tuple-element.51), channel_id=1, source_target_pairs={{0,6},{1,3},{2,4},{3,1},{4,2},{5,7},{6,0},{7,5},{8,14},{9,11},{10,... | collective-permute-start | bytes 393224 | tf_op jit(solution)/shard_map/ppermute | solution.py:428
  8.8 0.1 collective-permute-start.5
  8.9 0.4 collective-permute-done.3.a.refs_0_
  9.3 6.5 %collective-permute-done.4.b.refs_1_ = bf16[128,512]{1,0:T(8,128)(2,1)S(1)} collective-permute-done((bf16[128,512]{1,0:T(8,128)(2,1)S(1)}, bf16[128,512]{1,0:T(8,128)(2,1)S(1)}, u32[]{:S(2)}, u32[]{:S(2)}) %collective-permute-start.4) | collective-permute-done | bytes 131104 | tf_op jit(solution)/shard_map/ppermute | solution.py:428
  15.7 0.0 collective-permute-done.8.og_recv
  15.7 1.2 %soft_forward.1 = (bf16[256,128]{1,0:T(8,128)(2,1)S(1)}, bf16[512,128]{1,0:T(8,128)(2,1)S(1)}, bf16[512,128]{1,0:T(8,128)(2,1)S(1)}, bf16[256,1024]{1,0:T(8,128)...) custom-call(bf16[128,768]{1,0:T(8,128)(2,1)S(1)} %get-tuple-element., ...), custom_call_target="tpu_custom_call" | custom-call | flops 67108864 | bytes 2949120 | tf_op jit(solution)/shard_map/soft_forward/pallas_call | solution.py:66
  16.9 0.0 collective-permute-done.5.c.refs_2_
  17.0 0.7 %lin_forward.1 = (f32[256,128]{1,0:T(8,128)S(1)}, f32[128,128]{1,0:T(8,128)S(1)}, f32[128,512]{1,0:T(8,128)S(1)}, bf16[256,512]{1,0:T(8,128)(2,1)S(1)}) custom-call(f32[128,128]{1,0:T(8,128)S(1)} %get-tuple-element.58.state, bf16[128,768]{1,0:T(8,128)(2,1)S(1)} %get-tuple-element.49.mine.refs_6_, bf16[128,768]{1,0:T(8,128)(2,1)S(1)} %get-tuple-element.55.pair.refs_7_, ...), custom_call_target="tpu_custom_call" | custom-call | flops 67108864 | bytes 2163200 | tf_op jit(solution)/shard_map/lin_forward/pallas_call | solution.py:66
  17.6 1.6 %collective-permute-start.9 = (bf16[256,512]{1,0:T(8,128)(2,1)S(1)}, bf16[256,512]{1,0:T(8,128)(2,1)S(1)}, u32[]{:S(2)}, u32[]{:S(2)}) collective-permute-start(bf16[256,512]{1,0:T(8,128)(2,1)S(1)} %get-tuple-element.63), channel_id=1, source_target_pairs={{0,8},{1,17},{8,0},{9,25},{16,24},{17,1},{24,16},{25,9},{2,10},{3,... | collective-permute-start | bytes 786440 | tf_op jit(solution)/shard_map/ppermute | solution.py:434
  19.2 0.1 collective-permute-start.6
  19.3 1.2 %collective-permute-done.6.got = bf16[2,64,256]{2,1,0:T(8,128)(2,1)S(1)} collective-permute-done((bf16[2,64,256]{2,1,0:T(8,128)(2,1)S(1)}, bf16[2,64,256]{2,1,0:T(8,128)(2,1)S(1)}, u32[]{:S(2)}, u32[]{:S(2)}) %collective-permute-start.6) | collective-permute-done | bytes 65568 | tf_op jit(solution)/shard_map/ppermute | solution.py:417
  20.6 0.6 %collective-permute-start.7 = (bf16[256,256]{1,0:T(8,128)(2,1)S(1)}, bf16[256,256]{1,0:T(8,128)(2,1)S(1)}, u32[]{:S(2)}, u32[]{:S(2)}) collective-permute-start(bf16[256,256]{1,0:T(8,128)(2,1)S(1)} %w_rows.1.first), channel_id=1, source_target_pairs={{0,8},{1,17},{8,0},{9,25},{16,24},{17,1},{24,16},{25,9},{2,10},{3,... | collective-permute-start | bytes 393224 | tf_op jit(solution)/shard_map/ppermute | solution.py:434
  21.2 2.9 %collective-permute-done.9.got = bf16[256,512]{1,0:T(8,128)(2,1)S(1)} collective-permute-done((bf16[256,512]{1,0:T(8,128)(2,1)S(1)}, bf16[256,512]{1,0:T(8,128)(2,1)S(1)}, u32[]{:S(2)}, u32[]{:S(2)}) %collective-permute-start.9) | collective-permute-done | bytes 262176 | tf_op jit(solution)/shard_map/ppermute | solution.py:434
  24.1 0.1 fold.1
  24.1 1.9 %collective-permute-start.11 = (bf16[256,256]{1,0:T(8,128)(2,1)S(1)}, bf16[256,256]{1,0:T(8,128)(2,1)S(1)}, u32[]{:S(2)}, u32[]{:S(2)}) collective-permute-start(bf16[256,256]{1,0:T(8,128)(2,1)S(1)} %get-tuple-element.64.refs_0_), channel_id=1, source_target_pairs={{0,16},{1,9},{8,24},{9,1},{16,0},{17,25},{24,8},{25,17},{2,18},{3,... | collective-permute-start | bytes 393224 | tf_op jit(solution)/shard_map/ppermute | solution.py:434
  26.0 0.5 collective-permute-done.7.second
  26.6 1.9 %collective-permute-start.10 = (bf16[256,512]{1,0:T(8,128)(2,1)S(1)}, bf16[256,512]{1,0:T(8,128)(2,1)S(1)}, u32[]{:S(2)}, u32[]{:S(2)}) collective-permute-start(bf16[256,512]{1,0:T(8,128)(2,1)S(1)} %w_half.1.refs_0_), channel_id=1, source_target_pairs={{0,16},{1,9},{8,24},{9,1},{16,0},{17,25},{24,8},{25,17},{2,18},{3,... | collective-permute-start | bytes 786440 | tf_op jit(solution)/shard_map/ppermute | solution.py:434
  28.5 0.7 %collective-permute-done.11.got = bf16[256,256]{1,0:T(8,128)(2,1)S(1)} collective-permute-done((bf16[256,256]{1,0:T(8,128)(2,1)S(1)}, bf16[256,256]{1,0:T(8,128)(2,1)S(1)}, u32[]{:S(2)}, u32[]{:S(2)}) %collective-permute-start.11) | collective-permute-done | bytes 131104 | tf_op jit(solution)/shard_map/ppermute | solution.py:434
  29.2 0.1 rows.1
  29.2 0.1 collective-permute-start.12
  29.3 1.3 %collective-permute-done.12.got = f32[128,256]{1,0:T(8,128)S(1)} collective-permute-done((f32[128,256]{1,0:T(8,128)S(1)}, f32[128,256]{1,0:T(8,128)S(1)}, u32[]{:S(2)}, u32[]{:S(2)}) %collective-permute-start.12) | collective-permute-done | bytes 131104 | tf_op jit(solution)/shard_map/ppermute | solution.py:417
  30.7 0.8 %collective-permute-start.13 = (bf16[128,256]{1,0:T(8,128)(2,1)S(1)}, bf16[128,256]{1,0:T(8,128)(2,1)S(1)}, u32[]{:S(2)}, u32[]{:S(2)}) collective-permute-start(bf16[128,256]{1,0:T(8,128)(2,1)S(1)} %get-tuple-element.82), channel_id=1, source_target_pairs={{0,2},{1,7},{2,0},{3,5},{4,6},{5,3},{6,4},{7,1},{8,10},{9,15},{10,... | collective-permute-start | bytes 196616 | tf_op jit(solution)/shard_map/ppermute | solution.py:428
  31.5 1.5 %collective-permute-done.10.refs_1_ = bf16[256,512]{1,0:T(8,128)(2,1)S(1)} collective-permute-done((bf16[256,512]{1,0:T(8,128)(2,1)S(1)}, bf16[256,512]{1,0:T(8,128)(2,1)S(1)}, u32[]{:S(2)}, u32[]{:S(2)}) %collective-permute-start.10) | collective-permute-done | bytes 262176 | tf_op jit(solution)/shard_map/ppermute | solution.py:434
  33.0 1.5 %backward.1 = (bf16[128,128]{1,0:T(8,128)(2,1)S(1)}, bf16[128,128]{1,0:T(8,128)(2,1)S(1)}, f32[128,128]{1,0:T(8,128)S(1)}, f32[256,128]{1,0:T(8,128)S(1)}, f32[5...) custom-call(bf16[256,512]{1,0:T(8,128)(2,1)S(1)} %w_half.1.refs_0_, bf16[256,512]{1,0:T(8,128)(2,1)S(1)} %collective-permute-done.10.refs_1_, ...), custom_call_target="tpu_custom_call" | custom-call | flops 335544320 | bytes 3408384 | tf_op jit(solution)/shard_map/backward/pallas_call | solution.py:66
  34.5 0.5 collective-permute-done.13.got
  35.0 2.7 %collective-permute-start.14 = (bf16[128,256]{1,0:T(8,128)(2,1)S(1)}, bf16[128,256]{1,0:T(8,128)(2,1)S(1)}, u32[]{:S(2)}, u32[]{:S(2)}) collective-permute-start(bf16[128,256]{1,0:T(8,128)(2,1)S(1)} %get-tuple-element.84), channel_id=1, source_target_pairs={{0,4},{1,5},{2,6},{3,7},{4,0},{5,1},{6,2},{7,3},{8,12},{9,13},{10,... | collective-permute-start | bytes 196616 | tf_op jit(solution)/shard_map/ppermute | solution.py:428
  37.8 4.4 %collective-permute-done.14.got.refs_0_ = bf16[128,256]{1,0:T(8,128)(2,1)S(1)} collective-permute-done((bf16[128,256]{1,0:T(8,128)(2,1)S(1)}, bf16[128,256]{1,0:T(8,128)(2,1)S(1)}, u32[]{:S(2)}, u32[]{:S(2)}) %collective-permute-start.14) | collective-permute-done | bytes 65568 | tf_op jit(solution)/shard_map/ppermute | solution.py:428
  42.2 1.8 %collective-permute-start.17 = (bf16[64,256]{1,0:T(8,128)(2,1)S(1)}, bf16[64,256]{1,0:T(8,128)(2,1)S(1)}, u32[]{:S(2)}, u32[]{:S(2)}) collective-permute-start(bf16[64,256]{1,0:T(8,128)(2,1)S(1)} %weight_sum.1.refs_1_.first), channel_id=1, source_target_pairs={{0,8},{1,17},{8,0},{9,25},{16,24},{17,1},{24,16},{25,9},{2,10},{3,... | collective-permute-start | bytes 98312 | tf_op jit(solution)/shard_map/ppermute | solution.py:434
  44.0 0.1 collective-permute-start.15
  44.1 2.9 %collective-permute-start.16 = (bf16[128,384]{1,0:T(8,128)(2,1)S(1)}, bf16[128,384]{1,0:T(8,128)(2,1)S(1)}, u32[]{:S(2)}, u32[]{:S(2)}) collective-permute-start(bf16[128,384]{1,0:T(8,128)(2,1)S(1)} %get-tuple-element.86), channel_id=1, source_target_pairs={{0,6},{1,3},{2,4},{3,1},{4,2},{5,7},{6,0},{7,5},{8,14},{9,11},{10,... | collective-permute-start | bytes 294920 | tf_op jit(solution)/shard_map/ppermute | solution.py:428
  47.0 0.0 collective-permute-done.17.second
  47.0 1.9 %collective-permute-start.18 = (bf16[64,512]{1,0:T(8,128)(2,1)S(1)}, bf16[64,512]{1,0:T(8,128)(2,1)S(1)}, u32[]{:S(2)}, u32[]{:S(2)}) collective-permute-start(bf16[64,512]{1,0:T(8,128)(2,1)S(1)} %both.1), channel_id=1, source_target_pairs={{0,16},{1,9},{8,24},{9,1},{16,0},{17,25},{24,8},{25,17},{2,18},{3,... | collective-permute-start | bytes 196616 | tf_op jit(solution)/shard_map/ppermute | solution.py:434
  48.9 2.5 %collective-permute-done.18.refs_1_.got = bf16[64,512]{1,0:T(8,128)(2,1)S(1)} collective-permute-done((bf16[64,512]{1,0:T(8,128)(2,1)S(1)}, bf16[64,512]{1,0:T(8,128)(2,1)S(1)}, u32[]{:S(2)}, u32[]{:S(2)}) %collective-permute-start.18) | collective-permute-done | bytes 65568 | tf_op jit(solution)/shard_map/ppermute | solution.py:434
  51.3 0.0 collective-permute-done.15.a
  51.3 1.1 %collective-permute-done.16.b = bf16[128,384]{1,0:T(8,128)(2,1)S(1)} collective-permute-done((bf16[128,384]{1,0:T(8,128)(2,1)S(1)}, bf16[128,384]{1,0:T(8,128)(2,1)S(1)}, u32[]{:S(2)}, u32[]{:S(2)}) %collective-permute-start.16) | collective-permute-done | bytes 98336 | tf_op jit(solution)/shard_map/ppermute | solution.py:428
  52.4 0.4 final.1
  52.8 0.1 collective-permute-start.19
  52.9 1.4 %collective-permute-done.19.pair = bf16[128,768]{1,0:T(8,128)(2,1)S(1)} collective-permute-done((bf16[128,768]{1,0:T(8,128)(2,1)S(1)}, bf16[128,768]{1,0:T(8,128)(2,1)S(1)}, u32[]{:S(2)}, u32[]{:S(2)}) %collective-permute-start.19) | collective-permute-done | bytes 196640 | tf_op jit(solution)/shard_map/ppermute | solution.py:417
  54.3 0.8 %outputs.1 = (bf16[1,128,512]{2,1,0:T(8,128)(2,1)}, bf16[1,128,512]{2,1,0:T(8,128)(2,1)}, bf16[1,128,512]{2,1,0:T(8,128)(2,1)}) custom-call(bf16[128,768]{1,0:T(8,128)(2,1)S(1)} %get-tuple-element.87.own, bf16[128,768]{1,0:T(8,128)(2,1)S(1)} %collective-permute-done.19.pair), custom_call_target="tpu_custom_call" | custom-call | bytes 786432 | tf_op jit(solution)/shard_map/outputs/pallas_call | solution.py:66
  55.1 0.7 %weight_join.1 = f32[64,1024]{1,0:T(8,128)} custom-call(bf16[64,512]{1,0:T(8,128)(2,1)S(1)} %both.1, bf16[64,512]{1,0:T(8,128)(2,1)S(1)} %collective-permute-done.18.refs_1_.got, bf16[1,128,512]{2,1,0:T(8,128)(2,1)} %get-tuple-element.44._), custom_call_target="tpu_custom_call" | custom-call | bytes 524288 | tf_op jit(solution)/shard_map/weight_join/pallas_call | solution.py:66
  (8 shorter events, 0.2 us)
Async XLA Ops:
  0.6 2.3 %collective-permute-start = (bf16[1,128,512]{2,1,0:T(8,128)(2,1)}, bf16[1,128,512]{2,1,0:T(8,128)(2,1)S(1)}, u32[]{:S(2)}, u32[]{:S(2)}) collective-permute-start(bf16[1,128,512]{2,1,0:T(8,128)(2,1)} %q.1), channel_id=1, source_target_pairs={{0,1},{1,0},{2,3},{3,2},{4,5},{5,4},{6,7},{7,6},{8,9},{9,8},{10,11... | collective-permute-start | bytes 393224 | tf_op jit(solution)/shard_map/ppermute | solution.py:417
  1.2 1.8 %collective-permute-start.1 = (bf16[1,128,512]{2,1,0:T(8,128)(2,1)}, bf16[1,128,512]{2,1,0:T(8,128)(2,1)S(1)}, u32[]{:S(2)}, u32[]{:S(2)}) collective-permute-start(bf16[1,128,512]{2,1,0:T(8,128)(2,1)} %k.1), channel_id=1, source_target_pairs={{0,1},{1,0},{2,3},{3,2},{4,5},{5,4},{6,7},{7,6},{8,9},{9,8},{10,11... | collective-permute-start | bytes 393224 | tf_op jit(solution)/shard_map/ppermute | solution.py:417
  1.2 1.7 %collective-permute-start.2 = (bf16[1,128,512]{2,1,0:T(8,128)(2,1)}, bf16[1,128,512]{2,1,0:T(8,128)(2,1)S(1)}, u32[]{:S(2)}, u32[]{:S(2)}) collective-permute-start(bf16[1,128,512]{2,1,0:T(8,128)(2,1)} %v.1), channel_id=1, source_target_pairs={{0,1},{1,0},{2,3},{3,2},{4,5},{5,4},{6,7},{7,6},{8,9},{9,8},{10,11... | collective-permute-start | bytes 393224 | tf_op jit(solution)/shard_map/ppermute | solution.py:417
  1.7 14.1 %collective-permute-start.8 = (bf16[128,1024]{1,0:T(8,128)(2,1)}, bf16[128,1024]{1,0:T(8,128)(2,1)S(1)}, u32[]{:S(2)}, u32[]{:S(2)}) collective-permute-start(bf16[128,1024]{1,0:T(8,128)(2,1)} %bitcast.1), channel_id=1, source_target_pairs={{0,1},{1,0},{2,3},{3,2},{4,5},{5,4},{6,7},{7,6},{8,9},{9,8},{10,11... | collective-permute-start | bytes 786440 | tf_op jit(solution)/shard_map/ppermute | solution.py:417
  3.2 6.0 %collective-permute-start.3 = (bf16[128,512]{1,0:T(8,128)(2,1)S(1)}, bf16[128,512]{1,0:T(8,128)(2,1)S(1)}, u32[]{:S(2)}, u32[]{:S(2)}) collective-permute-start(bf16[128,512]{1,0:T(8,128)(2,1)S(1)} %get-tuple-element.50), channel_id=1, source_target_pairs={{0,2},{1,7},{2,0},{3,5},{4,6},{5,3},{6,4},{7,1},{8,10},{9,15},{10,... | collective-permute-start | bytes 393224 | tf_op jit(solution)/shard_map/ppermute | solution.py:428
  6.3 9.4 %collective-permute-start.4 = (bf16[128,512]{1,0:T(8,128)(2,1)S(1)}, bf16[128,512]{1,0:T(8,128)(2,1)S(1)}, u32[]{:S(2)}, u32[]{:S(2)}) collective-permute-start(bf16[128,512]{1,0:T(8,128)(2,1)S(1)} %get-tuple-element.51), channel_id=1, source_target_pairs={{0,6},{1,3},{2,4},{3,1},{4,2},{5,7},{6,0},{7,5},{8,14},{9,11},{10,... | collective-permute-start | bytes 393224 | tf_op jit(solution)/shard_map/ppermute | solution.py:428
  8.8 8.2 %collective-permute-start.5 = (bf16[128,256]{1,0:T(8,128)(2,1)S(1)}, bf16[128,256]{1,0:T(8,128)(2,1)S(1)}, u32[]{:S(2)}, u32[]{:S(2)}) collective-permute-start(bf16[128,256]{1,0:T(8,128)(2,1)S(1)} %get-tuple-element.52), channel_id=1, source_target_pairs={{0,4},{1,5},{2,6},{3,7},{4,0},{5,1},{6,2},{7,3},{8,12},{9,13},{10,... | collective-permute-start | bytes 196616 | tf_op jit(solution)/shard_map/ppermute | solution.py:428
  17.6 6.4 %collective-permute-start.9 = (bf16[256,512]{1,0:T(8,128)(2,1)S(1)}, bf16[256,512]{1,0:T(8,128)(2,1)S(1)}, u32[]{:S(2)}, u32[]{:S(2)}) collective-permute-start(bf16[256,512]{1,0:T(8,128)(2,1)S(1)} %get-tuple-element.63), channel_id=1, source_target_pairs={{0,8},{1,17},{8,0},{9,25},{16,24},{17,1},{24,16},{25,9},{2,10},{3,... | collective-permute-start | bytes 786440 | tf_op jit(solution)/shard_map/ppermute | solution.py:434
  19.2 1.3 %collective-permute-start.6 = (bf16[2,64,256]{2,1,0:T(8,128)(2,1)S(1)}, bf16[2,64,256]{2,1,0:T(8,128)(2,1)S(1)}, u32[]{:S(2)}, u32[]{:S(2)}) collective-permute-start(bf16[2,64,256]{2,1,0:T(8,128)(2,1)S(1)} %get-tuple-element.54), channel_id=1, source_target_pairs={{0,1},{1,0},{2,3},{3,2},{4,5},{5,4},{6,7},{7,6},{8,9},{9,8},{10,11... | collective-permute-start | bytes 196616 | tf_op jit(solution)/shard_map/ppermute | solution.py:417
  20.6 6.0 %collective-permute-start.7 = (bf16[256,256]{1,0:T(8,128)(2,1)S(1)}, bf16[256,256]{1,0:T(8,128)(2,1)S(1)}, u32[]{:S(2)}, u32[]{:S(2)}) collective-permute-start(bf16[256,256]{1,0:T(8,128)(2,1)S(1)} %w_rows.1.first), channel_id=1, source_target_pairs={{0,8},{1,17},{8,0},{9,25},{16,24},{17,1},{24,16},{25,9},{2,10},{3,... | collective-permute-start | bytes 393224 | tf_op jit(solution)/shard_map/ppermute | solution.py:434
  24.1 5.0 %collective-permute-start.11 = (bf16[256,256]{1,0:T(8,128)(2,1)S(1)}, bf16[256,256]{1,0:T(8,128)(2,1)S(1)}, u32[]{:S(2)}, u32[]{:S(2)}) collective-permute-start(bf16[256,256]{1,0:T(8,128)(2,1)S(1)} %get-tuple-element.64.refs_0_), channel_id=1, source_target_pairs={{0,16},{1,9},{8,24},{9,1},{16,0},{17,25},{24,8},{25,17},{2,18},{3,... | collective-permute-start | bytes 393224 | tf_op jit(solution)/shard_map/ppermute | solution.py:434
  26.6 6.4 %collective-permute-start.10 = (bf16[256,512]{1,0:T(8,128)(2,1)S(1)}, bf16[256,512]{1,0:T(8,128)(2,1)S(1)}, u32[]{:S(2)}, u32[]{:S(2)}) collective-permute-start(bf16[256,512]{1,0:T(8,128)(2,1)S(1)} %w_half.1.refs_0_), channel_id=1, source_target_pairs={{0,16},{1,9},{8,24},{9,1},{16,0},{17,25},{24,8},{25,17},{2,18},{3,... | collective-permute-start | bytes 786440 | tf_op jit(solution)/shard_map/ppermute | solution.py:434
  29.2 1.4 %collective-permute-start.12 = (f32[128,256]{1,0:T(8,128)S(1)}, f32[128,256]{1,0:T(8,128)S(1)}, u32[]{:S(2)}, u32[]{:S(2)}) collective-permute-start(f32[128,256]{1,0:T(8,128)S(1)} %get-tuple-element.67), channel_id=1, source_target_pairs={{0,1},{1,0},{2,3},{3,2},{4,5},{5,4},{6,7},{7,6},{8,9},{9,8},{10,11... | collective-permute-start | bytes 393224 | tf_op jit(solution)/shard_map/ppermute | solution.py:417
  30.7 4.3 %collective-permute-start.13 = (bf16[128,256]{1,0:T(8,128)(2,1)S(1)}, bf16[128,256]{1,0:T(8,128)(2,1)S(1)}, u32[]{:S(2)}, u32[]{:S(2)}) collective-permute-start(bf16[128,256]{1,0:T(8,128)(2,1)S(1)} %get-tuple-element.82), channel_id=1, source_target_pairs={{0,2},{1,7},{2,0},{3,5},{4,6},{5,3},{6,4},{7,1},{8,10},{9,15},{10,... | collective-permute-start | bytes 196616 | tf_op jit(solution)/shard_map/ppermute | solution.py:428
  35.0 7.2 %collective-permute-start.14 = (bf16[128,256]{1,0:T(8,128)(2,1)S(1)}, bf16[128,256]{1,0:T(8,128)(2,1)S(1)}, u32[]{:S(2)}, u32[]{:S(2)}) collective-permute-start(bf16[128,256]{1,0:T(8,128)(2,1)S(1)} %get-tuple-element.84), channel_id=1, source_target_pairs={{0,4},{1,5},{2,6},{3,7},{4,0},{5,1},{6,2},{7,3},{8,12},{9,13},{10,... | collective-permute-start | bytes 196616 | tf_op jit(solution)/shard_map/ppermute | solution.py:428
  42.2 4.8 %collective-permute-start.17 = (bf16[64,256]{1,0:T(8,128)(2,1)S(1)}, bf16[64,256]{1,0:T(8,128)(2,1)S(1)}, u32[]{:S(2)}, u32[]{:S(2)}) collective-permute-start(bf16[64,256]{1,0:T(8,128)(2,1)S(1)} %weight_sum.1.refs_1_.first), channel_id=1, source_target_pairs={{0,8},{1,17},{8,0},{9,25},{16,24},{17,1},{24,16},{25,9},{2,10},{3,... | collective-permute-start | bytes 98312 | tf_op jit(solution)/shard_map/ppermute | solution.py:434
  44.0 7.3 %collective-permute-start.15 = (bf16[128,384]{1,0:T(8,128)(2,1)S(1)}, bf16[128,384]{1,0:T(8,128)(2,1)S(1)}, u32[]{:S(2)}, u32[]{:S(2)}) collective-permute-start(bf16[128,384]{1,0:T(8,128)(2,1)S(1)} %get-tuple-element.85), channel_id=1, source_target_pairs={{0,2},{1,7},{2,0},{3,5},{4,6},{5,3},{6,4},{7,1},{8,10},{9,15},{10,... | collective-permute-start | bytes 294920 | tf_op jit(solution)/shard_map/ppermute | solution.py:428
  44.1 8.3 %collective-permute-start.16 = (bf16[128,384]{1,0:T(8,128)(2,1)S(1)}, bf16[128,384]{1,0:T(8,128)(2,1)S(1)}, u32[]{:S(2)}, u32[]{:S(2)}) collective-permute-start(bf16[128,384]{1,0:T(8,128)(2,1)S(1)} %get-tuple-element.86), channel_id=1, source_target_pairs={{0,6},{1,3},{2,4},{3,1},{4,2},{5,7},{6,0},{7,5},{8,14},{9,11},{10,... | collective-permute-start | bytes 294920 | tf_op jit(solution)/shard_map/ppermute | solution.py:428
  47.0 4.3 %collective-permute-start.18 = (bf16[64,512]{1,0:T(8,128)(2,1)S(1)}, bf16[64,512]{1,0:T(8,128)(2,1)S(1)}, u32[]{:S(2)}, u32[]{:S(2)}) collective-permute-start(bf16[64,512]{1,0:T(8,128)(2,1)S(1)} %both.1), channel_id=1, source_target_pairs={{0,16},{1,9},{8,24},{9,1},{16,0},{17,25},{24,8},{25,17},{2,18},{3,... | collective-permute-start | bytes 196616 | tf_op jit(solution)/shard_map/ppermute | solution.py:434
  52.8 1.5 %collective-permute-start.19 = (bf16[128,768]{1,0:T(8,128)(2,1)S(1)}, bf16[128,768]{1,0:T(8,128)(2,1)S(1)}, u32[]{:S(2)}, u32[]{:S(2)}) collective-permute-start(bf16[128,768]{1,0:T(8,128)(2,1)S(1)} %get-tuple-element.88), channel_id=1, source_target_pairs={{0,1},{1,0},{2,3},{3,2},{4,5},{5,4},{6,7},{7,6},{8,9},{9,8},{10,11... | collective-permute-start | bytes 589832 | tf_op jit(solution)/shard_map/ppermute | solution.py:417

commit v17 on v13

--- a/solution.py
+++ b/solution.py
@@ -225,7 +225,7 @@
     rows = mine.shape[0]
     total = state[...]
     if direct:
-        a, b, c, soft_send, u_out, total_out, keep, out = refs
+        a, b, c, soft_send, _, u_out, total_out, keep, out = refs
         total = total + a[:, 2 * DH : 3 * DH].astype(F32) + b[:, 2 * DH : 3 * DH].astype(F32)
         total = total + c[:, :DH].astype(F32)
     else:
@@ -334,7 +334,7 @@
         rows = slice(group * half, (group + 1) * half)
         heads[2 * group + core] = own[rows, :]
         heads[2 * group + 1 - core] = got[rows, :]
-    for index, step in enumerate((way["first"], way["second"])):
+    for index, step in enumerate((1, 3)):
         send[index * half : (index + 1) * half, :] = heads[z ^ step].astype(BF)
     for index, step in enumerate((0, 2)):
         keep[index * half : (index + 1) * half, :] = heads[z ^ step]
@@ -425,7 +425,7 @@
         for z in range(n_z):
             for c in range(2):
                 if direct:
-                    there = z ^ (1 + 2 * c, 3 - 2 * c, 2)[which]
+                    there = z ^ (1 + 2 * c, 3 - 2 * c, 2, 1)[which]
                 else:
                     there = (z + (1 if (which == 1) != back else -1)) % n_z
                 pairs.append((2 * z + c, 2 * there + c))
@@ -495,7 +495,7 @@
         functools.partial(lin_forward_kernel, direct), "lin_forward",
         [like((2 * rows, DH), F32), like((DH, DH), F32), like((DH, keep_width), F32)]
         + [like((2 * DH, 2 * width), BF)] * direct,
-        [state, mine, pair, ogs, gain] + ([a, b] + c + soft_send if direct else []),
+        [state, mine, pair, ogs, gain] + ([a, b] + c + soft_send + [w_own] if direct else []),
         flops=wg_flops,
     )
     if direct:
@@ -518,7 +518,7 @@
             chunk_kernel, "chunk", [like((DH, width), BF), like((DH, width), F32)],
             [row_own, row_recv], scratch=[pltpu.VMEM((HEADS, half, width), F32)],
         )
-        piece_got = over_z(piece_send, 0)
+        piece_got = over_z(piece_send, 3)
         weights.append(piece_keep)
     dq_lin, dq_lin_pair, dstate, dq_soft, dk_soft, dv_soft = call(
         functools.partial(backward_kernel, direct), "backward",

time: 53.1 us -> 53.7 us (1.011)
  waiting for transfers between devices: 23.7 us -> 25.7 us
  starting transfers between devices: 21.4 us -> 20 us
    ppermute x6, waiting for transfers between devices: 9.88 us -> 11.9 us  [over_dp(): return lax.ppermute(value, ('dp', 'core'), pairs)]
    ppermute x7, waiting for transfers between devices: 11.3 us -> 12.5 us  [over_z(): return lax.ppermute(value, axes, pairs)]
    ppermute x7, waiting for transfers between devices: 2.59 us -> 1.37 us  [over_core(): return lax.ppermute(value, 'core', pair_perm)]
    ppermute x6, starting transfers between devices: 9.16 us -> 8.16 us  [over_dp(): return lax.ppermute(value, ('dp', 'core'), pairs)]
  transfers between devices with their start and end apart: 20 -> 20, of which waited for: 12 -> 9; matrix products, arithmetic and copies ran while one was open for 0% -> 0% of each run, Pallas kernels for 10% -> 10%
where the time goes in v17:
time: 53.7 us; the launch traced here: 53.6 us
  waiting for transfers between devices  25.7 us (48%)
  starting transfers between devices  20 us (37%)
  Pallas kernels  7.06 us (13%)
  between operations  0.79 us (1%)
    ppermute x7, waiting for transfers between devices, over_z(): return lax.ppermute(value, axes, pairs)  12.5 us
    ppermute x6, waiting for transfers between devices, over_dp(): return lax.ppermute(value, ('dp', 'core'), pairs)  11.9 us
    ppermute x7, starting transfers between devices, over_z(): return lax.ppermute(value, axes, pairs)  10.5 us
    ppermute x6, starting transfers between devices, over_dp(): return lax.ppermute(value, ('dp', 'core'), pairs)  8.16 us
    pallas_call x17, Pallas kernels, call(): pl.pallas_call(kernel, name=name, out_shape=list(outs), in_specs=spaces o...  7.06 us
    ppermute x7, waiting for transfers between devices, over_core(): return lax.ppermute(value, 'core', pair_perm)  1.37 us
    ppermute x7, starting transfers between devices, over_core(): return lax.ppermute(value, 'core', pair_perm)  1.32 us
  transfers between devices with their start and end apart: 20, of which 9 were waited for; matrix products, arithmetic and copies ran while one was open for 0% of the time, Pallas kernels for 10%

profile of v17, /device:TPU:0, one launch (start us, length us, event | category | flops | bytes accessed | tf_op | source)
XLA Modules:
  0.0 53.6 jit_solution(730120990904829288)
XLA Ops:
  0.6 0.5 collective-permute-start
  1.2 0.1 collective-permute-start.1
  1.2 0.4 collective-permute-start.2
  1.7 0.1 collective-permute-start.8
  1.7 1.2 %pack.1 = (bf16[128,768]{1,0:T(8,128)(2,1)S(1)}, bf16[128,1024]{1,0:T(8,128)(2,1)S(1)}, bf16[64,256]{1,0:T(8,128)(2,1)S(1)}, f32[1,128]{1,0:T(1,128)S(1)}) custom-call(bf16[1,128,512]{2,1,0:T(8,128)(2,1)} %q.1, bf16[1,128,512]{2,1,0:T(8,128)(2,1)} %k.1, bf16[1,128,512]{2,1,0:T(8,128)(2,1)} %v.1, bf16[1,128,1024]{2,1,0:T(8,128)(2,1)} %og.1, ...), custom_call_target="tpu_custom_call" | custom-call | bytes 1279488 | tf_op jit(solution)/shard_map/pack/pallas_call | solution.py:66
  2.9 0.0 collective-permute-done.q_pair
  2.9 0.0 collective-permute-done.1.k_pair
  2.9 0.0 collective-permute-done.2.v_pair
  3.0 0.3 state.1
  3.2 3.1 %collective-permute-start.3 = (bf16[128,512]{1,0:T(8,128)(2,1)S(1)}, bf16[128,512]{1,0:T(8,128)(2,1)S(1)}, u32[]{:S(2)}, u32[]{:S(2)}) collective-permute-start(bf16[128,512]{1,0:T(8,128)(2,1)S(1)} %get-tuple-element.50), channel_id=1, source_target_pairs={{0,2},{1,7},{2,0},{3,5},{4,6},{5,3},{6,4},{7,1},{8,10},{9,15},{10,... | collective-permute-start | bytes 393224 | tf_op jit(solution)/shard_map/ppermute | solution.py:432
  6.3 2.5 %collective-permute-start.4 = (bf16[128,512]{1,0:T(8,128)(2,1)S(1)}, bf16[128,512]{1,0:T(8,128)(2,1)S(1)}, u32[]{:S(2)}, u32[]{:S(2)}) collective-permute-start(bf16[128,512]{1,0:T(8,128)(2,1)S(1)} %get-tuple-element.51), channel_id=1, source_target_pairs={{0,6},{1,3},{2,4},{3,1},{4,2},{5,7},{6,0},{7,5},{8,14},{9,11},{10,... | collective-permute-start | bytes 393224 | tf_op jit(solution)/shard_map/ppermute | solution.py:432
  8.8 0.1 collective-permute-start.5
  8.9 7.9 %collective-permute-done.5.c.refs_2_ = bf16[128,256]{1,0:T(8,128)(2,1)S(1)} collective-permute-done((bf16[128,256]{1,0:T(8,128)(2,1)S(1)}, bf16[128,256]{1,0:T(8,128)(2,1)S(1)}, u32[]{:S(2)}, u32[]{:S(2)}) %collective-permute-start.5) | collective-permute-done | bytes 65568 | tf_op jit(solution)/shard_map/ppermute | solution.py:432
  16.8 0.0 collective-permute-done.3.a.refs_0_
  16.8 0.0 collective-permute-done.4.b.refs_1_
  16.9 0.1 collective-permute-start.6
  17.0 0.0 collective-permute-done.8.og_recv
  17.0 1.2 %soft_forward.1 = (bf16[256,128]{1,0:T(8,128)(2,1)S(1)}, bf16[512,128]{1,0:T(8,128)(2,1)S(1)}, bf16[512,128]{1,0:T(8,128)(2,1)S(1)}, bf16[256,1024]{1,0:T(8,128)...) custom-call(bf16[128,768]{1,0:T(8,128)(2,1)S(1)} %get-tuple-element., ...), custom_call_target="tpu_custom_call" | custom-call | flops 67108864 | bytes 2949120 | tf_op jit(solution)/shard_map/soft_forward/pallas_call | solution.py:66
  18.2 0.0 collective-permute-done.6.got
  18.2 0.7 %lin_forward.1 = (f32[256,128]{1,0:T(8,128)S(1)}, f32[128,128]{1,0:T(8,128)S(1)}, f32[128,512]{1,0:T(8,128)S(1)}, bf16[256,512]{1,0:T(8,128)(2,1)S(1)}) custom-call(f32[128,128]{1,0:T(8,128)S(1)} %get-tuple-element.58.state, bf16[128,768]{1,0:T(8,128)(2,1)S(1)} %get-tuple-element.49.mine.refs_6_, bf16[128,768]{1,0:T(8,128)(2,1)S(1)} %get-tuple-element.55.pair.refs_7_, ...), custom_call_target="tpu_custom_call" | custom-call | flops 67108864 | bytes 2294272 | tf_op jit(solution)/shard_map/lin_forward/pallas_call | solution.py:66
  18.9 1.6 %collective-permute-start.9 = (bf16[256,512]{1,0:T(8,128)(2,1)S(1)}, bf16[256,512]{1,0:T(8,128)(2,1)S(1)}, u32[]{:S(2)}, u32[]{:S(2)}) collective-permute-start(bf16[256,512]{1,0:T(8,128)(2,1)S(1)} %get-tuple-element.63), channel_id=1, source_target_pairs={{0,8},{1,17},{8,0},{9,25},{16,24},{17,1},{24,16},{25,9},{2,10},{3,... | collective-permute-start | bytes 786440 | tf_op jit(solution)/shard_map/ppermute | solution.py:438
  20.5 0.5 %collective-permute-start.7 = (bf16[256,256]{1,0:T(8,128)(2,1)S(1)}, bf16[256,256]{1,0:T(8,128)(2,1)S(1)}, u32[]{:S(2)}, u32[]{:S(2)}) collective-permute-start(bf16[256,256]{1,0:T(8,128)(2,1)S(1)} %w_rows.1.refs_4_.first), channel_id=1, source_target_pairs={{0,8},{1,17},{8,0},{9,25},{16,24},{17,1},{24,16},{25,9},{2,10},{3,... | collective-permute-start | bytes 393224 | tf_op jit(solution)/shard_map/ppermute | solution.py:438
  21.0 4.3 %collective-permute-done.9.got = bf16[256,512]{1,0:T(8,128)(2,1)S(1)} collective-permute-done((bf16[256,512]{1,0:T(8,128)(2,1)S(1)}, bf16[256,512]{1,0:T(8,128)(2,1)S(1)}, u32[]{:S(2)}, u32[]{:S(2)}) %collective-permute-start.9) | collective-permute-done | bytes 262176 | tf_op jit(solution)/shard_map/ppermute | solution.py:438
  25.4 0.1 fold.1
  25.4 1.6 %collective-permute-start.11 = (bf16[256,256]{1,0:T(8,128)(2,1)S(1)}, bf16[256,256]{1,0:T(8,128)(2,1)S(1)}, u32[]{:S(2)}, u32[]{:S(2)}) collective-permute-start(bf16[256,256]{1,0:T(8,128)(2,1)S(1)} %get-tuple-element.64.refs_0_), channel_id=1, source_target_pairs={{0,16},{1,9},{8,24},{9,1},{16,0},{17,25},{24,8},{25,17},{2,18},{3,... | collective-permute-start | bytes 393224 | tf_op jit(solution)/shard_map/ppermute | solution.py:438
  27.0 0.0 collective-permute-done.7.second
  27.0 1.3 %collective-permute-start.10 = (bf16[256,512]{1,0:T(8,128)(2,1)S(1)}, bf16[256,512]{1,0:T(8,128)(2,1)S(1)}, u32[]{:S(2)}, u32[]{:S(2)}) collective-permute-start(bf16[256,512]{1,0:T(8,128)(2,1)S(1)} %w_half.1.refs_0_), channel_id=1, source_target_pairs={{0,16},{1,9},{8,24},{9,1},{16,0},{17,25},{24,8},{25,17},{2,18},{3,... | collective-permute-start | bytes 786440 | tf_op jit(solution)/shard_map/ppermute | solution.py:438
  28.4 2.1 %collective-permute-done.11.got = bf16[256,256]{1,0:T(8,128)(2,1)S(1)} collective-permute-done((bf16[256,256]{1,0:T(8,128)(2,1)S(1)}, bf16[256,256]{1,0:T(8,128)(2,1)S(1)}, u32[]{:S(2)}, u32[]{:S(2)}) %collective-permute-start.11) | collective-permute-done | bytes 131104 | tf_op jit(solution)/shard_map/ppermute | solution.py:438
  30.5 0.1 rows.1
  30.5 0.1 collective-permute-start.12
  30.6 1.3 %collective-permute-done.12.got = f32[128,256]{1,0:T(8,128)S(1)} collective-permute-done((f32[128,256]{1,0:T(8,128)S(1)}, f32[128,256]{1,0:T(8,128)S(1)}, u32[]{:S(2)}, u32[]{:S(2)}) %collective-permute-start.12) | collective-permute-done | bytes 131104 | tf_op jit(solution)/shard_map/ppermute | solution.py:421
  32.0 0.4 collective-permute-start.13
  32.4 1.1 %collective-permute-done.10.refs_1_ = bf16[256,512]{1,0:T(8,128)(2,1)S(1)} collective-permute-done((bf16[256,512]{1,0:T(8,128)(2,1)S(1)}, bf16[256,512]{1,0:T(8,128)(2,1)S(1)}, u32[]{:S(2)}, u32[]{:S(2)}) %collective-permute-start.10) | collective-permute-done | bytes 262176 | tf_op jit(solution)/shard_map/ppermute | solution.py:438
  33.5 1.5 %backward.1 = (bf16[128,128]{1,0:T(8,128)(2,1)S(1)}, bf16[128,128]{1,0:T(8,128)(2,1)S(1)}, f32[128,128]{1,0:T(8,128)S(1)}, f32[256,128]{1,0:T(8,128)S(1)}, f32[5...) custom-call(bf16[256,512]{1,0:T(8,128)(2,1)S(1)} %w_half.1.refs_0_, bf16[256,512]{1,0:T(8,128)(2,1)S(1)} %collective-permute-done.10.refs_1_, ...), custom_call_target="tpu_custom_call" | custom-call | flops 335544320 | bytes 3408384 | tf_op jit(solution)/shard_map/backward/pallas_call | solution.py:66
  35.0 1.3 %collective-permute-done.13.got = bf16[128,256]{1,0:T(8,128)(2,1)S(1)} collective-permute-done((bf16[128,256]{1,0:T(8,128)(2,1)S(1)}, bf16[128,256]{1,0:T(8,128)(2,1)S(1)}, u32[]{:S(2)}, u32[]{:S(2)}) %collective-permute-start.13) | collective-permute-done | bytes 65568 | tf_op jit(solution)/shard_map/ppermute | solution.py:432
  36.4 1.9 %collective-permute-start.16 = (bf16[128,256]{1,0:T(8,128)(2,1)S(1)}, bf16[128,256]{1,0:T(8,128)(2,1)S(1)}, u32[]{:S(2)}, u32[]{:S(2)}) collective-permute-start(bf16[128,256]{1,0:T(8,128)(2,1)S(1)} %get-tuple-element.85), channel_id=1, source_target_pairs={{0,4},{1,5},{2,6},{3,7},{4,0},{5,1},{6,2},{7,3},{8,12},{9,13},{10,... | collective-permute-start | bytes 196616 | tf_op jit(solution)/shard_map/ppermute | solution.py:432
  38.3 1.9 %collective-permute-start.14 = (bf16[128,384]{1,0:T(8,128)(2,1)S(1)}, bf16[128,384]{1,0:T(8,128)(2,1)S(1)}, u32[]{:S(2)}, u32[]{:S(2)}) collective-permute-start(bf16[128,384]{1,0:T(8,128)(2,1)S(1)} %get-tuple-element.83), channel_id=1, source_target_pairs={{0,2},{1,7},{2,0},{3,5},{4,6},{5,3},{6,4},{7,1},{8,10},{9,15},{10,... | collective-permute-start | bytes 294920 | tf_op jit(solution)/shard_map/ppermute | solution.py:432
  40.1 0.7 %collective-permute-start.15 = (bf16[128,384]{1,0:T(8,128)(2,1)S(1)}, bf16[128,384]{1,0:T(8,128)(2,1)S(1)}, u32[]{:S(2)}, u32[]{:S(2)}) collective-permute-start(bf16[128,384]{1,0:T(8,128)(2,1)S(1)} %get-tuple-element.84), channel_id=1, source_target_pairs={{0,6},{1,3},{2,4},{3,1},{4,2},{5,7},{6,0},{7,5},{8,14},{9,11},{10,... | collective-permute-start | bytes 294920 | tf_op jit(solution)/shard_map/ppermute | solution.py:432
  40.8 3.2 %collective-permute-done.16.got.refs_0_ = bf16[128,256]{1,0:T(8,128)(2,1)S(1)} collective-permute-done((bf16[128,256]{1,0:T(8,128)(2,1)S(1)}, bf16[128,256]{1,0:T(8,128)(2,1)S(1)}, u32[]{:S(2)}, u32[]{:S(2)}) %collective-permute-start.16) | collective-permute-done | bytes 65568 | tf_op jit(solution)/shard_map/ppermute | solution.py:432
  44.1 1.6 %collective-permute-start.17 = (bf16[64,256]{1,0:T(8,128)(2,1)S(1)}, bf16[64,256]{1,0:T(8,128)(2,1)S(1)}, u32[]{:S(2)}, u32[]{:S(2)}) collective-permute-start(bf16[64,256]{1,0:T(8,128)(2,1)S(1)} %weight_sum.1.first), channel_id=1, source_target_pairs={{0,8},{1,17},{8,0},{9,25},{16,24},{17,1},{24,16},{25,9},{2,10},{3,... | collective-permute-start | bytes 98312 | tf_op jit(solution)/shard_map/ppermute | solution.py:438
  45.6 2.4 %collective-permute-done.17.second = bf16[64,256]{1,0:T(8,128)(2,1)S(1)} collective-permute-done((bf16[64,256]{1,0:T(8,128)(2,1)S(1)}, bf16[64,256]{1,0:T(8,128)(2,1)S(1)}, u32[]{:S(2)}, u32[]{:S(2)}) %collective-permute-start.17) | collective-permute-done | bytes 32800 | tf_op jit(solution)/shard_map/ppermute | solution.py:438
  48.0 0.0 collective-permute-done.14.a
  48.0 0.0 collective-permute-done.15.b
  48.1 0.4 final.1
  48.4 0.1 collective-permute-start.18
  48.5 1.6 %collective-permute-start.19 = (bf16[64,512]{1,0:T(8,128)(2,1)S(1)}, bf16[64,512]{1,0:T(8,128)(2,1)S(1)}, u32[]{:S(2)}, u32[]{:S(2)}) collective-permute-start(bf16[64,512]{1,0:T(8,128)(2,1)S(1)} %both.1.refs_1_), channel_id=1, source_target_pairs={{0,16},{1,9},{8,24},{9,1},{16,0},{17,25},{24,8},{25,17},{2,18},{3,... | collective-permute-start | bytes 196616 | tf_op jit(solution)/shard_map/ppermute | solution.py:438
  50.1 0.0 collective-permute-done.18.pair
  50.1 0.8 %outputs.1 = (bf16[1,128,512]{2,1,0:T(8,128)(2,1)}, bf16[1,128,512]{2,1,0:T(8,128)(2,1)}, bf16[1,128,512]{2,1,0:T(8,128)(2,1)}) custom-call(bf16[128,768]{1,0:T(8,128)(2,1)S(1)} %get-tuple-element.87.own, bf16[128,768]{1,0:T(8,128)(2,1)S(1)} %collective-permute-done.18.pair), custom_call_target="tpu_custom_call" | custom-call | bytes 786432 | tf_op jit(solution)/shard_map/outputs/pallas_call | solution.py:66
  50.9 1.9 %collective-permute-done.19.got = bf16[64,512]{1,0:T(8,128)(2,1)S(1)} collective-permute-done((bf16[64,512]{1,0:T(8,128)(2,1)S(1)}, bf16[64,512]{1,0:T(8,128)(2,1)S(1)}, u32[]{:S(2)}, u32[]{:S(2)}) %collective-permute-start.19) | collective-permute-done | bytes 65568 | tf_op jit(solution)/shard_map/ppermute | solution.py:438
  52.8 0.7 %weight_join.1 = f32[64,1024]{1,0:T(8,128)} custom-call(bf16[64,512]{1,0:T(8,128)(2,1)S(1)} %both.1.refs_1_, bf16[64,512]{1,0:T(8,128)(2,1)S(1)} %collective-permute-done.19.got, bf16[1,128,512]{2,1,0:T(8,128)(2,1)} %get-tuple-element.44._), custom_call_target="tpu_custom_call" | custom-call | bytes 524288 | tf_op jit(solution)/shard_map/weight_join/pallas_call | solution.py:66
  (7 shorter events, 0.2 us)
Async XLA Ops:
  0.6 2.3 %collective-permute-start = (bf16[1,128,512]{2,1,0:T(8,128)(2,1)}, bf16[1,128,512]{2,1,0:T(8,128)(2,1)S(1)}, u32[]{:S(2)}, u32[]{:S(2)}) collective-permute-start(bf16[1,128,512]{2,1,0:T(8,128)(2,1)} %q.1), channel_id=1, source_target_pairs={{0,1},{1,0},{2,3},{3,2},{4,5},{5,4},{6,7},{7,6},{8,9},{9,8},{10,11... | collective-permute-start | bytes 393224 | tf_op jit(solution)/shard_map/ppermute | solution.py:421
  1.2 1.8 %collective-permute-start.1 = (bf16[1,128,512]{2,1,0:T(8,128)(2,1)}, bf16[1,128,512]{2,1,0:T(8,128)(2,1)S(1)}, u32[]{:S(2)}, u32[]{:S(2)}) collective-permute-start(bf16[1,128,512]{2,1,0:T(8,128)(2,1)} %k.1), channel_id=1, source_target_pairs={{0,1},{1,0},{2,3},{3,2},{4,5},{5,4},{6,7},{7,6},{8,9},{9,8},{10,11... | collective-permute-start | bytes 393224 | tf_op jit(solution)/shard_map/ppermute | solution.py:421
  1.2 1.7 %collective-permute-start.2 = (bf16[1,128,512]{2,1,0:T(8,128)(2,1)}, bf16[1,128,512]{2,1,0:T(8,128)(2,1)S(1)}, u32[]{:S(2)}, u32[]{:S(2)}) collective-permute-start(bf16[1,128,512]{2,1,0:T(8,128)(2,1)} %v.1), channel_id=1, source_target_pairs={{0,1},{1,0},{2,3},{3,2},{4,5},{5,4},{6,7},{7,6},{8,9},{9,8},{10,11... | collective-permute-start | bytes 393224 | tf_op jit(solution)/shard_map/ppermute | solution.py:421
  1.7 15.3 %collective-permute-start.8 = (bf16[128,1024]{1,0:T(8,128)(2,1)}, bf16[128,1024]{1,0:T(8,128)(2,1)S(1)}, u32[]{:S(2)}, u32[]{:S(2)}) collective-permute-start(bf16[128,1024]{1,0:T(8,128)(2,1)} %bitcast.1), channel_id=1, source_target_pairs={{0,1},{1,0},{2,3},{3,2},{4,5},{5,4},{6,7},{7,6},{8,9},{9,8},{10,11... | collective-permute-start | bytes 786440 | tf_op jit(solution)/shard_map/ppermute | solution.py:421
  3.2 13.6 %collective-permute-start.3 = (bf16[128,512]{1,0:T(8,128)(2,1)S(1)}, bf16[128,512]{1,0:T(8,128)(2,1)S(1)}, u32[]{:S(2)}, u32[]{:S(2)}) collective-permute-start(bf16[128,512]{1,0:T(8,128)(2,1)S(1)} %get-tuple-element.50), channel_id=1, source_target_pairs={{0,2},{1,7},{2,0},{3,5},{4,6},{5,3},{6,4},{7,1},{8,10},{9,15},{10,... | collective-permute-start | bytes 393224 | tf_op jit(solution)/shard_map/ppermute | solution.py:432
  6.3 10.5 %collective-permute-start.4 = (bf16[128,512]{1,0:T(8,128)(2,1)S(1)}, bf16[128,512]{1,0:T(8,128)(2,1)S(1)}, u32[]{:S(2)}, u32[]{:S(2)}) collective-permute-start(bf16[128,512]{1,0:T(8,128)(2,1)S(1)} %get-tuple-element.51), channel_id=1, source_target_pairs={{0,6},{1,3},{2,4},{3,1},{4,2},{5,7},{6,0},{7,5},{8,14},{9,11},{10,... | collective-permute-start | bytes 393224 | tf_op jit(solution)/shard_map/ppermute | solution.py:432
  8.8 8.1 %collective-permute-start.5 = (bf16[128,256]{1,0:T(8,128)(2,1)S(1)}, bf16[128,256]{1,0:T(8,128)(2,1)S(1)}, u32[]{:S(2)}, u32[]{:S(2)}) collective-permute-start(bf16[128,256]{1,0:T(8,128)(2,1)S(1)} %get-tuple-element.52), channel_id=1, source_target_pairs={{0,4},{1,5},{2,6},{3,7},{4,0},{5,1},{6,2},{7,3},{8,12},{9,13},{10,... | collective-permute-start | bytes 196616 | tf_op jit(solution)/shard_map/ppermute | solution.py:432
  16.9 1.3 %collective-permute-start.6 = (bf16[2,64,256]{2,1,0:T(8,128)(2,1)S(1)}, bf16[2,64,256]{2,1,0:T(8,128)(2,1)S(1)}, u32[]{:S(2)}, u32[]{:S(2)}) collective-permute-start(bf16[2,64,256]{2,1,0:T(8,128)(2,1)S(1)} %get-tuple-element.54), channel_id=1, source_target_pairs={{0,1},{1,0},{2,3},{3,2},{4,5},{5,4},{6,7},{7,6},{8,9},{9,8},{10,11... | collective-permute-start | bytes 196616 | tf_op jit(solution)/shard_map/ppermute | solution.py:421
  18.9 6.4 %collective-permute-start.9 = (bf16[256,512]{1,0:T(8,128)(2,1)S(1)}, bf16[256,512]{1,0:T(8,128)(2,1)S(1)}, u32[]{:S(2)}, u32[]{:S(2)}) collective-permute-start(bf16[256,512]{1,0:T(8,128)(2,1)S(1)} %get-tuple-element.63), channel_id=1, source_target_pairs={{0,8},{1,17},{8,0},{9,25},{16,24},{17,1},{24,16},{25,9},{2,10},{3,... | collective-permute-start | bytes 786440 | tf_op jit(solution)/shard_map/ppermute | solution.py:438
  20.5 6.5 %collective-permute-start.7 = (bf16[256,256]{1,0:T(8,128)(2,1)S(1)}, bf16[256,256]{1,0:T(8,128)(2,1)S(1)}, u32[]{:S(2)}, u32[]{:S(2)}) collective-permute-start(bf16[256,256]{1,0:T(8,128)(2,1)S(1)} %w_rows.1.refs_4_.first), channel_id=1, source_target_pairs={{0,8},{1,17},{8,0},{9,25},{16,24},{17,1},{24,16},{25,9},{2,10},{3,... | collective-permute-start | bytes 393224 | tf_op jit(solution)/shard_map/ppermute | solution.py:438
  25.4 5.0 %collective-permute-start.11 = (bf16[256,256]{1,0:T(8,128)(2,1)S(1)}, bf16[256,256]{1,0:T(8,128)(2,1)S(1)}, u32[]{:S(2)}, u32[]{:S(2)}) collective-permute-start(bf16[256,256]{1,0:T(8,128)(2,1)S(1)} %get-tuple-element.64.refs_0_), channel_id=1, source_target_pairs={{0,16},{1,9},{8,24},{9,1},{16,0},{17,25},{24,8},{25,17},{2,18},{3,... | collective-permute-start | bytes 393224 | tf_op jit(solution)/shard_map/ppermute | solution.py:438
  27.0 6.4 %collective-permute-start.10 = (bf16[256,512]{1,0:T(8,128)(2,1)S(1)}, bf16[256,512]{1,0:T(8,128)(2,1)S(1)}, u32[]{:S(2)}, u32[]{:S(2)}) collective-permute-start(bf16[256,512]{1,0:T(8,128)(2,1)S(1)} %w_half.1.refs_0_), channel_id=1, source_target_pairs={{0,16},{1,9},{8,24},{9,1},{16,0},{17,25},{24,8},{25,17},{2,18},{3,... | collective-permute-start | bytes 786440 | tf_op jit(solution)/shard_map/ppermute | solution.py:438
  30.5 1.4 %collective-permute-start.12 = (f32[128,256]{1,0:T(8,128)S(1)}, f32[128,256]{1,0:T(8,128)S(1)}, u32[]{:S(2)}, u32[]{:S(2)}) collective-permute-start(f32[128,256]{1,0:T(8,128)S(1)} %get-tuple-element.67), channel_id=1, source_target_pairs={{0,1},{1,0},{2,3},{3,2},{4,5},{5,4},{6,7},{7,6},{8,9},{9,8},{10,11... | collective-permute-start | bytes 393224 | tf_op jit(solution)/shard_map/ppermute | solution.py:421
  32.0 4.3 %collective-permute-start.13 = (bf16[128,256]{1,0:T(8,128)(2,1)S(1)}, bf16[128,256]{1,0:T(8,128)(2,1)S(1)}, u32[]{:S(2)}, u32[]{:S(2)}) collective-permute-start(bf16[128,256]{1,0:T(8,128)(2,1)S(1)} %get-tuple-element.82), channel_id=1, source_target_pairs={{0,2},{1,3},{2,0},{3,1},{4,6},{5,7},{6,4},{7,5},{8,10},{9,11},{10,... | collective-permute-start | bytes 196616 | tf_op jit(solution)/shard_map/ppermute | solution.py:432
  36.4 7.7 %collective-permute-start.16 = (bf16[128,256]{1,0:T(8,128)(2,1)S(1)}, bf16[128,256]{1,0:T(8,128)(2,1)S(1)}, u32[]{:S(2)}, u32[]{:S(2)}) collective-permute-start(bf16[128,256]{1,0:T(8,128)(2,1)S(1)} %get-tuple-element.85), channel_id=1, source_target_pairs={{0,4},{1,5},{2,6},{3,7},{4,0},{5,1},{6,2},{7,3},{8,12},{9,13},{10,... | collective-permute-start | bytes 196616 | tf_op jit(solution)/shard_map/ppermute | solution.py:432
  38.3 9.8 %collective-permute-start.14 = (bf16[128,384]{1,0:T(8,128)(2,1)S(1)}, bf16[128,384]{1,0:T(8,128)(2,1)S(1)}, u32[]{:S(2)}, u32[]{:S(2)}) collective-permute-start(bf16[128,384]{1,0:T(8,128)(2,1)S(1)} %get-tuple-element.83), channel_id=1, source_target_pairs={{0,2},{1,7},{2,0},{3,5},{4,6},{5,3},{6,4},{7,1},{8,10},{9,15},{10,... | collective-permute-start | bytes 294920 | tf_op jit(solution)/shard_map/ppermute | solution.py:432
  40.1 7.9 %collective-permute-start.15 = (bf16[128,384]{1,0:T(8,128)(2,1)S(1)}, bf16[128,384]{1,0:T(8,128)(2,1)S(1)}, u32[]{:S(2)}, u32[]{:S(2)}) collective-permute-start(bf16[128,384]{1,0:T(8,128)(2,1)S(1)} %get-tuple-element.84), channel_id=1, source_target_pairs={{0,6},{1,3},{2,4},{3,1},{4,2},{5,7},{6,0},{7,5},{8,14},{9,11},{10,... | collective-permute-start | bytes 294920 | tf_op jit(solution)/shard_map/ppermute | solution.py:432
  44.1 4.0 %collective-permute-start.17 = (bf16[64,256]{1,0:T(8,128)(2,1)S(1)}, bf16[64,256]{1,0:T(8,128)(2,1)S(1)}, u32[]{:S(2)}, u32[]{:S(2)}) collective-permute-start(bf16[64,256]{1,0:T(8,128)(2,1)S(1)} %weight_sum.1.first), channel_id=1, source_target_pairs={{0,8},{1,17},{8,0},{9,25},{16,24},{17,1},{24,16},{25,9},{2,10},{3,... | collective-permute-start | bytes 98312 | tf_op jit(solution)/shard_map/ppermute | solution.py:438
  48.4 1.7 %collective-permute-start.18 = (bf16[128,768]{1,0:T(8,128)(2,1)S(1)}, bf16[128,768]{1,0:T(8,128)(2,1)S(1)}, u32[]{:S(2)}, u32[]{:S(2)}) collective-permute-start(bf16[128,768]{1,0:T(8,128)(2,1)S(1)} %get-tuple-element.88), channel_id=1, source_target_pairs={{0,1},{1,0},{2,3},{3,2},{4,5},{5,4},{6,7},{7,6},{8,9},{9,8},{10,11... | collective-permute-start | bytes 589832 | tf_op jit(solution)/shard_map/ppermute | solution.py:421
  48.5 4.3 %collective-permute-start.19 = (bf16[64,512]{1,0:T(8,128)(2,1)S(1)}, bf16[64,512]{1,0:T(8,128)(2,1)S(1)}, u32[]{:S(2)}, u32[]{:S(2)}) collective-permute-start(bf16[64,512]{1,0:T(8,128)(2,1)S(1)} %both.1.refs_1_), channel_id=1, source_target_pairs={{0,16},{1,9},{8,24},{9,1},{16,0},{17,25},{24,8},{25,17},{2,18},{3,... | collective-permute-start | bytes 196616 | tf_op jit(solution)/shard_map/ppermute | solution.py:438

commit v18 on v13

--- a/solution.py
+++ b/solution.py
@@ -213,8 +213,8 @@
         scores = mm(qs[here, :], ks[window, :], NT) * FACTOR
         scores = jnp.where(inside, scores, -1e30)
         peak = jnp.max(scores, axis=1, keepdims=True)
-        terms = jnp.where(inside, jnp.exp(scores - peak), 0.0)
-        share = terms / jnp.sum(terms, axis=1, keepdims=True)
+        terms = jnp.exp(scores - peak)
+        share = terms * (1.0 / jnp.sum(terms, axis=1, keepdims=True))
         probs[block] = share
         attn[here, :] = mm(share.astype(BF), vs[window, :])
     weight_parts(direct, attn[...], ogs, send[0] if send else None, keep)
@@ -398,12 +398,12 @@
             out[0, :, at(SOFT + first)] = source[:, (3 + index) * DH : (4 + index) * DH]
 
 
-def weight_join_kernel(both, got, _, out):
+def weight_join_kernel(own, near, next_near, far, out):
     _, _, dp = places()
     way = links(True)
-    width = both.shape[1] // 2
-    for source, index, step in ((both, 0, 0), (both, 1, way["step"]), (got, 0, way["other"]), (got, 1, 3)):
-        out[:, at((dp ^ step) * width, width)] = source[:, index * width : (index + 1) * width].astype(F32)
+    width = own.shape[1]
+    for source, step in ((own, 0), (near, way["step"]), (next_near, way["other"]), (far, 3)):
+        out[:, at((dp ^ step) * width, width)] = source[...].astype(F32)
 
 
 def body(n_dp, n_z, queries, key_rows, value_rows, out_grad, out_weight, norm_gain):
@@ -433,7 +433,7 @@
 
     def over_dp(value, which):
         pairs = [
-            (2 * d + c, 2 * (d ^ (1 + c, 2 - c)[which]) + c) for d in range(n_dp) for c in range(2)
+            (2 * d + c, 2 * (d ^ (1 + c, 2 - c, 3)[which]) + c) for d in range(n_dp) for c in range(2)
         ]
         return lax.ppermute(value, ("dp", "core"), pairs)
 
@@ -546,9 +546,10 @@
             functools.partial(weight_sum_kernel, scale), "weight_sum", [like((half, width), BF)],
             [chunk] + c,
         )[0]
-        got = over_dp(summed, 0)
-        both = call(join_kernel, "both", [like((half, 2 * width), BF)], [summed, got])[0]
-        gathered = over_dp(both, 1)
+        gathered = [over_dp(summed, which) for which in range(3)]
+        weight_grad = call(
+            weight_join_kernel, "weight_join", [like((half, model), F32)], [summed] + gathered
+        )[0]
     else:
         to_a, to_b = call(halo_kernel, "halo", [like((rows, 2 * DH), BF)] * 2, [dk_soft, dv_soft])
         a, b = over_z(to_a, 0, True), over_z(to_b, 1, True)
@@ -564,18 +565,13 @@
         functools.partial(final_kernel, direct), "final",
         [like((rows, 6 * DH), BF), like((rows, 6 * DH), BF)],
         [dstate, mine, pair, dq_soft, dk_soft, dv_soft, dq_lin, dq_lin_pair, a, b]
-        + (c + [both] if direct else []),
+        + (c + gathered if direct else []),
         scratch=[pltpu.VMEM((2 * rows, DH), F32)] * 2,
         flops=wg_flops // 4,
     )
     from_pair = over_core(to_pair)
     shape = like((1, rows, HEADS * DH), BF)
     dq, dk, dv = call(output_kernel, "outputs", [shape] * 3, [own_out, from_pair])
-    if direct:
-        weight_grad = call(
-            weight_join_kernel, "weight_join", [like((half, model), F32)], [both, gathered, hbm(dq)],
-            spaces=[vmem, vmem, pl.BlockSpec(memory_space=pltpu.HBM)],
-        )[0]
     return dq, dk, dv, weight_grad
 
 

time: 53.1 us -> 54.5 us (1.026)
  waiting for transfers between devices: 23.7 us -> 24.7 us
    ppermute x7, waiting for transfers between devices: 2.59 us -> 3.28 us  [over_core(): return lax.ppermute(value, 'core', pair_perm)]
    ppermute x6 -> x7, starting transfers between devices: 9.16 us -> 9.51 us  [over_dp(): return lax.ppermute(value, ('dp', 'core'), pairs)]
    ppermute x6 -> x7, waiting for transfers between devices: 9.88 us -> 10.2 us  [over_dp(): return lax.ppermute(value, ('dp', 'core'), pairs)]
    pallas_call x17 -> x16, Pallas kernels: 7.06 us -> 7.07 us  [call(): pl.pallas_call(kernel, name=name, out_shape=list(outs), in_specs=spaces o...]
  transfers between devices with their start and end apart: 20 -> 21, of which waited for: 12 -> 14; matrix products, arithmetic and copies ran while one was open for 0% -> 0% of each run, Pallas kernels for 10% -> 9%
where the time goes in v18:
time: 54.5 us; the launch traced here: 54.4 us
  waiting for transfers between devices  24.7 us (45%)
  starting transfers between devices  21.8 us (40%)
  Pallas kernels  7.07 us (13%)
  between operations  0.78 us (1%)
    ppermute x7, waiting for transfers between devices, over_z(): return lax.ppermute(value, axes, pairs)  11.3 us
    ppermute x7, starting transfers between devices, over_z(): return lax.ppermute(value, axes, pairs)  10.9 us
    ppermute x7, waiting for transfers between devices, over_dp(): return lax.ppermute(value, ('dp', 'core'), pairs)  10.2 us
    ppermute x7, starting transfers between devices, over_dp(): return lax.ppermute(value, ('dp', 'core'), pairs)  9.51 us
    pallas_call x16, Pallas kernels, call(): pl.pallas_call(kernel, name=name, out_shape=list(outs), in_specs=spaces o...  7.07 us
    ppermute x7, waiting for transfers between devices, over_core(): return lax.ppermute(value, 'core', pair_perm)  3.28 us
    ppermute x7, starting transfers between devices, over_core(): return lax.ppermute(value, 'core', pair_perm)  1.32 us
  transfers between devices with their start and end apart: 21, of which 14 were waited for; matrix products, arithmetic and copies ran while one was open for 0% of the time, Pallas kernels for 9%

profile of v18, /device:TPU:0, one launch (start us, length us, event | category | flops | bytes accessed | tf_op | source)
XLA Modules:
  0.0 54.4 jit_solution(7033775740340310868)
XLA Ops:
  0.6 0.5 collective-permute-start
  1.2 0.1 collective-permute-start.1
  1.2 0.4 collective-permute-start.2
  1.7 0.1 collective-permute-start.8
  1.7 1.2 %pack.1 = (bf16[128,768]{1,0:T(8,128)(2,1)S(1)}, bf16[128,1024]{1,0:T(8,128)(2,1)S(1)}, bf16[64,256]{1,0:T(8,128)(2,1)S(1)}, f32[1,128]{1,0:T(1,128)S(1)}) custom-call(bf16[1,128,512]{2,1,0:T(8,128)(2,1)} %q.1, bf16[1,128,512]{2,1,0:T(8,128)(2,1)} %k.1, bf16[1,128,512]{2,1,0:T(8,128)(2,1)} %v.1, bf16[1,128,1024]{2,1,0:T(8,128)(2,1)} %og.1, ...), custom_call_target="tpu_custom_call" | custom-call | bytes 1279488 | tf_op jit(solution)/shard_map/pack/pallas_call | solution.py:66
  2.9 0.0 collective-permute-done.q_pair
  2.9 0.0 collective-permute-done.1.k_pair
  2.9 0.0 collective-permute-done.2.v_pair
  3.0 0.3 state.1
  3.2 3.1 %collective-permute-start.3 = (bf16[128,512]{1,0:T(8,128)(2,1)S(1)}, bf16[128,512]{1,0:T(8,128)(2,1)S(1)}, u32[]{:S(2)}, u32[]{:S(2)}) collective-permute-start(bf16[128,512]{1,0:T(8,128)(2,1)S(1)} %get-tuple-element.50), channel_id=1, source_target_pairs={{0,2},{1,7},{2,0},{3,5},{4,6},{5,3},{6,4},{7,1},{8,10},{9,15},{10,... | collective-permute-start | bytes 393224 | tf_op jit(solution)/shard_map/ppermute | solution.py:432
  6.3 2.5 %collective-permute-start.4 = (bf16[128,512]{1,0:T(8,128)(2,1)S(1)}, bf16[128,512]{1,0:T(8,128)(2,1)S(1)}, u32[]{:S(2)}, u32[]{:S(2)}) collective-permute-start(bf16[128,512]{1,0:T(8,128)(2,1)S(1)} %get-tuple-element.51), channel_id=1, source_target_pairs={{0,6},{1,3},{2,4},{3,1},{4,2},{5,7},{6,0},{7,5},{8,14},{9,11},{10,... | collective-permute-start | bytes 393224 | tf_op jit(solution)/shard_map/ppermute | solution.py:432
  8.8 0.1 collective-permute-start.5
  8.9 0.4 collective-permute-done.3.a.refs_0_
  9.3 6.5 %collective-permute-done.4.b.refs_1_ = bf16[128,512]{1,0:T(8,128)(2,1)S(1)} collective-permute-done((bf16[128,512]{1,0:T(8,128)(2,1)S(1)}, bf16[128,512]{1,0:T(8,128)(2,1)S(1)}, u32[]{:S(2)}, u32[]{:S(2)}) %collective-permute-start.4) | collective-permute-done | bytes 131104 | tf_op jit(solution)/shard_map/ppermute | solution.py:432
  15.7 0.0 collective-permute-done.8.og_recv
  15.7 1.2 %soft_forward.1 = (bf16[256,128]{1,0:T(8,128)(2,1)S(1)}, bf16[512,128]{1,0:T(8,128)(2,1)S(1)}, bf16[512,128]{1,0:T(8,128)(2,1)S(1)}, bf16[256,1024]{1,0:T(8,128)...) custom-call(bf16[128,768]{1,0:T(8,128)(2,1)S(1)} %get-tuple-element., ...), custom_call_target="tpu_custom_call" | custom-call | flops 67108864 | bytes 2949120 | tf_op jit(solution)/shard_map/soft_forward/pallas_call | solution.py:66
  16.9 0.0 collective-permute-done.5.c.refs_2_
  17.0 0.7 %lin_forward.1 = (f32[256,128]{1,0:T(8,128)S(1)}, f32[128,128]{1,0:T(8,128)S(1)}, f32[128,512]{1,0:T(8,128)S(1)}, bf16[256,512]{1,0:T(8,128)(2,1)S(1)}) custom-call(f32[128,128]{1,0:T(8,128)S(1)} %get-tuple-element.58.state, bf16[128,768]{1,0:T(8,128)(2,1)S(1)} %get-tuple-element.49.mine.refs_6_, bf16[128,768]{1,0:T(8,128)(2,1)S(1)} %get-tuple-element.55.pair.refs_7_, ...), custom_call_target="tpu_custom_call" | custom-call | flops 67108864 | bytes 2163200 | tf_op jit(solution)/shard_map/lin_forward/pallas_call | solution.py:66
  17.7 1.6 %collective-permute-start.9 = (bf16[256,512]{1,0:T(8,128)(2,1)S(1)}, bf16[256,512]{1,0:T(8,128)(2,1)S(1)}, u32[]{:S(2)}, u32[]{:S(2)}) collective-permute-start(bf16[256,512]{1,0:T(8,128)(2,1)S(1)} %get-tuple-element.63), channel_id=1, source_target_pairs={{0,8},{1,17},{8,0},{9,25},{16,24},{17,1},{24,16},{25,9},{2,10},{3,... | collective-permute-start | bytes 786440 | tf_op jit(solution)/shard_map/ppermute | solution.py:438
  19.2 0.1 collective-permute-start.6
  19.3 1.2 %collective-permute-done.6.got = bf16[2,64,256]{2,1,0:T(8,128)(2,1)S(1)} collective-permute-done((bf16[2,64,256]{2,1,0:T(8,128)(2,1)S(1)}, bf16[2,64,256]{2,1,0:T(8,128)(2,1)S(1)}, u32[]{:S(2)}, u32[]{:S(2)}) %collective-permute-start.6) | collective-permute-done | bytes 65568 | tf_op jit(solution)/shard_map/ppermute | solution.py:421
  20.6 0.6 %collective-permute-start.7 = (bf16[256,256]{1,0:T(8,128)(2,1)S(1)}, bf16[256,256]{1,0:T(8,128)(2,1)S(1)}, u32[]{:S(2)}, u32[]{:S(2)}) collective-permute-start(bf16[256,256]{1,0:T(8,128)(2,1)S(1)} %w_rows.1.first), channel_id=1, source_target_pairs={{0,8},{1,17},{8,0},{9,25},{16,24},{17,1},{24,16},{25,9},{2,10},{3,... | collective-permute-start | bytes 393224 | tf_op jit(solution)/shard_map/ppermute | solution.py:438
  21.2 2.9 %collective-permute-done.9.got = bf16[256,512]{1,0:T(8,128)(2,1)S(1)} collective-permute-done((bf16[256,512]{1,0:T(8,128)(2,1)S(1)}, bf16[256,512]{1,0:T(8,128)(2,1)S(1)}, u32[]{:S(2)}, u32[]{:S(2)}) %collective-permute-start.9) | collective-permute-done | bytes 262176 | tf_op jit(solution)/shard_map/ppermute | solution.py:438
  24.1 0.1 fold.1
  24.1 1.9 %collective-permute-start.11 = (bf16[256,256]{1,0:T(8,128)(2,1)S(1)}, bf16[256,256]{1,0:T(8,128)(2,1)S(1)}, u32[]{:S(2)}, u32[]{:S(2)}) collective-permute-start(bf16[256,256]{1,0:T(8,128)(2,1)S(1)} %get-tuple-element.64.refs_0_), channel_id=1, source_target_pairs={{0,16},{1,9},{8,24},{9,1},{16,0},{17,25},{24,8},{25,17},{2,18},{3,... | collective-permute-start | bytes 393224 | tf_op jit(solution)/shard_map/ppermute | solution.py:438
  26.0 0.5 collective-permute-done.7.second
  26.6 1.9 %collective-permute-start.10 = (bf16[256,512]{1,0:T(8,128)(2,1)S(1)}, bf16[256,512]{1,0:T(8,128)(2,1)S(1)}, u32[]{:S(2)}, u32[]{:S(2)}) collective-permute-start(bf16[256,512]{1,0:T(8,128)(2,1)S(1)} %w_half.1.refs_0_), channel_id=1, source_target_pairs={{0,16},{1,9},{8,24},{9,1},{16,0},{17,25},{24,8},{25,17},{2,18},{3,... | collective-permute-start | bytes 786440 | tf_op jit(solution)/shard_map/ppermute | solution.py:438
  28.5 0.7 %collective-permute-done.11.got = bf16[256,256]{1,0:T(8,128)(2,1)S(1)} collective-permute-done((bf16[256,256]{1,0:T(8,128)(2,1)S(1)}, bf16[256,256]{1,0:T(8,128)(2,1)S(1)}, u32[]{:S(2)}, u32[]{:S(2)}) %collective-permute-start.11) | collective-permute-done | bytes 131104 | tf_op jit(solution)/shard_map/ppermute | solution.py:438
  29.2 0.1 rows.1
  29.2 0.1 collective-permute-start.12
  29.3 1.3 %collective-permute-done.12.got = f32[128,256]{1,0:T(8,128)S(1)} collective-permute-done((f32[128,256]{1,0:T(8,128)S(1)}, f32[128,256]{1,0:T(8,128)S(1)}, u32[]{:S(2)}, u32[]{:S(2)}) %collective-permute-start.12) | collective-permute-done | bytes 131104 | tf_op jit(solution)/shard_map/ppermute | solution.py:421
  30.7 0.8 %collective-permute-start.13 = (bf16[128,256]{1,0:T(8,128)(2,1)S(1)}, bf16[128,256]{1,0:T(8,128)(2,1)S(1)}, u32[]{:S(2)}, u32[]{:S(2)}) collective-permute-start(bf16[128,256]{1,0:T(8,128)(2,1)S(1)} %get-tuple-element.82), channel_id=1, source_target_pairs={{0,2},{1,7},{2,0},{3,5},{4,6},{5,3},{6,4},{7,1},{8,10},{9,15},{10,... | collective-permute-start | bytes 196616 | tf_op jit(solution)/shard_map/ppermute | solution.py:432
  31.5 1.5 %collective-permute-done.10.refs_1_ = bf16[256,512]{1,0:T(8,128)(2,1)S(1)} collective-permute-done((bf16[256,512]{1,0:T(8,128)(2,1)S(1)}, bf16[256,512]{1,0:T(8,128)(2,1)S(1)}, u32[]{:S(2)}, u32[]{:S(2)}) %collective-permute-start.10) | collective-permute-done | bytes 262176 | tf_op jit(solution)/shard_map/ppermute | solution.py:438
  33.0 1.5 %backward.1 = (bf16[128,128]{1,0:T(8,128)(2,1)S(1)}, bf16[128,128]{1,0:T(8,128)(2,1)S(1)}, f32[128,128]{1,0:T(8,128)S(1)}, f32[256,128]{1,0:T(8,128)S(1)}, f32[5...) custom-call(bf16[256,512]{1,0:T(8,128)(2,1)S(1)} %w_half.1.refs_0_, bf16[256,512]{1,0:T(8,128)(2,1)S(1)} %collective-permute-done.10.refs_1_, ...), custom_call_target="tpu_custom_call" | custom-call | flops 335544320 | bytes 3408384 | tf_op jit(solution)/shard_map/backward/pallas_call | solution.py:66
  34.5 0.5 collective-permute-done.13.got
  35.1 2.7 %collective-permute-start.16 = (bf16[128,256]{1,0:T(8,128)(2,1)S(1)}, bf16[128,256]{1,0:T(8,128)(2,1)S(1)}, u32[]{:S(2)}, u32[]{:S(2)}) collective-permute-start(bf16[128,256]{1,0:T(8,128)(2,1)S(1)} %get-tuple-element.85), channel_id=1, source_target_pairs={{0,4},{1,5},{2,6},{3,7},{4,0},{5,1},{6,2},{7,3},{8,12},{9,13},{10,... | collective-permute-start | bytes 196616 | tf_op jit(solution)/shard_map/ppermute | solution.py:432
  37.8 0.9 %collective-permute-start.14 = (bf16[128,384]{1,0:T(8,128)(2,1)S(1)}, bf16[128,384]{1,0:T(8,128)(2,1)S(1)}, u32[]{:S(2)}, u32[]{:S(2)}) collective-permute-start(bf16[128,384]{1,0:T(8,128)(2,1)S(1)} %get-tuple-element.83), channel_id=1, source_target_pairs={{0,2},{1,7},{2,0},{3,5},{4,6},{5,3},{6,4},{7,1},{8,10},{9,15},{10,... | collective-permute-start | bytes 294920 | tf_op jit(solution)/shard_map/ppermute | solution.py:432
  38.7 0.8 %collective-permute-start.15 = (bf16[128,384]{1,0:T(8,128)(2,1)S(1)}, bf16[128,384]{1,0:T(8,128)(2,1)S(1)}, u32[]{:S(2)}, u32[]{:S(2)}) collective-permute-start(bf16[128,384]{1,0:T(8,128)(2,1)S(1)} %get-tuple-element.84), channel_id=1, source_target_pairs={{0,6},{1,3},{2,4},{3,1},{4,2},{5,7},{6,0},{7,5},{8,14},{9,11},{10,... | collective-permute-start | bytes 294920 | tf_op jit(solution)/shard_map/ppermute | solution.py:432
  39.5 3.9 %collective-permute-done.16.got.refs_0_ = bf16[128,256]{1,0:T(8,128)(2,1)S(1)} collective-permute-done((bf16[128,256]{1,0:T(8,128)(2,1)S(1)}, bf16[128,256]{1,0:T(8,128)(2,1)S(1)}, u32[]{:S(2)}, u32[]{:S(2)}) %collective-permute-start.16) | collective-permute-done | bytes 65568 | tf_op jit(solution)/shard_map/ppermute | solution.py:432
  43.5 1.3 %collective-permute-start.17 = (bf16[64,256]{1,0:T(8,128)(2,1)S(1)}, bf16[64,256]{1,0:T(8,128)(2,1)S(1)}, u32[]{:S(2)}, u32[]{:S(2)}) collective-permute-start(bf16[64,256]{1,0:T(8,128)(2,1)S(1)} %weight_sum.1.own), channel_id=1, source_target_pairs={{0,8},{1,17},{8,0},{9,25},{16,24},{17,1},{24,16},{25,9},{2,10},{3,... | collective-permute-start | bytes 98312 | tf_op jit(solution)/shard_map/ppermute | solution.py:438
  44.8 2.0 %collective-permute-start.18 = (bf16[64,256]{1,0:T(8,128)(2,1)S(1)}, bf16[64,256]{1,0:T(8,128)(2,1)S(1)}, u32[]{:S(2)}, u32[]{:S(2)}) collective-permute-start(bf16[64,256]{1,0:T(8,128)(2,1)S(1)} %weight_sum.1.own), channel_id=1, source_target_pairs={{0,16},{1,9},{8,24},{9,1},{16,0},{17,25},{24,8},{25,17},{2,18},{3,... | collective-permute-start | bytes 98312 | tf_op jit(solution)/shard_map/ppermute | solution.py:438
  46.8 0.2 collective-permute-start.19
  47.0 0.5 collective-permute-done.17.refs_1_.near
  47.5 1.2 %collective-permute-done.18.refs_2_.next_near = bf16[64,256]{1,0:T(8,128)(2,1)S(1)} collective-permute-done((bf16[64,256]{1,0:T(8,128)(2,1)S(1)}, bf16[64,256]{1,0:T(8,128)(2,1)S(1)}, u32[]{:S(2)}, u32[]{:S(2)}) %collective-permute-start.18) | collective-permute-done | bytes 32800 | tf_op jit(solution)/shard_map/ppermute | solution.py:438
  48.7 2.9 %collective-permute-done.19.refs_3_.far = bf16[64,256]{1,0:T(8,128)(2,1)S(1)} collective-permute-done((bf16[64,256]{1,0:T(8,128)(2,1)S(1)}, bf16[64,256]{1,0:T(8,128)(2,1)S(1)}, u32[]{:S(2)}, u32[]{:S(2)}) %collective-permute-start.19) | collective-permute-done | bytes 32800 | tf_op jit(solution)/shard_map/ppermute | solution.py:438
  51.7 0.0 collective-permute-done.14.a
  51.7 0.0 collective-permute-done.15.b
  51.7 0.4 final.1
  52.0 0.1 collective-permute-start.20
  52.1 0.7 %weight_join.1 = f32[64,1024]{1,0:T(8,128)} custom-call(bf16[64,256]{1,0:T(8,128)(2,1)S(1)} %weight_sum.1.own, bf16[64,256]{1,0:T(8,128)(2,1)S(1)} %collective-permute-done.17.refs_1_.near, bf16[64,256]{1,0:T(8,128)(2,1)S(1)} %collective-permute-done.18.refs_2_.next_near, bf16[64,256]{1,0:T(8,128)(2,1)S(1)} %collective-permute-done.19.refs_3_.far), custom_call_target="tpu_custom_call" | custom-call | bytes 393216 | tf_op jit(solution)/shard_map/weight_join/pallas_call | solution.py:66
  52.8 0.7 %collective-permute-done.20.pair = bf16[128,768]{1,0:T(8,128)(2,1)S(1)} collective-permute-done((bf16[128,768]{1,0:T(8,128)(2,1)S(1)}, bf16[128,768]{1,0:T(8,128)(2,1)S(1)}, u32[]{:S(2)}, u32[]{:S(2)}) %collective-permute-start.20) | collective-permute-done | bytes 196640 | tf_op jit(solution)/shard_map/ppermute | solution.py:421
  53.5 0.8 %outputs.1 = (bf16[1,128,512]{2,1,0:T(8,128)(2,1)}, bf16[1,128,512]{2,1,0:T(8,128)(2,1)}, bf16[1,128,512]{2,1,0:T(8,128)(2,1)}) custom-call(bf16[128,768]{1,0:T(8,128)(2,1)S(1)} %get-tuple-element.87.own, bf16[128,768]{1,0:T(8,128)(2,1)S(1)} %collective-permute-done.20.pair), custom_call_target="tpu_custom_call" | custom-call | bytes 786432 | tf_op jit(solution)/shard_map/outputs/pallas_call | solution.py:66
  (6 shorter events, 0.2 us)
Async XLA Ops:
  0.6 2.3 %collective-permute-start = (bf16[1,128,512]{2,1,0:T(8,128)(2,1)}, bf16[1,128,512]{2,1,0:T(8,128)(2,1)S(1)}, u32[]{:S(2)}, u32[]{:S(2)}) collective-permute-start(bf16[1,128,512]{2,1,0:T(8,128)(2,1)} %q.1), channel_id=1, source_target_pairs={{0,1},{1,0},{2,3},{3,2},{4,5},{5,4},{6,7},{7,6},{8,9},{9,8},{10,11... | collective-permute-start | bytes 393224 | tf_op jit(solution)/shard_map/ppermute | solution.py:421
  1.2 1.8 %collective-permute-start.1 = (bf16[1,128,512]{2,1,0:T(8,128)(2,1)}, bf16[1,128,512]{2,1,0:T(8,128)(2,1)S(1)}, u32[]{:S(2)}, u32[]{:S(2)}) collective-permute-start(bf16[1,128,512]{2,1,0:T(8,128)(2,1)} %k.1), channel_id=1, source_target_pairs={{0,1},{1,0},{2,3},{3,2},{4,5},{5,4},{6,7},{7,6},{8,9},{9,8},{10,11... | collective-permute-start | bytes 393224 | tf_op jit(solution)/shard_map/ppermute | solution.py:421
  1.2 1.7 %collective-permute-start.2 = (bf16[1,128,512]{2,1,0:T(8,128)(2,1)}, bf16[1,128,512]{2,1,0:T(8,128)(2,1)S(1)}, u32[]{:S(2)}, u32[]{:S(2)}) collective-permute-start(bf16[1,128,512]{2,1,0:T(8,128)(2,1)} %v.1), channel_id=1, source_target_pairs={{0,1},{1,0},{2,3},{3,2},{4,5},{5,4},{6,7},{7,6},{8,9},{9,8},{10,11... | collective-permute-start | bytes 393224 | tf_op jit(solution)/shard_map/ppermute | solution.py:421
  1.7 14.1 %collective-permute-start.8 = (bf16[128,1024]{1,0:T(8,128)(2,1)}, bf16[128,1024]{1,0:T(8,128)(2,1)S(1)}, u32[]{:S(2)}, u32[]{:S(2)}) collective-permute-start(bf16[128,1024]{1,0:T(8,128)(2,1)} %bitcast.1), channel_id=1, source_target_pairs={{0,1},{1,0},{2,3},{3,2},{4,5},{5,4},{6,7},{7,6},{8,9},{9,8},{10,11... | collective-permute-start | bytes 786440 | tf_op jit(solution)/shard_map/ppermute | solution.py:421
  3.2 6.0 %collective-permute-start.3 = (bf16[128,512]{1,0:T(8,128)(2,1)S(1)}, bf16[128,512]{1,0:T(8,128)(2,1)S(1)}, u32[]{:S(2)}, u32[]{:S(2)}) collective-permute-start(bf16[128,512]{1,0:T(8,128)(2,1)S(1)} %get-tuple-element.50), channel_id=1, source_target_pairs={{0,2},{1,7},{2,0},{3,5},{4,6},{5,3},{6,4},{7,1},{8,10},{9,15},{10,... | collective-permute-start | bytes 393224 | tf_op jit(solution)/shard_map/ppermute | solution.py:432
  6.3 9.4 %collective-permute-start.4 = (bf16[128,512]{1,0:T(8,128)(2,1)S(1)}, bf16[128,512]{1,0:T(8,128)(2,1)S(1)}, u32[]{:S(2)}, u32[]{:S(2)}) collective-permute-start(bf16[128,512]{1,0:T(8,128)(2,1)S(1)} %get-tuple-element.51), channel_id=1, source_target_pairs={{0,6},{1,3},{2,4},{3,1},{4,2},{5,7},{6,0},{7,5},{8,14},{9,11},{10,... | collective-permute-start | bytes 393224 | tf_op jit(solution)/shard_map/ppermute | solution.py:432
  8.8 8.2 %collective-permute-start.5 = (bf16[128,256]{1,0:T(8,128)(2,1)S(1)}, bf16[128,256]{1,0:T(8,128)(2,1)S(1)}, u32[]{:S(2)}, u32[]{:S(2)}) collective-permute-start(bf16[128,256]{1,0:T(8,128)(2,1)S(1)} %get-tuple-element.52), channel_id=1, source_target_pairs={{0,4},{1,5},{2,6},{3,7},{4,0},{5,1},{6,2},{7,3},{8,12},{9,13},{10,... | collective-permute-start | bytes 196616 | tf_op jit(solution)/shard_map/ppermute | solution.py:432
  17.7 6.4 %collective-permute-start.9 = (bf16[256,512]{1,0:T(8,128)(2,1)S(1)}, bf16[256,512]{1,0:T(8,128)(2,1)S(1)}, u32[]{:S(2)}, u32[]{:S(2)}) collective-permute-start(bf16[256,512]{1,0:T(8,128)(2,1)S(1)} %get-tuple-element.63), channel_id=1, source_target_pairs={{0,8},{1,17},{8,0},{9,25},{16,24},{17,1},{24,16},{25,9},{2,10},{3,... | collective-permute-start | bytes 786440 | tf_op jit(solution)/shard_map/ppermute | solution.py:438
  19.2 1.3 %collective-permute-start.6 = (bf16[2,64,256]{2,1,0:T(8,128)(2,1)S(1)}, bf16[2,64,256]{2,1,0:T(8,128)(2,1)S(1)}, u32[]{:S(2)}, u32[]{:S(2)}) collective-permute-start(bf16[2,64,256]{2,1,0:T(8,128)(2,1)S(1)} %get-tuple-element.54), channel_id=1, source_target_pairs={{0,1},{1,0},{2,3},{3,2},{4,5},{5,4},{6,7},{7,6},{8,9},{9,8},{10,11... | collective-permute-start | bytes 196616 | tf_op jit(solution)/shard_map/ppermute | solution.py:421
  20.6 6.0 %collective-permute-start.7 = (bf16[256,256]{1,0:T(8,128)(2,1)S(1)}, bf16[256,256]{1,0:T(8,128)(2,1)S(1)}, u32[]{:S(2)}, u32[]{:S(2)}) collective-permute-start(bf16[256,256]{1,0:T(8,128)(2,1)S(1)} %w_rows.1.first), channel_id=1, source_target_pairs={{0,8},{1,17},{8,0},{9,25},{16,24},{17,1},{24,16},{25,9},{2,10},{3,... | collective-permute-start | bytes 393224 | tf_op jit(solution)/shard_map/ppermute | solution.py:438
  24.1 5.0 %collective-permute-start.11 = (bf16[256,256]{1,0:T(8,128)(2,1)S(1)}, bf16[256,256]{1,0:T(8,128)(2,1)S(1)}, u32[]{:S(2)}, u32[]{:S(2)}) collective-permute-start(bf16[256,256]{1,0:T(8,128)(2,1)S(1)} %get-tuple-element.64.refs_0_), channel_id=1, source_target_pairs={{0,16},{1,9},{8,24},{9,1},{16,0},{17,25},{24,8},{25,17},{2,18},{3,... | collective-permute-start | bytes 393224 | tf_op jit(solution)/shard_map/ppermute | solution.py:438
  26.6 6.4 %collective-permute-start.10 = (bf16[256,512]{1,0:T(8,128)(2,1)S(1)}, bf16[256,512]{1,0:T(8,128)(2,1)S(1)}, u32[]{:S(2)}, u32[]{:S(2)}) collective-permute-start(bf16[256,512]{1,0:T(8,128)(2,1)S(1)} %w_half.1.refs_0_), channel_id=1, source_target_pairs={{0,16},{1,9},{8,24},{9,1},{16,0},{17,25},{24,8},{25,17},{2,18},{3,... | collective-permute-start | bytes 786440 | tf_op jit(solution)/shard_map/ppermute | solution.py:438
  29.2 1.4 %collective-permute-start.12 = (f32[128,256]{1,0:T(8,128)S(1)}, f32[128,256]{1,0:T(8,128)S(1)}, u32[]{:S(2)}, u32[]{:S(2)}) collective-permute-start(f32[128,256]{1,0:T(8,128)S(1)} %get-tuple-element.67), channel_id=1, source_target_pairs={{0,1},{1,0},{2,3},{3,2},{4,5},{5,4},{6,7},{7,6},{8,9},{9,8},{10,11... | collective-permute-start | bytes 393224 | tf_op jit(solution)/shard_map/ppermute | solution.py:421
  30.7 4.3 %collective-permute-start.13 = (bf16[128,256]{1,0:T(8,128)(2,1)S(1)}, bf16[128,256]{1,0:T(8,128)(2,1)S(1)}, u32[]{:S(2)}, u32[]{:S(2)}) collective-permute-start(bf16[128,256]{1,0:T(8,128)(2,1)S(1)} %get-tuple-element.82), channel_id=1, source_target_pairs={{0,2},{1,7},{2,0},{3,5},{4,6},{5,3},{6,4},{7,1},{8,10},{9,15},{10,... | collective-permute-start | bytes 196616 | tf_op jit(solution)/shard_map/ppermute | solution.py:432
  35.1 8.4 %collective-permute-start.16 = (bf16[128,256]{1,0:T(8,128)(2,1)S(1)}, bf16[128,256]{1,0:T(8,128)(2,1)S(1)}, u32[]{:S(2)}, u32[]{:S(2)}) collective-permute-start(bf16[128,256]{1,0:T(8,128)(2,1)S(1)} %get-tuple-element.85), channel_id=1, source_target_pairs={{0,4},{1,5},{2,6},{3,7},{4,0},{5,1},{6,2},{7,3},{8,12},{9,13},{10,... | collective-permute-start | bytes 196616 | tf_op jit(solution)/shard_map/ppermute | solution.py:432
  37.8 13.9 %collective-permute-start.14 = (bf16[128,384]{1,0:T(8,128)(2,1)S(1)}, bf16[128,384]{1,0:T(8,128)(2,1)S(1)}, u32[]{:S(2)}, u32[]{:S(2)}) collective-permute-start(bf16[128,384]{1,0:T(8,128)(2,1)S(1)} %get-tuple-element.83), channel_id=1, source_target_pairs={{0,2},{1,7},{2,0},{3,5},{4,6},{5,3},{6,4},{7,1},{8,10},{9,15},{10,... | collective-permute-start | bytes 294920 | tf_op jit(solution)/shard_map/ppermute | solution.py:432
  38.7 12.9 %collective-permute-start.15 = (bf16[128,384]{1,0:T(8,128)(2,1)S(1)}, bf16[128,384]{1,0:T(8,128)(2,1)S(1)}, u32[]{:S(2)}, u32[]{:S(2)}) collective-permute-start(bf16[128,384]{1,0:T(8,128)(2,1)S(1)} %get-tuple-element.84), channel_id=1, source_target_pairs={{0,6},{1,3},{2,4},{3,1},{4,2},{5,7},{6,0},{7,5},{8,14},{9,11},{10,... | collective-permute-start | bytes 294920 | tf_op jit(solution)/shard_map/ppermute | solution.py:432
  43.5 4.1 %collective-permute-start.17 = (bf16[64,256]{1,0:T(8,128)(2,1)S(1)}, bf16[64,256]{1,0:T(8,128)(2,1)S(1)}, u32[]{:S(2)}, u32[]{:S(2)}) collective-permute-start(bf16[64,256]{1,0:T(8,128)(2,1)S(1)} %weight_sum.1.own), channel_id=1, source_target_pairs={{0,8},{1,17},{8,0},{9,25},{16,24},{17,1},{24,16},{25,9},{2,10},{3,... | collective-permute-start | bytes 98312 | tf_op jit(solution)/shard_map/ppermute | solution.py:438
  44.8 3.9 %collective-permute-start.18 = (bf16[64,256]{1,0:T(8,128)(2,1)S(1)}, bf16[64,256]{1,0:T(8,128)(2,1)S(1)}, u32[]{:S(2)}, u32[]{:S(2)}) collective-permute-start(bf16[64,256]{1,0:T(8,128)(2,1)S(1)} %weight_sum.1.own), channel_id=1, source_target_pairs={{0,16},{1,9},{8,24},{9,1},{16,0},{17,25},{24,8},{25,17},{2,18},{3,... | collective-permute-start | bytes 98312 | tf_op jit(solution)/shard_map/ppermute | solution.py:438
  46.8 4.8 %collective-permute-start.19 = (bf16[64,256]{1,0:T(8,128)(2,1)S(1)}, bf16[64,256]{1,0:T(8,128)(2,1)S(1)}, u32[]{:S(2)}, u32[]{:S(2)}) collective-permute-start(bf16[64,256]{1,0:T(8,128)(2,1)S(1)} %weight_sum.1.own), channel_id=1, source_target_pairs={{0,24},{1,25},{8,16},{9,17},{16,8},{17,9},{24,0},{25,1},{2,26},{3,... | collective-permute-start | bytes 98312 | tf_op jit(solution)/shard_map/ppermute | solution.py:438
  52.0 1.5 %collective-permute-start.20 = (bf16[128,768]{1,0:T(8,128)(2,1)S(1)}, bf16[128,768]{1,0:T(8,128)(2,1)S(1)}, u32[]{:S(2)}, u32[]{:S(2)}) collective-permute-start(bf16[128,768]{1,0:T(8,128)(2,1)S(1)} %get-tuple-element.88), channel_id=1, source_target_pairs={{0,1},{1,0},{2,3},{3,2},{4,5},{5,4},{6,7},{7,6},{8,9},{9,8},{10,11... | collective-permute-start | bytes 589832 | tf_op jit(solution)/shard_map/ppermute | solution.py:421

commit v19 on v18

--- a/solution.py
+++ b/solution.py
@@ -398,7 +398,7 @@
             out[0, :, at(SOFT + first)] = source[:, (3 + index) * DH : (4 + index) * DH]
 
 
-def weight_join_kernel(own, near, next_near, far, out):
+def weight_join_kernel(own, far, near, next_near, out):
     _, _, dp = places()
     way = links(True)
     width = own.shape[1]
@@ -546,7 +546,7 @@
             functools.partial(weight_sum_kernel, scale), "weight_sum", [like((half, width), BF)],
             [chunk] + c,
         )[0]
-        gathered = [over_dp(summed, which) for which in range(3)]
+        gathered = [over_dp(summed, which) for which in (2, 0, 1)]
         weight_grad = call(
             weight_join_kernel, "weight_join", [like((half, model), F32)], [summed] + gathered
         )[0]

time: 54.5 us -> 53.6 us (0.983)
  waiting for transfers between devices: 24.7 us -> 23.8 us
    ppermute x7, waiting for transfers between devices: 10.2 us -> 9.27 us  [over_dp(): return lax.ppermute(value, ('dp', 'core'), pairs)]
  transfers between devices with their start and end apart: 21 -> 21, of which waited for: 14 -> 14; matrix products, arithmetic and copies ran while one was open for 0% -> 0% of each run, Pallas kernels for 9% -> 10%
where the time goes in v19:
time: 53.6 us; the launch traced here: 53.4 us
  waiting for transfers between devices  23.8 us (44%)
  starting transfers between devices  21.8 us (41%)
  Pallas kernels  7.07 us (13%)
  between operations  0.78 us (1%)
    ppermute x7, waiting for transfers between devices, over_z(): return lax.ppermute(value, axes, pairs)  11.3 us
    ppermute x7, starting transfers between devices, over_z(): return lax.ppermute(value, axes, pairs)  10.9 us
    ppermute x7, starting transfers between devices, over_dp(): return lax.ppermute(value, ('dp', 'core'), pairs)  9.51 us
    ppermute x7, waiting for transfers between devices, over_dp(): return lax.ppermute(value, ('dp', 'core'), pairs)  9.27 us
    pallas_call x16, Pallas kernels, call(): pl.pallas_call(kernel, name=name, out_shape=list(outs), in_specs=spaces o...  7.07 us
    ppermute x7, waiting for transfers between devices, over_core(): return lax.ppermute(value, 'core', pair_perm)  3.28 us
    ppermute x7, starting transfers between devices, over_core(): return lax.ppermute(value, 'core', pair_perm)  1.32 us
  transfers between devices with their start and end apart: 21, of which 14 were waited for; matrix products, arithmetic and copies ran while one was open for 0% of the time, Pallas kernels for 10%

profile of v19, /device:TPU:0, one launch (start us, length us, event | category | flops | bytes accessed | tf_op | source)
XLA Modules:
  0.0 53.4 jit_solution(7391931124155346366)
XLA Ops:
  0.6 0.5 collective-permute-start
  1.2 0.1 collective-permute-start.1
  1.2 0.4 collective-permute-start.2
  1.7 0.1 collective-permute-start.8
  1.7 1.2 %pack.1 = (bf16[128,768]{1,0:T(8,128)(2,1)S(1)}, bf16[128,1024]{1,0:T(8,128)(2,1)S(1)}, bf16[64,256]{1,0:T(8,128)(2,1)S(1)}, f32[1,128]{1,0:T(1,128)S(1)}) custom-call(bf16[1,128,512]{2,1,0:T(8,128)(2,1)} %q.1, bf16[1,128,512]{2,1,0:T(8,128)(2,1)} %k.1, bf16[1,128,512]{2,1,0:T(8,128)(2,1)} %v.1, bf16[1,128,1024]{2,1,0:T(8,128)(2,1)} %og.1, ...), custom_call_target="tpu_custom_call" | custom-call | bytes 1279488 | tf_op jit(solution)/shard_map/pack/pallas_call | solution.py:66
  2.9 0.0 collective-permute-done.q_pair
  2.9 0.0 collective-permute-done.1.k_pair
  2.9 0.0 collective-permute-done.2.v_pair
  3.0 0.3 state.1
  3.2 3.1 %collective-permute-start.3 = (bf16[128,512]{1,0:T(8,128)(2,1)S(1)}, bf16[128,512]{1,0:T(8,128)(2,1)S(1)}, u32[]{:S(2)}, u32[]{:S(2)}) collective-permute-start(bf16[128,512]{1,0:T(8,128)(2,1)S(1)} %get-tuple-element.50), channel_id=1, source_target_pairs={{0,2},{1,7},{2,0},{3,5},{4,6},{5,3},{6,4},{7,1},{8,10},{9,15},{10,... | collective-permute-start | bytes 393224 | tf_op jit(solution)/shard_map/ppermute | solution.py:432
  6.3 2.5 %collective-permute-start.4 = (bf16[128,512]{1,0:T(8,128)(2,1)S(1)}, bf16[128,512]{1,0:T(8,128)(2,1)S(1)}, u32[]{:S(2)}, u32[]{:S(2)}) collective-permute-start(bf16[128,512]{1,0:T(8,128)(2,1)S(1)} %get-tuple-element.51), channel_id=1, source_target_pairs={{0,6},{1,3},{2,4},{3,1},{4,2},{5,7},{6,0},{7,5},{8,14},{9,11},{10,... | collective-permute-start | bytes 393224 | tf_op jit(solution)/shard_map/ppermute | solution.py:432
  8.8 0.1 collective-permute-start.5
  8.9 0.4 collective-permute-done.3.a.refs_0_
  9.3 6.5 %collective-permute-done.4.b.refs_1_ = bf16[128,512]{1,0:T(8,128)(2,1)S(1)} collective-permute-done((bf16[128,512]{1,0:T(8,128)(2,1)S(1)}, bf16[128,512]{1,0:T(8,128)(2,1)S(1)}, u32[]{:S(2)}, u32[]{:S(2)}) %collective-permute-start.4) | collective-permute-done | bytes 131104 | tf_op jit(solution)/shard_map/ppermute | solution.py:432
  15.7 0.0 collective-permute-done.8.og_recv
  15.7 1.2 %soft_forward.1 = (bf16[256,128]{1,0:T(8,128)(2,1)S(1)}, bf16[512,128]{1,0:T(8,128)(2,1)S(1)}, bf16[512,128]{1,0:T(8,128)(2,1)S(1)}, bf16[256,1024]{1,0:T(8,128)...) custom-call(bf16[128,768]{1,0:T(8,128)(2,1)S(1)} %get-tuple-element., ...), custom_call_target="tpu_custom_call" | custom-call | flops 67108864 | bytes 2949120 | tf_op jit(solution)/shard_map/soft_forward/pallas_call | solution.py:66
  16.9 0.0 collective-permute-done.5.c.refs_2_
  17.0 0.7 %lin_forward.1 = (f32[256,128]{1,0:T(8,128)S(1)}, f32[128,128]{1,0:T(8,128)S(1)}, f32[128,512]{1,0:T(8,128)S(1)}, bf16[256,512]{1,0:T(8,128)(2,1)S(1)}) custom-call(f32[128,128]{1,0:T(8,128)S(1)} %get-tuple-element.58.state, bf16[128,768]{1,0:T(8,128)(2,1)S(1)} %get-tuple-element.49.mine.refs_6_, bf16[128,768]{1,0:T(8,128)(2,1)S(1)} %get-tuple-element.55.pair.refs_7_, ...), custom_call_target="tpu_custom_call" | custom-call | flops 67108864 | bytes 2163200 | tf_op jit(solution)/shard_map/lin_forward/pallas_call | solution.py:66
  17.7 1.6 %collective-permute-start.9 = (bf16[256,512]{1,0:T(8,128)(2,1)S(1)}, bf16[256,512]{1,0:T(8,128)(2,1)S(1)}, u32[]{:S(2)}, u32[]{:S(2)}) collective-permute-start(bf16[256,512]{1,0:T(8,128)(2,1)S(1)} %get-tuple-element.63), channel_id=1, source_target_pairs={{0,8},{1,17},{8,0},{9,25},{16,24},{17,1},{24,16},{25,9},{2,10},{3,... | collective-permute-start | bytes 786440 | tf_op jit(solution)/shard_map/ppermute | solution.py:438
  19.2 0.1 collective-permute-start.6
  19.3 1.2 %collective-permute-done.6.got = bf16[2,64,256]{2,1,0:T(8,128)(2,1)S(1)} collective-permute-done((bf16[2,64,256]{2,1,0:T(8,128)(2,1)S(1)}, bf16[2,64,256]{2,1,0:T(8,128)(2,1)S(1)}, u32[]{:S(2)}, u32[]{:S(2)}) %collective-permute-start.6) | collective-permute-done | bytes 65568 | tf_op jit(solution)/shard_map/ppermute | solution.py:421
  20.6 0.6 %collective-permute-start.7 = (bf16[256,256]{1,0:T(8,128)(2,1)S(1)}, bf16[256,256]{1,0:T(8,128)(2,1)S(1)}, u32[]{:S(2)}, u32[]{:S(2)}) collective-permute-start(bf16[256,256]{1,0:T(8,128)(2,1)S(1)} %w_rows.1.first), channel_id=1, source_target_pairs={{0,8},{1,17},{8,0},{9,25},{16,24},{17,1},{24,16},{25,9},{2,10},{3,... | collective-permute-start | bytes 393224 | tf_op jit(solution)/shard_map/ppermute | solution.py:438
  21.2 2.9 %collective-permute-done.9.got = bf16[256,512]{1,0:T(8,128)(2,1)S(1)} collective-permute-done((bf16[256,512]{1,0:T(8,128)(2,1)S(1)}, bf16[256,512]{1,0:T(8,128)(2,1)S(1)}, u32[]{:S(2)}, u32[]{:S(2)}) %collective-permute-start.9) | collective-permute-done | bytes 262176 | tf_op jit(solution)/shard_map/ppermute | solution.py:438
  24.1 0.1 fold.1
  24.1 1.9 %collective-permute-start.11 = (bf16[256,256]{1,0:T(8,128)(2,1)S(1)}, bf16[256,256]{1,0:T(8,128)(2,1)S(1)}, u32[]{:S(2)}, u32[]{:S(2)}) collective-permute-start(bf16[256,256]{1,0:T(8,128)(2,1)S(1)} %get-tuple-element.64.refs_0_), channel_id=1, source_target_pairs={{0,16},{1,9},{8,24},{9,1},{16,0},{17,25},{24,8},{25,17},{2,18},{3,... | collective-permute-start | bytes 393224 | tf_op jit(solution)/shard_map/ppermute | solution.py:438
  26.0 0.5 %collective-permute-done.7.second = bf16[256,256]{1,0:T(8,128)(2,1)S(1)} collective-permute-done((bf16[256,256]{1,0:T(8,128)(2,1)S(1)}, bf16[256,256]{1,0:T(8,128)(2,1)S(1)}, u32[]{:S(2)}, u32[]{:S(2)}) %collective-permute-start.7) | collective-permute-done | bytes 131104 | tf_op jit(solution)/shard_map/ppermute | solution.py:438
  26.6 1.9 %collective-permute-start.10 = (bf16[256,512]{1,0:T(8,128)(2,1)S(1)}, bf16[256,512]{1,0:T(8,128)(2,1)S(1)}, u32[]{:S(2)}, u32[]{:S(2)}) collective-permute-start(bf16[256,512]{1,0:T(8,128)(2,1)S(1)} %w_half.1.refs_0_), channel_id=1, source_target_pairs={{0,16},{1,9},{8,24},{9,1},{16,0},{17,25},{24,8},{25,17},{2,18},{3,... | collective-permute-start | bytes 786440 | tf_op jit(solution)/shard_map/ppermute | solution.py:438
  28.5 0.7 %collective-permute-done.11.got = bf16[256,256]{1,0:T(8,128)(2,1)S(1)} collective-permute-done((bf16[256,256]{1,0:T(8,128)(2,1)S(1)}, bf16[256,256]{1,0:T(8,128)(2,1)S(1)}, u32[]{:S(2)}, u32[]{:S(2)}) %collective-permute-start.11) | collective-permute-done | bytes 131104 | tf_op jit(solution)/shard_map/ppermute | solution.py:438
  29.2 0.1 rows.1
  29.2 0.1 collective-permute-start.12
  29.3 1.3 %collective-permute-done.12.got = f32[128,256]{1,0:T(8,128)S(1)} collective-permute-done((f32[128,256]{1,0:T(8,128)S(1)}, f32[128,256]{1,0:T(8,128)S(1)}, u32[]{:S(2)}, u32[]{:S(2)}) %collective-permute-start.12) | collective-permute-done | bytes 131104 | tf_op jit(solution)/shard_map/ppermute | solution.py:421
  30.7 0.8 %collective-permute-start.13 = (bf16[128,256]{1,0:T(8,128)(2,1)S(1)}, bf16[128,256]{1,0:T(8,128)(2,1)S(1)}, u32[]{:S(2)}, u32[]{:S(2)}) collective-permute-start(bf16[128,256]{1,0:T(8,128)(2,1)S(1)} %get-tuple-element.82), channel_id=1, source_target_pairs={{0,2},{1,7},{2,0},{3,5},{4,6},{5,3},{6,4},{7,1},{8,10},{9,15},{10,... | collective-permute-start | bytes 196616 | tf_op jit(solution)/shard_map/ppermute | solution.py:432
  31.5 1.5 %collective-permute-done.10.refs_1_ = bf16[256,512]{1,0:T(8,128)(2,1)S(1)} collective-permute-done((bf16[256,512]{1,0:T(8,128)(2,1)S(1)}, bf16[256,512]{1,0:T(8,128)(2,1)S(1)}, u32[]{:S(2)}, u32[]{:S(2)}) %collective-permute-start.10) | collective-permute-done | bytes 262176 | tf_op jit(solution)/shard_map/ppermute | solution.py:438
  33.0 1.5 %backward.1 = (bf16[128,128]{1,0:T(8,128)(2,1)S(1)}, bf16[128,128]{1,0:T(8,128)(2,1)S(1)}, f32[128,128]{1,0:T(8,128)S(1)}, f32[256,128]{1,0:T(8,128)S(1)}, f32[5...) custom-call(bf16[256,512]{1,0:T(8,128)(2,1)S(1)} %w_half.1.refs_0_, bf16[256,512]{1,0:T(8,128)(2,1)S(1)} %collective-permute-done.10.refs_1_, ...), custom_call_target="tpu_custom_call" | custom-call | flops 335544320 | bytes 3408384 | tf_op jit(solution)/shard_map/backward/pallas_call | solution.py:66
  34.5 0.5 collective-permute-done.13.got
  35.1 2.7 %collective-permute-start.16 = (bf16[128,256]{1,0:T(8,128)(2,1)S(1)}, bf16[128,256]{1,0:T(8,128)(2,1)S(1)}, u32[]{:S(2)}, u32[]{:S(2)}) collective-permute-start(bf16[128,256]{1,0:T(8,128)(2,1)S(1)} %get-tuple-element.85), channel_id=1, source_target_pairs={{0,4},{1,5},{2,6},{3,7},{4,0},{5,1},{6,2},{7,3},{8,12},{9,13},{10,... | collective-permute-start | bytes 196616 | tf_op jit(solution)/shard_map/ppermute | solution.py:432
  37.8 0.9 %collective-permute-start.14 = (bf16[128,384]{1,0:T(8,128)(2,1)S(1)}, bf16[128,384]{1,0:T(8,128)(2,1)S(1)}, u32[]{:S(2)}, u32[]{:S(2)}) collective-permute-start(bf16[128,384]{1,0:T(8,128)(2,1)S(1)} %get-tuple-element.83), channel_id=1, source_target_pairs={{0,2},{1,7},{2,0},{3,5},{4,6},{5,3},{6,4},{7,1},{8,10},{9,15},{10,... | collective-permute-start | bytes 294920 | tf_op jit(solution)/shard_map/ppermute | solution.py:432
  38.7 0.8 %collective-permute-start.15 = (bf16[128,384]{1,0:T(8,128)(2,1)S(1)}, bf16[128,384]{1,0:T(8,128)(2,1)S(1)}, u32[]{:S(2)}, u32[]{:S(2)}) collective-permute-start(bf16[128,384]{1,0:T(8,128)(2,1)S(1)} %get-tuple-element.84), channel_id=1, source_target_pairs={{0,6},{1,3},{2,4},{3,1},{4,2},{5,7},{6,0},{7,5},{8,14},{9,11},{10,... | collective-permute-start | bytes 294920 | tf_op jit(solution)/shard_map/ppermute | solution.py:432
  39.5 3.9 %collective-permute-done.16.got.refs_0_ = bf16[128,256]{1,0:T(8,128)(2,1)S(1)} collective-permute-done((bf16[128,256]{1,0:T(8,128)(2,1)S(1)}, bf16[128,256]{1,0:T(8,128)(2,1)S(1)}, u32[]{:S(2)}, u32[]{:S(2)}) %collective-permute-start.16) | collective-permute-done | bytes 65568 | tf_op jit(solution)/shard_map/ppermute | solution.py:432
  43.5 2.8 %collective-permute-start.17 = (bf16[64,256]{1,0:T(8,128)(2,1)S(1)}, bf16[64,256]{1,0:T(8,128)(2,1)S(1)}, u32[]{:S(2)}, u32[]{:S(2)}) collective-permute-start(bf16[64,256]{1,0:T(8,128)(2,1)S(1)} %weight_sum.1.own), channel_id=1, source_target_pairs={{0,24},{1,25},{8,16},{9,17},{16,8},{17,9},{24,0},{25,1},{2,26},{3,... | collective-permute-start | bytes 98312 | tf_op jit(solution)/shard_map/ppermute | solution.py:438
  46.3 0.5 %collective-permute-start.18 = (bf16[64,256]{1,0:T(8,128)(2,1)S(1)}, bf16[64,256]{1,0:T(8,128)(2,1)S(1)}, u32[]{:S(2)}, u32[]{:S(2)}) collective-permute-start(bf16[64,256]{1,0:T(8,128)(2,1)S(1)} %weight_sum.1.own), channel_id=1, source_target_pairs={{0,8},{1,17},{8,0},{9,25},{16,24},{17,1},{24,16},{25,9},{2,10},{3,... | collective-permute-start | bytes 98312 | tf_op jit(solution)/shard_map/ppermute | solution.py:438
  46.8 0.2 collective-permute-start.19
  47.0 1.3 %collective-permute-done.17.refs_1_.far = bf16[64,256]{1,0:T(8,128)(2,1)S(1)} collective-permute-done((bf16[64,256]{1,0:T(8,128)(2,1)S(1)}, bf16[64,256]{1,0:T(8,128)(2,1)S(1)}, u32[]{:S(2)}, u32[]{:S(2)}) %collective-permute-start.17) | collective-permute-done | bytes 32800 | tf_op jit(solution)/shard_map/ppermute | solution.py:438
  48.4 1.8 %collective-permute-done.18.refs_2_.near = bf16[64,256]{1,0:T(8,128)(2,1)S(1)} collective-permute-done((bf16[64,256]{1,0:T(8,128)(2,1)S(1)}, bf16[64,256]{1,0:T(8,128)(2,1)S(1)}, u32[]{:S(2)}, u32[]{:S(2)}) %collective-permute-start.18) | collective-permute-done | bytes 32800 | tf_op jit(solution)/shard_map/ppermute | solution.py:438
  50.2 0.5 %collective-permute-done.19.refs_3_.next_near = bf16[64,256]{1,0:T(8,128)(2,1)S(1)} collective-permute-done((bf16[64,256]{1,0:T(8,128)(2,1)S(1)}, bf16[64,256]{1,0:T(8,128)(2,1)S(1)}, u32[]{:S(2)}, u32[]{:S(2)}) %collective-permute-start.19) | collective-permute-done | bytes 32800 | tf_op jit(solution)/shard_map/ppermute | solution.py:438
  50.7 0.0 collective-permute-done.14.a
  50.7 0.0 collective-permute-done.15.b
  50.7 0.4 final.1
  51.1 0.1 collective-permute-start.20
  51.2 0.7 %weight_join.1 = f32[64,1024]{1,0:T(8,128)} custom-call(bf16[64,256]{1,0:T(8,128)(2,1)S(1)} %weight_sum.1.own, bf16[64,256]{1,0:T(8,128)(2,1)S(1)} %collective-permute-done.17.refs_1_.far, bf16[64,256]{1,0:T(8,128)(2,1)S(1)} %collective-permute-done.18.refs_2_.near, bf16[64,256]{1,0:T(8,128)(2,1)S(1)} %collective-permute-done.19.refs_3_.next_near), custom_call_target="tpu_custom_call" | custom-call | bytes 393216 | tf_op jit(solution)/shard_map/weight_join/pallas_call | solution.py:66
  51.9 0.7 %collective-permute-done.20.pair = bf16[128,768]{1,0:T(8,128)(2,1)S(1)} collective-permute-done((bf16[128,768]{1,0:T(8,128)(2,1)S(1)}, bf16[128,768]{1,0:T(8,128)(2,1)S(1)}, u32[]{:S(2)}, u32[]{:S(2)}) %collective-permute-start.20) | collective-permute-done | bytes 196640 | tf_op jit(solution)/shard_map/ppermute | solution.py:421
  52.6 0.8 %outputs.1 = (bf16[1,128,512]{2,1,0:T(8,128)(2,1)}, bf16[1,128,512]{2,1,0:T(8,128)(2,1)}, bf16[1,128,512]{2,1,0:T(8,128)(2,1)}) custom-call(bf16[128,768]{1,0:T(8,128)(2,1)S(1)} %get-tuple-element.87.own, bf16[128,768]{1,0:T(8,128)(2,1)S(1)} %collective-permute-done.20.pair), custom_call_target="tpu_custom_call" | custom-call | bytes 786432 | tf_op jit(solution)/shard_map/outputs/pallas_call | solution.py:66
  (6 shorter events, 0.2 us)
Async XLA Ops:
  0.6 2.3 %collective-permute-start = (bf16[1,128,512]{2,1,0:T(8,128)(2,1)}, bf16[1,128,512]{2,1,0:T(8,128)(2,1)S(1)}, u32[]{:S(2)}, u32[]{:S(2)}) collective-permute-start(bf16[1,128,512]{2,1,0:T(8,128)(2,1)} %q.1), channel_id=1, source_target_pairs={{0,1},{1,0},{2,3},{3,2},{4,5},{5,4},{6,7},{7,6},{8,9},{9,8},{10,11... | collective-permute-start | bytes 393224 | tf_op jit(solution)/shard_map/ppermute | solution.py:421
  1.2 1.8 %collective-permute-start.1 = (bf16[1,128,512]{2,1,0:T(8,128)(2,1)}, bf16[1,128,512]{2,1,0:T(8,128)(2,1)S(1)}, u32[]{:S(2)}, u32[]{:S(2)}) collective-permute-start(bf16[1,128,512]{2,1,0:T(8,128)(2,1)} %k.1), channel_id=1, source_target_pairs={{0,1},{1,0},{2,3},{3,2},{4,5},{5,4},{6,7},{7,6},{8,9},{9,8},{10,11... | collective-permute-start | bytes 393224 | tf_op jit(solution)/shard_map/ppermute | solution.py:421
  1.2 1.7 %collective-permute-start.2 = (bf16[1,128,512]{2,1,0:T(8,128)(2,1)}, bf16[1,128,512]{2,1,0:T(8,128)(2,1)S(1)}, u32[]{:S(2)}, u32[]{:S(2)}) collective-permute-start(bf16[1,128,512]{2,1,0:T(8,128)(2,1)} %v.1), channel_id=1, source_target_pairs={{0,1},{1,0},{2,3},{3,2},{4,5},{5,4},{6,7},{7,6},{8,9},{9,8},{10,11... | collective-permute-start | bytes 393224 | tf_op jit(solution)/shard_map/ppermute | solution.py:421
  1.7 14.1 %collective-permute-start.8 = (bf16[128,1024]{1,0:T(8,128)(2,1)}, bf16[128,1024]{1,0:T(8,128)(2,1)S(1)}, u32[]{:S(2)}, u32[]{:S(2)}) collective-permute-start(bf16[128,1024]{1,0:T(8,128)(2,1)} %bitcast.1), channel_id=1, source_target_pairs={{0,1},{1,0},{2,3},{3,2},{4,5},{5,4},{6,7},{7,6},{8,9},{9,8},{10,11... | collective-permute-start | bytes 786440 | tf_op jit(solution)/shard_map/ppermute | solution.py:421
  3.2 6.0 %collective-permute-start.3 = (bf16[128,512]{1,0:T(8,128)(2,1)S(1)}, bf16[128,512]{1,0:T(8,128)(2,1)S(1)}, u32[]{:S(2)}, u32[]{:S(2)}) collective-permute-start(bf16[128,512]{1,0:T(8,128)(2,1)S(1)} %get-tuple-element.50), channel_id=1, source_target_pairs={{0,2},{1,7},{2,0},{3,5},{4,6},{5,3},{6,4},{7,1},{8,10},{9,15},{10,... | collective-permute-start | bytes 393224 | tf_op jit(solution)/shard_map/ppermute | solution.py:432
  6.3 9.4 %collective-permute-start.4 = (bf16[128,512]{1,0:T(8,128)(2,1)S(1)}, bf16[128,512]{1,0:T(8,128)(2,1)S(1)}, u32[]{:S(2)}, u32[]{:S(2)}) collective-permute-start(bf16[128,512]{1,0:T(8,128)(2,1)S(1)} %get-tuple-element.51), channel_id=1, source_target_pairs={{0,6},{1,3},{2,4},{3,1},{4,2},{5,7},{6,0},{7,5},{8,14},{9,11},{10,... | collective-permute-start | bytes 393224 | tf_op jit(solution)/shard_map/ppermute | solution.py:432
  8.8 8.2 %collective-permute-start.5 = (bf16[128,256]{1,0:T(8,128)(2,1)S(1)}, bf16[128,256]{1,0:T(8,128)(2,1)S(1)}, u32[]{:S(2)}, u32[]{:S(2)}) collective-permute-start(bf16[128,256]{1,0:T(8,128)(2,1)S(1)} %get-tuple-element.52), channel_id=1, source_target_pairs={{0,4},{1,5},{2,6},{3,7},{4,0},{5,1},{6,2},{7,3},{8,12},{9,13},{10,... | collective-permute-start | bytes 196616 | tf_op jit(solution)/shard_map/ppermute | solution.py:432
  17.7 6.4 %collective-permute-start.9 = (bf16[256,512]{1,0:T(8,128)(2,1)S(1)}, bf16[256,512]{1,0:T(8,128)(2,1)S(1)}, u32[]{:S(2)}, u32[]{:S(2)}) collective-permute-start(bf16[256,512]{1,0:T(8,128)(2,1)S(1)} %get-tuple-element.63), channel_id=1, source_target_pairs={{0,8},{1,17},{8,0},{9,25},{16,24},{17,1},{24,16},{25,9},{2,10},{3,... | collective-permute-start | bytes 786440 | tf_op jit(solution)/shard_map/ppermute | solution.py:438
  19.2 1.3 %collective-permute-start.6 = (bf16[2,64,256]{2,1,0:T(8,128)(2,1)S(1)}, bf16[2,64,256]{2,1,0:T(8,128)(2,1)S(1)}, u32[]{:S(2)}, u32[]{:S(2)}) collective-permute-start(bf16[2,64,256]{2,1,0:T(8,128)(2,1)S(1)} %get-tuple-element.54), channel_id=1, source_target_pairs={{0,1},{1,0},{2,3},{3,2},{4,5},{5,4},{6,7},{7,6},{8,9},{9,8},{10,11... | collective-permute-start | bytes 196616 | tf_op jit(solution)/shard_map/ppermute | solution.py:421
  20.6 6.0 %collective-permute-start.7 = (bf16[256,256]{1,0:T(8,128)(2,1)S(1)}, bf16[256,256]{1,0:T(8,128)(2,1)S(1)}, u32[]{:S(2)}, u32[]{:S(2)}) collective-permute-start(bf16[256,256]{1,0:T(8,128)(2,1)S(1)} %w_rows.1.first), channel_id=1, source_target_pairs={{0,8},{1,17},{8,0},{9,25},{16,24},{17,1},{24,16},{25,9},{2,10},{3,... | collective-permute-start | bytes 393224 | tf_op jit(solution)/shard_map/ppermute | solution.py:438
  24.1 5.0 %collective-permute-start.11 = (bf16[256,256]{1,0:T(8,128)(2,1)S(1)}, bf16[256,256]{1,0:T(8,128)(2,1)S(1)}, u32[]{:S(2)}, u32[]{:S(2)}) collective-permute-start(bf16[256,256]{1,0:T(8,128)(2,1)S(1)} %get-tuple-element.64.refs_0_), channel_id=1, source_target_pairs={{0,16},{1,9},{8,24},{9,1},{16,0},{17,25},{24,8},{25,17},{2,18},{3,... | collective-permute-start | bytes 393224 | tf_op jit(solution)/shard_map/ppermute | solution.py:438
  26.6 6.4 %collective-permute-start.10 = (bf16[256,512]{1,0:T(8,128)(2,1)S(1)}, bf16[256,512]{1,0:T(8,128)(2,1)S(1)}, u32[]{:S(2)}, u32[]{:S(2)}) collective-permute-start(bf16[256,512]{1,0:T(8,128)(2,1)S(1)} %w_half.1.refs_0_), channel_id=1, source_target_pairs={{0,16},{1,9},{8,24},{9,1},{16,0},{17,25},{24,8},{25,17},{2,18},{3,... | collective-permute-start | bytes 786440 | tf_op jit(solution)/shard_map/ppermute | solution.py:438
  29.2 1.4 %collective-permute-start.12 = (f32[128,256]{1,0:T(8,128)S(1)}, f32[128,256]{1,0:T(8,128)S(1)}, u32[]{:S(2)}, u32[]{:S(2)}) collective-permute-start(f32[128,256]{1,0:T(8,128)S(1)} %get-tuple-element.67), channel_id=1, source_target_pairs={{0,1},{1,0},{2,3},{3,2},{4,5},{5,4},{6,7},{7,6},{8,9},{9,8},{10,11... | collective-permute-start | bytes 393224 | tf_op jit(solution)/shard_map/ppermute | solution.py:421
  30.7 4.3 %collective-permute-start.13 = (bf16[128,256]{1,0:T(8,128)(2,1)S(1)}, bf16[128,256]{1,0:T(8,128)(2,1)S(1)}, u32[]{:S(2)}, u32[]{:S(2)}) collective-permute-start(bf16[128,256]{1,0:T(8,128)(2,1)S(1)} %get-tuple-element.82), channel_id=1, source_target_pairs={{0,2},{1,7},{2,0},{3,5},{4,6},{5,3},{6,4},{7,1},{8,10},{9,15},{10,... | collective-permute-start | bytes 196616 | tf_op jit(solution)/shard_map/ppermute | solution.py:432
  35.1 8.4 %collective-permute-start.16 = (bf16[128,256]{1,0:T(8,128)(2,1)S(1)}, bf16[128,256]{1,0:T(8,128)(2,1)S(1)}, u32[]{:S(2)}, u32[]{:S(2)}) collective-permute-start(bf16[128,256]{1,0:T(8,128)(2,1)S(1)} %get-tuple-element.85), channel_id=1, source_target_pairs={{0,4},{1,5},{2,6},{3,7},{4,0},{5,1},{6,2},{7,3},{8,12},{9,13},{10,... | collective-permute-start | bytes 196616 | tf_op jit(solution)/shard_map/ppermute | solution.py:432
  37.8 12.9 %collective-permute-start.14 = (bf16[128,384]{1,0:T(8,128)(2,1)S(1)}, bf16[128,384]{1,0:T(8,128)(2,1)S(1)}, u32[]{:S(2)}, u32[]{:S(2)}) collective-permute-start(bf16[128,384]{1,0:T(8,128)(2,1)S(1)} %get-tuple-element.83), channel_id=1, source_target_pairs={{0,2},{1,7},{2,0},{3,5},{4,6},{5,3},{6,4},{7,1},{8,10},{9,15},{10,... | collective-permute-start | bytes 294920 | tf_op jit(solution)/shard_map/ppermute | solution.py:432
  38.7 12.0 %collective-permute-start.15 = (bf16[128,384]{1,0:T(8,128)(2,1)S(1)}, bf16[128,384]{1,0:T(8,128)(2,1)S(1)}, u32[]{:S(2)}, u32[]{:S(2)}) collective-permute-start(bf16[128,384]{1,0:T(8,128)(2,1)S(1)} %get-tuple-element.84), channel_id=1, source_target_pairs={{0,6},{1,3},{2,4},{3,1},{4,2},{5,7},{6,0},{7,5},{8,14},{9,11},{10,... | collective-permute-start | bytes 294920 | tf_op jit(solution)/shard_map/ppermute | solution.py:432
  43.5 4.9 %collective-permute-start.17 = (bf16[64,256]{1,0:T(8,128)(2,1)S(1)}, bf16[64,256]{1,0:T(8,128)(2,1)S(1)}, u32[]{:S(2)}, u32[]{:S(2)}) collective-permute-start(bf16[64,256]{1,0:T(8,128)(2,1)S(1)} %weight_sum.1.own), channel_id=1, source_target_pairs={{0,24},{1,25},{8,16},{9,17},{16,8},{17,9},{24,0},{25,1},{2,26},{3,... | collective-permute-start | bytes 98312 | tf_op jit(solution)/shard_map/ppermute | solution.py:438
  46.3 3.9 %collective-permute-start.18 = (bf16[64,256]{1,0:T(8,128)(2,1)S(1)}, bf16[64,256]{1,0:T(8,128)(2,1)S(1)}, u32[]{:S(2)}, u32[]{:S(2)}) collective-permute-start(bf16[64,256]{1,0:T(8,128)(2,1)S(1)} %weight_sum.1.own), channel_id=1, source_target_pairs={{0,8},{1,17},{8,0},{9,25},{16,24},{17,1},{24,16},{25,9},{2,10},{3,... | collective-permute-start | bytes 98312 | tf_op jit(solution)/shard_map/ppermute | solution.py:438
  46.8 3.9 %collective-permute-start.19 = (bf16[64,256]{1,0:T(8,128)(2,1)S(1)}, bf16[64,256]{1,0:T(8,128)(2,1)S(1)}, u32[]{:S(2)}, u32[]{:S(2)}) collective-permute-start(bf16[64,256]{1,0:T(8,128)(2,1)S(1)} %weight_sum.1.own), channel_id=1, source_target_pairs={{0,16},{1,9},{8,24},{9,1},{16,0},{17,25},{24,8},{25,17},{2,18},{3,... | collective-permute-start | bytes 98312 | tf_op jit(solution)/shard_map/ppermute | solution.py:438
  51.1 1.5 %collective-permute-start.20 = (bf16[128,768]{1,0:T(8,128)(2,1)S(1)}, bf16[128,768]{1,0:T(8,128)(2,1)S(1)}, u32[]{:S(2)}, u32[]{:S(2)}) collective-permute-start(bf16[128,768]{1,0:T(8,128)(2,1)S(1)} %get-tuple-element.88), channel_id=1, source_target_pairs={{0,1},{1,0},{2,3},{3,2},{4,5},{5,4},{6,7},{7,6},{8,9},{9,8},{10,11... | collective-permute-start | bytes 589832 | tf_op jit(solution)/shard_map/ppermute | solution.py:421

commit v20 on v13

--- a/solution.py
+++ b/solution.py
@@ -187,42 +187,53 @@
         send[:, cols] = (mm(high, ogs[:, far], TN) + mm(low, ogs[:, far], TN)).astype(BF)
 
 
-def soft_forward_kernel(
-    direct, mine, pair, og, og_recv, a, b, qs, ks, vs, ogs, probs, attn, keep, *send
+def prep_kernel(
+    mine, pair, og, og_recv, qs, ks, vs, ogs, scores, phi_high, phi_low, slope
 ):
     core, _, _ = places()
+    rows = og.shape[0]
+    for source, wide, place in ((mine, og, core), (pair, og_recv, 1 - core)):
+        here = at(place * rows, rows)
+        qs[here, :] = source[:, QS]
+        ks[here, :] = source[:, KS]
+        vs[here, :] = source[:, VS]
+        ogs[here, :] = wide[...]
+        lin = source[:, QL].astype(F32)
+        phi_high[here, :], phi_low[here, :] = halves(unit_plus(lin))
+        slope[here, :] = unit_slope(lin)
+    for block in range(2):
+        scores[block] = mm(qs[block * rows : (block + 1) * rows, :], ks[...], NT) * FACTOR
+
+
+def soft_forward_kernel(direct, qs, k_chip, v_chip, ogs, chip_scores, a, b, *refs):
+    ks, vs, probs, attn, keep, *send = refs
     way = links(direct)
-    rows = og.shape[0]
-    own_at, pair_at = core * rows, (1 - core) * rows
-    for source, first in ((mine, own_at), (pair, pair_at)):
-        qs[at(first, rows), :] = source[:, QS]
-        ks[at(HALF + first, rows), :] = source[:, KS]
-        vs[at(HALF + first, rows), :] = source[:, VS]
+    rows = qs.shape[0] // 2
+    span = rows + 2 * HALF
+    ks[HALF : HALF + 2 * rows, :] = k_chip[...]
+    vs[HALF : HALF + 2 * rows, :] = v_chip[...]
     for source, side in ((a, way["halo_a"]), (b, way["halo_b"])):
         first = side * (HALF + 2 * rows)
         ks[at(first), :] = source[:, :DH]
         vs[at(first), :] = source[:, DH : 2 * DH]
-    ogs[at(own_at, rows), :] = og[...]
-    ogs[at(pair_at, rows), :] = og_recv[...]
-    span = rows + 2 * HALF
     row_pos = lax.broadcasted_iota(jnp.int32, (rows, span), 0)
     col_pos = lax.broadcasted_iota(jnp.int32, (rows, span), 1)
     inside = (col_pos >= row_pos) & (col_pos < row_pos + WINDOW)
     for block in range(2):
         here, window = slice(block * rows, (block + 1) * rows), slice(block * rows, block * rows + span)
-        scores = mm(qs[here, :], ks[window, :], NT) * FACTOR
-        scores = jnp.where(inside, scores, -1e30)
+        halo = slice(0, HALF) if block == 0 else slice(HALF + 2 * rows, 2 * HALF + 2 * rows)
+        edge = mm(qs[here, :], ks[halo, :], NT) * FACTOR
+        parts = [edge, chip_scores[block]] if block == 0 else [chip_scores[block], edge]
+        scores = jnp.where(inside, jnp.concatenate(parts, axis=1), -1e30)
         peak = jnp.max(scores, axis=1, keepdims=True)
-        terms = jnp.where(inside, jnp.exp(scores - peak), 0.0)
-        share = terms / jnp.sum(terms, axis=1, keepdims=True)
+        terms = jnp.exp(scores - peak)
+        share = terms * (1.0 / jnp.sum(terms, axis=1, keepdims=True))
         probs[block] = share
         attn[here, :] = mm(share.astype(BF), vs[window, :])
     weight_parts(direct, attn[...], ogs, send[0] if send else None, keep)
 
 
-def lin_forward_kernel(direct, state, mine, pair, ogs, gain, *refs):
-    core, _, _ = places()
-    rows = mine.shape[0]
+def lin_forward_kernel(direct, state, phi_high, phi_low, ogs, gain, *refs):
     total = state[...]
     if direct:
         a, b, c, soft_send, u_out, total_out, keep, out = refs
@@ -231,9 +242,9 @@
     else:
         u_out, total_out, keep = refs
     total_out[...] = total
-    u_out[at(core * rows, rows), :] = mm3(unit_plus(mine[:, QL].astype(F32)), total)
-    u_out[at((1 - core) * rows, rows), :] = mm3(unit_plus(pair[:, QL].astype(F32)), total)
-    u = u_out[...]
+    high, low = halves(total)
+    u = mm(phi_high[...], high) + (mm(phi_high[...], low) + mm(phi_low[...], high))
+    u_out[...] = u
     r = lax.rsqrt(jnp.mean(u * u, axis=1, keepdims=True) + norm_eps)
     attn = gain[...] * u * r
     weight_parts(direct, attn, ogs, out.at[DH:, :] if direct else None, keep)
@@ -258,21 +269,14 @@
         send[out, :] = total[at(group * DH + (1 - core) * half, half), :]
 
 
-def lin_backward(u, total, dattn, mine, pair, gain, dq_own, dq_pair, dstate, grads):
-    core, _, _ = places()
-    rows = mine.shape[0]
+def lin_backward(u, total, dattn, phi_high, phi_low, slope, gain, dq, dstate):
     u_all = u[...]
     r = lax.rsqrt(jnp.mean(u_all * u_all, axis=1, keepdims=True) + norm_eps)
     lin_grad = gain[...] * dattn[:, DH:]
-    grads[...] = r * lin_grad - u_all * (r * r * r) * jnp.mean(lin_grad * u_all, axis=1, keepdims=True)
-    total_state = total[...]
-    result = jnp.zeros(dstate.shape, F32)
-    for first, source, out in ((core * rows, mine, dq_own), ((1 - core) * rows, pair, dq_pair)):
-        wide = source[:, QL].astype(F32)
-        part = grads[at(first, rows), :]
-        result = result + mm3(unit_plus(wide), part, TN)
-        out[...] = (mm3(part, total_state, NT) * unit_slope(wide)).astype(BF)
-    dstate[...] = result
+    grads = r * lin_grad - u_all * (r * r * r) * jnp.mean(lin_grad * u_all, axis=1, keepdims=True)
+    high, low = halves(grads)
+    dstate[...] = mm(phi_high[...], high, TN) + (mm(phi_high[...], low, TN) + mm(phi_low[...], high, TN))
+    dq[...] = (mm3(grads, total[...], NT) * slope[...]).astype(BF)
 
 
 def soft_backward(qs, ks, vs, probs, attn, dattn, dq_all, dk_all, dv_all):
@@ -298,8 +302,8 @@
     else:
         weights = refs[0]
         refs = refs[1:]
-    (ogs, u, total, mine, pair, gain, qs, ks, vs, probs, attn,
-     dq_lin, dq_lin_pair, dstate, dq_soft, dk_soft, dv_soft, dattn, grads, *scratch) = refs
+    (ogs, u, total, phi_high, phi_low, slope, gain, qs, ks, vs, probs, attn,
+     dq_lin, dstate, dq_soft, dk_soft, dv_soft, dattn, *scratch) = refs
     if direct:
         _, _, dp = places()
         way = links(True)
@@ -310,7 +314,7 @@
         ):
             weights[:, at((dp ^ step) * width, width)] = source[:, index * width : (index + 1) * width]
     dattn[...] = mm(ogs[...], weights[...], NT)
-    lin_backward(u, total, dattn, mine, pair, gain, dq_lin, dq_lin_pair, dstate, grads)
+    lin_backward(u, total, dattn, phi_high, phi_low, slope, gain, dq_lin, dstate)
     soft_backward(qs, ks, vs, probs, attn, dattn, dq_soft, dk_soft, dv_soft)
 
 
@@ -364,7 +368,7 @@
 
 
 def final_kernel(
-    direct, dstate, mine, pair, dq_soft, dk_soft, dv_soft, dq_lin, dq_lin_pair, a, b, *refs
+    direct, dstate, mine, pair, dq_soft, dk_soft, dv_soft, dq_lin, a, b, *refs
 ):
     core, _, _ = places()
     way = links(direct)
@@ -379,13 +383,13 @@
         out[at(way["block_a"] * rows, rows), :] += a[:, cols].astype(F32)
         out[at(way["block_b"] * rows, rows), :] += b[:, cols].astype(F32)
     high, low = halves(total)
-    for source, dq, out, place in ((mine, dq_lin, own_out, core), (pair, dq_lin_pair, pair_out, 1 - core)):
+    for source, out, place in ((mine, own_out, core), (pair, pair_out, 1 - core)):
         here = at(place * rows, rows)
         out[:, QS] = dq_soft[here, :].astype(BF)
         out[:, KS] = dk_all[here, :].astype(BF)
         out[:, VS] = dv_all[here, :].astype(BF)
         wide, values = source[:, KL].astype(F32), source[:, VL]
-        out[:, QL] = dq[...]
+        out[:, QL] = dq_lin[here, :]
         out[:, KL] = ((mm(values, high, NT) + mm(values, low, NT)) * unit_slope(wide)).astype(BF)
         out[:, VL] = mm3(unit_plus(wide), total).astype(BF)
 
@@ -481,21 +485,30 @@
     span = 2 * rows + 2 * HALF
     keep_width = 2 * width if direct else model
     wg_flops = 2 * 2 * rows * DH * model
-    qs, ks, vs, ogs, probs, attn, keep_soft, *soft_send = call(
+    tokens = like((2 * rows, DH), BF)
+    qs, k_chip, v_chip, ogs, chip_scores, phi_high, phi_low, slope = call(
+        prep_kernel, "prep",
+        [
+            tokens, tokens, tokens, like((2 * rows, model), BF), like((2, rows, 2 * rows), F32),
+            tokens, tokens, like((2 * rows, DH), F32),
+        ],
+        [mine, pair, og, og_recv],
+        flops=wg_flops // 4,
+    )
+    ks, vs, probs, attn, keep_soft, *soft_send = call(
         functools.partial(soft_forward_kernel, direct), "soft_forward",
         [
-            like((2 * rows, DH), BF), like((span, DH), BF), like((span, DH), BF),
-            like((2 * rows, model), BF), like((2, rows, rows + 2 * HALF), F32), like((2 * rows, DH), F32),
-            like((DH, keep_width), F32),
+            like((span, DH), BF), like((span, DH), BF), like((2, rows, rows + 2 * HALF), F32),
+            like((2 * rows, DH), F32), like((DH, keep_width), F32),
         ] + [like((DH, 2 * width), BF)] * direct,
-        [mine, pair, og, og_recv, a, b],
+        [qs, k_chip, v_chip, ogs, chip_scores, a, b],
         flops=wg_flops,
     )
     u, total, keep_lin, *sent = call(
         functools.partial(lin_forward_kernel, direct), "lin_forward",
         [like((2 * rows, DH), F32), like((DH, DH), F32), like((DH, keep_width), F32)]
         + [like((2 * DH, 2 * width), BF)] * direct,
-        [state, mine, pair, ogs, gain] + ([a, b] + c + soft_send if direct else []),
+        [state, phi_high, phi_low, ogs, gain] + ([a, b] + c + soft_send if direct else []),
         flops=wg_flops,
     )
     if direct:
@@ -520,14 +533,14 @@
         )
         piece_got = over_z(piece_send, 0)
         weights.append(piece_keep)
-    dq_lin, dq_lin_pair, dstate, dq_soft, dk_soft, dv_soft = call(
+    dq_lin, dstate, dq_soft, dk_soft, dv_soft = call(
         functools.partial(backward_kernel, direct), "backward",
         [
-            like((rows, DH), BF), like((rows, DH), BF), like((DH, DH), F32),
+            tokens, like((DH, DH), F32),
             like((2 * rows, DH), F32), like((span, DH), F32), like((span, DH), F32),
         ],
-        weights + [ogs, u, total, mine, pair, gain, qs, ks, vs, probs, attn],
-        scratch=[pltpu.VMEM((2 * rows, 2 * DH), F32), pltpu.VMEM((2 * rows, DH), F32)]
+        weights + [ogs, u, total, phi_high, phi_low, slope, gain, qs, ks, vs, probs, attn],
+        scratch=[pltpu.VMEM((2 * rows, 2 * DH), F32)]
         + [pltpu.VMEM((2 * DH, model), BF)] * direct,
         flops=5 * wg_flops,
     )
@@ -563,7 +576,7 @@
     own_out, to_pair = call(
         functools.partial(final_kernel, direct), "final",
         [like((rows, 6 * DH), BF), like((rows, 6 * DH), BF)],
-        [dstate, mine, pair, dq_soft, dk_soft, dv_soft, dq_lin, dq_lin_pair, a, b]
+        [dstate, mine, pair, dq_soft, dk_soft, dv_soft, dq_lin, a, b]
         + (c + [both] if direct else []),
         scratch=[pltpu.VMEM((2 * rows, DH), F32)] * 2,
         flops=wg_flops // 4,

time: 53.1 us -> 53.1 us (level)
    pallas_call x17 -> x18, Pallas kernels: 7.06 us -> 7.21 us  [call(): pl.pallas_call(kernel, name=name, out_shape=list(outs), in_specs=spaces o...]
where the time goes in v20:
time: 53.1 us; the launch traced here: 52.9 us
  waiting for transfers between devices  23.6 us (44%)
  starting transfers between devices  21.4 us (40%)
  Pallas kernels  7.21 us (14%)
  between operations  0.79 us (1%)
    ppermute x7, waiting for transfers between devices, over_z(): return lax.ppermute(value, axes, pairs)  11.1 us
    ppermute x7, starting transfers between devices, over_z(): return lax.ppermute(value, axes, pairs)  10.9 us
    ppermute x6, waiting for transfers between devices, over_dp(): return lax.ppermute(value, ('dp', 'core'), pairs)  9.9 us
    ppermute x6, starting transfers between devices, over_dp(): return lax.ppermute(value, ('dp', 'core'), pairs)  9.13 us
    pallas_call x18, Pallas kernels, call(): pl.pallas_call(kernel, name=name, out_shape=list(outs), in_specs=spaces o...  7.21 us
    ppermute x7, waiting for transfers between devices, over_core(): return lax.ppermute(value, 'core', pair_perm)  2.59 us
    ppermute x7, starting transfers between devices, over_core(): return lax.ppermute(value, 'core', pair_perm)  1.32 us
  transfers between devices with their start and end apart: 20, of which 12 were waited for; matrix products, arithmetic and copies ran while one was open for 0% of the time, Pallas kernels for 10%

profile of v20, /device:TPU:0, one launch (start us, length us, event | category | flops | bytes accessed | tf_op | source)
XLA Modules:
  0.0 52.9 jit_solution(12890385133564331085)
XLA Ops:
  0.6 0.5 collective-permute-start
  1.2 0.1 collective-permute-start.1
  1.2 0.4 collective-permute-start.2
  1.7 0.1 collective-permute-start.8
  1.7 1.2 %pack.1 = (bf16[128,768]{1,0:T(8,128)(2,1)S(1)}, bf16[128,1024]{1,0:T(8,128)(2,1)S(1)}, bf16[64,256]{1,0:T(8,128)(2,1)S(1)}, f32[1,128]{1,0:T(1,128)S(1)}) custom-call(bf16[1,128,512]{2,1,0:T(8,128)(2,1)} %q.1, bf16[1,128,512]{2,1,0:T(8,128)(2,1)} %k.1, bf16[1,128,512]{2,1,0:T(8,128)(2,1)} %v.1, bf16[1,128,1024]{2,1,0:T(8,128)(2,1)} %og.1, ...), custom_call_target="tpu_custom_call" | custom-call | bytes 1279488 | tf_op jit(solution)/shard_map/pack/pallas_call | solution.py:66
  2.9 0.0 collective-permute-done.q_pair
  2.9 0.0 collective-permute-done.1.k_pair
  2.9 0.0 collective-permute-done.2.v_pair
  3.0 0.3 state.1
  3.2 3.1 %collective-permute-start.3 = (bf16[128,512]{1,0:T(8,128)(2,1)S(1)}, bf16[128,512]{1,0:T(8,128)(2,1)S(1)}, u32[]{:S(2)}, u32[]{:S(2)}) collective-permute-start(bf16[128,512]{1,0:T(8,128)(2,1)S(1)} %get-tuple-element.55), channel_id=1, source_target_pairs={{0,2},{1,7},{2,0},{3,5},{4,6},{5,3},{6,4},{7,1},{8,10},{9,15},{10,... | collective-permute-start | bytes 393224 | tf_op jit(solution)/shard_map/ppermute | solution.py:436
  6.3 2.5 %collective-permute-start.4 = (bf16[128,512]{1,0:T(8,128)(2,1)S(1)}, bf16[128,512]{1,0:T(8,128)(2,1)S(1)}, u32[]{:S(2)}, u32[]{:S(2)}) collective-permute-start(bf16[128,512]{1,0:T(8,128)(2,1)S(1)} %get-tuple-element.56), channel_id=1, source_target_pairs={{0,6},{1,3},{2,4},{3,1},{4,2},{5,7},{6,0},{7,5},{8,14},{9,11},{10,... | collective-permute-start | bytes 393224 | tf_op jit(solution)/shard_map/ppermute | solution.py:436
  8.8 0.1 collective-permute-start.5
  8.9 0.0 collective-permute-done.8.og_recv
  8.9 0.3 prep.1
  9.2 0.1 collective-permute-done.3.a.refs_0_
  9.3 6.5 %collective-permute-done.4.b.refs_1_ = bf16[128,512]{1,0:T(8,128)(2,1)S(1)} collective-permute-done((bf16[128,512]{1,0:T(8,128)(2,1)S(1)}, bf16[128,512]{1,0:T(8,128)(2,1)S(1)}, u32[]{:S(2)}, u32[]{:S(2)}) %collective-permute-start.4) | collective-permute-done | bytes 131104 | tf_op jit(solution)/shard_map/ppermute | solution.py:436
  15.7 1.2 %soft_forward.1 = (bf16[512,128]{1,0:T(8,128)(2,1)S(1)}, bf16[512,128]{1,0:T(8,128)(2,1)S(1)}, f32[2,128,384]{2,1,0:T(8,128)S(1)}, f32[256,128]{1,0:T(8,128)S(1)...) custom-call(bf16[256,128]{1,0:T(8,128)(2,1)S(1)} %get-tuple-element.62.qs.refs_10_, ...), custom_call_target="tpu_custom_call" | custom-call | flops 67108864 | bytes 2424832 | tf_op jit(solution)/shard_map/soft_forward/pallas_call | solution.py:66
  16.9 0.0 collective-permute-done.5.c.refs_2_
  16.9 0.7 %lin_forward.1 = (f32[256,128]{1,0:T(8,128)S(1)}, f32[128,128]{1,0:T(8,128)S(1)}, f32[128,512]{1,0:T(8,128)S(1)}, bf16[256,512]{1,0:T(8,128)(2,1)S(1)}) custom-call(f32[128,128]{1,0:T(8,128)S(1)} %get-tuple-element.68.state, bf16[256,128]{1,0:T(8,128)(2,1)S(1)} %get-tuple-element.69.phi_high.refs_6_, bf16[256,128]{1,0:T(8,128)(2,1)S(1)} %get-tuple-element.70.phi_low.refs_7_, ...), custom_call_target="tpu_custom_call" | custom-call | flops 67108864 | bytes 1901056 | tf_op jit(solution)/shard_map/lin_forward/pallas_call | solution.py:66
  17.6 1.6 %collective-permute-start.9 = (bf16[256,512]{1,0:T(8,128)(2,1)S(1)}, bf16[256,512]{1,0:T(8,128)(2,1)S(1)}, u32[]{:S(2)}, u32[]{:S(2)}) collective-permute-start(bf16[256,512]{1,0:T(8,128)(2,1)S(1)} %get-tuple-element.74), channel_id=1, source_target_pairs={{0,8},{1,17},{8,0},{9,25},{16,24},{17,1},{24,16},{25,9},{2,10},{3,... | collective-permute-start | bytes 786440 | tf_op jit(solution)/shard_map/ppermute | solution.py:442
  19.2 0.1 collective-permute-start.6
  19.3 1.2 %collective-permute-done.6.got = bf16[2,64,256]{2,1,0:T(8,128)(2,1)S(1)} collective-permute-done((bf16[2,64,256]{2,1,0:T(8,128)(2,1)S(1)}, bf16[2,64,256]{2,1,0:T(8,128)(2,1)S(1)}, u32[]{:S(2)}, u32[]{:S(2)}) %collective-permute-start.6) | collective-permute-done | bytes 65568 | tf_op jit(solution)/shard_map/ppermute | solution.py:425
  20.5 0.6 %collective-permute-start.7 = (bf16[256,256]{1,0:T(8,128)(2,1)S(1)}, bf16[256,256]{1,0:T(8,128)(2,1)S(1)}, u32[]{:S(2)}, u32[]{:S(2)}) collective-permute-start(bf16[256,256]{1,0:T(8,128)(2,1)S(1)} %w_rows.1.first), channel_id=1, source_target_pairs={{0,8},{1,17},{8,0},{9,25},{16,24},{17,1},{24,16},{25,9},{2,10},{3,... | collective-permute-start | bytes 393224 | tf_op jit(solution)/shard_map/ppermute | solution.py:442
  21.1 2.9 %collective-permute-done.9.got = bf16[256,512]{1,0:T(8,128)(2,1)S(1)} collective-permute-done((bf16[256,512]{1,0:T(8,128)(2,1)S(1)}, bf16[256,512]{1,0:T(8,128)(2,1)S(1)}, u32[]{:S(2)}, u32[]{:S(2)}) %collective-permute-start.9) | collective-permute-done | bytes 262176 | tf_op jit(solution)/shard_map/ppermute | solution.py:442
  24.0 0.1 fold.1
  24.1 1.8 %collective-permute-start.11 = (bf16[256,256]{1,0:T(8,128)(2,1)S(1)}, bf16[256,256]{1,0:T(8,128)(2,1)S(1)}, u32[]{:S(2)}, u32[]{:S(2)}) collective-permute-start(bf16[256,256]{1,0:T(8,128)(2,1)S(1)} %get-tuple-element.75.refs_0_), channel_id=1, source_target_pairs={{0,16},{1,9},{8,24},{9,1},{16,0},{17,25},{24,8},{25,17},{2,18},{3,... | collective-permute-start | bytes 393224 | tf_op jit(solution)/shard_map/ppermute | solution.py:442
  25.9 0.5 %collective-permute-done.7.second = bf16[256,256]{1,0:T(8,128)(2,1)S(1)} collective-permute-done((bf16[256,256]{1,0:T(8,128)(2,1)S(1)}, bf16[256,256]{1,0:T(8,128)(2,1)S(1)}, u32[]{:S(2)}, u32[]{:S(2)}) %collective-permute-start.7) | collective-permute-done | bytes 131104 | tf_op jit(solution)/shard_map/ppermute | solution.py:442
  26.5 1.9 %collective-permute-start.10 = (bf16[256,512]{1,0:T(8,128)(2,1)S(1)}, bf16[256,512]{1,0:T(8,128)(2,1)S(1)}, u32[]{:S(2)}, u32[]{:S(2)}) collective-permute-start(bf16[256,512]{1,0:T(8,128)(2,1)S(1)} %w_half.1.refs_0_), channel_id=1, source_target_pairs={{0,16},{1,9},{8,24},{9,1},{16,0},{17,25},{24,8},{25,17},{2,18},{3,... | collective-permute-start | bytes 786440 | tf_op jit(solution)/shard_map/ppermute | solution.py:442
  28.5 0.7 %collective-permute-done.11.got = bf16[256,256]{1,0:T(8,128)(2,1)S(1)} collective-permute-done((bf16[256,256]{1,0:T(8,128)(2,1)S(1)}, bf16[256,256]{1,0:T(8,128)(2,1)S(1)}, u32[]{:S(2)}, u32[]{:S(2)}) %collective-permute-start.11) | collective-permute-done | bytes 131104 | tf_op jit(solution)/shard_map/ppermute | solution.py:442
  29.1 0.1 rows.1
  29.2 0.1 collective-permute-start.12
  29.3 1.3 %collective-permute-done.12.got = f32[128,256]{1,0:T(8,128)S(1)} collective-permute-done((f32[128,256]{1,0:T(8,128)S(1)}, f32[128,256]{1,0:T(8,128)S(1)}, u32[]{:S(2)}, u32[]{:S(2)}) %collective-permute-start.12) | collective-permute-done | bytes 131104 | tf_op jit(solution)/shard_map/ppermute | solution.py:425
  30.7 0.8 %collective-permute-start.13 = (bf16[128,256]{1,0:T(8,128)(2,1)S(1)}, bf16[128,256]{1,0:T(8,128)(2,1)S(1)}, u32[]{:S(2)}, u32[]{:S(2)}) collective-permute-start(bf16[128,256]{1,0:T(8,128)(2,1)S(1)} %get-tuple-element.92), channel_id=1, source_target_pairs={{0,2},{1,7},{2,0},{3,5},{4,6},{5,3},{6,4},{7,1},{8,10},{9,15},{10,... | collective-permute-start | bytes 196616 | tf_op jit(solution)/shard_map/ppermute | solution.py:436
  31.5 1.5 %collective-permute-done.10.refs_1_ = bf16[256,512]{1,0:T(8,128)(2,1)S(1)} collective-permute-done((bf16[256,512]{1,0:T(8,128)(2,1)S(1)}, bf16[256,512]{1,0:T(8,128)(2,1)S(1)}, u32[]{:S(2)}, u32[]{:S(2)}) %collective-permute-start.10) | collective-permute-done | bytes 262176 | tf_op jit(solution)/shard_map/ppermute | solution.py:442
  32.9 1.5 %backward.1 = (bf16[256,128]{1,0:T(8,128)(2,1)S(1)}, f32[128,128]{1,0:T(8,128)S(1)}, f32[256,128]{1,0:T(8,128)S(1)}, f32[512,128]{1,0:T(8,128)S(1)}, f32[512,128]{1,0:T(8,128)S(1)}) custom-call(bf16[256,512]{1,0:T(8,128)(2,1)S(1)} %w_half.1.refs_0_, bf16[256,512]{1,0:T(8,128)(2,1)S(1)} %collective-permute-done.10.refs_1_, ...), custom_call_target="tpu_custom_call" | custom-call | flops 335544320 | bytes 3277312 | tf_op jit(solution)/shard_map/backward/pallas_call | solution.py:66
  34.4 0.6 %collective-permute-done.13.got = bf16[128,256]{1,0:T(8,128)(2,1)S(1)} collective-permute-done((bf16[128,256]{1,0:T(8,128)(2,1)S(1)}, bf16[128,256]{1,0:T(8,128)(2,1)S(1)}, u32[]{:S(2)}, u32[]{:S(2)}) %collective-permute-start.13) | collective-permute-done | bytes 65568 | tf_op jit(solution)/shard_map/ppermute | solution.py:436
  35.0 2.7 %collective-permute-start.16 = (bf16[128,256]{1,0:T(8,128)(2,1)S(1)}, bf16[128,256]{1,0:T(8,128)(2,1)S(1)}, u32[]{:S(2)}, u32[]{:S(2)}) collective-permute-start(bf16[128,256]{1,0:T(8,128)(2,1)S(1)} %get-tuple-element.95), channel_id=1, source_target_pairs={{0,4},{1,5},{2,6},{3,7},{4,0},{5,1},{6,2},{7,3},{8,12},{9,13},{10,... | collective-permute-start | bytes 196616 | tf_op jit(solution)/shard_map/ppermute | solution.py:436
  37.7 1.0 %collective-permute-start.14 = (bf16[128,384]{1,0:T(8,128)(2,1)S(1)}, bf16[128,384]{1,0:T(8,128)(2,1)S(1)}, u32[]{:S(2)}, u32[]{:S(2)}) collective-permute-start(bf16[128,384]{1,0:T(8,128)(2,1)S(1)} %get-tuple-element.93), channel_id=1, source_target_pairs={{0,2},{1,7},{2,0},{3,5},{4,6},{5,3},{6,4},{7,1},{8,10},{9,15},{10,... | collective-permute-start | bytes 294920 | tf_op jit(solution)/shard_map/ppermute | solution.py:436
  38.7 0.8 %collective-permute-start.15 = (bf16[128,384]{1,0:T(8,128)(2,1)S(1)}, bf16[128,384]{1,0:T(8,128)(2,1)S(1)}, u32[]{:S(2)}, u32[]{:S(2)}) collective-permute-start(bf16[128,384]{1,0:T(8,128)(2,1)S(1)} %get-tuple-element.94), channel_id=1, source_target_pairs={{0,6},{1,3},{2,4},{3,1},{4,2},{5,7},{6,0},{7,5},{8,14},{9,11},{10,... | collective-permute-start | bytes 294920 | tf_op jit(solution)/shard_map/ppermute | solution.py:436
  39.5 3.9 %collective-permute-done.16.got.refs_0_ = bf16[128,256]{1,0:T(8,128)(2,1)S(1)} collective-permute-done((bf16[128,256]{1,0:T(8,128)(2,1)S(1)}, bf16[128,256]{1,0:T(8,128)(2,1)S(1)}, u32[]{:S(2)}, u32[]{:S(2)}) %collective-permute-start.16) | collective-permute-done | bytes 65568 | tf_op jit(solution)/shard_map/ppermute | solution.py:436
  43.4 1.3 %collective-permute-start.17 = (bf16[64,256]{1,0:T(8,128)(2,1)S(1)}, bf16[64,256]{1,0:T(8,128)(2,1)S(1)}, u32[]{:S(2)}, u32[]{:S(2)}) collective-permute-start(bf16[64,256]{1,0:T(8,128)(2,1)S(1)} %weight_sum.1.first), channel_id=1, source_target_pairs={{0,8},{1,17},{8,0},{9,25},{16,24},{17,1},{24,16},{25,9},{2,10},{3,... | collective-permute-start | bytes 98312 | tf_op jit(solution)/shard_map/ppermute | solution.py:442
  44.7 2.7 %collective-permute-done.17.second = bf16[64,256]{1,0:T(8,128)(2,1)S(1)} collective-permute-done((bf16[64,256]{1,0:T(8,128)(2,1)S(1)}, bf16[64,256]{1,0:T(8,128)(2,1)S(1)}, u32[]{:S(2)}, u32[]{:S(2)}) %collective-permute-start.17) | collective-permute-done | bytes 32800 | tf_op jit(solution)/shard_map/ppermute | solution.py:442
  47.4 0.0 collective-permute-done.14.a
  47.4 0.0 collective-permute-done.15.b
  47.4 0.4 final.1
  47.8 0.1 collective-permute-start.18
  47.9 1.9 %collective-permute-start.19 = (bf16[64,512]{1,0:T(8,128)(2,1)S(1)}, bf16[64,512]{1,0:T(8,128)(2,1)S(1)}, u32[]{:S(2)}, u32[]{:S(2)}) collective-permute-start(bf16[64,512]{1,0:T(8,128)(2,1)S(1)} %both.1.refs_1_), channel_id=1, source_target_pairs={{0,16},{1,9},{8,24},{9,1},{16,0},{17,25},{24,8},{25,17},{2,18},{3,... | collective-permute-start | bytes 196616 | tf_op jit(solution)/shard_map/ppermute | solution.py:442
  49.8 0.0 collective-permute-done.18.pair
  49.8 0.8 %outputs.1 = (bf16[1,128,512]{2,1,0:T(8,128)(2,1)}, bf16[1,128,512]{2,1,0:T(8,128)(2,1)}, bf16[1,128,512]{2,1,0:T(8,128)(2,1)}) custom-call(bf16[128,768]{1,0:T(8,128)(2,1)S(1)} %get-tuple-element.97.own, bf16[128,768]{1,0:T(8,128)(2,1)S(1)} %collective-permute-done.18.pair), custom_call_target="tpu_custom_call" | custom-call | bytes 786432 | tf_op jit(solution)/shard_map/outputs/pallas_call | solution.py:66
  50.6 1.6 %collective-permute-done.19.got = bf16[64,512]{1,0:T(8,128)(2,1)S(1)} collective-permute-done((bf16[64,512]{1,0:T(8,128)(2,1)S(1)}, bf16[64,512]{1,0:T(8,128)(2,1)S(1)}, u32[]{:S(2)}, u32[]{:S(2)}) %collective-permute-start.19) | collective-permute-done | bytes 65568 | tf_op jit(solution)/shard_map/ppermute | solution.py:442
  52.2 0.7 %weight_join.1 = f32[64,1024]{1,0:T(8,128)} custom-call(bf16[64,512]{1,0:T(8,128)(2,1)S(1)} %both.1.refs_1_, bf16[64,512]{1,0:T(8,128)(2,1)S(1)} %collective-permute-done.19.got, bf16[1,128,512]{2,1,0:T(8,128)(2,1)} %get-tuple-element.49._), custom_call_target="tpu_custom_call" | custom-call | bytes 524288 | tf_op jit(solution)/shard_map/weight_join/pallas_call | solution.py:66
  (7 shorter events, 0.2 us)
Async XLA Ops:
  0.6 2.3 %collective-permute-start = (bf16[1,128,512]{2,1,0:T(8,128)(2,1)}, bf16[1,128,512]{2,1,0:T(8,128)(2,1)S(1)}, u32[]{:S(2)}, u32[]{:S(2)}) collective-permute-start(bf16[1,128,512]{2,1,0:T(8,128)(2,1)} %q.1), channel_id=1, source_target_pairs={{0,1},{1,0},{2,3},{3,2},{4,5},{5,4},{6,7},{7,6},{8,9},{9,8},{10,11... | collective-permute-start | bytes 393224 | tf_op jit(solution)/shard_map/ppermute | solution.py:425
  1.2 1.8 %collective-permute-start.1 = (bf16[1,128,512]{2,1,0:T(8,128)(2,1)}, bf16[1,128,512]{2,1,0:T(8,128)(2,1)S(1)}, u32[]{:S(2)}, u32[]{:S(2)}) collective-permute-start(bf16[1,128,512]{2,1,0:T(8,128)(2,1)} %k.1), channel_id=1, source_target_pairs={{0,1},{1,0},{2,3},{3,2},{4,5},{5,4},{6,7},{7,6},{8,9},{9,8},{10,11... | collective-permute-start | bytes 393224 | tf_op jit(solution)/shard_map/ppermute | solution.py:425
  1.2 1.7 %collective-permute-start.2 = (bf16[1,128,512]{2,1,0:T(8,128)(2,1)}, bf16[1,128,512]{2,1,0:T(8,128)(2,1)S(1)}, u32[]{:S(2)}, u32[]{:S(2)}) collective-permute-start(bf16[1,128,512]{2,1,0:T(8,128)(2,1)} %v.1), channel_id=1, source_target_pairs={{0,1},{1,0},{2,3},{3,2},{4,5},{5,4},{6,7},{7,6},{8,9},{9,8},{10,11... | collective-permute-start | bytes 393224 | tf_op jit(solution)/shard_map/ppermute | solution.py:425
  1.7 7.2 %collective-permute-start.8 = (bf16[128,1024]{1,0:T(8,128)(2,1)}, bf16[128,1024]{1,0:T(8,128)(2,1)S(1)}, u32[]{:S(2)}, u32[]{:S(2)}) collective-permute-start(bf16[128,1024]{1,0:T(8,128)(2,1)} %bitcast.1), channel_id=1, source_target_pairs={{0,1},{1,0},{2,3},{3,2},{4,5},{5,4},{6,7},{7,6},{8,9},{9,8},{10,11... | collective-permute-start | bytes 786440 | tf_op jit(solution)/shard_map/ppermute | solution.py:425
  3.2 6.0 %collective-permute-start.3 = (bf16[128,512]{1,0:T(8,128)(2,1)S(1)}, bf16[128,512]{1,0:T(8,128)(2,1)S(1)}, u32[]{:S(2)}, u32[]{:S(2)}) collective-permute-start(bf16[128,512]{1,0:T(8,128)(2,1)S(1)} %get-tuple-element.55), channel_id=1, source_target_pairs={{0,2},{1,7},{2,0},{3,5},{4,6},{5,3},{6,4},{7,1},{8,10},{9,15},{10,... | collective-permute-start | bytes 393224 | tf_op jit(solution)/shard_map/ppermute | solution.py:436
  6.3 9.4 %collective-permute-start.4 = (bf16[128,512]{1,0:T(8,128)(2,1)S(1)}, bf16[128,512]{1,0:T(8,128)(2,1)S(1)}, u32[]{:S(2)}, u32[]{:S(2)}) collective-permute-start(bf16[128,512]{1,0:T(8,128)(2,1)S(1)} %get-tuple-element.56), channel_id=1, source_target_pairs={{0,6},{1,3},{2,4},{3,1},{4,2},{5,7},{6,0},{7,5},{8,14},{9,11},{10,... | collective-permute-start | bytes 393224 | tf_op jit(solution)/shard_map/ppermute | solution.py:436
  8.8 8.1 %collective-permute-start.5 = (bf16[128,256]{1,0:T(8,128)(2,1)S(1)}, bf16[128,256]{1,0:T(8,128)(2,1)S(1)}, u32[]{:S(2)}, u32[]{:S(2)}) collective-permute-start(bf16[128,256]{1,0:T(8,128)(2,1)S(1)} %get-tuple-element.57), channel_id=1, source_target_pairs={{0,4},{1,5},{2,6},{3,7},{4,0},{5,1},{6,2},{7,3},{8,12},{9,13},{10,... | collective-permute-start | bytes 196616 | tf_op jit(solution)/shard_map/ppermute | solution.py:436
  17.6 6.4 %collective-permute-start.9 = (bf16[256,512]{1,0:T(8,128)(2,1)S(1)}, bf16[256,512]{1,0:T(8,128)(2,1)S(1)}, u32[]{:S(2)}, u32[]{:S(2)}) collective-permute-start(bf16[256,512]{1,0:T(8,128)(2,1)S(1)} %get-tuple-element.74), channel_id=1, source_target_pairs={{0,8},{1,17},{8,0},{9,25},{16,24},{17,1},{24,16},{25,9},{2,10},{3,... | collective-permute-start | bytes 786440 | tf_op jit(solution)/shard_map/ppermute | solution.py:442
  19.2 1.3 %collective-permute-start.6 = (bf16[2,64,256]{2,1,0:T(8,128)(2,1)S(1)}, bf16[2,64,256]{2,1,0:T(8,128)(2,1)S(1)}, u32[]{:S(2)}, u32[]{:S(2)}) collective-permute-start(bf16[2,64,256]{2,1,0:T(8,128)(2,1)S(1)} %get-tuple-element.59), channel_id=1, source_target_pairs={{0,1},{1,0},{2,3},{3,2},{4,5},{5,4},{6,7},{7,6},{8,9},{9,8},{10,11... | collective-permute-start | bytes 196616 | tf_op jit(solution)/shard_map/ppermute | solution.py:425
  20.5 5.9 %collective-permute-start.7 = (bf16[256,256]{1,0:T(8,128)(2,1)S(1)}, bf16[256,256]{1,0:T(8,128)(2,1)S(1)}, u32[]{:S(2)}, u32[]{:S(2)}) collective-permute-start(bf16[256,256]{1,0:T(8,128)(2,1)S(1)} %w_rows.1.first), channel_id=1, source_target_pairs={{0,8},{1,17},{8,0},{9,25},{16,24},{17,1},{24,16},{25,9},{2,10},{3,... | collective-permute-start | bytes 393224 | tf_op jit(solution)/shard_map/ppermute | solution.py:442
  24.1 5.0 %collective-permute-start.11 = (bf16[256,256]{1,0:T(8,128)(2,1)S(1)}, bf16[256,256]{1,0:T(8,128)(2,1)S(1)}, u32[]{:S(2)}, u32[]{:S(2)}) collective-permute-start(bf16[256,256]{1,0:T(8,128)(2,1)S(1)} %get-tuple-element.75.refs_0_), channel_id=1, source_target_pairs={{0,16},{1,9},{8,24},{9,1},{16,0},{17,25},{24,8},{25,17},{2,18},{3,... | collective-permute-start | bytes 393224 | tf_op jit(solution)/shard_map/ppermute | solution.py:442
  26.5 6.4 %collective-permute-start.10 = (bf16[256,512]{1,0:T(8,128)(2,1)S(1)}, bf16[256,512]{1,0:T(8,128)(2,1)S(1)}, u32[]{:S(2)}, u32[]{:S(2)}) collective-permute-start(bf16[256,512]{1,0:T(8,128)(2,1)S(1)} %w_half.1.refs_0_), channel_id=1, source_target_pairs={{0,16},{1,9},{8,24},{9,1},{16,0},{17,25},{24,8},{25,17},{2,18},{3,... | collective-permute-start | bytes 786440 | tf_op jit(solution)/shard_map/ppermute | solution.py:442
  29.2 1.4 %collective-permute-start.12 = (f32[128,256]{1,0:T(8,128)S(1)}, f32[128,256]{1,0:T(8,128)S(1)}, u32[]{:S(2)}, u32[]{:S(2)}) collective-permute-start(f32[128,256]{1,0:T(8,128)S(1)} %get-tuple-element.78), channel_id=1, source_target_pairs={{0,1},{1,0},{2,3},{3,2},{4,5},{5,4},{6,7},{7,6},{8,9},{9,8},{10,11... | collective-permute-start | bytes 393224 | tf_op jit(solution)/shard_map/ppermute | solution.py:425
  30.7 4.3 %collective-permute-start.13 = (bf16[128,256]{1,0:T(8,128)(2,1)S(1)}, bf16[128,256]{1,0:T(8,128)(2,1)S(1)}, u32[]{:S(2)}, u32[]{:S(2)}) collective-permute-start(bf16[128,256]{1,0:T(8,128)(2,1)S(1)} %get-tuple-element.92), channel_id=1, source_target_pairs={{0,2},{1,7},{2,0},{3,5},{4,6},{5,3},{6,4},{7,1},{8,10},{9,15},{10,... | collective-permute-start | bytes 196616 | tf_op jit(solution)/shard_map/ppermute | solution.py:436
  35.0 8.4 %collective-permute-start.16 = (bf16[128,256]{1,0:T(8,128)(2,1)S(1)}, bf16[128,256]{1,0:T(8,128)(2,1)S(1)}, u32[]{:S(2)}, u32[]{:S(2)}) collective-permute-start(bf16[128,256]{1,0:T(8,128)(2,1)S(1)} %get-tuple-element.95), channel_id=1, source_target_pairs={{0,4},{1,5},{2,6},{3,7},{4,0},{5,1},{6,2},{7,3},{8,12},{9,13},{10,... | collective-permute-start | bytes 196616 | tf_op jit(solution)/shard_map/ppermute | solution.py:436
  37.7 9.7 %collective-permute-start.14 = (bf16[128,384]{1,0:T(8,128)(2,1)S(1)}, bf16[128,384]{1,0:T(8,128)(2,1)S(1)}, u32[]{:S(2)}, u32[]{:S(2)}) collective-permute-start(bf16[128,384]{1,0:T(8,128)(2,1)S(1)} %get-tuple-element.93), channel_id=1, source_target_pairs={{0,2},{1,7},{2,0},{3,5},{4,6},{5,3},{6,4},{7,1},{8,10},{9,15},{10,... | collective-permute-start | bytes 294920 | tf_op jit(solution)/shard_map/ppermute | solution.py:436
  38.7 8.7 %collective-permute-start.15 = (bf16[128,384]{1,0:T(8,128)(2,1)S(1)}, bf16[128,384]{1,0:T(8,128)(2,1)S(1)}, u32[]{:S(2)}, u32[]{:S(2)}) collective-permute-start(bf16[128,384]{1,0:T(8,128)(2,1)S(1)} %get-tuple-element.94), channel_id=1, source_target_pairs={{0,6},{1,3},{2,4},{3,1},{4,2},{5,7},{6,0},{7,5},{8,14},{9,11},{10,... | collective-permute-start | bytes 294920 | tf_op jit(solution)/shard_map/ppermute | solution.py:436
  43.4 4.0 %collective-permute-start.17 = (bf16[64,256]{1,0:T(8,128)(2,1)S(1)}, bf16[64,256]{1,0:T(8,128)(2,1)S(1)}, u32[]{:S(2)}, u32[]{:S(2)}) collective-permute-start(bf16[64,256]{1,0:T(8,128)(2,1)S(1)} %weight_sum.1.first), channel_id=1, source_target_pairs={{0,8},{1,17},{8,0},{9,25},{16,24},{17,1},{24,16},{25,9},{2,10},{3,... | collective-permute-start | bytes 98312 | tf_op jit(solution)/shard_map/ppermute | solution.py:442
  47.8 2.0 %collective-permute-start.18 = (bf16[128,768]{1,0:T(8,128)(2,1)S(1)}, bf16[128,768]{1,0:T(8,128)(2,1)S(1)}, u32[]{:S(2)}, u32[]{:S(2)}) collective-permute-start(bf16[128,768]{1,0:T(8,128)(2,1)S(1)} %get-tuple-element.98), channel_id=1, source_target_pairs={{0,1},{1,0},{2,3},{3,2},{4,5},{5,4},{6,7},{7,6},{8,9},{9,8},{10,11... | collective-permute-start | bytes 589832 | tf_op jit(solution)/shard_map/ppermute | solution.py:425
  47.9 4.3 %collective-permute-start.19 = (bf16[64,512]{1,0:T(8,128)(2,1)S(1)}, bf16[64,512]{1,0:T(8,128)(2,1)S(1)}, u32[]{:S(2)}, u32[]{:S(2)}) collective-permute-start(bf16[64,512]{1,0:T(8,128)(2,1)S(1)} %both.1.refs_1_), channel_id=1, source_target_pairs={{0,16},{1,9},{8,24},{9,1},{16,0},{17,25},{24,8},{25,17},{2,18},{3,... | collective-permute-start | bytes 196616 | tf_op jit(solution)/shard_map/ppermute | solution.py:442

commit v21 on v20

--- a/solution.py
+++ b/solution.py
@@ -173,9 +173,14 @@
 
 
 def weight_parts(direct, attn, ogs, send, keep):
-    high, low = halves(attn)
+    both = jnp.concatenate(halves(attn), axis=1)
+
+    def product(cols):
+        wide = mm(both, cols, TN)
+        return wide[:DH] + wide[DH:]
+
     if not direct:
-        keep[...] = mm(high, ogs[...], TN) + mm(low, ogs[...], TN)
+        keep[...] = product(ogs[...])
         return
     _, _, dp = places()
     way = links(True)
@@ -183,8 +188,14 @@
     for index, step in enumerate((0, way["other"])):
         cols = slice(index * width, (index + 1) * width)
         near, far = at((dp ^ step) * width, width), at((dp ^ step ^ way["step"]) * width, width)
-        keep[:, cols] = mm(high, ogs[:, near], TN) + mm(low, ogs[:, near], TN)
-        send[:, cols] = (mm(high, ogs[:, far], TN) + mm(low, ogs[:, far], TN)).astype(BF)
+        keep[:, cols] = product(ogs[:, near])
+        send[:, cols] = product(ogs[:, far]).astype(BF)
+
+
+def mm_pair(a_high, a_low, b, dims, axis):
+    b_high, b_low = halves(b)
+    wide = mm(a_high, jnp.concatenate([b_high, b_low], axis=axis), dims)
+    return wide[:, :DH] + (wide[:, DH:] + mm(a_low, b_high, dims))
 
 
 def prep_kernel(
@@ -242,8 +253,7 @@
     else:
         u_out, total_out, keep = refs
     total_out[...] = total
-    high, low = halves(total)
-    u = mm(phi_high[...], high) + (mm(phi_high[...], low) + mm(phi_low[...], high))
+    u = mm_pair(phi_high[...], phi_low[...], total, NN, 1)
     u_out[...] = u
     r = lax.rsqrt(jnp.mean(u * u, axis=1, keepdims=True) + norm_eps)
     attn = gain[...] * u * r
@@ -274,9 +284,8 @@
     r = lax.rsqrt(jnp.mean(u_all * u_all, axis=1, keepdims=True) + norm_eps)
     lin_grad = gain[...] * dattn[:, DH:]
     grads = r * lin_grad - u_all * (r * r * r) * jnp.mean(lin_grad * u_all, axis=1, keepdims=True)
-    high, low = halves(grads)
-    dstate[...] = mm(phi_high[...], high, TN) + (mm(phi_high[...], low, TN) + mm(phi_low[...], high, TN))
-    dq[...] = (mm3(grads, total[...], NT) * slope[...]).astype(BF)
+    dstate[...] = mm_pair(phi_high[...], phi_low[...], grads, TN, 1)
+    dq[...] = (mm_pair(*halves(grads), total[...], NT, 0) * slope[...]).astype(BF)
 
 
 def soft_backward(qs, ks, vs, probs, attn, dattn, dq_all, dk_all, dv_all):

time: 53.1 us -> 53 us (level)
  no operation moved by 1% of the time
where the time goes in v21:
time: 53 us; the launch traced here: 52.8 us
  waiting for transfers between devices  23.5 us (44%)
  starting transfers between devices  21.4 us (40%)
  Pallas kernels  7.13 us (13%)
  between operations  0.79 us (1%)
    ppermute x7, waiting for transfers between devices, over_z(): return lax.ppermute(value, axes, pairs)  11 us
    ppermute x7, starting transfers between devices, over_z(): return lax.ppermute(value, axes, pairs)  10.9 us
    ppermute x6, waiting for transfers between devices, over_dp(): return lax.ppermute(value, ('dp', 'core'), pairs)  9.88 us
    ppermute x6, starting transfers between devices, over_dp(): return lax.ppermute(value, ('dp', 'core'), pairs)  9.14 us
    pallas_call x18, Pallas kernels, call(): pl.pallas_call(kernel, name=name, out_shape=list(outs), in_specs=spaces o...  7.13 us
    ppermute x7, waiting for transfers between devices, over_core(): return lax.ppermute(value, 'core', pair_perm)  2.59 us
    ppermute x7, starting transfers between devices, over_core(): return lax.ppermute(value, 'core', pair_perm)  1.32 us
  transfers between devices with their start and end apart: 20, of which 12 were waited for; matrix products, arithmetic and copies ran while one was open for 0% of the time, Pallas kernels for 10%

profile of v21, /device:TPU:0, one launch (start us, length us, event | category | flops | bytes accessed | tf_op | source)
XLA Modules:
  0.0 52.8 jit_solution(15877354557016165117)
XLA Ops:
  0.6 0.5 collective-permute-start
  1.2 0.1 collective-permute-start.1
  1.2 0.4 collective-permute-start.2
  1.7 0.1 collective-permute-start.8
  1.7 1.2 %pack.1 = (bf16[128,768]{1,0:T(8,128)(2,1)S(1)}, bf16[128,1024]{1,0:T(8,128)(2,1)S(1)}, bf16[64,256]{1,0:T(8,128)(2,1)S(1)}, f32[1,128]{1,0:T(1,128)S(1)}) custom-call(bf16[1,128,512]{2,1,0:T(8,128)(2,1)} %q.1, bf16[1,128,512]{2,1,0:T(8,128)(2,1)} %k.1, bf16[1,128,512]{2,1,0:T(8,128)(2,1)} %v.1, bf16[1,128,1024]{2,1,0:T(8,128)(2,1)} %og.1, ...), custom_call_target="tpu_custom_call" | custom-call | bytes 1279488 | tf_op jit(solution)/shard_map/pack/pallas_call | solution.py:66
  2.9 0.0 collective-permute-done.q_pair
  2.9 0.0 collective-permute-done.1.k_pair
  2.9 0.0 collective-permute-done.2.v_pair
  3.0 0.3 state.1
  3.2 3.1 %collective-permute-start.3 = (bf16[128,512]{1,0:T(8,128)(2,1)S(1)}, bf16[128,512]{1,0:T(8,128)(2,1)S(1)}, u32[]{:S(2)}, u32[]{:S(2)}) collective-permute-start(bf16[128,512]{1,0:T(8,128)(2,1)S(1)} %get-tuple-element.55), channel_id=1, source_target_pairs={{0,2},{1,7},{2,0},{3,5},{4,6},{5,3},{6,4},{7,1},{8,10},{9,15},{10,... | collective-permute-start | bytes 393224 | tf_op jit(solution)/shard_map/ppermute | solution.py:445
  6.3 2.5 %collective-permute-start.4 = (bf16[128,512]{1,0:T(8,128)(2,1)S(1)}, bf16[128,512]{1,0:T(8,128)(2,1)S(1)}, u32[]{:S(2)}, u32[]{:S(2)}) collective-permute-start(bf16[128,512]{1,0:T(8,128)(2,1)S(1)} %get-tuple-element.56), channel_id=1, source_target_pairs={{0,6},{1,3},{2,4},{3,1},{4,2},{5,7},{6,0},{7,5},{8,14},{9,11},{10,... | collective-permute-start | bytes 393224 | tf_op jit(solution)/shard_map/ppermute | solution.py:445
  8.8 0.1 collective-permute-start.5
  8.9 0.0 collective-permute-done.8.og_recv
  8.9 0.3 prep.1
  9.2 0.1 collective-permute-done.3.a.refs_0_
  9.3 6.5 %collective-permute-done.4.b.refs_1_ = bf16[128,512]{1,0:T(8,128)(2,1)S(1)} collective-permute-done((bf16[128,512]{1,0:T(8,128)(2,1)S(1)}, bf16[128,512]{1,0:T(8,128)(2,1)S(1)}, u32[]{:S(2)}, u32[]{:S(2)}) %collective-permute-start.4) | collective-permute-done | bytes 131104 | tf_op jit(solution)/shard_map/ppermute | solution.py:445
  15.7 1.1 %soft_forward.1 = (bf16[512,128]{1,0:T(8,128)(2,1)S(1)}, bf16[512,128]{1,0:T(8,128)(2,1)S(1)}, f32[2,128,384]{2,1,0:T(8,128)S(1)}, f32[256,128]{1,0:T(8,128)S(1)...) custom-call(bf16[256,128]{1,0:T(8,128)(2,1)S(1)} %get-tuple-element.62.qs.refs_10_, ...), custom_call_target="tpu_custom_call" | custom-call | flops 67108864 | bytes 2424832 | tf_op jit(solution)/shard_map/soft_forward/pallas_call | solution.py:66
  16.9 0.0 collective-permute-done.5.c.refs_2_
  16.9 0.6 %lin_forward.1 = (f32[256,128]{1,0:T(8,128)S(1)}, f32[128,128]{1,0:T(8,128)S(1)}, f32[128,512]{1,0:T(8,128)S(1)}, bf16[256,512]{1,0:T(8,128)(2,1)S(1)}) custom-call(f32[128,128]{1,0:T(8,128)S(1)} %get-tuple-element.68.state, bf16[256,128]{1,0:T(8,128)(2,1)S(1)} %get-tuple-element.69.phi_high.refs_6_, bf16[256,128]{1,0:T(8,128)(2,1)S(1)} %get-tuple-element.70.phi_low.refs_7_, ...), custom_call_target="tpu_custom_call" | custom-call | flops 67108864 | bytes 1901056 | tf_op jit(solution)/shard_map/lin_forward/pallas_call | solution.py:66
  17.5 1.6 %collective-permute-start.9 = (bf16[256,512]{1,0:T(8,128)(2,1)S(1)}, bf16[256,512]{1,0:T(8,128)(2,1)S(1)}, u32[]{:S(2)}, u32[]{:S(2)}) collective-permute-start(bf16[256,512]{1,0:T(8,128)(2,1)S(1)} %get-tuple-element.74), channel_id=1, source_target_pairs={{0,8},{1,17},{8,0},{9,25},{16,24},{17,1},{24,16},{25,9},{2,10},{3,... | collective-permute-start | bytes 786440 | tf_op jit(solution)/shard_map/ppermute | solution.py:451
  19.1 0.1 collective-permute-start.6
  19.2 1.2 %collective-permute-done.6.got = bf16[2,64,256]{2,1,0:T(8,128)(2,1)S(1)} collective-permute-done((bf16[2,64,256]{2,1,0:T(8,128)(2,1)S(1)}, bf16[2,64,256]{2,1,0:T(8,128)(2,1)S(1)}, u32[]{:S(2)}, u32[]{:S(2)}) %collective-permute-start.6) | collective-permute-done | bytes 65568 | tf_op jit(solution)/shard_map/ppermute | solution.py:434
  20.4 0.6 %collective-permute-start.7 = (bf16[256,256]{1,0:T(8,128)(2,1)S(1)}, bf16[256,256]{1,0:T(8,128)(2,1)S(1)}, u32[]{:S(2)}, u32[]{:S(2)}) collective-permute-start(bf16[256,256]{1,0:T(8,128)(2,1)S(1)} %w_rows.1.first), channel_id=1, source_target_pairs={{0,8},{1,17},{8,0},{9,25},{16,24},{17,1},{24,16},{25,9},{2,10},{3,... | collective-permute-start | bytes 393224 | tf_op jit(solution)/shard_map/ppermute | solution.py:451
  21.0 2.9 %collective-permute-done.9.got = bf16[256,512]{1,0:T(8,128)(2,1)S(1)} collective-permute-done((bf16[256,512]{1,0:T(8,128)(2,1)S(1)}, bf16[256,512]{1,0:T(8,128)(2,1)S(1)}, u32[]{:S(2)}, u32[]{:S(2)}) %collective-permute-start.9) | collective-permute-done | bytes 262176 | tf_op jit(solution)/shard_map/ppermute | solution.py:451
  23.9 0.1 fold.1
  24.0 1.8 %collective-permute-start.11 = (bf16[256,256]{1,0:T(8,128)(2,1)S(1)}, bf16[256,256]{1,0:T(8,128)(2,1)S(1)}, u32[]{:S(2)}, u32[]{:S(2)}) collective-permute-start(bf16[256,256]{1,0:T(8,128)(2,1)S(1)} %get-tuple-element.75.refs_0_), channel_id=1, source_target_pairs={{0,16},{1,9},{8,24},{9,1},{16,0},{17,25},{24,8},{25,17},{2,18},{3,... | collective-permute-start | bytes 393224 | tf_op jit(solution)/shard_map/ppermute | solution.py:451
  25.8 0.5 %collective-permute-done.7.second = bf16[256,256]{1,0:T(8,128)(2,1)S(1)} collective-permute-done((bf16[256,256]{1,0:T(8,128)(2,1)S(1)}, bf16[256,256]{1,0:T(8,128)(2,1)S(1)}, u32[]{:S(2)}, u32[]{:S(2)}) %collective-permute-start.7) | collective-permute-done | bytes 131104 | tf_op jit(solution)/shard_map/ppermute | solution.py:451
  26.4 1.9 %collective-permute-start.10 = (bf16[256,512]{1,0:T(8,128)(2,1)S(1)}, bf16[256,512]{1,0:T(8,128)(2,1)S(1)}, u32[]{:S(2)}, u32[]{:S(2)}) collective-permute-start(bf16[256,512]{1,0:T(8,128)(2,1)S(1)} %w_half.1.refs_0_), channel_id=1, source_target_pairs={{0,16},{1,9},{8,24},{9,1},{16,0},{17,25},{24,8},{25,17},{2,18},{3,... | collective-permute-start | bytes 786440 | tf_op jit(solution)/shard_map/ppermute | solution.py:451
  28.4 0.7 %collective-permute-done.11.got = bf16[256,256]{1,0:T(8,128)(2,1)S(1)} collective-permute-done((bf16[256,256]{1,0:T(8,128)(2,1)S(1)}, bf16[256,256]{1,0:T(8,128)(2,1)S(1)}, u32[]{:S(2)}, u32[]{:S(2)}) %collective-permute-start.11) | collective-permute-done | bytes 131104 | tf_op jit(solution)/shard_map/ppermute | solution.py:451
  29.0 0.1 rows.1
  29.1 0.1 collective-permute-start.12
  29.2 1.3 %collective-permute-done.12.got = f32[128,256]{1,0:T(8,128)S(1)} collective-permute-done((f32[128,256]{1,0:T(8,128)S(1)}, f32[128,256]{1,0:T(8,128)S(1)}, u32[]{:S(2)}, u32[]{:S(2)}) %collective-permute-start.12) | collective-permute-done | bytes 131104 | tf_op jit(solution)/shard_map/ppermute | solution.py:434
  30.5 0.8 %collective-permute-start.13 = (bf16[128,256]{1,0:T(8,128)(2,1)S(1)}, bf16[128,256]{1,0:T(8,128)(2,1)S(1)}, u32[]{:S(2)}, u32[]{:S(2)}) collective-permute-start(bf16[128,256]{1,0:T(8,128)(2,1)S(1)} %get-tuple-element.92), channel_id=1, source_target_pairs={{0,2},{1,7},{2,0},{3,5},{4,6},{5,3},{6,4},{7,1},{8,10},{9,15},{10,... | collective-permute-start | bytes 196616 | tf_op jit(solution)/shard_map/ppermute | solution.py:445
  31.4 1.5 %collective-permute-done.10.refs_1_ = bf16[256,512]{1,0:T(8,128)(2,1)S(1)} collective-permute-done((bf16[256,512]{1,0:T(8,128)(2,1)S(1)}, bf16[256,512]{1,0:T(8,128)(2,1)S(1)}, u32[]{:S(2)}, u32[]{:S(2)}) %collective-permute-start.10) | collective-permute-done | bytes 262176 | tf_op jit(solution)/shard_map/ppermute | solution.py:451
  32.8 1.5 %backward.1 = (bf16[256,128]{1,0:T(8,128)(2,1)S(1)}, f32[128,128]{1,0:T(8,128)S(1)}, f32[256,128]{1,0:T(8,128)S(1)}, f32[512,128]{1,0:T(8,128)S(1)}, f32[512,128]{1,0:T(8,128)S(1)}) custom-call(bf16[256,512]{1,0:T(8,128)(2,1)S(1)} %w_half.1.refs_0_, bf16[256,512]{1,0:T(8,128)(2,1)S(1)} %collective-permute-done.10.refs_1_, ...), custom_call_target="tpu_custom_call" | custom-call | flops 335544320 | bytes 3277312 | tf_op jit(solution)/shard_map/backward/pallas_call | solution.py:66
  34.3 0.5 %collective-permute-done.13.got = bf16[128,256]{1,0:T(8,128)(2,1)S(1)} collective-permute-done((bf16[128,256]{1,0:T(8,128)(2,1)S(1)}, bf16[128,256]{1,0:T(8,128)(2,1)S(1)}, u32[]{:S(2)}, u32[]{:S(2)}) %collective-permute-start.13) | collective-permute-done | bytes 65568 | tf_op jit(solution)/shard_map/ppermute | solution.py:445
  34.9 2.7 %collective-permute-start.16 = (bf16[128,256]{1,0:T(8,128)(2,1)S(1)}, bf16[128,256]{1,0:T(8,128)(2,1)S(1)}, u32[]{:S(2)}, u32[]{:S(2)}) collective-permute-start(bf16[128,256]{1,0:T(8,128)(2,1)S(1)} %get-tuple-element.95), channel_id=1, source_target_pairs={{0,4},{1,5},{2,6},{3,7},{4,0},{5,1},{6,2},{7,3},{8,12},{9,13},{10,... | collective-permute-start | bytes 196616 | tf_op jit(solution)/shard_map/ppermute | solution.py:445
  37.7 1.0 %collective-permute-start.14 = (bf16[128,384]{1,0:T(8,128)(2,1)S(1)}, bf16[128,384]{1,0:T(8,128)(2,1)S(1)}, u32[]{:S(2)}, u32[]{:S(2)}) collective-permute-start(bf16[128,384]{1,0:T(8,128)(2,1)S(1)} %get-tuple-element.93), channel_id=1, source_target_pairs={{0,2},{1,7},{2,0},{3,5},{4,6},{5,3},{6,4},{7,1},{8,10},{9,15},{10,... | collective-permute-start | bytes 294920 | tf_op jit(solution)/shard_map/ppermute | solution.py:445
  38.7 0.7 %collective-permute-start.15 = (bf16[128,384]{1,0:T(8,128)(2,1)S(1)}, bf16[128,384]{1,0:T(8,128)(2,1)S(1)}, u32[]{:S(2)}, u32[]{:S(2)}) collective-permute-start(bf16[128,384]{1,0:T(8,128)(2,1)S(1)} %get-tuple-element.94), channel_id=1, source_target_pairs={{0,6},{1,3},{2,4},{3,1},{4,2},{5,7},{6,0},{7,5},{8,14},{9,11},{10,... | collective-permute-start | bytes 294920 | tf_op jit(solution)/shard_map/ppermute | solution.py:445
  39.4 3.9 %collective-permute-done.16.got.refs_0_ = bf16[128,256]{1,0:T(8,128)(2,1)S(1)} collective-permute-done((bf16[128,256]{1,0:T(8,128)(2,1)S(1)}, bf16[128,256]{1,0:T(8,128)(2,1)S(1)}, u32[]{:S(2)}, u32[]{:S(2)}) %collective-permute-start.16) | collective-permute-done | bytes 65568 | tf_op jit(solution)/shard_map/ppermute | solution.py:445
  43.3 1.3 %collective-permute-start.17 = (bf16[64,256]{1,0:T(8,128)(2,1)S(1)}, bf16[64,256]{1,0:T(8,128)(2,1)S(1)}, u32[]{:S(2)}, u32[]{:S(2)}) collective-permute-start(bf16[64,256]{1,0:T(8,128)(2,1)S(1)} %weight_sum.1.first), channel_id=1, source_target_pairs={{0,8},{1,17},{8,0},{9,25},{16,24},{17,1},{24,16},{25,9},{2,10},{3,... | collective-permute-start | bytes 98312 | tf_op jit(solution)/shard_map/ppermute | solution.py:451
  44.6 2.7 %collective-permute-done.17.second = bf16[64,256]{1,0:T(8,128)(2,1)S(1)} collective-permute-done((bf16[64,256]{1,0:T(8,128)(2,1)S(1)}, bf16[64,256]{1,0:T(8,128)(2,1)S(1)}, u32[]{:S(2)}, u32[]{:S(2)}) %collective-permute-start.17) | collective-permute-done | bytes 32800 | tf_op jit(solution)/shard_map/ppermute | solution.py:451
  47.3 0.0 collective-permute-done.14.a
  47.3 0.0 collective-permute-done.15.b
  47.3 0.4 final.1
  47.7 0.1 collective-permute-start.18
  47.8 1.9 %collective-permute-start.19 = (bf16[64,512]{1,0:T(8,128)(2,1)S(1)}, bf16[64,512]{1,0:T(8,128)(2,1)S(1)}, u32[]{:S(2)}, u32[]{:S(2)}) collective-permute-start(bf16[64,512]{1,0:T(8,128)(2,1)S(1)} %both.1.refs_1_), channel_id=1, source_target_pairs={{0,16},{1,9},{8,24},{9,1},{16,0},{17,25},{24,8},{25,17},{2,18},{3,... | collective-permute-start | bytes 196616 | tf_op jit(solution)/shard_map/ppermute | solution.py:451
  49.7 0.0 collective-permute-done.18.pair
  49.7 0.8 %outputs.1 = (bf16[1,128,512]{2,1,0:T(8,128)(2,1)}, bf16[1,128,512]{2,1,0:T(8,128)(2,1)}, bf16[1,128,512]{2,1,0:T(8,128)(2,1)}) custom-call(bf16[128,768]{1,0:T(8,128)(2,1)S(1)} %get-tuple-element.97.own, bf16[128,768]{1,0:T(8,128)(2,1)S(1)} %collective-permute-done.18.pair), custom_call_target="tpu_custom_call" | custom-call | bytes 786432 | tf_op jit(solution)/shard_map/outputs/pallas_call | solution.py:66
  50.5 1.6 %collective-permute-done.19.got = bf16[64,512]{1,0:T(8,128)(2,1)S(1)} collective-permute-done((bf16[64,512]{1,0:T(8,128)(2,1)S(1)}, bf16[64,512]{1,0:T(8,128)(2,1)S(1)}, u32[]{:S(2)}, u32[]{:S(2)}) %collective-permute-start.19) | collective-permute-done | bytes 65568 | tf_op jit(solution)/shard_map/ppermute | solution.py:451
  52.1 0.7 %weight_join.1 = f32[64,1024]{1,0:T(8,128)} custom-call(bf16[64,512]{1,0:T(8,128)(2,1)S(1)} %both.1.refs_1_, bf16[64,512]{1,0:T(8,128)(2,1)S(1)} %collective-permute-done.19.got, bf16[1,128,512]{2,1,0:T(8,128)(2,1)} %get-tuple-element.49._), custom_call_target="tpu_custom_call" | custom-call | bytes 524288 | tf_op jit(solution)/shard_map/weight_join/pallas_call | solution.py:66
  (7 shorter events, 0.2 us)
Async XLA Ops:
  0.6 2.3 %collective-permute-start = (bf16[1,128,512]{2,1,0:T(8,128)(2,1)}, bf16[1,128,512]{2,1,0:T(8,128)(2,1)S(1)}, u32[]{:S(2)}, u32[]{:S(2)}) collective-permute-start(bf16[1,128,512]{2,1,0:T(8,128)(2,1)} %q.1), channel_id=1, source_target_pairs={{0,1},{1,0},{2,3},{3,2},{4,5},{5,4},{6,7},{7,6},{8,9},{9,8},{10,11... | collective-permute-start | bytes 393224 | tf_op jit(solution)/shard_map/ppermute | solution.py:434
  1.2 1.8 %collective-permute-start.1 = (bf16[1,128,512]{2,1,0:T(8,128)(2,1)}, bf16[1,128,512]{2,1,0:T(8,128)(2,1)S(1)}, u32[]{:S(2)}, u32[]{:S(2)}) collective-permute-start(bf16[1,128,512]{2,1,0:T(8,128)(2,1)} %k.1), channel_id=1, source_target_pairs={{0,1},{1,0},{2,3},{3,2},{4,5},{5,4},{6,7},{7,6},{8,9},{9,8},{10,11... | collective-permute-start | bytes 393224 | tf_op jit(solution)/shard_map/ppermute | solution.py:434
  1.2 1.7 %collective-permute-start.2 = (bf16[1,128,512]{2,1,0:T(8,128)(2,1)}, bf16[1,128,512]{2,1,0:T(8,128)(2,1)S(1)}, u32[]{:S(2)}, u32[]{:S(2)}) collective-permute-start(bf16[1,128,512]{2,1,0:T(8,128)(2,1)} %v.1), channel_id=1, source_target_pairs={{0,1},{1,0},{2,3},{3,2},{4,5},{5,4},{6,7},{7,6},{8,9},{9,8},{10,11... | collective-permute-start | bytes 393224 | tf_op jit(solution)/shard_map/ppermute | solution.py:434
  1.7 7.2 %collective-permute-start.8 = (bf16[128,1024]{1,0:T(8,128)(2,1)}, bf16[128,1024]{1,0:T(8,128)(2,1)S(1)}, u32[]{:S(2)}, u32[]{:S(2)}) collective-permute-start(bf16[128,1024]{1,0:T(8,128)(2,1)} %bitcast.1), channel_id=1, source_target_pairs={{0,1},{1,0},{2,3},{3,2},{4,5},{5,4},{6,7},{7,6},{8,9},{9,8},{10,11... | collective-permute-start | bytes 786440 | tf_op jit(solution)/shard_map/ppermute | solution.py:434
  3.2 6.0 %collective-permute-start.3 = (bf16[128,512]{1,0:T(8,128)(2,1)S(1)}, bf16[128,512]{1,0:T(8,128)(2,1)S(1)}, u32[]{:S(2)}, u32[]{:S(2)}) collective-permute-start(bf16[128,512]{1,0:T(8,128)(2,1)S(1)} %get-tuple-element.55), channel_id=1, source_target_pairs={{0,2},{1,7},{2,0},{3,5},{4,6},{5,3},{6,4},{7,1},{8,10},{9,15},{10,... | collective-permute-start | bytes 393224 | tf_op jit(solution)/shard_map/ppermute | solution.py:445
  6.3 9.4 %collective-permute-start.4 = (bf16[128,512]{1,0:T(8,128)(2,1)S(1)}, bf16[128,512]{1,0:T(8,128)(2,1)S(1)}, u32[]{:S(2)}, u32[]{:S(2)}) collective-permute-start(bf16[128,512]{1,0:T(8,128)(2,1)S(1)} %get-tuple-element.56), channel_id=1, source_target_pairs={{0,6},{1,3},{2,4},{3,1},{4,2},{5,7},{6,0},{7,5},{8,14},{9,11},{10,... | collective-permute-start | bytes 393224 | tf_op jit(solution)/shard_map/ppermute | solution.py:445
  8.8 8.1 %collective-permute-start.5 = (bf16[128,256]{1,0:T(8,128)(2,1)S(1)}, bf16[128,256]{1,0:T(8,128)(2,1)S(1)}, u32[]{:S(2)}, u32[]{:S(2)}) collective-permute-start(bf16[128,256]{1,0:T(8,128)(2,1)S(1)} %get-tuple-element.57), channel_id=1, source_target_pairs={{0,4},{1,5},{2,6},{3,7},{4,0},{5,1},{6,2},{7,3},{8,12},{9,13},{10,... | collective-permute-start | bytes 196616 | tf_op jit(solution)/shard_map/ppermute | solution.py:445
  17.5 6.4 %collective-permute-start.9 = (bf16[256,512]{1,0:T(8,128)(2,1)S(1)}, bf16[256,512]{1,0:T(8,128)(2,1)S(1)}, u32[]{:S(2)}, u32[]{:S(2)}) collective-permute-start(bf16[256,512]{1,0:T(8,128)(2,1)S(1)} %get-tuple-element.74), channel_id=1, source_target_pairs={{0,8},{1,17},{8,0},{9,25},{16,24},{17,1},{24,16},{25,9},{2,10},{3,... | collective-permute-start | bytes 786440 | tf_op jit(solution)/shard_map/ppermute | solution.py:451
  19.1 1.3 %collective-permute-start.6 = (bf16[2,64,256]{2,1,0:T(8,128)(2,1)S(1)}, bf16[2,64,256]{2,1,0:T(8,128)(2,1)S(1)}, u32[]{:S(2)}, u32[]{:S(2)}) collective-permute-start(bf16[2,64,256]{2,1,0:T(8,128)(2,1)S(1)} %get-tuple-element.59), channel_id=1, source_target_pairs={{0,1},{1,0},{2,3},{3,2},{4,5},{5,4},{6,7},{7,6},{8,9},{9,8},{10,11... | collective-permute-start | bytes 196616 | tf_op jit(solution)/shard_map/ppermute | solution.py:434
  20.4 5.9 %collective-permute-start.7 = (bf16[256,256]{1,0:T(8,128)(2,1)S(1)}, bf16[256,256]{1,0:T(8,128)(2,1)S(1)}, u32[]{:S(2)}, u32[]{:S(2)}) collective-permute-start(bf16[256,256]{1,0:T(8,128)(2,1)S(1)} %w_rows.1.first), channel_id=1, source_target_pairs={{0,8},{1,17},{8,0},{9,25},{16,24},{17,1},{24,16},{25,9},{2,10},{3,... | collective-permute-start | bytes 393224 | tf_op jit(solution)/shard_map/ppermute | solution.py:451
  24.0 5.0 %collective-permute-start.11 = (bf16[256,256]{1,0:T(8,128)(2,1)S(1)}, bf16[256,256]{1,0:T(8,128)(2,1)S(1)}, u32[]{:S(2)}, u32[]{:S(2)}) collective-permute-start(bf16[256,256]{1,0:T(8,128)(2,1)S(1)} %get-tuple-element.75.refs_0_), channel_id=1, source_target_pairs={{0,16},{1,9},{8,24},{9,1},{16,0},{17,25},{24,8},{25,17},{2,18},{3,... | collective-permute-start | bytes 393224 | tf_op jit(solution)/shard_map/ppermute | solution.py:451
  26.4 6.4 %collective-permute-start.10 = (bf16[256,512]{1,0:T(8,128)(2,1)S(1)}, bf16[256,512]{1,0:T(8,128)(2,1)S(1)}, u32[]{:S(2)}, u32[]{:S(2)}) collective-permute-start(bf16[256,512]{1,0:T(8,128)(2,1)S(1)} %w_half.1.refs_0_), channel_id=1, source_target_pairs={{0,16},{1,9},{8,24},{9,1},{16,0},{17,25},{24,8},{25,17},{2,18},{3,... | collective-permute-start | bytes 786440 | tf_op jit(solution)/shard_map/ppermute | solution.py:451
  29.1 1.4 %collective-permute-start.12 = (f32[128,256]{1,0:T(8,128)S(1)}, f32[128,256]{1,0:T(8,128)S(1)}, u32[]{:S(2)}, u32[]{:S(2)}) collective-permute-start(f32[128,256]{1,0:T(8,128)S(1)} %get-tuple-element.78), channel_id=1, source_target_pairs={{0,1},{1,0},{2,3},{3,2},{4,5},{5,4},{6,7},{7,6},{8,9},{9,8},{10,11... | collective-permute-start | bytes 393224 | tf_op jit(solution)/shard_map/ppermute | solution.py:434
  30.5 4.3 %collective-permute-start.13 = (bf16[128,256]{1,0:T(8,128)(2,1)S(1)}, bf16[128,256]{1,0:T(8,128)(2,1)S(1)}, u32[]{:S(2)}, u32[]{:S(2)}) collective-permute-start(bf16[128,256]{1,0:T(8,128)(2,1)S(1)} %get-tuple-element.92), channel_id=1, source_target_pairs={{0,2},{1,7},{2,0},{3,5},{4,6},{5,3},{6,4},{7,1},{8,10},{9,15},{10,... | collective-permute-start | bytes 196616 | tf_op jit(solution)/shard_map/ppermute | solution.py:445
  34.9 8.4 %collective-permute-start.16 = (bf16[128,256]{1,0:T(8,128)(2,1)S(1)}, bf16[128,256]{1,0:T(8,128)(2,1)S(1)}, u32[]{:S(2)}, u32[]{:S(2)}) collective-permute-start(bf16[128,256]{1,0:T(8,128)(2,1)S(1)} %get-tuple-element.95), channel_id=1, source_target_pairs={{0,4},{1,5},{2,6},{3,7},{4,0},{5,1},{6,2},{7,3},{8,12},{9,13},{10,... | collective-permute-start | bytes 196616 | tf_op jit(solution)/shard_map/ppermute | solution.py:445
  37.7 9.7 %collective-permute-start.14 = (bf16[128,384]{1,0:T(8,128)(2,1)S(1)}, bf16[128,384]{1,0:T(8,128)(2,1)S(1)}, u32[]{:S(2)}, u32[]{:S(2)}) collective-permute-start(bf16[128,384]{1,0:T(8,128)(2,1)S(1)} %get-tuple-element.93), channel_id=1, source_target_pairs={{0,2},{1,7},{2,0},{3,5},{4,6},{5,3},{6,4},{7,1},{8,10},{9,15},{10,... | collective-permute-start | bytes 294920 | tf_op jit(solution)/shard_map/ppermute | solution.py:445
  38.7 8.7 %collective-permute-start.15 = (bf16[128,384]{1,0:T(8,128)(2,1)S(1)}, bf16[128,384]{1,0:T(8,128)(2,1)S(1)}, u32[]{:S(2)}, u32[]{:S(2)}) collective-permute-start(bf16[128,384]{1,0:T(8,128)(2,1)S(1)} %get-tuple-element.94), channel_id=1, source_target_pairs={{0,6},{1,3},{2,4},{3,1},{4,2},{5,7},{6,0},{7,5},{8,14},{9,11},{10,... | collective-permute-start | bytes 294920 | tf_op jit(solution)/shard_map/ppermute | solution.py:445
  43.3 4.0 %collective-permute-start.17 = (bf16[64,256]{1,0:T(8,128)(2,1)S(1)}, bf16[64,256]{1,0:T(8,128)(2,1)S(1)}, u32[]{:S(2)}, u32[]{:S(2)}) collective-permute-start(bf16[64,256]{1,0:T(8,128)(2,1)S(1)} %weight_sum.1.first), channel_id=1, source_target_pairs={{0,8},{1,17},{8,0},{9,25},{16,24},{17,1},{24,16},{25,9},{2,10},{3,... | collective-permute-start | bytes 98312 | tf_op jit(solution)/shard_map/ppermute | solution.py:451
  47.7 2.0 %collective-permute-start.18 = (bf16[128,768]{1,0:T(8,128)(2,1)S(1)}, bf16[128,768]{1,0:T(8,128)(2,1)S(1)}, u32[]{:S(2)}, u32[]{:S(2)}) collective-permute-start(bf16[128,768]{1,0:T(8,128)(2,1)S(1)} %get-tuple-element.98), channel_id=1, source_target_pairs={{0,1},{1,0},{2,3},{3,2},{4,5},{5,4},{6,7},{7,6},{8,9},{9,8},{10,11... | collective-permute-start | bytes 589832 | tf_op jit(solution)/shard_map/ppermute | solution.py:434
  47.8 4.3 %collective-permute-start.19 = (bf16[64,512]{1,0:T(8,128)(2,1)S(1)}, bf16[64,512]{1,0:T(8,128)(2,1)S(1)}, u32[]{:S(2)}, u32[]{:S(2)}) collective-permute-start(bf16[64,512]{1,0:T(8,128)(2,1)S(1)} %both.1.refs_1_), channel_id=1, source_target_pairs={{0,16},{1,9},{8,24},{9,1},{16,0},{17,25},{24,8},{25,17},{2,18},{3,... | collective-permute-start | bytes 196616 | tf_op jit(solution)/shard_map/ppermute | solution.py:451

commit v22 on v20

--- a/solution.py
+++ b/solution.py
@@ -344,27 +344,24 @@
         keep[index * half : (index + 1) * half, :] = heads[z ^ step]
 
 
-def second_kernel(keep, got, dstate, dk_soft, dv_soft, chunk, to_a, to_b, to_c):
-    way = links(True)
+def second_kernel(keep, got, chunk, send):
     half = chunk.shape[0]
     chunk[...] = keep[:half, :] + got[:half, :].astype(F32)
-    for side in range(2):
-        cols, rows = slice(side * DH, (side + 1) * DH), slice(side * half, (side + 1) * half)
-        piece = keep[half:, cols] + got[half:, cols].astype(F32)
-        to_c[rows, DH:] = piece.astype(BF)
+    send[...] = (keep[half:, :] + got[half:, :].astype(F32)).astype(BF)
+
+
+def halo_direct_kernel(dstate, dk_soft, dv_soft, to_a, to_b, to_c):
+    way = links(True)
     halo_part(to_a, 0, dk_soft, dv_soft, way["halo_a"])
     halo_part(to_b, 0, dk_soft, dv_soft, way["halo_b"])
     low = dstate[...].astype(BF)
     to_a[:, 2 * DH :] = low
     to_b[:, 2 * DH :] = low
-    to_c[:, :DH] = low
+    to_c[...] = low
 
 
 def weight_sum_kernel(scale, chunk, got, summed):
-    half = chunk.shape[0]
-    for side in range(2):
-        cols, rows = slice(side * DH, (side + 1) * DH), slice(side * half, (side + 1) * half)
-        summed[:, cols] = (scale * (chunk[:, cols] + got[rows, DH:].astype(F32))).astype(summed.dtype)
+    summed[...] = (scale * (chunk[...] + got[...].astype(F32))).astype(summed.dtype)
 
 
 def final_kernel(
@@ -377,7 +374,7 @@
     own_out, pair_out, dk_all, dv_all = refs[-4:]
     if direct:
         total = total + a[:, 2 * DH :].astype(F32) + b[:, 2 * DH :].astype(F32)
-        total = total + refs[0][:, :DH].astype(F32)
+        total = total + refs[0][...].astype(F32)
     for source, out, cols in ((dk_soft, dk_all, slice(0, DH)), (dv_soft, dv_all, slice(DH, 2 * DH))):
         out[...] = source[HALF : HALF + 2 * rows, :]
         out[at(way["block_a"] * rows, rows), :] += a[:, cols].astype(F32)
@@ -546,19 +543,19 @@
     )
     wide = 3 * DH if direct else 2 * DH
     if direct:
-        chunk, to_a, to_b, to_c = call(
-            second_kernel, "second",
-            [
-                like((half, width), F32), like((rows, 3 * DH), BF), like((rows, 3 * DH), BF),
-                like((rows, 2 * DH), BF),
-            ],
-            [piece_keep, piece_got, dstate, dk_soft, dv_soft],
+        chunk, piece = call(
+            second_kernel, "second", [like((half, width), F32), like((half, width), BF)],
+            [piece_keep, piece_got],
+        )
+        summed = call(
+            functools.partial(weight_sum_kernel, scale), "weight_sum", [like((half, width), BF)],
+            [chunk, over_z(piece, 2)],
+        )[0]
+        to_a, to_b, to_c = call(
+            halo_direct_kernel, "halo", [like((rows, 3 * DH), BF)] * 2 + [like((DH, DH), BF)],
+            [dstate, dk_soft, dv_soft],
         )
         a, b, c = over_z(to_a, 0), over_z(to_b, 1), [over_z(to_c, 2)]
-        summed = call(
-            functools.partial(weight_sum_kernel, scale), "weight_sum", [like((half, width), BF)],
-            [chunk] + c,
-        )[0]
         got = over_dp(summed, 0)
         both = call(join_kernel, "both", [like((half, 2 * width), BF)], [summed, got])[0]
         gathered = over_dp(both, 1)
@@ -577,7 +574,7 @@
         functools.partial(final_kernel, direct), "final",
         [like((rows, 6 * DH), BF), like((rows, 6 * DH), BF)],
         [dstate, mine, pair, dq_soft, dk_soft, dv_soft, dq_lin, a, b]
-        + (c + [both] if direct else []),
+        + (c + [gathered] if direct else []),
         scratch=[pltpu.VMEM((2 * rows, DH), F32)] * 2,
         flops=wg_flops // 4,
     )

time: 53.1 us -> 56 us (1.055)
  starting transfers between devices: 21.4 us -> 25.1 us
  waiting for transfers between devices: 23.6 us -> 22.8 us
    ppermute x6, waiting for transfers between devices: 9.9 us -> 4.13 us  [over_dp(): return lax.ppermute(value, ('dp', 'core'), pairs)]
    ppermute x7 -> x8, waiting for transfers between devices: 11.1 us -> 14.7 us  [over_z(): return lax.ppermute(value, axes, pairs)]
    ppermute x7 -> x8, starting transfers between devices: 10.9 us -> 14.2 us  [over_z(): return lax.ppermute(value, axes, pairs)]
    ppermute x7, waiting for transfers between devices: 2.59 us -> 4.01 us  [over_core(): return lax.ppermute(value, 'core', pair_perm)]
    pallas_call x18 -> x19, Pallas kernels: 7.21 us -> 7.21 us  [call(): pl.pallas_call(kernel, name=name, out_shape=list(outs), in_specs=spaces o...]
  transfers between devices with their start and end apart: 20 -> 21, of which waited for: 12 -> 11; matrix products, arithmetic and copies ran while one was open for 0% -> 0% of each run, Pallas kernels for 10% -> 8%
where the time goes in v22:
time: 56 us; the launch traced here: 55.9 us
  starting transfers between devices  25.1 us (45%)
  waiting for transfers between devices  22.8 us (41%)
  Pallas kernels  7.21 us (13%)
  between operations  0.79 us (1%)
    ppermute x8, waiting for transfers between devices, over_z(): return lax.ppermute(value, axes, pairs)  14.7 us
    ppermute x8, starting transfers between devices, over_z(): return lax.ppermute(value, axes, pairs)  14.2 us
    ppermute x6, starting transfers between devices, over_dp(): return lax.ppermute(value, ('dp', 'core'), pairs)  9.6 us
    pallas_call x19, Pallas kernels, call(): pl.pallas_call(kernel, name=name, out_shape=list(outs), in_specs=spaces o...  7.21 us
    ppermute x6, waiting for transfers between devices, over_dp(): return lax.ppermute(value, ('dp', 'core'), pairs)  4.13 us
    ppermute x7, waiting for transfers between devices, over_core(): return lax.ppermute(value, 'core', pair_perm)  4.01 us
    ppermute x7, starting transfers between devices, over_core(): return lax.ppermute(value, 'core', pair_perm)  1.32 us
  transfers between devices with their start and end apart: 21, of which 11 were waited for; matrix products, arithmetic and copies ran while one was open for 0% of the time, Pallas kernels for 8%

profile of v22, /device:TPU:0, one launch (start us, length us, event | category | flops | bytes accessed | tf_op | source)
XLA Modules:
  0.0 55.9 jit_solution(13186548162052490210)
XLA Ops:
  0.6 0.5 collective-permute-start
  1.2 0.1 collective-permute-start.1
  1.2 0.4 collective-permute-start.2
  1.7 0.1 collective-permute-start.8
  1.7 1.2 %pack.1 = (bf16[128,768]{1,0:T(8,128)(2,1)S(1)}, bf16[128,1024]{1,0:T(8,128)(2,1)S(1)}, bf16[64,256]{1,0:T(8,128)(2,1)S(1)}, f32[1,128]{1,0:T(1,128)S(1)}) custom-call(bf16[1,128,512]{2,1,0:T(8,128)(2,1)} %q.1, bf16[1,128,512]{2,1,0:T(8,128)(2,1)} %k.1, bf16[1,128,512]{2,1,0:T(8,128)(2,1)} %v.1, bf16[1,128,1024]{2,1,0:T(8,128)(2,1)} %og.1, ...), custom_call_target="tpu_custom_call" | custom-call | bytes 1279488 | tf_op jit(solution)/shard_map/pack/pallas_call | solution.py:66
  2.9 0.0 collective-permute-done.q_pair
  2.9 0.0 collective-permute-done.1.k_pair
  2.9 0.0 collective-permute-done.2.v_pair
  3.0 0.3 state.1
  3.2 3.1 %collective-permute-start.3 = (bf16[128,512]{1,0:T(8,128)(2,1)S(1)}, bf16[128,512]{1,0:T(8,128)(2,1)S(1)}, u32[]{:S(2)}, u32[]{:S(2)}) collective-permute-start(bf16[128,512]{1,0:T(8,128)(2,1)S(1)} %get-tuple-element.56), channel_id=1, source_target_pairs={{0,2},{1,7},{2,0},{3,5},{4,6},{5,3},{6,4},{7,1},{8,10},{9,15},{10,... | collective-permute-start | bytes 393224 | tf_op jit(solution)/shard_map/ppermute | solution.py:433
  6.3 2.5 %collective-permute-start.4 = (bf16[128,512]{1,0:T(8,128)(2,1)S(1)}, bf16[128,512]{1,0:T(8,128)(2,1)S(1)}, u32[]{:S(2)}, u32[]{:S(2)}) collective-permute-start(bf16[128,512]{1,0:T(8,128)(2,1)S(1)} %get-tuple-element.57), channel_id=1, source_target_pairs={{0,6},{1,3},{2,4},{3,1},{4,2},{5,7},{6,0},{7,5},{8,14},{9,11},{10,... | collective-permute-start | bytes 393224 | tf_op jit(solution)/shard_map/ppermute | solution.py:433
  8.8 0.1 collective-permute-start.5
  8.9 0.0 collective-permute-done.8.og_recv
  8.9 0.3 prep.1
  9.2 0.1 collective-permute-done.3.a.refs_0_
  9.3 6.5 %collective-permute-done.4.b.refs_1_ = bf16[128,512]{1,0:T(8,128)(2,1)S(1)} collective-permute-done((bf16[128,512]{1,0:T(8,128)(2,1)S(1)}, bf16[128,512]{1,0:T(8,128)(2,1)S(1)}, u32[]{:S(2)}, u32[]{:S(2)}) %collective-permute-start.4) | collective-permute-done | bytes 131104 | tf_op jit(solution)/shard_map/ppermute | solution.py:433
  15.7 1.2 %soft_forward.1 = (bf16[512,128]{1,0:T(8,128)(2,1)S(1)}, bf16[512,128]{1,0:T(8,128)(2,1)S(1)}, f32[2,128,384]{2,1,0:T(8,128)S(1)}, f32[256,128]{1,0:T(8,128)S(1)...) custom-call(bf16[256,128]{1,0:T(8,128)(2,1)S(1)} %get-tuple-element.63.qs.refs_10_, ...), custom_call_target="tpu_custom_call" | custom-call | flops 67108864 | bytes 2424832 | tf_op jit(solution)/shard_map/soft_forward/pallas_call | solution.py:66
  16.9 0.0 collective-permute-done.5.c.refs_2_
  16.9 0.7 %lin_forward.1 = (f32[256,128]{1,0:T(8,128)S(1)}, f32[128,128]{1,0:T(8,128)S(1)}, f32[128,512]{1,0:T(8,128)S(1)}, bf16[256,512]{1,0:T(8,128)(2,1)S(1)}) custom-call(f32[128,128]{1,0:T(8,128)S(1)} %get-tuple-element.69.state, bf16[256,128]{1,0:T(8,128)(2,1)S(1)} %get-tuple-element.70.phi_high.refs_6_, bf16[256,128]{1,0:T(8,128)(2,1)S(1)} %get-tuple-element.71.phi_low.refs_7_, ...), custom_call_target="tpu_custom_call" | custom-call | flops 67108864 | bytes 1901056 | tf_op jit(solution)/shard_map/lin_forward/pallas_call | solution.py:66
  17.6 1.6 %collective-permute-start.9 = (bf16[256,512]{1,0:T(8,128)(2,1)S(1)}, bf16[256,512]{1,0:T(8,128)(2,1)S(1)}, u32[]{:S(2)}, u32[]{:S(2)}) collective-permute-start(bf16[256,512]{1,0:T(8,128)(2,1)S(1)} %get-tuple-element.75), channel_id=1, source_target_pairs={{0,8},{1,17},{8,0},{9,25},{16,24},{17,1},{24,16},{25,9},{2,10},{3,... | collective-permute-start | bytes 786440 | tf_op jit(solution)/shard_map/ppermute | solution.py:439
  19.2 0.1 collective-permute-start.6
  19.3 1.2 %collective-permute-done.6.got = bf16[2,64,256]{2,1,0:T(8,128)(2,1)S(1)} collective-permute-done((bf16[2,64,256]{2,1,0:T(8,128)(2,1)S(1)}, bf16[2,64,256]{2,1,0:T(8,128)(2,1)S(1)}, u32[]{:S(2)}, u32[]{:S(2)}) %collective-permute-start.6) | collective-permute-done | bytes 65568 | tf_op jit(solution)/shard_map/ppermute | solution.py:422
  20.5 0.6 %collective-permute-start.7 = (bf16[256,256]{1,0:T(8,128)(2,1)S(1)}, bf16[256,256]{1,0:T(8,128)(2,1)S(1)}, u32[]{:S(2)}, u32[]{:S(2)}) collective-permute-start(bf16[256,256]{1,0:T(8,128)(2,1)S(1)} %w_rows.1.first), channel_id=1, source_target_pairs={{0,8},{1,17},{8,0},{9,25},{16,24},{17,1},{24,16},{25,9},{2,10},{3,... | collective-permute-start | bytes 393224 | tf_op jit(solution)/shard_map/ppermute | solution.py:439
  21.1 2.9 %collective-permute-done.9.got = bf16[256,512]{1,0:T(8,128)(2,1)S(1)} collective-permute-done((bf16[256,512]{1,0:T(8,128)(2,1)S(1)}, bf16[256,512]{1,0:T(8,128)(2,1)S(1)}, u32[]{:S(2)}, u32[]{:S(2)}) %collective-permute-start.9) | collective-permute-done | bytes 262176 | tf_op jit(solution)/shard_map/ppermute | solution.py:439
  24.0 0.1 fold.1
  24.1 1.8 %collective-permute-start.11 = (bf16[256,256]{1,0:T(8,128)(2,1)S(1)}, bf16[256,256]{1,0:T(8,128)(2,1)S(1)}, u32[]{:S(2)}, u32[]{:S(2)}) collective-permute-start(bf16[256,256]{1,0:T(8,128)(2,1)S(1)} %get-tuple-element.76.refs_0_), channel_id=1, source_target_pairs={{0,16},{1,9},{8,24},{9,1},{16,0},{17,25},{24,8},{25,17},{2,18},{3,... | collective-permute-start | bytes 393224 | tf_op jit(solution)/shard_map/ppermute | solution.py:439
  25.9 0.5 collective-permute-done.7.second
  26.5 1.9 %collective-permute-start.10 = (bf16[256,512]{1,0:T(8,128)(2,1)S(1)}, bf16[256,512]{1,0:T(8,128)(2,1)S(1)}, u32[]{:S(2)}, u32[]{:S(2)}) collective-permute-start(bf16[256,512]{1,0:T(8,128)(2,1)S(1)} %w_half.1.refs_0_), channel_id=1, source_target_pairs={{0,16},{1,9},{8,24},{9,1},{16,0},{17,25},{24,8},{25,17},{2,18},{3,... | collective-permute-start | bytes 786440 | tf_op jit(solution)/shard_map/ppermute | solution.py:439
  28.5 0.7 %collective-permute-done.11.got = bf16[256,256]{1,0:T(8,128)(2,1)S(1)} collective-permute-done((bf16[256,256]{1,0:T(8,128)(2,1)S(1)}, bf16[256,256]{1,0:T(8,128)(2,1)S(1)}, u32[]{:S(2)}, u32[]{:S(2)}) %collective-permute-start.11) | collective-permute-done | bytes 131104 | tf_op jit(solution)/shard_map/ppermute | solution.py:439
  29.1 0.1 rows.1
  29.2 0.1 collective-permute-start.12
  29.3 1.3 %collective-permute-done.12.got = f32[128,256]{1,0:T(8,128)S(1)} collective-permute-done((f32[128,256]{1,0:T(8,128)S(1)}, f32[128,256]{1,0:T(8,128)S(1)}, u32[]{:S(2)}, u32[]{:S(2)}) %collective-permute-start.12) | collective-permute-done | bytes 131104 | tf_op jit(solution)/shard_map/ppermute | solution.py:422
  30.7 0.8 %collective-permute-start.16 = (bf16[128,256]{1,0:T(8,128)(2,1)S(1)}, bf16[128,256]{1,0:T(8,128)(2,1)S(1)}, u32[]{:S(2)}, u32[]{:S(2)}) collective-permute-start(bf16[128,256]{1,0:T(8,128)(2,1)S(1)} %get-tuple-element.96), channel_id=1, source_target_pairs={{0,2},{1,7},{2,0},{3,5},{4,6},{5,3},{6,4},{7,1},{8,10},{9,15},{10,... | collective-permute-start | bytes 196616 | tf_op jit(solution)/shard_map/ppermute | solution.py:433
  31.5 3.5 %collective-permute-done.16.got = bf16[128,256]{1,0:T(8,128)(2,1)S(1)} collective-permute-done((bf16[128,256]{1,0:T(8,128)(2,1)S(1)}, bf16[128,256]{1,0:T(8,128)(2,1)S(1)}, u32[]{:S(2)}, u32[]{:S(2)}) %collective-permute-start.16) | collective-permute-done | bytes 65568 | tf_op jit(solution)/shard_map/ppermute | solution.py:433
  35.0 2.7 %collective-permute-start.17 = (bf16[64,256]{1,0:T(8,128)(2,1)S(1)}, bf16[64,256]{1,0:T(8,128)(2,1)S(1)}, u32[]{:S(2)}, u32[]{:S(2)}) collective-permute-start(bf16[64,256]{1,0:T(8,128)(2,1)S(1)} %get-tuple-element.98), channel_id=1, source_target_pairs={{0,4},{1,5},{2,6},{3,7},{4,0},{5,1},{6,2},{7,3},{8,12},{9,13},{10,... | collective-permute-start | bytes 98312 | tf_op jit(solution)/shard_map/ppermute | solution.py:433
  37.7 0.0 collective-permute-done.10.refs_1_
  37.7 1.5 %backward.1 = (bf16[256,128]{1,0:T(8,128)(2,1)S(1)}, f32[128,128]{1,0:T(8,128)S(1)}, f32[256,128]{1,0:T(8,128)S(1)}, f32[512,128]{1,0:T(8,128)S(1)}, f32[512,128]{1,0:T(8,128)S(1)}) custom-call(bf16[256,512]{1,0:T(8,128)(2,1)S(1)} %w_half.1.refs_0_, bf16[256,512]{1,0:T(8,128)(2,1)S(1)} %collective-permute-done.10.refs_1_, ...), custom_call_target="tpu_custom_call" | custom-call | flops 335544320 | bytes 3277312 | tf_op jit(solution)/shard_map/backward/pallas_call | solution.py:66
  39.2 1.0 %collective-permute-start.13 = (bf16[128,384]{1,0:T(8,128)(2,1)S(1)}, bf16[128,384]{1,0:T(8,128)(2,1)S(1)}, u32[]{:S(2)}, u32[]{:S(2)}) collective-permute-start(bf16[128,384]{1,0:T(8,128)(2,1)S(1)} %get-tuple-element.93), channel_id=1, source_target_pairs={{0,2},{1,7},{2,0},{3,5},{4,6},{5,3},{6,4},{7,1},{8,10},{9,15},{10,... | collective-permute-start | bytes 294920 | tf_op jit(solution)/shard_map/ppermute | solution.py:433
  40.3 0.5 collective-permute-done.17.got
  40.8 1.8 %collective-permute-start.18 = (bf16[64,256]{1,0:T(8,128)(2,1)S(1)}, bf16[64,256]{1,0:T(8,128)(2,1)S(1)}, u32[]{:S(2)}, u32[]{:S(2)}) collective-permute-start(bf16[64,256]{1,0:T(8,128)(2,1)S(1)} %weight_sum.1.first), channel_id=1, source_target_pairs={{0,8},{1,17},{8,0},{9,25},{16,24},{17,1},{24,16},{25,9},{2,10},{3,... | collective-permute-start | bytes 98312 | tf_op jit(solution)/shard_map/ppermute | solution.py:439
  42.6 3.2 %collective-permute-start.14 = (bf16[128,384]{1,0:T(8,128)(2,1)S(1)}, bf16[128,384]{1,0:T(8,128)(2,1)S(1)}, u32[]{:S(2)}, u32[]{:S(2)}) collective-permute-start(bf16[128,384]{1,0:T(8,128)(2,1)S(1)} %get-tuple-element.94), channel_id=1, source_target_pairs={{0,6},{1,3},{2,4},{3,1},{4,2},{5,7},{6,0},{7,5},{8,14},{9,11},{10,... | collective-permute-start | bytes 294920 | tf_op jit(solution)/shard_map/ppermute | solution.py:433
  45.8 0.0 collective-permute-done.18.second
  45.8 1.8 %collective-permute-start.19 = (bf16[64,512]{1,0:T(8,128)(2,1)S(1)}, bf16[64,512]{1,0:T(8,128)(2,1)S(1)}, u32[]{:S(2)}, u32[]{:S(2)}) collective-permute-start(bf16[64,512]{1,0:T(8,128)(2,1)S(1)} %both.1), channel_id=1, source_target_pairs={{0,16},{1,9},{8,24},{9,1},{16,0},{17,25},{24,8},{25,17},{2,18},{3,... | collective-permute-start | bytes 196616 | tf_op jit(solution)/shard_map/ppermute | solution.py:439
  47.7 0.7 %collective-permute-start.15 = (bf16[128,128]{1,0:T(8,128)(2,1)S(1)}, bf16[128,128]{1,0:T(8,128)(2,1)S(1)}, u32[]{:S(2)}, u32[]{:S(2)}) collective-permute-start(bf16[128,128]{1,0:T(8,128)(2,1)S(1)} %get-tuple-element.95), channel_id=1, source_target_pairs={{0,4},{1,5},{2,6},{3,7},{4,0},{5,1},{6,2},{7,3},{8,12},{9,13},{10,... | collective-permute-start | bytes 98312 | tf_op jit(solution)/shard_map/ppermute | solution.py:433
  48.4 4.1 %collective-permute-done.15.refs_0_ = bf16[128,128]{1,0:T(8,128)(2,1)S(1)} collective-permute-done((bf16[128,128]{1,0:T(8,128)(2,1)S(1)}, bf16[128,128]{1,0:T(8,128)(2,1)S(1)}, u32[]{:S(2)}, u32[]{:S(2)}) %collective-permute-start.15) | collective-permute-done | bytes 32800 | tf_op jit(solution)/shard_map/ppermute | solution.py:433
  52.5 0.0 collective-permute-done.13.a
  52.5 0.0 collective-permute-done.14.b
  52.5 0.0 collective-permute-done.19.refs_1_.got
  52.5 0.4 final.1
  52.9 0.1 collective-permute-start.20
  52.9 1.4 %collective-permute-done.20.pair = bf16[128,768]{1,0:T(8,128)(2,1)S(1)} collective-permute-done((bf16[128,768]{1,0:T(8,128)(2,1)S(1)}, bf16[128,768]{1,0:T(8,128)(2,1)S(1)}, u32[]{:S(2)}, u32[]{:S(2)}) %collective-permute-start.20) | collective-permute-done | bytes 196640 | tf_op jit(solution)/shard_map/ppermute | solution.py:422
  54.4 0.8 %outputs.1 = (bf16[1,128,512]{2,1,0:T(8,128)(2,1)}, bf16[1,128,512]{2,1,0:T(8,128)(2,1)}, bf16[1,128,512]{2,1,0:T(8,128)(2,1)}) custom-call(bf16[128,768]{1,0:T(8,128)(2,1)S(1)} %get-tuple-element.99.own, bf16[128,768]{1,0:T(8,128)(2,1)S(1)} %collective-permute-done.20.pair), custom_call_target="tpu_custom_call" | custom-call | bytes 786432 | tf_op jit(solution)/shard_map/outputs/pallas_call | solution.py:66
  55.2 0.7 %weight_join.1 = f32[64,1024]{1,0:T(8,128)} custom-call(bf16[64,512]{1,0:T(8,128)(2,1)S(1)} %both.1, bf16[64,512]{1,0:T(8,128)(2,1)S(1)} %collective-permute-done.19.refs_1_.got, bf16[1,128,512]{2,1,0:T(8,128)(2,1)} %get-tuple-element.50._), custom_call_target="tpu_custom_call" | custom-call | bytes 524288 | tf_op jit(solution)/shard_map/weight_join/pallas_call | solution.py:66
  (8 shorter events, 0.2 us)
Async XLA Ops:
  0.6 2.3 %collective-permute-start = (bf16[1,128,512]{2,1,0:T(8,128)(2,1)}, bf16[1,128,512]{2,1,0:T(8,128)(2,1)S(1)}, u32[]{:S(2)}, u32[]{:S(2)}) collective-permute-start(bf16[1,128,512]{2,1,0:T(8,128)(2,1)} %q.1), channel_id=1, source_target_pairs={{0,1},{1,0},{2,3},{3,2},{4,5},{5,4},{6,7},{7,6},{8,9},{9,8},{10,11... | collective-permute-start | bytes 393224 | tf_op jit(solution)/shard_map/ppermute | solution.py:422
  1.2 1.8 %collective-permute-start.1 = (bf16[1,128,512]{2,1,0:T(8,128)(2,1)}, bf16[1,128,512]{2,1,0:T(8,128)(2,1)S(1)}, u32[]{:S(2)}, u32[]{:S(2)}) collective-permute-start(bf16[1,128,512]{2,1,0:T(8,128)(2,1)} %k.1), channel_id=1, source_target_pairs={{0,1},{1,0},{2,3},{3,2},{4,5},{5,4},{6,7},{7,6},{8,9},{9,8},{10,11... | collective-permute-start | bytes 393224 | tf_op jit(solution)/shard_map/ppermute | solution.py:422
  1.2 1.7 %collective-permute-start.2 = (bf16[1,128,512]{2,1,0:T(8,128)(2,1)}, bf16[1,128,512]{2,1,0:T(8,128)(2,1)S(1)}, u32[]{:S(2)}, u32[]{:S(2)}) collective-permute-start(bf16[1,128,512]{2,1,0:T(8,128)(2,1)} %v.1), channel_id=1, source_target_pairs={{0,1},{1,0},{2,3},{3,2},{4,5},{5,4},{6,7},{7,6},{8,9},{9,8},{10,11... | collective-permute-start | bytes 393224 | tf_op jit(solution)/shard_map/ppermute | solution.py:422
  1.7 7.2 %collective-permute-start.8 = (bf16[128,1024]{1,0:T(8,128)(2,1)}, bf16[128,1024]{1,0:T(8,128)(2,1)S(1)}, u32[]{:S(2)}, u32[]{:S(2)}) collective-permute-start(bf16[128,1024]{1,0:T(8,128)(2,1)} %bitcast.1), channel_id=1, source_target_pairs={{0,1},{1,0},{2,3},{3,2},{4,5},{5,4},{6,7},{7,6},{8,9},{9,8},{10,11... | collective-permute-start | bytes 786440 | tf_op jit(solution)/shard_map/ppermute | solution.py:422
  3.2 6.0 %collective-permute-start.3 = (bf16[128,512]{1,0:T(8,128)(2,1)S(1)}, bf16[128,512]{1,0:T(8,128)(2,1)S(1)}, u32[]{:S(2)}, u32[]{:S(2)}) collective-permute-start(bf16[128,512]{1,0:T(8,128)(2,1)S(1)} %get-tuple-element.56), channel_id=1, source_target_pairs={{0,2},{1,7},{2,0},{3,5},{4,6},{5,3},{6,4},{7,1},{8,10},{9,15},{10,... | collective-permute-start | bytes 393224 | tf_op jit(solution)/shard_map/ppermute | solution.py:433
  6.3 9.4 %collective-permute-start.4 = (bf16[128,512]{1,0:T(8,128)(2,1)S(1)}, bf16[128,512]{1,0:T(8,128)(2,1)S(1)}, u32[]{:S(2)}, u32[]{:S(2)}) collective-permute-start(bf16[128,512]{1,0:T(8,128)(2,1)S(1)} %get-tuple-element.57), channel_id=1, source_target_pairs={{0,6},{1,3},{2,4},{3,1},{4,2},{5,7},{6,0},{7,5},{8,14},{9,11},{10,... | collective-permute-start | bytes 393224 | tf_op jit(solution)/shard_map/ppermute | solution.py:433
  8.8 8.1 %collective-permute-start.5 = (bf16[128,256]{1,0:T(8,128)(2,1)S(1)}, bf16[128,256]{1,0:T(8,128)(2,1)S(1)}, u32[]{:S(2)}, u32[]{:S(2)}) collective-permute-start(bf16[128,256]{1,0:T(8,128)(2,1)S(1)} %get-tuple-element.58), channel_id=1, source_target_pairs={{0,4},{1,5},{2,6},{3,7},{4,0},{5,1},{6,2},{7,3},{8,12},{9,13},{10,... | collective-permute-start | bytes 196616 | tf_op jit(solution)/shard_map/ppermute | solution.py:433
  17.6 6.4 %collective-permute-start.9 = (bf16[256,512]{1,0:T(8,128)(2,1)S(1)}, bf16[256,512]{1,0:T(8,128)(2,1)S(1)}, u32[]{:S(2)}, u32[]{:S(2)}) collective-permute-start(bf16[256,512]{1,0:T(8,128)(2,1)S(1)} %get-tuple-element.75), channel_id=1, source_target_pairs={{0,8},{1,17},{8,0},{9,25},{16,24},{17,1},{24,16},{25,9},{2,10},{3,... | collective-permute-start | bytes 786440 | tf_op jit(solution)/shard_map/ppermute | solution.py:439
  19.2 1.3 %collective-permute-start.6 = (bf16[2,64,256]{2,1,0:T(8,128)(2,1)S(1)}, bf16[2,64,256]{2,1,0:T(8,128)(2,1)S(1)}, u32[]{:S(2)}, u32[]{:S(2)}) collective-permute-start(bf16[2,64,256]{2,1,0:T(8,128)(2,1)S(1)} %get-tuple-element.60), channel_id=1, source_target_pairs={{0,1},{1,0},{2,3},{3,2},{4,5},{5,4},{6,7},{7,6},{8,9},{9,8},{10,11... | collective-permute-start | bytes 196616 | tf_op jit(solution)/shard_map/ppermute | solution.py:422
  20.5 5.9 %collective-permute-start.7 = (bf16[256,256]{1,0:T(8,128)(2,1)S(1)}, bf16[256,256]{1,0:T(8,128)(2,1)S(1)}, u32[]{:S(2)}, u32[]{:S(2)}) collective-permute-start(bf16[256,256]{1,0:T(8,128)(2,1)S(1)} %w_rows.1.first), channel_id=1, source_target_pairs={{0,8},{1,17},{8,0},{9,25},{16,24},{17,1},{24,16},{25,9},{2,10},{3,... | collective-permute-start | bytes 393224 | tf_op jit(solution)/shard_map/ppermute | solution.py:439
  24.1 5.0 %collective-permute-start.11 = (bf16[256,256]{1,0:T(8,128)(2,1)S(1)}, bf16[256,256]{1,0:T(8,128)(2,1)S(1)}, u32[]{:S(2)}, u32[]{:S(2)}) collective-permute-start(bf16[256,256]{1,0:T(8,128)(2,1)S(1)} %get-tuple-element.76.refs_0_), channel_id=1, source_target_pairs={{0,16},{1,9},{8,24},{9,1},{16,0},{17,25},{24,8},{25,17},{2,18},{3,... | collective-permute-start | bytes 393224 | tf_op jit(solution)/shard_map/ppermute | solution.py:439
  26.5 11.2 %collective-permute-start.10 = (bf16[256,512]{1,0:T(8,128)(2,1)S(1)}, bf16[256,512]{1,0:T(8,128)(2,1)S(1)}, u32[]{:S(2)}, u32[]{:S(2)}) collective-permute-start(bf16[256,512]{1,0:T(8,128)(2,1)S(1)} %w_half.1.refs_0_), channel_id=1, source_target_pairs={{0,16},{1,9},{8,24},{9,1},{16,0},{17,25},{24,8},{25,17},{2,18},{3,... | collective-permute-start | bytes 786440 | tf_op jit(solution)/shard_map/ppermute | solution.py:439
  29.2 1.4 %collective-permute-start.12 = (f32[128,256]{1,0:T(8,128)S(1)}, f32[128,256]{1,0:T(8,128)S(1)}, u32[]{:S(2)}, u32[]{:S(2)}) collective-permute-start(f32[128,256]{1,0:T(8,128)S(1)} %get-tuple-element.79), channel_id=1, source_target_pairs={{0,1},{1,0},{2,3},{3,2},{4,5},{5,4},{6,7},{7,6},{8,9},{9,8},{10,11... | collective-permute-start | bytes 393224 | tf_op jit(solution)/shard_map/ppermute | solution.py:422
  30.7 4.3 %collective-permute-start.16 = (bf16[128,256]{1,0:T(8,128)(2,1)S(1)}, bf16[128,256]{1,0:T(8,128)(2,1)S(1)}, u32[]{:S(2)}, u32[]{:S(2)}) collective-permute-start(bf16[128,256]{1,0:T(8,128)(2,1)S(1)} %get-tuple-element.96), channel_id=1, source_target_pairs={{0,2},{1,7},{2,0},{3,5},{4,6},{5,3},{6,4},{7,1},{8,10},{9,15},{10,... | collective-permute-start | bytes 196616 | tf_op jit(solution)/shard_map/ppermute | solution.py:433
  35.0 5.8 %collective-permute-start.17 = (bf16[64,256]{1,0:T(8,128)(2,1)S(1)}, bf16[64,256]{1,0:T(8,128)(2,1)S(1)}, u32[]{:S(2)}, u32[]{:S(2)}) collective-permute-start(bf16[64,256]{1,0:T(8,128)(2,1)S(1)} %get-tuple-element.98), channel_id=1, source_target_pairs={{0,4},{1,5},{2,6},{3,7},{4,0},{5,1},{6,2},{7,3},{8,12},{9,13},{10,... | collective-permute-start | bytes 98312 | tf_op jit(solution)/shard_map/ppermute | solution.py:433
  39.2 13.2 %collective-permute-start.13 = (bf16[128,384]{1,0:T(8,128)(2,1)S(1)}, bf16[128,384]{1,0:T(8,128)(2,1)S(1)}, u32[]{:S(2)}, u32[]{:S(2)}) collective-permute-start(bf16[128,384]{1,0:T(8,128)(2,1)S(1)} %get-tuple-element.93), channel_id=1, source_target_pairs={{0,2},{1,7},{2,0},{3,5},{4,6},{5,3},{6,4},{7,1},{8,10},{9,15},{10,... | collective-permute-start | bytes 294920 | tf_op jit(solution)/shard_map/ppermute | solution.py:433
  40.8 5.0 %collective-permute-start.18 = (bf16[64,256]{1,0:T(8,128)(2,1)S(1)}, bf16[64,256]{1,0:T(8,128)(2,1)S(1)}, u32[]{:S(2)}, u32[]{:S(2)}) collective-permute-start(bf16[64,256]{1,0:T(8,128)(2,1)S(1)} %weight_sum.1.first), channel_id=1, source_target_pairs={{0,8},{1,17},{8,0},{9,25},{16,24},{17,1},{24,16},{25,9},{2,10},{3,... | collective-permute-start | bytes 98312 | tf_op jit(solution)/shard_map/ppermute | solution.py:439
  42.6 9.9 %collective-permute-start.14 = (bf16[128,384]{1,0:T(8,128)(2,1)S(1)}, bf16[128,384]{1,0:T(8,128)(2,1)S(1)}, u32[]{:S(2)}, u32[]{:S(2)}) collective-permute-start(bf16[128,384]{1,0:T(8,128)(2,1)S(1)} %get-tuple-element.94), channel_id=1, source_target_pairs={{0,6},{1,3},{2,4},{3,1},{4,2},{5,7},{6,0},{7,5},{8,14},{9,11},{10,... | collective-permute-start | bytes 294920 | tf_op jit(solution)/shard_map/ppermute | solution.py:433
  45.8 6.7 %collective-permute-start.19 = (bf16[64,512]{1,0:T(8,128)(2,1)S(1)}, bf16[64,512]{1,0:T(8,128)(2,1)S(1)}, u32[]{:S(2)}, u32[]{:S(2)}) collective-permute-start(bf16[64,512]{1,0:T(8,128)(2,1)S(1)} %both.1), channel_id=1, source_target_pairs={{0,16},{1,9},{8,24},{9,1},{16,0},{17,25},{24,8},{25,17},{2,18},{3,... | collective-permute-start | bytes 196616 | tf_op jit(solution)/shard_map/ppermute | solution.py:439
  47.7 4.8 %collective-permute-start.15 = (bf16[128,128]{1,0:T(8,128)(2,1)S(1)}, bf16[128,128]{1,0:T(8,128)(2,1)S(1)}, u32[]{:S(2)}, u32[]{:S(2)}) collective-permute-start(bf16[128,128]{1,0:T(8,128)(2,1)S(1)} %get-tuple-element.95), channel_id=1, source_target_pairs={{0,4},{1,5},{2,6},{3,7},{4,0},{5,1},{6,2},{7,3},{8,12},{9,13},{10,... | collective-permute-start | bytes 98312 | tf_op jit(solution)/shard_map/ppermute | solution.py:433
  52.9 1.5 %collective-permute-start.20 = (bf16[128,768]{1,0:T(8,128)(2,1)S(1)}, bf16[128,768]{1,0:T(8,128)(2,1)S(1)}, u32[]{:S(2)}, u32[]{:S(2)}) collective-permute-start(bf16[128,768]{1,0:T(8,128)(2,1)S(1)} %get-tuple-element.100), channel_id=1, source_target_pairs={{0,1},{1,0},{2,3},{3,2},{4,5},{5,4},{6,7},{7,6},{8,9},{9,8},{10,11... | collective-permute-start | bytes 589832 | tf_op jit(solution)/shard_map/ppermute | solution.py:422

commit v23 on v22

--- a/solution.py
+++ b/solution.py
@@ -574,7 +574,7 @@
         functools.partial(final_kernel, direct), "final",
         [like((rows, 6 * DH), BF), like((rows, 6 * DH), BF)],
         [dstate, mine, pair, dq_soft, dk_soft, dv_soft, dq_lin, a, b]
-        + (c + [gathered] if direct else []),
+        + (c + [both] if direct else []),
         scratch=[pltpu.VMEM((2 * rows, DH), F32)] * 2,
         flops=wg_flops // 4,
     )

time: 56 us -> 56.4 us (level)
  waiting for transfers between devices: 22.8 us -> 26.6 us
  starting transfers between devices: 25.1 us -> 21.7 us
    ppermute x6, waiting for transfers between devices: 4.13 us -> 9.41 us  [over_dp(): return lax.ppermute(value, ('dp', 'core'), pairs)]
    ppermute x8, starting transfers between devices: 14.2 us -> 11.6 us  [over_z(): return lax.ppermute(value, axes, pairs)]
    ppermute x7, waiting for transfers between devices: 4.01 us -> 2.59 us  [over_core(): return lax.ppermute(value, 'core', pair_perm)]
    ppermute x6, starting transfers between devices: 9.6 us -> 8.76 us  [over_dp(): return lax.ppermute(value, ('dp', 'core'), pairs)]
  transfers between devices with their start and end apart: 21 -> 21, of which waited for: 11 -> 12; matrix products, arithmetic and copies ran while one was open for 0% -> 0% of each run, Pallas kernels for 8% -> 10%
where the time goes in v23:
time: 56.4 us; the launch traced here: 56.3 us
  waiting for transfers between devices  26.6 us (47%)
  starting transfers between devices  21.7 us (38%)
  Pallas kernels  7.21 us (13%)
  between operations  0.79 us (1%)
    ppermute x8, waiting for transfers between devices, over_z(): return lax.ppermute(value, axes, pairs)  14.6 us
    ppermute x8, starting transfers between devices, over_z(): return lax.ppermute(value, axes, pairs)  11.6 us
    ppermute x6, waiting for transfers between devices, over_dp(): return lax.ppermute(value, ('dp', 'core'), pairs)  9.41 us
    ppermute x6, starting transfers between devices, over_dp(): return lax.ppermute(value, ('dp', 'core'), pairs)  8.76 us
    pallas_call x19, Pallas kernels, call(): pl.pallas_call(kernel, name=name, out_shape=list(outs), in_specs=spaces o...  7.21 us
    ppermute x7, waiting for transfers between devices, over_core(): return lax.ppermute(value, 'core', pair_perm)  2.59 us
    ppermute x7, starting transfers between devices, over_core(): return lax.ppermute(value, 'core', pair_perm)  1.32 us
  transfers between devices with their start and end apart: 21, of which 12 were waited for; matrix products, arithmetic and copies ran while one was open for 0% of the time, Pallas kernels for 10%

profile of v23, /device:TPU:0, one launch (start us, length us, event | category | flops | bytes accessed | tf_op | source)
XLA Modules:
  0.0 56.3 jit_solution(9709148351496403660)
XLA Ops:
  0.6 0.5 collective-permute-start
  1.2 0.1 collective-permute-start.1
  1.2 0.4 collective-permute-start.2
  1.7 0.1 collective-permute-start.8
  1.7 1.2 %pack.1 = (bf16[128,768]{1,0:T(8,128)(2,1)S(1)}, bf16[128,1024]{1,0:T(8,128)(2,1)S(1)}, bf16[64,256]{1,0:T(8,128)(2,1)S(1)}, f32[1,128]{1,0:T(1,128)S(1)}) custom-call(bf16[1,128,512]{2,1,0:T(8,128)(2,1)} %q.1, bf16[1,128,512]{2,1,0:T(8,128)(2,1)} %k.1, bf16[1,128,512]{2,1,0:T(8,128)(2,1)} %v.1, bf16[1,128,1024]{2,1,0:T(8,128)(2,1)} %og.1, ...), custom_call_target="tpu_custom_call" | custom-call | bytes 1279488 | tf_op jit(solution)/shard_map/pack/pallas_call | solution.py:66
  2.9 0.0 collective-permute-done.q_pair
  2.9 0.0 collective-permute-done.1.k_pair
  2.9 0.0 collective-permute-done.2.v_pair
  3.0 0.3 state.1
  3.2 3.1 %collective-permute-start.3 = (bf16[128,512]{1,0:T(8,128)(2,1)S(1)}, bf16[128,512]{1,0:T(8,128)(2,1)S(1)}, u32[]{:S(2)}, u32[]{:S(2)}) collective-permute-start(bf16[128,512]{1,0:T(8,128)(2,1)S(1)} %get-tuple-element.56), channel_id=1, source_target_pairs={{0,2},{1,7},{2,0},{3,5},{4,6},{5,3},{6,4},{7,1},{8,10},{9,15},{10,... | collective-permute-start | bytes 393224 | tf_op jit(solution)/shard_map/ppermute | solution.py:433
  6.3 2.5 %collective-permute-start.4 = (bf16[128,512]{1,0:T(8,128)(2,1)S(1)}, bf16[128,512]{1,0:T(8,128)(2,1)S(1)}, u32[]{:S(2)}, u32[]{:S(2)}) collective-permute-start(bf16[128,512]{1,0:T(8,128)(2,1)S(1)} %get-tuple-element.57), channel_id=1, source_target_pairs={{0,6},{1,3},{2,4},{3,1},{4,2},{5,7},{6,0},{7,5},{8,14},{9,11},{10,... | collective-permute-start | bytes 393224 | tf_op jit(solution)/shard_map/ppermute | solution.py:433
  8.8 0.1 collective-permute-start.5
  8.9 0.0 collective-permute-done.8.og_recv
  8.9 0.3 prep.1
  9.2 0.1 collective-permute-done.3.a.refs_0_
  9.3 6.5 %collective-permute-done.4.b.refs_1_ = bf16[128,512]{1,0:T(8,128)(2,1)S(1)} collective-permute-done((bf16[128,512]{1,0:T(8,128)(2,1)S(1)}, bf16[128,512]{1,0:T(8,128)(2,1)S(1)}, u32[]{:S(2)}, u32[]{:S(2)}) %collective-permute-start.4) | collective-permute-done | bytes 131104 | tf_op jit(solution)/shard_map/ppermute | solution.py:433
  15.7 1.2 %soft_forward.1 = (bf16[512,128]{1,0:T(8,128)(2,1)S(1)}, bf16[512,128]{1,0:T(8,128)(2,1)S(1)}, f32[2,128,384]{2,1,0:T(8,128)S(1)}, f32[256,128]{1,0:T(8,128)S(1)...) custom-call(bf16[256,128]{1,0:T(8,128)(2,1)S(1)} %get-tuple-element.63.qs.refs_10_, ...), custom_call_target="tpu_custom_call" | custom-call | flops 67108864 | bytes 2424832 | tf_op jit(solution)/shard_map/soft_forward/pallas_call | solution.py:66
  16.9 0.0 collective-permute-done.5.c.refs_2_
  16.9 0.7 %lin_forward.1 = (f32[256,128]{1,0:T(8,128)S(1)}, f32[128,128]{1,0:T(8,128)S(1)}, f32[128,512]{1,0:T(8,128)S(1)}, bf16[256,512]{1,0:T(8,128)(2,1)S(1)}) custom-call(f32[128,128]{1,0:T(8,128)S(1)} %get-tuple-element.69.state, bf16[256,128]{1,0:T(8,128)(2,1)S(1)} %get-tuple-element.70.phi_high.refs_6_, bf16[256,128]{1,0:T(8,128)(2,1)S(1)} %get-tuple-element.71.phi_low.refs_7_, ...), custom_call_target="tpu_custom_call" | custom-call | flops 67108864 | bytes 1901056 | tf_op jit(solution)/shard_map/lin_forward/pallas_call | solution.py:66
  17.6 1.6 %collective-permute-start.9 = (bf16[256,512]{1,0:T(8,128)(2,1)S(1)}, bf16[256,512]{1,0:T(8,128)(2,1)S(1)}, u32[]{:S(2)}, u32[]{:S(2)}) collective-permute-start(bf16[256,512]{1,0:T(8,128)(2,1)S(1)} %get-tuple-element.75), channel_id=1, source_target_pairs={{0,8},{1,17},{8,0},{9,25},{16,24},{17,1},{24,16},{25,9},{2,10},{3,... | collective-permute-start | bytes 786440 | tf_op jit(solution)/shard_map/ppermute | solution.py:439
  19.2 0.1 collective-permute-start.6
  19.3 1.2 %collective-permute-done.6.got = bf16[2,64,256]{2,1,0:T(8,128)(2,1)S(1)} collective-permute-done((bf16[2,64,256]{2,1,0:T(8,128)(2,1)S(1)}, bf16[2,64,256]{2,1,0:T(8,128)(2,1)S(1)}, u32[]{:S(2)}, u32[]{:S(2)}) %collective-permute-start.6) | collective-permute-done | bytes 65568 | tf_op jit(solution)/shard_map/ppermute | solution.py:422
  20.5 0.6 %collective-permute-start.7 = (bf16[256,256]{1,0:T(8,128)(2,1)S(1)}, bf16[256,256]{1,0:T(8,128)(2,1)S(1)}, u32[]{:S(2)}, u32[]{:S(2)}) collective-permute-start(bf16[256,256]{1,0:T(8,128)(2,1)S(1)} %w_rows.1.first), channel_id=1, source_target_pairs={{0,8},{1,17},{8,0},{9,25},{16,24},{17,1},{24,16},{25,9},{2,10},{3,... | collective-permute-start | bytes 393224 | tf_op jit(solution)/shard_map/ppermute | solution.py:439
  21.1 2.9 %collective-permute-done.9.got = bf16[256,512]{1,0:T(8,128)(2,1)S(1)} collective-permute-done((bf16[256,512]{1,0:T(8,128)(2,1)S(1)}, bf16[256,512]{1,0:T(8,128)(2,1)S(1)}, u32[]{:S(2)}, u32[]{:S(2)}) %collective-permute-start.9) | collective-permute-done | bytes 262176 | tf_op jit(solution)/shard_map/ppermute | solution.py:439
  24.0 0.1 fold.1
  24.1 1.8 %collective-permute-start.11 = (bf16[256,256]{1,0:T(8,128)(2,1)S(1)}, bf16[256,256]{1,0:T(8,128)(2,1)S(1)}, u32[]{:S(2)}, u32[]{:S(2)}) collective-permute-start(bf16[256,256]{1,0:T(8,128)(2,1)S(1)} %get-tuple-element.76.refs_0_), channel_id=1, source_target_pairs={{0,16},{1,9},{8,24},{9,1},{16,0},{17,25},{24,8},{25,17},{2,18},{3,... | collective-permute-start | bytes 393224 | tf_op jit(solution)/shard_map/ppermute | solution.py:439
  25.9 0.5 collective-permute-done.7.second
  26.5 1.9 %collective-permute-start.10 = (bf16[256,512]{1,0:T(8,128)(2,1)S(1)}, bf16[256,512]{1,0:T(8,128)(2,1)S(1)}, u32[]{:S(2)}, u32[]{:S(2)}) collective-permute-start(bf16[256,512]{1,0:T(8,128)(2,1)S(1)} %w_half.1.refs_0_), channel_id=1, source_target_pairs={{0,16},{1,9},{8,24},{9,1},{16,0},{17,25},{24,8},{25,17},{2,18},{3,... | collective-permute-start | bytes 786440 | tf_op jit(solution)/shard_map/ppermute | solution.py:439
  28.5 0.7 %collective-permute-done.11.got = bf16[256,256]{1,0:T(8,128)(2,1)S(1)} collective-permute-done((bf16[256,256]{1,0:T(8,128)(2,1)S(1)}, bf16[256,256]{1,0:T(8,128)(2,1)S(1)}, u32[]{:S(2)}, u32[]{:S(2)}) %collective-permute-start.11) | collective-permute-done | bytes 131104 | tf_op jit(solution)/shard_map/ppermute | solution.py:439
  29.1 0.1 rows.1
  29.2 0.1 collective-permute-start.12
  29.3 1.3 %collective-permute-done.12.got = f32[128,256]{1,0:T(8,128)S(1)} collective-permute-done((f32[128,256]{1,0:T(8,128)S(1)}, f32[128,256]{1,0:T(8,128)S(1)}, u32[]{:S(2)}, u32[]{:S(2)}) %collective-permute-start.12) | collective-permute-done | bytes 131104 | tf_op jit(solution)/shard_map/ppermute | solution.py:422
  30.7 0.8 %collective-permute-start.16 = (bf16[128,256]{1,0:T(8,128)(2,1)S(1)}, bf16[128,256]{1,0:T(8,128)(2,1)S(1)}, u32[]{:S(2)}, u32[]{:S(2)}) collective-permute-start(bf16[128,256]{1,0:T(8,128)(2,1)S(1)} %get-tuple-element.96), channel_id=1, source_target_pairs={{0,2},{1,7},{2,0},{3,5},{4,6},{5,3},{6,4},{7,1},{8,10},{9,15},{10,... | collective-permute-start | bytes 196616 | tf_op jit(solution)/shard_map/ppermute | solution.py:433
  31.5 1.5 %collective-permute-done.10.refs_1_ = bf16[256,512]{1,0:T(8,128)(2,1)S(1)} collective-permute-done((bf16[256,512]{1,0:T(8,128)(2,1)S(1)}, bf16[256,512]{1,0:T(8,128)(2,1)S(1)}, u32[]{:S(2)}, u32[]{:S(2)}) %collective-permute-start.10) | collective-permute-done | bytes 262176 | tf_op jit(solution)/shard_map/ppermute | solution.py:439
  32.9 1.5 %backward.1 = (bf16[256,128]{1,0:T(8,128)(2,1)S(1)}, f32[128,128]{1,0:T(8,128)S(1)}, f32[256,128]{1,0:T(8,128)S(1)}, f32[512,128]{1,0:T(8,128)S(1)}, f32[512,128]{1,0:T(8,128)S(1)}) custom-call(bf16[256,512]{1,0:T(8,128)(2,1)S(1)} %w_half.1.refs_0_, bf16[256,512]{1,0:T(8,128)(2,1)S(1)} %collective-permute-done.10.refs_1_, ...), custom_call_target="tpu_custom_call" | custom-call | flops 335544320 | bytes 3277312 | tf_op jit(solution)/shard_map/backward/pallas_call | solution.py:66
  34.4 0.4 collective-permute-start.13
  34.9 3.7 %collective-permute-start.14 = (bf16[128,384]{1,0:T(8,128)(2,1)S(1)}, bf16[128,384]{1,0:T(8,128)(2,1)S(1)}, u32[]{:S(2)}, u32[]{:S(2)}) collective-permute-start(bf16[128,384]{1,0:T(8,128)(2,1)S(1)} %get-tuple-element.94), channel_id=1, source_target_pairs={{0,6},{1,3},{2,4},{3,1},{4,2},{5,7},{6,0},{7,5},{8,14},{9,11},{10,... | collective-permute-start | bytes 294920 | tf_op jit(solution)/shard_map/ppermute | solution.py:433
  38.6 0.0 collective-permute-done.16.got
  38.6 0.1 collective-permute-start.17
  38.7 6.1 %collective-permute-done.17.got = bf16[64,256]{1,0:T(8,128)(2,1)S(1)} collective-permute-done((bf16[64,256]{1,0:T(8,128)(2,1)S(1)}, bf16[64,256]{1,0:T(8,128)(2,1)S(1)}, u32[]{:S(2)}, u32[]{:S(2)}) %collective-permute-start.17) | collective-permute-done | bytes 32800 | tf_op jit(solution)/shard_map/ppermute | solution.py:433
  44.8 1.1 %collective-permute-start.18 = (bf16[64,256]{1,0:T(8,128)(2,1)S(1)}, bf16[64,256]{1,0:T(8,128)(2,1)S(1)}, u32[]{:S(2)}, u32[]{:S(2)}) collective-permute-start(bf16[64,256]{1,0:T(8,128)(2,1)S(1)} %weight_sum.1.first), channel_id=1, source_target_pairs={{0,8},{1,17},{8,0},{9,25},{16,24},{17,1},{24,16},{25,9},{2,10},{3,... | collective-permute-start | bytes 98312 | tf_op jit(solution)/shard_map/ppermute | solution.py:439
  45.9 0.9 %collective-permute-start.15 = (bf16[128,128]{1,0:T(8,128)(2,1)S(1)}, bf16[128,128]{1,0:T(8,128)(2,1)S(1)}, u32[]{:S(2)}, u32[]{:S(2)}) collective-permute-start(bf16[128,128]{1,0:T(8,128)(2,1)S(1)} %get-tuple-element.95), channel_id=1, source_target_pairs={{0,4},{1,5},{2,6},{3,7},{4,0},{5,1},{6,2},{7,3},{8,12},{9,13},{10,... | collective-permute-start | bytes 98312 | tf_op jit(solution)/shard_map/ppermute | solution.py:433
  46.8 2.0 %collective-permute-done.18.second = bf16[64,256]{1,0:T(8,128)(2,1)S(1)} collective-permute-done((bf16[64,256]{1,0:T(8,128)(2,1)S(1)}, bf16[64,256]{1,0:T(8,128)(2,1)S(1)}, u32[]{:S(2)}, u32[]{:S(2)}) %collective-permute-start.18) | collective-permute-done | bytes 32800 | tf_op jit(solution)/shard_map/ppermute | solution.py:439
  48.8 2.0 %collective-permute-done.15.refs_0_ = bf16[128,128]{1,0:T(8,128)(2,1)S(1)} collective-permute-done((bf16[128,128]{1,0:T(8,128)(2,1)S(1)}, bf16[128,128]{1,0:T(8,128)(2,1)S(1)}, u32[]{:S(2)}, u32[]{:S(2)}) %collective-permute-start.15) | collective-permute-done | bytes 32800 | tf_op jit(solution)/shard_map/ppermute | solution.py:433
  50.7 0.0 collective-permute-done.13.a
  50.8 0.0 collective-permute-done.14.b
  50.8 0.4 final.1
  51.1 0.1 collective-permute-start.19
  51.2 1.7 %collective-permute-start.20 = (bf16[64,512]{1,0:T(8,128)(2,1)S(1)}, bf16[64,512]{1,0:T(8,128)(2,1)S(1)}, u32[]{:S(2)}, u32[]{:S(2)}) collective-permute-start(bf16[64,512]{1,0:T(8,128)(2,1)S(1)} %both.1.refs_1_), channel_id=1, source_target_pairs={{0,16},{1,9},{8,24},{9,1},{16,0},{17,25},{24,8},{25,17},{2,18},{3,... | collective-permute-start | bytes 196616 | tf_op jit(solution)/shard_map/ppermute | solution.py:439
  52.9 0.0 collective-permute-done.19.pair
  52.9 0.8 %outputs.1 = (bf16[1,128,512]{2,1,0:T(8,128)(2,1)}, bf16[1,128,512]{2,1,0:T(8,128)(2,1)}, bf16[1,128,512]{2,1,0:T(8,128)(2,1)}) custom-call(bf16[128,768]{1,0:T(8,128)(2,1)S(1)} %get-tuple-element.99.own, bf16[128,768]{1,0:T(8,128)(2,1)S(1)} %collective-permute-done.19.pair), custom_call_target="tpu_custom_call" | custom-call | bytes 786432 | tf_op jit(solution)/shard_map/outputs/pallas_call | solution.py:66
  53.7 1.8 %collective-permute-done.20.got = bf16[64,512]{1,0:T(8,128)(2,1)S(1)} collective-permute-done((bf16[64,512]{1,0:T(8,128)(2,1)S(1)}, bf16[64,512]{1,0:T(8,128)(2,1)S(1)}, u32[]{:S(2)}, u32[]{:S(2)}) %collective-permute-start.20) | collective-permute-done | bytes 65568 | tf_op jit(solution)/shard_map/ppermute | solution.py:439
  55.5 0.7 %weight_join.1 = f32[64,1024]{1,0:T(8,128)} custom-call(bf16[64,512]{1,0:T(8,128)(2,1)S(1)} %both.1.refs_1_, bf16[64,512]{1,0:T(8,128)(2,1)S(1)} %collective-permute-done.20.got, bf16[1,128,512]{2,1,0:T(8,128)(2,1)} %get-tuple-element.50._), custom_call_target="tpu_custom_call" | custom-call | bytes 524288 | tf_op jit(solution)/shard_map/weight_join/pallas_call | solution.py:66
  (8 shorter events, 0.2 us)
Async XLA Ops:
  0.6 2.3 %collective-permute-start = (bf16[1,128,512]{2,1,0:T(8,128)(2,1)}, bf16[1,128,512]{2,1,0:T(8,128)(2,1)S(1)}, u32[]{:S(2)}, u32[]{:S(2)}) collective-permute-start(bf16[1,128,512]{2,1,0:T(8,128)(2,1)} %q.1), channel_id=1, source_target_pairs={{0,1},{1,0},{2,3},{3,2},{4,5},{5,4},{6,7},{7,6},{8,9},{9,8},{10,11... | collective-permute-start | bytes 393224 | tf_op jit(solution)/shard_map/ppermute | solution.py:422
  1.2 1.8 %collective-permute-start.1 = (bf16[1,128,512]{2,1,0:T(8,128)(2,1)}, bf16[1,128,512]{2,1,0:T(8,128)(2,1)S(1)}, u32[]{:S(2)}, u32[]{:S(2)}) collective-permute-start(bf16[1,128,512]{2,1,0:T(8,128)(2,1)} %k.1), channel_id=1, source_target_pairs={{0,1},{1,0},{2,3},{3,2},{4,5},{5,4},{6,7},{7,6},{8,9},{9,8},{10,11... | collective-permute-start | bytes 393224 | tf_op jit(solution)/shard_map/ppermute | solution.py:422
  1.2 1.7 %collective-permute-start.2 = (bf16[1,128,512]{2,1,0:T(8,128)(2,1)}, bf16[1,128,512]{2,1,0:T(8,128)(2,1)S(1)}, u32[]{:S(2)}, u32[]{:S(2)}) collective-permute-start(bf16[1,128,512]{2,1,0:T(8,128)(2,1)} %v.1), channel_id=1, source_target_pairs={{0,1},{1,0},{2,3},{3,2},{4,5},{5,4},{6,7},{7,6},{8,9},{9,8},{10,11... | collective-permute-start | bytes 393224 | tf_op jit(solution)/shard_map/ppermute | solution.py:422
  1.7 7.2 %collective-permute-start.8 = (bf16[128,1024]{1,0:T(8,128)(2,1)}, bf16[128,1024]{1,0:T(8,128)(2,1)S(1)}, u32[]{:S(2)}, u32[]{:S(2)}) collective-permute-start(bf16[128,1024]{1,0:T(8,128)(2,1)} %bitcast.1), channel_id=1, source_target_pairs={{0,1},{1,0},{2,3},{3,2},{4,5},{5,4},{6,7},{7,6},{8,9},{9,8},{10,11... | collective-permute-start | bytes 786440 | tf_op jit(solution)/shard_map/ppermute | solution.py:422
  3.2 6.0 %collective-permute-start.3 = (bf16[128,512]{1,0:T(8,128)(2,1)S(1)}, bf16[128,512]{1,0:T(8,128)(2,1)S(1)}, u32[]{:S(2)}, u32[]{:S(2)}) collective-permute-start(bf16[128,512]{1,0:T(8,128)(2,1)S(1)} %get-tuple-element.56), channel_id=1, source_target_pairs={{0,2},{1,7},{2,0},{3,5},{4,6},{5,3},{6,4},{7,1},{8,10},{9,15},{10,... | collective-permute-start | bytes 393224 | tf_op jit(solution)/shard_map/ppermute | solution.py:433
  6.3 9.4 %collective-permute-start.4 = (bf16[128,512]{1,0:T(8,128)(2,1)S(1)}, bf16[128,512]{1,0:T(8,128)(2,1)S(1)}, u32[]{:S(2)}, u32[]{:S(2)}) collective-permute-start(bf16[128,512]{1,0:T(8,128)(2,1)S(1)} %get-tuple-element.57), channel_id=1, source_target_pairs={{0,6},{1,3},{2,4},{3,1},{4,2},{5,7},{6,0},{7,5},{8,14},{9,11},{10,... | collective-permute-start | bytes 393224 | tf_op jit(solution)/shard_map/ppermute | solution.py:433
  8.8 8.1 %collective-permute-start.5 = (bf16[128,256]{1,0:T(8,128)(2,1)S(1)}, bf16[128,256]{1,0:T(8,128)(2,1)S(1)}, u32[]{:S(2)}, u32[]{:S(2)}) collective-permute-start(bf16[128,256]{1,0:T(8,128)(2,1)S(1)} %get-tuple-element.58), channel_id=1, source_target_pairs={{0,4},{1,5},{2,6},{3,7},{4,0},{5,1},{6,2},{7,3},{8,12},{9,13},{10,... | collective-permute-start | bytes 196616 | tf_op jit(solution)/shard_map/ppermute | solution.py:433
  17.6 6.4 %collective-permute-start.9 = (bf16[256,512]{1,0:T(8,128)(2,1)S(1)}, bf16[256,512]{1,0:T(8,128)(2,1)S(1)}, u32[]{:S(2)}, u32[]{:S(2)}) collective-permute-start(bf16[256,512]{1,0:T(8,128)(2,1)S(1)} %get-tuple-element.75), channel_id=1, source_target_pairs={{0,8},{1,17},{8,0},{9,25},{16,24},{17,1},{24,16},{25,9},{2,10},{3,... | collective-permute-start | bytes 786440 | tf_op jit(solution)/shard_map/ppermute | solution.py:439
  19.2 1.3 %collective-permute-start.6 = (bf16[2,64,256]{2,1,0:T(8,128)(2,1)S(1)}, bf16[2,64,256]{2,1,0:T(8,128)(2,1)S(1)}, u32[]{:S(2)}, u32[]{:S(2)}) collective-permute-start(bf16[2,64,256]{2,1,0:T(8,128)(2,1)S(1)} %get-tuple-element.60), channel_id=1, source_target_pairs={{0,1},{1,0},{2,3},{3,2},{4,5},{5,4},{6,7},{7,6},{8,9},{9,8},{10,11... | collective-permute-start | bytes 196616 | tf_op jit(solution)/shard_map/ppermute | solution.py:422
  20.5 5.9 %collective-permute-start.7 = (bf16[256,256]{1,0:T(8,128)(2,1)S(1)}, bf16[256,256]{1,0:T(8,128)(2,1)S(1)}, u32[]{:S(2)}, u32[]{:S(2)}) collective-permute-start(bf16[256,256]{1,0:T(8,128)(2,1)S(1)} %w_rows.1.first), channel_id=1, source_target_pairs={{0,8},{1,17},{8,0},{9,25},{16,24},{17,1},{24,16},{25,9},{2,10},{3,... | collective-permute-start | bytes 393224 | tf_op jit(solution)/shard_map/ppermute | solution.py:439
  24.1 5.0 %collective-permute-start.11 = (bf16[256,256]{1,0:T(8,128)(2,1)S(1)}, bf16[256,256]{1,0:T(8,128)(2,1)S(1)}, u32[]{:S(2)}, u32[]{:S(2)}) collective-permute-start(bf16[256,256]{1,0:T(8,128)(2,1)S(1)} %get-tuple-element.76.refs_0_), channel_id=1, source_target_pairs={{0,16},{1,9},{8,24},{9,1},{16,0},{17,25},{24,8},{25,17},{2,18},{3,... | collective-permute-start | bytes 393224 | tf_op jit(solution)/shard_map/ppermute | solution.py:439
  26.5 6.4 %collective-permute-start.10 = (bf16[256,512]{1,0:T(8,128)(2,1)S(1)}, bf16[256,512]{1,0:T(8,128)(2,1)S(1)}, u32[]{:S(2)}, u32[]{:S(2)}) collective-permute-start(bf16[256,512]{1,0:T(8,128)(2,1)S(1)} %w_half.1.refs_0_), channel_id=1, source_target_pairs={{0,16},{1,9},{8,24},{9,1},{16,0},{17,25},{24,8},{25,17},{2,18},{3,... | collective-permute-start | bytes 786440 | tf_op jit(solution)/shard_map/ppermute | solution.py:439
  29.2 1.4 %collective-permute-start.12 = (f32[128,256]{1,0:T(8,128)S(1)}, f32[128,256]{1,0:T(8,128)S(1)}, u32[]{:S(2)}, u32[]{:S(2)}) collective-permute-start(f32[128,256]{1,0:T(8,128)S(1)} %get-tuple-element.79), channel_id=1, source_target_pairs={{0,1},{1,0},{2,3},{3,2},{4,5},{5,4},{6,7},{7,6},{8,9},{9,8},{10,11... | collective-permute-start | bytes 393224 | tf_op jit(solution)/shard_map/ppermute | solution.py:422
  30.7 8.0 %collective-permute-start.16 = (bf16[128,256]{1,0:T(8,128)(2,1)S(1)}, bf16[128,256]{1,0:T(8,128)(2,1)S(1)}, u32[]{:S(2)}, u32[]{:S(2)}) collective-permute-start(bf16[128,256]{1,0:T(8,128)(2,1)S(1)} %get-tuple-element.96), channel_id=1, source_target_pairs={{0,2},{1,7},{2,0},{3,5},{4,6},{5,3},{6,4},{7,1},{8,10},{9,15},{10,... | collective-permute-start | bytes 196616 | tf_op jit(solution)/shard_map/ppermute | solution.py:433
  34.4 16.3 %collective-permute-start.13 = (bf16[128,384]{1,0:T(8,128)(2,1)S(1)}, bf16[128,384]{1,0:T(8,128)(2,1)S(1)}, u32[]{:S(2)}, u32[]{:S(2)}) collective-permute-start(bf16[128,384]{1,0:T(8,128)(2,1)S(1)} %get-tuple-element.93), channel_id=1, source_target_pairs={{0,2},{1,7},{2,0},{3,5},{4,6},{5,3},{6,4},{7,1},{8,10},{9,15},{10,... | collective-permute-start | bytes 294920 | tf_op jit(solution)/shard_map/ppermute | solution.py:433
  34.9 15.9 %collective-permute-start.14 = (bf16[128,384]{1,0:T(8,128)(2,1)S(1)}, bf16[128,384]{1,0:T(8,128)(2,1)S(1)}, u32[]{:S(2)}, u32[]{:S(2)}) collective-permute-start(bf16[128,384]{1,0:T(8,128)(2,1)S(1)} %get-tuple-element.94), channel_id=1, source_target_pairs={{0,6},{1,3},{2,4},{3,1},{4,2},{5,7},{6,0},{7,5},{8,14},{9,11},{10,... | collective-permute-start | bytes 294920 | tf_op jit(solution)/shard_map/ppermute | solution.py:433
  38.6 6.1 %collective-permute-start.17 = (bf16[64,256]{1,0:T(8,128)(2,1)S(1)}, bf16[64,256]{1,0:T(8,128)(2,1)S(1)}, u32[]{:S(2)}, u32[]{:S(2)}) collective-permute-start(bf16[64,256]{1,0:T(8,128)(2,1)S(1)} %get-tuple-element.98), channel_id=1, source_target_pairs={{0,4},{1,5},{2,6},{3,7},{4,0},{5,1},{6,2},{7,3},{8,12},{9,13},{10,... | collective-permute-start | bytes 98312 | tf_op jit(solution)/shard_map/ppermute | solution.py:433
  44.8 4.0 %collective-permute-start.18 = (bf16[64,256]{1,0:T(8,128)(2,1)S(1)}, bf16[64,256]{1,0:T(8,128)(2,1)S(1)}, u32[]{:S(2)}, u32[]{:S(2)}) collective-permute-start(bf16[64,256]{1,0:T(8,128)(2,1)S(1)} %weight_sum.1.first), channel_id=1, source_target_pairs={{0,8},{1,17},{8,0},{9,25},{16,24},{17,1},{24,16},{25,9},{2,10},{3,... | collective-permute-start | bytes 98312 | tf_op jit(solution)/shard_map/ppermute | solution.py:439
  45.9 4.8 %collective-permute-start.15 = (bf16[128,128]{1,0:T(8,128)(2,1)S(1)}, bf16[128,128]{1,0:T(8,128)(2,1)S(1)}, u32[]{:S(2)}, u32[]{:S(2)}) collective-permute-start(bf16[128,128]{1,0:T(8,128)(2,1)S(1)} %get-tuple-element.95), channel_id=1, source_target_pairs={{0,4},{1,5},{2,6},{3,7},{4,0},{5,1},{6,2},{7,3},{8,12},{9,13},{10,... | collective-permute-start | bytes 98312 | tf_op jit(solution)/shard_map/ppermute | solution.py:433
  51.1 1.8 %collective-permute-start.19 = (bf16[128,768]{1,0:T(8,128)(2,1)S(1)}, bf16[128,768]{1,0:T(8,128)(2,1)S(1)}, u32[]{:S(2)}, u32[]{:S(2)}) collective-permute-start(bf16[128,768]{1,0:T(8,128)(2,1)S(1)} %get-tuple-element.100), channel_id=1, source_target_pairs={{0,1},{1,0},{2,3},{3,2},{4,5},{5,4},{6,7},{7,6},{8,9},{9,8},{10,11... | collective-permute-start | bytes 589832 | tf_op jit(solution)/shard_map/ppermute | solution.py:422
  51.2 4.3 %collective-permute-start.20 = (bf16[64,512]{1,0:T(8,128)(2,1)S(1)}, bf16[64,512]{1,0:T(8,128)(2,1)S(1)}, u32[]{:S(2)}, u32[]{:S(2)}) collective-permute-start(bf16[64,512]{1,0:T(8,128)(2,1)S(1)} %both.1.refs_1_), channel_id=1, source_target_pairs={{0,16},{1,9},{8,24},{9,1},{16,0},{17,25},{24,8},{25,17},{2,18},{3,... | collective-permute-start | bytes 196616 | tf_op jit(solution)/shard_map/ppermute | solution.py:439
